TPU v7x, 32 devices: a whole 2x2x4 slice. The times are simulated.
32 devices in a mesh: dp: 2 (over y), tensor: 4 (over x, core), expert: 4 (over z).
Axes of the slice: x: 2, y: 2, z: 4, core: 2. Of those that a mesh axis runs over, the one named last changes fastest.
Arguments:
- tokens: bfloat16 [1024, 2048], P('dp', 'tensor'), may hold values from -6 to 6
- grad_out: bfloat16 [1024, 2048], P('dp', 'tensor'), may hold values from -6 to 6
- routes: int32 [1024, 8], P('dp'), may hold values from 0 to 127, all different within a row; in each aligned block of 512 rows (0 to 511, 512 to 1023, ...) at most 48 rows name the same one
- gates: float32 [1024, 8], P('dp'), may hold values from 0.03 to 0.3
- gate_weight: bfloat16 [16, 1536, 2048], P(('expert', 'tensor'), 'dp'), may hold values from -0.125 to 0.125
- up_weight: bfloat16 [16, 1536, 2048], P(('expert', 'tensor'), 'dp'), may hold values from -0.125 to 0.125
- down_weight: bfloat16 [16, 1536, 2048], P(('expert', 'tensor'), 'dp'), may hold values from -0.15625 to 0.15625
Outputs:
- mixed: bfloat16 [1024, 2048], P('dp', 'tensor')
- grad_tokens: bfloat16 [1024, 2048], P('dp', 'tensor')
- grad_gates: float32 [1024, 8], P('dp')
Inputs may be any that keep to these rules, and one draw needn't show every extreme that they name: `routes`: each row names 8 different experts. Among the 512 rows of one block no expert is named more than 48 times, a bound that some block reaches.
All inputs are finite; a program needn't handle non-finite values.
Results may differ from a plain program's by a relative error of at most 0.017.
Values may be sent and summed in bfloat16 or wider, within the bound.
No kernel may reach another device: no remote copies, remote signals or barrier semaphores. Data moves between devices by JAX's collectives and lax.ppermute only.
A program may use at most 64 MiB of HBM per device.

v0:
```python
import jax
import jax.numpy as jnp
from jax import lax
from jax.sharding import PartitionSpec as P

CAP = 48


def silu_parts(gate_pre):
    sigmoid_val = jax.nn.sigmoid(gate_pre)
    return (gate_pre * sigmoid_val, sigmoid_val * (1.0 + gate_pre * (1.0 - sigmoid_val)))


def body(tokens, grad_out, routes, gates, gate_weight, up_weight, down_weight):
    tok_rows = tokens.shape[0]
    route_count = routes.shape[1]
    groups = lax.axis_size("tensor")
    hid_dev = gate_weight.shape[1]
    capacity = CAP
    contract = (((1,), (1,)), ((), ()))
    pick_dims = (((0,), (0,)), ((), ()))
    first_id = lax.axis_index("expert") * groups
    local_ids = first_id + jnp.arange(groups, dtype=jnp.int32)
    flat_ids = routes.reshape(-1)
    onehot = (flat_ids[:, None] == local_ids[None, :]).astype(jnp.int32)
    ranking = jnp.sum((jnp.cumsum(onehot, axis=0) - 1) * onehot, axis=1)
    position = jnp.sum(onehot * jnp.arange(groups, dtype=jnp.int32)[None, :], axis=1)
    inside = jnp.sum(onehot, axis=1) > 0
    slot_ids = jnp.where(inside, position * capacity + ranking, -1).reshape(tok_rows, -1)
    slot_iota = jnp.arange(groups * capacity, dtype=jnp.int32)
    weighted = jnp.zeros((tok_rows, groups * capacity), jnp.float32)
    slot_hits = jnp.zeros((tok_rows, groups * capacity), jnp.float32)
    for route_col in range(route_count):
        matches = slot_ids[:, route_col, None] == slot_iota[None, :]
        weighted = weighted + jnp.where(matches, gates[:, route_col, None], 0.0)
        slot_hits = slot_hits + matches.astype(jnp.float32)
    weight_map = weighted.astype(jnp.bfloat16)
    picker = slot_hits.astype(jnp.bfloat16)
    tok_slots = (
        lax.dot_general(picker, tokens, pick_dims, preferred_element_type=jnp.float32)
        .astype(jnp.bfloat16)
        .reshape(groups, capacity, -1)
    )
    grad_slots = (
        lax.dot_general(picker, grad_out, pick_dims, preferred_element_type=jnp.float32)
        .astype(jnp.bfloat16)
        .reshape(groups, capacity, -1)
    )
    w_gate = gate_weight[0]
    w_up = up_weight[0]
    w_down = down_weight[0]
    tok_full = lax.all_to_all(tok_slots, "tensor", split_axis=0, concat_axis=2, tiled=True)
    row_block = lax.all_gather(tok_full[0], "dp", axis=0, tiled=True)
    gate_part = lax.dot_general(row_block, w_gate, contract, preferred_element_type=jnp.float32)
    up_part = lax.dot_general(row_block, w_up, contract, preferred_element_type=jnp.float32)
    projected = jnp.concatenate([gate_part, up_part], axis=1)
    gate_pre = projected[:, :hid_dev]
    up_pre = projected[:, hid_dev:]
    activated, slope_val = silu_parts(gate_pre)
    hidden = (activated * up_pre).astype(jnp.bfloat16)
    row_block = hidden
    expert_out = lax.psum_scatter(
        jnp.dot(row_block, w_down, preferred_element_type=jnp.float32).astype(jnp.bfloat16),
        "dp",
        scatter_dimension=0,
        tiled=True,
    )
    returned = lax.all_to_all(
        expert_out[None], "tensor", split_axis=2, concat_axis=0, tiled=True
    ).reshape(groups * capacity, -1)
    out_part = jnp.dot(weight_map, returned, preferred_element_type=jnp.float32)
    mixed = lax.psum(out_part.astype(jnp.bfloat16), "expert")
    gate_scale = up_pre * slope_val
    grad_own = lax.all_to_all(grad_slots, "tensor", split_axis=0, concat_axis=2, tiled=True)[0]
    grad_hid = lax.dot_general(
        lax.all_gather(grad_own, "dp", axis=0, tiled=True),
        w_down,
        contract,
        preferred_element_type=jnp.float32,
    )
    grad_gate = (grad_hid * gate_scale).astype(jnp.bfloat16)
    grad_up = (grad_hid * activated).astype(jnp.bfloat16)
    grad_joint = jnp.concatenate([grad_gate, grad_up], axis=1)
    stacked = jnp.concatenate([w_gate, w_up], axis=0)
    row_block = grad_joint
    expert_back = lax.psum_scatter(
        jnp.dot(row_block, stacked, preferred_element_type=jnp.float32).astype(jnp.bfloat16),
        "dp",
        scatter_dimension=0,
        tiled=True,
    )
    back_slots = lax.all_to_all(
        expert_back[None], "tensor", split_axis=2, concat_axis=0, tiled=True
    ).reshape(groups * capacity, -1)
    grad_part = jnp.dot(weight_map, back_slots, preferred_element_type=jnp.float32)
    grad_tokens = lax.psum(grad_part.astype(jnp.bfloat16), "expert")
    slot_grads = jnp.sum(expert_out.astype(jnp.float32) * grad_own.astype(jnp.float32), axis=1)
    own_slots = lax.axis_index("tensor") * capacity + jnp.arange(capacity, dtype=jnp.int32)
    columns = []
    for route_col in range(route_count):
        matches = slot_ids[:, route_col, None] == own_slots[None, :]
        columns.append(jnp.sum(jnp.where(matches, slot_grads[None, :], 0.0), axis=1))
    gate_part = jnp.stack(columns, axis=1)
    grad_gates = lax.psum(gate_part, ("expert", "tensor"))
    return (mixed, grad_tokens, grad_gates)


def solution(mesh):
    return jax.shard_map(
        body,
        mesh=mesh,
        in_specs=(
            P("dp", "tensor"),
            P("dp", "tensor"),
            P("dp", None),
            P("dp", None),
            P(("expert", "tensor"), "dp", None),
            P(("expert", "tensor"), "dp", None),
            P(("expert", "tensor"), "dp", None),
        ),
        out_specs=(P("dp", "tensor"), P("dp", "tensor"), P("dp", None)),
        check_vma=False,
    )
```

profile of v0, /device:TPU:0, one launch (start us, length us, event | category | flops | bytes accessed | tf_op | source)
XLA Modules:
  0.0 212.8 jit_solution(12083880330423881430)
XLA Ops:
  7.2 1.0 copy.33
  8.6 1.1 reduce-window.6
  9.7 0.2 slice_reduce_fusion.8
  9.9 0.2 reduce-window.9
  10.3 0.2 fusion.18
  10.5 0.2 select_n.59
  10.6 1.1 slice_reduce_fusion.7
  11.8 2.7 %convolution_convert_fusion.2 = bf16[192,512]{1,0:T(8,128)(2,1)} fusion(bf16[512,512]{1,0:T(8,128)(2,1)} %param.8, s32[512]{0:T(512)S(1)} %get-tuple-element.4, s32[512]{0:T(512)S(1)} %get-tuple-element.5, s32[512]{0:T(512)S(1)} %get-tuple-element.6, s32[512]{0:T(512)S(1)} %get-tuple-element.7, s32[512]{0:T(512)S(1)} %get-tuple-element.8, ...), kind=kOutput, calls=%fused_computation.12 | convolution fusion | flops 103120896 | bytes 737280 | tf_op jit(solution)/shard_map/dot_general | solution.py:45
  14.5 4.2 %all-to-all-start.2 = ((bf16[4,48,512]{2,1,0:T(8,128)(2,1)}), bf16[4,48,512]{2,1,0:T(8,128)(2,1)S(1)}, u32[]{:S(2)}, u32[]{:S(2)}) async-start(bf16[4,48,512]{2,1,0:T(8,128)(2,1)} %bitcast.18), calls=%async_computation.3 | async-start | bytes 393216 | tf_op jit(solution)/shard_map/all_to_all | solution.py:74
  18.7 2.7 %convolution_convert_fusion.3 = bf16[192,512]{1,0:T(8,128)(2,1)} fusion(bf16[512,512]{1,0:T(8,128)(2,1)} %param.7, s32[512]{0:T(512)S(1)} %get-tuple-element.4, s32[512]{0:T(512)S(1)} %get-tuple-element.5, s32[512]{0:T(512)S(1)} %get-tuple-element.6, s32[512]{0:T(512)S(1)} %get-tuple-element.7, s32[512]{0:T(512)S(1)} %get-tuple-element.8, ...), kind=kOutput, calls=%fused_computation.13 | convolution fusion | flops 103120896 | bytes 737280 | tf_op jit(solution)/shard_map/dot_general | solution.py:40
  21.4 2.6 %all-to-all-done.2 = bf16[4,48,512]{2,1,0:T(8,128)(2,1)S(1)} async-done(((bf16[4,48,512]{2,1,0:T(8,128)(2,1)}), bf16[4,48,512]{2,1,0:T(8,128)(2,1)S(1)}, u32[]{:S(2)}, u32[]{:S(2)}) %all-to-all-start.2) | async-done | bytes 196640 | tf_op jit(solution)/shard_map/all_to_all | solution.py:74
  24.1 3.4 %all-to-all-start = ((bf16[4,48,512]{2,1,0:T(8,128)(2,1)}), bf16[4,48,512]{2,1,0:T(8,128)(2,1)S(1)}, u32[]{:S(2)}, u32[]{:S(2)}) async-start(bf16[4,48,512]{2,1,0:T(8,128)(2,1)} %bitcast.90), calls=%async_computation | async-start | bytes 393216 | tf_op jit(solution)/shard_map/all_to_all | solution.py:52
  27.6 0.2 copy.39
  27.8 5.0 %all-to-all-done = bf16[4,48,512]{2,1,0:T(8,128)(2,1)S(1)} async-done(((bf16[4,48,512]{2,1,0:T(8,128)(2,1)}), bf16[4,48,512]{2,1,0:T(8,128)(2,1)S(1)}, u32[]{:S(2)}, u32[]{:S(2)}) %all-to-all-start) | async-done | bytes 196640 | tf_op jit(solution)/shard_map/all_to_all | solution.py:52
  33.0 7.6 %all_gather.6 = bf16[96,2048]{1,0:T(8,128)(2,1)S(1)} all-gather(bf16[48,2048]{1,0:T(8,128)(2,1)S(1)} %bitcast.88), channel_id=1, replica_groups=mesh['dp'=2,'tensor'=4,'expert'=4] {'dp'}, dimensions={0}, use_global_device_ids=true | all-gather | bytes 589824 | tf_op jit(solution)/shard_map/all_gather | solution.py:53
  40.6 3.0 %fusion.23 = f32[96,768]{1,0:T(8,128)S(1)} fusion(bf16[96,2048]{1,0:T(8,128)(2,1)S(1)} %all_gather.6, bf16[1,768,2048]{2,1,0:T(8,128)(2,1)} %param.12), kind=kOutput, calls=%fused_computation.63 | convolution fusion | flops 301989888 | bytes 3833856 | tf_op jit(solution)/shard_map/dot_general | solution.py:55
  43.6 1.1 fusion.25
  44.8 6.7 %all_gather.7 = bf16[96,2048]{1,0:T(8,128)(2,1)S(1)} all-gather(bf16[48,2048]{1,0:T(8,128)(2,1)S(1)} %bitcast.79), channel_id=1, replica_groups=mesh['dp'=2,'tensor'=4,'expert'=4] {'dp'}, dimensions={0}, use_global_device_ids=true | all-gather | bytes 589824 | tf_op jit(solution)/shard_map/all_gather | solution.py:76
  51.4 1.1 multiply_convert_fusion.1
  52.6 2.0 fusion.11
  54.6 0.2 reduce-scatter.3.cloned.1.call-start
  54.8 2.4 %fusion.8 = bf16[96,2048]{1,0:T(8,128)(2,1)} fusion(bf16[1,768,2048]{2,1,0:T(8,128)(2,1)S(1)} %copy-done, f32[96,768]{1,0:T(8,128)} %copy-done.3, f32[96,768]{1,0:T(8,128)} %copy-done.4), kind=kOutput, calls=%fused_computation.8 | convolution fusion | flops 302628864 | bytes 4128768 | tf_op jit(solution)/shard_map/dot_general | solution.py:63
  57.3 11.2 %reduce-scatter.5.cloned.1.call-done = bf16[48,2048]{1,0:T(8,128)(2,1)} async-done(((bf16[96,2048]{1,0:T(8,128)(2,1)}), bf16[48,2048]{1,0:T(8,128)(2,1)}) %reduce-scatter.5.cloned.1.call-update) | async-done | bytes 196624 | tf_op jit(solution)/shard_map/reduce_scatter | solution.py:86
  68.5 3.3 %copy.40 = bf16[1,48,2048]{1,0,2:T(2,128)(2,1)} copy(bf16[1,48,2048]{2,1,0:T(8,128)(2,1)} %bitcast.89) | data formatting | bytes 393216 | tf_op jit(solution)/shard_map/broadcast_in_dim | solution.py:93
  71.8 0.5 broadcast.68
  72.4 13.4 %reduce.19 = bf16[2048,48]{1,0:T(8,128)(2,1)} reduce(bf16[2048,1,48]{2,1,0:T(2,128)(2,1)} %bitcast.75, bf16[]{:T(256)} %broadcast.68), dimensions={1}, to_apply=%bitcast.61.reduce_sub_computation | reduce | bytes 393218
  85.7 2.5 %reshape.79 = bf16[4,2,12288]{2,1,0:T(2,128)(2,1)} reshape(bf16[2048,48]{1,0:T(8,128)(2,1)} %reduce.19) | data formatting | bytes 393216
  88.2 3.6 %all-to-all-start.3 = ((bf16[4,2,12288]{2,1,0:T(2,128)(2,1)}), bf16[4,2,12288]{2,1,0:T(2,128)(2,1)S(1)}, u32[]{:S(2)}, u32[]{:S(2)}) async-start(bf16[4,2,12288]{2,1,0:T(2,128)(2,1)} %reshape.79), calls=%async_computation.5 | async-start | bytes 393216 | tf_op jit(solution)/shard_map/all_to_all | solution.py:92
  91.8 3.3 %copy.36 = bf16[1,48,2048]{1,0,2:T(2,128)(2,1)} copy(bf16[1,48,2048]{2,1,0:T(8,128)(2,1)} %bitcast.81) | data formatting | bytes 393216 | tf_op jit(solution)/shard_map/broadcast_in_dim | solution.py:69
  95.2 13.4 %reduce.18 = bf16[2048,48]{1,0:T(8,128)(2,1)} reduce(bf16[2048,1,48]{2,1,0:T(2,128)(2,1)} %bitcast.76, bf16[]{:T(256)} %broadcast.68), dimensions={1}, to_apply=%bitcast.59.reduce_sub_computation | reduce | bytes 393218
  108.5 2.5 %reshape.77 = bf16[4,2,12288]{2,1,0:T(2,128)(2,1)} reshape(bf16[2048,48]{1,0:T(8,128)(2,1)} %reduce.18) | data formatting | bytes 393216
  111.0 4.0 %all-to-all-start.1 = ((bf16[4,2,12288]{2,1,0:T(2,128)(2,1)}), bf16[4,2,12288]{2,1,0:T(2,128)(2,1)}, u32[]{:S(2)}, u32[]{:S(2)}) async-start(bf16[4,2,12288]{2,1,0:T(2,128)(2,1)} %reshape.77), calls=%async_computation.2 | async-start | bytes 393216 | tf_op jit(solution)/shard_map/all_to_all | solution.py:68
  115.1 0.6 fusion.28
  115.7 2.2 %reshape.80 = bf16[2048,1,48]{2,1,0:T(2,128)(2,1)} reshape(bf16[4,2,12288]{2,1,0:T(2,128)(2,1)S(1)} %all-to-all-done.3) | data formatting | bytes 393216
  117.9 2.3 %copy.41 = bf16[1,48,2048]{2,1,0:T(8,128)(2,1)S(1)} copy(bf16[1,48,2048]{1,0,2:T(2,128)(2,1)} %bitcast.73) | data formatting | bytes 393216 | tf_op jit(solution)/shard_map/all_to_all | solution.py:92
  120.2 0.8 all_to_all.54
  121.0 1.6 copy.42
  122.6 3.5 %reshape.78 = bf16[2048,1,48]{2,1,0:T(2,128)(2,1)} reshape(bf16[4,2,12288]{2,1,0:T(2,128)(2,1)} %all-to-all-done.1) | data formatting | bytes 393216
  126.1 2.3 %copy.37 = bf16[1,48,2048]{2,1,0:T(8,128)(2,1)S(1)} copy(bf16[1,48,2048]{1,0,2:T(2,128)(2,1)} %bitcast.74) | data formatting | bytes 393216 | tf_op jit(solution)/shard_map/all_to_all | solution.py:68
  128.4 0.8 all_to_all.48
  129.2 1.0 copy.38
  130.2 4.0 %convolution_convert_fusion = bf16[512,512]{1,0:T(8,128)(2,1)} fusion(bf16[192,512]{1,0:T(8,128)(2,1)} %bitcast.91, f32[512]{0:T(512)} %bitcast.114, s32[512]{0:T(512)S(1)} %copy-done.10, f32[512]{0:T(512)} %bitcast.116, s32[512]{0:T(512)S(1)} %copy-done.12, f32[512]{0:T(512)} %bitcast.104, s32[512]{0:T(512)S(1)} %copy-done.14, f32[512]{0:T(512)} %bitcast.106, ...), kind=kOutput, calls=%fused_computation.10 | convolution fusion | flops 103284736 | bytes 753664 | tf_op jit(solution)/shard_map/dot_general | solution.py:95
  134.2 3.7 %convolution_convert_fusion.1 = bf16[512,512]{1,0:T(8,128)(2,1)} fusion(bf16[192,512]{1,0:T(8,128)(2,1)S(1)} %bitcast.92, f32[512]{0:T(512)} %bitcast.115, s32[512]{0:T(512)S(1)} %copy-done.10, f32[512]{0:T(512)} %bitcast.117, s32[512]{0:T(512)S(1)} %copy-done.12, f32[512]{0:T(512)} %bitcast.105, s32[512]{0:T(512)S(1)} %copy-done.14, f32[512]{0:T(512)} %bitcast.107, ...), kind=kOutput, calls=%fused_computation.11 | convolution fusion | flops 103284736 | bytes 753664 | tf_op jit(solution)/shard_map/dot_general | solution.py:71
  137.9 0.2 multiply_reduce_fusion
  138.1 0.9 select_reduce_fusion
  139.0 63.5 %psum.23 = f32[512,8]{0,1:T(8,128)} all-reduce(f32[512,8]{0,1:T(8,128)S(1)} %stack.35), channel_id=1, replica_groups=mesh['dp'=2,'tensor'=4,'expert'=4] {'expert','tensor'}, use_global_device_ids=true, to_apply=%region_18.19 | all-reduce | flops 4096 | bytes 32768 | tf_op jit(solution)/shard_map/psum | solution.py:104
  202.5 1.9 copy.49
  204.4 1.9 copy.50
  (58 shorter events, 1.0 us)
Async XLA Ops:
  7.2 44.3 %copy-start = (bf16[1,768,2048]{2,1,0:T(8,128)(2,1)S(1)}, bf16[1,768,2048]{2,1,0:T(8,128)(2,1)}, u32[]{:S(2)}) copy-start(bf16[1,768,2048]{2,1,0:T(8,128)(2,1)} %param.13) | copy-start | bytes 9437188
  11.8 12.3 %copy-start.7 = (s32[512]{0:T(512)}, s32[512]{0:T(512)S(1)}, u32[]{:S(2)}) copy-start(s32[512]{0:T(512)S(1)} %get-tuple-element.3) | copy-start | bytes 6148
  11.8 12.3 %copy-start.9 = (s32[512]{0:T(512)}, s32[512]{0:T(512)S(1)}, u32[]{:S(2)}) copy-start(s32[512]{0:T(512)S(1)} %get-tuple-element.4) | copy-start | bytes 6148
  11.8 12.3 %copy-start.11 = (s32[512]{0:T(512)}, s32[512]{0:T(512)S(1)}, u32[]{:S(2)}) copy-start(s32[512]{0:T(512)S(1)} %get-tuple-element.5) | copy-start | bytes 6148
  11.8 12.3 %copy-start.13 = (s32[512]{0:T(512)}, s32[512]{0:T(512)S(1)}, u32[]{:S(2)}) copy-start(s32[512]{0:T(512)S(1)} %get-tuple-element.6) | copy-start | bytes 6148
  11.8 12.3 %copy-start.15 = (s32[512]{0:T(512)}, s32[512]{0:T(512)S(1)}, u32[]{:S(2)}) copy-start(s32[512]{0:T(512)S(1)} %get-tuple-element.7) | copy-start | bytes 6148
  11.8 12.3 %copy-start.16 = (s32[512]{0:T(512)}, s32[512]{0:T(512)S(1)}, u32[]{:S(2)}) copy-start(s32[512]{0:T(512)S(1)} %get-tuple-element.8) | copy-start | bytes 6148
  11.8 12.3 %copy-start.17 = (s32[512]{0:T(512)}, s32[512]{0:T(512)S(1)}, u32[]{:S(2)}) copy-start(s32[512]{0:T(512)S(1)} %get-tuple-element.9) | copy-start | bytes 6148
  11.8 12.3 %copy-start.18 = (s32[512]{0:T(512)}, s32[512]{0:T(512)S(1)}, u32[]{:S(2)}) copy-start(s32[512]{0:T(512)S(1)} %get-tuple-element.10) | copy-start | bytes 6148
  14.5 9.5 %all-to-all-start.2 = ((bf16[4,48,512]{2,1,0:T(8,128)(2,1)}), bf16[4,48,512]{2,1,0:T(8,128)(2,1)S(1)}, u32[]{:S(2)}, u32[]{:S(2)}) async-start(bf16[4,48,512]{2,1,0:T(8,128)(2,1)} %bitcast.18), calls=%async_computation.3 | async-start | bytes 393216 | tf_op jit(solution)/shard_map/all_to_all | solution.py:74
  24.1 8.7 %all-to-all-start = ((bf16[4,48,512]{2,1,0:T(8,128)(2,1)}), bf16[4,48,512]{2,1,0:T(8,128)(2,1)S(1)}, u32[]{:S(2)}, u32[]{:S(2)}) async-start(bf16[4,48,512]{2,1,0:T(8,128)(2,1)} %bitcast.90), calls=%async_computation | async-start | bytes 393216 | tf_op jit(solution)/shard_map/all_to_all | solution.py:52
  27.5 41.0 %reduce-scatter.5.cloned.1.call-start = ((), (), s32[]{:S(2)}) async-start(), calls=%async_computation.7 | async-start | bytes 589824 | tf_op jit(solution)/shard_map/reduce_scatter | solution.py:86
  32.8 10.8 %copy-start.2 = (bf16[1,768,2048]{2,1,0:T(8,128)(2,1)S(1)}, bf16[1,768,2048]{2,1,0:T(8,128)(2,1)}, u32[]{:S(2)}) copy-start(bf16[1,768,2048]{2,1,0:T(8,128)(2,1)} %param.11) | copy-start | bytes 9437188
  43.6 8.9 %copy-start.3 = (f32[96,768]{1,0:T(8,128)}, f32[96,768]{1,0:T(8,128)S(1)}, u32[]{:S(2)}) copy-start(f32[96,768]{1,0:T(8,128)S(1)} %fusion.23) | copy-start | bytes 884740
  44.7 7.8 %copy-start.4 = (f32[96,768]{1,0:T(8,128)}, f32[96,768]{1,0:T(8,128)S(1)}, u32[]{:S(2)}) copy-start(f32[96,768]{1,0:T(8,128)S(1)} %fusion.25) | copy-start | bytes 884740
  44.8 7.8 %copy-start.1 = (bf16[1,768,2048]{2,1,0:T(8,128)(2,1)S(1)}, bf16[1,768,2048]{2,1,0:T(8,128)(2,1)}, u32[]{:S(2)}) copy-start(bf16[1,768,2048]{2,1,0:T(8,128)(2,1)} %param.12) | copy-start | bytes 9437188
  54.6 37.2 %reduce-scatter.3.cloned.1.call-start = ((), (), s32[]{:S(2)}) async-start(), calls=%async_computation.6 | async-start | bytes 589824 | tf_op jit(solution)/shard_map/reduce_scatter | solution.py:62
  72.4 42.7 %copy-start.6 = (f32[512,8]{0,1:T(8,128)S(1)}, f32[512,8]{0,1:T(8,128)}, u32[]{:S(2)}) copy-start(f32[512,8]{0,1:T(8,128)} %param.10) | copy-start | bytes 49156
  88.2 22.8 %all-to-all-start.3 = ((bf16[4,2,12288]{2,1,0:T(2,128)(2,1)}), bf16[4,2,12288]{2,1,0:T(2,128)(2,1)S(1)}, u32[]{:S(2)}, u32[]{:S(2)}) async-start(bf16[4,2,12288]{2,1,0:T(2,128)(2,1)} %reshape.79), calls=%async_computation.5 | async-start | bytes 393216 | tf_op jit(solution)/shard_map/all_to_all | solution.py:92
  111.0 11.6 %all-to-all-start.1 = ((bf16[4,2,12288]{2,1,0:T(2,128)(2,1)}), bf16[4,2,12288]{2,1,0:T(2,128)(2,1)}, u32[]{:S(2)}, u32[]{:S(2)}) async-start(bf16[4,2,12288]{2,1,0:T(2,128)(2,1)} %reshape.77), calls=%async_computation.2 | async-start | bytes 393216 | tf_op jit(solution)/shard_map/all_to_all | solution.py:68
  115.0 87.5 %all-reduce.3.cloned.1.call-start = ((), (), s32[]{:S(2)}) async-start(), calls=%async_computation.8 | async-start | bytes 2097152 | tf_op jit(solution)/shard_map/psum | solution.py:72
  115.7 14.4 %copy-start.8 = (s32[512]{0:T(512)S(1)}, s32[512]{0:T(512)}, u32[]{:S(2)}) copy-start(s32[512]{0:T(512)} %copy-done.7) | copy-start | bytes 6148
  115.7 14.5 %copy-start.10 = (s32[512]{0:T(512)S(1)}, s32[512]{0:T(512)}, u32[]{:S(2)}) copy-start(s32[512]{0:T(512)} %copy-done.9) | copy-start | bytes 6148
  115.7 14.5 %copy-start.12 = (s32[512]{0:T(512)S(1)}, s32[512]{0:T(512)}, u32[]{:S(2)}) copy-start(s32[512]{0:T(512)} %copy-done.11) | copy-start | bytes 6148
  115.7 14.5 %copy-start.14 = (s32[512]{0:T(512)S(1)}, s32[512]{0:T(512)}, u32[]{:S(2)}) copy-start(s32[512]{0:T(512)} %copy-done.13) | copy-start | bytes 6148
  134.2 3.7 %copy-start.5 = (bf16[48,2048]{1,0:T(8,128)(2,1)S(1)}, bf16[48,2048]{1,0:T(8,128)(2,1)}, u32[]{:S(2)}) copy-start(bf16[48,2048]{1,0:T(8,128)(2,1)} %reduce-scatter.3.cloned.1.call-done) | copy-start | bytes 589828
Sparse Core Ops, SparseCore 0:
  54.7 13.7 reduce-scatter.4
  71.4 13.1 reduce-scatter.2
  138.0 53.4 all-reduce.2
where the time goes:
time: 215 us; the launch traced here: 213 us
  blocking collectives  77.8 us (36%)
  local copies, waits for them, and re-layouts  34.2 us (16%)
  other arithmetic  29.5 us (14%)
  matrix products  22.7 us (11%)
  waiting for transfers between devices  19 us (9%)
  starting transfers between devices  15.5 us (7%)
  between operations  14.2 us (7%)
    psum x1, blocking collectives, body(): grad_gates = lax.psum(gate_part, ('expert', 'tensor'))  63.5 us
    unnamed x3, other arithmetic  26.8 us
    unnamed x48, local copies, waits for them, and re-layouts  16 us
    reduce_scatter x1, waiting for transfers between devices, body(): lax.psum_scatter(jnp.dot(row_block, stacked, preferred_element_type=jnp.f...  11.2 us
    all_gather x1, blocking collectives, body(): row_block = lax.all_gather(tok_full[0], 'dp', axis=0, tiled=True)  7.59 us
    all_gather x1, blocking collectives, body(): lax.all_gather(grad_own, 'dp', axis=0, tiled=True)  6.67 us
    all_to_all x1, waiting for transfers between devices, body(): lax.all_to_all(tok_slots, 'tensor', split_axis=0, concat_axis=2, tiled=True)  5.04 us
    all_to_all x3, local copies, waits for them, and re-layouts, body(): lax.all_to_all(expert_back[None], 'tensor', split_axis=2, concat_axis=0,...  4.72 us
  transfers between devices with their start and end apart: 7, of which 3 were waited for; matrix products, arithmetic and copies ran while one was open for 24% of the time, Pallas kernels for 0%

commit v1 on v0

v1 whole, which is shorter than its diff:
```python
import functools

import jax
import jax.numpy as jnp
from jax import lax
from jax.experimental import pallas as pl
from jax.experimental.pallas import tpu as pltpu
from jax.sharding import PartitionSpec as P

CAP = 48
LANES = 128
BF16 = jnp.bfloat16
F32 = jnp.float32
CONTRACT_LAST = (((1,), (1,)), ((), ()))


def vmem():
    return pl.BlockSpec(memory_space=pltpu.VMEM)


def cost(flops, moved):
    return pl.CostEstimate(flops=int(flops), bytes_accessed=int(moved), transcendentals=0)


def pick_rows(key_ref, source_ref, piece_refs):
    groups = len(piece_refs)
    rows = source_ref.shape[0]
    t, e = lax.axis_index("tensor"), lax.axis_index("expert")
    slot = lax.broadcasted_iota(jnp.int32, (CAP, rows), 0).astype(F32)
    masks = []
    for dt in range(groups):
        expert = e * groups + lax.rem(t + dt, groups)
        masks.append((key_ref[pl.ds(expert, 1), :] == slot).astype(BF16))
    picked = jnp.dot(jnp.concatenate(masks, axis=0), source_ref[...], preferred_element_type=F32).astype(BF16)
    for dt in range(groups):
        piece_refs[dt][...] = picked[dt * CAP : (dt + 1) * CAP]


def number_kernel(routes_ref, tokens_ref, key_ref, *piece_refs):
    experts, rows = key_ref.shape
    ids = lax.broadcasted_iota(jnp.int32, (experts, rows), 0)
    hit = jnp.zeros((experts, rows), F32)
    for r in range(routes_ref.shape[0]):
        hit = hit + (routes_ref[r : r + 1, :] == ids).astype(F32)
    before = (
        lax.broadcasted_iota(jnp.int32, (LANES, LANES), 0) < lax.broadcasted_iota(jnp.int32, (LANES, LANES), 1)
    ).astype(BF16)
    offset = jnp.zeros((experts, 1), F32)
    for start in range(0, rows, LANES):
        part = hit[:, start : start + LANES]
        rank = jnp.dot(part.astype(BF16), before, preferred_element_type=F32) + offset
        offset = offset + jnp.sum(part, axis=1, keepdims=True)
        key_ref[:, start : start + LANES] = jnp.where(part > 0.0, rank, -1.0)
    pick_rows(key_ref, tokens_ref, piece_refs)


def pick_kernel(key_ref, source_ref, *piece_refs):
    pick_rows(key_ref, source_ref, piece_refs)


def gather_pieces(x_ref, piece_refs, groups):
    t = lax.axis_index("tensor")
    width = piece_refs[0].shape[1]
    for index, piece in enumerate(piece_refs):
        db, dt = divmod(index, groups)
        owner = lax.rem(t - dt + groups, groups)
        x_ref[db * CAP : (db + 1) * CAP, pl.ds(pl.multiple_of(owner * width, width), width)] = piece[...]


def scatter_pieces(y_ref, piece_refs, groups):
    t = lax.axis_index("tensor")
    blocks = len(piece_refs) // groups
    width = piece_refs[0].shape[1]
    for index, piece in enumerate(piece_refs):
        db, dt = divmod(index, groups)
        row = (-db) % blocks * CAP
        owner = lax.rem(t + dt, groups)
        piece[...] = y_ref[row : row + CAP, pl.ds(pl.multiple_of(owner * width, width), width)].astype(BF16)


def forward_kernel(groups, count, *refs):
    pieces, (gate_ref, up_ref, down_ref) = refs[:count], refs[count : count + 3]
    act_ref, scale_ref, hid_ref = refs[count + 3 : count + 6]
    outs, (x_ref, y_ref) = refs[count + 6 : 2 * count + 6], refs[2 * count + 6 :]
    step = pl.program_id(0)

    @pl.when(step == 0)
    def _():
        gather_pieces(x_ref, pieces, groups)
        y_ref[...] = jnp.zeros_like(y_ref)

    gate_pre = lax.dot_general(x_ref[...], gate_ref[0], CONTRACT_LAST, preferred_element_type=F32)
    up_pre = lax.dot_general(x_ref[...], up_ref[0], CONTRACT_LAST, preferred_element_type=F32)
    sig = jax.nn.sigmoid(gate_pre)
    act = gate_pre * sig
    hidden = (act * up_pre).astype(BF16)
    act_ref[...] = act
    scale_ref[...] = up_pre * (sig * (1.0 + gate_pre * (1.0 - sig)))
    hid_ref[...] = hidden
    y_ref[...] += jnp.dot(hidden, down_ref[0], preferred_element_type=F32)

    @pl.when(step == pl.num_programs(0) - 1)
    def _():
        scatter_pieces(y_ref, outs, groups)


def backward_kernel(groups, count, *refs):
    pieces, (gate_ref, up_ref, down_ref) = refs[:count], refs[count : count + 3]
    act_ref, scale_ref, hid_ref = refs[count + 3 : count + 6]
    outs, sum_ref = refs[count + 6 : 2 * count + 6], refs[2 * count + 6]
    x_ref, y_ref = refs[2 * count + 7 :]
    step = pl.program_id(0)

    @pl.when(step == 0)
    def _():
        gather_pieces(x_ref, pieces, groups)
        y_ref[...] = jnp.zeros_like(y_ref)
        sum_ref[...] = jnp.zeros_like(sum_ref)

    grad_hid = lax.dot_general(x_ref[...], down_ref[0], CONTRACT_LAST, preferred_element_type=F32)
    grad_gate = (grad_hid * scale_ref[...]).astype(BF16)
    grad_up = (grad_hid * act_ref[...]).astype(BF16)
    sum_ref[...] += lax.dot_general(
        jnp.ones((sum_ref.shape[0], grad_hid.shape[1]), F32),
        grad_hid * hid_ref[...].astype(F32),
        CONTRACT_LAST,
        preferred_element_type=F32,
        precision=lax.Precision.HIGHEST,
    )
    y_ref[...] += jnp.dot(grad_gate, gate_ref[0], preferred_element_type=F32) + jnp.dot(
        grad_up, up_ref[0], preferred_element_type=F32
    )

    @pl.when(step == pl.num_programs(0) - 1)
    def _():
        scatter_pieces(y_ref, outs, groups)


def add_blocks_kernel(groups, *refs):
    pieces, out_ref = refs[:-1], refs[-1]
    for dt in range(groups):
        total = pieces[dt][...].astype(F32)
        for piece in pieces[groups + dt :: groups]:
            total = total + piece[...].astype(F32)
        out_ref[dt * CAP : (dt + 1) * CAP, :] = total.astype(BF16)


def weights_kernel(groups, columns, routes_ref, gates_ref, key_ref, out_ref, gate_ref):
    experts, rows = key_ref.shape
    t, e = lax.axis_index("tensor"), lax.axis_index("expert")
    ids = lax.broadcasted_iota(jnp.int32, (experts, rows), 0)
    gate = jnp.zeros((experts, rows), F32)
    for r in range(routes_ref.shape[0]):
        gate = gate + jnp.where(routes_ref[r : r + 1, :] == ids, gates_ref[r : r + 1, :], 0.0)
    gate_ref[...] = gate
    slot = lax.broadcasted_iota(jnp.int32, (CAP, rows), 0).astype(F32)
    for dz in range(columns):
        blocks = []
        for dt in range(groups):
            expert = lax.rem(e - dz + columns, columns) * groups + lax.rem(t - dt + groups, groups)
            same = key_ref[pl.ds(expert, 1), :] == slot
            blocks.append(jnp.where(same, gate_ref[pl.ds(expert, 1), :], 0.0))
        width = groups * CAP
        out_ref[dz * width : (dz + 1) * width, :] = jnp.concatenate(blocks, axis=0).astype(BF16)


def combine_kernel(weight_ref, *refs):
    parts, out_ref, all_ref = refs[:-2], refs[-2], refs[-1]
    height = parts[0].shape[0]
    for index, part in enumerate(parts):
        all_ref[index * height : (index + 1) * height, :] = part[...]
    out_ref[...] = lax.dot_general(
        weight_ref[...], all_ref[...], (((0,), (0,)), ((), ())), preferred_element_type=F32
    ).astype(BF16)


def gate_grad_kernel(routes_ref, key_ref, sums_ref, out_ref):
    experts, rows = key_ref.shape
    slot = lax.broadcasted_iota(jnp.int32, (CAP, rows), 0).astype(F32)
    total = jnp.zeros(out_ref.shape, F32)
    routes = routes_ref[...]
    for expert in range(experts):
        same = key_ref[expert : expert + 1, :] == slot
        row = jnp.sum(jnp.where(same, sums_ref[:, expert : expert + 1], 0.0), axis=0, keepdims=True)
        total = total + jnp.where(routes == expert, row, 0.0)
    out_ref[...] = total


def body(sizes, tokens, grad_out, routes, gates, gate_weight, up_weight, down_weight):
    n_dp, groups, columns = sizes
    experts = groups * columns
    rows, width = tokens.shape
    _, hid_dev, feats = gate_weight.shape
    count = n_dp * groups
    tall = n_dp * CAP
    chunk = 256 if hid_dev % 256 == 0 else hid_dev
    routes_t, gates_t = routes.T, gates.T

    piece = jax.ShapeDtypeStruct((CAP, width), BF16)
    key, *tok_pieces = pl.pallas_call(
        number_kernel,
        out_shape=[jax.ShapeDtypeStruct((experts, rows), F32)] + [piece] * groups,
        in_specs=[vmem()] * 2,
        out_specs=[vmem()] * (groups + 1),
        cost_estimate=cost(2 * groups * CAP * rows * width, 2 * rows * width),
        name="number",
    )(routes_t, tokens)
    grad_pieces = pl.pallas_call(
        pick_kernel,
        out_shape=[piece] * groups,
        in_specs=[vmem()] * 2,
        out_specs=[vmem()] * groups,
        cost_estimate=cost(2 * groups * CAP * rows * width, 2 * rows * width),
        name="pick",
    )(key, grad_out)

    def shift(value, db, dt):
        if (db, dt) == (0, 0):
            return value
        pairs = []
        for b in range(n_dp):
            for t in range(groups):
                pairs.append((b * groups + t, (b + db) % n_dp * groups + (t + dt) % groups))
        return lax.ppermute(value, ("dp", "tensor"), pairs)

    def spread(pieces):
        return [shift(pieces[dt], db, dt) for db in range(n_dp) for dt in range(groups)]

    def exchange(pieces):
        return [shift(pieces[db * groups + dt], db, dt) for db in range(n_dp) for dt in range(groups)]

    def whole_block(shape):
        return pl.BlockSpec(shape, lambda i: (0,) * len(shape))

    weight_block = pl.BlockSpec((1, chunk, feats), lambda i: (0, i, 0))
    hidden_block = pl.BlockSpec((tall, chunk), lambda i: (0, i))
    piece_block = whole_block((CAP, width))
    scratch = [pltpu.VMEM((tall, feats), BF16), pltpu.VMEM((tall, feats), F32)]
    matmul_flops = 2 * tall * hid_dev * feats

    tok_in = spread(tok_pieces)
    grad_in = spread(grad_pieces)
    act, scale, hidden, *outs = pl.pallas_call(
        functools.partial(forward_kernel, groups, count),
        grid=(hid_dev // chunk,),
        out_shape=[
            jax.ShapeDtypeStruct((tall, hid_dev), F32),
            jax.ShapeDtypeStruct((tall, hid_dev), F32),
            jax.ShapeDtypeStruct((tall, hid_dev), BF16),
        ]
        + [piece] * count,
        in_specs=[piece_block] * count + [weight_block] * 3,
        out_specs=[hidden_block] * 3 + [piece_block] * count,
        scratch_shapes=scratch,
        cost_estimate=cost(3 * matmul_flops, 6 * hid_dev * feats),
        name="forward",
    )(*tok_in, gate_weight, up_weight, down_weight)
    out_in = exchange(outs)
    *backs, sums = pl.pallas_call(
        functools.partial(backward_kernel, groups, count),
        grid=(hid_dev // chunk,),
        out_shape=[piece] * count + [jax.ShapeDtypeStruct((8, tall), F32)],
        in_specs=[piece_block] * count + [weight_block] * 3 + [hidden_block] * 3,
        out_specs=[piece_block] * count + [whole_block((8, tall))],
        scratch_shapes=scratch,
        cost_estimate=cost(3 * matmul_flops, 6 * hid_dev * feats),
        name="backward",
    )(*grad_in, gate_weight, up_weight, down_weight, act, scale, hidden)
    back_in = exchange(backs)

    weight_map = pl.pallas_call(
        functools.partial(weights_kernel, groups, columns),
        out_shape=jax.ShapeDtypeStruct((experts * CAP, rows), BF16),
        in_specs=[vmem()] * 3,
        out_specs=vmem(),
        scratch_shapes=[pltpu.VMEM((experts, rows), F32)],
        cost_estimate=cost(experts * CAP * rows, 2 * experts * CAP * rows),
        name="weights",
    )(routes_t, gates_t, key)

    def add_blocks(pieces):
        return pl.pallas_call(
            functools.partial(add_blocks_kernel, groups),
            out_shape=jax.ShapeDtypeStruct((groups * CAP, width), BF16),
            in_specs=[vmem()] * count,
            out_specs=vmem(),
            cost_estimate=cost(count * CAP * width, 4 * count * CAP * width),
            name="add_blocks",
        )(*pieces)

    def across(value):
        parts = [value]
        for dz in range(1, columns):
            parts.append(lax.ppermute(value, "expert", [(z, (z + dz) % columns) for z in range(columns)]))
        return parts

    def combine(parts):
        return pl.pallas_call(
            combine_kernel,
            out_shape=jax.ShapeDtypeStruct((rows, width), BF16),
            in_specs=[vmem()] * (columns + 1),
            out_specs=vmem(),
            scratch_shapes=[pltpu.VMEM((experts * CAP, width), BF16)],
            cost_estimate=cost(2 * experts * CAP * rows * width, 2 * experts * CAP * (rows + width)),
            name="combine",
        )(weight_map, *parts)

    mixed_parts = across(add_blocks(out_in))
    back_parts = across(add_blocks(back_in))
    mixed = combine(mixed_parts)
    grad_tokens = combine(back_parts)

    own = sums[0, :CAP]
    for db in range(1, n_dp):
        row = (-db) % n_dp * CAP
        own = own + lax.ppermute(sums[0, row : row + CAP], "dp", [(b, (b + db) % n_dp) for b in range(n_dp)])
    sums_all = lax.all_gather(own, ("expert", "tensor"), axis=0, tiled=False)
    grad_gates = pl.pallas_call(
        gate_grad_kernel,
        out_shape=jax.ShapeDtypeStruct(routes_t.shape, F32),
        in_specs=[vmem()] * 3,
        out_specs=vmem(),
        cost_estimate=cost(experts * CAP * rows, experts * CAP * rows),
        name="gate_grad",
    )(routes_t, key, sums_all.T)
    return (mixed, grad_tokens, grad_gates.T)


def solution(mesh):
    sizes = (mesh.shape["dp"], mesh.shape["tensor"], mesh.shape["expert"])
    return jax.shard_map(
        functools.partial(body, sizes),
        mesh=mesh,
        in_specs=(
            P("dp", "tensor"),
            P("dp", "tensor"),
            P("dp", None),
            P("dp", None),
            P(("expert", "tensor"), "dp", None),
            P(("expert", "tensor"), "dp", None),
            P(("expert", "tensor"), "dp", None),
        ),
        out_specs=(P("dp", "tensor"), P("dp", "tensor"), P("dp", None)),
        check_vma=False,
    )
```

time: 215 us -> 123 us (0.57)
  blocking collectives: 77.8 us -> 39.9 us
  Pallas kernels: 0 us -> 32 us
  other arithmetic: 29.5 us -> 0.77 us
  local copies, waits for them, and re-layouts: 34.2 us -> 6.67 us
  starting transfers between devices: 15.5 us -> 40.7 us
  matrix products: 22.7 us -> 0 us
  waiting for transfers between devices: 19 us -> 0.21 us
  between operations: 14.2 us -> 1.68 us
    psum x1 -> x0, blocking collectives: 63.5 us -> none  [body(): grad_gates = lax.psum(gate_part, ('expert', 'tensor'))]
    ppermute x0 -> x35, starting transfers between devices: none -> 40.7 us  [the longest x28 29.8 us: shift(): return lax.ppermute(value, ('dp', 'tensor'), pairs)]
    unnamed x0 -> x1, blocking collectives: none -> 39.9 us
    pallas_call x0 -> x10, Pallas kernels: none -> 32 us  [the longest x1 8.12 us: body(): pl.pallas_call(functools.partial(backward_kernel, groups, count), grid=(h...]
    unnamed x3 -> x1, other arithmetic: 26.8 us -> 0.77 us
    dot_general x9 -> x0, matrix products: 22.7 us -> none  [the longest x1 3.97 us: body(): jnp.dot(weight_map, back_slots, preferred_element_type=jnp.float32)]
    all_to_all x4 -> x0, starting transfers between devices: 15.2 us -> none  [the longest x1 4.21 us: body(): lax.all_to_all(grad_slots, 'tensor', split_axis=0, concat_axis=2, tiled=T...]
    all_gather x2 -> x0, blocking collectives: 14.3 us -> none  [the longest x1 7.59 us: body(): row_block = lax.all_gather(tok_full[0], 'dp', axis=0, tiled=True)]
  transfers between devices with their start and end apart: 7 -> 35, of which waited for: 3 -> 1; matrix products, arithmetic and copies ran while one was open for 24% -> 2% of each run, Pallas kernels for 0% -> 16%
where the time goes in v1:
time: 123 us; the launch traced here: 122 us
  starting transfers between devices  40.7 us (33%)
  blocking collectives  39.9 us (32%)
  Pallas kernels  32 us (26%)
  local copies, waits for them, and re-layouts  6.67 us (5%)
  between operations  1.68 us (1%)
    unnamed x1, blocking collectives  39.9 us
    ppermute x28, starting transfers between devices, shift(): return lax.ppermute(value, ('dp', 'tensor'), pairs)  29.8 us
    ppermute x6, starting transfers between devices, across(): lax.ppermute(value, 'expert', [(z, (z + dz) % columns) for z in range(col...  9.42 us
    pallas_call x1, Pallas kernels, body(): pl.pallas_call(functools.partial(backward_kernel, groups, count), grid=(h...  8.12 us
    pallas_call x1, Pallas kernels, body(): pl.pallas_call(functools.partial(forward_kernel, groups, count), grid=(hi...  7.21 us
    pallas_call x2, Pallas kernels, combine(): pl.pallas_call(combine_kernel, out_shape=jax.ShapeDtypeStruct((rows, widt...  5.63 us
    unnamed x86, local copies, waits for them, and re-layouts  5.15 us
    pallas_call x2, Pallas kernels, add_blocks(): pl.pallas_call(functools.partial(add_blocks_kernel, groups), out_shape=ja...  3.4 us
  transfers between devices with their start and end apart: 35, of which 1 were waited for; matrix products, arithmetic and copies ran while one was open for 2% of the time, Pallas kernels for 16%

profile of v1, /device:TPU:0, one launch (start us, length us, event | category | flops | bytes accessed | tf_op | source)
XLA Modules:
  0.0 121.9 jit_solution(15465470324187362178)
XLA Ops:
  0.6 2.1 %number.1 = (f32[16,512]{1,0:T(8,128)}, bf16[48,512]{1,0:T(8,128)(2,1)}, bf16[48,512]{1,0:T(8,128)(2,1)}, bf16[48,512]{1,0:T(8,128)(2,1)}, bf16[48,512]{1,0:T(8,128)(2,1)}) custom-call(s32[8,512]{1,0:T(8,128)} %bitcast.11, bf16[512,512]{1,0:T(8,128)(2,1)} %tokens_ref.1), custom_call_target="tpu_custom_call" | custom-call | flops 100663296 | bytes 524288 | tf_op jit(solution)/shard_map/number/pallas_call | solution.py:200
  2.7 0.5 collective-permute-start
  3.2 2.5 %collective-permute-start.1 = (bf16[48,512]{1,0:T(8,128)(2,1)}, bf16[48,512]{1,0:T(8,128)(2,1)S(1)}, u32[]{:S(2)}, u32[]{:S(2)}) collective-permute-start(bf16[48,512]{1,0:T(8,128)(2,1)} %get-tuple-element.35), channel_id=1, source_target_pairs={{0,8},{4,12},{8,0},{12,4},{16,24},{20,28},{24,16},{28,20},{1,9},{5... | collective-permute-start | bytes 147464 | tf_op jit(solution)/shard_map/ppermute | solution.py:224
  5.7 1.4 %collective-permute-start.2 = (bf16[48,512]{1,0:T(8,128)(2,1)}, bf16[48,512]{1,0:T(8,128)(2,1)S(1)}, u32[]{:S(2)}, u32[]{:S(2)}) collective-permute-start(bf16[48,512]{1,0:T(8,128)(2,1)} %get-tuple-element.36), channel_id=1, source_target_pairs={{0,12},{4,0},{8,4},{12,8},{16,28},{20,16},{24,20},{28,24},{1,13},{... | collective-permute-start | bytes 147464 | tf_op jit(solution)/shard_map/ppermute | solution.py:224
  7.1 1.5 %collective-permute-start.3 = (bf16[48,512]{1,0:T(8,128)(2,1)}, bf16[48,512]{1,0:T(8,128)(2,1)S(1)}, u32[]{:S(2)}, u32[]{:S(2)}) collective-permute-start(bf16[48,512]{1,0:T(8,128)(2,1)} %get-tuple-element.33.refs_0_), channel_id=1, source_target_pairs={{0,16},{4,20},{8,24},{12,28},{16,0},{20,4},{24,8},{28,12},{1,17},{... | collective-permute-start | bytes 147464 | tf_op jit(solution)/shard_map/ppermute | solution.py:224
  8.6 2.0 %pick.1 = (bf16[48,512]{1,0:T(8,128)(2,1)}, bf16[48,512]{1,0:T(8,128)(2,1)}, bf16[48,512]{1,0:T(8,128)(2,1)}, bf16[48,512]{1,0:T(8,128)(2,1)}) custom-call(f32[16,512]{1,0:T(8,128)} %get-tuple-element.32.key_ref, bf16[512,512]{1,0:T(8,128)(2,1)} %source_ref.1), custom_call_target="tpu_custom_call" | custom-call | flops 100663296 | bytes 524288 | tf_op jit(solution)/shard_map/pick/pallas_call | solution.py:208
  10.6 1.2 %collective-permute-start.5 = (bf16[48,512]{1,0:T(8,128)(2,1)}, bf16[48,512]{1,0:T(8,128)(2,1)S(1)}, u32[]{:S(2)}, u32[]{:S(2)}) collective-permute-start(bf16[48,512]{1,0:T(8,128)(2,1)} %get-tuple-element.35), channel_id=1, source_target_pairs={{0,24},{4,28},{8,16},{12,20},{16,8},{20,12},{24,0},{28,4},{1,25},{... | collective-permute-start | bytes 147464 | tf_op jit(solution)/shard_map/ppermute | solution.py:224
  11.9 1.5 %collective-permute-start.6 = (bf16[48,512]{1,0:T(8,128)(2,1)}, bf16[48,512]{1,0:T(8,128)(2,1)S(1)}, u32[]{:S(2)}, u32[]{:S(2)}) collective-permute-start(bf16[48,512]{1,0:T(8,128)(2,1)} %get-tuple-element.36), channel_id=1, source_target_pairs={{0,28},{4,16},{8,20},{12,24},{16,12},{20,0},{24,4},{28,8},{1,29},{... | collective-permute-start | bytes 147464 | tf_op jit(solution)/shard_map/ppermute | solution.py:224
  13.5 1.6 %collective-permute-start.18 = (bf16[48,512]{1,0:T(8,128)(2,1)}, bf16[48,512]{1,0:T(8,128)(2,1)S(1)}, u32[]{:S(2)}, u32[]{:S(2)}) collective-permute-start(bf16[48,512]{1,0:T(8,128)(2,1)} %get-tuple-element.47), channel_id=1, source_target_pairs={{0,8},{4,12},{8,0},{12,4},{16,24},{20,28},{24,16},{28,20},{1,9},{5... | collective-permute-start | bytes 147464 | tf_op jit(solution)/shard_map/ppermute | solution.py:224
  15.1 1.4 %collective-permute-start.21 = (bf16[48,512]{1,0:T(8,128)(2,1)}, bf16[48,512]{1,0:T(8,128)(2,1)S(1)}, u32[]{:S(2)}, u32[]{:S(2)}) collective-permute-start(bf16[48,512]{1,0:T(8,128)(2,1)} %get-tuple-element.46), channel_id=1, source_target_pairs={{0,20},{4,24},{8,28},{12,16},{16,4},{20,8},{24,12},{28,0},{1,21},{... | collective-permute-start | bytes 147464 | tf_op jit(solution)/shard_map/ppermute | solution.py:224
  16.5 1.4 %collective-permute-start.22 = (bf16[48,512]{1,0:T(8,128)(2,1)}, bf16[48,512]{1,0:T(8,128)(2,1)S(1)}, u32[]{:S(2)}, u32[]{:S(2)}) collective-permute-start(bf16[48,512]{1,0:T(8,128)(2,1)} %get-tuple-element.47), channel_id=1, source_target_pairs={{0,24},{4,28},{8,16},{12,20},{16,8},{20,12},{24,0},{28,4},{1,25},{... | collective-permute-start | bytes 147464 | tf_op jit(solution)/shard_map/ppermute | solution.py:224
  18.2 1.4 %collective-permute-start.23 = (bf16[48,512]{1,0:T(8,128)(2,1)}, bf16[48,512]{1,0:T(8,128)(2,1)S(1)}, u32[]{:S(2)}, u32[]{:S(2)}) collective-permute-start(bf16[48,512]{1,0:T(8,128)(2,1)} %get-tuple-element.48), channel_id=1, source_target_pairs={{0,28},{4,16},{8,20},{12,24},{16,12},{20,0},{24,4},{28,8},{1,29},{... | collective-permute-start | bytes 147464 | tf_op jit(solution)/shard_map/ppermute | solution.py:224
  19.6 0.6 collective-permute-start.20
  20.2 7.2 %forward.1 = (f32[96,768]{1,0:T(8,128)}, f32[96,768]{1,0:T(8,128)}, bf16[96,768]{1,0:T(8,128)(2,1)}, bf16[48,512]{1,0:T(8,128)(2,1)}, bf16[48,512]{1,0:T(8,128)(...) custom-call(bf16[48,512]{1,0:T(8,128)(2,1)} %get-tuple-element.33.re, ...), custom_call_target="tpu_custom_call" | custom-call | flops 905969664 | bytes 9437184 | tf_op jit(solution)/shard_map/forward/pallas_call | solution.py:243
  27.6 0.5 copy-done.17
  28.2 8.1 %backward.1 = (bf16[48,512]{1,0:T(8,128)(2,1)}, bf16[48,512]{1,0:T(8,128)(2,1)}, bf16[48,512]{1,0:T(8,128)(2,1)}, bf16[48,512]{1,0:T(8,128)(2,1)}, bf16[48,512]{...) custom-call(bf16[48,512]{1,0:T(8,128)(2,1)} %get-tuple-element.45.re, ...), custom_call_target="tpu_custom_call" | custom-call | flops 905969664 | bytes 9437184 | tf_op jit(solution)/shard_map/backward/pallas_call | solution.py:259
  36.4 2.0 %collective-permute-start.25 = (bf16[48,512]{1,0:T(8,128)(2,1)}, bf16[48,512]{1,0:T(8,128)(2,1)S(1)}, u32[]{:S(2)}, u32[]{:S(2)}) collective-permute-start(bf16[48,512]{1,0:T(8,128)(2,1)} %get-tuple-element.54), channel_id=1, source_target_pairs={{0,8},{4,12},{8,0},{12,4},{16,24},{20,28},{24,16},{28,20},{1,9},{5... | collective-permute-start | bytes 147464 | tf_op jit(solution)/shard_map/ppermute | solution.py:224
  38.4 1.1 collective-permute-start.26
  39.5 1.3 %collective-permute-start.27 = (bf16[48,512]{1,0:T(8,128)(2,1)}, bf16[48,512]{1,0:T(8,128)(2,1)S(1)}, u32[]{:S(2)}, u32[]{:S(2)}) collective-permute-start(bf16[48,512]{1,0:T(8,128)(2,1)} %get-tuple-element.56), channel_id=1, source_target_pairs={{0,16},{4,20},{8,24},{12,28},{16,0},{20,4},{24,8},{28,12},{1,17},{... | collective-permute-start | bytes 147464 | tf_op jit(solution)/shard_map/ppermute | solution.py:224
  40.8 1.7 %collective-permute-start.29 = (bf16[48,512]{1,0:T(8,128)(2,1)}, bf16[48,512]{1,0:T(8,128)(2,1)S(1)}, u32[]{:S(2)}, u32[]{:S(2)}) collective-permute-start(bf16[48,512]{1,0:T(8,128)(2,1)} %get-tuple-element.58), channel_id=1, source_target_pairs={{0,24},{4,28},{8,16},{12,20},{16,8},{20,12},{24,0},{28,4},{1,25},{... | collective-permute-start | bytes 147464 | tf_op jit(solution)/shard_map/ppermute | solution.py:224
  42.5 1.2 collective-permute-start.30
  43.7 1.5 %collective-permute-start.10 = (bf16[48,512]{1,0:T(8,128)(2,1)S(1)}, bf16[48,512]{1,0:T(8,128)(2,1)S(1)}, u32[]{:S(2)}, u32[]{:S(2)}) collective-permute-start(bf16[48,512]{1,0:T(8,128)(2,1)S(1)} %copy-done.40), channel_id=1, source_target_pairs={{0,16},{4,20},{8,24},{12,28},{16,0},{20,4},{24,8},{28,12},{1,17},{... | collective-permute-start | bytes 147464 | tf_op jit(solution)/shard_map/ppermute | solution.py:224
  45.5 1.7 %collective-permute-start.12 = (bf16[48,512]{1,0:T(8,128)(2,1)S(1)}, bf16[48,512]{1,0:T(8,128)(2,1)S(1)}, u32[]{:S(2)}, u32[]{:S(2)}) collective-permute-start(bf16[48,512]{1,0:T(8,128)(2,1)S(1)} %copy-done.38), channel_id=1, source_target_pairs={{0,24},{4,28},{8,16},{12,20},{16,8},{20,12},{24,0},{28,4},{1,25},{... | collective-permute-start | bytes 147464 | tf_op jit(solution)/shard_map/ppermute | solution.py:224
  47.1 1.9 %weights.1.weight_ref = bf16[768,512]{1,0:T(8,128)(2,1)} custom-call(s32[8,512]{1,0:T(8,128)} %bitcast.12, f32[8,512]{1,0:T(8,128)} %bitcast.16, f32[16,512]{1,0:T(8,128)} %get-tuple-element.32.key_ref), custom_call_target="tpu_custom_call" | custom-call | flops 393216 | bytes 786432 | tf_op jit(solution)/shard_map/weights/pallas_call | solution.py:271
  49.0 0.6 dynamic-slice
  50.3 2.4 %collective-permute-start.13 = (bf16[48,512]{1,0:T(8,128)(2,1)S(1)}, bf16[48,512]{1,0:T(8,128)(2,1)S(1)}, u32[]{:S(2)}, u32[]{:S(2)}) collective-permute-start(bf16[48,512]{1,0:T(8,128)(2,1)S(1)} %copy-done.37), channel_id=1, source_target_pairs={{0,28},{4,16},{8,20},{12,24},{16,12},{20,0},{24,4},{28,8},{1,29},{... | collective-permute-start | bytes 147464 | tf_op jit(solution)/shard_map/ppermute | solution.py:224
  52.8 0.5 copy-done.31
  53.3 1.7 %add_blocks.3.refs_0_ = bf16[192,512]{1,0:T(8,128)(2,1)} custom-call(bf16[48,512]{1,0:T(8,128)(2,1)} %get-tuple-element.52.refs_0_, bf16[48,512]{1,0:T(8,128)(2,1)} %copy-done.23, bf16[48,512]{1,0:T(8,128)(2,1)} %copy-done.24, bf16[48,512]{1,0:T(8,128)(2,1)} %copy-done.25, bf16[48,512]{1,0:T(8,128)(2,1)} %copy-done.26, bf16[48,512]{1,0:T(8,128)(2,1)} %copy-done.27, ...), custom_call_target="tpu_custom_call" | custom-call | flops 196608 | bytes 786432 | tf_op jit(solution)/shard_map/add_blocks/pallas_call | solution.py:282
  55.4 1.0 collective-permute-start.9
  56.4 1.6 %collective-permute-start.31 = (bf16[192,512]{1,0:T(8,128)(2,1)}, bf16[192,512]{1,0:T(8,128)(2,1)S(1)}, u32[]{:S(2)}, u32[]{:S(2)}) collective-permute-start(bf16[192,512]{1,0:T(8,128)(2,1)} %add_blocks.3.refs_0_), channel_id=1, source_target_pairs={{0,1},{1,2},{2,3},{3,0},{4,5},{5,6},{6,7},{7,4},{8,9},{9,10},{10,1... | collective-permute-start | bytes 589832 | tf_op jit(solution)/shard_map/ppermute | solution.py:294
  58.0 0.8 slice_bitcast_fusion
  58.8 1.5 %collective-permute-start.34 = (f32[48]{0:T(128)S(1)}, f32[48]{0:T(128)S(1)}, u32[]{:S(2)}, u32[]{:S(2)}) collective-permute-start(f32[48]{0:T(128)S(1)} %slice_bitcast_fusion), channel_id=1, source_target_pairs={{0,16},{16,0},{1,17},{17,1},{2,18},{18,2},{3,19},{19,3},{4,20},{20... | collective-permute-start | bytes 584 | tf_op jit(solution)/shard_map/ppermute | solution.py:316
  60.2 2.6 %collective-permute-start.32 = (bf16[192,512]{1,0:T(8,128)(2,1)}, bf16[192,512]{1,0:T(8,128)(2,1)S(1)}, u32[]{:S(2)}, u32[]{:S(2)}) collective-permute-start(bf16[192,512]{1,0:T(8,128)(2,1)} %add_blocks.3.refs_0_), channel_id=1, source_target_pairs={{0,2},{1,3},{2,0},{3,1},{4,6},{5,7},{6,4},{7,5},{8,10},{9,11},{10,... | collective-permute-start | bytes 589832 | tf_op jit(solution)/shard_map/ppermute | solution.py:294
  62.8 1.3 %collective-permute-start.33 = (bf16[192,512]{1,0:T(8,128)(2,1)}, bf16[192,512]{1,0:T(8,128)(2,1)S(1)}, u32[]{:S(2)}, u32[]{:S(2)}) collective-permute-start(bf16[192,512]{1,0:T(8,128)(2,1)} %add_blocks.3.refs_0_), channel_id=1, source_target_pairs={{0,3},{1,0},{2,1},{3,2},{4,7},{5,4},{6,5},{7,6},{8,11},{9,8},{10,9... | collective-permute-start | bytes 589832 | tf_op jit(solution)/shard_map/ppermute | solution.py:294
  64.2 0.6 copy-done.33
  64.8 1.7 %add_blocks.2.refs_0_ = bf16[192,512]{1,0:T(8,128)(2,1)} custom-call(bf16[48,512]{1,0:T(8,128)(2,1)} %get-tuple-element.37.refs_0_, bf16[48,512]{1,0:T(8,128)(2,1)} %copy-done.30, bf16[48,512]{1,0:T(8,128)(2,1)} %copy-done.32, bf16[48,512]{1,0:T(8,128)(2,1)} %copy-done.33, bf16[48,512]{1,0:T(8,128)(2,1)} %copy-done.20, bf16[48,512]{1,0:T(8,128)(2,1)} %copy-done.21, ...), custom_call_target="tpu_custom_call" | custom-call | flops 196608 | bytes 786432 | tf_op jit(solution)/shard_map/add_blocks/pallas_call | solution.py:282
  66.5 0.7 collective-permute-start.14
  67.5 2.9 %collective-permute-start.16 = (bf16[192,512]{1,0:T(8,128)(2,1)}, bf16[192,512]{1,0:T(8,128)(2,1)S(1)}, u32[]{:S(2)}, u32[]{:S(2)}) collective-permute-start(bf16[192,512]{1,0:T(8,128)(2,1)} %add_blocks.2.refs_0_), channel_id=1, source_target_pairs={{0,3},{1,0},{2,1},{3,2},{4,7},{5,4},{6,5},{7,6},{8,11},{9,8},{10,9... | collective-permute-start | bytes 589832 | tf_op jit(solution)/shard_map/ppermute | solution.py:294
  70.4 0.8 fusion
  71.2 39.9 %all-reduce = f32[768]{0:T(1024)S(1)} all-reduce(f32[768]{0:T(1024)S(1)} %fusion), channel_id=2, replica_groups=mesh['dp'=2,'tensor'=4,'expert'=4] {'expert','tensor'}, use_global_device_ids=true, to_apply=%add | all-reduce | flops 768 | bytes 6144
  111.1 0.7 copy.10
  111.8 1.7 %gate_grad.1 = f32[8,512]{1,0:T(8,128)} custom-call(s32[8,512]{1,0:T(8,128)} %bitcast.13, f32[16,512]{1,0:T(8,128)} %get-tuple-element.32.key_ref, f32[48,16]{1,0:T(8,128)} %bitcast.14), custom_call_target="tpu_custom_call" | custom-call | flops 393216 | bytes 393216 | tf_op jit(solution)/shard_map/gate_grad/pallas_call | solution.py:318
  113.5 0.7 copy-done.1
  114.2 0.7 copy-done.2
  114.9 2.8 %combine.3 = bf16[512,512]{1,0:T(8,128)(2,1)} custom-call(bf16[768,512]{1,0:T(8,128)(2,1)} %weights.1.weight_ref, bf16[192,512]{1,0:T(8,128)(2,1)} %add_blocks.3.refs_0_, bf16[192,512]{1,0:T(8,128)(2,1)} %copy-done, bf16[192,512]{1,0:T(8,128)(2,1)} %copy-done.1, bf16[192,512]{1,0:T(8,128)(2,1)} %copy-done.2), custom_call_target="tpu_custom_call" | custom-call | flops 402653184 | bytes 1572864 | tf_op jit(solution)/shard_map/combine/pallas_call | solution.py:298
  117.7 0.6 copy-done.3
  118.4 0.7 copy-done.5
  119.1 2.8 %combine.2 = bf16[512,512]{1,0:T(8,128)(2,1)} custom-call(bf16[768,512]{1,0:T(8,128)(2,1)} %weights.1.weight_ref, bf16[192,512]{1,0:T(8,128)(2,1)} %add_blocks.2.refs_0_, bf16[192,512]{1,0:T(8,128)(2,1)} %copy-done.3, bf16[192,512]{1,0:T(8,128)(2,1)} %copy-done.4, bf16[192,512]{1,0:T(8,128)(2,1)} %copy-done.5), custom_call_target="tpu_custom_call" | custom-call | flops 402653184 | bytes 1572864 | tf_op jit(solution)/shard_map/combine/pallas_call | solution.py:298
  (123 shorter events, 1.8 us)
Async XLA Ops:
  2.7 7.9 %collective-permute-start = (bf16[48,512]{1,0:T(8,128)(2,1)}, bf16[48,512]{1,0:T(8,128)(2,1)S(1)}, u32[]{:S(2)}, u32[]{:S(2)}) collective-permute-start(bf16[48,512]{1,0:T(8,128)(2,1)} %get-tuple-element.34), channel_id=1, source_target_pairs={{0,4},{4,8},{8,12},{12,0},{16,20},{20,24},{24,28},{28,16},{1,5},{5... | collective-permute-start | bytes 147464 | tf_op jit(solution)/shard_map/ppermute | solution.py:224
  3.2 8.7 %collective-permute-start.1 = (bf16[48,512]{1,0:T(8,128)(2,1)}, bf16[48,512]{1,0:T(8,128)(2,1)S(1)}, u32[]{:S(2)}, u32[]{:S(2)}) collective-permute-start(bf16[48,512]{1,0:T(8,128)(2,1)} %get-tuple-element.35), channel_id=1, source_target_pairs={{0,8},{4,12},{8,0},{12,4},{16,24},{20,28},{24,16},{28,20},{1,9},{5... | collective-permute-start | bytes 147464 | tf_op jit(solution)/shard_map/ppermute | solution.py:224
  5.7 7.7 %collective-permute-start.2 = (bf16[48,512]{1,0:T(8,128)(2,1)}, bf16[48,512]{1,0:T(8,128)(2,1)S(1)}, u32[]{:S(2)}, u32[]{:S(2)}) collective-permute-start(bf16[48,512]{1,0:T(8,128)(2,1)} %get-tuple-element.36), channel_id=1, source_target_pairs={{0,12},{4,0},{8,4},{12,8},{16,28},{20,16},{24,20},{28,24},{1,13},{... | collective-permute-start | bytes 147464 | tf_op jit(solution)/shard_map/ppermute | solution.py:224
  7.1 6.4 %collective-permute-start.3 = (bf16[48,512]{1,0:T(8,128)(2,1)}, bf16[48,512]{1,0:T(8,128)(2,1)S(1)}, u32[]{:S(2)}, u32[]{:S(2)}) collective-permute-start(bf16[48,512]{1,0:T(8,128)(2,1)} %get-tuple-element.33.refs_0_), channel_id=1, source_target_pairs={{0,16},{4,20},{8,24},{12,28},{16,0},{20,4},{24,8},{28,12},{1,17},{... | collective-permute-start | bytes 147464 | tf_op jit(solution)/shard_map/ppermute | solution.py:224
  8.6 6.5 %collective-permute-start.4 = (bf16[48,512]{1,0:T(8,128)(2,1)}, bf16[48,512]{1,0:T(8,128)(2,1)S(1)}, u32[]{:S(2)}, u32[]{:S(2)}) collective-permute-start(bf16[48,512]{1,0:T(8,128)(2,1)} %get-tuple-element.34), channel_id=1, source_target_pairs={{0,20},{4,24},{8,28},{12,16},{16,4},{20,8},{24,12},{28,0},{1,21},{... | collective-permute-start | bytes 147464 | tf_op jit(solution)/shard_map/ppermute | solution.py:224
  10.6 9.5 %copy-start.6 = (bf16[48,512]{1,0:T(8,128)(2,1)}, bf16[48,512]{1,0:T(8,128)(2,1)S(1)}, u32[]{:S(2)}) copy-start(bf16[48,512]{1,0:T(8,128)(2,1)S(1)} %collective-permute-done.refs_1_) | copy-start | bytes 147460
  10.6 5.9 %collective-permute-start.5 = (bf16[48,512]{1,0:T(8,128)(2,1)}, bf16[48,512]{1,0:T(8,128)(2,1)S(1)}, u32[]{:S(2)}, u32[]{:S(2)}) collective-permute-start(bf16[48,512]{1,0:T(8,128)(2,1)} %get-tuple-element.35), channel_id=1, source_target_pairs={{0,24},{4,28},{8,16},{12,20},{16,8},{20,12},{24,0},{28,4},{1,25},{... | collective-permute-start | bytes 147464 | tf_op jit(solution)/shard_map/ppermute | solution.py:224
  11.9 6.1 %collective-permute-start.6 = (bf16[48,512]{1,0:T(8,128)(2,1)}, bf16[48,512]{1,0:T(8,128)(2,1)S(1)}, u32[]{:S(2)}, u32[]{:S(2)}) collective-permute-start(bf16[48,512]{1,0:T(8,128)(2,1)} %get-tuple-element.36), channel_id=1, source_target_pairs={{0,28},{4,16},{8,20},{12,24},{16,12},{20,0},{24,4},{28,8},{1,29},{... | collective-permute-start | bytes 147464 | tf_op jit(solution)/shard_map/ppermute | solution.py:224
  13.4 4.8 %collective-permute-start.17 = (bf16[48,512]{1,0:T(8,128)(2,1)}, bf16[48,512]{1,0:T(8,128)(2,1)S(1)}, u32[]{:S(2)}, u32[]{:S(2)}) collective-permute-start(bf16[48,512]{1,0:T(8,128)(2,1)} %get-tuple-element.46), channel_id=1, source_target_pairs={{0,4},{4,8},{8,12},{12,0},{16,20},{20,24},{24,28},{28,16},{1,5},{5... | collective-permute-start | bytes 147464 | tf_op jit(solution)/shard_map/ppermute | solution.py:224
  13.5 6.1 %collective-permute-start.18 = (bf16[48,512]{1,0:T(8,128)(2,1)}, bf16[48,512]{1,0:T(8,128)(2,1)S(1)}, u32[]{:S(2)}, u32[]{:S(2)}) collective-permute-start(bf16[48,512]{1,0:T(8,128)(2,1)} %get-tuple-element.47), channel_id=1, source_target_pairs={{0,8},{4,12},{8,0},{12,4},{16,24},{20,28},{24,16},{28,20},{1,9},{5... | collective-permute-start | bytes 147464 | tf_op jit(solution)/shard_map/ppermute | solution.py:224
  15.1 12.4 %collective-permute-start.21 = (bf16[48,512]{1,0:T(8,128)(2,1)}, bf16[48,512]{1,0:T(8,128)(2,1)S(1)}, u32[]{:S(2)}, u32[]{:S(2)}) collective-permute-start(bf16[48,512]{1,0:T(8,128)(2,1)} %get-tuple-element.46), channel_id=1, source_target_pairs={{0,20},{4,24},{8,28},{12,16},{16,4},{20,8},{24,12},{28,0},{1,21},{... | collective-permute-start | bytes 147464 | tf_op jit(solution)/shard_map/ppermute | solution.py:224
  16.5 11.0 %collective-permute-start.22 = (bf16[48,512]{1,0:T(8,128)(2,1)}, bf16[48,512]{1,0:T(8,128)(2,1)S(1)}, u32[]{:S(2)}, u32[]{:S(2)}) collective-permute-start(bf16[48,512]{1,0:T(8,128)(2,1)} %get-tuple-element.47), channel_id=1, source_target_pairs={{0,24},{4,28},{8,16},{12,20},{16,8},{20,12},{24,0},{28,4},{1,25},{... | collective-permute-start | bytes 147464 | tf_op jit(solution)/shard_map/ppermute | solution.py:224
  18.0 9.5 %collective-permute-start.19 = (bf16[48,512]{1,0:T(8,128)(2,1)}, bf16[48,512]{1,0:T(8,128)(2,1)S(1)}, u32[]{:S(2)}, u32[]{:S(2)}) collective-permute-start(bf16[48,512]{1,0:T(8,128)(2,1)} %get-tuple-element.48), channel_id=1, source_target_pairs={{0,12},{4,0},{8,4},{12,8},{16,28},{20,16},{24,20},{28,24},{1,13},{... | collective-permute-start | bytes 147464 | tf_op jit(solution)/shard_map/ppermute | solution.py:224
  18.2 9.2 %copy-start.9 = (bf16[48,512]{1,0:T(8,128)(2,1)}, bf16[48,512]{1,0:T(8,128)(2,1)S(1)}, u32[]{:S(2)}) copy-start(bf16[48,512]{1,0:T(8,128)(2,1)S(1)} %collective-permute-done.17.refs_1_) | copy-start | bytes 147460
  18.2 9.3 %collective-permute-start.23 = (bf16[48,512]{1,0:T(8,128)(2,1)}, bf16[48,512]{1,0:T(8,128)(2,1)S(1)}, u32[]{:S(2)}, u32[]{:S(2)}) collective-permute-start(bf16[48,512]{1,0:T(8,128)(2,1)} %get-tuple-element.48), channel_id=1, source_target_pairs={{0,28},{4,16},{8,20},{12,24},{16,12},{20,0},{24,4},{28,8},{1,29},{... | collective-permute-start | bytes 147464 | tf_op jit(solution)/shard_map/ppermute | solution.py:224
  19.6 7.9 %collective-permute-start.20 = (bf16[48,512]{1,0:T(8,128)(2,1)}, bf16[48,512]{1,0:T(8,128)(2,1)S(1)}, u32[]{:S(2)}, u32[]{:S(2)}) collective-permute-start(bf16[48,512]{1,0:T(8,128)(2,1)} %get-tuple-element.45.refs_0_), channel_id=1, source_target_pairs={{0,16},{4,20},{8,24},{12,28},{16,0},{20,4},{24,8},{28,12},{1,17},{... | collective-permute-start | bytes 147464 | tf_op jit(solution)/shard_map/ppermute | solution.py:224
  28.2 15.6 %copy-start.40 = (bf16[48,512]{1,0:T(8,128)(2,1)S(1)}, bf16[48,512]{1,0:T(8,128)(2,1)}, u32[]{:S(2)}) copy-start(bf16[48,512]{1,0:T(8,128)(2,1)} %get-tuple-element.41) | copy-start | bytes 147460
  28.2 17.1 %copy-start.39 = (bf16[48,512]{1,0:T(8,128)(2,1)S(1)}, bf16[48,512]{1,0:T(8,128)(2,1)}, u32[]{:S(2)}) copy-start(bf16[48,512]{1,0:T(8,128)(2,1)} %get-tuple-element.42) | copy-start | bytes 147460
  28.2 17.3 %copy-start.38 = (bf16[48,512]{1,0:T(8,128)(2,1)S(1)}, bf16[48,512]{1,0:T(8,128)(2,1)}, u32[]{:S(2)}) copy-start(bf16[48,512]{1,0:T(8,128)(2,1)} %get-tuple-element.43) | copy-start | bytes 147460
  28.2 20.8 %copy-start.41 = (u32[32]{0:T(128)S(1)}, u32[32]{0:T(128)}, u32[]{:S(2)}) copy-start(u32[32]{0:T(128)} %constant.5) | copy-start | bytes 388
  28.2 22.1 %copy-start.37 = (bf16[48,512]{1,0:T(8,128)(2,1)S(1)}, bf16[48,512]{1,0:T(8,128)(2,1)}, u32[]{:S(2)}) copy-start(bf16[48,512]{1,0:T(8,128)(2,1)} %get-tuple-element.44) | copy-start | bytes 147460
  28.2 24.5 %copy-start.36 = (bf16[48,512]{1,0:T(8,128)(2,1)S(1)}, bf16[48,512]{1,0:T(8,128)(2,1)}, u32[]{:S(2)}) copy-start(bf16[48,512]{1,0:T(8,128)(2,1)} %get-tuple-element.38) | copy-start | bytes 147460
  28.2 26.8 %copy-start.35 = (bf16[48,512]{1,0:T(8,128)(2,1)S(1)}, bf16[48,512]{1,0:T(8,128)(2,1)}, u32[]{:S(2)}) copy-start(bf16[48,512]{1,0:T(8,128)(2,1)} %get-tuple-element.39) | copy-start | bytes 147460
  28.2 27.2 %copy-start.34 = (bf16[48,512]{1,0:T(8,128)(2,1)S(1)}, bf16[48,512]{1,0:T(8,128)(2,1)}, u32[]{:S(2)}) copy-start(bf16[48,512]{1,0:T(8,128)(2,1)} %get-tuple-element.40) | copy-start | bytes 147460
  36.4 4.5 %collective-permute-start.24 = (bf16[48,512]{1,0:T(8,128)(2,1)}, bf16[48,512]{1,0:T(8,128)(2,1)S(1)}, u32[]{:S(2)}, u32[]{:S(2)}) collective-permute-start(bf16[48,512]{1,0:T(8,128)(2,1)} %get-tuple-element.53), channel_id=1, source_target_pairs={{0,4},{4,8},{8,12},{12,0},{16,20},{20,24},{24,28},{28,16},{1,5},{5... | collective-permute-start | bytes 147464 | tf_op jit(solution)/shard_map/ppermute | solution.py:224
  36.4 6.1 %collective-permute-start.25 = (bf16[48,512]{1,0:T(8,128)(2,1)}, bf16[48,512]{1,0:T(8,128)(2,1)S(1)}, u32[]{:S(2)}, u32[]{:S(2)}) collective-permute-start(bf16[48,512]{1,0:T(8,128)(2,1)} %get-tuple-element.54), channel_id=1, source_target_pairs={{0,8},{4,12},{8,0},{12,4},{16,24},{20,28},{24,16},{28,20},{1,9},{5... | collective-permute-start | bytes 147464 | tf_op jit(solution)/shard_map/ppermute | solution.py:224
  38.4 5.3 %collective-permute-start.26 = (bf16[48,512]{1,0:T(8,128)(2,1)}, bf16[48,512]{1,0:T(8,128)(2,1)S(1)}, u32[]{:S(2)}, u32[]{:S(2)}) collective-permute-start(bf16[48,512]{1,0:T(8,128)(2,1)} %get-tuple-element.55), channel_id=1, source_target_pairs={{0,12},{4,0},{8,4},{12,8},{16,28},{20,16},{24,20},{28,24},{1,13},{... | collective-permute-start | bytes 147464 | tf_op jit(solution)/shard_map/ppermute | solution.py:224
  39.5 5.7 %collective-permute-start.27 = (bf16[48,512]{1,0:T(8,128)(2,1)}, bf16[48,512]{1,0:T(8,128)(2,1)S(1)}, u32[]{:S(2)}, u32[]{:S(2)}) collective-permute-start(bf16[48,512]{1,0:T(8,128)(2,1)} %get-tuple-element.56), channel_id=1, source_target_pairs={{0,16},{4,20},{8,24},{12,28},{16,0},{20,4},{24,8},{28,12},{1,17},{... | collective-permute-start | bytes 147464 | tf_op jit(solution)/shard_map/ppermute | solution.py:224
  40.8 4.6 %collective-permute-start.28 = (bf16[48,512]{1,0:T(8,128)(2,1)}, bf16[48,512]{1,0:T(8,128)(2,1)S(1)}, u32[]{:S(2)}, u32[]{:S(2)}) collective-permute-start(bf16[48,512]{1,0:T(8,128)(2,1)} %get-tuple-element.57), channel_id=1, source_target_pairs={{0,20},{4,24},{8,28},{12,16},{16,4},{20,8},{24,12},{28,0},{1,21},{... | collective-permute-start | bytes 147464 | tf_op jit(solution)/shard_map/ppermute | solution.py:224
  40.8 11.9 %copy-start.23 = (bf16[48,512]{1,0:T(8,128)(2,1)}, bf16[48,512]{1,0:T(8,128)(2,1)S(1)}, u32[]{:S(2)}) copy-start(bf16[48,512]{1,0:T(8,128)(2,1)S(1)} %collective-permute-done.24.refs_1_) | copy-start | bytes 147460
  40.8 9.4 %collective-permute-start.29 = (bf16[48,512]{1,0:T(8,128)(2,1)}, bf16[48,512]{1,0:T(8,128)(2,1)S(1)}, u32[]{:S(2)}, u32[]{:S(2)}) collective-permute-start(bf16[48,512]{1,0:T(8,128)(2,1)} %get-tuple-element.58), channel_id=1, source_target_pairs={{0,24},{4,28},{8,16},{12,20},{16,8},{20,12},{24,0},{28,4},{1,25},{... | collective-permute-start | bytes 147464 | tf_op jit(solution)/shard_map/ppermute | solution.py:224
  42.5 10.2 %copy-start.24 = (bf16[48,512]{1,0:T(8,128)(2,1)}, bf16[48,512]{1,0:T(8,128)(2,1)S(1)}, u32[]{:S(2)}) copy-start(bf16[48,512]{1,0:T(8,128)(2,1)S(1)} %collective-permute-done.25.refs_2_) | copy-start | bytes 147460
  42.5 10.1 %collective-permute-start.30 = (bf16[48,512]{1,0:T(8,128)(2,1)}, bf16[48,512]{1,0:T(8,128)(2,1)S(1)}, u32[]{:S(2)}, u32[]{:S(2)}) collective-permute-start(bf16[48,512]{1,0:T(8,128)(2,1)} %get-tuple-element.59), channel_id=1, source_target_pairs={{0,28},{4,16},{8,20},{12,24},{16,12},{20,0},{24,4},{28,8},{1,29},{... | collective-permute-start | bytes 147464 | tf_op jit(solution)/shard_map/ppermute | solution.py:224
  43.7 11.2 %collective-permute-start.10 = (bf16[48,512]{1,0:T(8,128)(2,1)S(1)}, bf16[48,512]{1,0:T(8,128)(2,1)S(1)}, u32[]{:S(2)}, u32[]{:S(2)}) collective-permute-start(bf16[48,512]{1,0:T(8,128)(2,1)S(1)} %copy-done.40), channel_id=1, source_target_pairs={{0,16},{4,20},{8,24},{12,28},{16,0},{20,4},{24,8},{28,12},{1,17},{... | collective-permute-start | bytes 147464 | tf_op jit(solution)/shard_map/ppermute | solution.py:224
  45.3 10.1 %collective-permute-start.11 = (bf16[48,512]{1,0:T(8,128)(2,1)S(1)}, bf16[48,512]{1,0:T(8,128)(2,1)S(1)}, u32[]{:S(2)}, u32[]{:S(2)}) collective-permute-start(bf16[48,512]{1,0:T(8,128)(2,1)S(1)} %copy-done.39), channel_id=1, source_target_pairs={{0,20},{4,24},{8,28},{12,16},{16,4},{20,8},{24,12},{28,0},{1,21},{... | collective-permute-start | bytes 147464 | tf_op jit(solution)/shard_map/ppermute | solution.py:224
  45.5 11.0 %collective-permute-start.12 = (bf16[48,512]{1,0:T(8,128)(2,1)S(1)}, bf16[48,512]{1,0:T(8,128)(2,1)S(1)}, u32[]{:S(2)}, u32[]{:S(2)}) collective-permute-start(bf16[48,512]{1,0:T(8,128)(2,1)S(1)} %copy-done.38), channel_id=1, source_target_pairs={{0,24},{4,28},{8,16},{12,20},{16,8},{20,12},{24,0},{28,4},{1,25},{... | collective-permute-start | bytes 147464 | tf_op jit(solution)/shard_map/ppermute | solution.py:224
  50.3 8.5 %collective-permute-start.13 = (bf16[48,512]{1,0:T(8,128)(2,1)S(1)}, bf16[48,512]{1,0:T(8,128)(2,1)S(1)}, u32[]{:S(2)}, u32[]{:S(2)}) collective-permute-start(bf16[48,512]{1,0:T(8,128)(2,1)S(1)} %copy-done.37), channel_id=1, source_target_pairs={{0,28},{4,16},{8,20},{12,24},{16,12},{20,0},{24,4},{28,8},{1,29},{... | collective-permute-start | bytes 147464 | tf_op jit(solution)/shard_map/ppermute | solution.py:224
  52.7 7.5 %collective-permute-start.7 = (bf16[48,512]{1,0:T(8,128)(2,1)S(1)}, bf16[48,512]{1,0:T(8,128)(2,1)S(1)}, u32[]{:S(2)}, u32[]{:S(2)}) collective-permute-start(bf16[48,512]{1,0:T(8,128)(2,1)S(1)} %copy-done.36), channel_id=1, source_target_pairs={{0,4},{4,8},{8,12},{12,0},{16,20},{20,24},{24,28},{28,16},{1,5},{5... | collective-permute-start | bytes 147464 | tf_op jit(solution)/shard_map/ppermute | solution.py:224
  55.0 7.8 %collective-permute-start.8 = (bf16[48,512]{1,0:T(8,128)(2,1)S(1)}, bf16[48,512]{1,0:T(8,128)(2,1)S(1)}, u32[]{:S(2)}, u32[]{:S(2)}) collective-permute-start(bf16[48,512]{1,0:T(8,128)(2,1)S(1)} %copy-done.35), channel_id=1, source_target_pairs={{0,8},{4,12},{8,0},{12,4},{16,24},{20,28},{24,16},{28,20},{1,9},{5... | collective-permute-start | bytes 147464 | tf_op jit(solution)/shard_map/ppermute | solution.py:224
  55.4 8.8 %collective-permute-start.9 = (bf16[48,512]{1,0:T(8,128)(2,1)S(1)}, bf16[48,512]{1,0:T(8,128)(2,1)S(1)}, u32[]{:S(2)}, u32[]{:S(2)}) collective-permute-start(bf16[48,512]{1,0:T(8,128)(2,1)S(1)} %copy-done.34), channel_id=1, source_target_pairs={{0,12},{4,0},{8,4},{12,8},{16,28},{20,16},{24,20},{28,24},{1,13},{... | collective-permute-start | bytes 147464 | tf_op jit(solution)/shard_map/ppermute | solution.py:224
  56.4 11.1 %collective-permute-start.31 = (bf16[192,512]{1,0:T(8,128)(2,1)}, bf16[192,512]{1,0:T(8,128)(2,1)S(1)}, u32[]{:S(2)}, u32[]{:S(2)}) collective-permute-start(bf16[192,512]{1,0:T(8,128)(2,1)} %add_blocks.3.refs_0_), channel_id=1, source_target_pairs={{0,1},{1,2},{2,3},{3,0},{4,5},{5,6},{6,7},{7,4},{8,9},{9,10},{10,1... | collective-permute-start | bytes 589832 | tf_op jit(solution)/shard_map/ppermute | solution.py:294
  58.8 8.4 %collective-permute-start.34 = (f32[48]{0:T(128)S(1)}, f32[48]{0:T(128)S(1)}, u32[]{:S(2)}, u32[]{:S(2)}) collective-permute-start(f32[48]{0:T(128)S(1)} %slice_bitcast_fusion), channel_id=1, source_target_pairs={{0,16},{16,0},{1,17},{17,1},{2,18},{18,2},{3,19},{19,3},{4,20},{20... | collective-permute-start | bytes 584 | tf_op jit(solution)/shard_map/ppermute | solution.py:316
  60.2 53.3 %collective-permute-start.32 = (bf16[192,512]{1,0:T(8,128)(2,1)}, bf16[192,512]{1,0:T(8,128)(2,1)S(1)}, u32[]{:S(2)}, u32[]{:S(2)}) collective-permute-start(bf16[192,512]{1,0:T(8,128)(2,1)} %add_blocks.3.refs_0_), channel_id=1, source_target_pairs={{0,2},{1,3},{2,0},{3,1},{4,6},{5,7},{6,4},{7,5},{8,10},{9,11},{10,... | collective-permute-start | bytes 589832 | tf_op jit(solution)/shard_map/ppermute | solution.py:294
  62.8 50.7 %collective-permute-start.33 = (bf16[192,512]{1,0:T(8,128)(2,1)}, bf16[192,512]{1,0:T(8,128)(2,1)S(1)}, u32[]{:S(2)}, u32[]{:S(2)}) collective-permute-start(bf16[192,512]{1,0:T(8,128)(2,1)} %add_blocks.3.refs_0_), channel_id=1, source_target_pairs={{0,3},{1,0},{2,1},{3,2},{4,7},{5,4},{6,5},{7,6},{8,11},{9,8},{10,9... | collective-permute-start | bytes 589832 | tf_op jit(solution)/shard_map/ppermute | solution.py:294
  66.5 51.2 %collective-permute-start.14 = (bf16[192,512]{1,0:T(8,128)(2,1)}, bf16[192,512]{1,0:T(8,128)(2,1)S(1)}, u32[]{:S(2)}, u32[]{:S(2)}) collective-permute-start(bf16[192,512]{1,0:T(8,128)(2,1)} %add_blocks.2.refs_0_), channel_id=1, source_target_pairs={{0,1},{1,2},{2,3},{3,0},{4,5},{5,6},{6,7},{7,4},{8,9},{9,10},{10,1... | collective-permute-start | bytes 589832 | tf_op jit(solution)/shard_map/ppermute | solution.py:294
  67.2 50.5 %collective-permute-start.15 = (bf16[192,512]{1,0:T(8,128)(2,1)}, bf16[192,512]{1,0:T(8,128)(2,1)S(1)}, u32[]{:S(2)}, u32[]{:S(2)}) collective-permute-start(bf16[192,512]{1,0:T(8,128)(2,1)} %add_blocks.2.refs_0_), channel_id=1, source_target_pairs={{0,2},{1,3},{2,0},{3,1},{4,6},{5,7},{6,4},{7,5},{8,10},{9,11},{10,... | collective-permute-start | bytes 589832 | tf_op jit(solution)/shard_map/ppermute | solution.py:294
  67.5 46.0 %copy-start = (bf16[192,512]{1,0:T(8,128)(2,1)}, bf16[192,512]{1,0:T(8,128)(2,1)S(1)}, u32[]{:S(2)}) copy-start(bf16[192,512]{1,0:T(8,128)(2,1)S(1)} %collective-permute-done.31.refs_1_) | copy-start | bytes 589828
  67.5 50.2 %collective-permute-start.16 = (bf16[192,512]{1,0:T(8,128)(2,1)}, bf16[192,512]{1,0:T(8,128)(2,1)S(1)}, u32[]{:S(2)}, u32[]{:S(2)}) collective-permute-start(bf16[192,512]{1,0:T(8,128)(2,1)} %add_blocks.2.refs_0_), channel_id=1, source_target_pairs={{0,3},{1,0},{2,1},{3,2},{4,7},{5,4},{6,5},{7,6},{8,11},{9,8},{10,9... | collective-permute-start | bytes 589832 | tf_op jit(solution)/shard_map/ppermute | solution.py:294
  (29 other events, 111.3 us)

commit v2 on v1

--- a/solution.py
+++ b/solution.py
@@ -80,8 +80,8 @@
 
 def forward_kernel(groups, count, *refs):
     pieces, (gate_ref, up_ref, down_ref) = refs[:count], refs[count : count + 3]
-    act_ref, scale_ref, hid_ref = refs[count + 3 : count + 6]
-    outs, (x_ref, y_ref) = refs[count + 6 : 2 * count + 6], refs[2 * count + 6 :]
+    act_ref, scale_ref = refs[count + 3 : count + 5]
+    outs, (x_ref, y_ref) = refs[count + 5 : 2 * count + 5], refs[2 * count + 5 :]
     step = pl.program_id(0)
 
     @pl.when(step == 0)
@@ -96,7 +96,6 @@
     hidden = (act * up_pre).astype(BF16)
     act_ref[...] = act
     scale_ref[...] = up_pre * (sig * (1.0 + gate_pre * (1.0 - sig)))
-    hid_ref[...] = hidden
     y_ref[...] += jnp.dot(hidden, down_ref[0], preferred_element_type=F32)
 
     @pl.when(step == pl.num_programs(0) - 1)
@@ -106,27 +105,18 @@
 
 def backward_kernel(groups, count, *refs):
     pieces, (gate_ref, up_ref, down_ref) = refs[:count], refs[count : count + 3]
-    act_ref, scale_ref, hid_ref = refs[count + 3 : count + 6]
-    outs, sum_ref = refs[count + 6 : 2 * count + 6], refs[2 * count + 6]
-    x_ref, y_ref = refs[2 * count + 7 :]
+    act_ref, scale_ref = refs[count + 3 : count + 5]
+    outs, (x_ref, y_ref) = refs[count + 5 : 2 * count + 5], refs[2 * count + 5 :]
     step = pl.program_id(0)
 
     @pl.when(step == 0)
     def _():
         gather_pieces(x_ref, pieces, groups)
         y_ref[...] = jnp.zeros_like(y_ref)
-        sum_ref[...] = jnp.zeros_like(sum_ref)
 
     grad_hid = lax.dot_general(x_ref[...], down_ref[0], CONTRACT_LAST, preferred_element_type=F32)
     grad_gate = (grad_hid * scale_ref[...]).astype(BF16)
     grad_up = (grad_hid * act_ref[...]).astype(BF16)
-    sum_ref[...] += lax.dot_general(
-        jnp.ones((sum_ref.shape[0], grad_hid.shape[1]), F32),
-        grad_hid * hid_ref[...].astype(F32),
-        CONTRACT_LAST,
-        preferred_element_type=F32,
-        precision=lax.Precision.HIGHEST,
-    )
     y_ref[...] += jnp.dot(grad_gate, gate_ref[0], preferred_element_type=F32) + jnp.dot(
         grad_up, up_ref[0], preferred_element_type=F32
     )
@@ -174,15 +164,20 @@
     ).astype(BF16)
 
 
-def gate_grad_kernel(routes_ref, key_ref, sums_ref, out_ref):
-    experts, rows = key_ref.shape
+def gate_grad_kernel(groups, columns, routes_ref, key_ref, grads_ref, *refs):
+    parts, (out_ref, sum_ref) = refs[:-2], refs[-2:]
+    rows = key_ref.shape[1]
+    t, e = lax.axis_index("tensor"), lax.axis_index("expert")
     slot = lax.broadcasted_iota(jnp.int32, (CAP, rows), 0).astype(F32)
+    routes = routes_ref[...]
     total = jnp.zeros(out_ref.shape, F32)
-    routes = routes_ref[...]
-    for expert in range(experts):
-        same = key_ref[expert : expert + 1, :] == slot
-        row = jnp.sum(jnp.where(same, sums_ref[:, expert : expert + 1], 0.0), axis=0, keepdims=True)
-        total = total + jnp.where(routes == expert, row, 0.0)
+    for dz, part in enumerate(parts):
+        sum_ref[...] = lax.dot_general(part[...], grads_ref[...], CONTRACT_LAST, preferred_element_type=F32)
+        for dt in range(groups):
+            expert = lax.rem(e - dz + columns, columns) * groups + lax.rem(t - dt + groups, groups)
+            same = key_ref[pl.ds(expert, 1), :] == slot
+            row = jnp.sum(jnp.where(same, sum_ref[dt * CAP : (dt + 1) * CAP, :], 0.0), axis=0, keepdims=True)
+            total = total + jnp.where(routes == expert, row, 0.0)
     out_ref[...] = total
 
 
@@ -240,32 +235,31 @@
 
     tok_in = spread(tok_pieces)
     grad_in = spread(grad_pieces)
-    act, scale, hidden, *outs = pl.pallas_call(
+    act, scale, *outs = pl.pallas_call(
         functools.partial(forward_kernel, groups, count),
         grid=(hid_dev // chunk,),
         out_shape=[
             jax.ShapeDtypeStruct((tall, hid_dev), F32),
             jax.ShapeDtypeStruct((tall, hid_dev), F32),
-            jax.ShapeDtypeStruct((tall, hid_dev), BF16),
         ]
         + [piece] * count,
         in_specs=[piece_block] * count + [weight_block] * 3,
-        out_specs=[hidden_block] * 3 + [piece_block] * count,
+        out_specs=[hidden_block] * 2 + [piece_block] * count,
         scratch_shapes=scratch,
         cost_estimate=cost(3 * matmul_flops, 6 * hid_dev * feats),
         name="forward",
     )(*tok_in, gate_weight, up_weight, down_weight)
     out_in = exchange(outs)
-    *backs, sums = pl.pallas_call(
+    backs = pl.pallas_call(
         functools.partial(backward_kernel, groups, count),
         grid=(hid_dev // chunk,),
-        out_shape=[piece] * count + [jax.ShapeDtypeStruct((8, tall), F32)],
-        in_specs=[piece_block] * count + [weight_block] * 3 + [hidden_block] * 3,
-        out_specs=[piece_block] * count + [whole_block((8, tall))],
+        out_shape=[piece] * count,
+        in_specs=[piece_block] * count + [weight_block] * 3 + [hidden_block] * 2,
+        out_specs=[piece_block] * count,
         scratch_shapes=scratch,
         cost_estimate=cost(3 * matmul_flops, 6 * hid_dev * feats),
         name="backward",
-    )(*grad_in, gate_weight, up_weight, down_weight, act, scale, hidden)
+    )(*grad_in, gate_weight, up_weight, down_weight, act, scale)
     back_in = exchange(backs)
 
     weight_map = pl.pallas_call(
@@ -289,10 +283,17 @@
         )(*pieces)
 
     def across(value):
-        parts = [value]
-        for dz in range(1, columns):
-            parts.append(lax.ppermute(value, "expert", [(z, (z + dz) % columns) for z in range(columns)]))
-        return parts
+        if columns != 4:
+            return [value] + [
+                lax.ppermute(value, "expert", [(z, (z + dz) % columns) for z in range(columns)])
+                for dz in range(1, columns)
+            ]
+        far = lax.ppermute(value, "expert", [(z, (z + 2) % columns) for z in range(columns)])
+        up = lax.ppermute(value, "expert", [(z, z + 1) for z in range(columns - 1)])
+        down = lax.ppermute(value, "expert", [(z + 1, z) for z in range(columns - 1)])
+        ends = lax.ppermute(far, "expert", [(2, 3), (1, 0)])
+        e = lax.axis_index("expert")
+        return [value, jnp.where(e == 0, ends, up), far, jnp.where(e == columns - 1, ends, down)]
 
     def combine(parts):
         return pl.pallas_call(
@@ -310,19 +311,16 @@
     mixed = combine(mixed_parts)
     grad_tokens = combine(back_parts)
 
-    own = sums[0, :CAP]
-    for db in range(1, n_dp):
-        row = (-db) % n_dp * CAP
-        own = own + lax.ppermute(sums[0, row : row + CAP], "dp", [(b, (b + db) % n_dp) for b in range(n_dp)])
-    sums_all = lax.all_gather(own, ("expert", "tensor"), axis=0, tiled=False)
-    grad_gates = pl.pallas_call(
-        gate_grad_kernel,
+    gate_part = pl.pallas_call(
+        functools.partial(gate_grad_kernel, groups, columns),
         out_shape=jax.ShapeDtypeStruct(routes_t.shape, F32),
-        in_specs=[vmem()] * 3,
+        in_specs=[vmem()] * (columns + 3),
         out_specs=vmem(),
-        cost_estimate=cost(experts * CAP * rows, experts * CAP * rows),
+        scratch_shapes=[pltpu.VMEM((groups * CAP, rows), F32)],
+        cost_estimate=cost(2 * experts * CAP * rows * width, 2 * experts * CAP * width),
         name="gate_grad",
-    )(routes_t, key, sums_all.T)
+    )(routes_t, key, grad_out, *mixed_parts)
+    grad_gates = lax.psum(gate_part, "tensor")
     return (mixed, grad_tokens, grad_gates.T)
 
 

time: 123 us -> 109 us (0.89)
  blocking collectives: 39.9 us -> 11.3 us
  waiting for transfers between devices: 0.21 us -> 10.4 us
  starting transfers between devices: 40.7 us -> 50.4 us
  local copies, waits for them, and re-layouts: 6.67 us -> 1.33 us
    unnamed x1 -> x0, blocking collectives: 39.9 us -> none
    psum x0 -> x1, blocking collectives: none -> 11.3 us  [body(): grad_gates = lax.psum(gate_part, 'tensor')]
    ppermute x7 -> x8, waiting for transfers between devices: 0.02 us -> 10.1 us  [the longest x2 5.73 us: across(): lax.ppermute(value, 'expert', [(z, (z + 2) % columns) for z in range(colu...]
    ppermute x7 -> x8, starting transfers between devices: 10.9 us -> 20.9 us  [the longest x2 12 us: across(): up = lax.ppermute(value, 'expert', [(z, z + 1) for z in range(columns - 1)])]
    unnamed x86 -> x74, local copies, waits for them, and re-layouts: 5.15 us -> 1.33 us
  transfers between devices with their start and end apart: 35 -> 36, of which waited for: 1 -> 6; matrix products, arithmetic and copies ran while one was open for 2% -> 0% of each run, Pallas kernels for 16% -> 13%
where the time goes in v2:
time: 109 us; the launch traced here: 108 us
  starting transfers between devices  50.4 us (46%)
  Pallas kernels  32.8 us (30%)
  blocking collectives  11.3 us (10%)
  waiting for transfers between devices  10.4 us (10%)
  local copies, waits for them, and re-layouts  1.33 us (1%)
    ppermute x28, starting transfers between devices, shift(): return lax.ppermute(value, ('dp', 'tensor'), pairs)  29.5 us
    ppermute x2, starting transfers between devices, across(): up = lax.ppermute(value, 'expert', [(z, z + 1) for z in range(columns - 1)])  12 us
    psum x1, blocking collectives, body(): grad_gates = lax.psum(gate_part, 'tensor')  11.3 us
    pallas_call x1, Pallas kernels, body(): pl.pallas_call(functools.partial(backward_kernel, groups, count), grid=(h...  7.83 us
    pallas_call x1, Pallas kernels, body(): pl.pallas_call(functools.partial(forward_kernel, groups, count), grid=(hi...  7.15 us
    ppermute x2, waiting for transfers between devices, across(): lax.ppermute(value, 'expert', [(z, (z + 2) % columns) for z in range(colu...  5.73 us
    pallas_call x2, Pallas kernels, combine(): pl.pallas_call(combine_kernel, out_shape=jax.ShapeDtypeStruct((rows, widt...  5.63 us
    ppermute x2, waiting for transfers between devices, across(): ends = lax.ppermute(far, 'expert', [(2, 3), (1, 0)])  4.35 us
  transfers between devices with their start and end apart: 36, of which 6 were waited for; matrix products, arithmetic and copies ran while one was open for 0% of the time, Pallas kernels for 13%

profile of v2, /device:TPU:0, one launch (start us, length us, event | category | flops | bytes accessed | tf_op | source)
XLA Modules:
  0.0 108.1 jit_solution(652058543551081530)
XLA Ops:
  0.6 2.1 %number.1 = (f32[16,512]{1,0:T(8,128)}, bf16[48,512]{1,0:T(8,128)(2,1)}, bf16[48,512]{1,0:T(8,128)(2,1)}, bf16[48,512]{1,0:T(8,128)(2,1)}, bf16[48,512]{1,0:T(8,128)(2,1)}) custom-call(s32[8,512]{1,0:T(8,128)} %bitcast.3, bf16[512,512]{1,0:T(8,128)(2,1)} %tokens_ref.1), custom_call_target="tpu_custom_call" | custom-call | flops 100663296 | bytes 524288 | tf_op jit(solution)/shard_map/number/pallas_call | solution.py:195
  2.7 3.0 %collective-permute-start.3 = (bf16[48,512]{1,0:T(8,128)(2,1)}, bf16[48,512]{1,0:T(8,128)(2,1)S(1)}, u32[]{:S(2)}, u32[]{:S(2)}) collective-permute-start(bf16[48,512]{1,0:T(8,128)(2,1)} %get-tuple-element.31.refs_0_), channel_id=1, source_target_pairs={{0,16},{4,20},{8,24},{12,28},{16,0},{20,4},{24,8},{28,12},{1,17},{... | collective-permute-start | bytes 147464 | tf_op jit(solution)/shard_map/ppermute | solution.py:219
  5.7 1.5 %collective-permute-start = (bf16[48,512]{1,0:T(8,128)(2,1)}, bf16[48,512]{1,0:T(8,128)(2,1)S(1)}, u32[]{:S(2)}, u32[]{:S(2)}) collective-permute-start(bf16[48,512]{1,0:T(8,128)(2,1)} %get-tuple-element.32), channel_id=1, source_target_pairs={{0,4},{4,8},{8,12},{12,0},{16,20},{20,24},{24,28},{28,16},{1,5},{5... | collective-permute-start | bytes 147464 | tf_op jit(solution)/shard_map/ppermute | solution.py:219
  7.2 1.5 %collective-permute-start.5 = (bf16[48,512]{1,0:T(8,128)(2,1)}, bf16[48,512]{1,0:T(8,128)(2,1)S(1)}, u32[]{:S(2)}, u32[]{:S(2)}) collective-permute-start(bf16[48,512]{1,0:T(8,128)(2,1)} %get-tuple-element.33), channel_id=1, source_target_pairs={{0,24},{4,28},{8,16},{12,20},{16,8},{20,12},{24,0},{28,4},{1,25},{... | collective-permute-start | bytes 147464 | tf_op jit(solution)/shard_map/ppermute | solution.py:219
  8.7 1.5 %collective-permute-start.1 = (bf16[48,512]{1,0:T(8,128)(2,1)}, bf16[48,512]{1,0:T(8,128)(2,1)S(1)}, u32[]{:S(2)}, u32[]{:S(2)}) collective-permute-start(bf16[48,512]{1,0:T(8,128)(2,1)} %get-tuple-element.33), channel_id=1, source_target_pairs={{0,8},{4,12},{8,0},{12,4},{16,24},{20,28},{24,16},{28,20},{1,9},{5... | collective-permute-start | bytes 147464 | tf_op jit(solution)/shard_map/ppermute | solution.py:219
  10.2 2.0 %pick.1 = (bf16[48,512]{1,0:T(8,128)(2,1)}, bf16[48,512]{1,0:T(8,128)(2,1)}, bf16[48,512]{1,0:T(8,128)(2,1)}, bf16[48,512]{1,0:T(8,128)(2,1)}) custom-call(f32[16,512]{1,0:T(8,128)} %get-tuple-element.30.key_ref, bf16[512,512]{1,0:T(8,128)(2,1)} %grads_ref.1), custom_call_target="tpu_custom_call" | custom-call | flops 100663296 | bytes 524288 | tf_op jit(solution)/shard_map/pick/pallas_call | solution.py:203
  12.3 0.3 collective-permute-start.2
  12.6 2.0 %collective-permute-start.21 = (bf16[48,512]{1,0:T(8,128)(2,1)}, bf16[48,512]{1,0:T(8,128)(2,1)S(1)}, u32[]{:S(2)}, u32[]{:S(2)}) collective-permute-start(bf16[48,512]{1,0:T(8,128)(2,1)} %get-tuple-element.43.refs_0_), channel_id=1, source_target_pairs={{0,16},{4,20},{8,24},{12,28},{16,0},{20,4},{24,8},{28,12},{1,17},{... | collective-permute-start | bytes 147464 | tf_op jit(solution)/shard_map/ppermute | solution.py:219
  14.6 1.5 %collective-permute-start.18 = (bf16[48,512]{1,0:T(8,128)(2,1)}, bf16[48,512]{1,0:T(8,128)(2,1)S(1)}, u32[]{:S(2)}, u32[]{:S(2)}) collective-permute-start(bf16[48,512]{1,0:T(8,128)(2,1)} %get-tuple-element.44), channel_id=1, source_target_pairs={{0,4},{4,8},{8,12},{12,0},{16,20},{20,24},{24,28},{28,16},{1,5},{5... | collective-permute-start | bytes 147464 | tf_op jit(solution)/shard_map/ppermute | solution.py:219
  16.1 1.5 %collective-permute-start.23 = (bf16[48,512]{1,0:T(8,128)(2,1)}, bf16[48,512]{1,0:T(8,128)(2,1)S(1)}, u32[]{:S(2)}, u32[]{:S(2)}) collective-permute-start(bf16[48,512]{1,0:T(8,128)(2,1)} %get-tuple-element.45), channel_id=1, source_target_pairs={{0,24},{4,28},{8,16},{12,20},{16,8},{20,12},{24,0},{28,4},{1,25},{... | collective-permute-start | bytes 147464 | tf_op jit(solution)/shard_map/ppermute | solution.py:219
  17.6 1.5 %collective-permute-start.19 = (bf16[48,512]{1,0:T(8,128)(2,1)}, bf16[48,512]{1,0:T(8,128)(2,1)S(1)}, u32[]{:S(2)}, u32[]{:S(2)}) collective-permute-start(bf16[48,512]{1,0:T(8,128)(2,1)} %get-tuple-element.45), channel_id=1, source_target_pairs={{0,8},{4,12},{8,0},{12,4},{16,24},{20,28},{24,16},{28,20},{1,9},{5... | collective-permute-start | bytes 147464 | tf_op jit(solution)/shard_map/ppermute | solution.py:219
  19.2 0.9 collective-permute-start.20
  20.1 7.2 %forward.1 = (f32[96,768]{1,0:T(8,128)}, f32[96,768]{1,0:T(8,128)}, bf16[48,512]{1,0:T(8,128)(2,1)}, bf16[48,512]{1,0:T(8,128)(2,1)}, bf16[48,512]{1,0:T(8,128)(...) custom-call(bf16[48,512]{1,0:T(8,128)(2,1)} %get-tuple-element.31.re, ...), custom_call_target="tpu_custom_call" | custom-call | flops 905969664 | bytes 9437184 | tf_op jit(solution)/shard_map/forward/pallas_call | solution.py:238
  27.4 0.5 copy-done.9
  28.0 7.8 %backward.1 = (bf16[48,512]{1,0:T(8,128)(2,1)}, bf16[48,512]{1,0:T(8,128)(2,1)}, bf16[48,512]{1,0:T(8,128)(2,1)}, bf16[48,512]{1,0:T(8,128)(2,1)}, bf16[48,512]{...) custom-call(bf16[48,512]{1,0:T(8,128)(2,1)} %get-tuple-element.43.refs_0_, ...), custom_call_target="tpu_custom_call" | custom-call | flops 905969664 | bytes 9437184 | tf_op jit(solution)/shard_map/backward/pallas_call | solution.py:253
  35.9 1.4 %collective-permute-start.26 = (bf16[48,512]{1,0:T(8,128)(2,1)}, bf16[48,512]{1,0:T(8,128)(2,1)S(1)}, u32[]{:S(2)}, u32[]{:S(2)}) collective-permute-start(bf16[48,512]{1,0:T(8,128)(2,1)} %get-tuple-element.51), channel_id=1, source_target_pairs={{0,8},{4,12},{8,0},{12,4},{16,24},{20,28},{24,16},{28,20},{1,9},{5... | collective-permute-start | bytes 147464 | tf_op jit(solution)/shard_map/ppermute | solution.py:219
  37.3 0.5 collective-permute-start.7
  37.8 1.3 %collective-permute-start.8 = (bf16[48,512]{1,0:T(8,128)(2,1)S(1)}, bf16[48,512]{1,0:T(8,128)(2,1)S(1)}, u32[]{:S(2)}, u32[]{:S(2)}) collective-permute-start(bf16[48,512]{1,0:T(8,128)(2,1)S(1)} %copy-done.35), channel_id=1, source_target_pairs={{0,8},{4,12},{8,0},{12,4},{16,24},{20,28},{24,16},{28,20},{1,9},{5... | collective-permute-start | bytes 147464 | tf_op jit(solution)/shard_map/ppermute | solution.py:219
  39.1 0.4 collective-permute-start.9
  39.5 0.1 collective-permute-done.25.refs_1_
  39.7 1.3 %collective-permute-start.10 = (bf16[48,512]{1,0:T(8,128)(2,1)S(1)}, bf16[48,512]{1,0:T(8,128)(2,1)S(1)}, u32[]{:S(2)}, u32[]{:S(2)}) collective-permute-start(bf16[48,512]{1,0:T(8,128)(2,1)S(1)} %copy-done.33), channel_id=1, source_target_pairs={{0,16},{4,20},{8,24},{12,28},{16,0},{20,4},{24,8},{28,12},{1,17},{... | collective-permute-start | bytes 147464 | tf_op jit(solution)/shard_map/ppermute | solution.py:219
  41.0 0.6 collective-permute-start.11
  41.6 1.9 %collective-permute-start.12 = (bf16[48,512]{1,0:T(8,128)(2,1)S(1)}, bf16[48,512]{1,0:T(8,128)(2,1)S(1)}, u32[]{:S(2)}, u32[]{:S(2)}) collective-permute-start(bf16[48,512]{1,0:T(8,128)(2,1)S(1)} %copy-done.31), channel_id=1, source_target_pairs={{0,24},{4,28},{8,16},{12,20},{16,8},{20,12},{24,0},{28,4},{1,25},{... | collective-permute-start | bytes 147464 | tf_op jit(solution)/shard_map/ppermute | solution.py:219
  43.5 2.0 %collective-permute-start.13 = (bf16[48,512]{1,0:T(8,128)(2,1)S(1)}, bf16[48,512]{1,0:T(8,128)(2,1)S(1)}, u32[]{:S(2)}, u32[]{:S(2)}) collective-permute-start(bf16[48,512]{1,0:T(8,128)(2,1)S(1)} %copy-done.30), channel_id=1, source_target_pairs={{0,28},{4,16},{8,20},{12,24},{16,12},{20,0},{24,4},{28,8},{1,29},{... | collective-permute-start | bytes 147464 | tf_op jit(solution)/shard_map/ppermute | solution.py:219
  45.6 1.0 collective-permute-start.28
  46.6 0.8 collective-permute-start.29
  47.4 1.4 %collective-permute-start.30 = (bf16[48,512]{1,0:T(8,128)(2,1)}, bf16[48,512]{1,0:T(8,128)(2,1)S(1)}, u32[]{:S(2)}, u32[]{:S(2)}) collective-permute-start(bf16[48,512]{1,0:T(8,128)(2,1)} %get-tuple-element.55), channel_id=1, source_target_pairs={{0,24},{4,28},{8,16},{12,20},{16,8},{20,12},{24,0},{28,4},{1,25},{... | collective-permute-start | bytes 147464 | tf_op jit(solution)/shard_map/ppermute | solution.py:219
  48.8 1.5 %collective-permute-start.31 = (bf16[48,512]{1,0:T(8,128)(2,1)}, bf16[48,512]{1,0:T(8,128)(2,1)S(1)}, u32[]{:S(2)}, u32[]{:S(2)}) collective-permute-start(bf16[48,512]{1,0:T(8,128)(2,1)} %get-tuple-element.56), channel_id=1, source_target_pairs={{0,28},{4,16},{8,20},{12,24},{16,12},{20,0},{24,4},{28,8},{1,29},{... | collective-permute-start | bytes 147464 | tf_op jit(solution)/shard_map/ppermute | solution.py:219
  50.4 1.7 %add_blocks.2.refs_0_ = bf16[192,512]{1,0:T(8,128)(2,1)} custom-call(bf16[48,512]{1,0:T(8,128)(2,1)} %get-tuple-element.35.refs_0_, bf16[48,512]{1,0:T(8,128)(2,1)} %copy-done.18, bf16[48,512]{1,0:T(8,128)(2,1)} %copy-done.19, bf16[48,512]{1,0:T(8,128)(2,1)} %copy-done.20, bf16[48,512]{1,0:T(8,128)(2,1)} %copy-done.22, bf16[48,512]{1,0:T(8,128)(2,1)} %copy-done.24, ...), custom_call_target="tpu_custom_call" | custom-call | flops 196608 | bytes 786432 | tf_op jit(solution)/shard_map/add_blocks/pallas_call | solution.py:276
  52.1 1.3 %collective-permute-start.17 = (bf16[192,512]{1,0:T(8,128)(2,1)}, bf16[192,512]{1,0:T(8,128)(2,1)S(1)}, u32[]{:S(2)}, u32[]{:S(2)}) collective-permute-start(bf16[192,512]{1,0:T(8,128)(2,1)} %add_blocks.2.refs_0_), channel_id=1, source_target_pairs={{1,0},{2,1},{3,2},{5,4},{6,5},{7,6},{9,8},{10,9},{11,10},{13,12},{... | collective-permute-start | bytes 589832 | tf_op jit(solution)/shard_map/ppermute | solution.py:293
  53.4 3.7 %collective-permute-start.14 = (bf16[192,512]{1,0:T(8,128)(2,1)}, bf16[192,512]{1,0:T(8,128)(2,1)S(1)}, u32[]{:S(2)}, u32[]{:S(2)}) collective-permute-start(bf16[192,512]{1,0:T(8,128)(2,1)} %add_blocks.2.refs_0_), channel_id=1, source_target_pairs={{0,2},{1,3},{2,0},{3,1},{4,6},{5,7},{6,4},{7,5},{8,10},{9,11},{10,... | collective-permute-start | bytes 589832 | tf_op jit(solution)/shard_map/ppermute | solution.py:291
  57.2 0.5 copy-done.25
  57.8 1.7 %add_blocks.3.refs_0_ = bf16[192,512]{1,0:T(8,128)(2,1)} custom-call(bf16[48,512]{1,0:T(8,128)(2,1)} %get-tuple-element.49.refs_0_, bf16[48,512]{1,0:T(8,128)(2,1)} %copy-done.16, bf16[48,512]{1,0:T(8,128)(2,1)} %copy-done.17, bf16[48,512]{1,0:T(8,128)(2,1)} %copy-done.21, bf16[48,512]{1,0:T(8,128)(2,1)} %copy-done.23, bf16[48,512]{1,0:T(8,128)(2,1)} %copy-done.25, ...), custom_call_target="tpu_custom_call" | custom-call | flops 196608 | bytes 786432 | tf_op jit(solution)/shard_map/add_blocks/pallas_call | solution.py:276
  59.5 3.8 %collective-permute-start.16 = (bf16[192,512]{1,0:T(8,128)(2,1)}, bf16[192,512]{1,0:T(8,128)(2,1)S(1)}, u32[]{:S(2)}, u32[]{:S(2)}) collective-permute-start(bf16[192,512]{1,0:T(8,128)(2,1)} %add_blocks.2.refs_0_), channel_id=1, source_target_pairs={{0,1},{1,2},{2,3},{4,5},{5,6},{6,7},{8,9},{9,10},{10,11},{12,13},{... | collective-permute-start | bytes 589832 | tf_op jit(solution)/shard_map/ppermute | solution.py:292
  63.3 1.3 %collective-permute-start.35 = (bf16[192,512]{1,0:T(8,128)(2,1)}, bf16[192,512]{1,0:T(8,128)(2,1)S(1)}, u32[]{:S(2)}, u32[]{:S(2)}) collective-permute-start(bf16[192,512]{1,0:T(8,128)(2,1)} %add_blocks.3.refs_0_), channel_id=1, source_target_pairs={{1,0},{2,1},{3,2},{5,4},{6,5},{7,6},{9,8},{10,9},{11,10},{13,12},{... | collective-permute-start | bytes 589832 | tf_op jit(solution)/shard_map/ppermute | solution.py:293
  64.6 8.2 %collective-permute-start.34 = (bf16[192,512]{1,0:T(8,128)(2,1)}, bf16[192,512]{1,0:T(8,128)(2,1)S(1)}, u32[]{:S(2)}, u32[]{:S(2)}) collective-permute-start(bf16[192,512]{1,0:T(8,128)(2,1)} %add_blocks.3.refs_0_), channel_id=1, source_target_pairs={{0,1},{1,2},{2,3},{4,5},{5,6},{6,7},{8,9},{9,10},{10,11},{12,13},{... | collective-permute-start | bytes 589832 | tf_op jit(solution)/shard_map/ppermute | solution.py:292
  72.9 2.8 %collective-permute-done.14.refs_2_ = bf16[192,512]{1,0:T(8,128)(2,1)S(1)} collective-permute-done((bf16[192,512]{1,0:T(8,128)(2,1)}, bf16[192,512]{1,0:T(8,128)(2,1)S(1)}, u32[]{:S(2)}, u32[]{:S(2)}) %collective-permute-start.14) | collective-permute-done | bytes 196640 | tf_op jit(solution)/shard_map/ppermute | solution.py:291
  75.7 1.3 %collective-permute-start.15 = (bf16[192,512]{1,0:T(8,128)(2,1)S(1)}, bf16[192,512]{1,0:T(8,128)(2,1)S(1)}, u32[]{:S(2)}, u32[]{:S(2)}) collective-permute-start(bf16[192,512]{1,0:T(8,128)(2,1)S(1)} %collective-permute-done.14.refs_2_), channel_id=1, source_target_pairs={{2,3},{1,0},{6,7},{5,4},{10,11},{9,8},{14,15},{13,12},{18,19},{17,... | collective-permute-start | bytes 589832 | tf_op jit(solution)/shard_map/ppermute | solution.py:294
  77.0 2.9 %collective-permute-done.32.refs_2_ = bf16[192,512]{1,0:T(8,128)(2,1)S(1)} collective-permute-done((bf16[192,512]{1,0:T(8,128)(2,1)}, bf16[192,512]{1,0:T(8,128)(2,1)S(1)}, u32[]{:S(2)}, u32[]{:S(2)}) %collective-permute-start.32) | collective-permute-done | bytes 196640 | tf_op jit(solution)/shard_map/ppermute | solution.py:291
  79.9 1.3 %collective-permute-start.33 = (bf16[192,512]{1,0:T(8,128)(2,1)S(1)}, bf16[192,512]{1,0:T(8,128)(2,1)S(1)}, u32[]{:S(2)}, u32[]{:S(2)}) collective-permute-start(bf16[192,512]{1,0:T(8,128)(2,1)S(1)} %collective-permute-done.32.refs_2_), channel_id=1, source_target_pairs={{2,3},{1,0},{6,7},{5,4},{10,11},{9,8},{14,15},{13,12},{18,19},{17,... | collective-permute-start | bytes 589832 | tf_op jit(solution)/shard_map/ppermute | solution.py:294
  81.2 1.9 %weights.1.weight_ref = bf16[768,512]{1,0:T(8,128)(2,1)} custom-call(s32[8,512]{1,0:T(8,128)} %bitcast.4, f32[8,512]{1,0:T(8,128)} %bitcast.7, f32[16,512]{1,0:T(8,128)} %get-tuple-element.30.key_ref), custom_call_target="tpu_custom_call" | custom-call | flops 393216 | bytes 786432 | tf_op jit(solution)/shard_map/weights/pallas_call | solution.py:265
  83.1 1.9 %collective-permute-done.15 = bf16[192,512]{1,0:T(8,128)(2,1)S(1)} collective-permute-done((bf16[192,512]{1,0:T(8,128)(2,1)S(1)}, bf16[192,512]{1,0:T(8,128)(2,1)S(1)}, u32[]{:S(2)}, u32[]{:S(2)}) %collective-permute-start.15) | collective-permute-done | bytes 196640 | tf_op jit(solution)/shard_map/ppermute | solution.py:294
  85.0 2.5 %collective-permute-done.33 = bf16[192,512]{1,0:T(8,128)(2,1)S(1)} collective-permute-done((bf16[192,512]{1,0:T(8,128)(2,1)S(1)}, bf16[192,512]{1,0:T(8,128)(2,1)S(1)}, u32[]{:S(2)}, u32[]{:S(2)}) %collective-permute-start.33) | collective-permute-done | bytes 196640 | tf_op jit(solution)/shard_map/ppermute | solution.py:294
  87.5 1.0 broadcast_select_fusion
  88.4 2.8 %gate_grad.1 = f32[8,512]{1,0:T(8,128)} custom-call(s32[8,512]{1,0:T(8,128)} %bitcast.5, f32[16,512]{1,0:T(8,128)} %get-tuple-element.30.key_ref, bf16[512,512]{1,0:T(8,128)(2,1)} %grads_ref.1, bf16[192,512]{1,0:T(8,128)(2,1)} %add_blocks.2.refs_0_, bf16[192,512]{1,0:T(8,128)(2,1)} %get-tuple-element.61.refs_1_, bf16[192,512]{1,0:T(8,128)(2,1)} %copy-done, ...), custom_call_target="tpu_custom_call" | custom-call | flops 402653184 | bytes 786432 | tf_op jit(solution)/shard_map/gate_grad/pallas_call | solution.py:314
  91.3 11.3 %psum.7 = f32[512,8]{0,1:T(8,128)} all-reduce(f32[512,8]{0,1:T(8,128)} %bitcast.6), channel_id=1, replica_groups=mesh['dp'=2,'tensor'=4,'expert'=4] {'tensor'}, use_global_device_ids=true, to_apply=%region_0.1 | all-reduce | flops 4096 | bytes 32768 | tf_op jit(solution)/shard_map/psum | solution.py:323
  102.5 2.8 %combine.2 = bf16[512,512]{1,0:T(8,128)(2,1)} custom-call(bf16[768,512]{1,0:T(8,128)(2,1)} %weights.1.weight_ref, bf16[192,512]{1,0:T(8,128)(2,1)} %add_blocks.2.refs_0_, bf16[192,512]{1,0:T(8,128)(2,1)} %get-tuple-element.61.refs_1_, bf16[192,512]{1,0:T(8,128)(2,1)} %copy-done, bf16[192,512]{1,0:T(8,128)(2,1)} %get-tuple-element.62.refs_3_), custom_call_target="tpu_custom_call" | custom-call | flops 402653184 | bytes 1572864 | tf_op jit(solution)/shard_map/combine/pallas_call | solution.py:299
  105.3 2.8 %combine.3 = bf16[512,512]{1,0:T(8,128)(2,1)} custom-call(bf16[768,512]{1,0:T(8,128)(2,1)} %weights.1.weight_ref, bf16[192,512]{1,0:T(8,128)(2,1)} %add_blocks.3.refs_0_, bf16[192,512]{1,0:T(8,128)(2,1)} %get-tuple-element.58.refs_1_, bf16[192,512]{1,0:T(8,128)(2,1)} %copy-done.1, bf16[192,512]{1,0:T(8,128)(2,1)} %get-tuple-element.57.refs_3_), custom_call_target="tpu_custom_call" | custom-call | flops 402653184 | bytes 1572864 | tf_op jit(solution)/shard_map/combine/pallas_call | solution.py:299
  (110 shorter events, 0.6 us)
Async XLA Ops:
  2.7 9.5 %collective-permute-start.3 = (bf16[48,512]{1,0:T(8,128)(2,1)}, bf16[48,512]{1,0:T(8,128)(2,1)S(1)}, u32[]{:S(2)}, u32[]{:S(2)}) collective-permute-start(bf16[48,512]{1,0:T(8,128)(2,1)} %get-tuple-element.31.refs_0_), channel_id=1, source_target_pairs={{0,16},{4,20},{8,24},{12,28},{16,0},{20,4},{24,8},{28,12},{1,17},{... | collective-permute-start | bytes 147464 | tf_op jit(solution)/shard_map/ppermute | solution.py:219
  5.7 6.6 %collective-permute-start.4 = (bf16[48,512]{1,0:T(8,128)(2,1)}, bf16[48,512]{1,0:T(8,128)(2,1)S(1)}, u32[]{:S(2)}, u32[]{:S(2)}) collective-permute-start(bf16[48,512]{1,0:T(8,128)(2,1)} %get-tuple-element.32), channel_id=1, source_target_pairs={{0,20},{4,24},{8,28},{12,16},{16,4},{20,8},{24,12},{28,0},{1,21},{... | collective-permute-start | bytes 147464 | tf_op jit(solution)/shard_map/ppermute | solution.py:219
  5.7 6.9 %collective-permute-start = (bf16[48,512]{1,0:T(8,128)(2,1)}, bf16[48,512]{1,0:T(8,128)(2,1)S(1)}, u32[]{:S(2)}, u32[]{:S(2)}) collective-permute-start(bf16[48,512]{1,0:T(8,128)(2,1)} %get-tuple-element.32), channel_id=1, source_target_pairs={{0,4},{4,8},{8,12},{12,0},{16,20},{20,24},{24,28},{28,16},{1,5},{5... | collective-permute-start | bytes 147464 | tf_op jit(solution)/shard_map/ppermute | solution.py:219
  7.2 7.3 %collective-permute-start.5 = (bf16[48,512]{1,0:T(8,128)(2,1)}, bf16[48,512]{1,0:T(8,128)(2,1)S(1)}, u32[]{:S(2)}, u32[]{:S(2)}) collective-permute-start(bf16[48,512]{1,0:T(8,128)(2,1)} %get-tuple-element.33), channel_id=1, source_target_pairs={{0,24},{4,28},{8,16},{12,20},{16,8},{20,12},{24,0},{28,4},{1,25},{... | collective-permute-start | bytes 147464 | tf_op jit(solution)/shard_map/ppermute | solution.py:219
  8.7 5.8 %collective-permute-start.1 = (bf16[48,512]{1,0:T(8,128)(2,1)}, bf16[48,512]{1,0:T(8,128)(2,1)S(1)}, u32[]{:S(2)}, u32[]{:S(2)}) collective-permute-start(bf16[48,512]{1,0:T(8,128)(2,1)} %get-tuple-element.33), channel_id=1, source_target_pairs={{0,8},{4,12},{8,0},{12,4},{16,24},{20,28},{24,16},{28,20},{1,9},{5... | collective-permute-start | bytes 147464 | tf_op jit(solution)/shard_map/ppermute | solution.py:219
  12.2 3.9 %collective-permute-start.6 = (bf16[48,512]{1,0:T(8,128)(2,1)}, bf16[48,512]{1,0:T(8,128)(2,1)S(1)}, u32[]{:S(2)}, u32[]{:S(2)}) collective-permute-start(bf16[48,512]{1,0:T(8,128)(2,1)} %get-tuple-element.34), channel_id=1, source_target_pairs={{0,28},{4,16},{8,20},{12,24},{16,12},{20,0},{24,4},{28,8},{1,29},{... | collective-permute-start | bytes 147464 | tf_op jit(solution)/shard_map/ppermute | solution.py:219
  12.3 5.3 %collective-permute-start.2 = (bf16[48,512]{1,0:T(8,128)(2,1)}, bf16[48,512]{1,0:T(8,128)(2,1)S(1)}, u32[]{:S(2)}, u32[]{:S(2)}) collective-permute-start(bf16[48,512]{1,0:T(8,128)(2,1)} %get-tuple-element.34), channel_id=1, source_target_pairs={{0,12},{4,0},{8,4},{12,8},{16,28},{20,16},{24,20},{28,24},{1,13},{... | collective-permute-start | bytes 147464 | tf_op jit(solution)/shard_map/ppermute | solution.py:219
  12.6 6.6 %collective-permute-start.21 = (bf16[48,512]{1,0:T(8,128)(2,1)}, bf16[48,512]{1,0:T(8,128)(2,1)S(1)}, u32[]{:S(2)}, u32[]{:S(2)}) collective-permute-start(bf16[48,512]{1,0:T(8,128)(2,1)} %get-tuple-element.43.refs_0_), channel_id=1, source_target_pairs={{0,16},{4,20},{8,24},{12,28},{16,0},{20,4},{24,8},{28,12},{1,17},{... | collective-permute-start | bytes 147464 | tf_op jit(solution)/shard_map/ppermute | solution.py:219
  14.6 4.6 %collective-permute-start.22 = (bf16[48,512]{1,0:T(8,128)(2,1)}, bf16[48,512]{1,0:T(8,128)(2,1)S(1)}, u32[]{:S(2)}, u32[]{:S(2)}) collective-permute-start(bf16[48,512]{1,0:T(8,128)(2,1)} %get-tuple-element.44), channel_id=1, source_target_pairs={{0,20},{4,24},{8,28},{12,16},{16,4},{20,8},{24,12},{28,0},{1,21},{... | collective-permute-start | bytes 147464 | tf_op jit(solution)/shard_map/ppermute | solution.py:219
  14.6 12.7 %collective-permute-start.18 = (bf16[48,512]{1,0:T(8,128)(2,1)}, bf16[48,512]{1,0:T(8,128)(2,1)S(1)}, u32[]{:S(2)}, u32[]{:S(2)}) collective-permute-start(bf16[48,512]{1,0:T(8,128)(2,1)} %get-tuple-element.44), channel_id=1, source_target_pairs={{0,4},{4,8},{8,12},{12,0},{16,20},{20,24},{24,28},{28,16},{1,5},{5... | collective-permute-start | bytes 147464 | tf_op jit(solution)/shard_map/ppermute | solution.py:219
  16.1 11.2 %collective-permute-start.23 = (bf16[48,512]{1,0:T(8,128)(2,1)}, bf16[48,512]{1,0:T(8,128)(2,1)S(1)}, u32[]{:S(2)}, u32[]{:S(2)}) collective-permute-start(bf16[48,512]{1,0:T(8,128)(2,1)} %get-tuple-element.45), channel_id=1, source_target_pairs={{0,24},{4,28},{8,16},{12,20},{16,8},{20,12},{24,0},{28,4},{1,25},{... | collective-permute-start | bytes 147464 | tf_op jit(solution)/shard_map/ppermute | solution.py:219
  17.6 9.7 %collective-permute-start.19 = (bf16[48,512]{1,0:T(8,128)(2,1)}, bf16[48,512]{1,0:T(8,128)(2,1)S(1)}, u32[]{:S(2)}, u32[]{:S(2)}) collective-permute-start(bf16[48,512]{1,0:T(8,128)(2,1)} %get-tuple-element.45), channel_id=1, source_target_pairs={{0,8},{4,12},{8,0},{12,4},{16,24},{20,28},{24,16},{28,20},{1,9},{5... | collective-permute-start | bytes 147464 | tf_op jit(solution)/shard_map/ppermute | solution.py:219
  19.1 8.2 %collective-permute-start.24 = (bf16[48,512]{1,0:T(8,128)(2,1)}, bf16[48,512]{1,0:T(8,128)(2,1)S(1)}, u32[]{:S(2)}, u32[]{:S(2)}) collective-permute-start(bf16[48,512]{1,0:T(8,128)(2,1)} %get-tuple-element.46), channel_id=1, source_target_pairs={{0,28},{4,16},{8,20},{12,24},{16,12},{20,0},{24,4},{28,8},{1,29},{... | collective-permute-start | bytes 147464 | tf_op jit(solution)/shard_map/ppermute | solution.py:219
  19.2 8.2 %collective-permute-start.20 = (bf16[48,512]{1,0:T(8,128)(2,1)}, bf16[48,512]{1,0:T(8,128)(2,1)S(1)}, u32[]{:S(2)}, u32[]{:S(2)}) collective-permute-start(bf16[48,512]{1,0:T(8,128)(2,1)} %get-tuple-element.46), channel_id=1, source_target_pairs={{0,12},{4,0},{8,4},{12,8},{16,28},{20,16},{24,20},{28,24},{1,13},{... | collective-permute-start | bytes 147464 | tf_op jit(solution)/shard_map/ppermute | solution.py:219
  28.0 9.3 %copy-start.36 = (bf16[48,512]{1,0:T(8,128)(2,1)S(1)}, bf16[48,512]{1,0:T(8,128)(2,1)}, u32[]{:S(2)}) copy-start(bf16[48,512]{1,0:T(8,128)(2,1)} %get-tuple-element.36) | copy-start | bytes 147460
  28.0 9.8 %copy-start.35 = (bf16[48,512]{1,0:T(8,128)(2,1)S(1)}, bf16[48,512]{1,0:T(8,128)(2,1)}, u32[]{:S(2)}) copy-start(bf16[48,512]{1,0:T(8,128)(2,1)} %get-tuple-element.37) | copy-start | bytes 147460
  28.0 11.1 %copy-start.34 = (bf16[48,512]{1,0:T(8,128)(2,1)S(1)}, bf16[48,512]{1,0:T(8,128)(2,1)}, u32[]{:S(2)}) copy-start(bf16[48,512]{1,0:T(8,128)(2,1)} %get-tuple-element.38) | copy-start | bytes 147460
  28.0 11.6 %copy-start.33 = (bf16[48,512]{1,0:T(8,128)(2,1)S(1)}, bf16[48,512]{1,0:T(8,128)(2,1)}, u32[]{:S(2)}) copy-start(bf16[48,512]{1,0:T(8,128)(2,1)} %get-tuple-element.39) | copy-start | bytes 147460
  28.0 13.0 %copy-start.32 = (bf16[48,512]{1,0:T(8,128)(2,1)S(1)}, bf16[48,512]{1,0:T(8,128)(2,1)}, u32[]{:S(2)}) copy-start(bf16[48,512]{1,0:T(8,128)(2,1)} %get-tuple-element.40) | copy-start | bytes 147460
  28.0 13.6 %copy-start.31 = (bf16[48,512]{1,0:T(8,128)(2,1)S(1)}, bf16[48,512]{1,0:T(8,128)(2,1)}, u32[]{:S(2)}) copy-start(bf16[48,512]{1,0:T(8,128)(2,1)} %get-tuple-element.41) | copy-start | bytes 147460
  28.0 15.5 %copy-start.30 = (bf16[48,512]{1,0:T(8,128)(2,1)S(1)}, bf16[48,512]{1,0:T(8,128)(2,1)}, u32[]{:S(2)}) copy-start(bf16[48,512]{1,0:T(8,128)(2,1)} %get-tuple-element.42) | copy-start | bytes 147460
  35.9 3.8 %collective-permute-start.25 = (bf16[48,512]{1,0:T(8,128)(2,1)}, bf16[48,512]{1,0:T(8,128)(2,1)S(1)}, u32[]{:S(2)}, u32[]{:S(2)}) collective-permute-start(bf16[48,512]{1,0:T(8,128)(2,1)} %get-tuple-element.50), channel_id=1, source_target_pairs={{0,4},{4,8},{8,12},{12,0},{16,20},{20,24},{24,28},{28,16},{1,5},{5... | collective-permute-start | bytes 147464 | tf_op jit(solution)/shard_map/ppermute | solution.py:219
  35.9 5.1 %collective-permute-start.26 = (bf16[48,512]{1,0:T(8,128)(2,1)}, bf16[48,512]{1,0:T(8,128)(2,1)S(1)}, u32[]{:S(2)}, u32[]{:S(2)}) collective-permute-start(bf16[48,512]{1,0:T(8,128)(2,1)} %get-tuple-element.51), channel_id=1, source_target_pairs={{0,8},{4,12},{8,0},{12,4},{16,24},{20,28},{24,16},{28,20},{1,9},{5... | collective-permute-start | bytes 147464 | tf_op jit(solution)/shard_map/ppermute | solution.py:219
  37.3 4.3 %collective-permute-start.7 = (bf16[48,512]{1,0:T(8,128)(2,1)S(1)}, bf16[48,512]{1,0:T(8,128)(2,1)S(1)}, u32[]{:S(2)}, u32[]{:S(2)}) collective-permute-start(bf16[48,512]{1,0:T(8,128)(2,1)S(1)} %copy-done.36), channel_id=1, source_target_pairs={{0,4},{4,8},{8,12},{12,0},{16,20},{20,24},{24,28},{28,16},{1,5},{5... | collective-permute-start | bytes 147464 | tf_op jit(solution)/shard_map/ppermute | solution.py:219
  37.8 5.7 %collective-permute-start.8 = (bf16[48,512]{1,0:T(8,128)(2,1)S(1)}, bf16[48,512]{1,0:T(8,128)(2,1)S(1)}, u32[]{:S(2)}, u32[]{:S(2)}) collective-permute-start(bf16[48,512]{1,0:T(8,128)(2,1)S(1)} %copy-done.35), channel_id=1, source_target_pairs={{0,8},{4,12},{8,0},{12,4},{16,24},{20,28},{24,16},{28,20},{1,9},{5... | collective-permute-start | bytes 147464 | tf_op jit(solution)/shard_map/ppermute | solution.py:219
  39.1 6.4 %collective-permute-start.9 = (bf16[48,512]{1,0:T(8,128)(2,1)S(1)}, bf16[48,512]{1,0:T(8,128)(2,1)S(1)}, u32[]{:S(2)}, u32[]{:S(2)}) collective-permute-start(bf16[48,512]{1,0:T(8,128)(2,1)S(1)} %copy-done.34), channel_id=1, source_target_pairs={{0,12},{4,0},{8,4},{12,8},{16,28},{20,16},{24,20},{28,24},{1,13},{... | collective-permute-start | bytes 147464 | tf_op jit(solution)/shard_map/ppermute | solution.py:219
  39.6 17.5 %copy-start.16 = (bf16[48,512]{1,0:T(8,128)(2,1)}, bf16[48,512]{1,0:T(8,128)(2,1)S(1)}, u32[]{:S(2)}) copy-start(bf16[48,512]{1,0:T(8,128)(2,1)S(1)} %collective-permute-done.25.refs_1_) | copy-start | bytes 147460
  39.7 5.9 %collective-permute-start.10 = (bf16[48,512]{1,0:T(8,128)(2,1)S(1)}, bf16[48,512]{1,0:T(8,128)(2,1)S(1)}, u32[]{:S(2)}, u32[]{:S(2)}) collective-permute-start(bf16[48,512]{1,0:T(8,128)(2,1)S(1)} %copy-done.33), channel_id=1, source_target_pairs={{0,16},{4,20},{8,24},{12,28},{16,0},{20,4},{24,8},{28,12},{1,17},{... | collective-permute-start | bytes 147464 | tf_op jit(solution)/shard_map/ppermute | solution.py:219
  41.0 16.2 %copy-start.17 = (bf16[48,512]{1,0:T(8,128)(2,1)}, bf16[48,512]{1,0:T(8,128)(2,1)S(1)}, u32[]{:S(2)}) copy-start(bf16[48,512]{1,0:T(8,128)(2,1)S(1)} %collective-permute-done.26.refs_2_) | copy-start | bytes 147460
  41.0 5.6 %collective-permute-start.11 = (bf16[48,512]{1,0:T(8,128)(2,1)S(1)}, bf16[48,512]{1,0:T(8,128)(2,1)S(1)}, u32[]{:S(2)}, u32[]{:S(2)}) collective-permute-start(bf16[48,512]{1,0:T(8,128)(2,1)S(1)} %copy-done.32), channel_id=1, source_target_pairs={{0,20},{4,24},{8,28},{12,16},{16,4},{20,8},{24,12},{28,0},{1,21},{... | collective-permute-start | bytes 147464 | tf_op jit(solution)/shard_map/ppermute | solution.py:219
  41.6 8.7 %copy-start.18 = (bf16[48,512]{1,0:T(8,128)(2,1)}, bf16[48,512]{1,0:T(8,128)(2,1)S(1)}, u32[]{:S(2)}) copy-start(bf16[48,512]{1,0:T(8,128)(2,1)S(1)} %collective-permute-done.7.refs_1_) | copy-start | bytes 147460
  41.6 5.8 %collective-permute-start.12 = (bf16[48,512]{1,0:T(8,128)(2,1)S(1)}, bf16[48,512]{1,0:T(8,128)(2,1)S(1)}, u32[]{:S(2)}, u32[]{:S(2)}) collective-permute-start(bf16[48,512]{1,0:T(8,128)(2,1)S(1)} %copy-done.31), channel_id=1, source_target_pairs={{0,24},{4,28},{8,16},{12,20},{16,8},{20,12},{24,0},{28,4},{1,25},{... | collective-permute-start | bytes 147464 | tf_op jit(solution)/shard_map/ppermute | solution.py:219
  43.5 5.3 %collective-permute-start.13 = (bf16[48,512]{1,0:T(8,128)(2,1)S(1)}, bf16[48,512]{1,0:T(8,128)(2,1)S(1)}, u32[]{:S(2)}, u32[]{:S(2)}) collective-permute-start(bf16[48,512]{1,0:T(8,128)(2,1)S(1)} %copy-done.30), channel_id=1, source_target_pairs={{0,28},{4,16},{8,20},{12,24},{16,12},{20,0},{24,4},{28,8},{1,29},{... | collective-permute-start | bytes 147464 | tf_op jit(solution)/shard_map/ppermute | solution.py:219
  45.5 6.6 %collective-permute-start.27 = (bf16[48,512]{1,0:T(8,128)(2,1)}, bf16[48,512]{1,0:T(8,128)(2,1)S(1)}, u32[]{:S(2)}, u32[]{:S(2)}) collective-permute-start(bf16[48,512]{1,0:T(8,128)(2,1)} %get-tuple-element.52), channel_id=1, source_target_pairs={{0,12},{4,0},{8,4},{12,8},{16,28},{20,16},{24,20},{28,24},{1,13},{... | collective-permute-start | bytes 147464 | tf_op jit(solution)/shard_map/ppermute | solution.py:219
  45.6 7.8 %collective-permute-start.28 = (bf16[48,512]{1,0:T(8,128)(2,1)}, bf16[48,512]{1,0:T(8,128)(2,1)S(1)}, u32[]{:S(2)}, u32[]{:S(2)}) collective-permute-start(bf16[48,512]{1,0:T(8,128)(2,1)} %get-tuple-element.53), channel_id=1, source_target_pairs={{0,16},{4,20},{8,24},{12,28},{16,0},{20,4},{24,8},{28,12},{1,17},{... | collective-permute-start | bytes 147464 | tf_op jit(solution)/shard_map/ppermute | solution.py:219
  46.6 10.6 %collective-permute-start.29 = (bf16[48,512]{1,0:T(8,128)(2,1)}, bf16[48,512]{1,0:T(8,128)(2,1)S(1)}, u32[]{:S(2)}, u32[]{:S(2)}) collective-permute-start(bf16[48,512]{1,0:T(8,128)(2,1)} %get-tuple-element.54), channel_id=1, source_target_pairs={{0,20},{4,24},{8,28},{12,16},{16,4},{20,8},{24,12},{28,0},{1,21},{... | collective-permute-start | bytes 147464 | tf_op jit(solution)/shard_map/ppermute | solution.py:219
  47.4 9.7 %collective-permute-start.30 = (bf16[48,512]{1,0:T(8,128)(2,1)}, bf16[48,512]{1,0:T(8,128)(2,1)S(1)}, u32[]{:S(2)}, u32[]{:S(2)}) collective-permute-start(bf16[48,512]{1,0:T(8,128)(2,1)} %get-tuple-element.55), channel_id=1, source_target_pairs={{0,24},{4,28},{8,16},{12,20},{16,8},{20,12},{24,0},{28,4},{1,25},{... | collective-permute-start | bytes 147464 | tf_op jit(solution)/shard_map/ppermute | solution.py:219
  48.8 8.4 %collective-permute-start.31 = (bf16[48,512]{1,0:T(8,128)(2,1)}, bf16[48,512]{1,0:T(8,128)(2,1)S(1)}, u32[]{:S(2)}, u32[]{:S(2)}) collective-permute-start(bf16[48,512]{1,0:T(8,128)(2,1)} %get-tuple-element.56), channel_id=1, source_target_pairs={{0,28},{4,16},{8,20},{12,24},{16,12},{20,0},{24,4},{28,8},{1,29},{... | collective-permute-start | bytes 147464 | tf_op jit(solution)/shard_map/ppermute | solution.py:219
  52.1 12.5 %collective-permute-start.17 = (bf16[192,512]{1,0:T(8,128)(2,1)}, bf16[192,512]{1,0:T(8,128)(2,1)S(1)}, u32[]{:S(2)}, u32[]{:S(2)}) collective-permute-start(bf16[192,512]{1,0:T(8,128)(2,1)} %add_blocks.2.refs_0_), channel_id=1, source_target_pairs={{1,0},{2,1},{3,2},{5,4},{6,5},{7,6},{9,8},{10,9},{11,10},{13,12},{... | collective-permute-start | bytes 589832 | tf_op jit(solution)/shard_map/ppermute | solution.py:293
  53.4 22.3 %collective-permute-start.14 = (bf16[192,512]{1,0:T(8,128)(2,1)}, bf16[192,512]{1,0:T(8,128)(2,1)S(1)}, u32[]{:S(2)}, u32[]{:S(2)}) collective-permute-start(bf16[192,512]{1,0:T(8,128)(2,1)} %add_blocks.2.refs_0_), channel_id=1, source_target_pairs={{0,2},{1,3},{2,0},{3,1},{4,6},{5,7},{6,4},{7,5},{8,10},{9,11},{10,... | collective-permute-start | bytes 589832 | tf_op jit(solution)/shard_map/ppermute | solution.py:291
  59.5 20.4 %collective-permute-start.32 = (bf16[192,512]{1,0:T(8,128)(2,1)}, bf16[192,512]{1,0:T(8,128)(2,1)S(1)}, u32[]{:S(2)}, u32[]{:S(2)}) collective-permute-start(bf16[192,512]{1,0:T(8,128)(2,1)} %add_blocks.3.refs_0_), channel_id=1, source_target_pairs={{0,2},{1,3},{2,0},{3,1},{4,6},{5,7},{6,4},{7,5},{8,10},{9,11},{10,... | collective-permute-start | bytes 589832 | tf_op jit(solution)/shard_map/ppermute | solution.py:291
  59.5 23.6 %collective-permute-start.16 = (bf16[192,512]{1,0:T(8,128)(2,1)}, bf16[192,512]{1,0:T(8,128)(2,1)S(1)}, u32[]{:S(2)}, u32[]{:S(2)}) collective-permute-start(bf16[192,512]{1,0:T(8,128)(2,1)} %add_blocks.2.refs_0_), channel_id=1, source_target_pairs={{0,1},{1,2},{2,3},{4,5},{5,6},{6,7},{8,9},{9,10},{10,11},{12,13},{... | collective-permute-start | bytes 589832 | tf_op jit(solution)/shard_map/ppermute | solution.py:292
  63.3 19.8 %collective-permute-start.35 = (bf16[192,512]{1,0:T(8,128)(2,1)}, bf16[192,512]{1,0:T(8,128)(2,1)S(1)}, u32[]{:S(2)}, u32[]{:S(2)}) collective-permute-start(bf16[192,512]{1,0:T(8,128)(2,1)} %add_blocks.3.refs_0_), channel_id=1, source_target_pairs={{1,0},{2,1},{3,2},{5,4},{6,5},{7,6},{9,8},{10,9},{11,10},{13,12},{... | collective-permute-start | bytes 589832 | tf_op jit(solution)/shard_map/ppermute | solution.py:293
  64.6 18.5 %collective-permute-start.34 = (bf16[192,512]{1,0:T(8,128)(2,1)}, bf16[192,512]{1,0:T(8,128)(2,1)S(1)}, u32[]{:S(2)}, u32[]{:S(2)}) collective-permute-start(bf16[192,512]{1,0:T(8,128)(2,1)} %add_blocks.3.refs_0_), channel_id=1, source_target_pairs={{0,1},{1,2},{2,3},{4,5},{5,6},{6,7},{8,9},{9,10},{10,11},{12,13},{... | collective-permute-start | bytes 589832 | tf_op jit(solution)/shard_map/ppermute | solution.py:292
  75.7 12.7 %copy-start = (bf16[192,512]{1,0:T(8,128)(2,1)}, bf16[192,512]{1,0:T(8,128)(2,1)S(1)}, u32[]{:S(2)}) copy-start(bf16[192,512]{1,0:T(8,128)(2,1)S(1)} %collective-permute-done.14.refs_2_) | copy-start | bytes 589828
  75.7 9.3 %collective-permute-start.15 = (bf16[192,512]{1,0:T(8,128)(2,1)S(1)}, bf16[192,512]{1,0:T(8,128)(2,1)S(1)}, u32[]{:S(2)}, u32[]{:S(2)}) collective-permute-start(bf16[192,512]{1,0:T(8,128)(2,1)S(1)} %collective-permute-done.14.refs_2_), channel_id=1, source_target_pairs={{2,3},{1,0},{6,7},{5,4},{10,11},{9,8},{14,15},{13,12},{18,19},{17,... | collective-permute-start | bytes 589832 | tf_op jit(solution)/shard_map/ppermute | solution.py:294
  79.9 25.4 %copy-start.1 = (bf16[192,512]{1,0:T(8,128)(2,1)}, bf16[192,512]{1,0:T(8,128)(2,1)S(1)}, u32[]{:S(2)}) copy-start(bf16[192,512]{1,0:T(8,128)(2,1)S(1)} %collective-permute-done.32.refs_2_) | copy-start | bytes 589828
  79.9 7.6 %collective-permute-start.33 = (bf16[192,512]{1,0:T(8,128)(2,1)S(1)}, bf16[192,512]{1,0:T(8,128)(2,1)S(1)}, u32[]{:S(2)}, u32[]{:S(2)}) collective-permute-start(bf16[192,512]{1,0:T(8,128)(2,1)S(1)} %collective-permute-done.32.refs_2_), channel_id=1, source_target_pairs={{2,3},{1,0},{6,7},{5,4},{10,11},{9,8},{14,15},{13,12},{18,19},{17,... | collective-permute-start | bytes 589832 | tf_op jit(solution)/shard_map/ppermute | solution.py:294
  (25 other events, 95.7 us)

commit v3 on v0

v3 whole, which is shorter than its diff:
```python
import functools

import jax
import jax.numpy as jnp
from jax import lax
from jax.experimental import pallas as pl
from jax.experimental.pallas import tpu as pltpu
from jax.sharding import PartitionSpec as P

CAP = 48
LANES = 128
MIB = 2**20
BF16 = jnp.bfloat16
F32 = jnp.float32
CONTRACT_LAST = (((1,), (1,)), ((), ()))


def call(kernel, name, out_shape, operands, flops, scratch=(), limit=8):
    outs = out_shape if isinstance(out_shape, list) else [out_shape]
    moved = sum(a.size * a.dtype.itemsize for a in [*operands, *outs])
    spec = pl.BlockSpec(memory_space=pltpu.VMEM)
    return pl.pallas_call(
        kernel,
        out_shape=out_shape,
        in_specs=[spec] * len(operands),
        out_specs=[spec] * len(outs) if isinstance(out_shape, list) else spec,
        scratch_shapes=list(scratch),
        compiler_params=pltpu.CompilerParams(vmem_limit_bytes=limit * MIB),
        cost_estimate=pl.CostEstimate(flops=int(flops), bytes_accessed=int(moved), transcendentals=0),
        name=name,
    )(*operands)


def number_kernel(routes_ref, key_ref):
    experts, rows = key_ref.shape
    ids = lax.broadcasted_iota(jnp.int32, (experts, rows), 0)
    hit = jnp.zeros((experts, rows), F32)
    for r in range(routes_ref.shape[0]):
        hit = hit + (routes_ref[r : r + 1, :] == ids).astype(F32)
    before = (
        lax.broadcasted_iota(jnp.int32, (LANES, LANES), 0) < lax.broadcasted_iota(jnp.int32, (LANES, LANES), 1)
    ).astype(BF16)
    offset = jnp.zeros((experts, 1), F32)
    for start in range(0, rows, LANES):
        part = hit[:, start : start + LANES]
        rank = jnp.dot(part.astype(BF16), before, preferred_element_type=F32) + offset
        offset = offset + jnp.sum(part, axis=1, keepdims=True)
        key_ref[:, start : start + LANES] = jnp.where(part > 0.0, rank, -1.0)


def position(cores):
    t = lax.axis_index("tensor")
    return lax.div(t, cores), lax.rem(t, cores), lax.axis_index("expert")


def pick_kernel(cores, key_ref, *refs):
    sources, pieces = refs[:cores], refs[cores:]
    chips = len(pieces)
    rows, width = sources[0].shape
    chip, core, e = position(cores)
    slot = lax.broadcasted_iota(jnp.int32, (CAP, rows), 0).astype(F32)
    masks = []
    for dh in range(chips):
        expert = (e * chips + lax.rem(chip + dh, chips)) * cores + core
        masks.append((key_ref[pl.ds(expert, 1), :] == slot).astype(BF16))
    mask = jnp.concatenate(masks, axis=0)
    for dc, source in enumerate(sources):
        picked = jnp.dot(mask, source[...], preferred_element_type=F32).astype(BF16)
        column = pl.multiple_of(lax.rem(core - dc + cores, cores) * width, width)
        for dh, piece in enumerate(pieces):
            piece[:, pl.ds(column, width)] = picked[dh * CAP : (dh + 1) * CAP]


def gather_pieces(x_ref, pieces, chips, cores):
    chip, _, _ = position(cores)
    width = pieces[0].shape[1]
    for index, piece in enumerate(pieces):
        db, dh = divmod(index, chips)
        column = pl.multiple_of(lax.rem(chip - dh + chips, chips) * width, width)
        x_ref[db * CAP : (db + 1) * CAP, pl.ds(column, width)] = piece[...]


def project_back(terms, pieces, chips, cores):
    chip, _, _ = position(cores)
    blocks = len(pieces) // chips
    width = pieces[0].shape[1]
    for dh in range(chips):
        column = pl.ds(pl.multiple_of(lax.rem(chip + dh, chips) * width, width), width)
        total = None
        for h_ref, w_ref in terms:
            term = jnp.dot(h_ref[...], w_ref[0, :, column], preferred_element_type=F32)
            total = term if total is None else total + term
        total = total.astype(BF16)
        for db in range(blocks):
            row = (-db) % blocks * CAP
            pieces[db * chips + dh][...] = total[row : row + CAP]


def chunks_of(hid_dev):
    size = 256 if hid_dev % 256 == 0 else hid_dev
    return [slice(start, start + size) for start in range(0, hid_dev, size)]


def forward_kernel(chips, cores, count, *refs):
    pieces, (gate_ref, up_ref, down_ref) = refs[:count], refs[count : count + 3]
    act_ref, scale_ref = refs[count + 3 : count + 5]
    outs, (x_ref, hid_ref) = refs[count + 5 : 2 * count + 5], refs[2 * count + 5 :]
    gather_pieces(x_ref, pieces, chips, cores)
    for part in chunks_of(gate_ref.shape[1]):
        gate_pre = lax.dot_general(x_ref[...], gate_ref[0, part, :], CONTRACT_LAST, preferred_element_type=F32)
        up_pre = lax.dot_general(x_ref[...], up_ref[0, part, :], CONTRACT_LAST, preferred_element_type=F32)
        sig = jax.nn.sigmoid(gate_pre)
        act = gate_pre * sig
        hid_ref[:, part] = (act * up_pre).astype(BF16)
        act_ref[:, part] = act
        scale_ref[:, part] = up_pre * (sig * (1.0 + gate_pre * (1.0 - sig)))
    project_back([(hid_ref, down_ref)], outs, chips, cores)


def backward_kernel(chips, cores, count, *refs):
    pieces, (gate_ref, up_ref, down_ref) = refs[:count], refs[count : count + 3]
    act_ref, scale_ref = refs[count + 3 : count + 5]
    outs, (x_ref, grad_gate_ref, grad_up_ref) = refs[count + 5 : 2 * count + 5], refs[2 * count + 5 :]
    gather_pieces(x_ref, pieces, chips, cores)
    for part in chunks_of(gate_ref.shape[1]):
        grad_hid = lax.dot_general(x_ref[...], down_ref[0, part, :], CONTRACT_LAST, preferred_element_type=F32)
        grad_gate_ref[:, part] = (grad_hid * scale_ref[:, part]).astype(BF16)
        grad_up_ref[:, part] = (grad_hid * act_ref[:, part]).astype(BF16)
    project_back([(grad_gate_ref, gate_ref), (grad_up_ref, up_ref)], outs, chips, cores)


def add_blocks_kernel(chips, cores, *refs):
    pieces, out_ref = refs[:-1], refs[-1]
    width = out_ref.shape[1]
    count = len(pieces) // cores
    _, core, _ = position(cores)
    column = pl.ds(pl.multiple_of(core * width, width), width)
    for dh in range(chips):
        for dc in range(cores):
            total = None
            for piece in pieces[dc * count + dh : (dc + 1) * count : chips]:
                term = piece[:, column].astype(F32)
                total = term if total is None else total + term
            row = (dh * cores + dc) * CAP
            out_ref[row : row + CAP, :] = total.astype(BF16)


def slot_experts(chips, cores, columns):
    chip, core, e = position(cores)
    experts = []
    for dz in range(columns):
        for dh in range(chips):
            for dc in range(cores):
                column = lax.rem(e - dz + columns, columns)
                owner = lax.rem(chip - dh + chips, chips)
                experts.append((column * chips + owner) * cores + lax.rem(core - dc + cores, cores))
    return experts


def weights_kernel(chips, cores, columns, routes_ref, gates_ref, key_ref, out_ref, gate_ref, all_ref):
    experts, rows = key_ref.shape
    ids = lax.broadcasted_iota(jnp.int32, (experts, rows), 0)
    gate = jnp.zeros((experts, rows), F32)
    for r in range(routes_ref.shape[0]):
        gate = gate + jnp.where(routes_ref[r : r + 1, :] == ids, gates_ref[r : r + 1, :], 0.0)
    gate_ref[...] = gate
    slot = lax.broadcasted_iota(jnp.int32, (CAP, rows), 0).astype(F32)
    for index, expert in enumerate(slot_experts(chips, cores, columns)):
        same = key_ref[pl.ds(expert, 1), :] == slot
        all_ref[index * CAP : (index + 1) * CAP, :] = jnp.where(same, gate_ref[pl.ds(expert, 1), :], 0.0)
    slots = all_ref.shape[0]
    step = LANES if slots % LANES == 0 else slots
    for start in range(0, slots, step):
        out_ref[:, start : start + step] = all_ref[start : start + step, :].T.astype(BF16)


def place_parts(parts, all_ref, columns):
    height = parts[0].shape[0]
    if len(parts) == columns:
        for index, part in enumerate(parts):
            all_ref[index * height : (index + 1) * height, :] = part[...]
        return
    own, far, up, down, ends = parts
    e = lax.axis_index("expert")
    all_ref[0:height, :] = own[...]
    all_ref[2 * height : 3 * height, :] = far[...]
    all_ref[height : 2 * height, :] = jnp.where(e == 0, ends[...], up[...])
    all_ref[3 * height : 4 * height, :] = jnp.where(e == columns - 1, ends[...], down[...])


def combine_kernel(columns, weight_ref, *refs):
    parts, (out_ref, all_ref) = refs[:-2], refs[-2:]
    place_parts(parts, all_ref, columns)
    out_ref[...] = jnp.dot(weight_ref[...], all_ref[...], preferred_element_type=F32).astype(BF16)


def combine_gate_kernel(chips, cores, columns, weight_ref, routes_ref, key_ref, grads_ref, *refs):
    parts, (out_ref, gate_ref, all_ref, sum_ref) = refs[:-4], refs[-4:]
    place_parts(parts, all_ref, columns)
    out_ref[...] = jnp.dot(weight_ref[...], all_ref[...], preferred_element_type=F32).astype(BF16)
    rows = key_ref.shape[1]
    slot = lax.broadcasted_iota(jnp.int32, (CAP, rows), 0).astype(F32)
    routes = routes_ref[...]
    sum_ref[...] = lax.dot_general(all_ref[...], grads_ref[...], CONTRACT_LAST, preferred_element_type=F32)
    total = jnp.zeros(gate_ref.shape, F32)
    for index, expert in enumerate(slot_experts(chips, cores, columns)):
        same = key_ref[pl.ds(expert, 1), :] == slot
        row = jnp.where(same, sum_ref[index * CAP : (index + 1) * CAP, :], 0.0)
        total = total + jnp.where(routes == expert, jnp.sum(row, axis=0, keepdims=True), 0.0)
    gate_ref[...] = total


def body(sizes, tokens, grad_out, routes, gates, gate_weight, up_weight, down_weight):
    n_dp, groups, columns = sizes
    cores = 2 if groups % 2 == 0 else 1
    chips = groups // cores
    experts = groups * columns
    rows, width = tokens.shape
    _, hid_dev, feats = gate_weight.shape
    count = n_dp * chips
    tall = n_dp * CAP
    slots = groups * CAP
    routes_t, gates_t = routes.T, gates.T

    def shape(height, length, dtype=BF16):
        return jax.ShapeDtypeStruct((height, length), dtype)

    def to_core(value, dc):
        if dc == 0:
            return value
        pairs = [(t, t // cores * cores + (t + dc) % cores) for t in range(groups)]
        return lax.ppermute(value, "tensor", pairs)

    def to_chip(value, db, dh):
        if (db, dh) == (0, 0):
            return value
        pairs = []
        for b in range(n_dp):
            for t in range(groups):
                target = (t // cores + dh) % chips * cores + t % cores
                pairs.append((b * groups + t, (b + db) % n_dp * groups + target))
        return lax.ppermute(value, ("dp", "tensor"), pairs)

    hops = [(db, dh) for db in range(n_dp) for dh in range(chips)]
    order = sorted(range(count), key=lambda index: (hops[index][0] == 0, -hops[index][1]))

    def dispatch(key, sources):
        pieces = call(
            functools.partial(pick_kernel, cores),
            "pick",
            [shape(CAP, cores * width)] * chips,
            [key, *sources],
            2 * slots * rows * width,
        )
        arrived = {index: to_chip(pieces[hops[index][1]], *hops[index]) for index in order}
        return [arrived[index] for index in range(count)]

    def give_back(pieces):
        arrived = {index: to_chip(pieces[index], *hops[index]) for index in order}
        pairs = [[to_core(arrived[index], dc) for index in range(count)] for dc in range(cores)]
        return call(
            functools.partial(add_blocks_kernel, chips, cores),
            "add_blocks",
            shape(slots, width),
            sum(pairs, []),
            2 * slots * width,
        )

    token_sources = [to_core(tokens, dc) for dc in range(cores)]
    grad_sources = [to_core(grad_out, dc) for dc in range(cores)]
    key = call(number_kernel, "number", shape(experts, rows, F32), [routes_t], experts * rows * LANES)
    tok_in = dispatch(key, token_sources)
    grad_in = dispatch(key, grad_sources)

    matmul_flops = 2 * tall * hid_dev * feats
    saved = [shape(tall, hid_dev, F32)] * 2
    piece = [shape(CAP, cores * width)] * count
    act, scale, *outs = call(
        functools.partial(forward_kernel, chips, cores, count),
        "forward",
        saved + piece,
        [*tok_in, gate_weight, up_weight, down_weight],
        3 * matmul_flops,
        [pltpu.VMEM((tall, feats), BF16), pltpu.VMEM((tall, hid_dev), BF16)],
        limit=24,
    )
    out_rows = give_back(outs)
    backs = call(
        functools.partial(backward_kernel, chips, cores, count),
        "backward",
        piece,
        [*grad_in, gate_weight, up_weight, down_weight, act, scale],
        3 * matmul_flops,
        [pltpu.VMEM((tall, feats), BF16)] + [pltpu.VMEM((tall, hid_dev), BF16)] * 2,
        limit=24,
    )
    back_rows = give_back(backs)

    weight_map = call(
        functools.partial(weights_kernel, chips, cores, columns),
        "weights",
        shape(rows, experts * CAP),
        [routes_t, gates_t, key],
        experts * CAP * rows,
        [pltpu.VMEM((experts, rows), F32), pltpu.VMEM((experts * CAP, rows), F32)],
        limit=16,
    )

    def across(value):
        if columns != 4:
            return [value] + [
                lax.ppermute(value, "expert", [(z, (z + dz) % columns) for z in range(columns)])
                for dz in range(1, columns)
            ]
        far = lax.ppermute(value, "expert", [(z, (z + 2) % columns) for z in range(columns)])
        up = lax.ppermute(value, "expert", [(z, z + 1) for z in range(columns - 1)])
        down = lax.ppermute(value, "expert", [(z + 1, z) for z in range(columns - 1)])
        ends = lax.ppermute(far, "expert", [(2, 3), (1, 0)])
        return [value, far, up, down, ends]

    out_parts = across(out_rows)
    back_parts = across(back_rows)
    combine_flops = 2 * experts * CAP * rows * width
    all_rows = pltpu.VMEM((experts * CAP, width), BF16)
    mixed, gate_part = call(
        functools.partial(combine_gate_kernel, chips, cores, columns),
        "combine_gate",
        [shape(rows, width), shape(routes_t.shape[0], rows, F32)],
        [weight_map, routes_t, key, grad_out, *out_parts],
        2 * combine_flops,
        [all_rows, pltpu.VMEM((experts * CAP, rows), F32)],
        limit=24,
    )
    for dc in range(1, cores):
        gate_part = gate_part + to_core(gate_part, dc)
    total = gate_part
    for dh in range(1, chips):
        total = total + to_chip(gate_part, 0, dh)
    grad_tokens = call(
        functools.partial(combine_kernel, columns),
        "combine",
        shape(rows, width),
        [weight_map, *back_parts],
        combine_flops,
        [all_rows],
        limit=16,
    )
    return (mixed, grad_tokens, total.T)


def solution(mesh):
    sizes = (mesh.shape["dp"], mesh.shape["tensor"], mesh.shape["expert"])
    return jax.shard_map(
        functools.partial(body, sizes),
        mesh=mesh,
        in_specs=(
            P("dp", "tensor"),
            P("dp", "tensor"),
            P("dp", None),
            P("dp", None),
            P(("expert", "tensor"), "dp", None),
            P(("expert", "tensor"), "dp", None),
            P(("expert", "tensor"), "dp", None),
        ),
        out_specs=(P("dp", "tensor"), P("dp", "tensor"), P("dp", None)),
        check_vma=False,
    )
```

time: 215 us -> 75 us (0.35)
  blocking collectives: 77.8 us -> 0 us
  other arithmetic: 29.5 us -> 0.61 us
  local copies, waits for them, and re-layouts: 34.2 us -> 8.5 us
  matrix products: 22.7 us -> 0 us
  starting transfers between devices: 15.5 us -> 35.4 us
  between operations: 14.2 us -> 0.87 us
  Pallas kernels: 0 us -> 9.28 us
    psum x1 -> x0, blocking collectives: 63.5 us -> none  [body(): grad_gates = lax.psum(gate_part, ('expert', 'tensor'))]
    ppermute x0 -> x32, starting transfers between devices: none -> 35.4 us  [the longest x13 17.5 us: to_chip(): return lax.ppermute(value, ('dp', 'tensor'), pairs)]
    unnamed x3 -> x0, other arithmetic: 26.8 us -> none
    dot_general x9 -> x0, matrix products: 22.7 us -> none  [the longest x1 3.97 us: body(): jnp.dot(weight_map, back_slots, preferred_element_type=jnp.float32)]
    ppermute x0 -> x32, waiting for transfers between devices: none -> 19.8 us  [the longest x2 9.27 us: across(): lax.ppermute(value, 'expert', [(z, (z + 2) % columns) for z in range(colu...]
    all_to_all x4 -> x0, starting transfers between devices: 15.2 us -> none  [the longest x1 4.21 us: body(): lax.all_to_all(grad_slots, 'tensor', split_axis=0, concat_axis=2, tiled=T...]
    all_gather x2 -> x0, blocking collectives: 14.3 us -> none  [the longest x1 7.59 us: body(): row_block = lax.all_gather(tok_full[0], 'dp', axis=0, tiled=True)]
    reduce_scatter x2 -> x0, waiting for transfers between devices: 11.2 us -> none  [the longest x1 11.2 us: body(): lax.psum_scatter(jnp.dot(row_block, stacked, preferred_element_type=jnp.f...]
  transfers between devices with their start and end apart: 7 -> 32, of which waited for: 3 -> 10; matrix products, arithmetic and copies ran while one was open for 24% -> 0% of each run, Pallas kernels for 0% -> 12%
where the time goes in v3:
time: 75 us; the launch traced here: 74.5 us
  starting transfers between devices  35.4 us (47%)
  waiting for transfers between devices  19.8 us (26%)
  Pallas kernels  9.28 us (12%)
  local copies, waits for them, and re-layouts  8.5 us (11%)
  between operations  0.87 us (1%)
    ppermute x13, starting transfers between devices, to_chip(): return lax.ppermute(value, ('dp', 'tensor'), pairs)  17.5 us
    pallas_call x10, Pallas kernels, call(): pl.pallas_call(kernel, out_shape=out_shape, in_specs=[spec] * len(operand...  9.28 us
    ppermute x2, waiting for transfers between devices, across(): lax.ppermute(value, 'expert', [(z, (z + 2) % columns) for z in range(colu...  9.27 us
    unnamed x24, local copies, waits for them, and re-layouts  8.5 us
    ppermute x2, starting transfers between devices, across(): up = lax.ppermute(value, 'expert', [(z, z + 1) for z in range(columns - 1)])  8.05 us
    ppermute x13, waiting for transfers between devices, to_chip(): return lax.ppermute(value, ('dp', 'tensor'), pairs)  4.95 us
    ppermute x2, starting transfers between devices, across(): lax.ppermute(value, 'expert', [(z, (z + 2) % columns) for z in range(colu...  3.04 us
    ppermute x2, waiting for transfers between devices, across(): ends = lax.ppermute(far, 'expert', [(2, 3), (1, 0)])  2.6 us
  transfers between devices with their start and end apart: 32, of which 10 were waited for; matrix products, arithmetic and copies ran while one was open for 0% of the time, Pallas kernels for 12%

profile of v3, /device:TPU:0, one launch (start us, length us, event | category | flops | bytes accessed | tf_op | source)
XLA Modules:
  0.0 74.5 jit_solution(5681238369749961032)
XLA Ops:
  0.6 0.5 collective-permute-start
  1.2 0.7 copy-done.9
  1.9 0.1 number.1.key_ref
  2.1 0.8 %collective-permute-done.refs_1_ = bf16[512,512]{1,0:T(8,128)(2,1)S(1)} collective-permute-done((bf16[512,512]{1,0:T(8,128)(2,1)}, bf16[512,512]{1,0:T(8,128)(2,1)S(1)}, u32[]{:S(2)}, u32[]{:S(2)}) %collective-permute-start) | collective-permute-done | bytes 524320 | tf_op jit(solution)/shard_map/ppermute | solution.py:232
  2.9 1.0 %copy-done.6 = bf16[512,512]{1,0:T(8,128)(2,1)S(1)} copy-done((bf16[512,512]{1,0:T(8,128)(2,1)S(1)}, bf16[512,512]{1,0:T(8,128)(2,1)}, u32[]{:S(2)}) %copy-start.6) | copy-done | bytes 524312
  3.9 0.3 pick.2
  4.2 2.9 %collective-permute-start.1 = (bf16[48,1024]{1,0:T(8,128)(2,1)S(1)}, bf16[48,1024]{1,0:T(8,128)(2,1)S(1)}, u32[]{:S(2)}, u32[]{:S(2)}) collective-permute-start(bf16[48,1024]{1,0:T(8,128)(2,1)S(1)} %get-tuple-element.20), channel_id=1, source_target_pairs={{0,8},{4,12},{8,0},{12,4},{16,24},{20,28},{24,16},{28,20},{1,9},{5... | collective-permute-start | bytes 294920 | tf_op jit(solution)/shard_map/ppermute | solution.py:242
  7.2 1.5 %collective-permute-start.2 = (bf16[48,1024]{1,0:T(8,128)(2,1)S(1)}, bf16[48,1024]{1,0:T(8,128)(2,1)S(1)}, u32[]{:S(2)}, u32[]{:S(2)}) collective-permute-start(bf16[48,1024]{1,0:T(8,128)(2,1)S(1)} %get-tuple-element.19.refs_0_), channel_id=1, source_target_pairs={{0,16},{4,20},{8,24},{12,28},{16,0},{20,4},{24,8},{28,12},{1,17},{... | collective-permute-start | bytes 294920 | tf_op jit(solution)/shard_map/ppermute | solution.py:242
  8.7 1.0 %copy-done.7 = bf16[512,512]{1,0:T(8,128)(2,1)S(1)} copy-done((bf16[512,512]{1,0:T(8,128)(2,1)S(1)}, bf16[512,512]{1,0:T(8,128)(2,1)}, u32[]{:S(2)}) %copy-start.7) | copy-done | bytes 524312
  9.8 0.3 pick.3
  10.1 2.0 %collective-permute-start.16 = (bf16[48,1024]{1,0:T(8,128)(2,1)S(1)}, bf16[48,1024]{1,0:T(8,128)(2,1)S(1)}, u32[]{:S(2)}, u32[]{:S(2)}) collective-permute-start(bf16[48,1024]{1,0:T(8,128)(2,1)S(1)} %get-tuple-element.27), channel_id=1, source_target_pairs={{0,8},{4,12},{8,0},{12,4},{16,24},{20,28},{24,16},{28,20},{1,9},{5... | collective-permute-start | bytes 294920 | tf_op jit(solution)/shard_map/ppermute | solution.py:242
  12.1 1.5 %collective-permute-start.17 = (bf16[48,1024]{1,0:T(8,128)(2,1)S(1)}, bf16[48,1024]{1,0:T(8,128)(2,1)S(1)}, u32[]{:S(2)}, u32[]{:S(2)}) collective-permute-start(bf16[48,1024]{1,0:T(8,128)(2,1)S(1)} %get-tuple-element.26.refs_0_), channel_id=1, source_target_pairs={{0,16},{4,20},{8,24},{12,28},{16,0},{20,4},{24,8},{28,12},{1,17},{... | collective-permute-start | bytes 294920 | tf_op jit(solution)/shard_map/ppermute | solution.py:242
  13.6 0.1 collective-permute-start.18
  13.7 1.3 %collective-permute-done.3.refs_3_ = bf16[48,1024]{1,0:T(8,128)(2,1)S(1)} collective-permute-done((bf16[48,1024]{1,0:T(8,128)(2,1)S(1)}, bf16[48,1024]{1,0:T(8,128)(2,1)S(1)}, u32[]{:S(2)}, u32[]{:S(2)}) %collective-permute-start.3) | collective-permute-done | bytes 98336 | tf_op jit(solution)/shard_map/ppermute | solution.py:242
  15.0 1.9 %copy-done = bf16[1,768,2048]{2,1,0:T(8,128)(2,1)S(1)} copy-done((bf16[1,768,2048]{2,1,0:T(8,128)(2,1)S(1)}, bf16[1,768,2048]{2,1,0:T(8,128)(2,1)}, u32[]{:S(2)}) %copy-start) | copy-done | bytes 3145752
  16.9 1.9 %copy-done.2 = bf16[1,768,2048]{2,1,0:T(8,128)(2,1)S(1)} copy-done((bf16[1,768,2048]{2,1,0:T(8,128)(2,1)S(1)}, bf16[1,768,2048]{2,1,0:T(8,128)(2,1)}, u32[]{:S(2)}) %copy-start.2) | copy-done | bytes 3145752
  18.8 1.9 %copy-done.4 = bf16[1,768,2048]{2,1,0:T(8,128)(2,1)S(1)} copy-done((bf16[1,768,2048]{2,1,0:T(8,128)(2,1)S(1)}, bf16[1,768,2048]{2,1,0:T(8,128)(2,1)}, u32[]{:S(2)}) %copy-start.4) | copy-done | bytes 3145752
  20.7 2.6 %forward.1 = (f32[96,768]{1,0:T(8,128)S(1)}, f32[96,768]{1,0:T(8,128)S(1)}, bf16[48,1024]{1,0:T(8,128)(2,1)S(1)}, bf16[48,1024]{1,0:T(8,128)(2,1)S(1)}, bf16[48,...) custom-call(bf16[48,1024]{1,0:T(8,128)(2,1)S(1)} %get-tuple-element.19.refs_0_, ...), custom_call_target="tpu_custom_call" | custom-call | flops 905969664 | bytes 10813440 | tf_op jit(solution)/shard_map/forward/pallas_call | solution.py:22
  23.2 1.6 %collective-permute-start.6 = (bf16[48,1024]{1,0:T(8,128)(2,1)S(1)}, bf16[48,1024]{1,0:T(8,128)(2,1)S(1)}, u32[]{:S(2)}, u32[]{:S(2)}) collective-permute-start(bf16[48,1024]{1,0:T(8,128)(2,1)S(1)} %get-tuple-element.24), channel_id=1, source_target_pairs={{0,24},{4,28},{8,16},{12,20},{16,8},{20,12},{24,0},{28,4},{1,25},{... | collective-permute-start | bytes 294920 | tf_op jit(solution)/shard_map/ppermute | solution.py:242
  24.9 0.6 collective-permute-start.4
  25.4 1.4 %collective-permute-start.5 = (bf16[48,1024]{1,0:T(8,128)(2,1)S(1)}, bf16[48,1024]{1,0:T(8,128)(2,1)S(1)}, u32[]{:S(2)}, u32[]{:S(2)}) collective-permute-start(bf16[48,1024]{1,0:T(8,128)(2,1)S(1)} %get-tuple-element.23), channel_id=1, source_target_pairs={{0,16},{4,20},{8,24},{12,28},{16,0},{20,4},{24,8},{28,12},{1,17},{... | collective-permute-start | bytes 294920 | tf_op jit(solution)/shard_map/ppermute | solution.py:242
  26.9 2.4 %backward.1 = (bf16[48,1024]{1,0:T(8,128)(2,1)S(1)}, bf16[48,1024]{1,0:T(8,128)(2,1)S(1)}, bf16[48,1024]{1,0:T(8,128)(2,1)S(1)}, bf16[48,1024]{1,0:T(8,128)(2,1)S(1)}) custom-call(bf16[48,1024]{1,0:T(8,128)(2,1)S(1)} %get-tuple-element.26.refs_0_, bf16[48,1024]{1,0:T(8,128)(2,1)S(1)} %collective-permute-done.16.refs_1_, ...), custom_call_target="tpu_custom_call" | custom-call | flops 905969664 | bytes 10813440 | tf_op jit(solution)/shard_map/backward/pallas_call | solution.py:22
  29.3 0.7 collective-permute-start.19
  30.0 1.5 %collective-permute-start.20 = (bf16[48,1024]{1,0:T(8,128)(2,1)S(1)}, bf16[48,1024]{1,0:T(8,128)(2,1)S(1)}, u32[]{:S(2)}, u32[]{:S(2)}) collective-permute-start(bf16[48,1024]{1,0:T(8,128)(2,1)S(1)} %get-tuple-element.32), channel_id=1, source_target_pairs={{0,16},{4,20},{8,24},{12,28},{16,0},{20,4},{24,8},{28,12},{1,17},{... | collective-permute-start | bytes 294920 | tf_op jit(solution)/shard_map/ppermute | solution.py:242
  31.5 1.4 %collective-permute-start.21 = (bf16[48,1024]{1,0:T(8,128)(2,1)S(1)}, bf16[48,1024]{1,0:T(8,128)(2,1)S(1)}, u32[]{:S(2)}, u32[]{:S(2)}) collective-permute-start(bf16[48,1024]{1,0:T(8,128)(2,1)S(1)} %get-tuple-element.33), channel_id=1, source_target_pairs={{0,24},{4,28},{8,16},{12,20},{16,8},{20,12},{24,0},{28,4},{1,25},{... | collective-permute-start | bytes 294920 | tf_op jit(solution)/shard_map/ppermute | solution.py:242
  32.9 0.5 collective-permute-start.8
  33.4 1.6 %collective-permute-done.19.refs_1_ = bf16[48,1024]{1,0:T(8,128)(2,1)S(1)} collective-permute-done((bf16[48,1024]{1,0:T(8,128)(2,1)S(1)}, bf16[48,1024]{1,0:T(8,128)(2,1)S(1)}, u32[]{:S(2)}, u32[]{:S(2)}) %collective-permute-start.19) | collective-permute-done | bytes 98336 | tf_op jit(solution)/shard_map/ppermute | solution.py:242
  35.0 1.1 %collective-permute-done.20.refs_2_ = bf16[48,1024]{1,0:T(8,128)(2,1)S(1)} collective-permute-done((bf16[48,1024]{1,0:T(8,128)(2,1)S(1)}, bf16[48,1024]{1,0:T(8,128)(2,1)S(1)}, u32[]{:S(2)}, u32[]{:S(2)}) %collective-permute-start.20) | collective-permute-done | bytes 98336 | tf_op jit(solution)/shard_map/ppermute | solution.py:242
  36.1 1.0 %collective-permute-done.21.refs_3_ = bf16[48,1024]{1,0:T(8,128)(2,1)S(1)} collective-permute-done((bf16[48,1024]{1,0:T(8,128)(2,1)S(1)}, bf16[48,1024]{1,0:T(8,128)(2,1)S(1)}, u32[]{:S(2)}, u32[]{:S(2)}) %collective-permute-start.21) | collective-permute-done | bytes 98336 | tf_op jit(solution)/shard_map/ppermute | solution.py:242
  37.1 0.5 collective-permute-start.24
  37.7 2.7 %collective-permute-start.11 = (bf16[192,512]{1,0:T(8,128)(2,1)S(1)}, bf16[192,512]{1,0:T(8,128)(2,1)S(1)}, u32[]{:S(2)}, u32[]{:S(2)}) collective-permute-start(bf16[192,512]{1,0:T(8,128)(2,1)S(1)} %add_blocks.2.refs_0_), channel_id=1, source_target_pairs={{0,2},{1,3},{2,0},{3,1},{4,6},{5,7},{6,4},{7,5},{8,10},{9,11},{10,... | collective-permute-start | bytes 589832 | tf_op jit(solution)/shard_map/ppermute | solution.py:315
  40.3 3.5 %collective-permute-start.12 = (bf16[192,512]{1,0:T(8,128)(2,1)S(1)}, bf16[192,512]{1,0:T(8,128)(2,1)S(1)}, u32[]{:S(2)}, u32[]{:S(2)}) collective-permute-start(bf16[192,512]{1,0:T(8,128)(2,1)S(1)} %add_blocks.2.refs_0_), channel_id=1, source_target_pairs={{0,1},{1,2},{2,3},{4,5},{5,6},{6,7},{8,9},{9,10},{10,11},{12,13},{... | collective-permute-start | bytes 589832 | tf_op jit(solution)/shard_map/ppermute | solution.py:316
  43.9 0.4 collective-permute-start.26
  44.3 1.3 %collective-permute-start.13 = (bf16[192,512]{1,0:T(8,128)(2,1)S(1)}, bf16[192,512]{1,0:T(8,128)(2,1)S(1)}, u32[]{:S(2)}, u32[]{:S(2)}) collective-permute-start(bf16[192,512]{1,0:T(8,128)(2,1)S(1)} %add_blocks.2.refs_0_), channel_id=1, source_target_pairs={{1,0},{2,1},{3,2},{5,4},{6,5},{7,6},{9,8},{10,9},{11,10},{13,12},{... | collective-permute-start | bytes 589832 | tf_op jit(solution)/shard_map/ppermute | solution.py:317
  45.6 9.3 %collective-permute-done.11.refs_1_ = bf16[192,512]{1,0:T(8,128)(2,1)S(1)} collective-permute-done((bf16[192,512]{1,0:T(8,128)(2,1)S(1)}, bf16[192,512]{1,0:T(8,128)(2,1)S(1)}, u32[]{:S(2)}, u32[]{:S(2)}) %collective-permute-start.11) | collective-permute-done | bytes 196640 | tf_op jit(solution)/shard_map/ppermute | solution.py:315
  54.9 1.3 %collective-permute-start.14 = (bf16[192,512]{1,0:T(8,128)(2,1)S(1)}, bf16[192,512]{1,0:T(8,128)(2,1)S(1)}, u32[]{:S(2)}, u32[]{:S(2)}) collective-permute-start(bf16[192,512]{1,0:T(8,128)(2,1)S(1)} %collective-permute-done.11.refs_1_), channel_id=1, source_target_pairs={{2,3},{1,0},{6,7},{5,4},{10,11},{9,8},{14,15},{13,12},{18,19},{17,... | collective-permute-start | bytes 589832 | tf_op jit(solution)/shard_map/ppermute | solution.py:318
  56.2 4.6 %collective-permute-start.27 = (bf16[192,512]{1,0:T(8,128)(2,1)S(1)}, bf16[192,512]{1,0:T(8,128)(2,1)S(1)}, u32[]{:S(2)}, u32[]{:S(2)}) collective-permute-start(bf16[192,512]{1,0:T(8,128)(2,1)S(1)} %add_blocks.3.refs_0_), channel_id=1, source_target_pairs={{0,1},{1,2},{2,3},{4,5},{5,6},{6,7},{8,9},{9,10},{10,11},{12,13},{... | collective-permute-start | bytes 589832 | tf_op jit(solution)/shard_map/ppermute | solution.py:316
  60.8 1.3 %collective-permute-start.28 = (bf16[192,512]{1,0:T(8,128)(2,1)S(1)}, bf16[192,512]{1,0:T(8,128)(2,1)S(1)}, u32[]{:S(2)}, u32[]{:S(2)}) collective-permute-start(bf16[192,512]{1,0:T(8,128)(2,1)S(1)} %add_blocks.3.refs_0_), channel_id=1, source_target_pairs={{1,0},{2,1},{3,2},{5,4},{6,5},{7,6},{9,8},{10,9},{11,10},{13,12},{... | collective-permute-start | bytes 589832 | tf_op jit(solution)/shard_map/ppermute | solution.py:317
  62.1 1.3 %collective-permute-start.29 = (bf16[192,512]{1,0:T(8,128)(2,1)S(1)}, bf16[192,512]{1,0:T(8,128)(2,1)S(1)}, u32[]{:S(2)}, u32[]{:S(2)}) collective-permute-start(bf16[192,512]{1,0:T(8,128)(2,1)S(1)} %collective-permute-done.26.refs_1_), channel_id=1, source_target_pairs={{2,3},{1,0},{6,7},{5,4},{10,11},{9,8},{14,15},{13,12},{18,19},{17,... | collective-permute-start | bytes 589832 | tf_op jit(solution)/shard_map/ppermute | solution.py:318
  63.4 0.3 weights.1.weight_ref
  63.7 0.5 collective-permute-done.14.refs_4_
  64.2 1.7 %combine_gate.1 = (bf16[512,512]{1,0:T(8,128)(2,1)}, f32[8,512]{1,0:T(8,128)S(1)}) custom-call(bf16[512,768]{1,0:T(8,128)(2,1)S(1)} %weights.1.weight_ref, s32[8,512]{1,0:T(8,128)S(1)} %bitcast.6, f32[16,512]{1,0:T(8,128)S(1)} %number.1.key_ref, bf16[512,512]{1,0:T(8,128)(2,1)S(1)} %copy-done.8, bf16[192,512]{1,0:T(8,128)(2,1)S(1)} %add_blocks.2.refs_0_, ...), custom_call_target="tpu_custom_call" | custom-call | flops 805306368 | bytes 2883584 | tf_op jit(solution)/shard_map/combine_gate/pallas_call | solution.py:22
  65.9 1.2 %collective-permute-done.30 = f32[8,512]{1,0:T(8,128)S(1)} collective-permute-done((f32[8,512]{1,0:T(8,128)S(1)}, f32[8,512]{1,0:T(8,128)S(1)}, u32[]{:S(2)}, u32[]{:S(2)}) %collective-permute-start.30) | collective-permute-done | bytes 16416 | tf_op jit(solution)/shard_map/ppermute | solution.py:232
  67.1 2.3 %collective-permute-start.31 = (f32[8,512]{1,0:T(8,128)S(1)}, f32[8,512]{1,0:T(8,128)S(1)}, u32[]{:S(2)}, u32[]{:S(2)}) collective-permute-start(f32[8,512]{1,0:T(8,128)S(1)} %add.6), channel_id=1, source_target_pairs={{0,8},{4,12},{8,0},{12,4},{16,24},{20,28},{24,16},{28,20},{1,9},{5... | collective-permute-start | bytes 49160 | tf_op jit(solution)/shard_map/ppermute | solution.py:242
  69.4 1.0 %collective-permute-done.28.refs_3_ = bf16[192,512]{1,0:T(8,128)(2,1)S(1)} collective-permute-done((bf16[192,512]{1,0:T(8,128)(2,1)S(1)}, bf16[192,512]{1,0:T(8,128)(2,1)S(1)}, u32[]{:S(2)}, u32[]{:S(2)}) %collective-permute-start.28) | collective-permute-done | bytes 196640 | tf_op jit(solution)/shard_map/ppermute | solution.py:317
  70.4 2.1 %collective-permute-done.29.refs_4_ = bf16[192,512]{1,0:T(8,128)(2,1)S(1)} collective-permute-done((bf16[192,512]{1,0:T(8,128)(2,1)S(1)}, bf16[192,512]{1,0:T(8,128)(2,1)S(1)}, u32[]{:S(2)}, u32[]{:S(2)}) %collective-permute-start.29) | collective-permute-done | bytes 196640 | tf_op jit(solution)/shard_map/ppermute | solution.py:318
  72.5 1.4 %combine.1 = bf16[512,512]{1,0:T(8,128)(2,1)} custom-call(bf16[512,768]{1,0:T(8,128)(2,1)S(1)} %weights.1.weight_ref, bf16[192,512]{1,0:T(8,128)(2,1)S(1)} %add_blocks.3.refs_0_, bf16[192,512]{1,0:T(8,128)(2,1)S(1)} %collective-permute-done.26.refs_1_, bf16[192,512]{1,0:T(8,128)(2,1)S(1)} %collective-permute-done.27.refs_2_, ...), custom_call_target="tpu_custom_call" | custom-call | flops 402653184 | bytes 2293760 | tf_op jit(solution)/shard_map/combine/pallas_call | solution.py:22
  73.9 0.6 add_bitcast_fusion
  (52 shorter events, 0.4 us)
Async XLA Ops:
  0.6 2.3 %collective-permute-start = (bf16[512,512]{1,0:T(8,128)(2,1)}, bf16[512,512]{1,0:T(8,128)(2,1)S(1)}, u32[]{:S(2)}, u32[]{:S(2)}) collective-permute-start(bf16[512,512]{1,0:T(8,128)(2,1)} %refs_0_.2), channel_id=1, source_target_pairs={{0,4},{4,0},{8,12},{12,8},{1,5},{5,1},{9,13},{13,9},{2,6},{6,2},{1... | collective-permute-start | bytes 1572872 | tf_op jit(solution)/shard_map/ppermute | solution.py:232
  1.1 7.6 %collective-permute-start.15 = (bf16[512,512]{1,0:T(8,128)(2,1)}, bf16[512,512]{1,0:T(8,128)(2,1)S(1)}, u32[]{:S(2)}, u32[]{:S(2)}) collective-permute-start(bf16[512,512]{1,0:T(8,128)(2,1)} %refs_0_.3), channel_id=1, source_target_pairs={{0,4},{4,0},{8,12},{12,8},{1,5},{5,1},{9,13},{13,9},{2,6},{6,2},{1... | collective-permute-start | bytes 1572872 | tf_op jit(solution)/shard_map/ppermute | solution.py:232
  1.2 0.7 copy-start.9
  2.9 1.0 %copy-start.6 = (bf16[512,512]{1,0:T(8,128)(2,1)S(1)}, bf16[512,512]{1,0:T(8,128)(2,1)}, u32[]{:S(2)}) copy-start(bf16[512,512]{1,0:T(8,128)(2,1)} %refs_0_.2) | copy-start | bytes 1572868
  4.2 9.4 %collective-permute-start.1 = (bf16[48,1024]{1,0:T(8,128)(2,1)S(1)}, bf16[48,1024]{1,0:T(8,128)(2,1)S(1)}, u32[]{:S(2)}, u32[]{:S(2)}) collective-permute-start(bf16[48,1024]{1,0:T(8,128)(2,1)S(1)} %get-tuple-element.20), channel_id=1, source_target_pairs={{0,8},{4,12},{8,0},{12,4},{16,24},{20,28},{24,16},{28,20},{1,9},{5... | collective-permute-start | bytes 294920 | tf_op jit(solution)/shard_map/ppermute | solution.py:242
  7.2 6.5 %collective-permute-start.2 = (bf16[48,1024]{1,0:T(8,128)(2,1)S(1)}, bf16[48,1024]{1,0:T(8,128)(2,1)S(1)}, u32[]{:S(2)}, u32[]{:S(2)}) collective-permute-start(bf16[48,1024]{1,0:T(8,128)(2,1)S(1)} %get-tuple-element.19.refs_0_), channel_id=1, source_target_pairs={{0,16},{4,20},{8,24},{12,28},{16,0},{20,4},{24,8},{28,12},{1,17},{... | collective-permute-start | bytes 294920 | tf_op jit(solution)/shard_map/ppermute | solution.py:242
  8.7 6.3 %collective-permute-start.3 = (bf16[48,1024]{1,0:T(8,128)(2,1)S(1)}, bf16[48,1024]{1,0:T(8,128)(2,1)S(1)}, u32[]{:S(2)}, u32[]{:S(2)}) collective-permute-start(bf16[48,1024]{1,0:T(8,128)(2,1)S(1)} %get-tuple-element.20), channel_id=1, source_target_pairs={{0,24},{4,28},{8,16},{12,20},{16,8},{20,12},{24,0},{28,4},{1,25},{... | collective-permute-start | bytes 294920 | tf_op jit(solution)/shard_map/ppermute | solution.py:242
  8.7 1.0 %copy-start.7 = (bf16[512,512]{1,0:T(8,128)(2,1)S(1)}, bf16[512,512]{1,0:T(8,128)(2,1)}, u32[]{:S(2)}) copy-start(bf16[512,512]{1,0:T(8,128)(2,1)} %refs_0_.3) | copy-start | bytes 1572868
  10.1 15.4 %collective-permute-start.16 = (bf16[48,1024]{1,0:T(8,128)(2,1)S(1)}, bf16[48,1024]{1,0:T(8,128)(2,1)S(1)}, u32[]{:S(2)}, u32[]{:S(2)}) collective-permute-start(bf16[48,1024]{1,0:T(8,128)(2,1)S(1)} %get-tuple-element.27), channel_id=1, source_target_pairs={{0,8},{4,12},{8,0},{12,4},{16,24},{20,28},{24,16},{28,20},{1,9},{5... | collective-permute-start | bytes 294920 | tf_op jit(solution)/shard_map/ppermute | solution.py:242
  12.1 14.7 %collective-permute-start.17 = (bf16[48,1024]{1,0:T(8,128)(2,1)S(1)}, bf16[48,1024]{1,0:T(8,128)(2,1)S(1)}, u32[]{:S(2)}, u32[]{:S(2)}) collective-permute-start(bf16[48,1024]{1,0:T(8,128)(2,1)S(1)} %get-tuple-element.26.refs_0_), channel_id=1, source_target_pairs={{0,16},{4,20},{8,24},{12,28},{16,0},{20,4},{24,8},{28,12},{1,17},{... | collective-permute-start | bytes 294920 | tf_op jit(solution)/shard_map/ppermute | solution.py:242
  13.6 13.2 %collective-permute-start.18 = (bf16[48,1024]{1,0:T(8,128)(2,1)S(1)}, bf16[48,1024]{1,0:T(8,128)(2,1)S(1)}, u32[]{:S(2)}, u32[]{:S(2)}) collective-permute-start(bf16[48,1024]{1,0:T(8,128)(2,1)S(1)} %get-tuple-element.27), channel_id=1, source_target_pairs={{0,24},{4,28},{8,16},{12,20},{16,8},{20,12},{24,0},{28,4},{1,25},{... | collective-permute-start | bytes 294920 | tf_op jit(solution)/shard_map/ppermute | solution.py:242
  15.0 1.9 %copy-start = (bf16[1,768,2048]{2,1,0:T(8,128)(2,1)S(1)}, bf16[1,768,2048]{2,1,0:T(8,128)(2,1)}, u32[]{:S(2)}) copy-start(bf16[1,768,2048]{2,1,0:T(8,128)(2,1)} %refs_4_.3) | copy-start | bytes 9437188
  16.9 1.9 %copy-start.2 = (bf16[1,768,2048]{2,1,0:T(8,128)(2,1)S(1)}, bf16[1,768,2048]{2,1,0:T(8,128)(2,1)}, u32[]{:S(2)}) copy-start(bf16[1,768,2048]{2,1,0:T(8,128)(2,1)} %refs_5_.3) | copy-start | bytes 9437188
  18.8 1.9 %copy-start.4 = (bf16[1,768,2048]{2,1,0:T(8,128)(2,1)S(1)}, bf16[1,768,2048]{2,1,0:T(8,128)(2,1)}, u32[]{:S(2)}) copy-start(bf16[1,768,2048]{2,1,0:T(8,128)(2,1)} %refs_6_.3) | copy-start | bytes 9437188
  20.7 6.2 %copy-start.1 = (bf16[1,768,2048]{2,1,0:T(8,128)(2,1)S(1)}, bf16[1,768,2048]{2,1,0:T(8,128)(2,1)}, u32[]{:S(2)}) copy-start(bf16[1,768,2048]{2,1,0:T(8,128)(2,1)} %refs_4_.3) | copy-start | bytes 9437188
  20.7 6.2 %copy-start.3 = (bf16[1,768,2048]{2,1,0:T(8,128)(2,1)S(1)}, bf16[1,768,2048]{2,1,0:T(8,128)(2,1)}, u32[]{:S(2)}) copy-start(bf16[1,768,2048]{2,1,0:T(8,128)(2,1)} %refs_5_.3) | copy-start | bytes 9437188
  20.7 6.2 %copy-start.5 = (bf16[1,768,2048]{2,1,0:T(8,128)(2,1)S(1)}, bf16[1,768,2048]{2,1,0:T(8,128)(2,1)}, u32[]{:S(2)}) copy-start(bf16[1,768,2048]{2,1,0:T(8,128)(2,1)} %refs_6_.3) | copy-start | bytes 9437188
  23.2 6.8 %collective-permute-start.6 = (bf16[48,1024]{1,0:T(8,128)(2,1)S(1)}, bf16[48,1024]{1,0:T(8,128)(2,1)S(1)}, u32[]{:S(2)}, u32[]{:S(2)}) collective-permute-start(bf16[48,1024]{1,0:T(8,128)(2,1)S(1)} %get-tuple-element.24), channel_id=1, source_target_pairs={{0,24},{4,28},{8,16},{12,20},{16,8},{20,12},{24,0},{28,4},{1,25},{... | collective-permute-start | bytes 294920 | tf_op jit(solution)/shard_map/ppermute | solution.py:242
  24.9 6.7 %collective-permute-start.4 = (bf16[48,1024]{1,0:T(8,128)(2,1)S(1)}, bf16[48,1024]{1,0:T(8,128)(2,1)S(1)}, u32[]{:S(2)}, u32[]{:S(2)}) collective-permute-start(bf16[48,1024]{1,0:T(8,128)(2,1)S(1)} %get-tuple-element.22), channel_id=1, source_target_pairs={{0,8},{4,12},{8,0},{12,4},{16,24},{20,28},{24,16},{28,20},{1,9},{5... | collective-permute-start | bytes 294920 | tf_op jit(solution)/shard_map/ppermute | solution.py:242
  25.4 7.5 %collective-permute-start.5 = (bf16[48,1024]{1,0:T(8,128)(2,1)S(1)}, bf16[48,1024]{1,0:T(8,128)(2,1)S(1)}, u32[]{:S(2)}, u32[]{:S(2)}) collective-permute-start(bf16[48,1024]{1,0:T(8,128)(2,1)S(1)} %get-tuple-element.23), channel_id=1, source_target_pairs={{0,16},{4,20},{8,24},{12,28},{16,0},{20,4},{24,8},{28,12},{1,17},{... | collective-permute-start | bytes 294920 | tf_op jit(solution)/shard_map/ppermute | solution.py:242
  26.8 6.1 %collective-permute-start.7 = (bf16[48,1024]{1,0:T(8,128)(2,1)S(1)}, bf16[48,1024]{1,0:T(8,128)(2,1)S(1)}, u32[]{:S(2)}, u32[]{:S(2)}) collective-permute-start(bf16[48,1024]{1,0:T(8,128)(2,1)S(1)} %get-tuple-element.21.refs_0_), channel_id=1, source_target_pairs={{0,4},{4,0},{8,12},{12,8},{1,5},{5,1},{9,13},{13,9},{2,6},{6,2},{1... | collective-permute-start | bytes 294920 | tf_op jit(solution)/shard_map/ppermute | solution.py:232
  26.8 36.5 %copy-start.10 = (s32[512,8]{0,1:T(8,128)S(1)}, s32[512,8]{0,1:T(8,128)}, u32[]{:S(2)}) copy-start(s32[512,8]{0,1:T(8,128)} %param.9) | copy-start | bytes 49156
  26.9 36.5 %copy-start.11 = (f32[512,8]{0,1:T(8,128)S(1)}, f32[512,8]{0,1:T(8,128)}, u32[]{:S(2)}) copy-start(f32[512,8]{0,1:T(8,128)} %param.10) | copy-start | bytes 49156
  26.9 37.4 %copy-start.8 = (bf16[512,512]{1,0:T(8,128)(2,1)S(1)}, bf16[512,512]{1,0:T(8,128)(2,1)}, u32[]{:S(2)}) copy-start(bf16[512,512]{1,0:T(8,128)(2,1)} %refs_0_.3) | copy-start | bytes 1572868
  29.3 5.7 %collective-permute-start.19 = (bf16[48,1024]{1,0:T(8,128)(2,1)S(1)}, bf16[48,1024]{1,0:T(8,128)(2,1)S(1)}, u32[]{:S(2)}, u32[]{:S(2)}) collective-permute-start(bf16[48,1024]{1,0:T(8,128)(2,1)S(1)} %get-tuple-element.31), channel_id=1, source_target_pairs={{0,8},{4,12},{8,0},{12,4},{16,24},{20,28},{24,16},{28,20},{1,9},{5... | collective-permute-start | bytes 294920 | tf_op jit(solution)/shard_map/ppermute | solution.py:242
  30.0 6.1 %collective-permute-start.20 = (bf16[48,1024]{1,0:T(8,128)(2,1)S(1)}, bf16[48,1024]{1,0:T(8,128)(2,1)S(1)}, u32[]{:S(2)}, u32[]{:S(2)}) collective-permute-start(bf16[48,1024]{1,0:T(8,128)(2,1)S(1)} %get-tuple-element.32), channel_id=1, source_target_pairs={{0,16},{4,20},{8,24},{12,28},{16,0},{20,4},{24,8},{28,12},{1,17},{... | collective-permute-start | bytes 294920 | tf_op jit(solution)/shard_map/ppermute | solution.py:242
  31.5 5.5 %collective-permute-start.21 = (bf16[48,1024]{1,0:T(8,128)(2,1)S(1)}, bf16[48,1024]{1,0:T(8,128)(2,1)S(1)}, u32[]{:S(2)}, u32[]{:S(2)}) collective-permute-start(bf16[48,1024]{1,0:T(8,128)(2,1)S(1)} %get-tuple-element.33), channel_id=1, source_target_pairs={{0,24},{4,28},{8,16},{12,20},{16,8},{20,12},{24,0},{28,4},{1,25},{... | collective-permute-start | bytes 294920 | tf_op jit(solution)/shard_map/ppermute | solution.py:242
  32.9 4.2 %collective-permute-start.10 = (bf16[48,1024]{1,0:T(8,128)(2,1)S(1)}, bf16[48,1024]{1,0:T(8,128)(2,1)S(1)}, u32[]{:S(2)}, u32[]{:S(2)}) collective-permute-start(bf16[48,1024]{1,0:T(8,128)(2,1)S(1)} %collective-permute-done.6.refs_3_), channel_id=1, source_target_pairs={{0,4},{4,0},{8,12},{12,8},{1,5},{5,1},{9,13},{13,9},{2,6},{6,2},{1... | collective-permute-start | bytes 294920 | tf_op jit(solution)/shard_map/ppermute | solution.py:232
  32.9 4.7 %collective-permute-start.8 = (bf16[48,1024]{1,0:T(8,128)(2,1)S(1)}, bf16[48,1024]{1,0:T(8,128)(2,1)S(1)}, u32[]{:S(2)}, u32[]{:S(2)}) collective-permute-start(bf16[48,1024]{1,0:T(8,128)(2,1)S(1)} %collective-permute-done.4.refs_1_), channel_id=1, source_target_pairs={{0,4},{4,0},{8,12},{12,8},{1,5},{5,1},{9,13},{13,9},{2,6},{6,2},{1... | collective-permute-start | bytes 294920 | tf_op jit(solution)/shard_map/ppermute | solution.py:232
  35.0 2.7 %collective-permute-start.9 = (bf16[48,1024]{1,0:T(8,128)(2,1)S(1)}, bf16[48,1024]{1,0:T(8,128)(2,1)S(1)}, u32[]{:S(2)}, u32[]{:S(2)}) collective-permute-start(bf16[48,1024]{1,0:T(8,128)(2,1)S(1)} %collective-permute-done.5.refs_2_), channel_id=1, source_target_pairs={{0,4},{4,0},{8,12},{12,8},{1,5},{5,1},{9,13},{13,9},{2,6},{6,2},{1... | collective-permute-start | bytes 294920 | tf_op jit(solution)/shard_map/ppermute | solution.py:232
  36.1 4.3 %collective-permute-start.22 = (bf16[48,1024]{1,0:T(8,128)(2,1)S(1)}, bf16[48,1024]{1,0:T(8,128)(2,1)S(1)}, u32[]{:S(2)}, u32[]{:S(2)}) collective-permute-start(bf16[48,1024]{1,0:T(8,128)(2,1)S(1)} %get-tuple-element.30.refs_0_), channel_id=1, source_target_pairs={{0,4},{4,0},{8,12},{12,8},{1,5},{5,1},{9,13},{13,9},{2,6},{6,2},{1... | collective-permute-start | bytes 294920 | tf_op jit(solution)/shard_map/ppermute | solution.py:232
  37.1 6.8 %collective-permute-start.23 = (bf16[48,1024]{1,0:T(8,128)(2,1)S(1)}, bf16[48,1024]{1,0:T(8,128)(2,1)S(1)}, u32[]{:S(2)}, u32[]{:S(2)}) collective-permute-start(bf16[48,1024]{1,0:T(8,128)(2,1)S(1)} %collective-permute-done.19.refs_1_), channel_id=1, source_target_pairs={{0,4},{4,0},{8,12},{12,8},{1,5},{5,1},{9,13},{13,9},{2,6},{6,2},{1... | collective-permute-start | bytes 294920 | tf_op jit(solution)/shard_map/ppermute | solution.py:232
  37.1 6.8 %collective-permute-start.24 = (bf16[48,1024]{1,0:T(8,128)(2,1)S(1)}, bf16[48,1024]{1,0:T(8,128)(2,1)S(1)}, u32[]{:S(2)}, u32[]{:S(2)}) collective-permute-start(bf16[48,1024]{1,0:T(8,128)(2,1)S(1)} %collective-permute-done.20.refs_2_), channel_id=1, source_target_pairs={{0,4},{4,0},{8,12},{12,8},{1,5},{5,1},{9,13},{13,9},{2,6},{6,2},{1... | collective-permute-start | bytes 294920 | tf_op jit(solution)/shard_map/ppermute | solution.py:232
  37.6 6.3 %collective-permute-start.25 = (bf16[48,1024]{1,0:T(8,128)(2,1)S(1)}, bf16[48,1024]{1,0:T(8,128)(2,1)S(1)}, u32[]{:S(2)}, u32[]{:S(2)}) collective-permute-start(bf16[48,1024]{1,0:T(8,128)(2,1)S(1)} %collective-permute-done.21.refs_3_), channel_id=1, source_target_pairs={{0,4},{4,0},{8,12},{12,8},{1,5},{5,1},{9,13},{13,9},{2,6},{6,2},{1... | collective-permute-start | bytes 294920 | tf_op jit(solution)/shard_map/ppermute | solution.py:232
  37.7 17.2 %collective-permute-start.11 = (bf16[192,512]{1,0:T(8,128)(2,1)S(1)}, bf16[192,512]{1,0:T(8,128)(2,1)S(1)}, u32[]{:S(2)}, u32[]{:S(2)}) collective-permute-start(bf16[192,512]{1,0:T(8,128)(2,1)S(1)} %add_blocks.2.refs_0_), channel_id=1, source_target_pairs={{0,2},{1,3},{2,0},{3,1},{4,6},{5,7},{6,4},{7,5},{8,10},{9,11},{10,... | collective-permute-start | bytes 589832 | tf_op jit(solution)/shard_map/ppermute | solution.py:315
  40.3 20.4 %collective-permute-start.12 = (bf16[192,512]{1,0:T(8,128)(2,1)S(1)}, bf16[192,512]{1,0:T(8,128)(2,1)S(1)}, u32[]{:S(2)}, u32[]{:S(2)}) collective-permute-start(bf16[192,512]{1,0:T(8,128)(2,1)S(1)} %add_blocks.2.refs_0_), channel_id=1, source_target_pairs={{0,1},{1,2},{2,3},{4,5},{5,6},{6,7},{8,9},{9,10},{10,11},{12,13},{... | collective-permute-start | bytes 589832 | tf_op jit(solution)/shard_map/ppermute | solution.py:316
  43.9 18.1 %collective-permute-start.26 = (bf16[192,512]{1,0:T(8,128)(2,1)S(1)}, bf16[192,512]{1,0:T(8,128)(2,1)S(1)}, u32[]{:S(2)}, u32[]{:S(2)}) collective-permute-start(bf16[192,512]{1,0:T(8,128)(2,1)S(1)} %add_blocks.3.refs_0_), channel_id=1, source_target_pairs={{0,2},{1,3},{2,0},{3,1},{4,6},{5,7},{6,4},{7,5},{8,10},{9,11},{10,... | collective-permute-start | bytes 589832 | tf_op jit(solution)/shard_map/ppermute | solution.py:315
  44.3 19.4 %collective-permute-start.13 = (bf16[192,512]{1,0:T(8,128)(2,1)S(1)}, bf16[192,512]{1,0:T(8,128)(2,1)S(1)}, u32[]{:S(2)}, u32[]{:S(2)}) collective-permute-start(bf16[192,512]{1,0:T(8,128)(2,1)S(1)} %add_blocks.2.refs_0_), channel_id=1, source_target_pairs={{1,0},{2,1},{3,2},{5,4},{6,5},{7,6},{9,8},{10,9},{11,10},{13,12},{... | collective-permute-start | bytes 589832 | tf_op jit(solution)/shard_map/ppermute | solution.py:317
  54.9 9.3 %collective-permute-start.14 = (bf16[192,512]{1,0:T(8,128)(2,1)S(1)}, bf16[192,512]{1,0:T(8,128)(2,1)S(1)}, u32[]{:S(2)}, u32[]{:S(2)}) collective-permute-start(bf16[192,512]{1,0:T(8,128)(2,1)S(1)} %collective-permute-done.11.refs_1_), channel_id=1, source_target_pairs={{2,3},{1,0},{6,7},{5,4},{10,11},{9,8},{14,15},{13,12},{18,19},{17,... | collective-permute-start | bytes 589832 | tf_op jit(solution)/shard_map/ppermute | solution.py:318
  56.2 13.2 %collective-permute-start.27 = (bf16[192,512]{1,0:T(8,128)(2,1)S(1)}, bf16[192,512]{1,0:T(8,128)(2,1)S(1)}, u32[]{:S(2)}, u32[]{:S(2)}) collective-permute-start(bf16[192,512]{1,0:T(8,128)(2,1)S(1)} %add_blocks.3.refs_0_), channel_id=1, source_target_pairs={{0,1},{1,2},{2,3},{4,5},{5,6},{6,7},{8,9},{9,10},{10,11},{12,13},{... | collective-permute-start | bytes 589832 | tf_op jit(solution)/shard_map/ppermute | solution.py:316
  60.8 9.6 %collective-permute-start.28 = (bf16[192,512]{1,0:T(8,128)(2,1)S(1)}, bf16[192,512]{1,0:T(8,128)(2,1)S(1)}, u32[]{:S(2)}, u32[]{:S(2)}) collective-permute-start(bf16[192,512]{1,0:T(8,128)(2,1)S(1)} %add_blocks.3.refs_0_), channel_id=1, source_target_pairs={{1,0},{2,1},{3,2},{5,4},{6,5},{7,6},{9,8},{10,9},{11,10},{13,12},{... | collective-permute-start | bytes 589832 | tf_op jit(solution)/shard_map/ppermute | solution.py:317
  62.1 10.4 %collective-permute-start.29 = (bf16[192,512]{1,0:T(8,128)(2,1)S(1)}, bf16[192,512]{1,0:T(8,128)(2,1)S(1)}, u32[]{:S(2)}, u32[]{:S(2)}) collective-permute-start(bf16[192,512]{1,0:T(8,128)(2,1)S(1)} %collective-permute-done.26.refs_1_), channel_id=1, source_target_pairs={{2,3},{1,0},{6,7},{5,4},{10,11},{9,8},{14,15},{13,12},{18,19},{17,... | collective-permute-start | bytes 589832 | tf_op jit(solution)/shard_map/ppermute | solution.py:318
  65.9 1.2 %collective-permute-start.30 = (f32[8,512]{1,0:T(8,128)S(1)}, f32[8,512]{1,0:T(8,128)S(1)}, u32[]{:S(2)}, u32[]{:S(2)}) collective-permute-start(f32[8,512]{1,0:T(8,128)S(1)} %get-tuple-element.34), channel_id=1, source_target_pairs={{0,4},{4,0},{8,12},{12,8},{1,5},{5,1},{9,13},{13,9},{2,6},{6,2},{1... | collective-permute-start | bytes 49160 | tf_op jit(solution)/shard_map/ppermute | solution.py:232
  67.1 6.7 %collective-permute-start.31 = (f32[8,512]{1,0:T(8,128)S(1)}, f32[8,512]{1,0:T(8,128)S(1)}, u32[]{:S(2)}, u32[]{:S(2)}) collective-permute-start(f32[8,512]{1,0:T(8,128)S(1)} %add.6), channel_id=1, source_target_pairs={{0,8},{4,12},{8,0},{12,4},{16,24},{20,28},{24,16},{28,20},{1,9},{5... | collective-permute-start | bytes 49160 | tf_op jit(solution)/shard_map/ppermute | solution.py:242

commit v4 on v3

--- a/solution.py
+++ b/solution.py
@@ -10,6 +10,7 @@
 CAP = 48
 LANES = 128
 MIB = 2**20
+EARLY = 6e9
 BF16 = jnp.bfloat16
 F32 = jnp.float32
 CONTRACT_LAST = (((1,), (1,)), ((), ()))
@@ -250,7 +251,7 @@
             "pick",
             [shape(CAP, cores * width)] * chips,
             [key, *sources],
-            2 * slots * rows * width,
+            EARLY,
         )
         arrived = {index: to_chip(pieces[hops[index][1]], *hops[index]) for index in order}
         return [arrived[index] for index in range(count)]
@@ -266,9 +267,21 @@
             2 * slots * width,
         )
 
+    def across(value):
+        if columns != 4:
+            return [value] + [
+                lax.ppermute(value, "expert", [(z, (z + dz) % columns) for z in range(columns)])
+                for dz in range(1, columns)
+            ]
+        far = lax.ppermute(value, "expert", [(z, (z + 2) % columns) for z in range(columns)])
+        up = lax.ppermute(value, "expert", [(z, z + 1) for z in range(columns - 1)])
+        down = lax.ppermute(value, "expert", [(z + 1, z) for z in range(columns - 1)])
+        ends = lax.ppermute(far, "expert", [(2, 3), (1, 0)])
+        return [value, far, up, down, ends]
+
     token_sources = [to_core(tokens, dc) for dc in range(cores)]
     grad_sources = [to_core(grad_out, dc) for dc in range(cores)]
-    key = call(number_kernel, "number", shape(experts, rows, F32), [routes_t], experts * rows * LANES)
+    key = call(number_kernel, "number", shape(experts, rows, F32), [routes_t], EARLY)
     tok_in = dispatch(key, token_sources)
     grad_in = dispatch(key, grad_sources)
 
@@ -294,6 +307,8 @@
         [pltpu.VMEM((tall, feats), BF16)] + [pltpu.VMEM((tall, hid_dev), BF16)] * 2,
         limit=24,
     )
+    out_parts = across(out_rows)
+    out_parts[1], backs = lax.optimization_barrier((out_parts[1], backs))
     back_rows = give_back(backs)
 
     weight_map = call(
@@ -306,19 +321,6 @@
         limit=16,
     )
 
-    def across(value):
-        if columns != 4:
-            return [value] + [
-                lax.ppermute(value, "expert", [(z, (z + dz) % columns) for z in range(columns)])
-                for dz in range(1, columns)
-            ]
-        far = lax.ppermute(value, "expert", [(z, (z + 2) % columns) for z in range(columns)])
-        up = lax.ppermute(value, "expert", [(z, z + 1) for z in range(columns - 1)])
-        down = lax.ppermute(value, "expert", [(z + 1, z) for z in range(columns - 1)])
-        ends = lax.ppermute(far, "expert", [(2, 3), (1, 0)])
-        return [value, far, up, down, ends]
-
-    out_parts = across(out_rows)
     back_parts = across(back_rows)
     combine_flops = 2 * experts * CAP * rows * width
     all_rows = pltpu.VMEM((experts * CAP, width), BF16)

time: 75 us -> 79.6 us (1.061)
  waiting for transfers between devices: 19.8 us -> 31.6 us
  local copies, waits for them, and re-layouts: 8.5 us -> 0.84 us
  starting transfers between devices: 35.4 us -> 36.2 us
    ppermute x13, waiting for transfers between devices: 4.95 us -> 14.8 us  [to_chip(): return lax.ppermute(value, ('dp', 'tensor'), pairs)]
    ppermute x2, waiting for transfers between devices: 9.27 us -> 0.01 us  [across(): lax.ppermute(value, 'expert', [(z, (z + 2) % columns) for z in range(colu...]
    unnamed x24 -> x16, local copies, waits for them, and re-layouts: 8.5 us -> 0.84 us
    ppermute x2, starting transfers between devices: 3.04 us -> 8.14 us  [across(): lax.ppermute(value, 'expert', [(z, (z + 2) % columns) for z in range(colu...]
    ppermute x2, waiting for transfers between devices: 0.99 us -> 5.4 us  [across(): lax.ppermute(value, 'expert', [(z + 1, z) for z in range(columns - 1)])]
    ppermute x2, waiting for transfers between devices: 2.6 us -> 6.08 us  [across(): ends = lax.ppermute(far, 'expert', [(2, 3), (1, 0)])]
    ppermute x2, starting transfers between devices: 8.05 us -> 4.7 us  [across(): up = lax.ppermute(value, 'expert', [(z, z + 1) for z in range(columns - 1)])]
    ppermute x11, waiting for transfers between devices: 2 us -> 4.27 us  [to_core(): return lax.ppermute(value, 'tensor', pairs)]
  transfers between devices with their start and end apart: 32 -> 32, of which waited for: 10 -> 19; matrix products, arithmetic and copies ran while one was open for 0% -> 1% of each run, Pallas kernels for 12% -> 10%
where the time goes in v4:
time: 79.6 us; the launch traced here: 79.3 us
  starting transfers between devices  36.2 us (45%)
  waiting for transfers between devices  31.6 us (40%)
  Pallas kernels  9.26 us (12%)
  local copies, waits for them, and re-layouts  0.84 us (1%)
  between operations  0.83 us (1%)
    ppermute x13, starting transfers between devices, to_chip(): return lax.ppermute(value, ('dp', 'tensor'), pairs)  17 us
    ppermute x13, waiting for transfers between devices, to_chip(): return lax.ppermute(value, ('dp', 'tensor'), pairs)  14.8 us
    pallas_call x10, Pallas kernels, call(): pl.pallas_call(kernel, out_shape=out_shape, in_specs=[spec] * len(operand...  9.26 us
    ppermute x2, starting transfers between devices, across(): lax.ppermute(value, 'expert', [(z, (z + 2) % columns) for z in range(colu...  8.14 us
    ppermute x2, waiting for transfers between devices, across(): ends = lax.ppermute(far, 'expert', [(2, 3), (1, 0)])  6.08 us
    ppermute x2, waiting for transfers between devices, across(): lax.ppermute(value, 'expert', [(z + 1, z) for z in range(columns - 1)])  5.4 us
    ppermute x2, starting transfers between devices, across(): up = lax.ppermute(value, 'expert', [(z, z + 1) for z in range(columns - 1)])  4.7 us
    ppermute x11, waiting for transfers between devices, to_core(): return lax.ppermute(value, 'tensor', pairs)  4.27 us
  transfers between devices with their start and end apart: 32, of which 19 were waited for; matrix products, arithmetic and copies ran while one was open for 1% of the time, Pallas kernels for 10%

profile of v4, /device:TPU:0, one launch (start us, length us, event | category | flops | bytes accessed | tf_op | source)
XLA Modules:
  0.0 79.3 jit_solution(1593892686430951734)
XLA Ops:
  0.6 0.5 collective-permute-start
  1.2 0.7 copy-done.4
  2.1 0.8 collective-permute-done.refs_1_
  3.0 0.3 pick.2
  3.3 3.0 %collective-permute-start.1 = (bf16[48,1024]{1,0:T(8,128)(2,1)S(1)}, bf16[48,1024]{1,0:T(8,128)(2,1)S(1)}, u32[]{:S(2)}, u32[]{:S(2)}) collective-permute-start(bf16[48,1024]{1,0:T(8,128)(2,1)S(1)} %get-tuple-element.25), channel_id=1, source_target_pairs={{0,8},{4,12},{8,0},{12,4},{16,24},{20,28},{24,16},{28,20},{1,9},{5... | collective-permute-start | bytes 294920 | tf_op jit(solution)/shard_map/ppermute | solution.py:243
  6.3 1.5 %collective-permute-start.2 = (bf16[48,1024]{1,0:T(8,128)(2,1)S(1)}, bf16[48,1024]{1,0:T(8,128)(2,1)S(1)}, u32[]{:S(2)}, u32[]{:S(2)}) collective-permute-start(bf16[48,1024]{1,0:T(8,128)(2,1)S(1)} %get-tuple-element.24.refs_0_), channel_id=1, source_target_pairs={{0,16},{4,20},{8,24},{12,28},{16,0},{20,4},{24,8},{28,12},{1,17},{... | collective-permute-start | bytes 294920 | tf_op jit(solution)/shard_map/ppermute | solution.py:243
  7.8 1.6 %collective-permute-done.1.refs_1_ = bf16[48,1024]{1,0:T(8,128)(2,1)S(1)} collective-permute-done((bf16[48,1024]{1,0:T(8,128)(2,1)S(1)}, bf16[48,1024]{1,0:T(8,128)(2,1)S(1)}, u32[]{:S(2)}, u32[]{:S(2)}) %collective-permute-start.1) | collective-permute-done | bytes 98336 | tf_op jit(solution)/shard_map/ppermute | solution.py:243
  9.4 2.6 %collective-permute-done.2.refs_2_ = bf16[48,1024]{1,0:T(8,128)(2,1)S(1)} collective-permute-done((bf16[48,1024]{1,0:T(8,128)(2,1)S(1)}, bf16[48,1024]{1,0:T(8,128)(2,1)S(1)}, u32[]{:S(2)}, u32[]{:S(2)}) %collective-permute-start.2) | collective-permute-done | bytes 98336 | tf_op jit(solution)/shard_map/ppermute | solution.py:243
  12.0 1.3 %collective-permute-done.3.refs_3_ = bf16[48,1024]{1,0:T(8,128)(2,1)S(1)} collective-permute-done((bf16[48,1024]{1,0:T(8,128)(2,1)S(1)}, bf16[48,1024]{1,0:T(8,128)(2,1)S(1)}, u32[]{:S(2)}, u32[]{:S(2)}) %collective-permute-start.3) | collective-permute-done | bytes 98336 | tf_op jit(solution)/shard_map/ppermute | solution.py:243
  13.3 2.6 %forward.1 = (f32[96,768]{1,0:T(8,128)S(1)}, f32[96,768]{1,0:T(8,128)S(1)}, bf16[48,1024]{1,0:T(8,128)(2,1)S(1)}, bf16[48,1024]{1,0:T(8,128)(2,1)S(1)}, bf16[48,...) custom-call(bf16[48,1024]{1,0:T(8,128)(2,1)S(1)} %get-tuple-element.24.refs_0_, ...), custom_call_target="tpu_custom_call" | custom-call | flops 905969664 | bytes 10813440 | tf_op jit(solution)/shard_map/forward/pallas_call | solution.py:23
  15.9 1.2 %collective-permute-start.6 = (bf16[48,1024]{1,0:T(8,128)(2,1)S(1)}, bf16[48,1024]{1,0:T(8,128)(2,1)S(1)}, u32[]{:S(2)}, u32[]{:S(2)}) collective-permute-start(bf16[48,1024]{1,0:T(8,128)(2,1)S(1)} %get-tuple-element.29), channel_id=1, source_target_pairs={{0,24},{4,28},{8,16},{12,20},{16,8},{20,12},{24,0},{28,4},{1,25},{... | collective-permute-start | bytes 294920 | tf_op jit(solution)/shard_map/ppermute | solution.py:243
  17.1 1.5 %collective-permute-start.4 = (bf16[48,1024]{1,0:T(8,128)(2,1)S(1)}, bf16[48,1024]{1,0:T(8,128)(2,1)S(1)}, u32[]{:S(2)}, u32[]{:S(2)}) collective-permute-start(bf16[48,1024]{1,0:T(8,128)(2,1)S(1)} %get-tuple-element.27), channel_id=1, source_target_pairs={{0,8},{4,12},{8,0},{12,4},{16,24},{20,28},{24,16},{28,20},{1,9},{5... | collective-permute-start | bytes 294920 | tf_op jit(solution)/shard_map/ppermute | solution.py:243
  18.6 0.9 %collective-permute-start.5 = (bf16[48,1024]{1,0:T(8,128)(2,1)S(1)}, bf16[48,1024]{1,0:T(8,128)(2,1)S(1)}, u32[]{:S(2)}, u32[]{:S(2)}) collective-permute-start(bf16[48,1024]{1,0:T(8,128)(2,1)S(1)} %get-tuple-element.28), channel_id=1, source_target_pairs={{0,16},{4,20},{8,24},{12,28},{16,0},{20,4},{24,8},{28,12},{1,17},{... | collective-permute-start | bytes 294920 | tf_op jit(solution)/shard_map/ppermute | solution.py:243
  19.5 2.0 %collective-permute-done.6.refs_3_ = bf16[48,1024]{1,0:T(8,128)(2,1)S(1)} collective-permute-done((bf16[48,1024]{1,0:T(8,128)(2,1)S(1)}, bf16[48,1024]{1,0:T(8,128)(2,1)S(1)}, u32[]{:S(2)}, u32[]{:S(2)}) %collective-permute-start.6) | collective-permute-done | bytes 98336 | tf_op jit(solution)/shard_map/ppermute | solution.py:243
  21.5 0.8 collective-permute-done.4.refs_1_
  22.2 1.0 %collective-permute-done.5.refs_2_ = bf16[48,1024]{1,0:T(8,128)(2,1)S(1)} collective-permute-done((bf16[48,1024]{1,0:T(8,128)(2,1)S(1)}, bf16[48,1024]{1,0:T(8,128)(2,1)S(1)}, u32[]{:S(2)}, u32[]{:S(2)}) %collective-permute-start.5) | collective-permute-done | bytes 98336 | tf_op jit(solution)/shard_map/ppermute | solution.py:243
  23.2 0.3 collective-permute-done.8.refs_5_
  23.5 1.0 %collective-permute-done.9.refs_6_ = bf16[48,1024]{1,0:T(8,128)(2,1)S(1)} collective-permute-done((bf16[48,1024]{1,0:T(8,128)(2,1)S(1)}, bf16[48,1024]{1,0:T(8,128)(2,1)S(1)}, u32[]{:S(2)}, u32[]{:S(2)}) %collective-permute-start.9) | collective-permute-done | bytes 98336 | tf_op jit(solution)/shard_map/ppermute | solution.py:233
  24.6 2.7 %collective-permute-start.11 = (bf16[192,512]{1,0:T(8,128)(2,1)S(1)}, bf16[192,512]{1,0:T(8,128)(2,1)S(1)}, u32[]{:S(2)}, u32[]{:S(2)}) collective-permute-start(bf16[192,512]{1,0:T(8,128)(2,1)S(1)} %add_blocks.2.refs_0_), channel_id=1, source_target_pairs={{0,2},{1,3},{2,0},{3,1},{4,6},{5,7},{6,4},{7,5},{8,10},{9,11},{10,... | collective-permute-start | bytes 589832 | tf_op jit(solution)/shard_map/ppermute | solution.py:276
  27.2 0.3 pick.3
  27.5 0.6 collective-permute-start.13
  28.1 1.1 %collective-permute-start.14 = (bf16[48,1024]{1,0:T(8,128)(2,1)S(1)}, bf16[48,1024]{1,0:T(8,128)(2,1)S(1)}, u32[]{:S(2)}, u32[]{:S(2)}) collective-permute-start(bf16[48,1024]{1,0:T(8,128)(2,1)S(1)} %get-tuple-element.30.refs_0_), channel_id=1, source_target_pairs={{0,16},{4,20},{8,24},{12,28},{16,0},{20,4},{24,8},{28,12},{1,17},{... | collective-permute-start | bytes 294920 | tf_op jit(solution)/shard_map/ppermute | solution.py:243
  29.3 1.8 %collective-permute-start.15 = (bf16[48,1024]{1,0:T(8,128)(2,1)S(1)}, bf16[48,1024]{1,0:T(8,128)(2,1)S(1)}, u32[]{:S(2)}, u32[]{:S(2)}) collective-permute-start(bf16[48,1024]{1,0:T(8,128)(2,1)S(1)} %get-tuple-element.31), channel_id=1, source_target_pairs={{0,24},{4,28},{8,16},{12,20},{16,8},{20,12},{24,0},{28,4},{1,25},{... | collective-permute-start | bytes 294920 | tf_op jit(solution)/shard_map/ppermute | solution.py:243
  31.1 1.8 %collective-permute-done.13.refs_1_ = bf16[48,1024]{1,0:T(8,128)(2,1)S(1)} collective-permute-done((bf16[48,1024]{1,0:T(8,128)(2,1)S(1)}, bf16[48,1024]{1,0:T(8,128)(2,1)S(1)}, u32[]{:S(2)}, u32[]{:S(2)}) %collective-permute-start.13) | collective-permute-done | bytes 98336 | tf_op jit(solution)/shard_map/ppermute | solution.py:243
  32.9 1.9 %collective-permute-done.14.refs_2_ = bf16[48,1024]{1,0:T(8,128)(2,1)S(1)} collective-permute-done((bf16[48,1024]{1,0:T(8,128)(2,1)S(1)}, bf16[48,1024]{1,0:T(8,128)(2,1)S(1)}, u32[]{:S(2)}, u32[]{:S(2)}) %collective-permute-start.14) | collective-permute-done | bytes 98336 | tf_op jit(solution)/shard_map/ppermute | solution.py:243
  34.9 2.4 %backward.1 = (bf16[48,1024]{1,0:T(8,128)(2,1)S(1)}, bf16[48,1024]{1,0:T(8,128)(2,1)S(1)}, bf16[48,1024]{1,0:T(8,128)(2,1)S(1)}, bf16[48,1024]{1,0:T(8,128)(2,1)S(1)}) custom-call(bf16[48,1024]{1,0:T(8,128)(2,1)S(1)} %get-tuple-element.30.refs_0_, bf16[48,1024]{1,0:T(8,128)(2,1)S(1)} %collective-permute-done.13.refs_1_, ...), custom_call_target="tpu_custom_call" | custom-call | flops 905969664 | bytes 10813440 | tf_op jit(solution)/shard_map/backward/pallas_call | solution.py:23
  37.3 1.6 %collective-permute-start.19 = (bf16[48,1024]{1,0:T(8,128)(2,1)S(1)}, bf16[48,1024]{1,0:T(8,128)(2,1)S(1)}, u32[]{:S(2)}, u32[]{:S(2)}) collective-permute-start(bf16[48,1024]{1,0:T(8,128)(2,1)S(1)} %get-tuple-element.41), channel_id=1, source_target_pairs={{0,8},{4,12},{8,0},{12,4},{16,24},{20,28},{24,16},{28,20},{1,9},{5... | collective-permute-start | bytes 294920 | tf_op jit(solution)/shard_map/ppermute | solution.py:243
  38.9 0.9 %collective-permute-start.20 = (bf16[48,1024]{1,0:T(8,128)(2,1)S(1)}, bf16[48,1024]{1,0:T(8,128)(2,1)S(1)}, u32[]{:S(2)}, u32[]{:S(2)}) collective-permute-start(bf16[48,1024]{1,0:T(8,128)(2,1)S(1)} %get-tuple-element.42), channel_id=1, source_target_pairs={{0,16},{4,20},{8,24},{12,28},{16,0},{20,4},{24,8},{28,12},{1,17},{... | collective-permute-start | bytes 294920 | tf_op jit(solution)/shard_map/ppermute | solution.py:243
  39.7 1.1 %collective-permute-start.21 = (bf16[48,1024]{1,0:T(8,128)(2,1)S(1)}, bf16[48,1024]{1,0:T(8,128)(2,1)S(1)}, u32[]{:S(2)}, u32[]{:S(2)}) collective-permute-start(bf16[48,1024]{1,0:T(8,128)(2,1)S(1)} %get-tuple-element.43), channel_id=1, source_target_pairs={{0,24},{4,28},{8,16},{12,20},{16,8},{20,12},{24,0},{28,4},{1,25},{... | collective-permute-start | bytes 294920 | tf_op jit(solution)/shard_map/ppermute | solution.py:243
  40.9 1.8 %collective-permute-done.19.refs_1_ = bf16[48,1024]{1,0:T(8,128)(2,1)S(1)} collective-permute-done((bf16[48,1024]{1,0:T(8,128)(2,1)S(1)}, bf16[48,1024]{1,0:T(8,128)(2,1)S(1)}, u32[]{:S(2)}, u32[]{:S(2)}) %collective-permute-start.19) | collective-permute-done | bytes 98336 | tf_op jit(solution)/shard_map/ppermute | solution.py:243
  42.7 3.3 %collective-permute-start.16 = (bf16[192,512]{1,0:T(8,128)(2,1)S(1)}, bf16[192,512]{1,0:T(8,128)(2,1)S(1)}, u32[]{:S(2)}, u32[]{:S(2)}) collective-permute-start(bf16[192,512]{1,0:T(8,128)(2,1)S(1)} %add_blocks.2.refs_0_), channel_id=1, source_target_pairs={{0,1},{1,2},{2,3},{4,5},{5,6},{6,7},{8,9},{9,10},{10,11},{12,13},{... | collective-permute-start | bytes 589832 | tf_op jit(solution)/shard_map/ppermute | solution.py:277
  45.9 1.3 %collective-permute-start.17 = (bf16[192,512]{1,0:T(8,128)(2,1)S(1)}, bf16[192,512]{1,0:T(8,128)(2,1)S(1)}, u32[]{:S(2)}, u32[]{:S(2)}) collective-permute-start(bf16[192,512]{1,0:T(8,128)(2,1)S(1)} %add_blocks.2.refs_0_), channel_id=1, source_target_pairs={{1,0},{2,1},{3,2},{5,4},{6,5},{7,6},{9,8},{10,9},{11,10},{13,12},{... | collective-permute-start | bytes 589832 | tf_op jit(solution)/shard_map/ppermute | solution.py:278
  47.3 1.3 %collective-permute-start.18 = (bf16[192,512]{1,0:T(8,128)(2,1)S(1)}, bf16[192,512]{1,0:T(8,128)(2,1)S(1)}, u32[]{:S(2)}, u32[]{:S(2)}) collective-permute-start(bf16[192,512]{1,0:T(8,128)(2,1)S(1)} %collective-permute-done.11.refs_1_), channel_id=1, source_target_pairs={{2,3},{1,0},{6,7},{5,4},{10,11},{9,8},{14,15},{13,12},{18,19},{17,... | collective-permute-start | bytes 589832 | tf_op jit(solution)/shard_map/ppermute | solution.py:279
  49.1 0.8 collective-permute-done.24.refs_6_
  50.2 5.5 %collective-permute-start.26 = (bf16[192,512]{1,0:T(8,128)(2,1)S(1)}, bf16[192,512]{1,0:T(8,128)(2,1)S(1)}, u32[]{:S(2)}, u32[]{:S(2)}) collective-permute-start(bf16[192,512]{1,0:T(8,128)(2,1)S(1)} %add_blocks.3.refs_0_), channel_id=1, source_target_pairs={{0,2},{1,3},{2,0},{3,1},{4,6},{5,7},{6,4},{7,5},{8,10},{9,11},{10,... | collective-permute-start | bytes 589832 | tf_op jit(solution)/shard_map/ppermute | solution.py:276
  55.7 0.3 weights.1.weight_ref
  56.0 3.1 %collective-permute-done.18.refs_4_ = bf16[192,512]{1,0:T(8,128)(2,1)S(1)} collective-permute-done((bf16[192,512]{1,0:T(8,128)(2,1)S(1)}, bf16[192,512]{1,0:T(8,128)(2,1)S(1)}, u32[]{:S(2)}, u32[]{:S(2)}) %collective-permute-start.18) | collective-permute-done | bytes 196640 | tf_op jit(solution)/shard_map/ppermute | solution.py:279
  59.2 1.7 %combine_gate.1 = (bf16[512,512]{1,0:T(8,128)(2,1)}, f32[8,512]{1,0:T(8,128)S(1)}) custom-call(bf16[512,768]{1,0:T(8,128)(2,1)S(1)} %weights.1.weight_ref, s32[8,512]{1,0:T(8,128)S(1)} %bitcast.7, f32[16,512]{1,0:T(8,128)S(1)} %number.1.key_ref, bf16[512,512]{1,0:T(8,128)(2,1)S(1)} %copy-done.7, bf16[192,512]{1,0:T(8,128)(2,1)S(1)} %add_blocks.2.refs_0_, ...), custom_call_target="tpu_custom_call" | custom-call | flops 805306368 | bytes 2883584 | tf_op jit(solution)/shard_map/combine_gate/pallas_call | solution.py:23
  60.9 1.2 %collective-permute-done.30 = f32[8,512]{1,0:T(8,128)S(1)} collective-permute-done((f32[8,512]{1,0:T(8,128)S(1)}, f32[8,512]{1,0:T(8,128)S(1)}, u32[]{:S(2)}, u32[]{:S(2)}) %collective-permute-start.30) | collective-permute-done | bytes 16416 | tf_op jit(solution)/shard_map/ppermute | solution.py:233
  62.1 1.8 %collective-permute-start.31 = (f32[8,512]{1,0:T(8,128)S(1)}, f32[8,512]{1,0:T(8,128)S(1)}, u32[]{:S(2)}, u32[]{:S(2)}) collective-permute-start(f32[8,512]{1,0:T(8,128)S(1)} %add.6), channel_id=1, source_target_pairs={{0,8},{4,12},{8,0},{12,4},{16,24},{20,28},{24,16},{28,20},{1,9},{5... | collective-permute-start | bytes 49160 | tf_op jit(solution)/shard_map/ppermute | solution.py:243
  63.9 1.4 %collective-permute-start.27 = (bf16[192,512]{1,0:T(8,128)(2,1)S(1)}, bf16[192,512]{1,0:T(8,128)(2,1)S(1)}, u32[]{:S(2)}, u32[]{:S(2)}) collective-permute-start(bf16[192,512]{1,0:T(8,128)(2,1)S(1)} %add_blocks.3.refs_0_), channel_id=1, source_target_pairs={{0,1},{1,2},{2,3},{4,5},{5,6},{6,7},{8,9},{9,10},{10,11},{12,13},{... | collective-permute-start | bytes 589832 | tf_op jit(solution)/shard_map/ppermute | solution.py:277
  65.3 1.3 %collective-permute-start.28 = (bf16[192,512]{1,0:T(8,128)(2,1)S(1)}, bf16[192,512]{1,0:T(8,128)(2,1)S(1)}, u32[]{:S(2)}, u32[]{:S(2)}) collective-permute-start(bf16[192,512]{1,0:T(8,128)(2,1)S(1)} %add_blocks.3.refs_0_), channel_id=1, source_target_pairs={{1,0},{2,1},{3,2},{5,4},{6,5},{7,6},{9,8},{10,9},{11,10},{13,12},{... | collective-permute-start | bytes 589832 | tf_op jit(solution)/shard_map/ppermute | solution.py:278
  66.6 1.3 %collective-permute-start.29 = (bf16[192,512]{1,0:T(8,128)(2,1)S(1)}, bf16[192,512]{1,0:T(8,128)(2,1)S(1)}, u32[]{:S(2)}, u32[]{:S(2)}) collective-permute-start(bf16[192,512]{1,0:T(8,128)(2,1)S(1)} %collective-permute-done.26.refs_1_), channel_id=1, source_target_pairs={{2,3},{1,0},{6,7},{5,4},{10,11},{9,8},{14,15},{13,12},{18,19},{17,... | collective-permute-start | bytes 589832 | tf_op jit(solution)/shard_map/ppermute | solution.py:279
  67.9 0.6 add_bitcast_fusion
  68.5 1.1 %collective-permute-done.27.refs_2_ = bf16[192,512]{1,0:T(8,128)(2,1)S(1)} collective-permute-done((bf16[192,512]{1,0:T(8,128)(2,1)S(1)}, bf16[192,512]{1,0:T(8,128)(2,1)S(1)}, u32[]{:S(2)}, u32[]{:S(2)}) %collective-permute-start.27) | collective-permute-done | bytes 196640 | tf_op jit(solution)/shard_map/ppermute | solution.py:277
  69.6 5.4 %collective-permute-done.28.refs_3_ = bf16[192,512]{1,0:T(8,128)(2,1)S(1)} collective-permute-done((bf16[192,512]{1,0:T(8,128)(2,1)S(1)}, bf16[192,512]{1,0:T(8,128)(2,1)S(1)}, u32[]{:S(2)}, u32[]{:S(2)}) %collective-permute-start.28) | collective-permute-done | bytes 196640 | tf_op jit(solution)/shard_map/ppermute | solution.py:278
  75.0 2.9 %collective-permute-done.29.refs_4_ = bf16[192,512]{1,0:T(8,128)(2,1)S(1)} collective-permute-done((bf16[192,512]{1,0:T(8,128)(2,1)S(1)}, bf16[192,512]{1,0:T(8,128)(2,1)S(1)}, u32[]{:S(2)}, u32[]{:S(2)}) %collective-permute-start.29) | collective-permute-done | bytes 196640 | tf_op jit(solution)/shard_map/ppermute | solution.py:279
  78.0 1.4 %combine.1 = bf16[512,512]{1,0:T(8,128)(2,1)} custom-call(bf16[512,768]{1,0:T(8,128)(2,1)S(1)} %weights.1.weight_ref, bf16[192,512]{1,0:T(8,128)(2,1)S(1)} %add_blocks.3.refs_0_, bf16[192,512]{1,0:T(8,128)(2,1)S(1)} %collective-permute-done.26.refs_1_, bf16[192,512]{1,0:T(8,128)(2,1)S(1)} %collective-permute-done.27.refs_2_, ...), custom_call_target="tpu_custom_call" | custom-call | flops 402653184 | bytes 2293760 | tf_op jit(solution)/shard_map/combine/pallas_call | solution.py:23
  (44 shorter events, 1.3 us)
Async XLA Ops:
  0.6 2.3 %collective-permute-start = (bf16[512,512]{1,0:T(8,128)(2,1)}, bf16[512,512]{1,0:T(8,128)(2,1)S(1)}, u32[]{:S(2)}, u32[]{:S(2)}) collective-permute-start(bf16[512,512]{1,0:T(8,128)(2,1)} %refs_0_.2), channel_id=1, source_target_pairs={{0,4},{4,0},{8,12},{12,8},{1,5},{5,1},{9,13},{13,9},{2,6},{6,2},{1... | collective-permute-start | bytes 1572872 | tf_op jit(solution)/shard_map/ppermute | solution.py:233
  1.1 26.1 %collective-permute-start.12 = (bf16[512,512]{1,0:T(8,128)(2,1)}, bf16[512,512]{1,0:T(8,128)(2,1)S(1)}, u32[]{:S(2)}, u32[]{:S(2)}) collective-permute-start(bf16[512,512]{1,0:T(8,128)(2,1)} %grads_ref.1), channel_id=1, source_target_pairs={{0,4},{4,0},{8,12},{12,8},{1,5},{5,1},{9,13},{13,9},{2,6},{6,2},{1... | collective-permute-start | bytes 1572872 | tf_op jit(solution)/shard_map/ppermute | solution.py:233
  1.2 0.7 copy-start.4
  1.9 1.0 %copy-start.6 = (bf16[512,512]{1,0:T(8,128)(2,1)S(1)}, bf16[512,512]{1,0:T(8,128)(2,1)}, u32[]{:S(2)}) copy-start(bf16[512,512]{1,0:T(8,128)(2,1)} %refs_0_.2) | copy-start | bytes 1572868
  2.1 11.2 %copy-start = (bf16[1,768,2048]{2,1,0:T(8,128)(2,1)S(1)}, bf16[1,768,2048]{2,1,0:T(8,128)(2,1)}, u32[]{:S(2)}) copy-start(bf16[1,768,2048]{2,1,0:T(8,128)(2,1)} %refs_4_.3) | copy-start | bytes 9437188
  2.1 11.2 %copy-start.1 = (bf16[1,768,2048]{2,1,0:T(8,128)(2,1)S(1)}, bf16[1,768,2048]{2,1,0:T(8,128)(2,1)}, u32[]{:S(2)}) copy-start(bf16[1,768,2048]{2,1,0:T(8,128)(2,1)} %refs_5_.3) | copy-start | bytes 9437188
  2.1 11.2 %copy-start.2 = (bf16[1,768,2048]{2,1,0:T(8,128)(2,1)S(1)}, bf16[1,768,2048]{2,1,0:T(8,128)(2,1)}, u32[]{:S(2)}) copy-start(bf16[1,768,2048]{2,1,0:T(8,128)(2,1)} %refs_6_.3) | copy-start | bytes 9437188
  3.3 6.1 %collective-permute-start.1 = (bf16[48,1024]{1,0:T(8,128)(2,1)S(1)}, bf16[48,1024]{1,0:T(8,128)(2,1)S(1)}, u32[]{:S(2)}, u32[]{:S(2)}) collective-permute-start(bf16[48,1024]{1,0:T(8,128)(2,1)S(1)} %get-tuple-element.25), channel_id=1, source_target_pairs={{0,8},{4,12},{8,0},{12,4},{16,24},{20,28},{24,16},{28,20},{1,9},{5... | collective-permute-start | bytes 294920 | tf_op jit(solution)/shard_map/ppermute | solution.py:243
  6.3 21.0 %copy-start.7 = (bf16[512,512]{1,0:T(8,128)(2,1)S(1)}, bf16[512,512]{1,0:T(8,128)(2,1)}, u32[]{:S(2)}) copy-start(bf16[512,512]{1,0:T(8,128)(2,1)} %grads_ref.1) | copy-start | bytes 1572868
  6.3 5.7 %collective-permute-start.2 = (bf16[48,1024]{1,0:T(8,128)(2,1)S(1)}, bf16[48,1024]{1,0:T(8,128)(2,1)S(1)}, u32[]{:S(2)}, u32[]{:S(2)}) collective-permute-start(bf16[48,1024]{1,0:T(8,128)(2,1)S(1)} %get-tuple-element.24.refs_0_), channel_id=1, source_target_pairs={{0,16},{4,20},{8,24},{12,28},{16,0},{20,4},{24,8},{28,12},{1,17},{... | collective-permute-start | bytes 294920 | tf_op jit(solution)/shard_map/ppermute | solution.py:243
  7.8 5.5 %collective-permute-start.3 = (bf16[48,1024]{1,0:T(8,128)(2,1)S(1)}, bf16[48,1024]{1,0:T(8,128)(2,1)S(1)}, u32[]{:S(2)}, u32[]{:S(2)}) collective-permute-start(bf16[48,1024]{1,0:T(8,128)(2,1)S(1)} %get-tuple-element.25), channel_id=1, source_target_pairs={{0,24},{4,28},{8,16},{12,20},{16,8},{20,12},{24,0},{28,4},{1,25},{... | collective-permute-start | bytes 294920 | tf_op jit(solution)/shard_map/ppermute | solution.py:243
  15.9 5.6 %collective-permute-start.6 = (bf16[48,1024]{1,0:T(8,128)(2,1)S(1)}, bf16[48,1024]{1,0:T(8,128)(2,1)S(1)}, u32[]{:S(2)}, u32[]{:S(2)}) collective-permute-start(bf16[48,1024]{1,0:T(8,128)(2,1)S(1)} %get-tuple-element.29), channel_id=1, source_target_pairs={{0,24},{4,28},{8,16},{12,20},{16,8},{20,12},{24,0},{28,4},{1,25},{... | collective-permute-start | bytes 294920 | tf_op jit(solution)/shard_map/ppermute | solution.py:243
  17.1 5.2 %collective-permute-start.4 = (bf16[48,1024]{1,0:T(8,128)(2,1)S(1)}, bf16[48,1024]{1,0:T(8,128)(2,1)S(1)}, u32[]{:S(2)}, u32[]{:S(2)}) collective-permute-start(bf16[48,1024]{1,0:T(8,128)(2,1)S(1)} %get-tuple-element.27), channel_id=1, source_target_pairs={{0,8},{4,12},{8,0},{12,4},{16,24},{20,28},{24,16},{28,20},{1,9},{5... | collective-permute-start | bytes 294920 | tf_op jit(solution)/shard_map/ppermute | solution.py:243
  18.6 4.6 %collective-permute-start.5 = (bf16[48,1024]{1,0:T(8,128)(2,1)S(1)}, bf16[48,1024]{1,0:T(8,128)(2,1)S(1)}, u32[]{:S(2)}, u32[]{:S(2)}) collective-permute-start(bf16[48,1024]{1,0:T(8,128)(2,1)S(1)} %get-tuple-element.28), channel_id=1, source_target_pairs={{0,16},{4,20},{8,24},{12,28},{16,0},{20,4},{24,8},{28,12},{1,17},{... | collective-permute-start | bytes 294920 | tf_op jit(solution)/shard_map/ppermute | solution.py:243
  19.5 3.8 %collective-permute-start.7 = (bf16[48,1024]{1,0:T(8,128)(2,1)S(1)}, bf16[48,1024]{1,0:T(8,128)(2,1)S(1)}, u32[]{:S(2)}, u32[]{:S(2)}) collective-permute-start(bf16[48,1024]{1,0:T(8,128)(2,1)S(1)} %get-tuple-element.26.refs_0_), channel_id=1, source_target_pairs={{0,4},{4,0},{8,12},{12,8},{1,5},{5,1},{9,13},{13,9},{2,6},{6,2},{1... | collective-permute-start | bytes 294920 | tf_op jit(solution)/shard_map/ppermute | solution.py:233
  21.5 1.7 %collective-permute-start.10 = (bf16[48,1024]{1,0:T(8,128)(2,1)S(1)}, bf16[48,1024]{1,0:T(8,128)(2,1)S(1)}, u32[]{:S(2)}, u32[]{:S(2)}) collective-permute-start(bf16[48,1024]{1,0:T(8,128)(2,1)S(1)} %collective-permute-done.6.refs_3_), channel_id=1, source_target_pairs={{0,4},{4,0},{8,12},{12,8},{1,5},{5,1},{9,13},{13,9},{2,6},{6,2},{1... | collective-permute-start | bytes 294920 | tf_op jit(solution)/shard_map/ppermute | solution.py:233
  22.2 1.3 %collective-permute-start.8 = (bf16[48,1024]{1,0:T(8,128)(2,1)S(1)}, bf16[48,1024]{1,0:T(8,128)(2,1)S(1)}, u32[]{:S(2)}, u32[]{:S(2)}) collective-permute-start(bf16[48,1024]{1,0:T(8,128)(2,1)S(1)} %collective-permute-done.4.refs_1_), channel_id=1, source_target_pairs={{0,4},{4,0},{8,12},{12,8},{1,5},{5,1},{9,13},{13,9},{2,6},{6,2},{1... | collective-permute-start | bytes 294920 | tf_op jit(solution)/shard_map/ppermute | solution.py:233
  23.2 1.3 %collective-permute-start.9 = (bf16[48,1024]{1,0:T(8,128)(2,1)S(1)}, bf16[48,1024]{1,0:T(8,128)(2,1)S(1)}, u32[]{:S(2)}, u32[]{:S(2)}) collective-permute-start(bf16[48,1024]{1,0:T(8,128)(2,1)S(1)} %collective-permute-done.5.refs_2_), channel_id=1, source_target_pairs={{0,4},{4,0},{8,12},{12,8},{1,5},{5,1},{9,13},{13,9},{2,6},{6,2},{1... | collective-permute-start | bytes 294920 | tf_op jit(solution)/shard_map/ppermute | solution.py:233
  24.6 12.8 %collective-permute-start.11 = (bf16[192,512]{1,0:T(8,128)(2,1)S(1)}, bf16[192,512]{1,0:T(8,128)(2,1)S(1)}, u32[]{:S(2)}, u32[]{:S(2)}) collective-permute-start(bf16[192,512]{1,0:T(8,128)(2,1)S(1)} %add_blocks.2.refs_0_), channel_id=1, source_target_pairs={{0,2},{1,3},{2,0},{3,1},{4,6},{5,7},{6,4},{7,5},{8,10},{9,11},{10,... | collective-permute-start | bytes 589832 | tf_op jit(solution)/shard_map/ppermute | solution.py:276
  27.5 5.4 %collective-permute-start.13 = (bf16[48,1024]{1,0:T(8,128)(2,1)S(1)}, bf16[48,1024]{1,0:T(8,128)(2,1)S(1)}, u32[]{:S(2)}, u32[]{:S(2)}) collective-permute-start(bf16[48,1024]{1,0:T(8,128)(2,1)S(1)} %get-tuple-element.31), channel_id=1, source_target_pairs={{0,8},{4,12},{8,0},{12,4},{16,24},{20,28},{24,16},{28,20},{1,9},{5... | collective-permute-start | bytes 294920 | tf_op jit(solution)/shard_map/ppermute | solution.py:243
  28.1 6.7 %collective-permute-start.14 = (bf16[48,1024]{1,0:T(8,128)(2,1)S(1)}, bf16[48,1024]{1,0:T(8,128)(2,1)S(1)}, u32[]{:S(2)}, u32[]{:S(2)}) collective-permute-start(bf16[48,1024]{1,0:T(8,128)(2,1)S(1)} %get-tuple-element.30.refs_0_), channel_id=1, source_target_pairs={{0,16},{4,20},{8,24},{12,28},{16,0},{20,4},{24,8},{28,12},{1,17},{... | collective-permute-start | bytes 294920 | tf_op jit(solution)/shard_map/ppermute | solution.py:243
  29.3 5.6 %collective-permute-start.15 = (bf16[48,1024]{1,0:T(8,128)(2,1)S(1)}, bf16[48,1024]{1,0:T(8,128)(2,1)S(1)}, u32[]{:S(2)}, u32[]{:S(2)}) collective-permute-start(bf16[48,1024]{1,0:T(8,128)(2,1)S(1)} %get-tuple-element.31), channel_id=1, source_target_pairs={{0,24},{4,28},{8,16},{12,20},{16,8},{20,12},{24,0},{28,4},{1,25},{... | collective-permute-start | bytes 294920 | tf_op jit(solution)/shard_map/ppermute | solution.py:243
  34.9 20.8 %copy-start.3 = (f32[512,8]{0,1:T(8,128)S(1)}, f32[512,8]{0,1:T(8,128)}, u32[]{:S(2)}) copy-start(f32[512,8]{0,1:T(8,128)} %param.10) | copy-start | bytes 49156
  34.9 20.8 %copy-start.5 = (s32[512,8]{0,1:T(8,128)S(1)}, s32[512,8]{0,1:T(8,128)}, u32[]{:S(2)}) copy-start(s32[512,8]{0,1:T(8,128)} %param.9) | copy-start | bytes 49156
  37.3 5.3 %collective-permute-start.19 = (bf16[48,1024]{1,0:T(8,128)(2,1)S(1)}, bf16[48,1024]{1,0:T(8,128)(2,1)S(1)}, u32[]{:S(2)}, u32[]{:S(2)}) collective-permute-start(bf16[48,1024]{1,0:T(8,128)(2,1)S(1)} %get-tuple-element.41), channel_id=1, source_target_pairs={{0,8},{4,12},{8,0},{12,4},{16,24},{20,28},{24,16},{28,20},{1,9},{5... | collective-permute-start | bytes 294920 | tf_op jit(solution)/shard_map/ppermute | solution.py:243
  38.9 7.0 %collective-permute-start.20 = (bf16[48,1024]{1,0:T(8,128)(2,1)S(1)}, bf16[48,1024]{1,0:T(8,128)(2,1)S(1)}, u32[]{:S(2)}, u32[]{:S(2)}) collective-permute-start(bf16[48,1024]{1,0:T(8,128)(2,1)S(1)} %get-tuple-element.42), channel_id=1, source_target_pairs={{0,16},{4,20},{8,24},{12,28},{16,0},{20,4},{24,8},{28,12},{1,17},{... | collective-permute-start | bytes 294920 | tf_op jit(solution)/shard_map/ppermute | solution.py:243
  39.7 7.5 %collective-permute-start.21 = (bf16[48,1024]{1,0:T(8,128)(2,1)S(1)}, bf16[48,1024]{1,0:T(8,128)(2,1)S(1)}, u32[]{:S(2)}, u32[]{:S(2)}) collective-permute-start(bf16[48,1024]{1,0:T(8,128)(2,1)S(1)} %get-tuple-element.43), channel_id=1, source_target_pairs={{0,24},{4,28},{8,16},{12,20},{16,8},{20,12},{24,0},{28,4},{1,25},{... | collective-permute-start | bytes 294920 | tf_op jit(solution)/shard_map/ppermute | solution.py:243
  40.9 7.7 %collective-permute-start.22 = (bf16[48,1024]{1,0:T(8,128)(2,1)S(1)}, bf16[48,1024]{1,0:T(8,128)(2,1)S(1)}, u32[]{:S(2)}, u32[]{:S(2)}) collective-permute-start(bf16[48,1024]{1,0:T(8,128)(2,1)S(1)} %get-tuple-element.40.refs_0_), channel_id=1, source_target_pairs={{0,4},{4,0},{8,12},{12,8},{1,5},{5,1},{9,13},{13,9},{2,6},{6,2},{1... | collective-permute-start | bytes 294920 | tf_op jit(solution)/shard_map/ppermute | solution.py:233
  42.7 6.2 %collective-permute-start.23 = (bf16[48,1024]{1,0:T(8,128)(2,1)S(1)}, bf16[48,1024]{1,0:T(8,128)(2,1)S(1)}, u32[]{:S(2)}, u32[]{:S(2)}) collective-permute-start(bf16[48,1024]{1,0:T(8,128)(2,1)S(1)} %collective-permute-done.19.refs_1_), channel_id=1, source_target_pairs={{0,4},{4,0},{8,12},{12,8},{1,5},{5,1},{9,13},{13,9},{2,6},{6,2},{1... | collective-permute-start | bytes 294920 | tf_op jit(solution)/shard_map/ppermute | solution.py:233
  42.7 13.4 %collective-permute-start.16 = (bf16[192,512]{1,0:T(8,128)(2,1)S(1)}, bf16[192,512]{1,0:T(8,128)(2,1)S(1)}, u32[]{:S(2)}, u32[]{:S(2)}) collective-permute-start(bf16[192,512]{1,0:T(8,128)(2,1)S(1)} %add_blocks.2.refs_0_), channel_id=1, source_target_pairs={{0,1},{1,2},{2,3},{4,5},{5,6},{6,7},{8,9},{9,10},{10,11},{12,13},{... | collective-permute-start | bytes 589832 | tf_op jit(solution)/shard_map/ppermute | solution.py:277
  45.9 10.1 %collective-permute-start.17 = (bf16[192,512]{1,0:T(8,128)(2,1)S(1)}, bf16[192,512]{1,0:T(8,128)(2,1)S(1)}, u32[]{:S(2)}, u32[]{:S(2)}) collective-permute-start(bf16[192,512]{1,0:T(8,128)(2,1)S(1)} %add_blocks.2.refs_0_), channel_id=1, source_target_pairs={{1,0},{2,1},{3,2},{5,4},{6,5},{7,6},{9,8},{10,9},{11,10},{13,12},{... | collective-permute-start | bytes 589832 | tf_op jit(solution)/shard_map/ppermute | solution.py:278
  47.3 11.9 %collective-permute-start.18 = (bf16[192,512]{1,0:T(8,128)(2,1)S(1)}, bf16[192,512]{1,0:T(8,128)(2,1)S(1)}, u32[]{:S(2)}, u32[]{:S(2)}) collective-permute-start(bf16[192,512]{1,0:T(8,128)(2,1)S(1)} %collective-permute-done.11.refs_1_), channel_id=1, source_target_pairs={{2,3},{1,0},{6,7},{5,4},{10,11},{9,8},{14,15},{13,12},{18,19},{17,... | collective-permute-start | bytes 589832 | tf_op jit(solution)/shard_map/ppermute | solution.py:279
  48.6 1.4 %collective-permute-start.24 = (bf16[48,1024]{1,0:T(8,128)(2,1)S(1)}, bf16[48,1024]{1,0:T(8,128)(2,1)S(1)}, u32[]{:S(2)}, u32[]{:S(2)}) collective-permute-start(bf16[48,1024]{1,0:T(8,128)(2,1)S(1)} %collective-permute-done.20.refs_2_), channel_id=1, source_target_pairs={{0,4},{4,0},{8,12},{12,8},{1,5},{5,1},{9,13},{13,9},{2,6},{6,2},{1... | collective-permute-start | bytes 294920 | tf_op jit(solution)/shard_map/ppermute | solution.py:233
  48.9 1.3 %collective-permute-start.25 = (bf16[48,1024]{1,0:T(8,128)(2,1)S(1)}, bf16[48,1024]{1,0:T(8,128)(2,1)S(1)}, u32[]{:S(2)}, u32[]{:S(2)}) collective-permute-start(bf16[48,1024]{1,0:T(8,128)(2,1)S(1)} %collective-permute-done.21.refs_3_), channel_id=1, source_target_pairs={{0,4},{4,0},{8,12},{12,8},{1,5},{5,1},{9,13},{13,9},{2,6},{6,2},{1... | collective-permute-start | bytes 294920 | tf_op jit(solution)/shard_map/ppermute | solution.py:233
  50.2 16.4 %collective-permute-start.26 = (bf16[192,512]{1,0:T(8,128)(2,1)S(1)}, bf16[192,512]{1,0:T(8,128)(2,1)S(1)}, u32[]{:S(2)}, u32[]{:S(2)}) collective-permute-start(bf16[192,512]{1,0:T(8,128)(2,1)S(1)} %add_blocks.3.refs_0_), channel_id=1, source_target_pairs={{0,2},{1,3},{2,0},{3,1},{4,6},{5,7},{6,4},{7,5},{8,10},{9,11},{10,... | collective-permute-start | bytes 589832 | tf_op jit(solution)/shard_map/ppermute | solution.py:276
  60.9 1.2 %collective-permute-start.30 = (f32[8,512]{1,0:T(8,128)S(1)}, f32[8,512]{1,0:T(8,128)S(1)}, u32[]{:S(2)}, u32[]{:S(2)}) collective-permute-start(f32[8,512]{1,0:T(8,128)S(1)} %get-tuple-element.44), channel_id=1, source_target_pairs={{0,4},{4,0},{8,12},{12,8},{1,5},{5,1},{9,13},{13,9},{2,6},{6,2},{1... | collective-permute-start | bytes 49160 | tf_op jit(solution)/shard_map/ppermute | solution.py:233
  62.1 5.8 %collective-permute-start.31 = (f32[8,512]{1,0:T(8,128)S(1)}, f32[8,512]{1,0:T(8,128)S(1)}, u32[]{:S(2)}, u32[]{:S(2)}) collective-permute-start(f32[8,512]{1,0:T(8,128)S(1)} %add.6), channel_id=1, source_target_pairs={{0,8},{4,12},{8,0},{12,4},{16,24},{20,28},{24,16},{28,20},{1,9},{5... | collective-permute-start | bytes 49160 | tf_op jit(solution)/shard_map/ppermute | solution.py:243
  63.9 5.8 %collective-permute-start.27 = (bf16[192,512]{1,0:T(8,128)(2,1)S(1)}, bf16[192,512]{1,0:T(8,128)(2,1)S(1)}, u32[]{:S(2)}, u32[]{:S(2)}) collective-permute-start(bf16[192,512]{1,0:T(8,128)(2,1)S(1)} %add_blocks.3.refs_0_), channel_id=1, source_target_pairs={{0,1},{1,2},{2,3},{4,5},{5,6},{6,7},{8,9},{9,10},{10,11},{12,13},{... | collective-permute-start | bytes 589832 | tf_op jit(solution)/shard_map/ppermute | solution.py:277
  65.3 9.7 %collective-permute-start.28 = (bf16[192,512]{1,0:T(8,128)(2,1)S(1)}, bf16[192,512]{1,0:T(8,128)(2,1)S(1)}, u32[]{:S(2)}, u32[]{:S(2)}) collective-permute-start(bf16[192,512]{1,0:T(8,128)(2,1)S(1)} %add_blocks.3.refs_0_), channel_id=1, source_target_pairs={{1,0},{2,1},{3,2},{5,4},{6,5},{7,6},{9,8},{10,9},{11,10},{13,12},{... | collective-permute-start | bytes 589832 | tf_op jit(solution)/shard_map/ppermute | solution.py:278
  66.6 11.3 %collective-permute-start.29 = (bf16[192,512]{1,0:T(8,128)(2,1)S(1)}, bf16[192,512]{1,0:T(8,128)(2,1)S(1)}, u32[]{:S(2)}, u32[]{:S(2)}) collective-permute-start(bf16[192,512]{1,0:T(8,128)(2,1)S(1)} %collective-permute-done.26.refs_1_), channel_id=1, source_target_pairs={{2,3},{1,0},{6,7},{5,4},{10,11},{9,8},{14,15},{13,12},{18,19},{17,... | collective-permute-start | bytes 589832 | tf_op jit(solution)/shard_map/ppermute | solution.py:279

commit v5 on v4

--- a/solution.py
+++ b/solution.py
@@ -147,14 +147,13 @@
 
 
 def slot_experts(chips, cores, columns):
-    chip, core, e = position(cores)
+    chip, core, _ = position(cores)
     experts = []
     for dz in range(columns):
         for dh in range(chips):
             for dc in range(cores):
-                column = lax.rem(e - dz + columns, columns)
                 owner = lax.rem(chip - dh + chips, chips)
-                experts.append((column * chips + owner) * cores + lax.rem(core - dc + cores, cores))
+                experts.append((dz * chips + owner) * cores + lax.rem(core - dc + cores, cores))
     return experts
 
 
@@ -175,29 +174,11 @@
         out_ref[:, start : start + step] = all_ref[start : start + step, :].T.astype(BF16)
 
 
-def place_parts(parts, all_ref, columns):
-    height = parts[0].shape[0]
-    if len(parts) == columns:
-        for index, part in enumerate(parts):
-            all_ref[index * height : (index + 1) * height, :] = part[...]
-        return
-    own, far, up, down, ends = parts
-    e = lax.axis_index("expert")
-    all_ref[0:height, :] = own[...]
-    all_ref[2 * height : 3 * height, :] = far[...]
-    all_ref[height : 2 * height, :] = jnp.where(e == 0, ends[...], up[...])
-    all_ref[3 * height : 4 * height, :] = jnp.where(e == columns - 1, ends[...], down[...])
-
-
-def combine_kernel(columns, weight_ref, *refs):
-    parts, (out_ref, all_ref) = refs[:-2], refs[-2:]
-    place_parts(parts, all_ref, columns)
+def combine_kernel(weight_ref, all_ref, out_ref):
     out_ref[...] = jnp.dot(weight_ref[...], all_ref[...], preferred_element_type=F32).astype(BF16)
 
 
-def combine_gate_kernel(chips, cores, columns, weight_ref, routes_ref, key_ref, grads_ref, *refs):
-    parts, (out_ref, gate_ref, all_ref, sum_ref) = refs[:-4], refs[-4:]
-    place_parts(parts, all_ref, columns)
+def combine_gate_kernel(chips, cores, columns, weight_ref, routes_ref, key_ref, grads_ref, all_ref, out_ref, gate_ref, sum_ref):
     out_ref[...] = jnp.dot(weight_ref[...], all_ref[...], preferred_element_type=F32).astype(BF16)
     rows = key_ref.shape[1]
     slot = lax.broadcasted_iota(jnp.int32, (CAP, rows), 0).astype(F32)
@@ -245,45 +226,41 @@
     hops = [(db, dh) for db in range(n_dp) for dh in range(chips)]
     order = sorted(range(count), key=lambda index: (hops[index][0] == 0, -hops[index][1]))
 
-    def dispatch(key, sources):
-        pieces = call(
+    def pick(key, sources):
+        return call(
             functools.partial(pick_kernel, cores),
             "pick",
             [shape(CAP, cores * width)] * chips,
             [key, *sources],
             EARLY,
         )
+
+    def dispatch(pieces):
         arrived = {index: to_chip(pieces[hops[index][1]], *hops[index]) for index in order}
         return [arrived[index] for index in range(count)]
 
     def give_back(pieces):
         arrived = {index: to_chip(pieces[index], *hops[index]) for index in order}
-        pairs = [[to_core(arrived[index], dc) for index in range(count)] for dc in range(cores)]
+        return [to_core(arrived[index], dc) for dc in range(cores) for index in range(count)]
+
+    def add_blocks(pieces):
         return call(
             functools.partial(add_blocks_kernel, chips, cores),
             "add_blocks",
             shape(slots, width),
-            sum(pairs, []),
+            pieces,
             2 * slots * width,
         )
 
     def across(value):
-        if columns != 4:
-            return [value] + [
-                lax.ppermute(value, "expert", [(z, (z + dz) % columns) for z in range(columns)])
-                for dz in range(1, columns)
-            ]
-        far = lax.ppermute(value, "expert", [(z, (z + 2) % columns) for z in range(columns)])
-        up = lax.ppermute(value, "expert", [(z, z + 1) for z in range(columns - 1)])
-        down = lax.ppermute(value, "expert", [(z + 1, z) for z in range(columns - 1)])
-        ends = lax.ppermute(far, "expert", [(2, 3), (1, 0)])
-        return [value, far, up, down, ends]
+        return lax.all_gather(value, "expert", axis=0, tiled=True)
 
     token_sources = [to_core(tokens, dc) for dc in range(cores)]
     grad_sources = [to_core(grad_out, dc) for dc in range(cores)]
     key = call(number_kernel, "number", shape(experts, rows, F32), [routes_t], EARLY)
-    tok_in = dispatch(key, token_sources)
-    grad_in = dispatch(key, grad_sources)
+    tok_in = dispatch(pick(key, token_sources))
+    tok_in[0], grad_pieces = lax.optimization_barrier((tok_in[0], pick(key, grad_sources)))
+    grad_in = dispatch(grad_pieces)
 
     matmul_flops = 2 * tall * hid_dev * feats
     saved = [shape(tall, hid_dev, F32)] * 2
@@ -297,7 +274,7 @@
         [pltpu.VMEM((tall, feats), BF16), pltpu.VMEM((tall, hid_dev), BF16)],
         limit=24,
     )
-    out_rows = give_back(outs)
+    out_pieces = give_back(outs)
     backs = call(
         functools.partial(backward_kernel, chips, cores, count),
         "backward",
@@ -307,9 +284,9 @@
         [pltpu.VMEM((tall, feats), BF16)] + [pltpu.VMEM((tall, hid_dev), BF16)] * 2,
         limit=24,
     )
-    out_parts = across(out_rows)
-    out_parts[1], backs = lax.optimization_barrier((out_parts[1], backs))
-    back_rows = give_back(backs)
+    out_pieces, backs = lax.optimization_barrier((out_pieces, backs))
+    out_all = across(add_blocks(out_pieces))
+    back_all = across(add_blocks(give_back(backs)))
 
     weight_map = call(
         functools.partial(weights_kernel, chips, cores, columns),
@@ -321,16 +298,14 @@
         limit=16,
     )
 
-    back_parts = across(back_rows)
     combine_flops = 2 * experts * CAP * rows * width
-    all_rows = pltpu.VMEM((experts * CAP, width), BF16)
     mixed, gate_part = call(
         functools.partial(combine_gate_kernel, chips, cores, columns),
         "combine_gate",
         [shape(rows, width), shape(routes_t.shape[0], rows, F32)],
-        [weight_map, routes_t, key, grad_out, *out_parts],
+        [weight_map, routes_t, key, grad_out, out_all],
         2 * combine_flops,
-        [all_rows, pltpu.VMEM((experts * CAP, rows), F32)],
+        [pltpu.VMEM((experts * CAP, rows), F32)],
         limit=24,
     )
     for dc in range(1, cores):
@@ -339,12 +314,11 @@
     for dh in range(1, chips):
         total = total + to_chip(gate_part, 0, dh)
     grad_tokens = call(
-        functools.partial(combine_kernel, columns),
+        combine_kernel,
         "combine",
         shape(rows, width),
-        [weight_map, *back_parts],
+        [weight_map, back_all],
         combine_flops,
-        [all_rows],
         limit=16,
     )
     return (mixed, grad_tokens, total.T)

time: 79.6 us -> 79.4 us (level)
  blocking collectives: 0 us -> 38 us
  waiting for transfers between devices: 31.6 us -> 9.5 us
  starting transfers between devices: 36.2 us -> 20.2 us
    all_gather x0 -> x2, blocking collectives: none -> 38 us  [across(): return lax.all_gather(value, 'expert', axis=0, tiled=True)]
    ppermute x8 -> x0, starting transfers between devices: 18 us -> none  [the longest x2 8.14 us: across(): lax.ppermute(value, 'expert', [(z, (z + 2) % columns) for z in range(colu...]
    ppermute x8 -> x0, waiting for transfers between devices: 12.6 us -> none  [the longest x2 6.08 us: across(): ends = lax.ppermute(far, 'expert', [(2, 3), (1, 0)])]
    ppermute x13, waiting for transfers between devices: 14.8 us -> 7.5 us  [to_chip(): return lax.ppermute(value, ('dp', 'tensor'), pairs)]
    ppermute x11, waiting for transfers between devices: 4.27 us -> 2 us  [to_core(): return lax.ppermute(value, 'tensor', pairs)]
    ppermute x13, starting transfers between devices: 17 us -> 18.1 us  [to_chip(): return lax.ppermute(value, ('dp', 'tensor'), pairs)]
    ppermute x11, starting transfers between devices: 1.19 us -> 2.14 us  [to_core(): return lax.ppermute(value, 'tensor', pairs)]
  transfers between devices with their start and end apart: 32 -> 24, of which waited for: 19 -> 7; matrix products, arithmetic and copies ran while one was open for 1% -> 1% of each run, Pallas kernels for 10% -> 10%
where the time goes in v5:
time: 79.4 us; the launch traced here: 79.2 us
  blocking collectives  38 us (48%)
  starting transfers between devices  20.2 us (25%)
  waiting for transfers between devices  9.5 us (12%)
  Pallas kernels  9.29 us (12%)
  local copies, waits for them, and re-layouts  0.84 us (1%)
    all_gather x2, blocking collectives, across(): return lax.all_gather(value, 'expert', axis=0, tiled=True)  38 us
    ppermute x13, starting transfers between devices, to_chip(): return lax.ppermute(value, ('dp', 'tensor'), pairs)  18.1 us
    pallas_call x10, Pallas kernels, call(): pl.pallas_call(kernel, out_shape=out_shape, in_specs=[spec] * len(operand...  9.29 us
    ppermute x13, waiting for transfers between devices, to_chip(): return lax.ppermute(value, ('dp', 'tensor'), pairs)  7.5 us
    ppermute x11, starting transfers between devices, to_core(): return lax.ppermute(value, 'tensor', pairs)  2.14 us
    ppermute x11, waiting for transfers between devices, to_core(): return lax.ppermute(value, 'tensor', pairs)  2 us
  transfers between devices with their start and end apart: 24, of which 7 were waited for; matrix products, arithmetic and copies ran while one was open for 1% of the time, Pallas kernels for 10%

profile of v5, /device:TPU:0, one launch (start us, length us, event | category | flops | bytes accessed | tf_op | source)
XLA Modules:
  0.0 79.2 jit_solution(350224028322039327)
XLA Ops:
  0.6 0.5 collective-permute-start
  1.1 0.1 collective-permute-start.1
  1.2 0.7 copy-done.4
  1.9 0.1 number.1.key_ref
  2.1 0.8 collective-permute-done.refs_1_
  2.9 0.1 copy-done.6
  3.0 0.3 pick.2
  3.3 3.0 %collective-permute-start.2 = (bf16[48,1024]{1,0:T(8,128)(2,1)S(1)}, bf16[48,1024]{1,0:T(8,128)(2,1)S(1)}, u32[]{:S(2)}, u32[]{:S(2)}) collective-permute-start(bf16[48,1024]{1,0:T(8,128)(2,1)S(1)} %get-tuple-element.38), channel_id=1, source_target_pairs={{0,8},{4,12},{8,0},{12,4},{16,24},{20,28},{24,16},{28,20},{1,9},{5... | collective-permute-start | bytes 294920 | tf_op jit(solution)/shard_map/ppermute | solution.py:224
  6.3 1.5 %collective-permute-start.4 = (bf16[48,1024]{1,0:T(8,128)(2,1)S(1)}, bf16[48,1024]{1,0:T(8,128)(2,1)S(1)}, u32[]{:S(2)}, u32[]{:S(2)}) collective-permute-start(bf16[48,1024]{1,0:T(8,128)(2,1)S(1)} %get-tuple-element.38), channel_id=1, source_target_pairs={{0,24},{4,28},{8,16},{12,20},{16,8},{20,12},{24,0},{28,4},{1,25},{... | collective-permute-start | bytes 294920 | tf_op jit(solution)/shard_map/ppermute | solution.py:224
  7.8 0.1 collective-permute-start.3
  7.9 0.3 pick.3
  8.2 0.0 copy-start.3
  8.2 0.0 copy-start.5
  8.2 2.0 %collective-permute-start.12 = (bf16[48,1024]{1,0:T(8,128)(2,1)S(1)}, bf16[48,1024]{1,0:T(8,128)(2,1)S(1)}, u32[]{:S(2)}, u32[]{:S(2)}) collective-permute-start(bf16[48,1024]{1,0:T(8,128)(2,1)S(1)} %get-tuple-element.44), channel_id=1, source_target_pairs={{0,8},{4,12},{8,0},{12,4},{16,24},{20,28},{24,16},{28,20},{1,9},{5... | collective-permute-start | bytes 294920 | tf_op jit(solution)/shard_map/ppermute | solution.py:224
  10.2 1.5 %collective-permute-start.13 = (bf16[48,1024]{1,0:T(8,128)(2,1)S(1)}, bf16[48,1024]{1,0:T(8,128)(2,1)S(1)}, u32[]{:S(2)}, u32[]{:S(2)}) collective-permute-start(bf16[48,1024]{1,0:T(8,128)(2,1)S(1)} %get-tuple-element.43.refs_0_), channel_id=1, source_target_pairs={{0,16},{4,20},{8,24},{12,28},{16,0},{20,4},{24,8},{28,12},{1,17},{... | collective-permute-start | bytes 294920 | tf_op jit(solution)/shard_map/ppermute | solution.py:224
  11.7 0.0 collective-permute-done.2.refs_1_
  11.7 3.1 %collective-permute-done.3.refs_2_ = bf16[48,1024]{1,0:T(8,128)(2,1)S(1)} collective-permute-done((bf16[48,1024]{1,0:T(8,128)(2,1)S(1)}, bf16[48,1024]{1,0:T(8,128)(2,1)S(1)}, u32[]{:S(2)}, u32[]{:S(2)}) %collective-permute-start.3) | collective-permute-done | bytes 98336 | tf_op jit(solution)/shard_map/ppermute | solution.py:224
  14.8 0.0 collective-permute-done.4.refs_3_
  14.8 2.6 %forward.1 = (f32[96,768]{1,0:T(8,128)S(1)}, f32[96,768]{1,0:T(8,128)S(1)}, bf16[48,1024]{1,0:T(8,128)(2,1)S(1)}, bf16[48,1024]{1,0:T(8,128)(2,1)S(1)}, bf16[48,...) custom-call(bf16[48,1024]{1,0:T(8,128)(2,1)S(1)} %get-tuple-element.37.refs_0_, ...), custom_call_target="tpu_custom_call" | custom-call | flops 905969664 | bytes 10813440 | tf_op jit(solution)/shard_map/forward/pallas_call | solution.py:23
  17.4 0.4 collective-permute-start.6
  17.7 2.6 %collective-permute-start.7 = (bf16[48,1024]{1,0:T(8,128)(2,1)S(1)}, bf16[48,1024]{1,0:T(8,128)(2,1)S(1)}, u32[]{:S(2)}, u32[]{:S(2)}) collective-permute-start(bf16[48,1024]{1,0:T(8,128)(2,1)S(1)} %get-tuple-element.42), channel_id=1, source_target_pairs={{0,24},{4,28},{8,16},{12,20},{16,8},{20,12},{24,0},{28,4},{1,25},{... | collective-permute-start | bytes 294920 | tf_op jit(solution)/shard_map/ppermute | solution.py:224
  20.4 0.5 collective-permute-start.5
  20.9 0.0 collective-permute-done.12.refs_1_
  20.9 1.4 %collective-permute-start.14 = (bf16[48,1024]{1,0:T(8,128)(2,1)S(1)}, bf16[48,1024]{1,0:T(8,128)(2,1)S(1)}, u32[]{:S(2)}, u32[]{:S(2)}) collective-permute-start(bf16[48,1024]{1,0:T(8,128)(2,1)S(1)} %get-tuple-element.44), channel_id=1, source_target_pairs={{0,24},{4,28},{8,16},{12,20},{16,8},{20,12},{24,0},{28,4},{1,25},{... | collective-permute-start | bytes 294920 | tf_op jit(solution)/shard_map/ppermute | solution.py:224
  22.4 0.0 collective-permute-done.13.refs_2_
  22.4 0.0 collective-permute-start.8
  22.4 1.8 %collective-permute-done.6.refs_2_ = bf16[48,1024]{1,0:T(8,128)(2,1)S(1)} collective-permute-done((bf16[48,1024]{1,0:T(8,128)(2,1)S(1)}, bf16[48,1024]{1,0:T(8,128)(2,1)S(1)}, u32[]{:S(2)}, u32[]{:S(2)}) %collective-permute-start.6) | collective-permute-done | bytes 98336 | tf_op jit(solution)/shard_map/ppermute | solution.py:224
  24.2 0.5 collective-permute-start.11
  24.7 0.3 collective-permute-done.5.refs_1_
  25.0 0.3 weights.1.weight_ref
  25.3 1.1 %collective-permute-done.14.refs_3_ = bf16[48,1024]{1,0:T(8,128)(2,1)S(1)} collective-permute-done((bf16[48,1024]{1,0:T(8,128)(2,1)S(1)}, bf16[48,1024]{1,0:T(8,128)(2,1)S(1)}, u32[]{:S(2)}, u32[]{:S(2)}) %collective-permute-start.14) | collective-permute-done | bytes 98336 | tf_op jit(solution)/shard_map/ppermute | solution.py:224
  26.4 2.4 %backward.1 = (bf16[48,1024]{1,0:T(8,128)(2,1)S(1)}, bf16[48,1024]{1,0:T(8,128)(2,1)S(1)}, bf16[48,1024]{1,0:T(8,128)(2,1)S(1)}, bf16[48,1024]{1,0:T(8,128)(2,1)S(1)}) custom-call(bf16[48,1024]{1,0:T(8,128)(2,1)S(1)} %get-tuple-element.43.refs_0_, bf16[48,1024]{1,0:T(8,128)(2,1)S(1)} %collective-permute-done.12.refs_1_, ...), custom_call_target="tpu_custom_call" | custom-call | flops 905969664 | bytes 10813440 | tf_op jit(solution)/shard_map/backward/pallas_call | solution.py:23
  28.9 0.1 add_blocks.2
  29.0 19.9 %all_gather.6.all_ref = bf16[768,512]{1,0:T(8,128)(2,1)S(1)} all-gather(bf16[192,512]{1,0:T(8,128)(2,1)S(1)} %add_blocks.2), channel_id=1, replica_groups=mesh['dp'=2,'tensor'=4,'expert'=4] {'expert'}, dimensions={0}, use_global_device_ids=true | all-gather | bytes 983040 | tf_op jit(solution)/shard_map/all_gather | solution.py:256
  48.9 1.5 %collective-permute-start.15 = (bf16[48,1024]{1,0:T(8,128)(2,1)S(1)}, bf16[48,1024]{1,0:T(8,128)(2,1)S(1)}, u32[]{:S(2)}, u32[]{:S(2)}) collective-permute-start(bf16[48,1024]{1,0:T(8,128)(2,1)S(1)} %get-tuple-element.61), channel_id=1, source_target_pairs={{0,8},{4,12},{8,0},{12,4},{16,24},{20,28},{24,16},{28,20},{1,9},{5... | collective-permute-start | bytes 294920 | tf_op jit(solution)/shard_map/ppermute | solution.py:224
  50.4 0.8 collective-permute-start.16
  51.2 1.2 %collective-permute-start.17 = (bf16[48,1024]{1,0:T(8,128)(2,1)S(1)}, bf16[48,1024]{1,0:T(8,128)(2,1)S(1)}, u32[]{:S(2)}, u32[]{:S(2)}) collective-permute-start(bf16[48,1024]{1,0:T(8,128)(2,1)S(1)} %get-tuple-element.63), channel_id=1, source_target_pairs={{0,24},{4,28},{8,16},{12,20},{16,8},{20,12},{24,0},{28,4},{1,25},{... | collective-permute-start | bytes 294920 | tf_op jit(solution)/shard_map/ppermute | solution.py:224
  52.4 1.7 %combine_gate.1 = (bf16[512,512]{1,0:T(8,128)(2,1)}, f32[8,512]{1,0:T(8,128)S(1)}) custom-call(bf16[512,768]{1,0:T(8,128)(2,1)S(1)} %weights.1.weight_ref, s32[8,512]{1,0:T(8,128)S(1)} %bitcast.7, f32[16,512]{1,0:T(8,128)S(1)} %number.1.key_ref, bf16[512,512]{1,0:T(8,128)(2,1)S(1)} %copy-done.7, bf16[768,512]{1,0:T(8,128)(2,1)S(1)} %all_gather.6.all_ref), custom_call_target="tpu_custom_call" | custom-call | flops 805306368 | bytes 2686976 | tf_op jit(solution)/shard_map/combine_gate/pallas_call | solution.py:23
  54.1 1.2 %collective-permute-done.22 = f32[8,512]{1,0:T(8,128)S(1)} collective-permute-done((f32[8,512]{1,0:T(8,128)S(1)}, f32[8,512]{1,0:T(8,128)S(1)}, u32[]{:S(2)}, u32[]{:S(2)}) %collective-permute-start.22) | collective-permute-done | bytes 16416 | tf_op jit(solution)/shard_map/ppermute | solution.py:214
  55.3 1.5 %collective-permute-start.23 = (f32[8,512]{1,0:T(8,128)S(1)}, f32[8,512]{1,0:T(8,128)S(1)}, u32[]{:S(2)}, u32[]{:S(2)}) collective-permute-start(f32[8,512]{1,0:T(8,128)S(1)} %add.6), channel_id=1, source_target_pairs={{0,8},{4,12},{8,0},{12,4},{16,24},{20,28},{24,16},{28,20},{1,9},{5... | collective-permute-start | bytes 49160 | tf_op jit(solution)/shard_map/ppermute | solution.py:224
  56.8 0.5 collective-permute-start.19
  57.3 0.1 collective-permute-start.20
  57.4 0.4 collective-permute-start.21
  57.8 1.2 %collective-permute-done.23 = f32[8,512]{1,0:T(8,128)S(1)} collective-permute-done((f32[8,512]{1,0:T(8,128)S(1)}, f32[8,512]{1,0:T(8,128)S(1)}, u32[]{:S(2)}, u32[]{:S(2)}) %collective-permute-start.23) | collective-permute-done | bytes 16416 | tf_op jit(solution)/shard_map/ppermute | solution.py:224
  59.0 0.6 add_bitcast_fusion
  59.7 0.1 add_blocks.3
  59.8 18.1 %all_gather.7.all_ref = bf16[768,512]{1,0:T(8,128)(2,1)S(1)} all-gather(bf16[192,512]{1,0:T(8,128)(2,1)S(1)} %add_blocks.3), channel_id=1, replica_groups=mesh['dp'=2,'tensor'=4,'expert'=4] {'expert'}, dimensions={0}, use_global_device_ids=true | all-gather | bytes 983040 | tf_op jit(solution)/shard_map/all_gather | solution.py:256
  77.8 1.4 %combine.1 = bf16[512,512]{1,0:T(8,128)(2,1)} custom-call(bf16[512,768]{1,0:T(8,128)(2,1)S(1)} %weights.1.weight_ref, bf16[768,512]{1,0:T(8,128)(2,1)S(1)} %all_gather.7.all_ref), custom_call_target="tpu_custom_call" | custom-call | flops 402653184 | bytes 2097152 | tf_op jit(solution)/shard_map/combine/pallas_call | solution.py:23
  (30 shorter events, 0.1 us)
Async XLA Ops:
  0.6 2.3 %collective-permute-start = (bf16[512,512]{1,0:T(8,128)(2,1)}, bf16[512,512]{1,0:T(8,128)(2,1)S(1)}, u32[]{:S(2)}, u32[]{:S(2)}) collective-permute-start(bf16[512,512]{1,0:T(8,128)(2,1)} %refs_0_.2), channel_id=1, source_target_pairs={{0,4},{4,0},{8,12},{12,8},{1,5},{5,1},{9,13},{13,9},{2,6},{6,2},{1... | collective-permute-start | bytes 1572872 | tf_op jit(solution)/shard_map/ppermute | solution.py:214
  1.1 6.7 %collective-permute-start.1 = (bf16[512,512]{1,0:T(8,128)(2,1)}, bf16[512,512]{1,0:T(8,128)(2,1)S(1)}, u32[]{:S(2)}, u32[]{:S(2)}) collective-permute-start(bf16[512,512]{1,0:T(8,128)(2,1)} %grads_ref.1), channel_id=1, source_target_pairs={{0,4},{4,0},{8,12},{12,8},{1,5},{5,1},{9,13},{13,9},{2,6},{6,2},{1... | collective-permute-start | bytes 1572872 | tf_op jit(solution)/shard_map/ppermute | solution.py:214
  1.2 0.7 copy-start.4
  1.9 1.0 %copy-start.6 = (bf16[512,512]{1,0:T(8,128)(2,1)S(1)}, bf16[512,512]{1,0:T(8,128)(2,1)}, u32[]{:S(2)}) copy-start(bf16[512,512]{1,0:T(8,128)(2,1)} %refs_0_.2) | copy-start | bytes 1572868
  2.1 5.8 %copy-start.7 = (bf16[512,512]{1,0:T(8,128)(2,1)S(1)}, bf16[512,512]{1,0:T(8,128)(2,1)}, u32[]{:S(2)}) copy-start(bf16[512,512]{1,0:T(8,128)(2,1)} %grads_ref.1) | copy-start | bytes 1572868
  3.3 8.4 %collective-permute-start.2 = (bf16[48,1024]{1,0:T(8,128)(2,1)S(1)}, bf16[48,1024]{1,0:T(8,128)(2,1)S(1)}, u32[]{:S(2)}, u32[]{:S(2)}) collective-permute-start(bf16[48,1024]{1,0:T(8,128)(2,1)S(1)} %get-tuple-element.38), channel_id=1, source_target_pairs={{0,8},{4,12},{8,0},{12,4},{16,24},{20,28},{24,16},{28,20},{1,9},{5... | collective-permute-start | bytes 294920 | tf_op jit(solution)/shard_map/ppermute | solution.py:224
  6.3 8.5 %collective-permute-start.4 = (bf16[48,1024]{1,0:T(8,128)(2,1)S(1)}, bf16[48,1024]{1,0:T(8,128)(2,1)S(1)}, u32[]{:S(2)}, u32[]{:S(2)}) collective-permute-start(bf16[48,1024]{1,0:T(8,128)(2,1)S(1)} %get-tuple-element.38), channel_id=1, source_target_pairs={{0,24},{4,28},{8,16},{12,20},{16,8},{20,12},{24,0},{28,4},{1,25},{... | collective-permute-start | bytes 294920 | tf_op jit(solution)/shard_map/ppermute | solution.py:224
  7.8 7.0 %copy-start = (bf16[1,768,2048]{2,1,0:T(8,128)(2,1)S(1)}, bf16[1,768,2048]{2,1,0:T(8,128)(2,1)}, u32[]{:S(2)}) copy-start(bf16[1,768,2048]{2,1,0:T(8,128)(2,1)} %refs_4_.3) | copy-start | bytes 9437188
  7.8 7.0 %copy-start.1 = (bf16[1,768,2048]{2,1,0:T(8,128)(2,1)S(1)}, bf16[1,768,2048]{2,1,0:T(8,128)(2,1)}, u32[]{:S(2)}) copy-start(bf16[1,768,2048]{2,1,0:T(8,128)(2,1)} %refs_5_.3) | copy-start | bytes 9437188
  7.8 7.0 %copy-start.2 = (bf16[1,768,2048]{2,1,0:T(8,128)(2,1)S(1)}, bf16[1,768,2048]{2,1,0:T(8,128)(2,1)}, u32[]{:S(2)}) copy-start(bf16[1,768,2048]{2,1,0:T(8,128)(2,1)} %refs_6_.3) | copy-start | bytes 9437188
  7.8 7.0 %collective-permute-start.3 = (bf16[48,1024]{1,0:T(8,128)(2,1)S(1)}, bf16[48,1024]{1,0:T(8,128)(2,1)S(1)}, u32[]{:S(2)}, u32[]{:S(2)}) collective-permute-start(bf16[48,1024]{1,0:T(8,128)(2,1)S(1)} %get-tuple-element.37.refs_0_), channel_id=1, source_target_pairs={{0,16},{4,20},{8,24},{12,28},{16,0},{20,4},{24,8},{28,12},{1,17},{... | collective-permute-start | bytes 294920 | tf_op jit(solution)/shard_map/ppermute | solution.py:224
  8.2 16.8 %copy-start.3 = (f32[512,8]{0,1:T(8,128)S(1)}, f32[512,8]{0,1:T(8,128)}, u32[]{:S(2)}) copy-start(f32[512,8]{0,1:T(8,128)} %param.10) | copy-start | bytes 49156
  8.2 16.8 %copy-start.5 = (s32[512,8]{0,1:T(8,128)S(1)}, s32[512,8]{0,1:T(8,128)}, u32[]{:S(2)}) copy-start(s32[512,8]{0,1:T(8,128)} %param.9) | copy-start | bytes 49156
  8.2 12.7 %collective-permute-start.12 = (bf16[48,1024]{1,0:T(8,128)(2,1)S(1)}, bf16[48,1024]{1,0:T(8,128)(2,1)S(1)}, u32[]{:S(2)}, u32[]{:S(2)}) collective-permute-start(bf16[48,1024]{1,0:T(8,128)(2,1)S(1)} %get-tuple-element.44), channel_id=1, source_target_pairs={{0,8},{4,12},{8,0},{12,4},{16,24},{20,28},{24,16},{28,20},{1,9},{5... | collective-permute-start | bytes 294920 | tf_op jit(solution)/shard_map/ppermute | solution.py:224
  10.2 12.2 %collective-permute-start.13 = (bf16[48,1024]{1,0:T(8,128)(2,1)S(1)}, bf16[48,1024]{1,0:T(8,128)(2,1)S(1)}, u32[]{:S(2)}, u32[]{:S(2)}) collective-permute-start(bf16[48,1024]{1,0:T(8,128)(2,1)S(1)} %get-tuple-element.43.refs_0_), channel_id=1, source_target_pairs={{0,16},{4,20},{8,24},{12,28},{16,0},{20,4},{24,8},{28,12},{1,17},{... | collective-permute-start | bytes 294920 | tf_op jit(solution)/shard_map/ppermute | solution.py:224
  17.4 6.8 %collective-permute-start.6 = (bf16[48,1024]{1,0:T(8,128)(2,1)S(1)}, bf16[48,1024]{1,0:T(8,128)(2,1)S(1)}, u32[]{:S(2)}, u32[]{:S(2)}) collective-permute-start(bf16[48,1024]{1,0:T(8,128)(2,1)S(1)} %get-tuple-element.41), channel_id=1, source_target_pairs={{0,16},{4,20},{8,24},{12,28},{16,0},{20,4},{24,8},{28,12},{1,17},{... | collective-permute-start | bytes 294920 | tf_op jit(solution)/shard_map/ppermute | solution.py:224
  17.7 6.4 %collective-permute-start.7 = (bf16[48,1024]{1,0:T(8,128)(2,1)S(1)}, bf16[48,1024]{1,0:T(8,128)(2,1)S(1)}, u32[]{:S(2)}, u32[]{:S(2)}) collective-permute-start(bf16[48,1024]{1,0:T(8,128)(2,1)S(1)} %get-tuple-element.42), channel_id=1, source_target_pairs={{0,24},{4,28},{8,16},{12,20},{16,8},{20,12},{24,0},{28,4},{1,25},{... | collective-permute-start | bytes 294920 | tf_op jit(solution)/shard_map/ppermute | solution.py:224
  20.4 4.6 %collective-permute-start.5 = (bf16[48,1024]{1,0:T(8,128)(2,1)S(1)}, bf16[48,1024]{1,0:T(8,128)(2,1)S(1)}, u32[]{:S(2)}, u32[]{:S(2)}) collective-permute-start(bf16[48,1024]{1,0:T(8,128)(2,1)S(1)} %get-tuple-element.40), channel_id=1, source_target_pairs={{0,8},{4,12},{8,0},{12,4},{16,24},{20,28},{24,16},{28,20},{1,9},{5... | collective-permute-start | bytes 294920 | tf_op jit(solution)/shard_map/ppermute | solution.py:224
  20.9 5.5 %collective-permute-start.14 = (bf16[48,1024]{1,0:T(8,128)(2,1)S(1)}, bf16[48,1024]{1,0:T(8,128)(2,1)S(1)}, u32[]{:S(2)}, u32[]{:S(2)}) collective-permute-start(bf16[48,1024]{1,0:T(8,128)(2,1)S(1)} %get-tuple-element.44), channel_id=1, source_target_pairs={{0,24},{4,28},{8,16},{12,20},{16,8},{20,12},{24,0},{28,4},{1,25},{... | collective-permute-start | bytes 294920 | tf_op jit(solution)/shard_map/ppermute | solution.py:224
  22.4 6.5 %collective-permute-start.8 = (bf16[48,1024]{1,0:T(8,128)(2,1)S(1)}, bf16[48,1024]{1,0:T(8,128)(2,1)S(1)}, u32[]{:S(2)}, u32[]{:S(2)}) collective-permute-start(bf16[48,1024]{1,0:T(8,128)(2,1)S(1)} %get-tuple-element.51.refs_0_), channel_id=1, source_target_pairs={{0,4},{4,0},{8,12},{12,8},{1,5},{5,1},{9,13},{13,9},{2,6},{6,2},{1... | collective-permute-start | bytes 294920 | tf_op jit(solution)/shard_map/ppermute | solution.py:214
  24.2 4.7 %collective-permute-start.10 = (bf16[48,1024]{1,0:T(8,128)(2,1)S(1)}, bf16[48,1024]{1,0:T(8,128)(2,1)S(1)}, u32[]{:S(2)}, u32[]{:S(2)}) collective-permute-start(bf16[48,1024]{1,0:T(8,128)(2,1)S(1)} %collective-permute-done.6.refs_2_), channel_id=1, source_target_pairs={{0,4},{4,0},{8,12},{12,8},{1,5},{5,1},{9,13},{13,9},{2,6},{6,2},{1... | collective-permute-start | bytes 294920 | tf_op jit(solution)/shard_map/ppermute | solution.py:214
  24.2 4.8 %collective-permute-start.11 = (bf16[48,1024]{1,0:T(8,128)(2,1)S(1)}, bf16[48,1024]{1,0:T(8,128)(2,1)S(1)}, u32[]{:S(2)}, u32[]{:S(2)}) collective-permute-start(bf16[48,1024]{1,0:T(8,128)(2,1)S(1)} %collective-permute-done.7.refs_3_), channel_id=1, source_target_pairs={{0,4},{4,0},{8,12},{12,8},{1,5},{5,1},{9,13},{13,9},{2,6},{6,2},{1... | collective-permute-start | bytes 294920 | tf_op jit(solution)/shard_map/ppermute | solution.py:214
  25.0 3.9 %collective-permute-start.9 = (bf16[48,1024]{1,0:T(8,128)(2,1)S(1)}, bf16[48,1024]{1,0:T(8,128)(2,1)S(1)}, u32[]{:S(2)}, u32[]{:S(2)}) collective-permute-start(bf16[48,1024]{1,0:T(8,128)(2,1)S(1)} %collective-permute-done.5.refs_1_), channel_id=1, source_target_pairs={{0,4},{4,0},{8,12},{12,8},{1,5},{5,1},{9,13},{13,9},{2,6},{6,2},{1... | collective-permute-start | bytes 294920 | tf_op jit(solution)/shard_map/ppermute | solution.py:214
  48.9 7.9 %collective-permute-start.15 = (bf16[48,1024]{1,0:T(8,128)(2,1)S(1)}, bf16[48,1024]{1,0:T(8,128)(2,1)S(1)}, u32[]{:S(2)}, u32[]{:S(2)}) collective-permute-start(bf16[48,1024]{1,0:T(8,128)(2,1)S(1)} %get-tuple-element.61), channel_id=1, source_target_pairs={{0,8},{4,12},{8,0},{12,4},{16,24},{20,28},{24,16},{28,20},{1,9},{5... | collective-permute-start | bytes 294920 | tf_op jit(solution)/shard_map/ppermute | solution.py:224
  50.4 6.9 %collective-permute-start.16 = (bf16[48,1024]{1,0:T(8,128)(2,1)S(1)}, bf16[48,1024]{1,0:T(8,128)(2,1)S(1)}, u32[]{:S(2)}, u32[]{:S(2)}) collective-permute-start(bf16[48,1024]{1,0:T(8,128)(2,1)S(1)} %get-tuple-element.62), channel_id=1, source_target_pairs={{0,16},{4,20},{8,24},{12,28},{16,0},{20,4},{24,8},{28,12},{1,17},{... | collective-permute-start | bytes 294920 | tf_op jit(solution)/shard_map/ppermute | solution.py:224
  51.2 6.2 %collective-permute-start.17 = (bf16[48,1024]{1,0:T(8,128)(2,1)S(1)}, bf16[48,1024]{1,0:T(8,128)(2,1)S(1)}, u32[]{:S(2)}, u32[]{:S(2)}) collective-permute-start(bf16[48,1024]{1,0:T(8,128)(2,1)S(1)} %get-tuple-element.63), channel_id=1, source_target_pairs={{0,24},{4,28},{8,16},{12,20},{16,8},{20,12},{24,0},{28,4},{1,25},{... | collective-permute-start | bytes 294920 | tf_op jit(solution)/shard_map/ppermute | solution.py:224
  54.1 1.2 %collective-permute-start.22 = (f32[8,512]{1,0:T(8,128)S(1)}, f32[8,512]{1,0:T(8,128)S(1)}, u32[]{:S(2)}, u32[]{:S(2)}) collective-permute-start(f32[8,512]{1,0:T(8,128)S(1)} %get-tuple-element.64), channel_id=1, source_target_pairs={{0,4},{4,0},{8,12},{12,8},{1,5},{5,1},{9,13},{13,9},{2,6},{6,2},{1... | collective-permute-start | bytes 49160 | tf_op jit(solution)/shard_map/ppermute | solution.py:214
  55.3 3.7 %collective-permute-start.23 = (f32[8,512]{1,0:T(8,128)S(1)}, f32[8,512]{1,0:T(8,128)S(1)}, u32[]{:S(2)}, u32[]{:S(2)}) collective-permute-start(f32[8,512]{1,0:T(8,128)S(1)} %add.6), channel_id=1, source_target_pairs={{0,8},{4,12},{8,0},{12,4},{16,24},{20,28},{24,16},{28,20},{1,9},{5... | collective-permute-start | bytes 49160 | tf_op jit(solution)/shard_map/ppermute | solution.py:224
  56.8 2.8 %collective-permute-start.18 = (bf16[48,1024]{1,0:T(8,128)(2,1)S(1)}, bf16[48,1024]{1,0:T(8,128)(2,1)S(1)}, u32[]{:S(2)}, u32[]{:S(2)}) collective-permute-start(bf16[48,1024]{1,0:T(8,128)(2,1)S(1)} %get-tuple-element.60.refs_0_), channel_id=1, source_target_pairs={{0,4},{4,0},{8,12},{12,8},{1,5},{5,1},{9,13},{13,9},{2,6},{6,2},{1... | collective-permute-start | bytes 294920 | tf_op jit(solution)/shard_map/ppermute | solution.py:214
  56.8 2.8 %collective-permute-start.19 = (bf16[48,1024]{1,0:T(8,128)(2,1)S(1)}, bf16[48,1024]{1,0:T(8,128)(2,1)S(1)}, u32[]{:S(2)}, u32[]{:S(2)}) collective-permute-start(bf16[48,1024]{1,0:T(8,128)(2,1)S(1)} %collective-permute-done.15.refs_1_), channel_id=1, source_target_pairs={{0,4},{4,0},{8,12},{12,8},{1,5},{5,1},{9,13},{13,9},{2,6},{6,2},{1... | collective-permute-start | bytes 294920 | tf_op jit(solution)/shard_map/ppermute | solution.py:214
  57.3 2.3 %collective-permute-start.20 = (bf16[48,1024]{1,0:T(8,128)(2,1)S(1)}, bf16[48,1024]{1,0:T(8,128)(2,1)S(1)}, u32[]{:S(2)}, u32[]{:S(2)}) collective-permute-start(bf16[48,1024]{1,0:T(8,128)(2,1)S(1)} %collective-permute-done.16.refs_2_), channel_id=1, source_target_pairs={{0,4},{4,0},{8,12},{12,8},{1,5},{5,1},{9,13},{13,9},{2,6},{6,2},{1... | collective-permute-start | bytes 294920 | tf_op jit(solution)/shard_map/ppermute | solution.py:214
  57.4 2.3 %collective-permute-start.21 = (bf16[48,1024]{1,0:T(8,128)(2,1)S(1)}, bf16[48,1024]{1,0:T(8,128)(2,1)S(1)}, u32[]{:S(2)}, u32[]{:S(2)}) collective-permute-start(bf16[48,1024]{1,0:T(8,128)(2,1)S(1)} %collective-permute-done.17.refs_3_), channel_id=1, source_target_pairs={{0,4},{4,0},{8,12},{12,8},{1,5},{5,1},{9,13},{13,9},{2,6},{6,2},{1... | collective-permute-start | bytes 294920 | tf_op jit(solution)/shard_map/ppermute | solution.py:214

commit v6 on v4

--- a/solution.py
+++ b/solution.py
@@ -30,6 +30,10 @@
         cost_estimate=pl.CostEstimate(flops=int(flops), bytes_accessed=int(moved), transcendentals=0),
         name=name,
     )(*operands)
+
+
+def after(values, earlier):
+    return lax.optimization_barrier((values, earlier))
 
 
 def number_kernel(routes_ref, key_ref):
@@ -245,25 +249,29 @@
     hops = [(db, dh) for db in range(n_dp) for dh in range(chips)]
     order = sorted(range(count), key=lambda index: (hops[index][0] == 0, -hops[index][1]))
 
-    def dispatch(key, sources):
-        pieces = call(
+    def pick(key, sources):
+        return call(
             functools.partial(pick_kernel, cores),
             "pick",
             [shape(CAP, cores * width)] * chips,
             [key, *sources],
             EARLY,
         )
+
+    def dispatch(pieces):
         arrived = {index: to_chip(pieces[hops[index][1]], *hops[index]) for index in order}
         return [arrived[index] for index in range(count)]
 
     def give_back(pieces):
         arrived = {index: to_chip(pieces[index], *hops[index]) for index in order}
-        pairs = [[to_core(arrived[index], dc) for index in range(count)] for dc in range(cores)]
+        return [to_core(arrived[index], dc) for dc in range(cores) for index in range(count)]
+
+    def add_blocks(pieces):
         return call(
             functools.partial(add_blocks_kernel, chips, cores),
             "add_blocks",
             shape(slots, width),
-            sum(pairs, []),
+            pieces,
             2 * slots * width,
         )
 
@@ -282,8 +290,9 @@
     token_sources = [to_core(tokens, dc) for dc in range(cores)]
     grad_sources = [to_core(grad_out, dc) for dc in range(cores)]
     key = call(number_kernel, "number", shape(experts, rows, F32), [routes_t], EARLY)
-    tok_in = dispatch(key, token_sources)
-    grad_in = dispatch(key, grad_sources)
+    tok_in = dispatch(pick(key, token_sources))
+    tok_in[0], grad_pieces = lax.optimization_barrier((tok_in[0], pick(key, grad_sources)))
+    grad_in = dispatch(grad_pieces)
 
     matmul_flops = 2 * tall * hid_dev * feats
     saved = [shape(tall, hid_dev, F32)] * 2
@@ -297,7 +306,8 @@
         [pltpu.VMEM((tall, feats), BF16), pltpu.VMEM((tall, hid_dev), BF16)],
         limit=24,
     )
-    out_rows = give_back(outs)
+    outs, grad_in = after(outs, grad_in)
+    out_pieces = give_back(outs)
     backs = call(
         functools.partial(backward_kernel, chips, cores, count),
         "backward",
@@ -307,9 +317,12 @@
         [pltpu.VMEM((tall, feats), BF16)] + [pltpu.VMEM((tall, hid_dev), BF16)] * 2,
         limit=24,
     )
-    out_parts = across(out_rows)
-    out_parts[1], backs = lax.optimization_barrier((out_parts[1], backs))
-    back_rows = give_back(backs)
+    out_pieces, backs = after(out_pieces, backs)
+    out_parts = across(add_blocks(out_pieces))
+    back_pieces = give_back(backs)
+    back_pieces, out_parts[1:4] = after(back_pieces, out_parts[1:4])
+    back_parts = across(add_blocks(back_pieces))
+    out_parts, back_parts[1:2] = after(out_parts, back_parts[1:2])
 
     weight_map = call(
         functools.partial(weights_kernel, chips, cores, columns),
@@ -321,18 +334,18 @@
         limit=16,
     )
 
-    back_parts = across(back_rows)
+    all_rows = pltpu.VMEM((experts * CAP, width), BF16)
     combine_flops = 2 * experts * CAP * rows * width
-    all_rows = pltpu.VMEM((experts * CAP, width), BF16)
     mixed, gate_part = call(
         functools.partial(combine_gate_kernel, chips, cores, columns),
         "combine_gate",
         [shape(rows, width), shape(routes_t.shape[0], rows, F32)],
         [weight_map, routes_t, key, grad_out, *out_parts],
-        2 * combine_flops,
+        0,
         [all_rows, pltpu.VMEM((experts * CAP, rows), F32)],
         limit=24,
     )
+    gate_part, back_parts[2:4] = after(gate_part, back_parts[2:4])
     for dc in range(1, cores):
         gate_part = gate_part + to_core(gate_part, dc)
     total = gate_part

time: 79.6 us -> 77.6 us (0.975)
  waiting for transfers between devices: 31.6 us -> 29.1 us
    ppermute x2, waiting for transfers between devices: 0.01 us -> 6.39 us  [across(): lax.ppermute(value, 'expert', [(z, (z + 2) % columns) for z in range(colu...]
    ppermute x13, waiting for transfers between devices: 14.8 us -> 11.1 us  [to_chip(): return lax.ppermute(value, ('dp', 'tensor'), pairs)]
    ppermute x11, waiting for transfers between devices: 4.27 us -> 1.98 us  [to_core(): return lax.ppermute(value, 'tensor', pairs)]
    ppermute x2, waiting for transfers between devices: 5.4 us -> 3.43 us  [across(): lax.ppermute(value, 'expert', [(z + 1, z) for z in range(columns - 1)])]
    ppermute x13, starting transfers between devices: 17 us -> 18.8 us  [to_chip(): return lax.ppermute(value, ('dp', 'tensor'), pairs)]
    ppermute x2, starting transfers between devices: 8.14 us -> 6.69 us  [across(): lax.ppermute(value, 'expert', [(z, (z + 2) % columns) for z in range(colu...]
    ppermute x2, waiting for transfers between devices: 1.07 us -> 0.01 us  [across(): up = lax.ppermute(value, 'expert', [(z, z + 1) for z in range(columns - 1)])]
  transfers between devices with their start and end apart: 32 -> 32, of which waited for: 19 -> 13; matrix products, arithmetic and copies ran while one was open for 1% -> 1% of each run, Pallas kernels for 10% -> 10%
where the time goes in v6:
time: 77.6 us; the launch traced here: 77.3 us
  starting transfers between devices  36.6 us (47%)
  waiting for transfers between devices  29.1 us (38%)
  Pallas kernels  9.28 us (12%)
  between operations  0.85 us (1%)
  local copies, waits for them, and re-layouts  0.83 us (1%)
    ppermute x13, starting transfers between devices, to_chip(): return lax.ppermute(value, ('dp', 'tensor'), pairs)  18.8 us
    ppermute x13, waiting for transfers between devices, to_chip(): return lax.ppermute(value, ('dp', 'tensor'), pairs)  11.1 us
    pallas_call x10, Pallas kernels, call(): pl.pallas_call(kernel, out_shape=out_shape, in_specs=[spec] * len(operand...  9.28 us
    ppermute x2, starting transfers between devices, across(): lax.ppermute(value, 'expert', [(z, (z + 2) % columns) for z in range(colu...  6.69 us
    ppermute x2, waiting for transfers between devices, across(): lax.ppermute(value, 'expert', [(z, (z + 2) % columns) for z in range(colu...  6.39 us
    ppermute x2, waiting for transfers between devices, across(): ends = lax.ppermute(far, 'expert', [(2, 3), (1, 0)])  6.16 us
    ppermute x2, starting transfers between devices, across(): up = lax.ppermute(value, 'expert', [(z, z + 1) for z in range(columns - 1)])  4.77 us
    ppermute x2, waiting for transfers between devices, across(): lax.ppermute(value, 'expert', [(z + 1, z) for z in range(columns - 1)])  3.43 us
  transfers between devices with their start and end apart: 32, of which 13 were waited for; matrix products, arithmetic and copies ran while one was open for 1% of the time, Pallas kernels for 10%

profile of v6, /device:TPU:0, one launch (start us, length us, event | category | flops | bytes accessed | tf_op | source)
XLA Modules:
  0.0 77.3 jit_solution(4963249157796045363)
XLA Ops:
  0.6 0.5 collective-permute-start
  1.1 0.1 collective-permute-start.1
  1.2 0.7 copy-done.4
  1.9 0.1 number.1.key_ref
  2.1 0.8 %collective-permute-done.refs_1_ = bf16[512,512]{1,0:T(8,128)(2,1)S(1)} collective-permute-done((bf16[512,512]{1,0:T(8,128)(2,1)}, bf16[512,512]{1,0:T(8,128)(2,1)S(1)}, u32[]{:S(2)}, u32[]{:S(2)}) %collective-permute-start) | collective-permute-done | bytes 524320 | tf_op jit(solution)/shard_map/ppermute | solution.py:237
  2.9 0.1 copy-done.7
  3.0 0.3 pick.2
  3.3 3.0 %collective-permute-start.2 = (bf16[48,1024]{1,0:T(8,128)(2,1)S(1)}, bf16[48,1024]{1,0:T(8,128)(2,1)S(1)}, u32[]{:S(2)}, u32[]{:S(2)}) collective-permute-start(bf16[48,1024]{1,0:T(8,128)(2,1)S(1)} %get-tuple-element.66), channel_id=1, source_target_pairs={{0,8},{4,12},{8,0},{12,4},{16,24},{20,28},{24,16},{28,20},{1,9},{5... | collective-permute-start | bytes 294920 | tf_op jit(solution)/shard_map/ppermute | solution.py:247
  6.3 1.5 %collective-permute-start.4 = (bf16[48,1024]{1,0:T(8,128)(2,1)S(1)}, bf16[48,1024]{1,0:T(8,128)(2,1)S(1)}, u32[]{:S(2)}, u32[]{:S(2)}) collective-permute-start(bf16[48,1024]{1,0:T(8,128)(2,1)S(1)} %get-tuple-element.66), channel_id=1, source_target_pairs={{0,24},{4,28},{8,16},{12,20},{16,8},{20,12},{24,0},{28,4},{1,25},{... | collective-permute-start | bytes 294920 | tf_op jit(solution)/shard_map/ppermute | solution.py:247
  7.8 0.1 collective-permute-start.3
  7.9 0.3 pick.3
  8.2 2.0 %collective-permute-start.5 = (bf16[48,1024]{1,0:T(8,128)(2,1)S(1)}, bf16[48,1024]{1,0:T(8,128)(2,1)S(1)}, u32[]{:S(2)}, u32[]{:S(2)}) collective-permute-start(bf16[48,1024]{1,0:T(8,128)(2,1)S(1)} %get-tuple-element.72), channel_id=1, source_target_pairs={{0,8},{4,12},{8,0},{12,4},{16,24},{20,28},{24,16},{28,20},{1,9},{5... | collective-permute-start | bytes 294920 | tf_op jit(solution)/shard_map/ppermute | solution.py:247
  10.1 1.5 %collective-permute-start.6 = (bf16[48,1024]{1,0:T(8,128)(2,1)S(1)}, bf16[48,1024]{1,0:T(8,128)(2,1)S(1)}, u32[]{:S(2)}, u32[]{:S(2)}) collective-permute-start(bf16[48,1024]{1,0:T(8,128)(2,1)S(1)} %get-tuple-element.77.refs_0_), channel_id=1, source_target_pairs={{0,16},{4,20},{8,24},{12,28},{16,0},{20,4},{24,8},{28,12},{1,17},{... | collective-permute-start | bytes 294920 | tf_op jit(solution)/shard_map/ppermute | solution.py:247
  11.7 1.2 %collective-permute-start.7 = (bf16[48,1024]{1,0:T(8,128)(2,1)S(1)}, bf16[48,1024]{1,0:T(8,128)(2,1)S(1)}, u32[]{:S(2)}, u32[]{:S(2)}) collective-permute-start(bf16[48,1024]{1,0:T(8,128)(2,1)S(1)} %get-tuple-element.72), channel_id=1, source_target_pairs={{0,24},{4,28},{8,16},{12,20},{16,8},{20,12},{24,0},{28,4},{1,25},{... | collective-permute-start | bytes 294920 | tf_op jit(solution)/shard_map/ppermute | solution.py:247
  12.9 2.9 %collective-permute-done.3.refs_2_ = bf16[48,1024]{1,0:T(8,128)(2,1)S(1)} collective-permute-done((bf16[48,1024]{1,0:T(8,128)(2,1)S(1)}, bf16[48,1024]{1,0:T(8,128)(2,1)S(1)}, u32[]{:S(2)}, u32[]{:S(2)}) %collective-permute-start.3) | collective-permute-done | bytes 98336 | tf_op jit(solution)/shard_map/ppermute | solution.py:247
  15.8 2.6 %forward.1 = (f32[96,768]{1,0:T(8,128)S(1)}, f32[96,768]{1,0:T(8,128)S(1)}, bf16[48,1024]{1,0:T(8,128)(2,1)S(1)}, bf16[48,1024]{1,0:T(8,128)(2,1)S(1)}, bf16[48,...) custom-call(bf16[48,1024]{1,0:T(8,128)(2,1)S(1)} %get-tuple-element.65.refs_0_, ...), custom_call_target="tpu_custom_call" | custom-call | flops 905969664 | bytes 10813440 | tf_op jit(solution)/shard_map/forward/pallas_call | solution.py:23
  18.4 1.6 %collective-permute-start.8 = (bf16[48,1024]{1,0:T(8,128)(2,1)S(1)}, bf16[48,1024]{1,0:T(8,128)(2,1)S(1)}, u32[]{:S(2)}, u32[]{:S(2)}) collective-permute-start(bf16[48,1024]{1,0:T(8,128)(2,1)S(1)} %get-tuple-element.74), channel_id=1, source_target_pairs={{0,8},{4,12},{8,0},{12,4},{16,24},{20,28},{24,16},{28,20},{1,9},{5... | collective-permute-start | bytes 294920 | tf_op jit(solution)/shard_map/ppermute | solution.py:247
  20.1 0.4 collective-permute-start.9
  20.5 1.5 %collective-permute-start.10 = (bf16[48,1024]{1,0:T(8,128)(2,1)S(1)}, bf16[48,1024]{1,0:T(8,128)(2,1)S(1)}, u32[]{:S(2)}, u32[]{:S(2)}) collective-permute-start(bf16[48,1024]{1,0:T(8,128)(2,1)S(1)} %get-tuple-element.76), channel_id=1, source_target_pairs={{0,24},{4,28},{8,16},{12,20},{16,8},{20,12},{24,0},{28,4},{1,25},{... | collective-permute-start | bytes 294920 | tf_op jit(solution)/shard_map/ppermute | solution.py:247
  22.0 1.8 %collective-permute-done.8.refs_1_ = bf16[48,1024]{1,0:T(8,128)(2,1)S(1)} collective-permute-done((bf16[48,1024]{1,0:T(8,128)(2,1)S(1)}, bf16[48,1024]{1,0:T(8,128)(2,1)S(1)}, u32[]{:S(2)}, u32[]{:S(2)}) %collective-permute-start.8) | collective-permute-done | bytes 98336 | tf_op jit(solution)/shard_map/ppermute | solution.py:247
  23.8 1.0 %collective-permute-done.9.refs_2_ = bf16[48,1024]{1,0:T(8,128)(2,1)S(1)} collective-permute-done((bf16[48,1024]{1,0:T(8,128)(2,1)S(1)}, bf16[48,1024]{1,0:T(8,128)(2,1)S(1)}, u32[]{:S(2)}, u32[]{:S(2)}) %collective-permute-start.9) | collective-permute-done | bytes 98336 | tf_op jit(solution)/shard_map/ppermute | solution.py:247
  24.9 1.2 %collective-permute-done.10.refs_3_ = bf16[48,1024]{1,0:T(8,128)(2,1)S(1)} collective-permute-done((bf16[48,1024]{1,0:T(8,128)(2,1)S(1)}, bf16[48,1024]{1,0:T(8,128)(2,1)S(1)}, u32[]{:S(2)}, u32[]{:S(2)}) %collective-permute-start.10) | collective-permute-done | bytes 98336 | tf_op jit(solution)/shard_map/ppermute | solution.py:247
  26.0 2.4 %backward.1 = (bf16[48,1024]{1,0:T(8,128)(2,1)S(1)}, bf16[48,1024]{1,0:T(8,128)(2,1)S(1)}, bf16[48,1024]{1,0:T(8,128)(2,1)S(1)}, bf16[48,1024]{1,0:T(8,128)(2,1)S(1)}) custom-call(bf16[48,1024]{1,0:T(8,128)(2,1)S(1)} %get-tuple-element.77.refs_0_, bf16[48,1024]{1,0:T(8,128)(2,1)S(1)} %collective-permute-done.5.refs_1_, ...), custom_call_target="tpu_custom_call" | custom-call | flops 905969664 | bytes 10813440 | tf_op jit(solution)/shard_map/backward/pallas_call | solution.py:23
  28.5 1.2 %collective-permute-start.15 = (bf16[48,1024]{1,0:T(8,128)(2,1)S(1)}, bf16[48,1024]{1,0:T(8,128)(2,1)S(1)}, u32[]{:S(2)}, u32[]{:S(2)}) collective-permute-start(bf16[48,1024]{1,0:T(8,128)(2,1)S(1)} %get-tuple-element.96), channel_id=1, source_target_pairs={{0,8},{4,12},{8,0},{12,4},{16,24},{20,28},{24,16},{28,20},{1,9},{5... | collective-permute-start | bytes 294920 | tf_op jit(solution)/shard_map/ppermute | solution.py:247
  29.7 0.9 %collective-permute-start.16 = (bf16[48,1024]{1,0:T(8,128)(2,1)S(1)}, bf16[48,1024]{1,0:T(8,128)(2,1)S(1)}, u32[]{:S(2)}, u32[]{:S(2)}) collective-permute-start(bf16[48,1024]{1,0:T(8,128)(2,1)S(1)} %get-tuple-element.97), channel_id=1, source_target_pairs={{0,16},{4,20},{8,24},{12,28},{16,0},{20,4},{24,8},{28,12},{1,17},{... | collective-permute-start | bytes 294920 | tf_op jit(solution)/shard_map/ppermute | solution.py:247
  30.7 2.7 %collective-permute-start.22 = (bf16[192,512]{1,0:T(8,128)(2,1)S(1)}, bf16[192,512]{1,0:T(8,128)(2,1)S(1)}, u32[]{:S(2)}, u32[]{:S(2)}) collective-permute-start(bf16[192,512]{1,0:T(8,128)(2,1)S(1)} %add_blocks.2.refs_0_), channel_id=1, source_target_pairs={{0,2},{1,3},{2,0},{3,1},{4,6},{5,7},{6,4},{7,5},{8,10},{9,11},{10,... | collective-permute-start | bytes 589832 | tf_op jit(solution)/shard_map/ppermute | solution.py:284
  33.4 3.5 %collective-permute-start.23 = (bf16[192,512]{1,0:T(8,128)(2,1)S(1)}, bf16[192,512]{1,0:T(8,128)(2,1)S(1)}, u32[]{:S(2)}, u32[]{:S(2)}) collective-permute-start(bf16[192,512]{1,0:T(8,128)(2,1)S(1)} %add_blocks.2.refs_0_), channel_id=1, source_target_pairs={{0,1},{1,2},{2,3},{4,5},{5,6},{6,7},{8,9},{9,10},{10,11},{12,13},{... | collective-permute-start | bytes 589832 | tf_op jit(solution)/shard_map/ppermute | solution.py:285
  36.8 1.3 %collective-permute-start.24 = (bf16[192,512]{1,0:T(8,128)(2,1)S(1)}, bf16[192,512]{1,0:T(8,128)(2,1)S(1)}, u32[]{:S(2)}, u32[]{:S(2)}) collective-permute-start(bf16[192,512]{1,0:T(8,128)(2,1)S(1)} %add_blocks.2.refs_0_), channel_id=1, source_target_pairs={{1,0},{2,1},{3,2},{5,4},{6,5},{7,6},{9,8},{10,9},{11,10},{13,12},{... | collective-permute-start | bytes 589832 | tf_op jit(solution)/shard_map/ppermute | solution.py:286
  38.2 2.2 %collective-permute-start.17 = (bf16[48,1024]{1,0:T(8,128)(2,1)S(1)}, bf16[48,1024]{1,0:T(8,128)(2,1)S(1)}, u32[]{:S(2)}, u32[]{:S(2)}) collective-permute-start(bf16[48,1024]{1,0:T(8,128)(2,1)S(1)} %get-tuple-element.98), channel_id=1, source_target_pairs={{0,24},{4,28},{8,16},{12,20},{16,8},{20,12},{24,0},{28,4},{1,25},{... | collective-permute-start | bytes 294920 | tf_op jit(solution)/shard_map/ppermute | solution.py:247
  40.4 3.4 %collective-permute-done.17.refs_3_ = bf16[48,1024]{1,0:T(8,128)(2,1)S(1)} collective-permute-done((bf16[48,1024]{1,0:T(8,128)(2,1)S(1)}, bf16[48,1024]{1,0:T(8,128)(2,1)S(1)}, u32[]{:S(2)}, u32[]{:S(2)}) %collective-permute-start.17) | collective-permute-done | bytes 98336 | tf_op jit(solution)/shard_map/ppermute | solution.py:247
  43.7 0.5 collective-permute-start.20
  44.3 1.3 %collective-permute-start.25 = (bf16[192,512]{1,0:T(8,128)(2,1)S(1)}, bf16[192,512]{1,0:T(8,128)(2,1)S(1)}, u32[]{:S(2)}, u32[]{:S(2)}) collective-permute-start(bf16[192,512]{1,0:T(8,128)(2,1)S(1)} %collective-permute-done.22.refs_1_), channel_id=1, source_target_pairs={{2,3},{1,0},{6,7},{5,4},{10,11},{9,8},{14,15},{13,12},{18,19},{17,... | collective-permute-start | bytes 589832 | tf_op jit(solution)/shard_map/ppermute | solution.py:287
  45.6 1.2 %collective-permute-done.24.refs_3_ = bf16[192,512]{1,0:T(8,128)(2,1)S(1)} collective-permute-done((bf16[192,512]{1,0:T(8,128)(2,1)S(1)}, bf16[192,512]{1,0:T(8,128)(2,1)S(1)}, u32[]{:S(2)}, u32[]{:S(2)}) %collective-permute-start.24) | collective-permute-done | bytes 196640 | tf_op jit(solution)/shard_map/ppermute | solution.py:286
  46.9 4.0 %collective-permute-start.26 = (bf16[192,512]{1,0:T(8,128)(2,1)S(1)}, bf16[192,512]{1,0:T(8,128)(2,1)S(1)}, u32[]{:S(2)}, u32[]{:S(2)}) collective-permute-start(bf16[192,512]{1,0:T(8,128)(2,1)S(1)} %add_blocks.3.refs_0_), channel_id=1, source_target_pairs={{0,2},{1,3},{2,0},{3,1},{4,6},{5,7},{6,4},{7,5},{8,10},{9,11},{10,... | collective-permute-start | bytes 589832 | tf_op jit(solution)/shard_map/ppermute | solution.py:284
  51.0 1.3 %collective-permute-start.27 = (bf16[192,512]{1,0:T(8,128)(2,1)S(1)}, bf16[192,512]{1,0:T(8,128)(2,1)S(1)}, u32[]{:S(2)}, u32[]{:S(2)}) collective-permute-start(bf16[192,512]{1,0:T(8,128)(2,1)S(1)} %add_blocks.3.refs_0_), channel_id=1, source_target_pairs={{0,1},{1,2},{2,3},{4,5},{5,6},{6,7},{8,9},{9,10},{10,11},{12,13},{... | collective-permute-start | bytes 589832 | tf_op jit(solution)/shard_map/ppermute | solution.py:285
  52.3 1.3 %collective-permute-start.28 = (bf16[192,512]{1,0:T(8,128)(2,1)S(1)}, bf16[192,512]{1,0:T(8,128)(2,1)S(1)}, u32[]{:S(2)}, u32[]{:S(2)}) collective-permute-start(bf16[192,512]{1,0:T(8,128)(2,1)S(1)} %add_blocks.3.refs_0_), channel_id=1, source_target_pairs={{1,0},{2,1},{3,2},{5,4},{6,5},{7,6},{9,8},{10,9},{11,10},{13,12},{... | collective-permute-start | bytes 589832 | tf_op jit(solution)/shard_map/ppermute | solution.py:286
  53.6 0.3 weights.1.weight_ref
  53.9 0.3 collective-permute-done.25.refs_4_
  54.2 6.4 %collective-permute-done.26.refs_1_ = bf16[192,512]{1,0:T(8,128)(2,1)S(1)} collective-permute-done((bf16[192,512]{1,0:T(8,128)(2,1)S(1)}, bf16[192,512]{1,0:T(8,128)(2,1)S(1)}, u32[]{:S(2)}, u32[]{:S(2)}) %collective-permute-start.26) | collective-permute-done | bytes 196640 | tf_op jit(solution)/shard_map/ppermute | solution.py:284
  60.6 1.7 %combine_gate.1 = (bf16[512,512]{1,0:T(8,128)(2,1)}, f32[8,512]{1,0:T(8,128)S(1)}) custom-call(bf16[512,768]{1,0:T(8,128)(2,1)S(1)} %weights.1.weight_ref, s32[8,512]{1,0:T(8,128)S(1)} %bitcast.6, f32[16,512]{1,0:T(8,128)S(1)} %number.1.key_ref, bf16[512,512]{1,0:T(8,128)(2,1)S(1)} %copy-done.3, bf16[192,512]{1,0:T(8,128)(2,1)S(1)} %add_blocks.2.refs_0_, ...), custom_call_target="tpu_custom_call" | custom-call | bytes 2883584 | tf_op jit(solution)/shard_map/combine_gate/pallas_call | solution.py:23
  62.3 2.2 %collective-permute-done.28.refs_3_ = bf16[192,512]{1,0:T(8,128)(2,1)S(1)} collective-permute-done((bf16[192,512]{1,0:T(8,128)(2,1)S(1)}, bf16[192,512]{1,0:T(8,128)(2,1)S(1)}, u32[]{:S(2)}, u32[]{:S(2)}) %collective-permute-start.28) | collective-permute-done | bytes 196640 | tf_op jit(solution)/shard_map/ppermute | solution.py:286
  64.5 1.2 %collective-permute-done.30 = f32[8,512]{1,0:T(8,128)S(1)} collective-permute-done((f32[8,512]{1,0:T(8,128)S(1)}, f32[8,512]{1,0:T(8,128)S(1)}, u32[]{:S(2)}, u32[]{:S(2)}) %collective-permute-start.30) | collective-permute-done | bytes 16416 | tf_op jit(solution)/shard_map/ppermute | solution.py:237
  65.7 1.7 %collective-permute-start.31 = (f32[8,512]{1,0:T(8,128)S(1)}, f32[8,512]{1,0:T(8,128)S(1)}, u32[]{:S(2)}, u32[]{:S(2)}) collective-permute-start(f32[8,512]{1,0:T(8,128)S(1)} %add.6), channel_id=1, source_target_pairs={{0,8},{4,12},{8,0},{12,4},{16,24},{20,28},{24,16},{28,20},{1,9},{5... | collective-permute-start | bytes 49160 | tf_op jit(solution)/shard_map/ppermute | solution.py:247
  67.3 1.3 %collective-permute-start.29 = (bf16[192,512]{1,0:T(8,128)(2,1)S(1)}, bf16[192,512]{1,0:T(8,128)(2,1)S(1)}, u32[]{:S(2)}, u32[]{:S(2)}) collective-permute-start(bf16[192,512]{1,0:T(8,128)(2,1)S(1)} %collective-permute-done.26.refs_1_), channel_id=1, source_target_pairs={{2,3},{1,0},{6,7},{5,4},{10,11},{9,8},{14,15},{13,12},{18,19},{17,... | collective-permute-start | bytes 589832 | tf_op jit(solution)/shard_map/ppermute | solution.py:287
  68.6 0.8 %collective-permute-done.31 = f32[8,512]{1,0:T(8,128)S(1)} collective-permute-done((f32[8,512]{1,0:T(8,128)S(1)}, f32[8,512]{1,0:T(8,128)S(1)}, u32[]{:S(2)}, u32[]{:S(2)}) %collective-permute-start.31) | collective-permute-done | bytes 16416 | tf_op jit(solution)/shard_map/ppermute | solution.py:247
  69.4 0.6 add_bitcast_fusion
  70.0 5.9 %collective-permute-done.29.refs_4_ = bf16[192,512]{1,0:T(8,128)(2,1)S(1)} collective-permute-done((bf16[192,512]{1,0:T(8,128)(2,1)S(1)}, bf16[192,512]{1,0:T(8,128)(2,1)S(1)}, u32[]{:S(2)}, u32[]{:S(2)}) %collective-permute-start.29) | collective-permute-done | bytes 196640 | tf_op jit(solution)/shard_map/ppermute | solution.py:287
  75.9 1.4 %combine.1 = bf16[512,512]{1,0:T(8,128)(2,1)} custom-call(bf16[512,768]{1,0:T(8,128)(2,1)S(1)} %weights.1.weight_ref, bf16[192,512]{1,0:T(8,128)(2,1)S(1)} %add_blocks.3.refs_0_, bf16[192,512]{1,0:T(8,128)(2,1)S(1)} %collective-permute-done.26.refs_1_, bf16[192,512]{1,0:T(8,128)(2,1)S(1)} %collective-permute-done.27.refs_2_, ...), custom_call_target="tpu_custom_call" | custom-call | flops 402653184 | bytes 2293760 | tf_op jit(solution)/shard_map/combine/pallas_call | solution.py:23
  (44 shorter events, 0.3 us)
Async XLA Ops:
  0.6 2.3 %collective-permute-start = (bf16[512,512]{1,0:T(8,128)(2,1)}, bf16[512,512]{1,0:T(8,128)(2,1)S(1)}, u32[]{:S(2)}, u32[]{:S(2)}) collective-permute-start(bf16[512,512]{1,0:T(8,128)(2,1)} %refs_0_.2), channel_id=1, source_target_pairs={{0,4},{4,0},{8,12},{12,8},{1,5},{5,1},{9,13},{13,9},{2,6},{6,2},{1... | collective-permute-start | bytes 1572872 | tf_op jit(solution)/shard_map/ppermute | solution.py:237
  1.1 6.7 %collective-permute-start.1 = (bf16[512,512]{1,0:T(8,128)(2,1)}, bf16[512,512]{1,0:T(8,128)(2,1)S(1)}, u32[]{:S(2)}, u32[]{:S(2)}) collective-permute-start(bf16[512,512]{1,0:T(8,128)(2,1)} %grads_ref.1), channel_id=1, source_target_pairs={{0,4},{4,0},{8,12},{12,8},{1,5},{5,1},{9,13},{13,9},{2,6},{6,2},{1... | collective-permute-start | bytes 1572872 | tf_op jit(solution)/shard_map/ppermute | solution.py:237
  1.2 0.7 copy-start.4
  1.9 1.0 %copy-start.7 = (bf16[512,512]{1,0:T(8,128)(2,1)S(1)}, bf16[512,512]{1,0:T(8,128)(2,1)}, u32[]{:S(2)}) copy-start(bf16[512,512]{1,0:T(8,128)(2,1)} %refs_0_.2) | copy-start | bytes 1572868
  2.1 5.8 %copy-start.3 = (bf16[512,512]{1,0:T(8,128)(2,1)S(1)}, bf16[512,512]{1,0:T(8,128)(2,1)}, u32[]{:S(2)}) copy-start(bf16[512,512]{1,0:T(8,128)(2,1)} %grads_ref.1) | copy-start | bytes 1572868
  3.3 8.4 %collective-permute-start.2 = (bf16[48,1024]{1,0:T(8,128)(2,1)S(1)}, bf16[48,1024]{1,0:T(8,128)(2,1)S(1)}, u32[]{:S(2)}, u32[]{:S(2)}) collective-permute-start(bf16[48,1024]{1,0:T(8,128)(2,1)S(1)} %get-tuple-element.66), channel_id=1, source_target_pairs={{0,8},{4,12},{8,0},{12,4},{16,24},{20,28},{24,16},{28,20},{1,9},{5... | collective-permute-start | bytes 294920 | tf_op jit(solution)/shard_map/ppermute | solution.py:247
  6.3 9.5 %collective-permute-start.4 = (bf16[48,1024]{1,0:T(8,128)(2,1)S(1)}, bf16[48,1024]{1,0:T(8,128)(2,1)S(1)}, u32[]{:S(2)}, u32[]{:S(2)}) collective-permute-start(bf16[48,1024]{1,0:T(8,128)(2,1)S(1)} %get-tuple-element.66), channel_id=1, source_target_pairs={{0,24},{4,28},{8,16},{12,20},{16,8},{20,12},{24,0},{28,4},{1,25},{... | collective-permute-start | bytes 294920 | tf_op jit(solution)/shard_map/ppermute | solution.py:247
  7.8 8.1 %copy-start = (bf16[1,768,2048]{2,1,0:T(8,128)(2,1)S(1)}, bf16[1,768,2048]{2,1,0:T(8,128)(2,1)}, u32[]{:S(2)}) copy-start(bf16[1,768,2048]{2,1,0:T(8,128)(2,1)} %refs_4_.3) | copy-start | bytes 9437188
  7.8 8.1 %copy-start.1 = (bf16[1,768,2048]{2,1,0:T(8,128)(2,1)S(1)}, bf16[1,768,2048]{2,1,0:T(8,128)(2,1)}, u32[]{:S(2)}) copy-start(bf16[1,768,2048]{2,1,0:T(8,128)(2,1)} %refs_5_.3) | copy-start | bytes 9437188
  7.8 8.1 %copy-start.2 = (bf16[1,768,2048]{2,1,0:T(8,128)(2,1)S(1)}, bf16[1,768,2048]{2,1,0:T(8,128)(2,1)}, u32[]{:S(2)}) copy-start(bf16[1,768,2048]{2,1,0:T(8,128)(2,1)} %refs_6_.3) | copy-start | bytes 9437188
  7.8 8.0 %collective-permute-start.3 = (bf16[48,1024]{1,0:T(8,128)(2,1)S(1)}, bf16[48,1024]{1,0:T(8,128)(2,1)S(1)}, u32[]{:S(2)}, u32[]{:S(2)}) collective-permute-start(bf16[48,1024]{1,0:T(8,128)(2,1)S(1)} %get-tuple-element.65.refs_0_), channel_id=1, source_target_pairs={{0,16},{4,20},{8,24},{12,28},{16,0},{20,4},{24,8},{28,12},{1,17},{... | collective-permute-start | bytes 294920 | tf_op jit(solution)/shard_map/ppermute | solution.py:247
  8.2 10.2 %collective-permute-start.5 = (bf16[48,1024]{1,0:T(8,128)(2,1)S(1)}, bf16[48,1024]{1,0:T(8,128)(2,1)S(1)}, u32[]{:S(2)}, u32[]{:S(2)}) collective-permute-start(bf16[48,1024]{1,0:T(8,128)(2,1)S(1)} %get-tuple-element.72), channel_id=1, source_target_pairs={{0,8},{4,12},{8,0},{12,4},{16,24},{20,28},{24,16},{28,20},{1,9},{5... | collective-permute-start | bytes 294920 | tf_op jit(solution)/shard_map/ppermute | solution.py:247
  10.1 8.3 %collective-permute-start.6 = (bf16[48,1024]{1,0:T(8,128)(2,1)S(1)}, bf16[48,1024]{1,0:T(8,128)(2,1)S(1)}, u32[]{:S(2)}, u32[]{:S(2)}) collective-permute-start(bf16[48,1024]{1,0:T(8,128)(2,1)S(1)} %get-tuple-element.77.refs_0_), channel_id=1, source_target_pairs={{0,16},{4,20},{8,24},{12,28},{16,0},{20,4},{24,8},{28,12},{1,17},{... | collective-permute-start | bytes 294920 | tf_op jit(solution)/shard_map/ppermute | solution.py:247
  11.7 6.8 %collective-permute-start.7 = (bf16[48,1024]{1,0:T(8,128)(2,1)S(1)}, bf16[48,1024]{1,0:T(8,128)(2,1)S(1)}, u32[]{:S(2)}, u32[]{:S(2)}) collective-permute-start(bf16[48,1024]{1,0:T(8,128)(2,1)S(1)} %get-tuple-element.72), channel_id=1, source_target_pairs={{0,24},{4,28},{8,16},{12,20},{16,8},{20,12},{24,0},{28,4},{1,25},{... | collective-permute-start | bytes 294920 | tf_op jit(solution)/shard_map/ppermute | solution.py:247
  18.4 5.4 %collective-permute-start.8 = (bf16[48,1024]{1,0:T(8,128)(2,1)S(1)}, bf16[48,1024]{1,0:T(8,128)(2,1)S(1)}, u32[]{:S(2)}, u32[]{:S(2)}) collective-permute-start(bf16[48,1024]{1,0:T(8,128)(2,1)S(1)} %get-tuple-element.74), channel_id=1, source_target_pairs={{0,8},{4,12},{8,0},{12,4},{16,24},{20,28},{24,16},{28,20},{1,9},{5... | collective-permute-start | bytes 294920 | tf_op jit(solution)/shard_map/ppermute | solution.py:247
  20.1 4.8 %collective-permute-start.9 = (bf16[48,1024]{1,0:T(8,128)(2,1)S(1)}, bf16[48,1024]{1,0:T(8,128)(2,1)S(1)}, u32[]{:S(2)}, u32[]{:S(2)}) collective-permute-start(bf16[48,1024]{1,0:T(8,128)(2,1)S(1)} %get-tuple-element.75), channel_id=1, source_target_pairs={{0,16},{4,20},{8,24},{12,28},{16,0},{20,4},{24,8},{28,12},{1,17},{... | collective-permute-start | bytes 294920 | tf_op jit(solution)/shard_map/ppermute | solution.py:247
  20.5 5.5 %collective-permute-start.10 = (bf16[48,1024]{1,0:T(8,128)(2,1)S(1)}, bf16[48,1024]{1,0:T(8,128)(2,1)S(1)}, u32[]{:S(2)}, u32[]{:S(2)}) collective-permute-start(bf16[48,1024]{1,0:T(8,128)(2,1)S(1)} %get-tuple-element.76), channel_id=1, source_target_pairs={{0,24},{4,28},{8,16},{12,20},{16,8},{20,12},{24,0},{28,4},{1,25},{... | collective-permute-start | bytes 294920 | tf_op jit(solution)/shard_map/ppermute | solution.py:247
  22.0 6.5 %collective-permute-start.11 = (bf16[48,1024]{1,0:T(8,128)(2,1)S(1)}, bf16[48,1024]{1,0:T(8,128)(2,1)S(1)}, u32[]{:S(2)}, u32[]{:S(2)}) collective-permute-start(bf16[48,1024]{1,0:T(8,128)(2,1)S(1)} %get-tuple-element.87.refs_0_), channel_id=1, source_target_pairs={{0,4},{4,0},{8,12},{12,8},{1,5},{5,1},{9,13},{13,9},{2,6},{6,2},{1... | collective-permute-start | bytes 294920 | tf_op jit(solution)/shard_map/ppermute | solution.py:237
  23.8 4.7 %collective-permute-start.12 = (bf16[48,1024]{1,0:T(8,128)(2,1)S(1)}, bf16[48,1024]{1,0:T(8,128)(2,1)S(1)}, u32[]{:S(2)}, u32[]{:S(2)}) collective-permute-start(bf16[48,1024]{1,0:T(8,128)(2,1)S(1)} %collective-permute-done.8.refs_1_), channel_id=1, source_target_pairs={{0,4},{4,0},{8,12},{12,8},{1,5},{5,1},{9,13},{13,9},{2,6},{6,2},{1... | collective-permute-start | bytes 294920 | tf_op jit(solution)/shard_map/ppermute | solution.py:237
  24.9 3.7 %collective-permute-start.13 = (bf16[48,1024]{1,0:T(8,128)(2,1)S(1)}, bf16[48,1024]{1,0:T(8,128)(2,1)S(1)}, u32[]{:S(2)}, u32[]{:S(2)}) collective-permute-start(bf16[48,1024]{1,0:T(8,128)(2,1)S(1)} %collective-permute-done.9.refs_2_), channel_id=1, source_target_pairs={{0,4},{4,0},{8,12},{12,8},{1,5},{5,1},{9,13},{13,9},{2,6},{6,2},{1... | collective-permute-start | bytes 294920 | tf_op jit(solution)/shard_map/ppermute | solution.py:237
  26.0 2.5 %collective-permute-start.14 = (bf16[48,1024]{1,0:T(8,128)(2,1)S(1)}, bf16[48,1024]{1,0:T(8,128)(2,1)S(1)}, u32[]{:S(2)}, u32[]{:S(2)}) collective-permute-start(bf16[48,1024]{1,0:T(8,128)(2,1)S(1)} %collective-permute-done.10.refs_3_), channel_id=1, source_target_pairs={{0,4},{4,0},{8,12},{12,8},{1,5},{5,1},{9,13},{13,9},{2,6},{6,2},{1... | collective-permute-start | bytes 294920 | tf_op jit(solution)/shard_map/ppermute | solution.py:237
  26.0 27.5 %copy-start.5 = (s32[512,8]{0,1:T(8,128)S(1)}, s32[512,8]{0,1:T(8,128)}, u32[]{:S(2)}) copy-start(s32[512,8]{0,1:T(8,128)} %param.9) | copy-start | bytes 49156
  26.0 27.5 %copy-start.6 = (f32[512,8]{0,1:T(8,128)S(1)}, f32[512,8]{0,1:T(8,128)}, u32[]{:S(2)}) copy-start(f32[512,8]{0,1:T(8,128)} %param.10) | copy-start | bytes 49156
  28.5 9.6 %collective-permute-start.15 = (bf16[48,1024]{1,0:T(8,128)(2,1)S(1)}, bf16[48,1024]{1,0:T(8,128)(2,1)S(1)}, u32[]{:S(2)}, u32[]{:S(2)}) collective-permute-start(bf16[48,1024]{1,0:T(8,128)(2,1)S(1)} %get-tuple-element.96), channel_id=1, source_target_pairs={{0,8},{4,12},{8,0},{12,4},{16,24},{20,28},{24,16},{28,20},{1,9},{5... | collective-permute-start | bytes 294920 | tf_op jit(solution)/shard_map/ppermute | solution.py:247
  29.7 10.6 %collective-permute-start.16 = (bf16[48,1024]{1,0:T(8,128)(2,1)S(1)}, bf16[48,1024]{1,0:T(8,128)(2,1)S(1)}, u32[]{:S(2)}, u32[]{:S(2)}) collective-permute-start(bf16[48,1024]{1,0:T(8,128)(2,1)S(1)} %get-tuple-element.97), channel_id=1, source_target_pairs={{0,16},{4,20},{8,24},{12,28},{16,0},{20,4},{24,8},{28,12},{1,17},{... | collective-permute-start | bytes 294920 | tf_op jit(solution)/shard_map/ppermute | solution.py:247
  30.7 13.6 %collective-permute-start.22 = (bf16[192,512]{1,0:T(8,128)(2,1)S(1)}, bf16[192,512]{1,0:T(8,128)(2,1)S(1)}, u32[]{:S(2)}, u32[]{:S(2)}) collective-permute-start(bf16[192,512]{1,0:T(8,128)(2,1)S(1)} %add_blocks.2.refs_0_), channel_id=1, source_target_pairs={{0,2},{1,3},{2,0},{3,1},{4,6},{5,7},{6,4},{7,5},{8,10},{9,11},{10,... | collective-permute-start | bytes 589832 | tf_op jit(solution)/shard_map/ppermute | solution.py:284
  33.4 11.0 %collective-permute-start.23 = (bf16[192,512]{1,0:T(8,128)(2,1)S(1)}, bf16[192,512]{1,0:T(8,128)(2,1)S(1)}, u32[]{:S(2)}, u32[]{:S(2)}) collective-permute-start(bf16[192,512]{1,0:T(8,128)(2,1)S(1)} %add_blocks.2.refs_0_), channel_id=1, source_target_pairs={{0,1},{1,2},{2,3},{4,5},{5,6},{6,7},{8,9},{9,10},{10,11},{12,13},{... | collective-permute-start | bytes 589832 | tf_op jit(solution)/shard_map/ppermute | solution.py:285
  36.8 10.0 %collective-permute-start.24 = (bf16[192,512]{1,0:T(8,128)(2,1)S(1)}, bf16[192,512]{1,0:T(8,128)(2,1)S(1)}, u32[]{:S(2)}, u32[]{:S(2)}) collective-permute-start(bf16[192,512]{1,0:T(8,128)(2,1)S(1)} %add_blocks.2.refs_0_), channel_id=1, source_target_pairs={{1,0},{2,1},{3,2},{5,4},{6,5},{7,6},{9,8},{10,9},{11,10},{13,12},{... | collective-permute-start | bytes 589832 | tf_op jit(solution)/shard_map/ppermute | solution.py:286
  38.2 5.6 %collective-permute-start.17 = (bf16[48,1024]{1,0:T(8,128)(2,1)S(1)}, bf16[48,1024]{1,0:T(8,128)(2,1)S(1)}, u32[]{:S(2)}, u32[]{:S(2)}) collective-permute-start(bf16[48,1024]{1,0:T(8,128)(2,1)S(1)} %get-tuple-element.98), channel_id=1, source_target_pairs={{0,24},{4,28},{8,16},{12,20},{16,8},{20,12},{24,0},{28,4},{1,25},{... | collective-permute-start | bytes 294920 | tf_op jit(solution)/shard_map/ppermute | solution.py:247
  40.4 3.4 %collective-permute-start.18 = (bf16[48,1024]{1,0:T(8,128)(2,1)S(1)}, bf16[48,1024]{1,0:T(8,128)(2,1)S(1)}, u32[]{:S(2)}, u32[]{:S(2)}) collective-permute-start(bf16[48,1024]{1,0:T(8,128)(2,1)S(1)} %get-tuple-element.102.refs_0_), channel_id=1, source_target_pairs={{0,4},{4,0},{8,12},{12,8},{1,5},{5,1},{9,13},{13,9},{2,6},{6,2},{1... | collective-permute-start | bytes 294920 | tf_op jit(solution)/shard_map/ppermute | solution.py:237
  43.7 3.1 %collective-permute-start.19 = (bf16[48,1024]{1,0:T(8,128)(2,1)S(1)}, bf16[48,1024]{1,0:T(8,128)(2,1)S(1)}, u32[]{:S(2)}, u32[]{:S(2)}) collective-permute-start(bf16[48,1024]{1,0:T(8,128)(2,1)S(1)} %collective-permute-done.15.refs_1_), channel_id=1, source_target_pairs={{0,4},{4,0},{8,12},{12,8},{1,5},{5,1},{9,13},{13,9},{2,6},{6,2},{1... | collective-permute-start | bytes 294920 | tf_op jit(solution)/shard_map/ppermute | solution.py:237
  43.7 3.1 %collective-permute-start.20 = (bf16[48,1024]{1,0:T(8,128)(2,1)S(1)}, bf16[48,1024]{1,0:T(8,128)(2,1)S(1)}, u32[]{:S(2)}, u32[]{:S(2)}) collective-permute-start(bf16[48,1024]{1,0:T(8,128)(2,1)S(1)} %collective-permute-done.16.refs_2_), channel_id=1, source_target_pairs={{0,4},{4,0},{8,12},{12,8},{1,5},{5,1},{9,13},{13,9},{2,6},{6,2},{1... | collective-permute-start | bytes 294920 | tf_op jit(solution)/shard_map/ppermute | solution.py:237
  44.3 2.6 %collective-permute-start.21 = (bf16[48,1024]{1,0:T(8,128)(2,1)S(1)}, bf16[48,1024]{1,0:T(8,128)(2,1)S(1)}, u32[]{:S(2)}, u32[]{:S(2)}) collective-permute-start(bf16[48,1024]{1,0:T(8,128)(2,1)S(1)} %collective-permute-done.17.refs_3_), channel_id=1, source_target_pairs={{0,4},{4,0},{8,12},{12,8},{1,5},{5,1},{9,13},{13,9},{2,6},{6,2},{1... | collective-permute-start | bytes 294920 | tf_op jit(solution)/shard_map/ppermute | solution.py:237
  44.3 9.8 %collective-permute-start.25 = (bf16[192,512]{1,0:T(8,128)(2,1)S(1)}, bf16[192,512]{1,0:T(8,128)(2,1)S(1)}, u32[]{:S(2)}, u32[]{:S(2)}) collective-permute-start(bf16[192,512]{1,0:T(8,128)(2,1)S(1)} %collective-permute-done.22.refs_1_), channel_id=1, source_target_pairs={{2,3},{1,0},{6,7},{5,4},{10,11},{9,8},{14,15},{13,12},{18,19},{17,... | collective-permute-start | bytes 589832 | tf_op jit(solution)/shard_map/ppermute | solution.py:287
  46.9 13.6 %collective-permute-start.26 = (bf16[192,512]{1,0:T(8,128)(2,1)S(1)}, bf16[192,512]{1,0:T(8,128)(2,1)S(1)}, u32[]{:S(2)}, u32[]{:S(2)}) collective-permute-start(bf16[192,512]{1,0:T(8,128)(2,1)S(1)} %add_blocks.3.refs_0_), channel_id=1, source_target_pairs={{0,2},{1,3},{2,0},{3,1},{4,6},{5,7},{6,4},{7,5},{8,10},{9,11},{10,... | collective-permute-start | bytes 589832 | tf_op jit(solution)/shard_map/ppermute | solution.py:284
  51.0 11.3 %collective-permute-start.27 = (bf16[192,512]{1,0:T(8,128)(2,1)S(1)}, bf16[192,512]{1,0:T(8,128)(2,1)S(1)}, u32[]{:S(2)}, u32[]{:S(2)}) collective-permute-start(bf16[192,512]{1,0:T(8,128)(2,1)S(1)} %add_blocks.3.refs_0_), channel_id=1, source_target_pairs={{0,1},{1,2},{2,3},{4,5},{5,6},{6,7},{8,9},{9,10},{10,11},{12,13},{... | collective-permute-start | bytes 589832 | tf_op jit(solution)/shard_map/ppermute | solution.py:285
  52.3 12.2 %collective-permute-start.28 = (bf16[192,512]{1,0:T(8,128)(2,1)S(1)}, bf16[192,512]{1,0:T(8,128)(2,1)S(1)}, u32[]{:S(2)}, u32[]{:S(2)}) collective-permute-start(bf16[192,512]{1,0:T(8,128)(2,1)S(1)} %add_blocks.3.refs_0_), channel_id=1, source_target_pairs={{1,0},{2,1},{3,2},{5,4},{6,5},{7,6},{9,8},{10,9},{11,10},{13,12},{... | collective-permute-start | bytes 589832 | tf_op jit(solution)/shard_map/ppermute | solution.py:286
  64.5 1.2 %collective-permute-start.30 = (f32[8,512]{1,0:T(8,128)S(1)}, f32[8,512]{1,0:T(8,128)S(1)}, u32[]{:S(2)}, u32[]{:S(2)}) collective-permute-start(f32[8,512]{1,0:T(8,128)S(1)} %get-tuple-element.120), channel_id=1, source_target_pairs={{0,4},{4,0},{8,12},{12,8},{1,5},{5,1},{9,13},{13,9},{2,6},{6,2},{1... | collective-permute-start | bytes 49160 | tf_op jit(solution)/shard_map/ppermute | solution.py:237
  65.7 3.7 %collective-permute-start.31 = (f32[8,512]{1,0:T(8,128)S(1)}, f32[8,512]{1,0:T(8,128)S(1)}, u32[]{:S(2)}, u32[]{:S(2)}) collective-permute-start(f32[8,512]{1,0:T(8,128)S(1)} %add.6), channel_id=1, source_target_pairs={{0,8},{4,12},{8,0},{12,4},{16,24},{20,28},{24,16},{28,20},{1,9},{5... | collective-permute-start | bytes 49160 | tf_op jit(solution)/shard_map/ppermute | solution.py:247
  67.3 8.6 %collective-permute-start.29 = (bf16[192,512]{1,0:T(8,128)(2,1)S(1)}, bf16[192,512]{1,0:T(8,128)(2,1)S(1)}, u32[]{:S(2)}, u32[]{:S(2)}) collective-permute-start(bf16[192,512]{1,0:T(8,128)(2,1)S(1)} %collective-permute-done.26.refs_1_), channel_id=1, source_target_pairs={{2,3},{1,0},{6,7},{5,4},{10,11},{9,8},{14,15},{13,12},{18,19},{17,... | collective-permute-start | bytes 589832 | tf_op jit(solution)/shard_map/ppermute | solution.py:287

commit v7 on v6

--- a/solution.py
+++ b/solution.py
@@ -59,7 +59,7 @@
 
 
 def pick_kernel(cores, key_ref, *refs):
-    sources, pieces = refs[:cores], refs[cores:]
+    sources, pieces = refs[: 2 * cores], refs[2 * cores :]
     chips = len(pieces)
     rows, width = sources[0].shape
     chip, core, e = position(cores)
@@ -69,20 +69,21 @@
         expert = (e * chips + lax.rem(chip + dh, chips)) * cores + core
         masks.append((key_ref[pl.ds(expert, 1), :] == slot).astype(BF16))
     mask = jnp.concatenate(masks, axis=0)
-    for dc, source in enumerate(sources):
+    for index, source in enumerate(sources):
+        kind, dc = divmod(index, cores)
         picked = jnp.dot(mask, source[...], preferred_element_type=F32).astype(BF16)
         column = pl.multiple_of(lax.rem(core - dc + cores, cores) * width, width)
         for dh, piece in enumerate(pieces):
-            piece[:, pl.ds(column, width)] = picked[dh * CAP : (dh + 1) * CAP]
-
-
-def gather_pieces(x_ref, pieces, chips, cores):
+            piece[kind * CAP : (kind + 1) * CAP, pl.ds(column, width)] = picked[dh * CAP : (dh + 1) * CAP]
+
+
+def gather_pieces(x_ref, pieces, kind, chips, cores):
     chip, _, _ = position(cores)
     width = pieces[0].shape[1]
     for index, piece in enumerate(pieces):
         db, dh = divmod(index, chips)
         column = pl.multiple_of(lax.rem(chip - dh + chips, chips) * width, width)
-        x_ref[db * CAP : (db + 1) * CAP, pl.ds(column, width)] = piece[...]
+        x_ref[db * CAP : (db + 1) * CAP, pl.ds(column, width)] = piece[kind * CAP : (kind + 1) * CAP, :]
 
 
 def project_back(terms, pieces, chips, cores):
@@ -110,7 +111,7 @@
     pieces, (gate_ref, up_ref, down_ref) = refs[:count], refs[count : count + 3]
     act_ref, scale_ref = refs[count + 3 : count + 5]
     outs, (x_ref, hid_ref) = refs[count + 5 : 2 * count + 5], refs[2 * count + 5 :]
-    gather_pieces(x_ref, pieces, chips, cores)
+    gather_pieces(x_ref, pieces, 0, chips, cores)
     for part in chunks_of(gate_ref.shape[1]):
         gate_pre = lax.dot_general(x_ref[...], gate_ref[0, part, :], CONTRACT_LAST, preferred_element_type=F32)
         up_pre = lax.dot_general(x_ref[...], up_ref[0, part, :], CONTRACT_LAST, preferred_element_type=F32)
@@ -126,7 +127,7 @@
     pieces, (gate_ref, up_ref, down_ref) = refs[:count], refs[count : count + 3]
     act_ref, scale_ref = refs[count + 3 : count + 5]
     outs, (x_ref, grad_gate_ref, grad_up_ref) = refs[count + 5 : 2 * count + 5], refs[2 * count + 5 :]
-    gather_pieces(x_ref, pieces, chips, cores)
+    gather_pieces(x_ref, pieces, 1, chips, cores)
     for part in chunks_of(gate_ref.shape[1]):
         grad_hid = lax.dot_general(x_ref[...], down_ref[0, part, :], CONTRACT_LAST, preferred_element_type=F32)
         grad_gate_ref[:, part] = (grad_hid * scale_ref[:, part]).astype(BF16)
@@ -194,9 +195,14 @@
 
 
 def combine_kernel(columns, weight_ref, *refs):
-    parts, (out_ref, all_ref) = refs[:-2], refs[-2:]
+    parts, gates = refs[:columns], refs[columns:-3]
+    out_ref, total_ref, all_ref = refs[-3:]
     place_parts(parts, all_ref, columns)
     out_ref[...] = jnp.dot(weight_ref[...], all_ref[...], preferred_element_type=F32).astype(BF16)
+    total = gates[0][...]
+    for gate in gates[1:]:
+        total = total + gate[...]
+    total_ref[...] = total
 
 
 def combine_gate_kernel(chips, cores, columns, weight_ref, routes_ref, key_ref, grads_ref, *refs):
@@ -249,15 +255,6 @@
     hops = [(db, dh) for db in range(n_dp) for dh in range(chips)]
     order = sorted(range(count), key=lambda index: (hops[index][0] == 0, -hops[index][1]))
 
-    def pick(key, sources):
-        return call(
-            functools.partial(pick_kernel, cores),
-            "pick",
-            [shape(CAP, cores * width)] * chips,
-            [key, *sources],
-            EARLY,
-        )
-
     def dispatch(pieces):
         arrived = {index: to_chip(pieces[hops[index][1]], *hops[index]) for index in order}
         return [arrived[index] for index in range(count)]
@@ -276,23 +273,30 @@
         )
 
     def across(value):
+        parts = [value]
+        for dz in range(1, columns):
+            parts.append(lax.ppermute(value, "expert", [(z, (z + dz) % columns) for z in range(columns)]))
+        return parts
+
+    def along(value):
         if columns != 4:
-            return [value] + [
-                lax.ppermute(value, "expert", [(z, (z + dz) % columns) for z in range(columns)])
-                for dz in range(1, columns)
-            ]
+            return across(value)
         far = lax.ppermute(value, "expert", [(z, (z + 2) % columns) for z in range(columns)])
         up = lax.ppermute(value, "expert", [(z, z + 1) for z in range(columns - 1)])
         down = lax.ppermute(value, "expert", [(z + 1, z) for z in range(columns - 1)])
         ends = lax.ppermute(far, "expert", [(2, 3), (1, 0)])
         return [value, far, up, down, ends]
 
-    token_sources = [to_core(tokens, dc) for dc in range(cores)]
-    grad_sources = [to_core(grad_out, dc) for dc in range(cores)]
+    sources = [to_core(tokens, dc) for dc in range(cores)] + [to_core(grad_out, dc) for dc in range(cores)]
     key = call(number_kernel, "number", shape(experts, rows, F32), [routes_t], EARLY)
-    tok_in = dispatch(pick(key, token_sources))
-    tok_in[0], grad_pieces = lax.optimization_barrier((tok_in[0], pick(key, grad_sources)))
-    grad_in = dispatch(grad_pieces)
+    picked = call(
+        functools.partial(pick_kernel, cores),
+        "pick",
+        [shape(2 * CAP, cores * width)] * chips,
+        [key, *sources],
+        EARLY,
+    )
+    rows_in = dispatch(picked)
 
     matmul_flops = 2 * tall * hid_dev * feats
     saved = [shape(tall, hid_dev, F32)] * 2
@@ -301,28 +305,30 @@
         functools.partial(forward_kernel, chips, cores, count),
         "forward",
         saved + piece,
-        [*tok_in, gate_weight, up_weight, down_weight],
+        [*rows_in, gate_weight, up_weight, down_weight],
         3 * matmul_flops,
         [pltpu.VMEM((tall, feats), BF16), pltpu.VMEM((tall, hid_dev), BF16)],
         limit=24,
     )
-    outs, grad_in = after(outs, grad_in)
     out_pieces = give_back(outs)
     backs = call(
         functools.partial(backward_kernel, chips, cores, count),
         "backward",
         piece,
-        [*grad_in, gate_weight, up_weight, down_weight, act, scale],
+        [*rows_in, gate_weight, up_weight, down_weight, act, scale],
         3 * matmul_flops,
         [pltpu.VMEM((tall, feats), BF16)] + [pltpu.VMEM((tall, hid_dev), BF16)] * 2,
         limit=24,
     )
     out_pieces, backs = after(out_pieces, backs)
-    out_parts = across(add_blocks(out_pieces))
+    out_rows = add_blocks(out_pieces)
+    out_rows, backs = after(out_rows, backs)
+    out_parts = along(out_rows)
     back_pieces = give_back(backs)
     back_pieces, out_parts[1:4] = after(back_pieces, out_parts[1:4])
-    back_parts = across(add_blocks(back_pieces))
-    out_parts, back_parts[1:2] = after(out_parts, back_parts[1:2])
+    back_rows = add_blocks(back_pieces)
+    back_parts = across(back_rows)
+    _, out_parts = after(back_rows, out_parts)
 
     weight_map = call(
         functools.partial(weights_kernel, chips, cores, columns),
@@ -345,22 +351,20 @@
         [all_rows, pltpu.VMEM((experts * CAP, rows), F32)],
         limit=24,
     )
-    gate_part, back_parts[2:4] = after(gate_part, back_parts[2:4])
-    for dc in range(1, cores):
-        gate_part = gate_part + to_core(gate_part, dc)
-    total = gate_part
-    for dh in range(1, chips):
-        total = total + to_chip(gate_part, 0, dh)
-    grad_tokens = call(
+    gate_parts = [gate_part]
+    for dt in range(1, groups):
+        pairs = [(t, (t + dt) % groups) for t in range(groups)]
+        gate_parts.append(lax.ppermute(gate_part, "tensor", pairs))
+    grad_tokens, grad_gates = call(
         functools.partial(combine_kernel, columns),
         "combine",
-        shape(rows, width),
-        [weight_map, *back_parts],
+        [shape(rows, width), shape(*gate_part.shape, F32)],
+        [weight_map, *back_parts, *gate_parts],
         combine_flops,
         [all_rows],
         limit=16,
     )
-    return (mixed, grad_tokens, total.T)
+    return (mixed, grad_tokens, grad_gates.T)
 
 
 def solution(mesh):

time: 77.6 us -> 70.8 us (0.912)
  starting transfers between devices: 36.6 us -> 30.9 us
    ppermute x13 -> x9, starting transfers between devices: 18.8 us -> 11.7 us  [to_chip(): return lax.ppermute(value, ('dp', 'tensor'), pairs)]
    ppermute x13 -> x9, waiting for transfers between devices: 11.1 us -> 17.9 us  [to_chip(): return lax.ppermute(value, ('dp', 'tensor'), pairs)]
    ppermute x8 -> x10, waiting for transfers between devices: 16 us -> 9.45 us  [the longest x1 4.93 us: along(): ends = lax.ppermute(far, 'expert', [(2, 3), (1, 0)])]
    ppermute x8 -> x10, starting transfers between devices: 16.6 us -> 18 us  [the longest x3 6.93 us: across(): lax.ppermute(value, 'expert', [(z, (z + dz) % columns) for z in range(col...]
    ppermute x11 -> x10, waiting for transfers between devices: 1.98 us -> 1.54 us  [to_core(): return lax.ppermute(value, 'tensor', pairs)]
    pallas_call x10 -> x9, Pallas kernels: 9.28 us -> 9.16 us  [call(): pl.pallas_call(kernel, out_shape=out_shape, in_specs=[spec] * len(operand...]
  transfers between devices with their start and end apart: 32 -> 29, of which waited for: 13 -> 13; matrix products, arithmetic and copies ran while one was open for 1% -> 0% of each run, Pallas kernels for 10% -> 7%
where the time goes in v7:
time: 70.8 us; the launch traced here: 70.5 us
  starting transfers between devices  30.9 us (44%)
  waiting for transfers between devices  28.9 us (41%)
  Pallas kernels  9.16 us (13%)
  between operations  0.79 us (1%)
  local copies, waits for them, and re-layouts  0.75 us (1%)
    ppermute x9, waiting for transfers between devices, to_chip(): return lax.ppermute(value, ('dp', 'tensor'), pairs)  17.9 us
    ppermute x9, starting transfers between devices, to_chip(): return lax.ppermute(value, ('dp', 'tensor'), pairs)  11.7 us
    pallas_call x9, Pallas kernels, call(): pl.pallas_call(kernel, out_shape=out_shape, in_specs=[spec] * len(operand...  9.16 us
    ppermute x3, starting transfers between devices, across(): lax.ppermute(value, 'expert', [(z, (z + dz) % columns) for z in range(col...  6.93 us
    ppermute x1, waiting for transfers between devices, along(): ends = lax.ppermute(far, 'expert', [(2, 3), (1, 0)])  4.93 us
    ppermute x1, starting transfers between devices, along(): up = lax.ppermute(value, 'expert', [(z, z + 1) for z in range(columns - 1)])  3.48 us
    ppermute x3, waiting for transfers between devices, across(): lax.ppermute(value, 'expert', [(z, (z + dz) % columns) for z in range(col...  3.27 us
    ppermute x1, starting transfers between devices, along(): lax.ppermute(value, 'expert', [(z, (z + 2) % columns) for z in range(colu...  2.58 us
  transfers between devices with their start and end apart: 29, of which 13 were waited for; matrix products, arithmetic and copies ran while one was open for 0% of the time, Pallas kernels for 7%

profile of v7, /device:TPU:0, one launch (start us, length us, event | category | flops | bytes accessed | tf_op | source)
XLA Modules:
  0.0 70.5 jit_solution(8533425564178348228)
XLA Ops:
  0.6 0.5 collective-permute-start
  1.1 0.1 collective-permute-start.1
  1.2 0.7 %copy-done.4 = s32[512,8]{0,1:T(8,128)S(1)} copy-done((s32[512,8]{0,1:T(8,128)S(1)}, s32[512,8]{0,1:T(8,128)}, u32[]{:S(2)}) %copy-start.4) | copy-done | bytes 16408
  1.9 0.1 number.1.key_ref
  2.1 0.0 copy-start.1
  2.1 0.0 copy-start.2
  2.1 0.8 %collective-permute-done.refs_1_ = bf16[512,512]{1,0:T(8,128)(2,1)S(1)} collective-permute-done((bf16[512,512]{1,0:T(8,128)(2,1)}, bf16[512,512]{1,0:T(8,128)(2,1)S(1)}, u32[]{:S(2)}, u32[]{:S(2)}) %collective-permute-start) | collective-permute-done | bytes 524320 | tf_op jit(solution)/shard_map/ppermute | solution.py:243
  2.9 0.7 %collective-permute-done.1.refs_3_ = bf16[512,512]{1,0:T(8,128)(2,1)S(1)} collective-permute-done((bf16[512,512]{1,0:T(8,128)(2,1)}, bf16[512,512]{1,0:T(8,128)(2,1)S(1)}, u32[]{:S(2)}, u32[]{:S(2)}) %collective-permute-start.1) | collective-permute-done | bytes 524320 | tf_op jit(solution)/shard_map/ppermute | solution.py:243
  3.7 0.5 pick.1
  4.1 3.0 %collective-permute-start.3 = (bf16[96,1024]{1,0:T(8,128)(2,1)S(1)}, bf16[96,1024]{1,0:T(8,128)(2,1)S(1)}, u32[]{:S(2)}, u32[]{:S(2)}) collective-permute-start(bf16[96,1024]{1,0:T(8,128)(2,1)S(1)} %get-tuple-element.52.refs_0_), channel_id=1, source_target_pairs={{0,16},{4,20},{8,24},{12,28},{16,0},{20,4},{24,8},{28,12},{1,17},{... | collective-permute-start | bytes 589832 | tf_op jit(solution)/shard_map/ppermute | solution.py:253
  7.1 1.5 %collective-permute-start.2 = (bf16[96,1024]{1,0:T(8,128)(2,1)S(1)}, bf16[96,1024]{1,0:T(8,128)(2,1)S(1)}, u32[]{:S(2)}, u32[]{:S(2)}) collective-permute-start(bf16[96,1024]{1,0:T(8,128)(2,1)S(1)} %get-tuple-element.53), channel_id=1, source_target_pairs={{0,8},{4,12},{8,0},{12,4},{16,24},{20,28},{24,16},{28,20},{1,9},{5... | collective-permute-start | bytes 589832 | tf_op jit(solution)/shard_map/ppermute | solution.py:253
  8.6 0.1 collective-permute-start.4
  8.6 3.7 %collective-permute-done.3.refs_2_ = bf16[96,1024]{1,0:T(8,128)(2,1)S(1)} collective-permute-done((bf16[96,1024]{1,0:T(8,128)(2,1)S(1)}, bf16[96,1024]{1,0:T(8,128)(2,1)S(1)}, u32[]{:S(2)}, u32[]{:S(2)}) %collective-permute-start.3) | collective-permute-done | bytes 196640 | tf_op jit(solution)/shard_map/ppermute | solution.py:253
  12.3 2.6 %collective-permute-done.2.refs_1_ = bf16[96,1024]{1,0:T(8,128)(2,1)S(1)} collective-permute-done((bf16[96,1024]{1,0:T(8,128)(2,1)S(1)}, bf16[96,1024]{1,0:T(8,128)(2,1)S(1)}, u32[]{:S(2)}, u32[]{:S(2)}) %collective-permute-start.2) | collective-permute-done | bytes 196640 | tf_op jit(solution)/shard_map/ppermute | solution.py:253
  14.9 2.9 %collective-permute-done.4.refs_3_ = bf16[96,1024]{1,0:T(8,128)(2,1)S(1)} collective-permute-done((bf16[96,1024]{1,0:T(8,128)(2,1)S(1)}, bf16[96,1024]{1,0:T(8,128)(2,1)S(1)}, u32[]{:S(2)}, u32[]{:S(2)}) %collective-permute-start.4) | collective-permute-done | bytes 196640 | tf_op jit(solution)/shard_map/ppermute | solution.py:253
  17.8 2.6 %forward.1 = (f32[96,768]{1,0:T(8,128)S(1)}, f32[96,768]{1,0:T(8,128)S(1)}, bf16[48,1024]{1,0:T(8,128)(2,1)S(1)}, bf16[48,1024]{1,0:T(8,128)(2,1)S(1)}, bf16[48,...) custom-call(bf16[96,1024]{1,0:T(8,128)(2,1)S(1)} %get-tuple-element.52.refs_0_, ...), custom_call_target="tpu_custom_call" | custom-call | flops 905969664 | bytes 11206656 | tf_op jit(solution)/shard_map/forward/pallas_call | solution.py:23
  20.3 1.7 %collective-permute-start.6 = (bf16[48,1024]{1,0:T(8,128)(2,1)S(1)}, bf16[48,1024]{1,0:T(8,128)(2,1)S(1)}, u32[]{:S(2)}, u32[]{:S(2)}) collective-permute-start(bf16[48,1024]{1,0:T(8,128)(2,1)S(1)} %get-tuple-element.56), channel_id=1, source_target_pairs={{0,16},{4,20},{8,24},{12,28},{16,0},{20,4},{24,8},{28,12},{1,17},{... | collective-permute-start | bytes 294920 | tf_op jit(solution)/shard_map/ppermute | solution.py:253
  22.1 1.4 %collective-permute-start.7 = (bf16[48,1024]{1,0:T(8,128)(2,1)S(1)}, bf16[48,1024]{1,0:T(8,128)(2,1)S(1)}, u32[]{:S(2)}, u32[]{:S(2)}) collective-permute-start(bf16[48,1024]{1,0:T(8,128)(2,1)S(1)} %get-tuple-element.57), channel_id=1, source_target_pairs={{0,24},{4,28},{8,16},{12,20},{16,8},{20,12},{24,0},{28,4},{1,25},{... | collective-permute-start | bytes 294920 | tf_op jit(solution)/shard_map/ppermute | solution.py:253
  23.5 0.4 collective-permute-start.5
  23.9 0.0 collective-permute-start.8
  23.9 2.2 %collective-permute-done.6.refs_2_ = bf16[48,1024]{1,0:T(8,128)(2,1)S(1)} collective-permute-done((bf16[48,1024]{1,0:T(8,128)(2,1)S(1)}, bf16[48,1024]{1,0:T(8,128)(2,1)S(1)}, u32[]{:S(2)}, u32[]{:S(2)}) %collective-permute-start.6) | collective-permute-done | bytes 98336 | tf_op jit(solution)/shard_map/ppermute | solution.py:253
  26.1 1.5 %collective-permute-done.7.refs_3_ = bf16[48,1024]{1,0:T(8,128)(2,1)S(1)} collective-permute-done((bf16[48,1024]{1,0:T(8,128)(2,1)S(1)}, bf16[48,1024]{1,0:T(8,128)(2,1)S(1)}, u32[]{:S(2)}, u32[]{:S(2)}) %collective-permute-start.7) | collective-permute-done | bytes 98336 | tf_op jit(solution)/shard_map/ppermute | solution.py:253
  27.6 0.5 collective-permute-done.5.refs_1_
  28.1 2.4 %backward.1 = (bf16[48,1024]{1,0:T(8,128)(2,1)S(1)}, bf16[48,1024]{1,0:T(8,128)(2,1)S(1)}, bf16[48,1024]{1,0:T(8,128)(2,1)S(1)}, bf16[48,1024]{1,0:T(8,128)(2,1)S(1)}) custom-call(bf16[96,1024]{1,0:T(8,128)(2,1)S(1)} %get-tuple-element.52.refs_0_, bf16[96,1024]{1,0:T(8,128)(2,1)S(1)} %collective-permute-done.2.refs_1_, ...), custom_call_target="tpu_custom_call" | custom-call | flops 905969664 | bytes 11206656 | tf_op jit(solution)/shard_map/backward/pallas_call | solution.py:23
  30.6 0.1 add_blocks.2.refs_0_
  30.7 1.5 %collective-permute-start.12 = (bf16[48,1024]{1,0:T(8,128)(2,1)S(1)}, bf16[48,1024]{1,0:T(8,128)(2,1)S(1)}, u32[]{:S(2)}, u32[]{:S(2)}) collective-permute-start(bf16[48,1024]{1,0:T(8,128)(2,1)S(1)} %get-tuple-element.77), channel_id=1, source_target_pairs={{0,8},{4,12},{8,0},{12,4},{16,24},{20,28},{24,16},{28,20},{1,9},{5... | collective-permute-start | bytes 294920 | tf_op jit(solution)/shard_map/ppermute | solution.py:253
  32.2 1.1 %collective-permute-start.13 = (bf16[48,1024]{1,0:T(8,128)(2,1)S(1)}, bf16[48,1024]{1,0:T(8,128)(2,1)S(1)}, u32[]{:S(2)}, u32[]{:S(2)}) collective-permute-start(bf16[48,1024]{1,0:T(8,128)(2,1)S(1)} %get-tuple-element.78), channel_id=1, source_target_pairs={{0,16},{4,20},{8,24},{12,28},{16,0},{20,4},{24,8},{28,12},{1,17},{... | collective-permute-start | bytes 294920 | tf_op jit(solution)/shard_map/ppermute | solution.py:253
  33.3 2.6 %collective-permute-start.19 = (bf16[192,512]{1,0:T(8,128)(2,1)S(1)}, bf16[192,512]{1,0:T(8,128)(2,1)S(1)}, u32[]{:S(2)}, u32[]{:S(2)}) collective-permute-start(bf16[192,512]{1,0:T(8,128)(2,1)S(1)} %add_blocks.2.refs_0_), channel_id=1, source_target_pairs={{0,2},{1,3},{2,0},{3,1},{4,6},{5,7},{6,4},{7,5},{8,10},{9,11},{10,... | collective-permute-start | bytes 589832 | tf_op jit(solution)/shard_map/ppermute | solution.py:284
  35.9 3.5 %collective-permute-start.20 = (bf16[192,512]{1,0:T(8,128)(2,1)S(1)}, bf16[192,512]{1,0:T(8,128)(2,1)S(1)}, u32[]{:S(2)}, u32[]{:S(2)}) collective-permute-start(bf16[192,512]{1,0:T(8,128)(2,1)S(1)} %add_blocks.2.refs_0_), channel_id=1, source_target_pairs={{0,1},{1,2},{2,3},{4,5},{5,6},{6,7},{8,9},{9,10},{10,11},{12,13},{... | collective-permute-start | bytes 589832 | tf_op jit(solution)/shard_map/ppermute | solution.py:285
  39.4 1.3 %collective-permute-start.21 = (bf16[192,512]{1,0:T(8,128)(2,1)S(1)}, bf16[192,512]{1,0:T(8,128)(2,1)S(1)}, u32[]{:S(2)}, u32[]{:S(2)}) collective-permute-start(bf16[192,512]{1,0:T(8,128)(2,1)S(1)} %add_blocks.2.refs_0_), channel_id=1, source_target_pairs={{1,0},{2,1},{3,2},{5,4},{6,5},{7,6},{9,8},{10,9},{11,10},{13,12},{... | collective-permute-start | bytes 589832 | tf_op jit(solution)/shard_map/ppermute | solution.py:286
  40.7 1.0 %collective-permute-start.14 = (bf16[48,1024]{1,0:T(8,128)(2,1)S(1)}, bf16[48,1024]{1,0:T(8,128)(2,1)S(1)}, u32[]{:S(2)}, u32[]{:S(2)}) collective-permute-start(bf16[48,1024]{1,0:T(8,128)(2,1)S(1)} %get-tuple-element.79), channel_id=1, source_target_pairs={{0,24},{4,28},{8,16},{12,20},{16,8},{20,12},{24,0},{28,4},{1,25},{... | collective-permute-start | bytes 294920 | tf_op jit(solution)/shard_map/ppermute | solution.py:253
  41.7 4.6 %collective-permute-done.14.refs_3_ = bf16[48,1024]{1,0:T(8,128)(2,1)S(1)} collective-permute-done((bf16[48,1024]{1,0:T(8,128)(2,1)S(1)}, bf16[48,1024]{1,0:T(8,128)(2,1)S(1)}, u32[]{:S(2)}, u32[]{:S(2)}) %collective-permute-start.14) | collective-permute-done | bytes 98336 | tf_op jit(solution)/shard_map/ppermute | solution.py:253
  46.3 0.5 collective-permute-start.17
  46.8 0.1 collective-permute-start.18
  46.9 1.3 %collective-permute-start.22 = (bf16[192,512]{1,0:T(8,128)(2,1)S(1)}, bf16[192,512]{1,0:T(8,128)(2,1)S(1)}, u32[]{:S(2)}, u32[]{:S(2)}) collective-permute-start(bf16[192,512]{1,0:T(8,128)(2,1)S(1)} %collective-permute-done.19.refs_1_), channel_id=1, source_target_pairs={{2,3},{1,0},{6,7},{5,4},{10,11},{9,8},{14,15},{13,12},{18,19},{17,... | collective-permute-start | bytes 589832 | tf_op jit(solution)/shard_map/ppermute | solution.py:287
  48.2 1.2 %collective-permute-done.21.refs_3_ = bf16[192,512]{1,0:T(8,128)(2,1)S(1)} collective-permute-done((bf16[192,512]{1,0:T(8,128)(2,1)S(1)}, bf16[192,512]{1,0:T(8,128)(2,1)S(1)}, u32[]{:S(2)}, u32[]{:S(2)}) %collective-permute-start.21) | collective-permute-done | bytes 196640 | tf_op jit(solution)/shard_map/ppermute | solution.py:286
  49.4 0.1 add_blocks.3.refs_0_
  49.5 2.1 %collective-permute-start.23 = (bf16[192,512]{1,0:T(8,128)(2,1)S(1)}, bf16[192,512]{1,0:T(8,128)(2,1)S(1)}, u32[]{:S(2)}, u32[]{:S(2)}) collective-permute-start(bf16[192,512]{1,0:T(8,128)(2,1)S(1)} %add_blocks.3.refs_0_), channel_id=1, source_target_pairs={{0,1},{1,2},{2,3},{3,0},{4,5},{5,6},{6,7},{7,4},{8,9},{9,10},{10,1... | collective-permute-start | bytes 589832 | tf_op jit(solution)/shard_map/ppermute | solution.py:278
  51.6 2.0 %collective-permute-start.24 = (bf16[192,512]{1,0:T(8,128)(2,1)S(1)}, bf16[192,512]{1,0:T(8,128)(2,1)S(1)}, u32[]{:S(2)}, u32[]{:S(2)}) collective-permute-start(bf16[192,512]{1,0:T(8,128)(2,1)S(1)} %add_blocks.3.refs_0_), channel_id=1, source_target_pairs={{0,2},{1,3},{2,0},{3,1},{4,6},{5,7},{6,4},{7,5},{8,10},{9,11},{10,... | collective-permute-start | bytes 589832 | tf_op jit(solution)/shard_map/ppermute | solution.py:278
  53.6 2.8 %collective-permute-start.25 = (bf16[192,512]{1,0:T(8,128)(2,1)S(1)}, bf16[192,512]{1,0:T(8,128)(2,1)S(1)}, u32[]{:S(2)}, u32[]{:S(2)}) collective-permute-start(bf16[192,512]{1,0:T(8,128)(2,1)S(1)} %add_blocks.3.refs_0_), channel_id=1, source_target_pairs={{0,3},{1,0},{2,1},{3,2},{4,7},{5,4},{6,5},{7,6},{8,11},{9,8},{10,9... | collective-permute-start | bytes 589832 | tf_op jit(solution)/shard_map/ppermute | solution.py:278
  56.4 0.3 weights.1.weight_ref
  56.8 4.9 %collective-permute-done.22.refs_4_ = bf16[192,512]{1,0:T(8,128)(2,1)S(1)} collective-permute-done((bf16[192,512]{1,0:T(8,128)(2,1)S(1)}, bf16[192,512]{1,0:T(8,128)(2,1)S(1)}, u32[]{:S(2)}, u32[]{:S(2)}) %collective-permute-start.22) | collective-permute-done | bytes 196640 | tf_op jit(solution)/shard_map/ppermute | solution.py:287
  61.7 1.7 %combine_gate.1 = (bf16[512,512]{1,0:T(8,128)(2,1)}, f32[8,512]{1,0:T(8,128)S(1)}) custom-call(bf16[512,768]{1,0:T(8,128)(2,1)S(1)} %weights.1.weight_ref, s32[8,512]{1,0:T(8,128)S(1)} %bitcast.5, f32[16,512]{1,0:T(8,128)S(1)} %number.1.key_ref, bf16[512,512]{1,0:T(8,128)(2,1)S(1)} %copy-done.3, bf16[192,512]{1,0:T(8,128)(2,1)S(1)} %add_blocks.2.refs_0_, ...), custom_call_target="tpu_custom_call" | custom-call | bytes 2883584 | tf_op jit(solution)/shard_map/combine_gate/pallas_call | solution.py:23
  63.4 1.0 %collective-permute-start.27 = (f32[8,512]{1,0:T(8,128)S(1)}, f32[8,512]{1,0:T(8,128)S(1)}, u32[]{:S(2)}, u32[]{:S(2)}) collective-permute-start(f32[8,512]{1,0:T(8,128)S(1)} %get-tuple-element.98.refs_4_), channel_id=1, source_target_pairs={{0,8},{4,12},{8,0},{12,4},{1,9},{5,13},{9,1},{13,5},{2,10},{6,14},... | collective-permute-start | bytes 49160 | tf_op jit(solution)/shard_map/ppermute | solution.py:357
  64.4 1.4 %collective-permute-start.28 = (f32[8,512]{1,0:T(8,128)S(1)}, f32[8,512]{1,0:T(8,128)S(1)}, u32[]{:S(2)}, u32[]{:S(2)}) collective-permute-start(f32[8,512]{1,0:T(8,128)S(1)} %get-tuple-element.98.refs_4_), channel_id=1, source_target_pairs={{0,12},{4,0},{8,4},{12,8},{1,13},{5,1},{9,5},{13,9},{2,14},{6,2},{... | collective-permute-start | bytes 49160 | tf_op jit(solution)/shard_map/ppermute | solution.py:357
  65.8 0.7 collective-permute-done.24.refs_2_
  66.5 2.6 %collective-permute-done.25.refs_3_ = bf16[192,512]{1,0:T(8,128)(2,1)S(1)} collective-permute-done((bf16[192,512]{1,0:T(8,128)(2,1)S(1)}, bf16[192,512]{1,0:T(8,128)(2,1)S(1)}, u32[]{:S(2)}, u32[]{:S(2)}) %collective-permute-start.25) | collective-permute-done | bytes 196640 | tf_op jit(solution)/shard_map/ppermute | solution.py:278
  69.1 1.4 %combine.1 = (bf16[512,512]{1,0:T(8,128)(2,1)}, f32[8,512]{1,0:T(8,128)}) custom-call(bf16[512,768]{1,0:T(8,128)(2,1)S(1)} %weights.1.weight_ref, bf16[192,512]{1,0:T(8,128)(2,1)S(1)} %add_blocks.3.refs_0_, bf16[192,512]{1,0:T(8,128)(2,1)S(1)} %collective-permute-done.23.refs_1_, bf16[192,512]{1,0:T(8,128)(2,1)S(1)} %collective-permute-done.24.refs_2_, ...), custom_call_target="tpu_custom_call" | custom-call | flops 402653184 | bytes 2179072 | tf_op jit(solution)/shard_map/combine/pallas_call | solution.py:23
  (35 shorter events, 0.1 us)
Async XLA Ops:
  0.6 2.3 %collective-permute-start = (bf16[512,512]{1,0:T(8,128)(2,1)}, bf16[512,512]{1,0:T(8,128)(2,1)S(1)}, u32[]{:S(2)}, u32[]{:S(2)}) collective-permute-start(bf16[512,512]{1,0:T(8,128)(2,1)} %refs_0_.1), channel_id=1, source_target_pairs={{0,4},{4,0},{8,12},{12,8},{1,5},{5,1},{9,13},{13,9},{2,6},{6,2},{1... | collective-permute-start | bytes 1572872 | tf_op jit(solution)/shard_map/ppermute | solution.py:243
  1.1 2.5 %collective-permute-start.1 = (bf16[512,512]{1,0:T(8,128)(2,1)}, bf16[512,512]{1,0:T(8,128)(2,1)S(1)}, u32[]{:S(2)}, u32[]{:S(2)}) collective-permute-start(bf16[512,512]{1,0:T(8,128)(2,1)} %grads_ref.1), channel_id=1, source_target_pairs={{0,4},{4,0},{8,12},{12,8},{1,5},{5,1},{9,13},{13,9},{2,6},{6,2},{1... | collective-permute-start | bytes 1572872 | tf_op jit(solution)/shard_map/ppermute | solution.py:243
  1.2 0.7 %copy-start.4 = (s32[512,8]{0,1:T(8,128)S(1)}, s32[512,8]{0,1:T(8,128)}, u32[]{:S(2)}) copy-start(s32[512,8]{0,1:T(8,128)} %param.9) | copy-start | bytes 49156
  1.9 1.7 %copy-start.3 = (bf16[512,512]{1,0:T(8,128)(2,1)S(1)}, bf16[512,512]{1,0:T(8,128)(2,1)}, u32[]{:S(2)}) copy-start(bf16[512,512]{1,0:T(8,128)(2,1)} %grads_ref.1) | copy-start | bytes 1572868
  1.9 1.7 %copy-start.7 = (bf16[512,512]{1,0:T(8,128)(2,1)S(1)}, bf16[512,512]{1,0:T(8,128)(2,1)}, u32[]{:S(2)}) copy-start(bf16[512,512]{1,0:T(8,128)(2,1)} %refs_0_.1) | copy-start | bytes 1572868
  2.1 15.6 %copy-start = (bf16[1,768,2048]{2,1,0:T(8,128)(2,1)S(1)}, bf16[1,768,2048]{2,1,0:T(8,128)(2,1)}, u32[]{:S(2)}) copy-start(bf16[1,768,2048]{2,1,0:T(8,128)(2,1)} %refs_4_.3) | copy-start | bytes 9437188
  2.1 15.6 %copy-start.1 = (bf16[1,768,2048]{2,1,0:T(8,128)(2,1)S(1)}, bf16[1,768,2048]{2,1,0:T(8,128)(2,1)}, u32[]{:S(2)}) copy-start(bf16[1,768,2048]{2,1,0:T(8,128)(2,1)} %refs_5_.3) | copy-start | bytes 9437188
  2.1 15.6 %copy-start.2 = (bf16[1,768,2048]{2,1,0:T(8,128)(2,1)S(1)}, bf16[1,768,2048]{2,1,0:T(8,128)(2,1)}, u32[]{:S(2)}) copy-start(bf16[1,768,2048]{2,1,0:T(8,128)(2,1)} %refs_6_.3) | copy-start | bytes 9437188
  4.1 8.2 %collective-permute-start.3 = (bf16[96,1024]{1,0:T(8,128)(2,1)S(1)}, bf16[96,1024]{1,0:T(8,128)(2,1)S(1)}, u32[]{:S(2)}, u32[]{:S(2)}) collective-permute-start(bf16[96,1024]{1,0:T(8,128)(2,1)S(1)} %get-tuple-element.52.refs_0_), channel_id=1, source_target_pairs={{0,16},{4,20},{8,24},{12,28},{16,0},{20,4},{24,8},{28,12},{1,17},{... | collective-permute-start | bytes 589832 | tf_op jit(solution)/shard_map/ppermute | solution.py:253
  7.1 7.8 %collective-permute-start.2 = (bf16[96,1024]{1,0:T(8,128)(2,1)S(1)}, bf16[96,1024]{1,0:T(8,128)(2,1)S(1)}, u32[]{:S(2)}, u32[]{:S(2)}) collective-permute-start(bf16[96,1024]{1,0:T(8,128)(2,1)S(1)} %get-tuple-element.53), channel_id=1, source_target_pairs={{0,8},{4,12},{8,0},{12,4},{16,24},{20,28},{24,16},{28,20},{1,9},{5... | collective-permute-start | bytes 589832 | tf_op jit(solution)/shard_map/ppermute | solution.py:253
  8.6 9.2 %collective-permute-start.4 = (bf16[96,1024]{1,0:T(8,128)(2,1)S(1)}, bf16[96,1024]{1,0:T(8,128)(2,1)S(1)}, u32[]{:S(2)}, u32[]{:S(2)}) collective-permute-start(bf16[96,1024]{1,0:T(8,128)(2,1)S(1)} %get-tuple-element.53), channel_id=1, source_target_pairs={{0,24},{4,28},{8,16},{12,20},{16,8},{20,12},{24,0},{28,4},{1,25},{... | collective-permute-start | bytes 589832 | tf_op jit(solution)/shard_map/ppermute | solution.py:253
  20.3 5.7 %collective-permute-start.6 = (bf16[48,1024]{1,0:T(8,128)(2,1)S(1)}, bf16[48,1024]{1,0:T(8,128)(2,1)S(1)}, u32[]{:S(2)}, u32[]{:S(2)}) collective-permute-start(bf16[48,1024]{1,0:T(8,128)(2,1)S(1)} %get-tuple-element.56), channel_id=1, source_target_pairs={{0,16},{4,20},{8,24},{12,28},{16,0},{20,4},{24,8},{28,12},{1,17},{... | collective-permute-start | bytes 294920 | tf_op jit(solution)/shard_map/ppermute | solution.py:253
  22.1 5.5 %collective-permute-start.7 = (bf16[48,1024]{1,0:T(8,128)(2,1)S(1)}, bf16[48,1024]{1,0:T(8,128)(2,1)S(1)}, u32[]{:S(2)}, u32[]{:S(2)}) collective-permute-start(bf16[48,1024]{1,0:T(8,128)(2,1)S(1)} %get-tuple-element.57), channel_id=1, source_target_pairs={{0,24},{4,28},{8,16},{12,20},{16,8},{20,12},{24,0},{28,4},{1,25},{... | collective-permute-start | bytes 294920 | tf_op jit(solution)/shard_map/ppermute | solution.py:253
  23.5 4.6 %collective-permute-start.5 = (bf16[48,1024]{1,0:T(8,128)(2,1)S(1)}, bf16[48,1024]{1,0:T(8,128)(2,1)S(1)}, u32[]{:S(2)}, u32[]{:S(2)}) collective-permute-start(bf16[48,1024]{1,0:T(8,128)(2,1)S(1)} %get-tuple-element.55), channel_id=1, source_target_pairs={{0,8},{4,12},{8,0},{12,4},{16,24},{20,28},{24,16},{28,20},{1,9},{5... | collective-permute-start | bytes 294920 | tf_op jit(solution)/shard_map/ppermute | solution.py:253
  23.9 6.7 %collective-permute-start.8 = (bf16[48,1024]{1,0:T(8,128)(2,1)S(1)}, bf16[48,1024]{1,0:T(8,128)(2,1)S(1)}, u32[]{:S(2)}, u32[]{:S(2)}) collective-permute-start(bf16[48,1024]{1,0:T(8,128)(2,1)S(1)} %get-tuple-element.64.refs_0_), channel_id=1, source_target_pairs={{0,4},{4,0},{8,12},{12,8},{1,5},{5,1},{9,13},{13,9},{2,6},{6,2},{1... | collective-permute-start | bytes 294920 | tf_op jit(solution)/shard_map/ppermute | solution.py:243
  26.1 4.5 %collective-permute-start.10 = (bf16[48,1024]{1,0:T(8,128)(2,1)S(1)}, bf16[48,1024]{1,0:T(8,128)(2,1)S(1)}, u32[]{:S(2)}, u32[]{:S(2)}) collective-permute-start(bf16[48,1024]{1,0:T(8,128)(2,1)S(1)} %collective-permute-done.6.refs_2_), channel_id=1, source_target_pairs={{0,4},{4,0},{8,12},{12,8},{1,5},{5,1},{9,13},{13,9},{2,6},{6,2},{1... | collective-permute-start | bytes 294920 | tf_op jit(solution)/shard_map/ppermute | solution.py:243
  27.6 3.0 %collective-permute-start.11 = (bf16[48,1024]{1,0:T(8,128)(2,1)S(1)}, bf16[48,1024]{1,0:T(8,128)(2,1)S(1)}, u32[]{:S(2)}, u32[]{:S(2)}) collective-permute-start(bf16[48,1024]{1,0:T(8,128)(2,1)S(1)} %collective-permute-done.7.refs_3_), channel_id=1, source_target_pairs={{0,4},{4,0},{8,12},{12,8},{1,5},{5,1},{9,13},{13,9},{2,6},{6,2},{1... | collective-permute-start | bytes 294920 | tf_op jit(solution)/shard_map/ppermute | solution.py:243
  28.1 2.5 %collective-permute-start.9 = (bf16[48,1024]{1,0:T(8,128)(2,1)S(1)}, bf16[48,1024]{1,0:T(8,128)(2,1)S(1)}, u32[]{:S(2)}, u32[]{:S(2)}) collective-permute-start(bf16[48,1024]{1,0:T(8,128)(2,1)S(1)} %collective-permute-done.5.refs_1_), channel_id=1, source_target_pairs={{0,4},{4,0},{8,12},{12,8},{1,5},{5,1},{9,13},{13,9},{2,6},{6,2},{1... | collective-permute-start | bytes 294920 | tf_op jit(solution)/shard_map/ppermute | solution.py:243
  28.1 28.3 %copy-start.5 = (s32[512,8]{0,1:T(8,128)S(1)}, s32[512,8]{0,1:T(8,128)}, u32[]{:S(2)}) copy-start(s32[512,8]{0,1:T(8,128)} %param.9) | copy-start | bytes 49156
  28.1 28.3 %copy-start.6 = (f32[512,8]{0,1:T(8,128)S(1)}, f32[512,8]{0,1:T(8,128)}, u32[]{:S(2)}) copy-start(f32[512,8]{0,1:T(8,128)} %param.10) | copy-start | bytes 49156
  30.7 10.0 %collective-permute-start.12 = (bf16[48,1024]{1,0:T(8,128)(2,1)S(1)}, bf16[48,1024]{1,0:T(8,128)(2,1)S(1)}, u32[]{:S(2)}, u32[]{:S(2)}) collective-permute-start(bf16[48,1024]{1,0:T(8,128)(2,1)S(1)} %get-tuple-element.77), channel_id=1, source_target_pairs={{0,8},{4,12},{8,0},{12,4},{16,24},{20,28},{24,16},{28,20},{1,9},{5... | collective-permute-start | bytes 294920 | tf_op jit(solution)/shard_map/ppermute | solution.py:253
  32.2 9.5 %collective-permute-start.13 = (bf16[48,1024]{1,0:T(8,128)(2,1)S(1)}, bf16[48,1024]{1,0:T(8,128)(2,1)S(1)}, u32[]{:S(2)}, u32[]{:S(2)}) collective-permute-start(bf16[48,1024]{1,0:T(8,128)(2,1)S(1)} %get-tuple-element.78), channel_id=1, source_target_pairs={{0,16},{4,20},{8,24},{12,28},{16,0},{20,4},{24,8},{28,12},{1,17},{... | collective-permute-start | bytes 294920 | tf_op jit(solution)/shard_map/ppermute | solution.py:253
  33.3 13.5 %collective-permute-start.19 = (bf16[192,512]{1,0:T(8,128)(2,1)S(1)}, bf16[192,512]{1,0:T(8,128)(2,1)S(1)}, u32[]{:S(2)}, u32[]{:S(2)}) collective-permute-start(bf16[192,512]{1,0:T(8,128)(2,1)S(1)} %add_blocks.2.refs_0_), channel_id=1, source_target_pairs={{0,2},{1,3},{2,0},{3,1},{4,6},{5,7},{6,4},{7,5},{8,10},{9,11},{10,... | collective-permute-start | bytes 589832 | tf_op jit(solution)/shard_map/ppermute | solution.py:284
  35.9 11.0 %collective-permute-start.20 = (bf16[192,512]{1,0:T(8,128)(2,1)S(1)}, bf16[192,512]{1,0:T(8,128)(2,1)S(1)}, u32[]{:S(2)}, u32[]{:S(2)}) collective-permute-start(bf16[192,512]{1,0:T(8,128)(2,1)S(1)} %add_blocks.2.refs_0_), channel_id=1, source_target_pairs={{0,1},{1,2},{2,3},{4,5},{5,6},{6,7},{8,9},{9,10},{10,11},{12,13},{... | collective-permute-start | bytes 589832 | tf_op jit(solution)/shard_map/ppermute | solution.py:285
  39.4 10.0 %collective-permute-start.21 = (bf16[192,512]{1,0:T(8,128)(2,1)S(1)}, bf16[192,512]{1,0:T(8,128)(2,1)S(1)}, u32[]{:S(2)}, u32[]{:S(2)}) collective-permute-start(bf16[192,512]{1,0:T(8,128)(2,1)S(1)} %add_blocks.2.refs_0_), channel_id=1, source_target_pairs={{1,0},{2,1},{3,2},{5,4},{6,5},{7,6},{9,8},{10,9},{11,10},{13,12},{... | collective-permute-start | bytes 589832 | tf_op jit(solution)/shard_map/ppermute | solution.py:286
  40.7 5.6 %collective-permute-start.14 = (bf16[48,1024]{1,0:T(8,128)(2,1)S(1)}, bf16[48,1024]{1,0:T(8,128)(2,1)S(1)}, u32[]{:S(2)}, u32[]{:S(2)}) collective-permute-start(bf16[48,1024]{1,0:T(8,128)(2,1)S(1)} %get-tuple-element.79), channel_id=1, source_target_pairs={{0,24},{4,28},{8,16},{12,20},{16,8},{20,12},{24,0},{28,4},{1,25},{... | collective-permute-start | bytes 294920 | tf_op jit(solution)/shard_map/ppermute | solution.py:253
  41.7 4.6 %collective-permute-start.15 = (bf16[48,1024]{1,0:T(8,128)(2,1)S(1)}, bf16[48,1024]{1,0:T(8,128)(2,1)S(1)}, u32[]{:S(2)}, u32[]{:S(2)}) collective-permute-start(bf16[48,1024]{1,0:T(8,128)(2,1)S(1)} %get-tuple-element.81.refs_0_), channel_id=1, source_target_pairs={{0,4},{4,0},{8,12},{12,8},{1,5},{5,1},{9,13},{13,9},{2,6},{6,2},{1... | collective-permute-start | bytes 294920 | tf_op jit(solution)/shard_map/ppermute | solution.py:243
  46.3 3.1 %collective-permute-start.16 = (bf16[48,1024]{1,0:T(8,128)(2,1)S(1)}, bf16[48,1024]{1,0:T(8,128)(2,1)S(1)}, u32[]{:S(2)}, u32[]{:S(2)}) collective-permute-start(bf16[48,1024]{1,0:T(8,128)(2,1)S(1)} %collective-permute-done.12.refs_1_), channel_id=1, source_target_pairs={{0,4},{4,0},{8,12},{12,8},{1,5},{5,1},{9,13},{13,9},{2,6},{6,2},{1... | collective-permute-start | bytes 294920 | tf_op jit(solution)/shard_map/ppermute | solution.py:243
  46.3 3.1 %collective-permute-start.17 = (bf16[48,1024]{1,0:T(8,128)(2,1)S(1)}, bf16[48,1024]{1,0:T(8,128)(2,1)S(1)}, u32[]{:S(2)}, u32[]{:S(2)}) collective-permute-start(bf16[48,1024]{1,0:T(8,128)(2,1)S(1)} %collective-permute-done.13.refs_2_), channel_id=1, source_target_pairs={{0,4},{4,0},{8,12},{12,8},{1,5},{5,1},{9,13},{13,9},{2,6},{6,2},{1... | collective-permute-start | bytes 294920 | tf_op jit(solution)/shard_map/ppermute | solution.py:243
  46.8 2.6 %collective-permute-start.18 = (bf16[48,1024]{1,0:T(8,128)(2,1)S(1)}, bf16[48,1024]{1,0:T(8,128)(2,1)S(1)}, u32[]{:S(2)}, u32[]{:S(2)}) collective-permute-start(bf16[48,1024]{1,0:T(8,128)(2,1)S(1)} %collective-permute-done.14.refs_3_), channel_id=1, source_target_pairs={{0,4},{4,0},{8,12},{12,8},{1,5},{5,1},{9,13},{13,9},{2,6},{6,2},{1... | collective-permute-start | bytes 294920 | tf_op jit(solution)/shard_map/ppermute | solution.py:243
  46.9 14.8 %collective-permute-start.22 = (bf16[192,512]{1,0:T(8,128)(2,1)S(1)}, bf16[192,512]{1,0:T(8,128)(2,1)S(1)}, u32[]{:S(2)}, u32[]{:S(2)}) collective-permute-start(bf16[192,512]{1,0:T(8,128)(2,1)S(1)} %collective-permute-done.19.refs_1_), channel_id=1, source_target_pairs={{2,3},{1,0},{6,7},{5,4},{10,11},{9,8},{14,15},{13,12},{18,19},{17,... | collective-permute-start | bytes 589832 | tf_op jit(solution)/shard_map/ppermute | solution.py:287
  49.5 14.9 %collective-permute-start.23 = (bf16[192,512]{1,0:T(8,128)(2,1)S(1)}, bf16[192,512]{1,0:T(8,128)(2,1)S(1)}, u32[]{:S(2)}, u32[]{:S(2)}) collective-permute-start(bf16[192,512]{1,0:T(8,128)(2,1)S(1)} %add_blocks.3.refs_0_), channel_id=1, source_target_pairs={{0,1},{1,2},{2,3},{3,0},{4,5},{5,6},{6,7},{7,4},{8,9},{9,10},{10,1... | collective-permute-start | bytes 589832 | tf_op jit(solution)/shard_map/ppermute | solution.py:278
  51.6 14.9 %collective-permute-start.24 = (bf16[192,512]{1,0:T(8,128)(2,1)S(1)}, bf16[192,512]{1,0:T(8,128)(2,1)S(1)}, u32[]{:S(2)}, u32[]{:S(2)}) collective-permute-start(bf16[192,512]{1,0:T(8,128)(2,1)S(1)} %add_blocks.3.refs_0_), channel_id=1, source_target_pairs={{0,2},{1,3},{2,0},{3,1},{4,6},{5,7},{6,4},{7,5},{8,10},{9,11},{10,... | collective-permute-start | bytes 589832 | tf_op jit(solution)/shard_map/ppermute | solution.py:278
  53.6 15.5 %collective-permute-start.25 = (bf16[192,512]{1,0:T(8,128)(2,1)S(1)}, bf16[192,512]{1,0:T(8,128)(2,1)S(1)}, u32[]{:S(2)}, u32[]{:S(2)}) collective-permute-start(bf16[192,512]{1,0:T(8,128)(2,1)S(1)} %add_blocks.3.refs_0_), channel_id=1, source_target_pairs={{0,3},{1,0},{2,1},{3,2},{4,7},{5,4},{6,5},{7,6},{8,11},{9,8},{10,9... | collective-permute-start | bytes 589832 | tf_op jit(solution)/shard_map/ppermute | solution.py:278
  63.4 5.7 %collective-permute-start.26 = (f32[8,512]{1,0:T(8,128)S(1)}, f32[8,512]{1,0:T(8,128)S(1)}, u32[]{:S(2)}, u32[]{:S(2)}) collective-permute-start(f32[8,512]{1,0:T(8,128)S(1)} %get-tuple-element.98.refs_4_), channel_id=1, source_target_pairs={{0,4},{4,8},{8,12},{12,0},{1,5},{5,9},{9,13},{13,1},{2,6},{6,10},{... | collective-permute-start | bytes 49160 | tf_op jit(solution)/shard_map/ppermute | solution.py:357
  63.4 5.7 %collective-permute-start.27 = (f32[8,512]{1,0:T(8,128)S(1)}, f32[8,512]{1,0:T(8,128)S(1)}, u32[]{:S(2)}, u32[]{:S(2)}) collective-permute-start(f32[8,512]{1,0:T(8,128)S(1)} %get-tuple-element.98.refs_4_), channel_id=1, source_target_pairs={{0,8},{4,12},{8,0},{12,4},{1,9},{5,13},{9,1},{13,5},{2,10},{6,14},... | collective-permute-start | bytes 49160 | tf_op jit(solution)/shard_map/ppermute | solution.py:357
  64.4 4.7 %collective-permute-start.28 = (f32[8,512]{1,0:T(8,128)S(1)}, f32[8,512]{1,0:T(8,128)S(1)}, u32[]{:S(2)}, u32[]{:S(2)}) collective-permute-start(f32[8,512]{1,0:T(8,128)S(1)} %get-tuple-element.98.refs_4_), channel_id=1, source_target_pairs={{0,12},{4,0},{8,4},{12,8},{1,13},{5,1},{9,5},{13,9},{2,14},{6,2},{... | collective-permute-start | bytes 49160 | tf_op jit(solution)/shard_map/ppermute | solution.py:357

commit v8 on v7

--- a/solution.py
+++ b/solution.py
@@ -261,7 +261,10 @@
 
     def give_back(pieces):
         arrived = {index: to_chip(pieces[index], *hops[index]) for index in order}
-        return [to_core(arrived[index], dc) for dc in range(cores) for index in range(count)]
+        return [arrived[index] for index in range(count)]
+
+    def swap(pieces):
+        return [to_core(piece, dc) for dc in range(cores) for piece in pieces]
 
     def add_blocks(pieces):
         return call(
@@ -321,12 +324,12 @@
         limit=24,
     )
     out_pieces, backs = after(out_pieces, backs)
-    out_rows = add_blocks(out_pieces)
+    out_rows = add_blocks(swap(out_pieces))
     out_rows, backs = after(out_rows, backs)
     out_parts = along(out_rows)
     back_pieces = give_back(backs)
     back_pieces, out_parts[1:4] = after(back_pieces, out_parts[1:4])
-    back_rows = add_blocks(back_pieces)
+    back_rows = add_blocks(swap(back_pieces))
     back_parts = across(back_rows)
     _, out_parts = after(back_rows, out_parts)
 

time: 70.8 us -> 72.5 us (1.024)
  waiting for transfers between devices: 28.9 us -> 30.8 us
  starting transfers between devices: 30.9 us -> 30.1 us
    ppermute x3, waiting for transfers between devices: 0.01 us -> 3.07 us  [body(): gate_parts.append(lax.ppermute(gate_part, 'tensor', pairs))]
    ppermute x3, waiting for transfers between devices: 3.27 us -> 0.59 us  [across(): lax.ppermute(value, 'expert', [(z, (z + dz) % columns) for z in range(col...]
    ppermute x9, waiting for transfers between devices: 17.9 us -> 15.3 us  [to_chip(): return lax.ppermute(value, ('dp', 'tensor'), pairs)]
    ppermute x1, waiting for transfers between devices: 4.93 us -> 7.07 us  [along(): ends = lax.ppermute(far, 'expert', [(2, 3), (1, 0)])]
    ppermute x10, starting transfers between devices: 1.19 us -> 2.64 us  [to_core(): return lax.ppermute(value, 'tensor', pairs)]
    ppermute x3, starting transfers between devices: 6.93 us -> 5.62 us  [across(): lax.ppermute(value, 'expert', [(z, (z + dz) % columns) for z in range(col...]
    ppermute x1, waiting for transfers between devices: 1.23 us -> 2.35 us  [along(): lax.ppermute(value, 'expert', [(z + 1, z) for z in range(columns - 1)])]
    ppermute x10, waiting for transfers between devices: 1.54 us -> 2.47 us  [to_core(): return lax.ppermute(value, 'tensor', pairs)]
  transfers between devices with their start and end apart: 29 -> 29, of which waited for: 13 -> 18; matrix products, arithmetic and copies ran while one was open for 0% -> 0% of each run, Pallas kernels for 7% -> 7%
where the time goes in v8:
time: 72.5 us; the launch traced here: 71.6 us
  waiting for transfers between devices  30.8 us (42%)
  starting transfers between devices  30.1 us (42%)
  Pallas kernels  9.14 us (13%)
  between operations  0.78 us (1%)
  local copies, waits for them, and re-layouts  0.75 us (1%)
    ppermute x9, waiting for transfers between devices, to_chip(): return lax.ppermute(value, ('dp', 'tensor'), pairs)  15.3 us
    ppermute x9, starting transfers between devices, to_chip(): return lax.ppermute(value, ('dp', 'tensor'), pairs)  11.7 us
    pallas_call x9, Pallas kernels, call(): pl.pallas_call(kernel, out_shape=out_shape, in_specs=[spec] * len(operand...  9.14 us
    ppermute x1, waiting for transfers between devices, along(): ends = lax.ppermute(far, 'expert', [(2, 3), (1, 0)])  7.07 us
    ppermute x3, starting transfers between devices, across(): lax.ppermute(value, 'expert', [(z, (z + dz) % columns) for z in range(col...  5.62 us
    ppermute x1, starting transfers between devices, along(): up = lax.ppermute(value, 'expert', [(z, z + 1) for z in range(columns - 1)])  3.48 us
    ppermute x3, waiting for transfers between devices, body(): gate_parts.append(lax.ppermute(gate_part, 'tensor', pairs))  3.07 us
    ppermute x10, starting transfers between devices, to_core(): return lax.ppermute(value, 'tensor', pairs)  2.64 us
  transfers between devices with their start and end apart: 29, of which 18 were waited for; matrix products, arithmetic and copies ran while one was open for 0% of the time, Pallas kernels for 7%

profile of v8, /device:TPU:0, one launch (start us, length us, event | category | flops | bytes accessed | tf_op | source)
XLA Modules:
  0.0 71.6 jit_solution(10193313491703787968)
XLA Ops:
  0.6 0.5 collective-permute-start
  1.1 0.1 collective-permute-start.1
  1.2 0.7 copy-done.4
  1.9 0.1 number.1.key_ref
  2.1 0.8 %collective-permute-done.refs_1_ = bf16[512,512]{1,0:T(8,128)(2,1)S(1)} collective-permute-done((bf16[512,512]{1,0:T(8,128)(2,1)}, bf16[512,512]{1,0:T(8,128)(2,1)S(1)}, u32[]{:S(2)}, u32[]{:S(2)}) %collective-permute-start) | collective-permute-done | bytes 524320 | tf_op jit(solution)/shard_map/ppermute | solution.py:243
  2.9 0.7 %collective-permute-done.1.refs_3_ = bf16[512,512]{1,0:T(8,128)(2,1)S(1)} collective-permute-done((bf16[512,512]{1,0:T(8,128)(2,1)}, bf16[512,512]{1,0:T(8,128)(2,1)S(1)}, u32[]{:S(2)}, u32[]{:S(2)}) %collective-permute-start.1) | collective-permute-done | bytes 524320 | tf_op jit(solution)/shard_map/ppermute | solution.py:243
  3.7 0.5 pick.1
  4.1 3.0 %collective-permute-start.3 = (bf16[96,1024]{1,0:T(8,128)(2,1)S(1)}, bf16[96,1024]{1,0:T(8,128)(2,1)S(1)}, u32[]{:S(2)}, u32[]{:S(2)}) collective-permute-start(bf16[96,1024]{1,0:T(8,128)(2,1)S(1)} %get-tuple-element.44.refs_0_), channel_id=1, source_target_pairs={{0,16},{4,20},{8,24},{12,28},{16,0},{20,4},{24,8},{28,12},{1,17},{... | collective-permute-start | bytes 589832 | tf_op jit(solution)/shard_map/ppermute | solution.py:253
  7.1 1.5 %collective-permute-start.2 = (bf16[96,1024]{1,0:T(8,128)(2,1)S(1)}, bf16[96,1024]{1,0:T(8,128)(2,1)S(1)}, u32[]{:S(2)}, u32[]{:S(2)}) collective-permute-start(bf16[96,1024]{1,0:T(8,128)(2,1)S(1)} %get-tuple-element.45), channel_id=1, source_target_pairs={{0,8},{4,12},{8,0},{12,4},{16,24},{20,28},{24,16},{28,20},{1,9},{5... | collective-permute-start | bytes 589832 | tf_op jit(solution)/shard_map/ppermute | solution.py:253
  8.6 3.7 %collective-permute-done.3.refs_2_ = bf16[96,1024]{1,0:T(8,128)(2,1)S(1)} collective-permute-done((bf16[96,1024]{1,0:T(8,128)(2,1)S(1)}, bf16[96,1024]{1,0:T(8,128)(2,1)S(1)}, u32[]{:S(2)}, u32[]{:S(2)}) %collective-permute-start.3) | collective-permute-done | bytes 196640 | tf_op jit(solution)/shard_map/ppermute | solution.py:253
  12.3 2.6 %collective-permute-done.2.refs_1_ = bf16[96,1024]{1,0:T(8,128)(2,1)S(1)} collective-permute-done((bf16[96,1024]{1,0:T(8,128)(2,1)S(1)}, bf16[96,1024]{1,0:T(8,128)(2,1)S(1)}, u32[]{:S(2)}, u32[]{:S(2)}) %collective-permute-start.2) | collective-permute-done | bytes 196640 | tf_op jit(solution)/shard_map/ppermute | solution.py:253
  14.9 2.9 %collective-permute-done.4.refs_3_ = bf16[96,1024]{1,0:T(8,128)(2,1)S(1)} collective-permute-done((bf16[96,1024]{1,0:T(8,128)(2,1)S(1)}, bf16[96,1024]{1,0:T(8,128)(2,1)S(1)}, u32[]{:S(2)}, u32[]{:S(2)}) %collective-permute-start.4) | collective-permute-done | bytes 196640 | tf_op jit(solution)/shard_map/ppermute | solution.py:253
  17.8 2.6 %forward.1 = (f32[96,768]{1,0:T(8,128)S(1)}, f32[96,768]{1,0:T(8,128)S(1)}, bf16[48,1024]{1,0:T(8,128)(2,1)S(1)}, bf16[48,1024]{1,0:T(8,128)(2,1)S(1)}, bf16[48,...) custom-call(bf16[96,1024]{1,0:T(8,128)(2,1)S(1)} %get-tuple-element.44.refs_0_, ...), custom_call_target="tpu_custom_call" | custom-call | flops 905969664 | bytes 11206656 | tf_op jit(solution)/shard_map/forward/pallas_call | solution.py:23
  20.3 1.7 %collective-permute-start.5 = (bf16[48,1024]{1,0:T(8,128)(2,1)S(1)}, bf16[48,1024]{1,0:T(8,128)(2,1)S(1)}, u32[]{:S(2)}, u32[]{:S(2)}) collective-permute-start(bf16[48,1024]{1,0:T(8,128)(2,1)S(1)} %get-tuple-element.47), channel_id=1, source_target_pairs={{0,8},{4,12},{8,0},{12,4},{16,24},{20,28},{24,16},{28,20},{1,9},{5... | collective-permute-start | bytes 294920 | tf_op jit(solution)/shard_map/ppermute | solution.py:253
  22.0 1.5 %collective-permute-start.6 = (bf16[48,1024]{1,0:T(8,128)(2,1)S(1)}, bf16[48,1024]{1,0:T(8,128)(2,1)S(1)}, u32[]{:S(2)}, u32[]{:S(2)}) collective-permute-start(bf16[48,1024]{1,0:T(8,128)(2,1)S(1)} %get-tuple-element.48), channel_id=1, source_target_pairs={{0,16},{4,20},{8,24},{12,28},{16,0},{20,4},{24,8},{28,12},{1,17},{... | collective-permute-start | bytes 294920 | tf_op jit(solution)/shard_map/ppermute | solution.py:253
  23.6 0.3 collective-permute-start.7
  23.9 2.4 %backward.1 = (bf16[48,1024]{1,0:T(8,128)(2,1)S(1)}, bf16[48,1024]{1,0:T(8,128)(2,1)S(1)}, bf16[48,1024]{1,0:T(8,128)(2,1)S(1)}, bf16[48,1024]{1,0:T(8,128)(2,1)S(1)}) custom-call(bf16[96,1024]{1,0:T(8,128)(2,1)S(1)} %get-tuple-element.44.refs_0_, bf16[96,1024]{1,0:T(8,128)(2,1)S(1)} %collective-permute-done.2.refs_1_, ...), custom_call_target="tpu_custom_call" | custom-call | flops 905969664 | bytes 11206656 | tf_op jit(solution)/shard_map/backward/pallas_call | solution.py:23
  26.4 1.3 %collective-permute-done.6.refs_2_ = bf16[48,1024]{1,0:T(8,128)(2,1)S(1)} collective-permute-done((bf16[48,1024]{1,0:T(8,128)(2,1)S(1)}, bf16[48,1024]{1,0:T(8,128)(2,1)S(1)}, u32[]{:S(2)}, u32[]{:S(2)}) %collective-permute-start.6) | collective-permute-done | bytes 98336 | tf_op jit(solution)/shard_map/ppermute | solution.py:253
  27.6 1.5 %collective-permute-done.7.refs_3_ = bf16[48,1024]{1,0:T(8,128)(2,1)S(1)} collective-permute-done((bf16[48,1024]{1,0:T(8,128)(2,1)S(1)}, bf16[48,1024]{1,0:T(8,128)(2,1)S(1)}, u32[]{:S(2)}, u32[]{:S(2)}) %collective-permute-start.7) | collective-permute-done | bytes 98336 | tf_op jit(solution)/shard_map/ppermute | solution.py:253
  29.1 0.5 collective-permute-start.11
  29.6 0.5 collective-permute-start.9
  30.1 0.3 collective-permute-done.10.refs_6_
  30.4 0.2 collective-permute-done.11.refs_7_
  30.5 0.4 collective-permute-done.8.refs_4_
  30.9 0.2 collective-permute-done.9.refs_5_
  31.1 0.6 collective-permute-start.12
  31.7 2.6 %collective-permute-start.15 = (bf16[192,512]{1,0:T(8,128)(2,1)S(1)}, bf16[192,512]{1,0:T(8,128)(2,1)S(1)}, u32[]{:S(2)}, u32[]{:S(2)}) collective-permute-start(bf16[192,512]{1,0:T(8,128)(2,1)S(1)} %add_blocks.2.refs_0_), channel_id=1, source_target_pairs={{0,2},{1,3},{2,0},{3,1},{4,6},{5,7},{6,4},{7,5},{8,10},{9,11},{10,... | collective-permute-start | bytes 589832 | tf_op jit(solution)/shard_map/ppermute | solution.py:287
  34.3 3.5 %collective-permute-start.16 = (bf16[192,512]{1,0:T(8,128)(2,1)S(1)}, bf16[192,512]{1,0:T(8,128)(2,1)S(1)}, u32[]{:S(2)}, u32[]{:S(2)}) collective-permute-start(bf16[192,512]{1,0:T(8,128)(2,1)S(1)} %add_blocks.2.refs_0_), channel_id=1, source_target_pairs={{0,1},{1,2},{2,3},{4,5},{5,6},{6,7},{8,9},{9,10},{10,11},{12,13},{... | collective-permute-start | bytes 589832 | tf_op jit(solution)/shard_map/ppermute | solution.py:288
  37.8 1.3 %collective-permute-start.17 = (bf16[192,512]{1,0:T(8,128)(2,1)S(1)}, bf16[192,512]{1,0:T(8,128)(2,1)S(1)}, u32[]{:S(2)}, u32[]{:S(2)}) collective-permute-start(bf16[192,512]{1,0:T(8,128)(2,1)S(1)} %add_blocks.2.refs_0_), channel_id=1, source_target_pairs={{1,0},{2,1},{3,2},{5,4},{6,5},{7,6},{9,8},{10,9},{11,10},{13,12},{... | collective-permute-start | bytes 589832 | tf_op jit(solution)/shard_map/ppermute | solution.py:289
  39.1 0.6 collective-permute-start.13
  39.7 2.4 %collective-permute-start.14 = (bf16[48,1024]{1,0:T(8,128)(2,1)S(1)}, bf16[48,1024]{1,0:T(8,128)(2,1)S(1)}, u32[]{:S(2)}, u32[]{:S(2)}) collective-permute-start(bf16[48,1024]{1,0:T(8,128)(2,1)S(1)} %get-tuple-element.67), channel_id=1, source_target_pairs={{0,24},{4,28},{8,16},{12,20},{16,8},{20,12},{24,0},{28,4},{1,25},{... | collective-permute-start | bytes 294920 | tf_op jit(solution)/shard_map/ppermute | solution.py:253
  42.1 3.4 %collective-permute-done.13.refs_2_ = bf16[48,1024]{1,0:T(8,128)(2,1)S(1)} collective-permute-done((bf16[48,1024]{1,0:T(8,128)(2,1)S(1)}, bf16[48,1024]{1,0:T(8,128)(2,1)S(1)}, u32[]{:S(2)}, u32[]{:S(2)}) %collective-permute-start.13) | collective-permute-done | bytes 98336 | tf_op jit(solution)/shard_map/ppermute | solution.py:253
  45.6 2.3 %collective-permute-done.17.refs_3_ = bf16[192,512]{1,0:T(8,128)(2,1)S(1)} collective-permute-done((bf16[192,512]{1,0:T(8,128)(2,1)S(1)}, bf16[192,512]{1,0:T(8,128)(2,1)S(1)}, u32[]{:S(2)}, u32[]{:S(2)}) %collective-permute-start.17) | collective-permute-done | bytes 196640 | tf_op jit(solution)/shard_map/ppermute | solution.py:289
  47.9 0.5 collective-permute-start.19
  48.4 0.5 collective-permute-start.21
  48.9 1.3 %collective-permute-start.22 = (bf16[192,512]{1,0:T(8,128)(2,1)S(1)}, bf16[192,512]{1,0:T(8,128)(2,1)S(1)}, u32[]{:S(2)}, u32[]{:S(2)}) collective-permute-start(bf16[192,512]{1,0:T(8,128)(2,1)S(1)} %collective-permute-done.15.refs_1_), channel_id=1, source_target_pairs={{2,3},{1,0},{6,7},{5,4},{10,11},{9,8},{14,15},{13,12},{18,19},{17,... | collective-permute-start | bytes 589832 | tf_op jit(solution)/shard_map/ppermute | solution.py:290
  50.3 2.7 %collective-permute-start.23 = (bf16[192,512]{1,0:T(8,128)(2,1)S(1)}, bf16[192,512]{1,0:T(8,128)(2,1)S(1)}, u32[]{:S(2)}, u32[]{:S(2)}) collective-permute-start(bf16[192,512]{1,0:T(8,128)(2,1)S(1)} %add_blocks.3.refs_0_), channel_id=1, source_target_pairs={{0,1},{1,2},{2,3},{3,0},{4,5},{5,6},{6,7},{7,4},{8,9},{9,10},{10,1... | collective-permute-start | bytes 589832 | tf_op jit(solution)/shard_map/ppermute | solution.py:281
  53.0 0.1 collective-permute-start.24
  53.1 2.8 %collective-permute-start.25 = (bf16[192,512]{1,0:T(8,128)(2,1)S(1)}, bf16[192,512]{1,0:T(8,128)(2,1)S(1)}, u32[]{:S(2)}, u32[]{:S(2)}) collective-permute-start(bf16[192,512]{1,0:T(8,128)(2,1)S(1)} %add_blocks.3.refs_0_), channel_id=1, source_target_pairs={{0,3},{1,0},{2,1},{3,2},{4,7},{5,4},{6,5},{7,6},{8,11},{9,8},{10,9... | collective-permute-start | bytes 589832 | tf_op jit(solution)/shard_map/ppermute | solution.py:281
  56.0 0.3 weights.1.weight_ref
  56.3 7.1 %collective-permute-done.22.refs_4_ = bf16[192,512]{1,0:T(8,128)(2,1)S(1)} collective-permute-done((bf16[192,512]{1,0:T(8,128)(2,1)S(1)}, bf16[192,512]{1,0:T(8,128)(2,1)S(1)}, u32[]{:S(2)}, u32[]{:S(2)}) %collective-permute-start.22) | collective-permute-done | bytes 196640 | tf_op jit(solution)/shard_map/ppermute | solution.py:290
  63.3 1.7 %combine_gate.1 = (bf16[512,512]{1,0:T(8,128)(2,1)}, f32[8,512]{1,0:T(8,128)S(1)}) custom-call(bf16[512,768]{1,0:T(8,128)(2,1)S(1)} %weights.1.weight_ref, s32[8,512]{1,0:T(8,128)S(1)} %bitcast.5, f32[16,512]{1,0:T(8,128)S(1)} %number.1.key_ref, bf16[512,512]{1,0:T(8,128)(2,1)S(1)} %copy-done.3, bf16[192,512]{1,0:T(8,128)(2,1)S(1)} %add_blocks.2.refs_0_, ...), custom_call_target="tpu_custom_call" | custom-call | bytes 2883584 | tf_op jit(solution)/shard_map/combine_gate/pallas_call | solution.py:23
  65.1 1.5 %collective-permute-start.27 = (f32[8,512]{1,0:T(8,128)S(1)}, f32[8,512]{1,0:T(8,128)S(1)}, u32[]{:S(2)}, u32[]{:S(2)}) collective-permute-start(f32[8,512]{1,0:T(8,128)S(1)} %get-tuple-element.82.refs_4_), channel_id=1, source_target_pairs={{0,8},{4,12},{8,0},{12,4},{1,9},{5,13},{9,1},{13,5},{2,10},{6,14},... | collective-permute-start | bytes 49160 | tf_op jit(solution)/shard_map/ppermute | solution.py:360
  66.6 1.6 %collective-permute-done.26.refs_5_ = f32[8,512]{1,0:T(8,128)S(1)} collective-permute-done((f32[8,512]{1,0:T(8,128)S(1)}, f32[8,512]{1,0:T(8,128)S(1)}, u32[]{:S(2)}, u32[]{:S(2)}) %collective-permute-start.26) | collective-permute-done | bytes 16416 | tf_op jit(solution)/shard_map/ppermute | solution.py:360
  68.2 0.6 collective-permute-done.27.refs_6_
  68.8 0.8 %collective-permute-done.28.refs_7_ = f32[8,512]{1,0:T(8,128)S(1)} collective-permute-done((f32[8,512]{1,0:T(8,128)S(1)}, f32[8,512]{1,0:T(8,128)S(1)}, u32[]{:S(2)}, u32[]{:S(2)}) %collective-permute-start.28) | collective-permute-done | bytes 16416 | tf_op jit(solution)/shard_map/ppermute | solution.py:360
  69.7 0.6 collective-permute-done.25.refs_3_
  70.3 1.4 %combine.1 = (bf16[512,512]{1,0:T(8,128)(2,1)}, f32[8,512]{1,0:T(8,128)}) custom-call(bf16[512,768]{1,0:T(8,128)(2,1)S(1)} %weights.1.weight_ref, bf16[192,512]{1,0:T(8,128)(2,1)S(1)} %add_blocks.3.refs_0_, bf16[192,512]{1,0:T(8,128)(2,1)S(1)} %collective-permute-done.23.refs_1_, bf16[192,512]{1,0:T(8,128)(2,1)S(1)} %collective-permute-done.24.refs_2_, ...), custom_call_target="tpu_custom_call" | custom-call | flops 402653184 | bytes 2179072 | tf_op jit(solution)/shard_map/combine/pallas_call | solution.py:23
  (35 shorter events, 0.2 us)
Async XLA Ops:
  0.6 2.3 %collective-permute-start = (bf16[512,512]{1,0:T(8,128)(2,1)}, bf16[512,512]{1,0:T(8,128)(2,1)S(1)}, u32[]{:S(2)}, u32[]{:S(2)}) collective-permute-start(bf16[512,512]{1,0:T(8,128)(2,1)} %refs_0_.1), channel_id=1, source_target_pairs={{0,4},{4,0},{8,12},{12,8},{1,5},{5,1},{9,13},{13,9},{2,6},{6,2},{1... | collective-permute-start | bytes 1572872 | tf_op jit(solution)/shard_map/ppermute | solution.py:243
  1.1 2.5 %collective-permute-start.1 = (bf16[512,512]{1,0:T(8,128)(2,1)}, bf16[512,512]{1,0:T(8,128)(2,1)S(1)}, u32[]{:S(2)}, u32[]{:S(2)}) collective-permute-start(bf16[512,512]{1,0:T(8,128)(2,1)} %grads_ref.1), channel_id=1, source_target_pairs={{0,4},{4,0},{8,12},{12,8},{1,5},{5,1},{9,13},{13,9},{2,6},{6,2},{1... | collective-permute-start | bytes 1572872 | tf_op jit(solution)/shard_map/ppermute | solution.py:243
  1.2 0.7 %copy-start.4 = (s32[512,8]{0,1:T(8,128)S(1)}, s32[512,8]{0,1:T(8,128)}, u32[]{:S(2)}) copy-start(s32[512,8]{0,1:T(8,128)} %param.9) | copy-start | bytes 49156
  1.9 1.7 %copy-start.3 = (bf16[512,512]{1,0:T(8,128)(2,1)S(1)}, bf16[512,512]{1,0:T(8,128)(2,1)}, u32[]{:S(2)}) copy-start(bf16[512,512]{1,0:T(8,128)(2,1)} %grads_ref.1) | copy-start | bytes 1572868
  1.9 1.7 %copy-start.7 = (bf16[512,512]{1,0:T(8,128)(2,1)S(1)}, bf16[512,512]{1,0:T(8,128)(2,1)}, u32[]{:S(2)}) copy-start(bf16[512,512]{1,0:T(8,128)(2,1)} %refs_0_.1) | copy-start | bytes 1572868
  2.1 15.6 %copy-start = (bf16[1,768,2048]{2,1,0:T(8,128)(2,1)S(1)}, bf16[1,768,2048]{2,1,0:T(8,128)(2,1)}, u32[]{:S(2)}) copy-start(bf16[1,768,2048]{2,1,0:T(8,128)(2,1)} %refs_4_.3) | copy-start | bytes 9437188
  2.1 15.6 %copy-start.1 = (bf16[1,768,2048]{2,1,0:T(8,128)(2,1)S(1)}, bf16[1,768,2048]{2,1,0:T(8,128)(2,1)}, u32[]{:S(2)}) copy-start(bf16[1,768,2048]{2,1,0:T(8,128)(2,1)} %refs_5_.3) | copy-start | bytes 9437188
  2.1 15.6 %copy-start.2 = (bf16[1,768,2048]{2,1,0:T(8,128)(2,1)S(1)}, bf16[1,768,2048]{2,1,0:T(8,128)(2,1)}, u32[]{:S(2)}) copy-start(bf16[1,768,2048]{2,1,0:T(8,128)(2,1)} %refs_6_.3) | copy-start | bytes 9437188
  4.1 8.2 %collective-permute-start.3 = (bf16[96,1024]{1,0:T(8,128)(2,1)S(1)}, bf16[96,1024]{1,0:T(8,128)(2,1)S(1)}, u32[]{:S(2)}, u32[]{:S(2)}) collective-permute-start(bf16[96,1024]{1,0:T(8,128)(2,1)S(1)} %get-tuple-element.44.refs_0_), channel_id=1, source_target_pairs={{0,16},{4,20},{8,24},{12,28},{16,0},{20,4},{24,8},{28,12},{1,17},{... | collective-permute-start | bytes 589832 | tf_op jit(solution)/shard_map/ppermute | solution.py:253
  7.1 7.8 %collective-permute-start.2 = (bf16[96,1024]{1,0:T(8,128)(2,1)S(1)}, bf16[96,1024]{1,0:T(8,128)(2,1)S(1)}, u32[]{:S(2)}, u32[]{:S(2)}) collective-permute-start(bf16[96,1024]{1,0:T(8,128)(2,1)S(1)} %get-tuple-element.45), channel_id=1, source_target_pairs={{0,8},{4,12},{8,0},{12,4},{16,24},{20,28},{24,16},{28,20},{1,9},{5... | collective-permute-start | bytes 589832 | tf_op jit(solution)/shard_map/ppermute | solution.py:253
  8.6 9.2 %collective-permute-start.4 = (bf16[96,1024]{1,0:T(8,128)(2,1)S(1)}, bf16[96,1024]{1,0:T(8,128)(2,1)S(1)}, u32[]{:S(2)}, u32[]{:S(2)}) collective-permute-start(bf16[96,1024]{1,0:T(8,128)(2,1)S(1)} %get-tuple-element.45), channel_id=1, source_target_pairs={{0,24},{4,28},{8,16},{12,20},{16,8},{20,12},{24,0},{28,4},{1,25},{... | collective-permute-start | bytes 589832 | tf_op jit(solution)/shard_map/ppermute | solution.py:253
  20.3 6.0 %collective-permute-start.5 = (bf16[48,1024]{1,0:T(8,128)(2,1)S(1)}, bf16[48,1024]{1,0:T(8,128)(2,1)S(1)}, u32[]{:S(2)}, u32[]{:S(2)}) collective-permute-start(bf16[48,1024]{1,0:T(8,128)(2,1)S(1)} %get-tuple-element.47), channel_id=1, source_target_pairs={{0,8},{4,12},{8,0},{12,4},{16,24},{20,28},{24,16},{28,20},{1,9},{5... | collective-permute-start | bytes 294920 | tf_op jit(solution)/shard_map/ppermute | solution.py:253
  22.0 5.6 %collective-permute-start.6 = (bf16[48,1024]{1,0:T(8,128)(2,1)S(1)}, bf16[48,1024]{1,0:T(8,128)(2,1)S(1)}, u32[]{:S(2)}, u32[]{:S(2)}) collective-permute-start(bf16[48,1024]{1,0:T(8,128)(2,1)S(1)} %get-tuple-element.48), channel_id=1, source_target_pairs={{0,16},{4,20},{8,24},{12,28},{16,0},{20,4},{24,8},{28,12},{1,17},{... | collective-permute-start | bytes 294920 | tf_op jit(solution)/shard_map/ppermute | solution.py:253
  23.6 5.5 %collective-permute-start.7 = (bf16[48,1024]{1,0:T(8,128)(2,1)S(1)}, bf16[48,1024]{1,0:T(8,128)(2,1)S(1)}, u32[]{:S(2)}, u32[]{:S(2)}) collective-permute-start(bf16[48,1024]{1,0:T(8,128)(2,1)S(1)} %get-tuple-element.49), channel_id=1, source_target_pairs={{0,24},{4,28},{8,16},{12,20},{16,8},{20,12},{24,0},{28,4},{1,25},{... | collective-permute-start | bytes 294920 | tf_op jit(solution)/shard_map/ppermute | solution.py:253
  23.9 32.1 %copy-start.5 = (s32[512,8]{0,1:T(8,128)S(1)}, s32[512,8]{0,1:T(8,128)}, u32[]{:S(2)}) copy-start(s32[512,8]{0,1:T(8,128)} %param.9) | copy-start | bytes 49156
  23.9 32.1 %copy-start.6 = (f32[512,8]{0,1:T(8,128)S(1)}, f32[512,8]{0,1:T(8,128)}, u32[]{:S(2)}) copy-start(f32[512,8]{0,1:T(8,128)} %param.10) | copy-start | bytes 49156
  29.1 1.3 %collective-permute-start.10 = (bf16[48,1024]{1,0:T(8,128)(2,1)S(1)}, bf16[48,1024]{1,0:T(8,128)(2,1)S(1)}, u32[]{:S(2)}, u32[]{:S(2)}) collective-permute-start(bf16[48,1024]{1,0:T(8,128)(2,1)S(1)} %collective-permute-done.6.refs_2_), channel_id=1, source_target_pairs={{0,4},{4,0},{8,12},{12,8},{1,5},{5,1},{9,13},{13,9},{2,6},{6,2},{1... | collective-permute-start | bytes 294920 | tf_op jit(solution)/shard_map/ppermute | solution.py:243
  29.1 1.5 %collective-permute-start.11 = (bf16[48,1024]{1,0:T(8,128)(2,1)S(1)}, bf16[48,1024]{1,0:T(8,128)(2,1)S(1)}, u32[]{:S(2)}, u32[]{:S(2)}) collective-permute-start(bf16[48,1024]{1,0:T(8,128)(2,1)S(1)} %collective-permute-done.7.refs_3_), channel_id=1, source_target_pairs={{0,4},{4,0},{8,12},{12,8},{1,5},{5,1},{9,13},{13,9},{2,6},{6,2},{1... | collective-permute-start | bytes 294920 | tf_op jit(solution)/shard_map/ppermute | solution.py:243
  29.6 1.3 %collective-permute-start.8 = (bf16[48,1024]{1,0:T(8,128)(2,1)S(1)}, bf16[48,1024]{1,0:T(8,128)(2,1)S(1)}, u32[]{:S(2)}, u32[]{:S(2)}) collective-permute-start(bf16[48,1024]{1,0:T(8,128)(2,1)S(1)} %get-tuple-element.56.refs_0_), channel_id=1, source_target_pairs={{0,4},{4,0},{8,12},{12,8},{1,5},{5,1},{9,13},{13,9},{2,6},{6,2},{1... | collective-permute-start | bytes 294920 | tf_op jit(solution)/shard_map/ppermute | solution.py:243
  29.6 1.5 %collective-permute-start.9 = (bf16[48,1024]{1,0:T(8,128)(2,1)S(1)}, bf16[48,1024]{1,0:T(8,128)(2,1)S(1)}, u32[]{:S(2)}, u32[]{:S(2)}) collective-permute-start(bf16[48,1024]{1,0:T(8,128)(2,1)S(1)} %collective-permute-done.5.refs_1_), channel_id=1, source_target_pairs={{0,4},{4,0},{8,12},{12,8},{1,5},{5,1},{9,13},{13,9},{2,6},{6,2},{1... | collective-permute-start | bytes 294920 | tf_op jit(solution)/shard_map/ppermute | solution.py:243
  31.1 8.6 %collective-permute-start.12 = (bf16[48,1024]{1,0:T(8,128)(2,1)S(1)}, bf16[48,1024]{1,0:T(8,128)(2,1)S(1)}, u32[]{:S(2)}, u32[]{:S(2)}) collective-permute-start(bf16[48,1024]{1,0:T(8,128)(2,1)S(1)} %get-tuple-element.65), channel_id=1, source_target_pairs={{0,8},{4,12},{8,0},{12,4},{16,24},{20,28},{24,16},{28,20},{1,9},{5... | collective-permute-start | bytes 294920 | tf_op jit(solution)/shard_map/ppermute | solution.py:253
  31.7 13.8 %collective-permute-start.15 = (bf16[192,512]{1,0:T(8,128)(2,1)S(1)}, bf16[192,512]{1,0:T(8,128)(2,1)S(1)}, u32[]{:S(2)}, u32[]{:S(2)}) collective-permute-start(bf16[192,512]{1,0:T(8,128)(2,1)S(1)} %add_blocks.2.refs_0_), channel_id=1, source_target_pairs={{0,2},{1,3},{2,0},{3,1},{4,6},{5,7},{6,4},{7,5},{8,10},{9,11},{10,... | collective-permute-start | bytes 589832 | tf_op jit(solution)/shard_map/ppermute | solution.py:287
  34.3 11.3 %collective-permute-start.16 = (bf16[192,512]{1,0:T(8,128)(2,1)S(1)}, bf16[192,512]{1,0:T(8,128)(2,1)S(1)}, u32[]{:S(2)}, u32[]{:S(2)}) collective-permute-start(bf16[192,512]{1,0:T(8,128)(2,1)S(1)} %add_blocks.2.refs_0_), channel_id=1, source_target_pairs={{0,1},{1,2},{2,3},{4,5},{5,6},{6,7},{8,9},{9,10},{10,11},{12,13},{... | collective-permute-start | bytes 589832 | tf_op jit(solution)/shard_map/ppermute | solution.py:288
  37.8 10.1 %collective-permute-start.17 = (bf16[192,512]{1,0:T(8,128)(2,1)S(1)}, bf16[192,512]{1,0:T(8,128)(2,1)S(1)}, u32[]{:S(2)}, u32[]{:S(2)}) collective-permute-start(bf16[192,512]{1,0:T(8,128)(2,1)S(1)} %add_blocks.2.refs_0_), channel_id=1, source_target_pairs={{1,0},{2,1},{3,2},{5,4},{6,5},{7,6},{9,8},{10,9},{11,10},{13,12},{... | collective-permute-start | bytes 589832 | tf_op jit(solution)/shard_map/ppermute | solution.py:289
  39.1 6.5 %collective-permute-start.13 = (bf16[48,1024]{1,0:T(8,128)(2,1)S(1)}, bf16[48,1024]{1,0:T(8,128)(2,1)S(1)}, u32[]{:S(2)}, u32[]{:S(2)}) collective-permute-start(bf16[48,1024]{1,0:T(8,128)(2,1)S(1)} %get-tuple-element.66), channel_id=1, source_target_pairs={{0,16},{4,20},{8,24},{12,28},{16,0},{20,4},{24,8},{28,12},{1,17},{... | collective-permute-start | bytes 294920 | tf_op jit(solution)/shard_map/ppermute | solution.py:253
  39.7 5.9 %collective-permute-start.14 = (bf16[48,1024]{1,0:T(8,128)(2,1)S(1)}, bf16[48,1024]{1,0:T(8,128)(2,1)S(1)}, u32[]{:S(2)}, u32[]{:S(2)}) collective-permute-start(bf16[48,1024]{1,0:T(8,128)(2,1)S(1)} %get-tuple-element.67), channel_id=1, source_target_pairs={{0,24},{4,28},{8,16},{12,20},{16,8},{20,12},{24,0},{28,4},{1,25},{... | collective-permute-start | bytes 294920 | tf_op jit(solution)/shard_map/ppermute | solution.py:253
  47.9 2.3 %collective-permute-start.18 = (bf16[48,1024]{1,0:T(8,128)(2,1)S(1)}, bf16[48,1024]{1,0:T(8,128)(2,1)S(1)}, u32[]{:S(2)}, u32[]{:S(2)}) collective-permute-start(bf16[48,1024]{1,0:T(8,128)(2,1)S(1)} %get-tuple-element.69.refs_0_), channel_id=1, source_target_pairs={{0,4},{4,0},{8,12},{12,8},{1,5},{5,1},{9,13},{13,9},{2,6},{6,2},{1... | collective-permute-start | bytes 294920 | tf_op jit(solution)/shard_map/ppermute | solution.py:243
  47.9 2.3 %collective-permute-start.19 = (bf16[48,1024]{1,0:T(8,128)(2,1)S(1)}, bf16[48,1024]{1,0:T(8,128)(2,1)S(1)}, u32[]{:S(2)}, u32[]{:S(2)}) collective-permute-start(bf16[48,1024]{1,0:T(8,128)(2,1)S(1)} %collective-permute-done.12.refs_1_), channel_id=1, source_target_pairs={{0,4},{4,0},{8,12},{12,8},{1,5},{5,1},{9,13},{13,9},{2,6},{6,2},{1... | collective-permute-start | bytes 294920 | tf_op jit(solution)/shard_map/ppermute | solution.py:243
  48.4 1.8 %collective-permute-start.20 = (bf16[48,1024]{1,0:T(8,128)(2,1)S(1)}, bf16[48,1024]{1,0:T(8,128)(2,1)S(1)}, u32[]{:S(2)}, u32[]{:S(2)}) collective-permute-start(bf16[48,1024]{1,0:T(8,128)(2,1)S(1)} %collective-permute-done.13.refs_2_), channel_id=1, source_target_pairs={{0,4},{4,0},{8,12},{12,8},{1,5},{5,1},{9,13},{13,9},{2,6},{6,2},{1... | collective-permute-start | bytes 294920 | tf_op jit(solution)/shard_map/ppermute | solution.py:243
  48.4 1.8 %collective-permute-start.21 = (bf16[48,1024]{1,0:T(8,128)(2,1)S(1)}, bf16[48,1024]{1,0:T(8,128)(2,1)S(1)}, u32[]{:S(2)}, u32[]{:S(2)}) collective-permute-start(bf16[48,1024]{1,0:T(8,128)(2,1)S(1)} %collective-permute-done.14.refs_3_), channel_id=1, source_target_pairs={{0,4},{4,0},{8,12},{12,8},{1,5},{5,1},{9,13},{13,9},{2,6},{6,2},{1... | collective-permute-start | bytes 294920 | tf_op jit(solution)/shard_map/ppermute | solution.py:243
  48.9 14.4 %collective-permute-start.22 = (bf16[192,512]{1,0:T(8,128)(2,1)S(1)}, bf16[192,512]{1,0:T(8,128)(2,1)S(1)}, u32[]{:S(2)}, u32[]{:S(2)}) collective-permute-start(bf16[192,512]{1,0:T(8,128)(2,1)S(1)} %collective-permute-done.15.refs_1_), channel_id=1, source_target_pairs={{2,3},{1,0},{6,7},{5,4},{10,11},{9,8},{14,15},{13,12},{18,19},{17,... | collective-permute-start | bytes 589832 | tf_op jit(solution)/shard_map/ppermute | solution.py:290
  50.3 19.3 %collective-permute-start.23 = (bf16[192,512]{1,0:T(8,128)(2,1)S(1)}, bf16[192,512]{1,0:T(8,128)(2,1)S(1)}, u32[]{:S(2)}, u32[]{:S(2)}) collective-permute-start(bf16[192,512]{1,0:T(8,128)(2,1)S(1)} %add_blocks.3.refs_0_), channel_id=1, source_target_pairs={{0,1},{1,2},{2,3},{3,0},{4,5},{5,6},{6,7},{7,4},{8,9},{9,10},{10,1... | collective-permute-start | bytes 589832 | tf_op jit(solution)/shard_map/ppermute | solution.py:281
  53.0 16.6 %collective-permute-start.24 = (bf16[192,512]{1,0:T(8,128)(2,1)S(1)}, bf16[192,512]{1,0:T(8,128)(2,1)S(1)}, u32[]{:S(2)}, u32[]{:S(2)}) collective-permute-start(bf16[192,512]{1,0:T(8,128)(2,1)S(1)} %add_blocks.3.refs_0_), channel_id=1, source_target_pairs={{0,2},{1,3},{2,0},{3,1},{4,6},{5,7},{6,4},{7,5},{8,10},{9,11},{10,... | collective-permute-start | bytes 589832 | tf_op jit(solution)/shard_map/ppermute | solution.py:281
  53.1 17.2 %collective-permute-start.25 = (bf16[192,512]{1,0:T(8,128)(2,1)S(1)}, bf16[192,512]{1,0:T(8,128)(2,1)S(1)}, u32[]{:S(2)}, u32[]{:S(2)}) collective-permute-start(bf16[192,512]{1,0:T(8,128)(2,1)S(1)} %add_blocks.3.refs_0_), channel_id=1, source_target_pairs={{0,3},{1,0},{2,1},{3,2},{4,7},{5,4},{6,5},{7,6},{8,11},{9,8},{10,9... | collective-permute-start | bytes 589832 | tf_op jit(solution)/shard_map/ppermute | solution.py:281
  65.1 3.2 %collective-permute-start.26 = (f32[8,512]{1,0:T(8,128)S(1)}, f32[8,512]{1,0:T(8,128)S(1)}, u32[]{:S(2)}, u32[]{:S(2)}) collective-permute-start(f32[8,512]{1,0:T(8,128)S(1)} %get-tuple-element.82.refs_4_), channel_id=1, source_target_pairs={{0,4},{4,8},{8,12},{12,0},{1,5},{5,9},{9,13},{13,1},{2,6},{6,10},{... | collective-permute-start | bytes 49160 | tf_op jit(solution)/shard_map/ppermute | solution.py:360
  65.1 3.8 %collective-permute-start.27 = (f32[8,512]{1,0:T(8,128)S(1)}, f32[8,512]{1,0:T(8,128)S(1)}, u32[]{:S(2)}, u32[]{:S(2)}) collective-permute-start(f32[8,512]{1,0:T(8,128)S(1)} %get-tuple-element.82.refs_4_), channel_id=1, source_target_pairs={{0,8},{4,12},{8,0},{12,4},{1,9},{5,13},{9,1},{13,5},{2,10},{6,14},... | collective-permute-start | bytes 49160 | tf_op jit(solution)/shard_map/ppermute | solution.py:360
  68.2 1.4 %collective-permute-start.28 = (f32[8,512]{1,0:T(8,128)S(1)}, f32[8,512]{1,0:T(8,128)S(1)}, u32[]{:S(2)}, u32[]{:S(2)}) collective-permute-start(f32[8,512]{1,0:T(8,128)S(1)} %get-tuple-element.82.refs_4_), channel_id=1, source_target_pairs={{0,12},{4,0},{8,4},{12,8},{1,13},{5,1},{9,5},{13,9},{2,14},{6,2},{... | collective-permute-start | bytes 49160 | tf_op jit(solution)/shard_map/ppermute | solution.py:360

commit v9 on v8

--- a/solution.py
+++ b/solution.py
@@ -59,7 +59,7 @@
 
 
 def pick_kernel(cores, key_ref, *refs):
-    sources, pieces = refs[: 2 * cores], refs[2 * cores :]
+    sources, pieces = refs[:cores], refs[cores:]
     chips = len(pieces)
     rows, width = sources[0].shape
     chip, core, e = position(cores)
@@ -69,21 +69,20 @@
         expert = (e * chips + lax.rem(chip + dh, chips)) * cores + core
         masks.append((key_ref[pl.ds(expert, 1), :] == slot).astype(BF16))
     mask = jnp.concatenate(masks, axis=0)
-    for index, source in enumerate(sources):
-        kind, dc = divmod(index, cores)
+    for dc, source in enumerate(sources):
         picked = jnp.dot(mask, source[...], preferred_element_type=F32).astype(BF16)
         column = pl.multiple_of(lax.rem(core - dc + cores, cores) * width, width)
         for dh, piece in enumerate(pieces):
-            piece[kind * CAP : (kind + 1) * CAP, pl.ds(column, width)] = picked[dh * CAP : (dh + 1) * CAP]
-
-
-def gather_pieces(x_ref, pieces, kind, chips, cores):
+            piece[:, pl.ds(column, width)] = picked[dh * CAP : (dh + 1) * CAP]
+
+
+def gather_pieces(x_ref, pieces, chips, cores):
     chip, _, _ = position(cores)
     width = pieces[0].shape[1]
     for index, piece in enumerate(pieces):
         db, dh = divmod(index, chips)
         column = pl.multiple_of(lax.rem(chip - dh + chips, chips) * width, width)
-        x_ref[db * CAP : (db + 1) * CAP, pl.ds(column, width)] = piece[kind * CAP : (kind + 1) * CAP, :]
+        x_ref[db * CAP : (db + 1) * CAP, pl.ds(column, width)] = piece[...]
 
 
 def project_back(terms, pieces, chips, cores):
@@ -111,7 +110,7 @@
     pieces, (gate_ref, up_ref, down_ref) = refs[:count], refs[count : count + 3]
     act_ref, scale_ref = refs[count + 3 : count + 5]
     outs, (x_ref, hid_ref) = refs[count + 5 : 2 * count + 5], refs[2 * count + 5 :]
-    gather_pieces(x_ref, pieces, 0, chips, cores)
+    gather_pieces(x_ref, pieces, chips, cores)
     for part in chunks_of(gate_ref.shape[1]):
         gate_pre = lax.dot_general(x_ref[...], gate_ref[0, part, :], CONTRACT_LAST, preferred_element_type=F32)
         up_pre = lax.dot_general(x_ref[...], up_ref[0, part, :], CONTRACT_LAST, preferred_element_type=F32)
@@ -127,7 +126,7 @@
     pieces, (gate_ref, up_ref, down_ref) = refs[:count], refs[count : count + 3]
     act_ref, scale_ref = refs[count + 3 : count + 5]
     outs, (x_ref, grad_gate_ref, grad_up_ref) = refs[count + 5 : 2 * count + 5], refs[2 * count + 5 :]
-    gather_pieces(x_ref, pieces, 1, chips, cores)
+    gather_pieces(x_ref, pieces, chips, cores)
     for part in chunks_of(gate_ref.shape[1]):
         grad_hid = lax.dot_general(x_ref[...], down_ref[0, part, :], CONTRACT_LAST, preferred_element_type=F32)
         grad_gate_ref[:, part] = (grad_hid * scale_ref[:, part]).astype(BF16)
@@ -253,6 +252,7 @@
         return lax.ppermute(value, ("dp", "tensor"), pairs)
 
     hops = [(db, dh) for db in range(n_dp) for dh in range(chips)]
+    first = (n_dp - 1) * chips
     order = sorted(range(count), key=lambda index: (hops[index][0] == 0, -hops[index][1]))
 
     def dispatch(pieces):
@@ -290,16 +290,21 @@
         ends = lax.ppermute(far, "expert", [(2, 3), (1, 0)])
         return [value, far, up, down, ends]
 
-    sources = [to_core(tokens, dc) for dc in range(cores)] + [to_core(grad_out, dc) for dc in range(cores)]
+    def pick(key, sources):
+        return call(
+            functools.partial(pick_kernel, cores),
+            "pick",
+            [shape(CAP, cores * width)] * chips,
+            [key, *sources],
+            EARLY,
+        )
+
+    token_sources = [to_core(tokens, dc) for dc in range(cores)]
+    grad_sources = [to_core(grad_out, dc) for dc in range(cores)]
     key = call(number_kernel, "number", shape(experts, rows, F32), [routes_t], EARLY)
-    picked = call(
-        functools.partial(pick_kernel, cores),
-        "pick",
-        [shape(2 * CAP, cores * width)] * chips,
-        [key, *sources],
-        EARLY,
-    )
-    rows_in = dispatch(picked)
+    tok_in = dispatch(pick(key, token_sources))
+    tok_in[0], grad_pieces = lax.optimization_barrier((tok_in[0], pick(key, grad_sources)))
+    grad_in = dispatch(grad_pieces)
 
     matmul_flops = 2 * tall * hid_dev * feats
     saved = [shape(tall, hid_dev, F32)] * 2
@@ -308,27 +313,28 @@
         functools.partial(forward_kernel, chips, cores, count),
         "forward",
         saved + piece,
-        [*rows_in, gate_weight, up_weight, down_weight],
+        [*tok_in, gate_weight, up_weight, down_weight],
         3 * matmul_flops,
         [pltpu.VMEM((tall, feats), BF16), pltpu.VMEM((tall, hid_dev), BF16)],
         limit=24,
     )
+    outs, grad_in = after(outs, grad_in)
     out_pieces = give_back(outs)
     backs = call(
         functools.partial(backward_kernel, chips, cores, count),
         "backward",
         piece,
-        [*rows_in, gate_weight, up_weight, down_weight, act, scale],
+        [*grad_in, gate_weight, up_weight, down_weight, act, scale],
         3 * matmul_flops,
         [pltpu.VMEM((tall, feats), BF16)] + [pltpu.VMEM((tall, hid_dev), BF16)] * 2,
         limit=24,
     )
-    out_pieces, backs = after(out_pieces, backs)
+    out_pieces[first], backs = after(out_pieces[first], backs)
     out_rows = add_blocks(swap(out_pieces))
     out_rows, backs = after(out_rows, backs)
     out_parts = along(out_rows)
     back_pieces = give_back(backs)
-    back_pieces, out_parts[1:4] = after(back_pieces, out_parts[1:4])
+    back_pieces[0], out_parts[1:4] = after(back_pieces[0], out_parts[1:4])
     back_rows = add_blocks(swap(back_pieces))
     back_parts = across(back_rows)
     _, out_parts = after(back_rows, out_parts)

time: 72.5 us -> 68.2 us (0.941)
  waiting for transfers between devices: 30.8 us -> 23.5 us
  starting transfers between devices: 30.1 us -> 33.5 us
    ppermute x9 -> x12, waiting for transfers between devices: 15.3 us -> 8.1 us  [to_chip(): return lax.ppermute(value, ('dp', 'tensor'), pairs)]
    ppermute x9 -> x12, starting transfers between devices: 11.7 us -> 16.4 us  [to_chip(): return lax.ppermute(value, ('dp', 'tensor'), pairs)]
    ppermute x3, waiting for transfers between devices: 0.59 us -> 1.61 us  [across(): lax.ppermute(value, 'expert', [(z, (z + dz) % columns) for z in range(col...]
    ppermute x1, waiting for transfers between devices: 2.35 us -> 1.46 us  [along(): lax.ppermute(value, 'expert', [(z + 1, z) for z in range(columns - 1)])]
    ppermute x10, starting transfers between devices: 2.64 us -> 1.85 us  [to_core(): return lax.ppermute(value, 'tensor', pairs)]
    pallas_call x9 -> x10, Pallas kernels: 9.14 us -> 9.28 us  [call(): pl.pallas_call(kernel, out_shape=out_shape, in_specs=[spec] * len(operand...]
  transfers between devices with their start and end apart: 29 -> 32, of which waited for: 18 -> 12; matrix products, arithmetic and copies ran while one was open for 0% -> 0% of each run, Pallas kernels for 7% -> 12%
where the time goes in v9:
time: 68.2 us; the launch traced here: 67.9 us
  starting transfers between devices  33.5 us (49%)
  waiting for transfers between devices  23.5 us (34%)
  Pallas kernels  9.28 us (14%)
  local copies, waits for them, and re-layouts  0.83 us (1%)
  between operations  0.8 us (1%)
    ppermute x12, starting transfers between devices, to_chip(): return lax.ppermute(value, ('dp', 'tensor'), pairs)  16.4 us
    pallas_call x10, Pallas kernels, call(): pl.pallas_call(kernel, out_shape=out_shape, in_specs=[spec] * len(operand...  9.28 us
    ppermute x12, waiting for transfers between devices, to_chip(): return lax.ppermute(value, ('dp', 'tensor'), pairs)  8.1 us
    ppermute x1, waiting for transfers between devices, along(): ends = lax.ppermute(far, 'expert', [(2, 3), (1, 0)])  6.47 us
    ppermute x3, starting transfers between devices, across(): lax.ppermute(value, 'expert', [(z, (z + dz) % columns) for z in range(col...  5.69 us
    ppermute x3, waiting for transfers between devices, body(): gate_parts.append(lax.ppermute(gate_part, 'tensor', pairs))  3.78 us
    ppermute x1, starting transfers between devices, along(): up = lax.ppermute(value, 'expert', [(z, z + 1) for z in range(columns - 1)])  3.43 us
    ppermute x1, starting transfers between devices, along(): lax.ppermute(value, 'expert', [(z, (z + 2) % columns) for z in range(colu...  2.7 us
  transfers between devices with their start and end apart: 32, of which 12 were waited for; matrix products, arithmetic and copies ran while one was open for 0% of the time, Pallas kernels for 12%

profile of v9, /device:TPU:0, one launch (start us, length us, event | category | flops | bytes accessed | tf_op | source)
XLA Modules:
  0.0 67.9 jit_solution(1069975381249513167)
XLA Ops:
  0.6 0.5 collective-permute-start
  1.1 0.1 collective-permute-start.1
  1.2 0.7 %copy-done.4 = s32[512,8]{0,1:T(8,128)S(1)} copy-done((s32[512,8]{0,1:T(8,128)S(1)}, s32[512,8]{0,1:T(8,128)}, u32[]{:S(2)}) %copy-start.4) | copy-done | bytes 16408
  1.9 0.1 number.1.key_ref
  2.1 0.8 %collective-permute-done.refs_1_ = bf16[512,512]{1,0:T(8,128)(2,1)S(1)} collective-permute-done((bf16[512,512]{1,0:T(8,128)(2,1)}, bf16[512,512]{1,0:T(8,128)(2,1)S(1)}, u32[]{:S(2)}, u32[]{:S(2)}) %collective-permute-start) | collective-permute-done | bytes 524320 | tf_op jit(solution)/shard_map/ppermute | solution.py:242
  2.9 0.1 copy-done.7
  3.0 0.3 pick.2
  3.3 3.0 %collective-permute-start.2 = (bf16[48,1024]{1,0:T(8,128)(2,1)S(1)}, bf16[48,1024]{1,0:T(8,128)(2,1)S(1)}, u32[]{:S(2)}, u32[]{:S(2)}) collective-permute-start(bf16[48,1024]{1,0:T(8,128)(2,1)S(1)} %get-tuple-element.55), channel_id=1, source_target_pairs={{0,8},{4,12},{8,0},{12,4},{16,24},{20,28},{24,16},{28,20},{1,9},{5... | collective-permute-start | bytes 294920 | tf_op jit(solution)/shard_map/ppermute | solution.py:252
  6.3 1.5 %collective-permute-start.4 = (bf16[48,1024]{1,0:T(8,128)(2,1)S(1)}, bf16[48,1024]{1,0:T(8,128)(2,1)S(1)}, u32[]{:S(2)}, u32[]{:S(2)}) collective-permute-start(bf16[48,1024]{1,0:T(8,128)(2,1)S(1)} %get-tuple-element.55), channel_id=1, source_target_pairs={{0,24},{4,28},{8,16},{12,20},{16,8},{20,12},{24,0},{28,4},{1,25},{... | collective-permute-start | bytes 294920 | tf_op jit(solution)/shard_map/ppermute | solution.py:252
  7.8 0.1 collective-permute-start.3
  7.9 0.3 pick.3
  8.2 2.0 %collective-permute-start.5 = (bf16[48,1024]{1,0:T(8,128)(2,1)S(1)}, bf16[48,1024]{1,0:T(8,128)(2,1)S(1)}, u32[]{:S(2)}, u32[]{:S(2)}) collective-permute-start(bf16[48,1024]{1,0:T(8,128)(2,1)S(1)} %get-tuple-element.61), channel_id=1, source_target_pairs={{0,8},{4,12},{8,0},{12,4},{16,24},{20,28},{24,16},{28,20},{1,9},{5... | collective-permute-start | bytes 294920 | tf_op jit(solution)/shard_map/ppermute | solution.py:252
  10.1 1.5 %collective-permute-start.6 = (bf16[48,1024]{1,0:T(8,128)(2,1)S(1)}, bf16[48,1024]{1,0:T(8,128)(2,1)S(1)}, u32[]{:S(2)}, u32[]{:S(2)}) collective-permute-start(bf16[48,1024]{1,0:T(8,128)(2,1)S(1)} %get-tuple-element.65.refs_0_), channel_id=1, source_target_pairs={{0,16},{4,20},{8,24},{12,28},{16,0},{20,4},{24,8},{28,12},{1,17},{... | collective-permute-start | bytes 294920 | tf_op jit(solution)/shard_map/ppermute | solution.py:252
  11.7 1.2 %collective-permute-start.7 = (bf16[48,1024]{1,0:T(8,128)(2,1)S(1)}, bf16[48,1024]{1,0:T(8,128)(2,1)S(1)}, u32[]{:S(2)}, u32[]{:S(2)}) collective-permute-start(bf16[48,1024]{1,0:T(8,128)(2,1)S(1)} %get-tuple-element.61), channel_id=1, source_target_pairs={{0,24},{4,28},{8,16},{12,20},{16,8},{20,12},{24,0},{28,4},{1,25},{... | collective-permute-start | bytes 294920 | tf_op jit(solution)/shard_map/ppermute | solution.py:252
  12.9 2.9 %collective-permute-done.3.refs_2_ = bf16[48,1024]{1,0:T(8,128)(2,1)S(1)} collective-permute-done((bf16[48,1024]{1,0:T(8,128)(2,1)S(1)}, bf16[48,1024]{1,0:T(8,128)(2,1)S(1)}, u32[]{:S(2)}, u32[]{:S(2)}) %collective-permute-start.3) | collective-permute-done | bytes 98336 | tf_op jit(solution)/shard_map/ppermute | solution.py:252
  15.8 2.6 %forward.1 = (f32[96,768]{1,0:T(8,128)S(1)}, f32[96,768]{1,0:T(8,128)S(1)}, bf16[48,1024]{1,0:T(8,128)(2,1)S(1)}, bf16[48,1024]{1,0:T(8,128)(2,1)S(1)}, bf16[48,...) custom-call(bf16[48,1024]{1,0:T(8,128)(2,1)S(1)} %get-tuple-element.54.refs_0_, ...), custom_call_target="tpu_custom_call" | custom-call | flops 905969664 | bytes 10813440 | tf_op jit(solution)/shard_map/forward/pallas_call | solution.py:23
  18.4 0.2 collective-permute-start.9
  18.7 1.8 %collective-permute-start.8 = (bf16[48,1024]{1,0:T(8,128)(2,1)S(1)}, bf16[48,1024]{1,0:T(8,128)(2,1)S(1)}, u32[]{:S(2)}, u32[]{:S(2)}) collective-permute-start(bf16[48,1024]{1,0:T(8,128)(2,1)S(1)} %get-tuple-element.63), channel_id=1, source_target_pairs={{0,8},{4,12},{8,0},{12,4},{16,24},{20,28},{24,16},{28,20},{1,9},{5... | collective-permute-start | bytes 294920 | tf_op jit(solution)/shard_map/ppermute | solution.py:252
  20.5 1.5 %collective-permute-start.10 = (bf16[48,1024]{1,0:T(8,128)(2,1)S(1)}, bf16[48,1024]{1,0:T(8,128)(2,1)S(1)}, u32[]{:S(2)}, u32[]{:S(2)}) collective-permute-start(bf16[48,1024]{1,0:T(8,128)(2,1)S(1)} %get-tuple-element.76), channel_id=1, source_target_pairs={{0,24},{4,28},{8,16},{12,20},{16,8},{20,12},{24,0},{28,4},{1,25},{... | collective-permute-start | bytes 294920 | tf_op jit(solution)/shard_map/ppermute | solution.py:252
  22.0 2.4 %backward.1 = (bf16[48,1024]{1,0:T(8,128)(2,1)S(1)}, bf16[48,1024]{1,0:T(8,128)(2,1)S(1)}, bf16[48,1024]{1,0:T(8,128)(2,1)S(1)}, bf16[48,1024]{1,0:T(8,128)(2,1)S(1)}) custom-call(bf16[48,1024]{1,0:T(8,128)(2,1)S(1)} %get-tuple-element.65.refs_0_, bf16[48,1024]{1,0:T(8,128)(2,1)S(1)} %collective-permute-done.5.refs_1_, ...), custom_call_target="tpu_custom_call" | custom-call | flops 905969664 | bytes 10813440 | tf_op jit(solution)/shard_map/backward/pallas_call | solution.py:23
  24.5 0.6 collective-permute-start.13
  25.0 0.1 collective-permute-start.12
  25.1 0.9 %collective-permute-done.10.refs_3_ = bf16[48,1024]{1,0:T(8,128)(2,1)S(1)} collective-permute-done((bf16[48,1024]{1,0:T(8,128)(2,1)S(1)}, bf16[48,1024]{1,0:T(8,128)(2,1)S(1)}, u32[]{:S(2)}, u32[]{:S(2)}) %collective-permute-start.10) | collective-permute-done | bytes 98336 | tf_op jit(solution)/shard_map/ppermute | solution.py:252
  26.0 0.3 collective-permute-done.12.refs_5_
  26.4 1.0 %collective-permute-done.14.refs_7_ = bf16[48,1024]{1,0:T(8,128)(2,1)S(1)} collective-permute-done((bf16[48,1024]{1,0:T(8,128)(2,1)S(1)}, bf16[48,1024]{1,0:T(8,128)(2,1)S(1)}, u32[]{:S(2)}, u32[]{:S(2)}) %collective-permute-start.14) | collective-permute-done | bytes 98336 | tf_op jit(solution)/shard_map/ppermute | solution.py:242
  27.4 1.2 %collective-permute-start.18 = (bf16[48,1024]{1,0:T(8,128)(2,1)S(1)}, bf16[48,1024]{1,0:T(8,128)(2,1)S(1)}, u32[]{:S(2)}, u32[]{:S(2)}) collective-permute-start(bf16[48,1024]{1,0:T(8,128)(2,1)S(1)} %get-tuple-element.84), channel_id=1, source_target_pairs={{0,8},{4,12},{8,0},{12,4},{16,24},{20,28},{24,16},{28,20},{1,9},{5... | collective-permute-start | bytes 294920 | tf_op jit(solution)/shard_map/ppermute | solution.py:252
  28.6 2.7 %collective-permute-start.15 = (bf16[192,512]{1,0:T(8,128)(2,1)S(1)}, bf16[192,512]{1,0:T(8,128)(2,1)S(1)}, u32[]{:S(2)}, u32[]{:S(2)}) collective-permute-start(bf16[192,512]{1,0:T(8,128)(2,1)S(1)} %add_blocks.2.refs_0_), channel_id=1, source_target_pairs={{0,2},{1,3},{2,0},{3,1},{4,6},{5,7},{6,4},{7,5},{8,10},{9,11},{10,... | collective-permute-start | bytes 589832 | tf_op jit(solution)/shard_map/ppermute | solution.py:287
  31.3 3.4 %collective-permute-start.16 = (bf16[192,512]{1,0:T(8,128)(2,1)S(1)}, bf16[192,512]{1,0:T(8,128)(2,1)S(1)}, u32[]{:S(2)}, u32[]{:S(2)}) collective-permute-start(bf16[192,512]{1,0:T(8,128)(2,1)S(1)} %add_blocks.2.refs_0_), channel_id=1, source_target_pairs={{0,1},{1,2},{2,3},{4,5},{5,6},{6,7},{8,9},{9,10},{10,11},{12,13},{... | collective-permute-start | bytes 589832 | tf_op jit(solution)/shard_map/ppermute | solution.py:288
  34.8 1.3 %collective-permute-start.17 = (bf16[192,512]{1,0:T(8,128)(2,1)S(1)}, bf16[192,512]{1,0:T(8,128)(2,1)S(1)}, u32[]{:S(2)}, u32[]{:S(2)}) collective-permute-start(bf16[192,512]{1,0:T(8,128)(2,1)S(1)} %add_blocks.2.refs_0_), channel_id=1, source_target_pairs={{1,0},{2,1},{3,2},{5,4},{6,5},{7,6},{9,8},{10,9},{11,10},{13,12},{... | collective-permute-start | bytes 589832 | tf_op jit(solution)/shard_map/ppermute | solution.py:289
  36.1 0.9 %collective-permute-start.19 = (bf16[48,1024]{1,0:T(8,128)(2,1)S(1)}, bf16[48,1024]{1,0:T(8,128)(2,1)S(1)}, u32[]{:S(2)}, u32[]{:S(2)}) collective-permute-start(bf16[48,1024]{1,0:T(8,128)(2,1)S(1)} %get-tuple-element.85), channel_id=1, source_target_pairs={{0,16},{4,20},{8,24},{12,28},{16,0},{20,4},{24,8},{28,12},{1,17},{... | collective-permute-start | bytes 294920 | tf_op jit(solution)/shard_map/ppermute | solution.py:252
  36.9 1.4 %collective-permute-start.20 = (bf16[48,1024]{1,0:T(8,128)(2,1)S(1)}, bf16[48,1024]{1,0:T(8,128)(2,1)S(1)}, u32[]{:S(2)}, u32[]{:S(2)}) collective-permute-start(bf16[48,1024]{1,0:T(8,128)(2,1)S(1)} %get-tuple-element.86), channel_id=1, source_target_pairs={{0,24},{4,28},{8,16},{12,20},{16,8},{20,12},{24,0},{28,4},{1,25},{... | collective-permute-start | bytes 294920 | tf_op jit(solution)/shard_map/ppermute | solution.py:252
  38.4 4.2 %collective-permute-done.19.refs_2_ = bf16[48,1024]{1,0:T(8,128)(2,1)S(1)} collective-permute-done((bf16[48,1024]{1,0:T(8,128)(2,1)S(1)}, bf16[48,1024]{1,0:T(8,128)(2,1)S(1)}, u32[]{:S(2)}, u32[]{:S(2)}) %collective-permute-start.19) | collective-permute-done | bytes 98336 | tf_op jit(solution)/shard_map/ppermute | solution.py:252
  42.6 0.5 collective-permute-start.23
  43.2 0.1 collective-permute-start.24
  43.2 1.5 %collective-permute-done.17.refs_3_ = bf16[192,512]{1,0:T(8,128)(2,1)S(1)} collective-permute-done((bf16[192,512]{1,0:T(8,128)(2,1)S(1)}, bf16[192,512]{1,0:T(8,128)(2,1)S(1)}, u32[]{:S(2)}, u32[]{:S(2)}) %collective-permute-start.17) | collective-permute-done | bytes 196640 | tf_op jit(solution)/shard_map/ppermute | solution.py:289
  44.7 1.3 %collective-permute-start.25 = (bf16[192,512]{1,0:T(8,128)(2,1)S(1)}, bf16[192,512]{1,0:T(8,128)(2,1)S(1)}, u32[]{:S(2)}, u32[]{:S(2)}) collective-permute-start(bf16[192,512]{1,0:T(8,128)(2,1)S(1)} %collective-permute-done.15.refs_1_), channel_id=1, source_target_pairs={{2,3},{1,0},{6,7},{5,4},{10,11},{9,8},{14,15},{13,12},{18,19},{17,... | collective-permute-start | bytes 589832 | tf_op jit(solution)/shard_map/ppermute | solution.py:290
  46.1 2.7 %collective-permute-start.26 = (bf16[192,512]{1,0:T(8,128)(2,1)S(1)}, bf16[192,512]{1,0:T(8,128)(2,1)S(1)}, u32[]{:S(2)}, u32[]{:S(2)}) collective-permute-start(bf16[192,512]{1,0:T(8,128)(2,1)S(1)} %add_blocks.3.refs_0_), channel_id=1, source_target_pairs={{0,1},{1,2},{2,3},{3,0},{4,5},{5,6},{6,7},{7,4},{8,9},{9,10},{10,1... | collective-permute-start | bytes 589832 | tf_op jit(solution)/shard_map/ppermute | solution.py:281
  48.8 0.1 collective-permute-start.27
  48.9 2.8 %collective-permute-start.28 = (bf16[192,512]{1,0:T(8,128)(2,1)S(1)}, bf16[192,512]{1,0:T(8,128)(2,1)S(1)}, u32[]{:S(2)}, u32[]{:S(2)}) collective-permute-start(bf16[192,512]{1,0:T(8,128)(2,1)S(1)} %add_blocks.3.refs_0_), channel_id=1, source_target_pairs={{0,3},{1,0},{2,1},{3,2},{4,7},{5,4},{6,5},{7,6},{8,11},{9,8},{10,9... | collective-permute-start | bytes 589832 | tf_op jit(solution)/shard_map/ppermute | solution.py:281
  51.8 0.3 weights.1.weight_ref
  52.1 6.5 %collective-permute-done.25.refs_4_ = bf16[192,512]{1,0:T(8,128)(2,1)S(1)} collective-permute-done((bf16[192,512]{1,0:T(8,128)(2,1)S(1)}, bf16[192,512]{1,0:T(8,128)(2,1)S(1)}, u32[]{:S(2)}, u32[]{:S(2)}) %collective-permute-start.25) | collective-permute-done | bytes 196640 | tf_op jit(solution)/shard_map/ppermute | solution.py:290
  58.6 1.7 %combine_gate.1 = (bf16[512,512]{1,0:T(8,128)(2,1)}, f32[8,512]{1,0:T(8,128)S(1)}) custom-call(bf16[512,768]{1,0:T(8,128)(2,1)S(1)} %weights.1.weight_ref, s32[8,512]{1,0:T(8,128)S(1)} %bitcast.5, f32[16,512]{1,0:T(8,128)S(1)} %number.1.key_ref, bf16[512,512]{1,0:T(8,128)(2,1)S(1)} %copy-done.3, bf16[192,512]{1,0:T(8,128)(2,1)S(1)} %add_blocks.2.refs_0_, ...), custom_call_target="tpu_custom_call" | custom-call | bytes 2883584 | tf_op jit(solution)/shard_map/combine_gate/pallas_call | solution.py:23
  60.3 0.8 %collective-permute-start.30 = (f32[8,512]{1,0:T(8,128)S(1)}, f32[8,512]{1,0:T(8,128)S(1)}, u32[]{:S(2)}, u32[]{:S(2)}) collective-permute-start(f32[8,512]{1,0:T(8,128)S(1)} %get-tuple-element.96.refs_4_), channel_id=1, source_target_pairs={{0,8},{4,12},{8,0},{12,4},{1,9},{5,13},{9,1},{13,5},{2,10},{6,14},... | collective-permute-start | bytes 49160 | tf_op jit(solution)/shard_map/ppermute | solution.py:366
  61.1 2.3 %collective-permute-done.29.refs_5_ = f32[8,512]{1,0:T(8,128)S(1)} collective-permute-done((f32[8,512]{1,0:T(8,128)S(1)}, f32[8,512]{1,0:T(8,128)S(1)}, u32[]{:S(2)}, u32[]{:S(2)}) %collective-permute-start.29) | collective-permute-done | bytes 16416 | tf_op jit(solution)/shard_map/ppermute | solution.py:366
  63.5 0.7 %collective-permute-done.30.refs_6_ = f32[8,512]{1,0:T(8,128)S(1)} collective-permute-done((f32[8,512]{1,0:T(8,128)S(1)}, f32[8,512]{1,0:T(8,128)S(1)}, u32[]{:S(2)}, u32[]{:S(2)}) %collective-permute-start.30) | collective-permute-done | bytes 16416 | tf_op jit(solution)/shard_map/ppermute | solution.py:366
  64.1 0.8 %collective-permute-done.31.refs_7_ = f32[8,512]{1,0:T(8,128)S(1)} collective-permute-done((f32[8,512]{1,0:T(8,128)S(1)}, f32[8,512]{1,0:T(8,128)S(1)}, u32[]{:S(2)}, u32[]{:S(2)}) %collective-permute-start.31) | collective-permute-done | bytes 16416 | tf_op jit(solution)/shard_map/ppermute | solution.py:366
  64.9 1.6 %collective-permute-done.28.refs_3_ = bf16[192,512]{1,0:T(8,128)(2,1)S(1)} collective-permute-done((bf16[192,512]{1,0:T(8,128)(2,1)S(1)}, bf16[192,512]{1,0:T(8,128)(2,1)S(1)}, u32[]{:S(2)}, u32[]{:S(2)}) %collective-permute-start.28) | collective-permute-done | bytes 196640 | tf_op jit(solution)/shard_map/ppermute | solution.py:281
  66.5 1.4 %combine.1 = (bf16[512,512]{1,0:T(8,128)(2,1)}, f32[8,512]{1,0:T(8,128)}) custom-call(bf16[512,768]{1,0:T(8,128)(2,1)S(1)} %weights.1.weight_ref, bf16[192,512]{1,0:T(8,128)(2,1)S(1)} %add_blocks.3.refs_0_, bf16[192,512]{1,0:T(8,128)(2,1)S(1)} %collective-permute-done.26.refs_1_, bf16[192,512]{1,0:T(8,128)(2,1)S(1)} %collective-permute-done.27.refs_2_, ...), custom_call_target="tpu_custom_call" | custom-call | flops 402653184 | bytes 2179072 | tf_op jit(solution)/shard_map/combine/pallas_call | solution.py:23
  (42 shorter events, 0.2 us)
Async XLA Ops:
  0.6 2.3 %collective-permute-start = (bf16[512,512]{1,0:T(8,128)(2,1)}, bf16[512,512]{1,0:T(8,128)(2,1)S(1)}, u32[]{:S(2)}, u32[]{:S(2)}) collective-permute-start(bf16[512,512]{1,0:T(8,128)(2,1)} %refs_0_.2), channel_id=1, source_target_pairs={{0,4},{4,0},{8,12},{12,8},{1,5},{5,1},{9,13},{13,9},{2,6},{6,2},{1... | collective-permute-start | bytes 1572872 | tf_op jit(solution)/shard_map/ppermute | solution.py:242
  1.1 6.7 %collective-permute-start.1 = (bf16[512,512]{1,0:T(8,128)(2,1)}, bf16[512,512]{1,0:T(8,128)(2,1)S(1)}, u32[]{:S(2)}, u32[]{:S(2)}) collective-permute-start(bf16[512,512]{1,0:T(8,128)(2,1)} %grads_ref.1), channel_id=1, source_target_pairs={{0,4},{4,0},{8,12},{12,8},{1,5},{5,1},{9,13},{13,9},{2,6},{6,2},{1... | collective-permute-start | bytes 1572872 | tf_op jit(solution)/shard_map/ppermute | solution.py:242
  1.2 0.7 %copy-start.4 = (s32[512,8]{0,1:T(8,128)S(1)}, s32[512,8]{0,1:T(8,128)}, u32[]{:S(2)}) copy-start(s32[512,8]{0,1:T(8,128)} %param.9) | copy-start | bytes 49156
  1.9 1.0 %copy-start.7 = (bf16[512,512]{1,0:T(8,128)(2,1)S(1)}, bf16[512,512]{1,0:T(8,128)(2,1)}, u32[]{:S(2)}) copy-start(bf16[512,512]{1,0:T(8,128)(2,1)} %refs_0_.2) | copy-start | bytes 1572868
  2.1 5.8 %copy-start.3 = (bf16[512,512]{1,0:T(8,128)(2,1)S(1)}, bf16[512,512]{1,0:T(8,128)(2,1)}, u32[]{:S(2)}) copy-start(bf16[512,512]{1,0:T(8,128)(2,1)} %grads_ref.1) | copy-start | bytes 1572868
  3.3 8.4 %collective-permute-start.2 = (bf16[48,1024]{1,0:T(8,128)(2,1)S(1)}, bf16[48,1024]{1,0:T(8,128)(2,1)S(1)}, u32[]{:S(2)}, u32[]{:S(2)}) collective-permute-start(bf16[48,1024]{1,0:T(8,128)(2,1)S(1)} %get-tuple-element.55), channel_id=1, source_target_pairs={{0,8},{4,12},{8,0},{12,4},{16,24},{20,28},{24,16},{28,20},{1,9},{5... | collective-permute-start | bytes 294920 | tf_op jit(solution)/shard_map/ppermute | solution.py:252
  6.3 9.5 %collective-permute-start.4 = (bf16[48,1024]{1,0:T(8,128)(2,1)S(1)}, bf16[48,1024]{1,0:T(8,128)(2,1)S(1)}, u32[]{:S(2)}, u32[]{:S(2)}) collective-permute-start(bf16[48,1024]{1,0:T(8,128)(2,1)S(1)} %get-tuple-element.55), channel_id=1, source_target_pairs={{0,24},{4,28},{8,16},{12,20},{16,8},{20,12},{24,0},{28,4},{1,25},{... | collective-permute-start | bytes 294920 | tf_op jit(solution)/shard_map/ppermute | solution.py:252
  7.8 8.1 %copy-start = (bf16[1,768,2048]{2,1,0:T(8,128)(2,1)S(1)}, bf16[1,768,2048]{2,1,0:T(8,128)(2,1)}, u32[]{:S(2)}) copy-start(bf16[1,768,2048]{2,1,0:T(8,128)(2,1)} %refs_4_.3) | copy-start | bytes 9437188
  7.8 8.1 %copy-start.1 = (bf16[1,768,2048]{2,1,0:T(8,128)(2,1)S(1)}, bf16[1,768,2048]{2,1,0:T(8,128)(2,1)}, u32[]{:S(2)}) copy-start(bf16[1,768,2048]{2,1,0:T(8,128)(2,1)} %refs_5_.3) | copy-start | bytes 9437188
  7.8 8.1 %copy-start.2 = (bf16[1,768,2048]{2,1,0:T(8,128)(2,1)S(1)}, bf16[1,768,2048]{2,1,0:T(8,128)(2,1)}, u32[]{:S(2)}) copy-start(bf16[1,768,2048]{2,1,0:T(8,128)(2,1)} %refs_6_.3) | copy-start | bytes 9437188
  7.8 8.0 %collective-permute-start.3 = (bf16[48,1024]{1,0:T(8,128)(2,1)S(1)}, bf16[48,1024]{1,0:T(8,128)(2,1)S(1)}, u32[]{:S(2)}, u32[]{:S(2)}) collective-permute-start(bf16[48,1024]{1,0:T(8,128)(2,1)S(1)} %get-tuple-element.54.refs_0_), channel_id=1, source_target_pairs={{0,16},{4,20},{8,24},{12,28},{16,0},{20,4},{24,8},{28,12},{1,17},{... | collective-permute-start | bytes 294920 | tf_op jit(solution)/shard_map/ppermute | solution.py:252
  8.2 10.2 %collective-permute-start.5 = (bf16[48,1024]{1,0:T(8,128)(2,1)S(1)}, bf16[48,1024]{1,0:T(8,128)(2,1)S(1)}, u32[]{:S(2)}, u32[]{:S(2)}) collective-permute-start(bf16[48,1024]{1,0:T(8,128)(2,1)S(1)} %get-tuple-element.61), channel_id=1, source_target_pairs={{0,8},{4,12},{8,0},{12,4},{16,24},{20,28},{24,16},{28,20},{1,9},{5... | collective-permute-start | bytes 294920 | tf_op jit(solution)/shard_map/ppermute | solution.py:252
  10.1 8.3 %collective-permute-start.6 = (bf16[48,1024]{1,0:T(8,128)(2,1)S(1)}, bf16[48,1024]{1,0:T(8,128)(2,1)S(1)}, u32[]{:S(2)}, u32[]{:S(2)}) collective-permute-start(bf16[48,1024]{1,0:T(8,128)(2,1)S(1)} %get-tuple-element.65.refs_0_), channel_id=1, source_target_pairs={{0,16},{4,20},{8,24},{12,28},{16,0},{20,4},{24,8},{28,12},{1,17},{... | collective-permute-start | bytes 294920 | tf_op jit(solution)/shard_map/ppermute | solution.py:252
  11.7 6.8 %collective-permute-start.7 = (bf16[48,1024]{1,0:T(8,128)(2,1)S(1)}, bf16[48,1024]{1,0:T(8,128)(2,1)S(1)}, u32[]{:S(2)}, u32[]{:S(2)}) collective-permute-start(bf16[48,1024]{1,0:T(8,128)(2,1)S(1)} %get-tuple-element.61), channel_id=1, source_target_pairs={{0,24},{4,28},{8,16},{12,20},{16,8},{20,12},{24,0},{28,4},{1,25},{... | collective-permute-start | bytes 294920 | tf_op jit(solution)/shard_map/ppermute | solution.py:252
  18.4 6.0 %collective-permute-start.9 = (bf16[48,1024]{1,0:T(8,128)(2,1)S(1)}, bf16[48,1024]{1,0:T(8,128)(2,1)S(1)}, u32[]{:S(2)}, u32[]{:S(2)}) collective-permute-start(bf16[48,1024]{1,0:T(8,128)(2,1)S(1)} %get-tuple-element.64), channel_id=1, source_target_pairs={{0,16},{4,20},{8,24},{12,28},{16,0},{20,4},{24,8},{28,12},{1,17},{... | collective-permute-start | bytes 294920 | tf_op jit(solution)/shard_map/ppermute | solution.py:252
  18.7 6.4 %collective-permute-start.8 = (bf16[48,1024]{1,0:T(8,128)(2,1)S(1)}, bf16[48,1024]{1,0:T(8,128)(2,1)S(1)}, u32[]{:S(2)}, u32[]{:S(2)}) collective-permute-start(bf16[48,1024]{1,0:T(8,128)(2,1)S(1)} %get-tuple-element.63), channel_id=1, source_target_pairs={{0,8},{4,12},{8,0},{12,4},{16,24},{20,28},{24,16},{28,20},{1,9},{5... | collective-permute-start | bytes 294920 | tf_op jit(solution)/shard_map/ppermute | solution.py:252
  20.5 5.5 %collective-permute-start.10 = (bf16[48,1024]{1,0:T(8,128)(2,1)S(1)}, bf16[48,1024]{1,0:T(8,128)(2,1)S(1)}, u32[]{:S(2)}, u32[]{:S(2)}) collective-permute-start(bf16[48,1024]{1,0:T(8,128)(2,1)S(1)} %get-tuple-element.76), channel_id=1, source_target_pairs={{0,24},{4,28},{8,16},{12,20},{16,8},{20,12},{24,0},{28,4},{1,25},{... | collective-permute-start | bytes 294920 | tf_op jit(solution)/shard_map/ppermute | solution.py:252
  22.0 4.0 %collective-permute-start.11 = (bf16[48,1024]{1,0:T(8,128)(2,1)S(1)}, bf16[48,1024]{1,0:T(8,128)(2,1)S(1)}, u32[]{:S(2)}, u32[]{:S(2)}) collective-permute-start(bf16[48,1024]{1,0:T(8,128)(2,1)S(1)} %get-tuple-element.62.refs_0_), channel_id=1, source_target_pairs={{0,4},{4,0},{8,12},{12,8},{1,5},{5,1},{9,13},{13,9},{2,6},{6,2},{1... | collective-permute-start | bytes 294920 | tf_op jit(solution)/shard_map/ppermute | solution.py:242
  22.0 29.8 %copy-start.5 = (s32[512,8]{0,1:T(8,128)S(1)}, s32[512,8]{0,1:T(8,128)}, u32[]{:S(2)}) copy-start(s32[512,8]{0,1:T(8,128)} %param.9) | copy-start | bytes 49156
  22.0 29.8 %copy-start.6 = (f32[512,8]{0,1:T(8,128)S(1)}, f32[512,8]{0,1:T(8,128)}, u32[]{:S(2)}) copy-start(f32[512,8]{0,1:T(8,128)} %param.10) | copy-start | bytes 49156
  24.5 1.9 %collective-permute-start.13 = (bf16[48,1024]{1,0:T(8,128)(2,1)S(1)}, bf16[48,1024]{1,0:T(8,128)(2,1)S(1)}, u32[]{:S(2)}, u32[]{:S(2)}) collective-permute-start(bf16[48,1024]{1,0:T(8,128)(2,1)S(1)} %collective-permute-done.9.refs_2_), channel_id=1, source_target_pairs={{0,4},{4,0},{8,12},{12,8},{1,5},{5,1},{9,13},{13,9},{2,6},{6,2},{1... | collective-permute-start | bytes 294920 | tf_op jit(solution)/shard_map/ppermute | solution.py:242
  25.0 1.3 %collective-permute-start.12 = (bf16[48,1024]{1,0:T(8,128)(2,1)S(1)}, bf16[48,1024]{1,0:T(8,128)(2,1)S(1)}, u32[]{:S(2)}, u32[]{:S(2)}) collective-permute-start(bf16[48,1024]{1,0:T(8,128)(2,1)S(1)} %collective-permute-done.8.refs_1_), channel_id=1, source_target_pairs={{0,4},{4,0},{8,12},{12,8},{1,5},{5,1},{9,13},{13,9},{2,6},{6,2},{1... | collective-permute-start | bytes 294920 | tf_op jit(solution)/shard_map/ppermute | solution.py:242
  26.0 1.3 %collective-permute-start.14 = (bf16[48,1024]{1,0:T(8,128)(2,1)S(1)}, bf16[48,1024]{1,0:T(8,128)(2,1)S(1)}, u32[]{:S(2)}, u32[]{:S(2)}) collective-permute-start(bf16[48,1024]{1,0:T(8,128)(2,1)S(1)} %collective-permute-done.10.refs_3_), channel_id=1, source_target_pairs={{0,4},{4,0},{8,12},{12,8},{1,5},{5,1},{9,13},{13,9},{2,6},{6,2},{1... | collective-permute-start | bytes 294920 | tf_op jit(solution)/shard_map/ppermute | solution.py:242
  27.4 9.6 %collective-permute-start.18 = (bf16[48,1024]{1,0:T(8,128)(2,1)S(1)}, bf16[48,1024]{1,0:T(8,128)(2,1)S(1)}, u32[]{:S(2)}, u32[]{:S(2)}) collective-permute-start(bf16[48,1024]{1,0:T(8,128)(2,1)S(1)} %get-tuple-element.84), channel_id=1, source_target_pairs={{0,8},{4,12},{8,0},{12,4},{16,24},{20,28},{24,16},{28,20},{1,9},{5... | collective-permute-start | bytes 294920 | tf_op jit(solution)/shard_map/ppermute | solution.py:252
  28.6 14.5 %collective-permute-start.15 = (bf16[192,512]{1,0:T(8,128)(2,1)S(1)}, bf16[192,512]{1,0:T(8,128)(2,1)S(1)}, u32[]{:S(2)}, u32[]{:S(2)}) collective-permute-start(bf16[192,512]{1,0:T(8,128)(2,1)S(1)} %add_blocks.2.refs_0_), channel_id=1, source_target_pairs={{0,2},{1,3},{2,0},{3,1},{4,6},{5,7},{6,4},{7,5},{8,10},{9,11},{10,... | collective-permute-start | bytes 589832 | tf_op jit(solution)/shard_map/ppermute | solution.py:287
  31.3 11.9 %collective-permute-start.16 = (bf16[192,512]{1,0:T(8,128)(2,1)S(1)}, bf16[192,512]{1,0:T(8,128)(2,1)S(1)}, u32[]{:S(2)}, u32[]{:S(2)}) collective-permute-start(bf16[192,512]{1,0:T(8,128)(2,1)S(1)} %add_blocks.2.refs_0_), channel_id=1, source_target_pairs={{0,1},{1,2},{2,3},{4,5},{5,6},{6,7},{8,9},{9,10},{10,11},{12,13},{... | collective-permute-start | bytes 589832 | tf_op jit(solution)/shard_map/ppermute | solution.py:288
  34.8 9.9 %collective-permute-start.17 = (bf16[192,512]{1,0:T(8,128)(2,1)S(1)}, bf16[192,512]{1,0:T(8,128)(2,1)S(1)}, u32[]{:S(2)}, u32[]{:S(2)}) collective-permute-start(bf16[192,512]{1,0:T(8,128)(2,1)S(1)} %add_blocks.2.refs_0_), channel_id=1, source_target_pairs={{1,0},{2,1},{3,2},{5,4},{6,5},{7,6},{9,8},{10,9},{11,10},{13,12},{... | collective-permute-start | bytes 589832 | tf_op jit(solution)/shard_map/ppermute | solution.py:289
  36.1 6.6 %collective-permute-start.19 = (bf16[48,1024]{1,0:T(8,128)(2,1)S(1)}, bf16[48,1024]{1,0:T(8,128)(2,1)S(1)}, u32[]{:S(2)}, u32[]{:S(2)}) collective-permute-start(bf16[48,1024]{1,0:T(8,128)(2,1)S(1)} %get-tuple-element.85), channel_id=1, source_target_pairs={{0,16},{4,20},{8,24},{12,28},{16,0},{20,4},{24,8},{28,12},{1,17},{... | collective-permute-start | bytes 294920 | tf_op jit(solution)/shard_map/ppermute | solution.py:252
  36.9 5.7 %collective-permute-start.20 = (bf16[48,1024]{1,0:T(8,128)(2,1)S(1)}, bf16[48,1024]{1,0:T(8,128)(2,1)S(1)}, u32[]{:S(2)}, u32[]{:S(2)}) collective-permute-start(bf16[48,1024]{1,0:T(8,128)(2,1)S(1)} %get-tuple-element.86), channel_id=1, source_target_pairs={{0,24},{4,28},{8,16},{12,20},{16,8},{20,12},{24,0},{28,4},{1,25},{... | collective-permute-start | bytes 294920 | tf_op jit(solution)/shard_map/ppermute | solution.py:252
  42.6 3.3 %collective-permute-start.22 = (bf16[48,1024]{1,0:T(8,128)(2,1)S(1)}, bf16[48,1024]{1,0:T(8,128)(2,1)S(1)}, u32[]{:S(2)}, u32[]{:S(2)}) collective-permute-start(bf16[48,1024]{1,0:T(8,128)(2,1)S(1)} %collective-permute-done.18.refs_1_), channel_id=1, source_target_pairs={{0,4},{4,0},{8,12},{12,8},{1,5},{5,1},{9,13},{13,9},{2,6},{6,2},{1... | collective-permute-start | bytes 294920 | tf_op jit(solution)/shard_map/ppermute | solution.py:242
  42.6 3.4 %collective-permute-start.23 = (bf16[48,1024]{1,0:T(8,128)(2,1)S(1)}, bf16[48,1024]{1,0:T(8,128)(2,1)S(1)}, u32[]{:S(2)}, u32[]{:S(2)}) collective-permute-start(bf16[48,1024]{1,0:T(8,128)(2,1)S(1)} %collective-permute-done.19.refs_2_), channel_id=1, source_target_pairs={{0,4},{4,0},{8,12},{12,8},{1,5},{5,1},{9,13},{13,9},{2,6},{6,2},{1... | collective-permute-start | bytes 294920 | tf_op jit(solution)/shard_map/ppermute | solution.py:242
  43.2 2.8 %collective-permute-start.24 = (bf16[48,1024]{1,0:T(8,128)(2,1)S(1)}, bf16[48,1024]{1,0:T(8,128)(2,1)S(1)}, u32[]{:S(2)}, u32[]{:S(2)}) collective-permute-start(bf16[48,1024]{1,0:T(8,128)(2,1)S(1)} %collective-permute-done.20.refs_3_), channel_id=1, source_target_pairs={{0,4},{4,0},{8,12},{12,8},{1,5},{5,1},{9,13},{13,9},{2,6},{6,2},{1... | collective-permute-start | bytes 294920 | tf_op jit(solution)/shard_map/ppermute | solution.py:242
  44.7 1.3 %collective-permute-start.21 = (bf16[48,1024]{1,0:T(8,128)(2,1)S(1)}, bf16[48,1024]{1,0:T(8,128)(2,1)S(1)}, u32[]{:S(2)}, u32[]{:S(2)}) collective-permute-start(bf16[48,1024]{1,0:T(8,128)(2,1)S(1)} %get-tuple-element.83.refs_0_), channel_id=1, source_target_pairs={{0,4},{4,0},{8,12},{12,8},{1,5},{5,1},{9,13},{13,9},{2,6},{6,2},{1... | collective-permute-start | bytes 294920 | tf_op jit(solution)/shard_map/ppermute | solution.py:242
  44.7 13.9 %collective-permute-start.25 = (bf16[192,512]{1,0:T(8,128)(2,1)S(1)}, bf16[192,512]{1,0:T(8,128)(2,1)S(1)}, u32[]{:S(2)}, u32[]{:S(2)}) collective-permute-start(bf16[192,512]{1,0:T(8,128)(2,1)S(1)} %collective-permute-done.15.refs_1_), channel_id=1, source_target_pairs={{2,3},{1,0},{6,7},{5,4},{10,11},{9,8},{14,15},{13,12},{18,19},{17,... | collective-permute-start | bytes 589832 | tf_op jit(solution)/shard_map/ppermute | solution.py:290
  46.1 18.8 %collective-permute-start.26 = (bf16[192,512]{1,0:T(8,128)(2,1)S(1)}, bf16[192,512]{1,0:T(8,128)(2,1)S(1)}, u32[]{:S(2)}, u32[]{:S(2)}) collective-permute-start(bf16[192,512]{1,0:T(8,128)(2,1)S(1)} %add_blocks.3.refs_0_), channel_id=1, source_target_pairs={{0,1},{1,2},{2,3},{3,0},{4,5},{5,6},{6,7},{7,4},{8,9},{9,10},{10,1... | collective-permute-start | bytes 589832 | tf_op jit(solution)/shard_map/ppermute | solution.py:281
  48.8 16.1 %collective-permute-start.27 = (bf16[192,512]{1,0:T(8,128)(2,1)S(1)}, bf16[192,512]{1,0:T(8,128)(2,1)S(1)}, u32[]{:S(2)}, u32[]{:S(2)}) collective-permute-start(bf16[192,512]{1,0:T(8,128)(2,1)S(1)} %add_blocks.3.refs_0_), channel_id=1, source_target_pairs={{0,2},{1,3},{2,0},{3,1},{4,6},{5,7},{6,4},{7,5},{8,10},{9,11},{10,... | collective-permute-start | bytes 589832 | tf_op jit(solution)/shard_map/ppermute | solution.py:281
  48.9 17.6 %collective-permute-start.28 = (bf16[192,512]{1,0:T(8,128)(2,1)S(1)}, bf16[192,512]{1,0:T(8,128)(2,1)S(1)}, u32[]{:S(2)}, u32[]{:S(2)}) collective-permute-start(bf16[192,512]{1,0:T(8,128)(2,1)S(1)} %add_blocks.3.refs_0_), channel_id=1, source_target_pairs={{0,3},{1,0},{2,1},{3,2},{4,7},{5,4},{6,5},{7,6},{8,11},{9,8},{10,9... | collective-permute-start | bytes 589832 | tf_op jit(solution)/shard_map/ppermute | solution.py:281
  60.3 3.2 %collective-permute-start.29 = (f32[8,512]{1,0:T(8,128)S(1)}, f32[8,512]{1,0:T(8,128)S(1)}, u32[]{:S(2)}, u32[]{:S(2)}) collective-permute-start(f32[8,512]{1,0:T(8,128)S(1)} %get-tuple-element.96.refs_4_), channel_id=1, source_target_pairs={{0,4},{4,8},{8,12},{12,0},{1,5},{5,9},{9,13},{13,1},{2,6},{6,10},{... | collective-permute-start | bytes 49160 | tf_op jit(solution)/shard_map/ppermute | solution.py:366
  60.3 3.8 %collective-permute-start.30 = (f32[8,512]{1,0:T(8,128)S(1)}, f32[8,512]{1,0:T(8,128)S(1)}, u32[]{:S(2)}, u32[]{:S(2)}) collective-permute-start(f32[8,512]{1,0:T(8,128)S(1)} %get-tuple-element.96.refs_4_), channel_id=1, source_target_pairs={{0,8},{4,12},{8,0},{12,4},{1,9},{5,13},{9,1},{13,5},{2,10},{6,14},... | collective-permute-start | bytes 49160 | tf_op jit(solution)/shard_map/ppermute | solution.py:366
  63.5 1.4 %collective-permute-start.31 = (f32[8,512]{1,0:T(8,128)S(1)}, f32[8,512]{1,0:T(8,128)S(1)}, u32[]{:S(2)}, u32[]{:S(2)}) collective-permute-start(f32[8,512]{1,0:T(8,128)S(1)} %get-tuple-element.96.refs_4_), channel_id=1, source_target_pairs={{0,12},{4,0},{8,4},{12,8},{1,13},{5,1},{9,5},{13,9},{2,14},{6,2},{... | collective-permute-start | bytes 49160 | tf_op jit(solution)/shard_map/ppermute | solution.py:366

commit v10 on v9

--- a/solution.py
+++ b/solution.py
@@ -150,13 +150,19 @@
             out_ref[row : row + CAP, :] = total.astype(BF16)
 
 
+def partner_column(e, dz, columns):
+    if columns & (columns - 1) == 0:
+        return e ^ dz
+    return (e - dz + columns) % columns
+
+
 def slot_experts(chips, cores, columns):
     chip, core, e = position(cores)
     experts = []
     for dz in range(columns):
         for dh in range(chips):
             for dc in range(cores):
-                column = lax.rem(e - dz + columns, columns)
+                column = partner_column(e, dz, columns)
                 owner = lax.rem(chip - dh + chips, chips)
                 experts.append((column * chips + owner) * cores + lax.rem(core - dc + cores, cores))
     return experts
@@ -179,24 +185,16 @@
         out_ref[:, start : start + step] = all_ref[start : start + step, :].T.astype(BF16)
 
 
-def place_parts(parts, all_ref, columns):
+def place_parts(parts, all_ref):
     height = parts[0].shape[0]
-    if len(parts) == columns:
-        for index, part in enumerate(parts):
-            all_ref[index * height : (index + 1) * height, :] = part[...]
-        return
-    own, far, up, down, ends = parts
-    e = lax.axis_index("expert")
-    all_ref[0:height, :] = own[...]
-    all_ref[2 * height : 3 * height, :] = far[...]
-    all_ref[height : 2 * height, :] = jnp.where(e == 0, ends[...], up[...])
-    all_ref[3 * height : 4 * height, :] = jnp.where(e == columns - 1, ends[...], down[...])
+    for index, part in enumerate(parts):
+        all_ref[index * height : (index + 1) * height, :] = part[...]
 
 
 def combine_kernel(columns, weight_ref, *refs):
     parts, gates = refs[:columns], refs[columns:-3]
     out_ref, total_ref, all_ref = refs[-3:]
-    place_parts(parts, all_ref, columns)
+    place_parts(parts, all_ref)
     out_ref[...] = jnp.dot(weight_ref[...], all_ref[...], preferred_element_type=F32).astype(BF16)
     total = gates[0][...]
     for gate in gates[1:]:
@@ -206,7 +204,7 @@
 
 def combine_gate_kernel(chips, cores, columns, weight_ref, routes_ref, key_ref, grads_ref, *refs):
     parts, (out_ref, gate_ref, all_ref, sum_ref) = refs[:-4], refs[-4:]
-    place_parts(parts, all_ref, columns)
+    place_parts(parts, all_ref)
     out_ref[...] = jnp.dot(weight_ref[...], all_ref[...], preferred_element_type=F32).astype(BF16)
     rows = key_ref.shape[1]
     slot = lax.broadcasted_iota(jnp.int32, (CAP, rows), 0).astype(F32)
@@ -275,20 +273,14 @@
             2 * slots * width,
         )
 
-    def across(value):
-        parts = [value]
-        for dz in range(1, columns):
-            parts.append(lax.ppermute(value, "expert", [(z, (z + dz) % columns) for z in range(columns)]))
-        return parts
-
-    def along(value):
-        if columns != 4:
-            return across(value)
-        far = lax.ppermute(value, "expert", [(z, (z + 2) % columns) for z in range(columns)])
-        up = lax.ppermute(value, "expert", [(z, z + 1) for z in range(columns - 1)])
-        down = lax.ppermute(value, "expert", [(z + 1, z) for z in range(columns - 1)])
-        ends = lax.ppermute(far, "expert", [(2, 3), (1, 0)])
-        return [value, far, up, down, ends]
+    def across(parts, dz):
+        if columns & (columns - 1) == 0:
+            hop = dz & -dz
+            return lax.ppermute(parts[dz - hop], "expert", [(z, z ^ hop) for z in range(columns)])
+        return lax.ppermute(parts[0], "expert", [(z, (z + dz) % columns) for z in range(columns)])
+
+    direct = [dz for dz in range(1, columns) if dz & (dz - 1) == 0][::-1]
+    later = [dz for dz in range(1, columns) if dz not in direct]
 
     def pick(key, sources):
         return call(
@@ -332,11 +324,17 @@
     out_pieces[first], backs = after(out_pieces[first], backs)
     out_rows = add_blocks(swap(out_pieces))
     out_rows, backs = after(out_rows, backs)
-    out_parts = along(out_rows)
+    out_parts = {0: out_rows}
+    for dz in direct:
+        out_parts[dz] = across(out_parts, dz)
     back_pieces = give_back(backs)
-    back_pieces[0], out_parts[1:4] = after(back_pieces[0], out_parts[1:4])
+    back_pieces[0], out_parts = after(back_pieces[0], out_parts)
+    for dz in later:
+        out_parts[dz] = across(out_parts, dz)
     back_rows = add_blocks(swap(back_pieces))
-    back_parts = across(back_rows)
+    back_parts = {0: back_rows}
+    for dz in direct:
+        back_parts[dz] = across(back_parts, dz)
     _, out_parts = after(back_rows, out_parts)
 
     weight_map = call(
@@ -355,7 +353,7 @@
         functools.partial(combine_gate_kernel, chips, cores, columns),
         "combine_gate",
         [shape(rows, width), shape(routes_t.shape[0], rows, F32)],
-        [weight_map, routes_t, key, grad_out, *out_parts],
+        [weight_map, routes_t, key, grad_out, *[out_parts[dz] for dz in range(columns)]],
         0,
         [all_rows, pltpu.VMEM((experts * CAP, rows), F32)],
         limit=24,
@@ -364,11 +362,14 @@
     for dt in range(1, groups):
         pairs = [(t, (t + dt) % groups) for t in range(groups)]
         gate_parts.append(lax.ppermute(gate_part, "tensor", pairs))
+    back_parts, gate_parts = after(back_parts, gate_parts)
+    for dz in later:
+        back_parts[dz] = across(back_parts, dz)
     grad_tokens, grad_gates = call(
         functools.partial(combine_kernel, columns),
         "combine",
         [shape(rows, width), shape(*gate_part.shape, F32)],
-        [weight_map, *back_parts, *gate_parts],
+        [weight_map, *[back_parts[dz] for dz in range(columns)], *gate_parts],
         combine_flops,
         [all_rows],
         limit=16,

time: 68.2 us -> 67.9 us (level)
  starting transfers between devices: 33.5 us -> 28.1 us
  waiting for transfers between devices: 23.5 us -> 28.7 us
    ppermute x7 -> x6, waiting for transfers between devices: 9.55 us -> 16.2 us  [across(): lax.ppermute(parts[dz - hop], 'expert', [(z, z ^ hop) for z in range(colu...]
    ppermute x7 -> x6, starting transfers between devices: 14.4 us -> 7.79 us  [across(): lax.ppermute(parts[dz - hop], 'expert', [(z, z ^ hop) for z in range(colu...]
    ppermute x3, waiting for transfers between devices: 3.78 us -> 1.44 us  [body(): gate_parts.append(lax.ppermute(gate_part, 'tensor', pairs))]
    ppermute x3, starting transfers between devices: 0.83 us -> 2.75 us  [body(): gate_parts.append(lax.ppermute(gate_part, 'tensor', pairs))]
    ppermute x10, waiting for transfers between devices: 2.1 us -> 2.94 us  [to_core(): return lax.ppermute(value, 'tensor', pairs)]
  transfers between devices with their start and end apart: 32 -> 31, of which waited for: 12 -> 15; matrix products, arithmetic and copies ran while one was open for 0% -> 0% of each run, Pallas kernels for 12% -> 12%
where the time goes in v10:
time: 67.9 us; the launch traced here: 67.7 us
  waiting for transfers between devices  28.7 us (42%)
  starting transfers between devices  28.1 us (41%)
  Pallas kernels  9.26 us (14%)
  local copies, waits for them, and re-layouts  0.83 us (1%)
  between operations  0.75 us (1%)
    ppermute x12, starting transfers between devices, to_chip(): return lax.ppermute(value, ('dp', 'tensor'), pairs)  16.3 us
    ppermute x6, waiting for transfers between devices, across(): lax.ppermute(parts[dz - hop], 'expert', [(z, z ^ hop) for z in range(colu...  16.2 us
    pallas_call x10, Pallas kernels, call(): pl.pallas_call(kernel, out_shape=out_shape, in_specs=[spec] * len(operand...  9.26 us
    ppermute x12, waiting for transfers between devices, to_chip(): return lax.ppermute(value, ('dp', 'tensor'), pairs)  8.16 us
    ppermute x6, starting transfers between devices, across(): lax.ppermute(parts[dz - hop], 'expert', [(z, z ^ hop) for z in range(colu...  7.79 us
    ppermute x10, waiting for transfers between devices, to_core(): return lax.ppermute(value, 'tensor', pairs)  2.94 us
    ppermute x3, starting transfers between devices, body(): gate_parts.append(lax.ppermute(gate_part, 'tensor', pairs))  2.75 us
    ppermute x3, waiting for transfers between devices, body(): gate_parts.append(lax.ppermute(gate_part, 'tensor', pairs))  1.44 us
  transfers between devices with their start and end apart: 31, of which 15 were waited for; matrix products, arithmetic and copies ran while one was open for 0% of the time, Pallas kernels for 12%

profile of v10, /device:TPU:0, one launch (start us, length us, event | category | flops | bytes accessed | tf_op | source)
XLA Modules:
  0.0 67.7 jit_solution(4288409509233971887)
XLA Ops:
  0.6 0.5 collective-permute-start
  1.1 0.1 collective-permute-start.1
  1.2 0.7 %copy-done.4 = s32[512,8]{0,1:T(8,128)S(1)} copy-done((s32[512,8]{0,1:T(8,128)S(1)}, s32[512,8]{0,1:T(8,128)}, u32[]{:S(2)}) %copy-start.4) | copy-done | bytes 16408
  1.9 0.1 number.1.key_ref
  2.1 0.8 %collective-permute-done.refs_1_ = bf16[512,512]{1,0:T(8,128)(2,1)S(1)} collective-permute-done((bf16[512,512]{1,0:T(8,128)(2,1)}, bf16[512,512]{1,0:T(8,128)(2,1)S(1)}, u32[]{:S(2)}, u32[]{:S(2)}) %collective-permute-start) | collective-permute-done | bytes 524320 | tf_op jit(solution)/shard_map/ppermute | solution.py:240
  2.9 0.1 copy-done.7
  3.0 0.3 pick.2
  3.3 3.0 %collective-permute-start.2 = (bf16[48,1024]{1,0:T(8,128)(2,1)S(1)}, bf16[48,1024]{1,0:T(8,128)(2,1)S(1)}, u32[]{:S(2)}, u32[]{:S(2)}) collective-permute-start(bf16[48,1024]{1,0:T(8,128)(2,1)S(1)} %get-tuple-element.61), channel_id=1, source_target_pairs={{0,8},{4,12},{8,0},{12,4},{16,24},{20,28},{24,16},{28,20},{1,9},{5... | collective-permute-start | bytes 294920 | tf_op jit(solution)/shard_map/ppermute | solution.py:250
  6.3 1.5 %collective-permute-start.4 = (bf16[48,1024]{1,0:T(8,128)(2,1)S(1)}, bf16[48,1024]{1,0:T(8,128)(2,1)S(1)}, u32[]{:S(2)}, u32[]{:S(2)}) collective-permute-start(bf16[48,1024]{1,0:T(8,128)(2,1)S(1)} %get-tuple-element.61), channel_id=1, source_target_pairs={{0,24},{4,28},{8,16},{12,20},{16,8},{20,12},{24,0},{28,4},{1,25},{... | collective-permute-start | bytes 294920 | tf_op jit(solution)/shard_map/ppermute | solution.py:250
  7.8 0.1 collective-permute-start.3
  7.9 0.3 pick.3
  8.2 2.0 %collective-permute-start.5 = (bf16[48,1024]{1,0:T(8,128)(2,1)S(1)}, bf16[48,1024]{1,0:T(8,128)(2,1)S(1)}, u32[]{:S(2)}, u32[]{:S(2)}) collective-permute-start(bf16[48,1024]{1,0:T(8,128)(2,1)S(1)} %get-tuple-element.67), channel_id=1, source_target_pairs={{0,8},{4,12},{8,0},{12,4},{16,24},{20,28},{24,16},{28,20},{1,9},{5... | collective-permute-start | bytes 294920 | tf_op jit(solution)/shard_map/ppermute | solution.py:250
  10.1 1.5 %collective-permute-start.6 = (bf16[48,1024]{1,0:T(8,128)(2,1)S(1)}, bf16[48,1024]{1,0:T(8,128)(2,1)S(1)}, u32[]{:S(2)}, u32[]{:S(2)}) collective-permute-start(bf16[48,1024]{1,0:T(8,128)(2,1)S(1)} %get-tuple-element.71.refs_0_), channel_id=1, source_target_pairs={{0,16},{4,20},{8,24},{12,28},{16,0},{20,4},{24,8},{28,12},{1,17},{... | collective-permute-start | bytes 294920 | tf_op jit(solution)/shard_map/ppermute | solution.py:250
  11.7 1.2 %collective-permute-start.7 = (bf16[48,1024]{1,0:T(8,128)(2,1)S(1)}, bf16[48,1024]{1,0:T(8,128)(2,1)S(1)}, u32[]{:S(2)}, u32[]{:S(2)}) collective-permute-start(bf16[48,1024]{1,0:T(8,128)(2,1)S(1)} %get-tuple-element.67), channel_id=1, source_target_pairs={{0,24},{4,28},{8,16},{12,20},{16,8},{20,12},{24,0},{28,4},{1,25},{... | collective-permute-start | bytes 294920 | tf_op jit(solution)/shard_map/ppermute | solution.py:250
  12.9 2.9 %collective-permute-done.3.refs_2_ = bf16[48,1024]{1,0:T(8,128)(2,1)S(1)} collective-permute-done((bf16[48,1024]{1,0:T(8,128)(2,1)S(1)}, bf16[48,1024]{1,0:T(8,128)(2,1)S(1)}, u32[]{:S(2)}, u32[]{:S(2)}) %collective-permute-start.3) | collective-permute-done | bytes 98336 | tf_op jit(solution)/shard_map/ppermute | solution.py:250
  15.8 2.6 %forward.1 = (f32[96,768]{1,0:T(8,128)S(1)}, f32[96,768]{1,0:T(8,128)S(1)}, bf16[48,1024]{1,0:T(8,128)(2,1)S(1)}, bf16[48,1024]{1,0:T(8,128)(2,1)S(1)}, bf16[48,...) custom-call(bf16[48,1024]{1,0:T(8,128)(2,1)S(1)} %get-tuple-element.60.refs_0_, ...), custom_call_target="tpu_custom_call" | custom-call | flops 905969664 | bytes 10813440 | tf_op jit(solution)/shard_map/forward/pallas_call | solution.py:23
  18.4 0.2 collective-permute-start.9
  18.7 1.8 %collective-permute-start.8 = (bf16[48,1024]{1,0:T(8,128)(2,1)S(1)}, bf16[48,1024]{1,0:T(8,128)(2,1)S(1)}, u32[]{:S(2)}, u32[]{:S(2)}) collective-permute-start(bf16[48,1024]{1,0:T(8,128)(2,1)S(1)} %get-tuple-element.69), channel_id=1, source_target_pairs={{0,8},{4,12},{8,0},{12,4},{16,24},{20,28},{24,16},{28,20},{1,9},{5... | collective-permute-start | bytes 294920 | tf_op jit(solution)/shard_map/ppermute | solution.py:250
  20.5 1.5 %collective-permute-start.10 = (bf16[48,1024]{1,0:T(8,128)(2,1)S(1)}, bf16[48,1024]{1,0:T(8,128)(2,1)S(1)}, u32[]{:S(2)}, u32[]{:S(2)}) collective-permute-start(bf16[48,1024]{1,0:T(8,128)(2,1)S(1)} %get-tuple-element.82), channel_id=1, source_target_pairs={{0,24},{4,28},{8,16},{12,20},{16,8},{20,12},{24,0},{28,4},{1,25},{... | collective-permute-start | bytes 294920 | tf_op jit(solution)/shard_map/ppermute | solution.py:250
  22.0 2.4 %backward.1 = (bf16[48,1024]{1,0:T(8,128)(2,1)S(1)}, bf16[48,1024]{1,0:T(8,128)(2,1)S(1)}, bf16[48,1024]{1,0:T(8,128)(2,1)S(1)}, bf16[48,1024]{1,0:T(8,128)(2,1)S(1)}) custom-call(bf16[48,1024]{1,0:T(8,128)(2,1)S(1)} %get-tuple-element.71.refs_0_, bf16[48,1024]{1,0:T(8,128)(2,1)S(1)} %collective-permute-done.5.refs_1_, ...), custom_call_target="tpu_custom_call" | custom-call | flops 905969664 | bytes 10813440 | tf_op jit(solution)/shard_map/backward/pallas_call | solution.py:23
  24.5 0.6 collective-permute-start.13
  25.0 0.1 collective-permute-start.12
  25.1 0.9 %collective-permute-done.10.refs_3_ = bf16[48,1024]{1,0:T(8,128)(2,1)S(1)} collective-permute-done((bf16[48,1024]{1,0:T(8,128)(2,1)S(1)}, bf16[48,1024]{1,0:T(8,128)(2,1)S(1)}, u32[]{:S(2)}, u32[]{:S(2)}) %collective-permute-start.10) | collective-permute-done | bytes 98336 | tf_op jit(solution)/shard_map/ppermute | solution.py:250
  26.0 0.3 collective-permute-done.12.refs_5_
  26.4 1.0 %collective-permute-done.14.refs_7_ = bf16[48,1024]{1,0:T(8,128)(2,1)S(1)} collective-permute-done((bf16[48,1024]{1,0:T(8,128)(2,1)S(1)}, bf16[48,1024]{1,0:T(8,128)(2,1)S(1)}, u32[]{:S(2)}, u32[]{:S(2)}) %collective-permute-start.14) | collective-permute-done | bytes 98336 | tf_op jit(solution)/shard_map/ppermute | solution.py:240
  27.4 1.6 %collective-permute-start.15 = (bf16[192,512]{1,0:T(8,128)(2,1)S(1)}, bf16[192,512]{1,0:T(8,128)(2,1)S(1)}, u32[]{:S(2)}, u32[]{:S(2)}) collective-permute-start(bf16[192,512]{1,0:T(8,128)(2,1)S(1)} %add_blocks.2.refs_0_), channel_id=1, source_target_pairs={{0,1},{1,0},{2,3},{3,2},{4,5},{5,4},{6,7},{7,6},{8,9},{9,8},{10,11... | collective-permute-start | bytes 589832 | tf_op jit(solution)/shard_map/ppermute | solution.py:279
  29.0 2.6 %collective-permute-start.16 = (bf16[192,512]{1,0:T(8,128)(2,1)S(1)}, bf16[192,512]{1,0:T(8,128)(2,1)S(1)}, u32[]{:S(2)}, u32[]{:S(2)}) collective-permute-start(bf16[192,512]{1,0:T(8,128)(2,1)S(1)} %add_blocks.2.refs_0_), channel_id=1, source_target_pairs={{0,2},{1,3},{2,0},{3,1},{4,6},{5,7},{6,4},{7,5},{8,10},{9,11},{10,... | collective-permute-start | bytes 589832 | tf_op jit(solution)/shard_map/ppermute | solution.py:279
  31.6 1.2 %collective-permute-start.17 = (bf16[48,1024]{1,0:T(8,128)(2,1)S(1)}, bf16[48,1024]{1,0:T(8,128)(2,1)S(1)}, u32[]{:S(2)}, u32[]{:S(2)}) collective-permute-start(bf16[48,1024]{1,0:T(8,128)(2,1)S(1)} %get-tuple-element.90), channel_id=1, source_target_pairs={{0,8},{4,12},{8,0},{12,4},{16,24},{20,28},{24,16},{28,20},{1,9},{5... | collective-permute-start | bytes 294920 | tf_op jit(solution)/shard_map/ppermute | solution.py:250
  32.9 0.8 %collective-permute-start.18 = (bf16[48,1024]{1,0:T(8,128)(2,1)S(1)}, bf16[48,1024]{1,0:T(8,128)(2,1)S(1)}, u32[]{:S(2)}, u32[]{:S(2)}) collective-permute-start(bf16[48,1024]{1,0:T(8,128)(2,1)S(1)} %get-tuple-element.91), channel_id=1, source_target_pairs={{0,16},{4,20},{8,24},{12,28},{16,0},{20,4},{24,8},{28,12},{1,17},{... | collective-permute-start | bytes 294920 | tf_op jit(solution)/shard_map/ppermute | solution.py:250
  33.7 1.4 %collective-permute-start.19 = (bf16[48,1024]{1,0:T(8,128)(2,1)S(1)}, bf16[48,1024]{1,0:T(8,128)(2,1)S(1)}, u32[]{:S(2)}, u32[]{:S(2)}) collective-permute-start(bf16[48,1024]{1,0:T(8,128)(2,1)S(1)} %get-tuple-element.92), channel_id=1, source_target_pairs={{0,24},{4,28},{8,16},{12,20},{16,8},{20,12},{24,0},{28,4},{1,25},{... | collective-permute-start | bytes 294920 | tf_op jit(solution)/shard_map/ppermute | solution.py:250
  35.1 1.5 %collective-permute-done.17.refs_1_ = bf16[48,1024]{1,0:T(8,128)(2,1)S(1)} collective-permute-done((bf16[48,1024]{1,0:T(8,128)(2,1)S(1)}, bf16[48,1024]{1,0:T(8,128)(2,1)S(1)}, u32[]{:S(2)}, u32[]{:S(2)}) %collective-permute-start.17) | collective-permute-done | bytes 98336 | tf_op jit(solution)/shard_map/ppermute | solution.py:250
  36.6 1.8 %collective-permute-done.18.refs_2_ = bf16[48,1024]{1,0:T(8,128)(2,1)S(1)} collective-permute-done((bf16[48,1024]{1,0:T(8,128)(2,1)S(1)}, bf16[48,1024]{1,0:T(8,128)(2,1)S(1)}, u32[]{:S(2)}, u32[]{:S(2)}) %collective-permute-start.18) | collective-permute-done | bytes 98336 | tf_op jit(solution)/shard_map/ppermute | solution.py:250
  38.4 1.0 %collective-permute-done.19.refs_3_ = bf16[48,1024]{1,0:T(8,128)(2,1)S(1)} collective-permute-done((bf16[48,1024]{1,0:T(8,128)(2,1)S(1)}, bf16[48,1024]{1,0:T(8,128)(2,1)S(1)}, u32[]{:S(2)}, u32[]{:S(2)}) %collective-permute-start.19) | collective-permute-done | bytes 98336 | tf_op jit(solution)/shard_map/ppermute | solution.py:250
  39.4 1.4 %collective-permute-done.16.refs_2_ = bf16[192,512]{1,0:T(8,128)(2,1)S(1)} collective-permute-done((bf16[192,512]{1,0:T(8,128)(2,1)S(1)}, bf16[192,512]{1,0:T(8,128)(2,1)S(1)}, u32[]{:S(2)}, u32[]{:S(2)}) %collective-permute-start.16) | collective-permute-done | bytes 196640 | tf_op jit(solution)/shard_map/ppermute | solution.py:279
  40.9 0.4 collective-permute-start.24
  41.3 0.8 %collective-permute-done.20.refs_4_ = bf16[48,1024]{1,0:T(8,128)(2,1)S(1)} collective-permute-done((bf16[48,1024]{1,0:T(8,128)(2,1)S(1)}, bf16[48,1024]{1,0:T(8,128)(2,1)S(1)}, u32[]{:S(2)}, u32[]{:S(2)}) %collective-permute-start.20) | collective-permute-done | bytes 98336 | tf_op jit(solution)/shard_map/ppermute | solution.py:240
  42.2 0.8 %collective-permute-start.25 = (bf16[192,512]{1,0:T(8,128)(2,1)S(1)}, bf16[192,512]{1,0:T(8,128)(2,1)S(1)}, u32[]{:S(2)}, u32[]{:S(2)}) collective-permute-start(bf16[192,512]{1,0:T(8,128)(2,1)S(1)} %add_blocks.3.refs_0_), channel_id=1, source_target_pairs={{0,1},{1,0},{2,3},{3,2},{4,5},{5,4},{6,7},{7,6},{8,9},{9,8},{10,11... | collective-permute-start | bytes 589832 | tf_op jit(solution)/shard_map/ppermute | solution.py:279
  43.1 2.3 %collective-permute-start.26 = (bf16[192,512]{1,0:T(8,128)(2,1)S(1)}, bf16[192,512]{1,0:T(8,128)(2,1)S(1)}, u32[]{:S(2)}, u32[]{:S(2)}) collective-permute-start(bf16[192,512]{1,0:T(8,128)(2,1)S(1)} %add_blocks.3.refs_0_), channel_id=1, source_target_pairs={{0,2},{1,3},{2,0},{3,1},{4,6},{5,7},{6,4},{7,5},{8,10},{9,11},{10,... | collective-permute-start | bytes 589832 | tf_op jit(solution)/shard_map/ppermute | solution.py:279
  45.3 0.3 weights.1.weight_ref
  45.6 7.1 %collective-permute-done.24.refs_3_ = bf16[192,512]{1,0:T(8,128)(2,1)S(1)} collective-permute-done((bf16[192,512]{1,0:T(8,128)(2,1)S(1)}, bf16[192,512]{1,0:T(8,128)(2,1)S(1)}, u32[]{:S(2)}, u32[]{:S(2)}) %collective-permute-start.24) | collective-permute-done | bytes 196640 | tf_op jit(solution)/shard_map/ppermute | solution.py:279
  52.8 1.7 %combine_gate.1 = (bf16[512,512]{1,0:T(8,128)(2,1)}, f32[8,512]{1,0:T(8,128)S(1)}) custom-call(bf16[512,768]{1,0:T(8,128)(2,1)S(1)} %weights.1.weight_ref, s32[8,512]{1,0:T(8,128)S(1)} %bitcast.5, f32[16,512]{1,0:T(8,128)S(1)} %number.1.key_ref, bf16[512,512]{1,0:T(8,128)(2,1)S(1)} %copy-done.3, bf16[192,512]{1,0:T(8,128)(2,1)S(1)} %add_blocks.2.refs_0_, ...), custom_call_target="tpu_custom_call" | custom-call | bytes 2686976 | tf_op jit(solution)/shard_map/combine_gate/pallas_call | solution.py:23
  54.5 1.3 %collective-permute-start.28 = (f32[8,512]{1,0:T(8,128)S(1)}, f32[8,512]{1,0:T(8,128)S(1)}, u32[]{:S(2)}, u32[]{:S(2)}) collective-permute-start(f32[8,512]{1,0:T(8,128)S(1)} %get-tuple-element.105.refs_4_), channel_id=1, source_target_pairs={{0,8},{4,12},{8,0},{12,4},{1,9},{5,13},{9,1},{13,5},{2,10},{6,14},... | collective-permute-start | bytes 49160 | tf_op jit(solution)/shard_map/ppermute | solution.py:364
  55.8 1.4 %collective-permute-start.29 = (f32[8,512]{1,0:T(8,128)S(1)}, f32[8,512]{1,0:T(8,128)S(1)}, u32[]{:S(2)}, u32[]{:S(2)}) collective-permute-start(f32[8,512]{1,0:T(8,128)S(1)} %get-tuple-element.105.refs_4_), channel_id=1, source_target_pairs={{0,12},{4,0},{8,4},{12,8},{1,13},{5,1},{9,5},{13,9},{2,14},{6,2},{... | collective-permute-start | bytes 49160 | tf_op jit(solution)/shard_map/ppermute | solution.py:364
  57.2 0.4 collective-permute-done.27.refs_5_
  57.7 0.6 collective-permute-done.28.refs_6_
  58.3 0.4 collective-permute-done.29.refs_7_
  58.7 7.6 %collective-permute-done.30.refs_3_ = bf16[192,512]{1,0:T(8,128)(2,1)S(1)} collective-permute-done((bf16[192,512]{1,0:T(8,128)(2,1)S(1)}, bf16[192,512]{1,0:T(8,128)(2,1)S(1)}, u32[]{:S(2)}, u32[]{:S(2)}) %collective-permute-start.30) | collective-permute-done | bytes 196640 | tf_op jit(solution)/shard_map/ppermute | solution.py:279
  66.3 1.4 %combine.1 = (bf16[512,512]{1,0:T(8,128)(2,1)}, f32[8,512]{1,0:T(8,128)}) custom-call(bf16[512,768]{1,0:T(8,128)(2,1)S(1)} %weights.1.weight_ref, bf16[192,512]{1,0:T(8,128)(2,1)S(1)} %add_blocks.3.refs_0_, bf16[192,512]{1,0:T(8,128)(2,1)S(1)} %collective-permute-done.25.refs_1_, bf16[192,512]{1,0:T(8,128)(2,1)S(1)} %collective-permute-done.26.refs_2_, ...), custom_call_target="tpu_custom_call" | custom-call | flops 402653184 | bytes 2179072 | tf_op jit(solution)/shard_map/combine/pallas_call | solution.py:23
  (40 shorter events, 0.2 us)
Async XLA Ops:
  0.6 2.3 %collective-permute-start = (bf16[512,512]{1,0:T(8,128)(2,1)}, bf16[512,512]{1,0:T(8,128)(2,1)S(1)}, u32[]{:S(2)}, u32[]{:S(2)}) collective-permute-start(bf16[512,512]{1,0:T(8,128)(2,1)} %refs_0_.2), channel_id=1, source_target_pairs={{0,4},{4,0},{8,12},{12,8},{1,5},{5,1},{9,13},{13,9},{2,6},{6,2},{1... | collective-permute-start | bytes 1572872 | tf_op jit(solution)/shard_map/ppermute | solution.py:240
  1.1 6.7 %collective-permute-start.1 = (bf16[512,512]{1,0:T(8,128)(2,1)}, bf16[512,512]{1,0:T(8,128)(2,1)S(1)}, u32[]{:S(2)}, u32[]{:S(2)}) collective-permute-start(bf16[512,512]{1,0:T(8,128)(2,1)} %grads_ref.1), channel_id=1, source_target_pairs={{0,4},{4,0},{8,12},{12,8},{1,5},{5,1},{9,13},{13,9},{2,6},{6,2},{1... | collective-permute-start | bytes 1572872 | tf_op jit(solution)/shard_map/ppermute | solution.py:240
  1.2 0.7 %copy-start.4 = (s32[512,8]{0,1:T(8,128)S(1)}, s32[512,8]{0,1:T(8,128)}, u32[]{:S(2)}) copy-start(s32[512,8]{0,1:T(8,128)} %param.9) | copy-start | bytes 49156
  1.9 1.0 %copy-start.7 = (bf16[512,512]{1,0:T(8,128)(2,1)S(1)}, bf16[512,512]{1,0:T(8,128)(2,1)}, u32[]{:S(2)}) copy-start(bf16[512,512]{1,0:T(8,128)(2,1)} %refs_0_.2) | copy-start | bytes 1572868
  2.1 5.8 %copy-start.3 = (bf16[512,512]{1,0:T(8,128)(2,1)S(1)}, bf16[512,512]{1,0:T(8,128)(2,1)}, u32[]{:S(2)}) copy-start(bf16[512,512]{1,0:T(8,128)(2,1)} %grads_ref.1) | copy-start | bytes 1572868
  3.3 8.4 %collective-permute-start.2 = (bf16[48,1024]{1,0:T(8,128)(2,1)S(1)}, bf16[48,1024]{1,0:T(8,128)(2,1)S(1)}, u32[]{:S(2)}, u32[]{:S(2)}) collective-permute-start(bf16[48,1024]{1,0:T(8,128)(2,1)S(1)} %get-tuple-element.61), channel_id=1, source_target_pairs={{0,8},{4,12},{8,0},{12,4},{16,24},{20,28},{24,16},{28,20},{1,9},{5... | collective-permute-start | bytes 294920 | tf_op jit(solution)/shard_map/ppermute | solution.py:250
  6.3 9.5 %collective-permute-start.4 = (bf16[48,1024]{1,0:T(8,128)(2,1)S(1)}, bf16[48,1024]{1,0:T(8,128)(2,1)S(1)}, u32[]{:S(2)}, u32[]{:S(2)}) collective-permute-start(bf16[48,1024]{1,0:T(8,128)(2,1)S(1)} %get-tuple-element.61), channel_id=1, source_target_pairs={{0,24},{4,28},{8,16},{12,20},{16,8},{20,12},{24,0},{28,4},{1,25},{... | collective-permute-start | bytes 294920 | tf_op jit(solution)/shard_map/ppermute | solution.py:250
  7.8 8.1 %copy-start = (bf16[1,768,2048]{2,1,0:T(8,128)(2,1)S(1)}, bf16[1,768,2048]{2,1,0:T(8,128)(2,1)}, u32[]{:S(2)}) copy-start(bf16[1,768,2048]{2,1,0:T(8,128)(2,1)} %refs_4_.3) | copy-start | bytes 9437188
  7.8 8.1 %copy-start.1 = (bf16[1,768,2048]{2,1,0:T(8,128)(2,1)S(1)}, bf16[1,768,2048]{2,1,0:T(8,128)(2,1)}, u32[]{:S(2)}) copy-start(bf16[1,768,2048]{2,1,0:T(8,128)(2,1)} %refs_5_.3) | copy-start | bytes 9437188
  7.8 8.1 %copy-start.2 = (bf16[1,768,2048]{2,1,0:T(8,128)(2,1)S(1)}, bf16[1,768,2048]{2,1,0:T(8,128)(2,1)}, u32[]{:S(2)}) copy-start(bf16[1,768,2048]{2,1,0:T(8,128)(2,1)} %refs_6_.3) | copy-start | bytes 9437188
  7.8 8.0 %collective-permute-start.3 = (bf16[48,1024]{1,0:T(8,128)(2,1)S(1)}, bf16[48,1024]{1,0:T(8,128)(2,1)S(1)}, u32[]{:S(2)}, u32[]{:S(2)}) collective-permute-start(bf16[48,1024]{1,0:T(8,128)(2,1)S(1)} %get-tuple-element.60.refs_0_), channel_id=1, source_target_pairs={{0,16},{4,20},{8,24},{12,28},{16,0},{20,4},{24,8},{28,12},{1,17},{... | collective-permute-start | bytes 294920 | tf_op jit(solution)/shard_map/ppermute | solution.py:250
  8.2 10.2 %collective-permute-start.5 = (bf16[48,1024]{1,0:T(8,128)(2,1)S(1)}, bf16[48,1024]{1,0:T(8,128)(2,1)S(1)}, u32[]{:S(2)}, u32[]{:S(2)}) collective-permute-start(bf16[48,1024]{1,0:T(8,128)(2,1)S(1)} %get-tuple-element.67), channel_id=1, source_target_pairs={{0,8},{4,12},{8,0},{12,4},{16,24},{20,28},{24,16},{28,20},{1,9},{5... | collective-permute-start | bytes 294920 | tf_op jit(solution)/shard_map/ppermute | solution.py:250
  10.1 8.3 %collective-permute-start.6 = (bf16[48,1024]{1,0:T(8,128)(2,1)S(1)}, bf16[48,1024]{1,0:T(8,128)(2,1)S(1)}, u32[]{:S(2)}, u32[]{:S(2)}) collective-permute-start(bf16[48,1024]{1,0:T(8,128)(2,1)S(1)} %get-tuple-element.71.refs_0_), channel_id=1, source_target_pairs={{0,16},{4,20},{8,24},{12,28},{16,0},{20,4},{24,8},{28,12},{1,17},{... | collective-permute-start | bytes 294920 | tf_op jit(solution)/shard_map/ppermute | solution.py:250
  11.7 6.8 %collective-permute-start.7 = (bf16[48,1024]{1,0:T(8,128)(2,1)S(1)}, bf16[48,1024]{1,0:T(8,128)(2,1)S(1)}, u32[]{:S(2)}, u32[]{:S(2)}) collective-permute-start(bf16[48,1024]{1,0:T(8,128)(2,1)S(1)} %get-tuple-element.67), channel_id=1, source_target_pairs={{0,24},{4,28},{8,16},{12,20},{16,8},{20,12},{24,0},{28,4},{1,25},{... | collective-permute-start | bytes 294920 | tf_op jit(solution)/shard_map/ppermute | solution.py:250
  18.4 6.0 %collective-permute-start.9 = (bf16[48,1024]{1,0:T(8,128)(2,1)S(1)}, bf16[48,1024]{1,0:T(8,128)(2,1)S(1)}, u32[]{:S(2)}, u32[]{:S(2)}) collective-permute-start(bf16[48,1024]{1,0:T(8,128)(2,1)S(1)} %get-tuple-element.70), channel_id=1, source_target_pairs={{0,16},{4,20},{8,24},{12,28},{16,0},{20,4},{24,8},{28,12},{1,17},{... | collective-permute-start | bytes 294920 | tf_op jit(solution)/shard_map/ppermute | solution.py:250
  18.7 6.4 %collective-permute-start.8 = (bf16[48,1024]{1,0:T(8,128)(2,1)S(1)}, bf16[48,1024]{1,0:T(8,128)(2,1)S(1)}, u32[]{:S(2)}, u32[]{:S(2)}) collective-permute-start(bf16[48,1024]{1,0:T(8,128)(2,1)S(1)} %get-tuple-element.69), channel_id=1, source_target_pairs={{0,8},{4,12},{8,0},{12,4},{16,24},{20,28},{24,16},{28,20},{1,9},{5... | collective-permute-start | bytes 294920 | tf_op jit(solution)/shard_map/ppermute | solution.py:250
  20.5 5.5 %collective-permute-start.10 = (bf16[48,1024]{1,0:T(8,128)(2,1)S(1)}, bf16[48,1024]{1,0:T(8,128)(2,1)S(1)}, u32[]{:S(2)}, u32[]{:S(2)}) collective-permute-start(bf16[48,1024]{1,0:T(8,128)(2,1)S(1)} %get-tuple-element.82), channel_id=1, source_target_pairs={{0,24},{4,28},{8,16},{12,20},{16,8},{20,12},{24,0},{28,4},{1,25},{... | collective-permute-start | bytes 294920 | tf_op jit(solution)/shard_map/ppermute | solution.py:250
  22.0 4.0 %collective-permute-start.11 = (bf16[48,1024]{1,0:T(8,128)(2,1)S(1)}, bf16[48,1024]{1,0:T(8,128)(2,1)S(1)}, u32[]{:S(2)}, u32[]{:S(2)}) collective-permute-start(bf16[48,1024]{1,0:T(8,128)(2,1)S(1)} %get-tuple-element.68.refs_0_), channel_id=1, source_target_pairs={{0,4},{4,0},{8,12},{12,8},{1,5},{5,1},{9,13},{13,9},{2,6},{6,2},{1... | collective-permute-start | bytes 294920 | tf_op jit(solution)/shard_map/ppermute | solution.py:240
  22.0 23.3 %copy-start.5 = (s32[512,8]{0,1:T(8,128)S(1)}, s32[512,8]{0,1:T(8,128)}, u32[]{:S(2)}) copy-start(s32[512,8]{0,1:T(8,128)} %param.9) | copy-start | bytes 49156
  22.0 23.3 %copy-start.6 = (f32[512,8]{0,1:T(8,128)S(1)}, f32[512,8]{0,1:T(8,128)}, u32[]{:S(2)}) copy-start(f32[512,8]{0,1:T(8,128)} %param.10) | copy-start | bytes 49156
  24.5 1.9 %collective-permute-start.13 = (bf16[48,1024]{1,0:T(8,128)(2,1)S(1)}, bf16[48,1024]{1,0:T(8,128)(2,1)S(1)}, u32[]{:S(2)}, u32[]{:S(2)}) collective-permute-start(bf16[48,1024]{1,0:T(8,128)(2,1)S(1)} %collective-permute-done.9.refs_2_), channel_id=1, source_target_pairs={{0,4},{4,0},{8,12},{12,8},{1,5},{5,1},{9,13},{13,9},{2,6},{6,2},{1... | collective-permute-start | bytes 294920 | tf_op jit(solution)/shard_map/ppermute | solution.py:240
  25.0 1.3 %collective-permute-start.12 = (bf16[48,1024]{1,0:T(8,128)(2,1)S(1)}, bf16[48,1024]{1,0:T(8,128)(2,1)S(1)}, u32[]{:S(2)}, u32[]{:S(2)}) collective-permute-start(bf16[48,1024]{1,0:T(8,128)(2,1)S(1)} %collective-permute-done.8.refs_1_), channel_id=1, source_target_pairs={{0,4},{4,0},{8,12},{12,8},{1,5},{5,1},{9,13},{13,9},{2,6},{6,2},{1... | collective-permute-start | bytes 294920 | tf_op jit(solution)/shard_map/ppermute | solution.py:240
  26.0 1.3 %collective-permute-start.14 = (bf16[48,1024]{1,0:T(8,128)(2,1)S(1)}, bf16[48,1024]{1,0:T(8,128)(2,1)S(1)}, u32[]{:S(2)}, u32[]{:S(2)}) collective-permute-start(bf16[48,1024]{1,0:T(8,128)(2,1)S(1)} %collective-permute-done.10.refs_3_), channel_id=1, source_target_pairs={{0,4},{4,0},{8,12},{12,8},{1,5},{5,1},{9,13},{13,9},{2,6},{6,2},{1... | collective-permute-start | bytes 294920 | tf_op jit(solution)/shard_map/ppermute | solution.py:240
  27.4 12.1 %collective-permute-start.15 = (bf16[192,512]{1,0:T(8,128)(2,1)S(1)}, bf16[192,512]{1,0:T(8,128)(2,1)S(1)}, u32[]{:S(2)}, u32[]{:S(2)}) collective-permute-start(bf16[192,512]{1,0:T(8,128)(2,1)S(1)} %add_blocks.2.refs_0_), channel_id=1, source_target_pairs={{0,1},{1,0},{2,3},{3,2},{4,5},{5,4},{6,7},{7,6},{8,9},{9,8},{10,11... | collective-permute-start | bytes 589832 | tf_op jit(solution)/shard_map/ppermute | solution.py:279
  29.0 11.8 %collective-permute-start.16 = (bf16[192,512]{1,0:T(8,128)(2,1)S(1)}, bf16[192,512]{1,0:T(8,128)(2,1)S(1)}, u32[]{:S(2)}, u32[]{:S(2)}) collective-permute-start(bf16[192,512]{1,0:T(8,128)(2,1)S(1)} %add_blocks.2.refs_0_), channel_id=1, source_target_pairs={{0,2},{1,3},{2,0},{3,1},{4,6},{5,7},{6,4},{7,5},{8,10},{9,11},{10,... | collective-permute-start | bytes 589832 | tf_op jit(solution)/shard_map/ppermute | solution.py:279
  31.6 4.9 %collective-permute-start.17 = (bf16[48,1024]{1,0:T(8,128)(2,1)S(1)}, bf16[48,1024]{1,0:T(8,128)(2,1)S(1)}, u32[]{:S(2)}, u32[]{:S(2)}) collective-permute-start(bf16[48,1024]{1,0:T(8,128)(2,1)S(1)} %get-tuple-element.90), channel_id=1, source_target_pairs={{0,8},{4,12},{8,0},{12,4},{16,24},{20,28},{24,16},{28,20},{1,9},{5... | collective-permute-start | bytes 294920 | tf_op jit(solution)/shard_map/ppermute | solution.py:250
  32.9 5.5 %collective-permute-start.18 = (bf16[48,1024]{1,0:T(8,128)(2,1)S(1)}, bf16[48,1024]{1,0:T(8,128)(2,1)S(1)}, u32[]{:S(2)}, u32[]{:S(2)}) collective-permute-start(bf16[48,1024]{1,0:T(8,128)(2,1)S(1)} %get-tuple-element.91), channel_id=1, source_target_pairs={{0,16},{4,20},{8,24},{12,28},{16,0},{20,4},{24,8},{28,12},{1,17},{... | collective-permute-start | bytes 294920 | tf_op jit(solution)/shard_map/ppermute | solution.py:250
  33.7 5.8 %collective-permute-start.19 = (bf16[48,1024]{1,0:T(8,128)(2,1)S(1)}, bf16[48,1024]{1,0:T(8,128)(2,1)S(1)}, u32[]{:S(2)}, u32[]{:S(2)}) collective-permute-start(bf16[48,1024]{1,0:T(8,128)(2,1)S(1)} %get-tuple-element.92), channel_id=1, source_target_pairs={{0,24},{4,28},{8,16},{12,20},{16,8},{20,12},{24,0},{28,4},{1,25},{... | collective-permute-start | bytes 294920 | tf_op jit(solution)/shard_map/ppermute | solution.py:250
  36.6 4.8 %collective-permute-start.21 = (bf16[48,1024]{1,0:T(8,128)(2,1)S(1)}, bf16[48,1024]{1,0:T(8,128)(2,1)S(1)}, u32[]{:S(2)}, u32[]{:S(2)}) collective-permute-start(bf16[48,1024]{1,0:T(8,128)(2,1)S(1)} %collective-permute-done.17.refs_1_), channel_id=1, source_target_pairs={{0,4},{4,0},{8,12},{12,8},{1,5},{5,1},{9,13},{13,9},{2,6},{6,2},{1... | collective-permute-start | bytes 294920 | tf_op jit(solution)/shard_map/ppermute | solution.py:240
  38.4 2.9 %collective-permute-start.22 = (bf16[48,1024]{1,0:T(8,128)(2,1)S(1)}, bf16[48,1024]{1,0:T(8,128)(2,1)S(1)}, u32[]{:S(2)}, u32[]{:S(2)}) collective-permute-start(bf16[48,1024]{1,0:T(8,128)(2,1)S(1)} %collective-permute-done.18.refs_2_), channel_id=1, source_target_pairs={{0,4},{4,0},{8,12},{12,8},{1,5},{5,1},{9,13},{13,9},{2,6},{6,2},{1... | collective-permute-start | bytes 294920 | tf_op jit(solution)/shard_map/ppermute | solution.py:240
  39.4 1.9 %collective-permute-start.23 = (bf16[48,1024]{1,0:T(8,128)(2,1)S(1)}, bf16[48,1024]{1,0:T(8,128)(2,1)S(1)}, u32[]{:S(2)}, u32[]{:S(2)}) collective-permute-start(bf16[48,1024]{1,0:T(8,128)(2,1)S(1)} %collective-permute-done.19.refs_3_), channel_id=1, source_target_pairs={{0,4},{4,0},{8,12},{12,8},{1,5},{5,1},{9,13},{13,9},{2,6},{6,2},{1... | collective-permute-start | bytes 294920 | tf_op jit(solution)/shard_map/ppermute | solution.py:240
  40.9 1.3 %collective-permute-start.20 = (bf16[48,1024]{1,0:T(8,128)(2,1)S(1)}, bf16[48,1024]{1,0:T(8,128)(2,1)S(1)}, u32[]{:S(2)}, u32[]{:S(2)}) collective-permute-start(bf16[48,1024]{1,0:T(8,128)(2,1)S(1)} %get-tuple-element.89.refs_0_), channel_id=1, source_target_pairs={{0,4},{4,0},{8,12},{12,8},{1,5},{5,1},{9,13},{13,9},{2,6},{6,2},{1... | collective-permute-start | bytes 294920 | tf_op jit(solution)/shard_map/ppermute | solution.py:240
  40.9 11.9 %collective-permute-start.24 = (bf16[192,512]{1,0:T(8,128)(2,1)S(1)}, bf16[192,512]{1,0:T(8,128)(2,1)S(1)}, u32[]{:S(2)}, u32[]{:S(2)}) collective-permute-start(bf16[192,512]{1,0:T(8,128)(2,1)S(1)} %collective-permute-done.16.refs_2_), channel_id=1, source_target_pairs={{0,1},{1,0},{2,3},{3,2},{4,5},{5,4},{6,7},{7,6},{8,9},{9,8},{10,11... | collective-permute-start | bytes 589832 | tf_op jit(solution)/shard_map/ppermute | solution.py:279
  42.2 16.5 %collective-permute-start.25 = (bf16[192,512]{1,0:T(8,128)(2,1)S(1)}, bf16[192,512]{1,0:T(8,128)(2,1)S(1)}, u32[]{:S(2)}, u32[]{:S(2)}) collective-permute-start(bf16[192,512]{1,0:T(8,128)(2,1)S(1)} %add_blocks.3.refs_0_), channel_id=1, source_target_pairs={{0,1},{1,0},{2,3},{3,2},{4,5},{5,4},{6,7},{7,6},{8,9},{9,8},{10,11... | collective-permute-start | bytes 589832 | tf_op jit(solution)/shard_map/ppermute | solution.py:279
  43.1 15.6 %collective-permute-start.26 = (bf16[192,512]{1,0:T(8,128)(2,1)S(1)}, bf16[192,512]{1,0:T(8,128)(2,1)S(1)}, u32[]{:S(2)}, u32[]{:S(2)}) collective-permute-start(bf16[192,512]{1,0:T(8,128)(2,1)S(1)} %add_blocks.3.refs_0_), channel_id=1, source_target_pairs={{0,2},{1,3},{2,0},{3,1},{4,6},{5,7},{6,4},{7,5},{8,10},{9,11},{10,... | collective-permute-start | bytes 589832 | tf_op jit(solution)/shard_map/ppermute | solution.py:279
  54.5 3.2 %collective-permute-start.27 = (f32[8,512]{1,0:T(8,128)S(1)}, f32[8,512]{1,0:T(8,128)S(1)}, u32[]{:S(2)}, u32[]{:S(2)}) collective-permute-start(f32[8,512]{1,0:T(8,128)S(1)} %get-tuple-element.105.refs_4_), channel_id=1, source_target_pairs={{0,4},{4,8},{8,12},{12,0},{1,5},{5,9},{9,13},{13,1},{2,6},{6,10},{... | collective-permute-start | bytes 49160 | tf_op jit(solution)/shard_map/ppermute | solution.py:364
  54.5 3.8 %collective-permute-start.28 = (f32[8,512]{1,0:T(8,128)S(1)}, f32[8,512]{1,0:T(8,128)S(1)}, u32[]{:S(2)}, u32[]{:S(2)}) collective-permute-start(f32[8,512]{1,0:T(8,128)S(1)} %get-tuple-element.105.refs_4_), channel_id=1, source_target_pairs={{0,8},{4,12},{8,0},{12,4},{1,9},{5,13},{9,1},{13,5},{2,10},{6,14},... | collective-permute-start | bytes 49160 | tf_op jit(solution)/shard_map/ppermute | solution.py:364
  55.8 2.9 %collective-permute-start.29 = (f32[8,512]{1,0:T(8,128)S(1)}, f32[8,512]{1,0:T(8,128)S(1)}, u32[]{:S(2)}, u32[]{:S(2)}) collective-permute-start(f32[8,512]{1,0:T(8,128)S(1)} %get-tuple-element.105.refs_4_), channel_id=1, source_target_pairs={{0,12},{4,0},{8,4},{12,8},{1,13},{5,1},{9,5},{13,9},{2,14},{6,2},{... | collective-permute-start | bytes 49160 | tf_op jit(solution)/shard_map/ppermute | solution.py:364
  58.7 7.6 %collective-permute-start.30 = (bf16[192,512]{1,0:T(8,128)(2,1)S(1)}, bf16[192,512]{1,0:T(8,128)(2,1)S(1)}, u32[]{:S(2)}, u32[]{:S(2)}) collective-permute-start(bf16[192,512]{1,0:T(8,128)(2,1)S(1)} %collective-permute-done.26.refs_2_), channel_id=1, source_target_pairs={{0,1},{1,0},{2,3},{3,2},{4,5},{5,4},{6,7},{7,6},{8,9},{9,8},{10,11... | collective-permute-start | bytes 589832 | tf_op jit(solution)/shard_map/ppermute | solution.py:279

commit v11 on v10

--- a/solution.py
+++ b/solution.py
@@ -273,11 +273,9 @@
             2 * slots * width,
         )
 
-    def across(parts, dz):
-        if columns & (columns - 1) == 0:
-            hop = dz & -dz
-            return lax.ppermute(parts[dz - hop], "expert", [(z, z ^ hop) for z in range(columns)])
-        return lax.ppermute(parts[0], "expert", [(z, (z + dz) % columns) for z in range(columns)])
+    def across(parts, dz, first=0):
+        pairs = [(partner_column(z, dz - first, columns), z) for z in range(columns)]
+        return lax.ppermute(parts[first], "expert", pairs)
 
     direct = [dz for dz in range(1, columns) if dz & (dz - 1) == 0][::-1]
     later = [dz for dz in range(1, columns) if dz not in direct]
@@ -330,10 +328,10 @@
     back_pieces = give_back(backs)
     back_pieces[0], out_parts = after(back_pieces[0], out_parts)
     for dz in later:
-        out_parts[dz] = across(out_parts, dz)
+        out_parts[dz] = across(out_parts, dz, dz & (dz - 1))
     back_rows = add_blocks(swap(back_pieces))
     back_parts = {0: back_rows}
-    for dz in direct:
+    for dz in direct + later:
         back_parts[dz] = across(back_parts, dz)
     _, out_parts = after(back_rows, out_parts)
 
@@ -362,9 +360,6 @@
     for dt in range(1, groups):
         pairs = [(t, (t + dt) % groups) for t in range(groups)]
         gate_parts.append(lax.ppermute(gate_part, "tensor", pairs))
-    back_parts, gate_parts = after(back_parts, gate_parts)
-    for dz in later:
-        back_parts[dz] = across(back_parts, dz)
     grad_tokens, grad_gates = call(
         functools.partial(combine_kernel, columns),
         "combine",

time: 67.9 us -> 63.3 us (0.932)
  waiting for transfers between devices: 28.7 us -> 24.1 us
    ppermute x6, waiting for transfers between devices: 16.2 us -> 9.76 us  [across(): return lax.ppermute(parts[first], 'expert', pairs)]
    ppermute x3, waiting for transfers between devices: 1.44 us -> 3.29 us  [body(): gate_parts.append(lax.ppermute(gate_part, 'tensor', pairs))]
    ppermute x3, starting transfers between devices: 2.75 us -> 1.32 us  [body(): gate_parts.append(lax.ppermute(gate_part, 'tensor', pairs))]
    ppermute x6, starting transfers between devices: 7.79 us -> 9.13 us  [across(): return lax.ppermute(parts[first], 'expert', pairs)]
where the time goes in v11:
time: 63.3 us; the launch traced here: 63 us
  starting transfers between devices  28 us (44%)
  waiting for transfers between devices  24.1 us (38%)
  Pallas kernels  9.26 us (15%)
  local copies, waits for them, and re-layouts  0.83 us (1%)
  between operations  0.75 us (1%)
    ppermute x12, starting transfers between devices, to_chip(): return lax.ppermute(value, ('dp', 'tensor'), pairs)  16.3 us
    ppermute x6, waiting for transfers between devices, across(): return lax.ppermute(parts[first], 'expert', pairs)  9.76 us
    pallas_call x10, Pallas kernels, call(): pl.pallas_call(kernel, out_shape=out_shape, in_specs=[spec] * len(operand...  9.26 us
    ppermute x6, starting transfers between devices, across(): return lax.ppermute(parts[first], 'expert', pairs)  9.13 us
    ppermute x12, waiting for transfers between devices, to_chip(): return lax.ppermute(value, ('dp', 'tensor'), pairs)  8.16 us
    ppermute x3, waiting for transfers between devices, body(): gate_parts.append(lax.ppermute(gate_part, 'tensor', pairs))  3.29 us
    ppermute x10, waiting for transfers between devices, to_core(): return lax.ppermute(value, 'tensor', pairs)  2.94 us
    ppermute x3, starting transfers between devices, body(): gate_parts.append(lax.ppermute(gate_part, 'tensor', pairs))  1.32 us
  transfers between devices with their start and end apart: 31, of which 15 were waited for; matrix products, arithmetic and copies ran while one was open for 0% of the time, Pallas kernels for 12%

profile of v11, /device:TPU:0, one launch (start us, length us, event | category | flops | bytes accessed | tf_op | source)
XLA Modules:
  0.0 63.0 jit_solution(2750871381567179013)
XLA Ops:
  0.6 0.5 collective-permute-start
  1.1 0.1 collective-permute-start.1
  1.2 0.7 %copy-done.4 = s32[512,8]{0,1:T(8,128)S(1)} copy-done((s32[512,8]{0,1:T(8,128)S(1)}, s32[512,8]{0,1:T(8,128)}, u32[]{:S(2)}) %copy-start.4) | copy-done | bytes 16408
  1.9 0.1 number.1.key_ref
  2.1 0.8 %collective-permute-done.refs_1_ = bf16[512,512]{1,0:T(8,128)(2,1)S(1)} collective-permute-done((bf16[512,512]{1,0:T(8,128)(2,1)}, bf16[512,512]{1,0:T(8,128)(2,1)S(1)}, u32[]{:S(2)}, u32[]{:S(2)}) %collective-permute-start) | collective-permute-done | bytes 524320 | tf_op jit(solution)/shard_map/ppermute | solution.py:240
  2.9 0.1 copy-done.7
  3.0 0.3 pick.2
  3.3 3.0 %collective-permute-start.2 = (bf16[48,1024]{1,0:T(8,128)(2,1)S(1)}, bf16[48,1024]{1,0:T(8,128)(2,1)S(1)}, u32[]{:S(2)}, u32[]{:S(2)}) collective-permute-start(bf16[48,1024]{1,0:T(8,128)(2,1)S(1)} %get-tuple-element.54), channel_id=1, source_target_pairs={{0,8},{4,12},{8,0},{12,4},{16,24},{20,28},{24,16},{28,20},{1,9},{5... | collective-permute-start | bytes 294920 | tf_op jit(solution)/shard_map/ppermute | solution.py:250
  6.3 1.5 %collective-permute-start.4 = (bf16[48,1024]{1,0:T(8,128)(2,1)S(1)}, bf16[48,1024]{1,0:T(8,128)(2,1)S(1)}, u32[]{:S(2)}, u32[]{:S(2)}) collective-permute-start(bf16[48,1024]{1,0:T(8,128)(2,1)S(1)} %get-tuple-element.54), channel_id=1, source_target_pairs={{0,24},{4,28},{8,16},{12,20},{16,8},{20,12},{24,0},{28,4},{1,25},{... | collective-permute-start | bytes 294920 | tf_op jit(solution)/shard_map/ppermute | solution.py:250
  7.8 0.1 collective-permute-start.3
  7.9 0.3 pick.3
  8.2 2.0 %collective-permute-start.5 = (bf16[48,1024]{1,0:T(8,128)(2,1)S(1)}, bf16[48,1024]{1,0:T(8,128)(2,1)S(1)}, u32[]{:S(2)}, u32[]{:S(2)}) collective-permute-start(bf16[48,1024]{1,0:T(8,128)(2,1)S(1)} %get-tuple-element.60), channel_id=1, source_target_pairs={{0,8},{4,12},{8,0},{12,4},{16,24},{20,28},{24,16},{28,20},{1,9},{5... | collective-permute-start | bytes 294920 | tf_op jit(solution)/shard_map/ppermute | solution.py:250
  10.1 1.5 %collective-permute-start.6 = (bf16[48,1024]{1,0:T(8,128)(2,1)S(1)}, bf16[48,1024]{1,0:T(8,128)(2,1)S(1)}, u32[]{:S(2)}, u32[]{:S(2)}) collective-permute-start(bf16[48,1024]{1,0:T(8,128)(2,1)S(1)} %get-tuple-element.64.refs_0_), channel_id=1, source_target_pairs={{0,16},{4,20},{8,24},{12,28},{16,0},{20,4},{24,8},{28,12},{1,17},{... | collective-permute-start | bytes 294920 | tf_op jit(solution)/shard_map/ppermute | solution.py:250
  11.7 1.2 %collective-permute-start.7 = (bf16[48,1024]{1,0:T(8,128)(2,1)S(1)}, bf16[48,1024]{1,0:T(8,128)(2,1)S(1)}, u32[]{:S(2)}, u32[]{:S(2)}) collective-permute-start(bf16[48,1024]{1,0:T(8,128)(2,1)S(1)} %get-tuple-element.60), channel_id=1, source_target_pairs={{0,24},{4,28},{8,16},{12,20},{16,8},{20,12},{24,0},{28,4},{1,25},{... | collective-permute-start | bytes 294920 | tf_op jit(solution)/shard_map/ppermute | solution.py:250
  12.9 2.9 %collective-permute-done.3.refs_2_ = bf16[48,1024]{1,0:T(8,128)(2,1)S(1)} collective-permute-done((bf16[48,1024]{1,0:T(8,128)(2,1)S(1)}, bf16[48,1024]{1,0:T(8,128)(2,1)S(1)}, u32[]{:S(2)}, u32[]{:S(2)}) %collective-permute-start.3) | collective-permute-done | bytes 98336 | tf_op jit(solution)/shard_map/ppermute | solution.py:250
  15.8 2.6 %forward.1 = (f32[96,768]{1,0:T(8,128)S(1)}, f32[96,768]{1,0:T(8,128)S(1)}, bf16[48,1024]{1,0:T(8,128)(2,1)S(1)}, bf16[48,1024]{1,0:T(8,128)(2,1)S(1)}, bf16[48,...) custom-call(bf16[48,1024]{1,0:T(8,128)(2,1)S(1)} %get-tuple-element.53.refs_0_, ...), custom_call_target="tpu_custom_call" | custom-call | flops 905969664 | bytes 10813440 | tf_op jit(solution)/shard_map/forward/pallas_call | solution.py:23
  18.4 0.2 collective-permute-start.9
  18.7 1.8 %collective-permute-start.8 = (bf16[48,1024]{1,0:T(8,128)(2,1)S(1)}, bf16[48,1024]{1,0:T(8,128)(2,1)S(1)}, u32[]{:S(2)}, u32[]{:S(2)}) collective-permute-start(bf16[48,1024]{1,0:T(8,128)(2,1)S(1)} %get-tuple-element.62), channel_id=1, source_target_pairs={{0,8},{4,12},{8,0},{12,4},{16,24},{20,28},{24,16},{28,20},{1,9},{5... | collective-permute-start | bytes 294920 | tf_op jit(solution)/shard_map/ppermute | solution.py:250
  20.5 1.5 %collective-permute-start.10 = (bf16[48,1024]{1,0:T(8,128)(2,1)S(1)}, bf16[48,1024]{1,0:T(8,128)(2,1)S(1)}, u32[]{:S(2)}, u32[]{:S(2)}) collective-permute-start(bf16[48,1024]{1,0:T(8,128)(2,1)S(1)} %get-tuple-element.75), channel_id=1, source_target_pairs={{0,24},{4,28},{8,16},{12,20},{16,8},{20,12},{24,0},{28,4},{1,25},{... | collective-permute-start | bytes 294920 | tf_op jit(solution)/shard_map/ppermute | solution.py:250
  22.0 2.4 %backward.1 = (bf16[48,1024]{1,0:T(8,128)(2,1)S(1)}, bf16[48,1024]{1,0:T(8,128)(2,1)S(1)}, bf16[48,1024]{1,0:T(8,128)(2,1)S(1)}, bf16[48,1024]{1,0:T(8,128)(2,1)S(1)}) custom-call(bf16[48,1024]{1,0:T(8,128)(2,1)S(1)} %get-tuple-element.64.refs_0_, bf16[48,1024]{1,0:T(8,128)(2,1)S(1)} %collective-permute-done.5.refs_1_, ...), custom_call_target="tpu_custom_call" | custom-call | flops 905969664 | bytes 10813440 | tf_op jit(solution)/shard_map/backward/pallas_call | solution.py:23
  24.5 0.6 collective-permute-start.13
  25.0 0.1 collective-permute-start.12
  25.1 0.9 %collective-permute-done.10.refs_3_ = bf16[48,1024]{1,0:T(8,128)(2,1)S(1)} collective-permute-done((bf16[48,1024]{1,0:T(8,128)(2,1)S(1)}, bf16[48,1024]{1,0:T(8,128)(2,1)S(1)}, u32[]{:S(2)}, u32[]{:S(2)}) %collective-permute-start.10) | collective-permute-done | bytes 98336 | tf_op jit(solution)/shard_map/ppermute | solution.py:250
  26.0 0.3 collective-permute-done.12.refs_5_
  26.4 1.0 %collective-permute-done.14.refs_7_ = bf16[48,1024]{1,0:T(8,128)(2,1)S(1)} collective-permute-done((bf16[48,1024]{1,0:T(8,128)(2,1)S(1)}, bf16[48,1024]{1,0:T(8,128)(2,1)S(1)}, u32[]{:S(2)}, u32[]{:S(2)}) %collective-permute-start.14) | collective-permute-done | bytes 98336 | tf_op jit(solution)/shard_map/ppermute | solution.py:240
  27.4 1.6 %collective-permute-start.15 = (bf16[192,512]{1,0:T(8,128)(2,1)S(1)}, bf16[192,512]{1,0:T(8,128)(2,1)S(1)}, u32[]{:S(2)}, u32[]{:S(2)}) collective-permute-start(bf16[192,512]{1,0:T(8,128)(2,1)S(1)} %add_blocks.2.refs_0_), channel_id=1, source_target_pairs={{1,0},{0,1},{3,2},{2,3},{5,4},{4,5},{7,6},{6,7},{9,8},{8,9},{11,10... | collective-permute-start | bytes 589832 | tf_op jit(solution)/shard_map/ppermute | solution.py:278
  29.0 2.6 %collective-permute-start.16 = (bf16[192,512]{1,0:T(8,128)(2,1)S(1)}, bf16[192,512]{1,0:T(8,128)(2,1)S(1)}, u32[]{:S(2)}, u32[]{:S(2)}) collective-permute-start(bf16[192,512]{1,0:T(8,128)(2,1)S(1)} %add_blocks.2.refs_0_), channel_id=1, source_target_pairs={{2,0},{3,1},{0,2},{1,3},{6,4},{7,5},{4,6},{5,7},{10,8},{11,9},{8,1... | collective-permute-start | bytes 589832 | tf_op jit(solution)/shard_map/ppermute | solution.py:278
  31.6 1.2 %collective-permute-start.17 = (bf16[48,1024]{1,0:T(8,128)(2,1)S(1)}, bf16[48,1024]{1,0:T(8,128)(2,1)S(1)}, u32[]{:S(2)}, u32[]{:S(2)}) collective-permute-start(bf16[48,1024]{1,0:T(8,128)(2,1)S(1)} %get-tuple-element.83), channel_id=1, source_target_pairs={{0,8},{4,12},{8,0},{12,4},{16,24},{20,28},{24,16},{28,20},{1,9},{5... | collective-permute-start | bytes 294920 | tf_op jit(solution)/shard_map/ppermute | solution.py:250
  32.9 0.8 %collective-permute-start.18 = (bf16[48,1024]{1,0:T(8,128)(2,1)S(1)}, bf16[48,1024]{1,0:T(8,128)(2,1)S(1)}, u32[]{:S(2)}, u32[]{:S(2)}) collective-permute-start(bf16[48,1024]{1,0:T(8,128)(2,1)S(1)} %get-tuple-element.84), channel_id=1, source_target_pairs={{0,16},{4,20},{8,24},{12,28},{16,0},{20,4},{24,8},{28,12},{1,17},{... | collective-permute-start | bytes 294920 | tf_op jit(solution)/shard_map/ppermute | solution.py:250
  33.7 1.4 %collective-permute-start.19 = (bf16[48,1024]{1,0:T(8,128)(2,1)S(1)}, bf16[48,1024]{1,0:T(8,128)(2,1)S(1)}, u32[]{:S(2)}, u32[]{:S(2)}) collective-permute-start(bf16[48,1024]{1,0:T(8,128)(2,1)S(1)} %get-tuple-element.85), channel_id=1, source_target_pairs={{0,24},{4,28},{8,16},{12,20},{16,8},{20,12},{24,0},{28,4},{1,25},{... | collective-permute-start | bytes 294920 | tf_op jit(solution)/shard_map/ppermute | solution.py:250
  35.1 1.5 %collective-permute-done.17.refs_1_ = bf16[48,1024]{1,0:T(8,128)(2,1)S(1)} collective-permute-done((bf16[48,1024]{1,0:T(8,128)(2,1)S(1)}, bf16[48,1024]{1,0:T(8,128)(2,1)S(1)}, u32[]{:S(2)}, u32[]{:S(2)}) %collective-permute-start.17) | collective-permute-done | bytes 98336 | tf_op jit(solution)/shard_map/ppermute | solution.py:250
  36.6 1.8 %collective-permute-done.18.refs_2_ = bf16[48,1024]{1,0:T(8,128)(2,1)S(1)} collective-permute-done((bf16[48,1024]{1,0:T(8,128)(2,1)S(1)}, bf16[48,1024]{1,0:T(8,128)(2,1)S(1)}, u32[]{:S(2)}, u32[]{:S(2)}) %collective-permute-start.18) | collective-permute-done | bytes 98336 | tf_op jit(solution)/shard_map/ppermute | solution.py:250
  38.4 1.0 %collective-permute-done.19.refs_3_ = bf16[48,1024]{1,0:T(8,128)(2,1)S(1)} collective-permute-done((bf16[48,1024]{1,0:T(8,128)(2,1)S(1)}, bf16[48,1024]{1,0:T(8,128)(2,1)S(1)}, u32[]{:S(2)}, u32[]{:S(2)}) %collective-permute-start.19) | collective-permute-done | bytes 98336 | tf_op jit(solution)/shard_map/ppermute | solution.py:250
  39.4 1.4 %collective-permute-done.16.refs_2_ = bf16[192,512]{1,0:T(8,128)(2,1)S(1)} collective-permute-done((bf16[192,512]{1,0:T(8,128)(2,1)S(1)}, bf16[192,512]{1,0:T(8,128)(2,1)S(1)}, u32[]{:S(2)}, u32[]{:S(2)}) %collective-permute-start.16) | collective-permute-done | bytes 196640 | tf_op jit(solution)/shard_map/ppermute | solution.py:278
  40.9 0.4 collective-permute-start.24
  41.3 0.8 %collective-permute-done.20.refs_4_ = bf16[48,1024]{1,0:T(8,128)(2,1)S(1)} collective-permute-done((bf16[48,1024]{1,0:T(8,128)(2,1)S(1)}, bf16[48,1024]{1,0:T(8,128)(2,1)S(1)}, u32[]{:S(2)}, u32[]{:S(2)}) %collective-permute-start.20) | collective-permute-done | bytes 98336 | tf_op jit(solution)/shard_map/ppermute | solution.py:240
  42.2 0.8 %collective-permute-start.25 = (bf16[192,512]{1,0:T(8,128)(2,1)S(1)}, bf16[192,512]{1,0:T(8,128)(2,1)S(1)}, u32[]{:S(2)}, u32[]{:S(2)}) collective-permute-start(bf16[192,512]{1,0:T(8,128)(2,1)S(1)} %add_blocks.3.refs_0_), channel_id=1, source_target_pairs={{1,0},{0,1},{3,2},{2,3},{5,4},{4,5},{7,6},{6,7},{9,8},{8,9},{11,10... | collective-permute-start | bytes 589832 | tf_op jit(solution)/shard_map/ppermute | solution.py:278
  43.1 2.3 %collective-permute-start.26 = (bf16[192,512]{1,0:T(8,128)(2,1)S(1)}, bf16[192,512]{1,0:T(8,128)(2,1)S(1)}, u32[]{:S(2)}, u32[]{:S(2)}) collective-permute-start(bf16[192,512]{1,0:T(8,128)(2,1)S(1)} %add_blocks.3.refs_0_), channel_id=1, source_target_pairs={{2,0},{3,1},{0,2},{1,3},{6,4},{7,5},{4,6},{5,7},{10,8},{11,9},{8,1... | collective-permute-start | bytes 589832 | tf_op jit(solution)/shard_map/ppermute | solution.py:278
  45.3 1.3 %collective-permute-start.27 = (bf16[192,512]{1,0:T(8,128)(2,1)S(1)}, bf16[192,512]{1,0:T(8,128)(2,1)S(1)}, u32[]{:S(2)}, u32[]{:S(2)}) collective-permute-start(bf16[192,512]{1,0:T(8,128)(2,1)S(1)} %add_blocks.3.refs_0_), channel_id=1, source_target_pairs={{3,0},{2,1},{1,2},{0,3},{7,4},{6,5},{5,6},{4,7},{11,8},{10,9},{9,1... | collective-permute-start | bytes 589832 | tf_op jit(solution)/shard_map/ppermute | solution.py:278
  46.7 0.3 weights.1.weight_ref
  47.0 5.8 %collective-permute-done.24.refs_3_ = bf16[192,512]{1,0:T(8,128)(2,1)S(1)} collective-permute-done((bf16[192,512]{1,0:T(8,128)(2,1)S(1)}, bf16[192,512]{1,0:T(8,128)(2,1)S(1)}, u32[]{:S(2)}, u32[]{:S(2)}) %collective-permute-start.24) | collective-permute-done | bytes 196640 | tf_op jit(solution)/shard_map/ppermute | solution.py:278
  52.8 1.7 %combine_gate.1 = (bf16[512,512]{1,0:T(8,128)(2,1)}, f32[8,512]{1,0:T(8,128)S(1)}) custom-call(bf16[512,768]{1,0:T(8,128)(2,1)S(1)} %weights.1.weight_ref, s32[8,512]{1,0:T(8,128)S(1)} %bitcast.5, f32[16,512]{1,0:T(8,128)S(1)} %number.1.key_ref, bf16[512,512]{1,0:T(8,128)(2,1)S(1)} %copy-done.3, bf16[192,512]{1,0:T(8,128)(2,1)S(1)} %add_blocks.2.refs_0_, ...), custom_call_target="tpu_custom_call" | custom-call | bytes 2686976 | tf_op jit(solution)/shard_map/combine_gate/pallas_call | solution.py:23
  54.5 1.3 %collective-permute-start.29 = (f32[8,512]{1,0:T(8,128)S(1)}, f32[8,512]{1,0:T(8,128)S(1)}, u32[]{:S(2)}, u32[]{:S(2)}) collective-permute-start(f32[8,512]{1,0:T(8,128)S(1)} %get-tuple-element.94.refs_4_), channel_id=1, source_target_pairs={{0,8},{4,12},{8,0},{12,4},{1,9},{5,13},{9,1},{13,5},{2,10},{6,14},... | collective-permute-start | bytes 49160 | tf_op jit(solution)/shard_map/ppermute | solution.py:362
  55.8 1.8 %collective-permute-done.28.refs_5_ = f32[8,512]{1,0:T(8,128)S(1)} collective-permute-done((f32[8,512]{1,0:T(8,128)S(1)}, f32[8,512]{1,0:T(8,128)S(1)}, u32[]{:S(2)}, u32[]{:S(2)}) %collective-permute-start.28) | collective-permute-done | bytes 16416 | tf_op jit(solution)/shard_map/ppermute | solution.py:362
  57.7 0.6 collective-permute-done.29.refs_6_
  58.3 0.8 %collective-permute-done.30.refs_7_ = f32[8,512]{1,0:T(8,128)S(1)} collective-permute-done((f32[8,512]{1,0:T(8,128)S(1)}, f32[8,512]{1,0:T(8,128)S(1)}, u32[]{:S(2)}, u32[]{:S(2)}) %collective-permute-start.30) | collective-permute-done | bytes 16416 | tf_op jit(solution)/shard_map/ppermute | solution.py:362
  59.1 2.5 %collective-permute-done.27.refs_3_ = bf16[192,512]{1,0:T(8,128)(2,1)S(1)} collective-permute-done((bf16[192,512]{1,0:T(8,128)(2,1)S(1)}, bf16[192,512]{1,0:T(8,128)(2,1)S(1)}, u32[]{:S(2)}, u32[]{:S(2)}) %collective-permute-start.27) | collective-permute-done | bytes 196640 | tf_op jit(solution)/shard_map/ppermute | solution.py:278
  61.7 1.4 %combine.1 = (bf16[512,512]{1,0:T(8,128)(2,1)}, f32[8,512]{1,0:T(8,128)}) custom-call(bf16[512,768]{1,0:T(8,128)(2,1)S(1)} %weights.1.weight_ref, bf16[192,512]{1,0:T(8,128)(2,1)S(1)} %add_blocks.3.refs_0_, bf16[192,512]{1,0:T(8,128)(2,1)S(1)} %collective-permute-done.25.refs_1_, bf16[192,512]{1,0:T(8,128)(2,1)S(1)} %collective-permute-done.26.refs_2_, ...), custom_call_target="tpu_custom_call" | custom-call | flops 402653184 | bytes 2179072 | tf_op jit(solution)/shard_map/combine/pallas_call | solution.py:23
  (40 shorter events, 0.2 us)
Async XLA Ops:
  0.6 2.3 %collective-permute-start = (bf16[512,512]{1,0:T(8,128)(2,1)}, bf16[512,512]{1,0:T(8,128)(2,1)S(1)}, u32[]{:S(2)}, u32[]{:S(2)}) collective-permute-start(bf16[512,512]{1,0:T(8,128)(2,1)} %refs_0_.2), channel_id=1, source_target_pairs={{0,4},{4,0},{8,12},{12,8},{1,5},{5,1},{9,13},{13,9},{2,6},{6,2},{1... | collective-permute-start | bytes 1572872 | tf_op jit(solution)/shard_map/ppermute | solution.py:240
  1.1 6.7 %collective-permute-start.1 = (bf16[512,512]{1,0:T(8,128)(2,1)}, bf16[512,512]{1,0:T(8,128)(2,1)S(1)}, u32[]{:S(2)}, u32[]{:S(2)}) collective-permute-start(bf16[512,512]{1,0:T(8,128)(2,1)} %grads_ref.1), channel_id=1, source_target_pairs={{0,4},{4,0},{8,12},{12,8},{1,5},{5,1},{9,13},{13,9},{2,6},{6,2},{1... | collective-permute-start | bytes 1572872 | tf_op jit(solution)/shard_map/ppermute | solution.py:240
  1.2 0.7 %copy-start.4 = (s32[512,8]{0,1:T(8,128)S(1)}, s32[512,8]{0,1:T(8,128)}, u32[]{:S(2)}) copy-start(s32[512,8]{0,1:T(8,128)} %param.9) | copy-start | bytes 49156
  1.9 1.0 %copy-start.7 = (bf16[512,512]{1,0:T(8,128)(2,1)S(1)}, bf16[512,512]{1,0:T(8,128)(2,1)}, u32[]{:S(2)}) copy-start(bf16[512,512]{1,0:T(8,128)(2,1)} %refs_0_.2) | copy-start | bytes 1572868
  2.1 5.8 %copy-start.3 = (bf16[512,512]{1,0:T(8,128)(2,1)S(1)}, bf16[512,512]{1,0:T(8,128)(2,1)}, u32[]{:S(2)}) copy-start(bf16[512,512]{1,0:T(8,128)(2,1)} %grads_ref.1) | copy-start | bytes 1572868
  3.3 8.4 %collective-permute-start.2 = (bf16[48,1024]{1,0:T(8,128)(2,1)S(1)}, bf16[48,1024]{1,0:T(8,128)(2,1)S(1)}, u32[]{:S(2)}, u32[]{:S(2)}) collective-permute-start(bf16[48,1024]{1,0:T(8,128)(2,1)S(1)} %get-tuple-element.54), channel_id=1, source_target_pairs={{0,8},{4,12},{8,0},{12,4},{16,24},{20,28},{24,16},{28,20},{1,9},{5... | collective-permute-start | bytes 294920 | tf_op jit(solution)/shard_map/ppermute | solution.py:250
  6.3 9.5 %collective-permute-start.4 = (bf16[48,1024]{1,0:T(8,128)(2,1)S(1)}, bf16[48,1024]{1,0:T(8,128)(2,1)S(1)}, u32[]{:S(2)}, u32[]{:S(2)}) collective-permute-start(bf16[48,1024]{1,0:T(8,128)(2,1)S(1)} %get-tuple-element.54), channel_id=1, source_target_pairs={{0,24},{4,28},{8,16},{12,20},{16,8},{20,12},{24,0},{28,4},{1,25},{... | collective-permute-start | bytes 294920 | tf_op jit(solution)/shard_map/ppermute | solution.py:250
  7.8 8.1 %copy-start = (bf16[1,768,2048]{2,1,0:T(8,128)(2,1)S(1)}, bf16[1,768,2048]{2,1,0:T(8,128)(2,1)}, u32[]{:S(2)}) copy-start(bf16[1,768,2048]{2,1,0:T(8,128)(2,1)} %refs_4_.3) | copy-start | bytes 9437188
  7.8 8.1 %copy-start.1 = (bf16[1,768,2048]{2,1,0:T(8,128)(2,1)S(1)}, bf16[1,768,2048]{2,1,0:T(8,128)(2,1)}, u32[]{:S(2)}) copy-start(bf16[1,768,2048]{2,1,0:T(8,128)(2,1)} %refs_5_.3) | copy-start | bytes 9437188
  7.8 8.1 %copy-start.2 = (bf16[1,768,2048]{2,1,0:T(8,128)(2,1)S(1)}, bf16[1,768,2048]{2,1,0:T(8,128)(2,1)}, u32[]{:S(2)}) copy-start(bf16[1,768,2048]{2,1,0:T(8,128)(2,1)} %refs_6_.3) | copy-start | bytes 9437188
  7.8 8.0 %collective-permute-start.3 = (bf16[48,1024]{1,0:T(8,128)(2,1)S(1)}, bf16[48,1024]{1,0:T(8,128)(2,1)S(1)}, u32[]{:S(2)}, u32[]{:S(2)}) collective-permute-start(bf16[48,1024]{1,0:T(8,128)(2,1)S(1)} %get-tuple-element.53.refs_0_), channel_id=1, source_target_pairs={{0,16},{4,20},{8,24},{12,28},{16,0},{20,4},{24,8},{28,12},{1,17},{... | collective-permute-start | bytes 294920 | tf_op jit(solution)/shard_map/ppermute | solution.py:250
  8.2 10.2 %collective-permute-start.5 = (bf16[48,1024]{1,0:T(8,128)(2,1)S(1)}, bf16[48,1024]{1,0:T(8,128)(2,1)S(1)}, u32[]{:S(2)}, u32[]{:S(2)}) collective-permute-start(bf16[48,1024]{1,0:T(8,128)(2,1)S(1)} %get-tuple-element.60), channel_id=1, source_target_pairs={{0,8},{4,12},{8,0},{12,4},{16,24},{20,28},{24,16},{28,20},{1,9},{5... | collective-permute-start | bytes 294920 | tf_op jit(solution)/shard_map/ppermute | solution.py:250
  10.1 8.3 %collective-permute-start.6 = (bf16[48,1024]{1,0:T(8,128)(2,1)S(1)}, bf16[48,1024]{1,0:T(8,128)(2,1)S(1)}, u32[]{:S(2)}, u32[]{:S(2)}) collective-permute-start(bf16[48,1024]{1,0:T(8,128)(2,1)S(1)} %get-tuple-element.64.refs_0_), channel_id=1, source_target_pairs={{0,16},{4,20},{8,24},{12,28},{16,0},{20,4},{24,8},{28,12},{1,17},{... | collective-permute-start | bytes 294920 | tf_op jit(solution)/shard_map/ppermute | solution.py:250
  11.7 6.8 %collective-permute-start.7 = (bf16[48,1024]{1,0:T(8,128)(2,1)S(1)}, bf16[48,1024]{1,0:T(8,128)(2,1)S(1)}, u32[]{:S(2)}, u32[]{:S(2)}) collective-permute-start(bf16[48,1024]{1,0:T(8,128)(2,1)S(1)} %get-tuple-element.60), channel_id=1, source_target_pairs={{0,24},{4,28},{8,16},{12,20},{16,8},{20,12},{24,0},{28,4},{1,25},{... | collective-permute-start | bytes 294920 | tf_op jit(solution)/shard_map/ppermute | solution.py:250
  18.4 6.0 %collective-permute-start.9 = (bf16[48,1024]{1,0:T(8,128)(2,1)S(1)}, bf16[48,1024]{1,0:T(8,128)(2,1)S(1)}, u32[]{:S(2)}, u32[]{:S(2)}) collective-permute-start(bf16[48,1024]{1,0:T(8,128)(2,1)S(1)} %get-tuple-element.63), channel_id=1, source_target_pairs={{0,16},{4,20},{8,24},{12,28},{16,0},{20,4},{24,8},{28,12},{1,17},{... | collective-permute-start | bytes 294920 | tf_op jit(solution)/shard_map/ppermute | solution.py:250
  18.7 6.4 %collective-permute-start.8 = (bf16[48,1024]{1,0:T(8,128)(2,1)S(1)}, bf16[48,1024]{1,0:T(8,128)(2,1)S(1)}, u32[]{:S(2)}, u32[]{:S(2)}) collective-permute-start(bf16[48,1024]{1,0:T(8,128)(2,1)S(1)} %get-tuple-element.62), channel_id=1, source_target_pairs={{0,8},{4,12},{8,0},{12,4},{16,24},{20,28},{24,16},{28,20},{1,9},{5... | collective-permute-start | bytes 294920 | tf_op jit(solution)/shard_map/ppermute | solution.py:250
  20.5 5.5 %collective-permute-start.10 = (bf16[48,1024]{1,0:T(8,128)(2,1)S(1)}, bf16[48,1024]{1,0:T(8,128)(2,1)S(1)}, u32[]{:S(2)}, u32[]{:S(2)}) collective-permute-start(bf16[48,1024]{1,0:T(8,128)(2,1)S(1)} %get-tuple-element.75), channel_id=1, source_target_pairs={{0,24},{4,28},{8,16},{12,20},{16,8},{20,12},{24,0},{28,4},{1,25},{... | collective-permute-start | bytes 294920 | tf_op jit(solution)/shard_map/ppermute | solution.py:250
  22.0 4.0 %collective-permute-start.11 = (bf16[48,1024]{1,0:T(8,128)(2,1)S(1)}, bf16[48,1024]{1,0:T(8,128)(2,1)S(1)}, u32[]{:S(2)}, u32[]{:S(2)}) collective-permute-start(bf16[48,1024]{1,0:T(8,128)(2,1)S(1)} %get-tuple-element.61.refs_0_), channel_id=1, source_target_pairs={{0,4},{4,0},{8,12},{12,8},{1,5},{5,1},{9,13},{13,9},{2,6},{6,2},{1... | collective-permute-start | bytes 294920 | tf_op jit(solution)/shard_map/ppermute | solution.py:240
  22.0 24.7 %copy-start.5 = (s32[512,8]{0,1:T(8,128)S(1)}, s32[512,8]{0,1:T(8,128)}, u32[]{:S(2)}) copy-start(s32[512,8]{0,1:T(8,128)} %param.9) | copy-start | bytes 49156
  22.0 24.7 %copy-start.6 = (f32[512,8]{0,1:T(8,128)S(1)}, f32[512,8]{0,1:T(8,128)}, u32[]{:S(2)}) copy-start(f32[512,8]{0,1:T(8,128)} %param.10) | copy-start | bytes 49156
  24.5 1.9 %collective-permute-start.13 = (bf16[48,1024]{1,0:T(8,128)(2,1)S(1)}, bf16[48,1024]{1,0:T(8,128)(2,1)S(1)}, u32[]{:S(2)}, u32[]{:S(2)}) collective-permute-start(bf16[48,1024]{1,0:T(8,128)(2,1)S(1)} %collective-permute-done.9.refs_2_), channel_id=1, source_target_pairs={{0,4},{4,0},{8,12},{12,8},{1,5},{5,1},{9,13},{13,9},{2,6},{6,2},{1... | collective-permute-start | bytes 294920 | tf_op jit(solution)/shard_map/ppermute | solution.py:240
  25.0 1.3 %collective-permute-start.12 = (bf16[48,1024]{1,0:T(8,128)(2,1)S(1)}, bf16[48,1024]{1,0:T(8,128)(2,1)S(1)}, u32[]{:S(2)}, u32[]{:S(2)}) collective-permute-start(bf16[48,1024]{1,0:T(8,128)(2,1)S(1)} %collective-permute-done.8.refs_1_), channel_id=1, source_target_pairs={{0,4},{4,0},{8,12},{12,8},{1,5},{5,1},{9,13},{13,9},{2,6},{6,2},{1... | collective-permute-start | bytes 294920 | tf_op jit(solution)/shard_map/ppermute | solution.py:240
  26.0 1.3 %collective-permute-start.14 = (bf16[48,1024]{1,0:T(8,128)(2,1)S(1)}, bf16[48,1024]{1,0:T(8,128)(2,1)S(1)}, u32[]{:S(2)}, u32[]{:S(2)}) collective-permute-start(bf16[48,1024]{1,0:T(8,128)(2,1)S(1)} %collective-permute-done.10.refs_3_), channel_id=1, source_target_pairs={{0,4},{4,0},{8,12},{12,8},{1,5},{5,1},{9,13},{13,9},{2,6},{6,2},{1... | collective-permute-start | bytes 294920 | tf_op jit(solution)/shard_map/ppermute | solution.py:240
  27.4 12.1 %collective-permute-start.15 = (bf16[192,512]{1,0:T(8,128)(2,1)S(1)}, bf16[192,512]{1,0:T(8,128)(2,1)S(1)}, u32[]{:S(2)}, u32[]{:S(2)}) collective-permute-start(bf16[192,512]{1,0:T(8,128)(2,1)S(1)} %add_blocks.2.refs_0_), channel_id=1, source_target_pairs={{1,0},{0,1},{3,2},{2,3},{5,4},{4,5},{7,6},{6,7},{9,8},{8,9},{11,10... | collective-permute-start | bytes 589832 | tf_op jit(solution)/shard_map/ppermute | solution.py:278
  29.0 11.8 %collective-permute-start.16 = (bf16[192,512]{1,0:T(8,128)(2,1)S(1)}, bf16[192,512]{1,0:T(8,128)(2,1)S(1)}, u32[]{:S(2)}, u32[]{:S(2)}) collective-permute-start(bf16[192,512]{1,0:T(8,128)(2,1)S(1)} %add_blocks.2.refs_0_), channel_id=1, source_target_pairs={{2,0},{3,1},{0,2},{1,3},{6,4},{7,5},{4,6},{5,7},{10,8},{11,9},{8,1... | collective-permute-start | bytes 589832 | tf_op jit(solution)/shard_map/ppermute | solution.py:278
  31.6 4.9 %collective-permute-start.17 = (bf16[48,1024]{1,0:T(8,128)(2,1)S(1)}, bf16[48,1024]{1,0:T(8,128)(2,1)S(1)}, u32[]{:S(2)}, u32[]{:S(2)}) collective-permute-start(bf16[48,1024]{1,0:T(8,128)(2,1)S(1)} %get-tuple-element.83), channel_id=1, source_target_pairs={{0,8},{4,12},{8,0},{12,4},{16,24},{20,28},{24,16},{28,20},{1,9},{5... | collective-permute-start | bytes 294920 | tf_op jit(solution)/shard_map/ppermute | solution.py:250
  32.9 5.5 %collective-permute-start.18 = (bf16[48,1024]{1,0:T(8,128)(2,1)S(1)}, bf16[48,1024]{1,0:T(8,128)(2,1)S(1)}, u32[]{:S(2)}, u32[]{:S(2)}) collective-permute-start(bf16[48,1024]{1,0:T(8,128)(2,1)S(1)} %get-tuple-element.84), channel_id=1, source_target_pairs={{0,16},{4,20},{8,24},{12,28},{16,0},{20,4},{24,8},{28,12},{1,17},{... | collective-permute-start | bytes 294920 | tf_op jit(solution)/shard_map/ppermute | solution.py:250
  33.7 5.8 %collective-permute-start.19 = (bf16[48,1024]{1,0:T(8,128)(2,1)S(1)}, bf16[48,1024]{1,0:T(8,128)(2,1)S(1)}, u32[]{:S(2)}, u32[]{:S(2)}) collective-permute-start(bf16[48,1024]{1,0:T(8,128)(2,1)S(1)} %get-tuple-element.85), channel_id=1, source_target_pairs={{0,24},{4,28},{8,16},{12,20},{16,8},{20,12},{24,0},{28,4},{1,25},{... | collective-permute-start | bytes 294920 | tf_op jit(solution)/shard_map/ppermute | solution.py:250
  36.6 4.8 %collective-permute-start.21 = (bf16[48,1024]{1,0:T(8,128)(2,1)S(1)}, bf16[48,1024]{1,0:T(8,128)(2,1)S(1)}, u32[]{:S(2)}, u32[]{:S(2)}) collective-permute-start(bf16[48,1024]{1,0:T(8,128)(2,1)S(1)} %collective-permute-done.17.refs_1_), channel_id=1, source_target_pairs={{0,4},{4,0},{8,12},{12,8},{1,5},{5,1},{9,13},{13,9},{2,6},{6,2},{1... | collective-permute-start | bytes 294920 | tf_op jit(solution)/shard_map/ppermute | solution.py:240
  38.4 2.9 %collective-permute-start.22 = (bf16[48,1024]{1,0:T(8,128)(2,1)S(1)}, bf16[48,1024]{1,0:T(8,128)(2,1)S(1)}, u32[]{:S(2)}, u32[]{:S(2)}) collective-permute-start(bf16[48,1024]{1,0:T(8,128)(2,1)S(1)} %collective-permute-done.18.refs_2_), channel_id=1, source_target_pairs={{0,4},{4,0},{8,12},{12,8},{1,5},{5,1},{9,13},{13,9},{2,6},{6,2},{1... | collective-permute-start | bytes 294920 | tf_op jit(solution)/shard_map/ppermute | solution.py:240
  39.4 1.9 %collective-permute-start.23 = (bf16[48,1024]{1,0:T(8,128)(2,1)S(1)}, bf16[48,1024]{1,0:T(8,128)(2,1)S(1)}, u32[]{:S(2)}, u32[]{:S(2)}) collective-permute-start(bf16[48,1024]{1,0:T(8,128)(2,1)S(1)} %collective-permute-done.19.refs_3_), channel_id=1, source_target_pairs={{0,4},{4,0},{8,12},{12,8},{1,5},{5,1},{9,13},{13,9},{2,6},{6,2},{1... | collective-permute-start | bytes 294920 | tf_op jit(solution)/shard_map/ppermute | solution.py:240
  40.9 1.3 %collective-permute-start.20 = (bf16[48,1024]{1,0:T(8,128)(2,1)S(1)}, bf16[48,1024]{1,0:T(8,128)(2,1)S(1)}, u32[]{:S(2)}, u32[]{:S(2)}) collective-permute-start(bf16[48,1024]{1,0:T(8,128)(2,1)S(1)} %get-tuple-element.82.refs_0_), channel_id=1, source_target_pairs={{0,4},{4,0},{8,12},{12,8},{1,5},{5,1},{9,13},{13,9},{2,6},{6,2},{1... | collective-permute-start | bytes 294920 | tf_op jit(solution)/shard_map/ppermute | solution.py:240
  40.9 11.9 %collective-permute-start.24 = (bf16[192,512]{1,0:T(8,128)(2,1)S(1)}, bf16[192,512]{1,0:T(8,128)(2,1)S(1)}, u32[]{:S(2)}, u32[]{:S(2)}) collective-permute-start(bf16[192,512]{1,0:T(8,128)(2,1)S(1)} %collective-permute-done.16.refs_2_), channel_id=1, source_target_pairs={{1,0},{0,1},{3,2},{2,3},{5,4},{4,5},{7,6},{6,7},{9,8},{8,9},{11,10... | collective-permute-start | bytes 589832 | tf_op jit(solution)/shard_map/ppermute | solution.py:278
  42.2 16.9 %collective-permute-start.25 = (bf16[192,512]{1,0:T(8,128)(2,1)S(1)}, bf16[192,512]{1,0:T(8,128)(2,1)S(1)}, u32[]{:S(2)}, u32[]{:S(2)}) collective-permute-start(bf16[192,512]{1,0:T(8,128)(2,1)S(1)} %add_blocks.3.refs_0_), channel_id=1, source_target_pairs={{1,0},{0,1},{3,2},{2,3},{5,4},{4,5},{7,6},{6,7},{9,8},{8,9},{11,10... | collective-permute-start | bytes 589832 | tf_op jit(solution)/shard_map/ppermute | solution.py:278
  43.1 16.1 %collective-permute-start.26 = (bf16[192,512]{1,0:T(8,128)(2,1)S(1)}, bf16[192,512]{1,0:T(8,128)(2,1)S(1)}, u32[]{:S(2)}, u32[]{:S(2)}) collective-permute-start(bf16[192,512]{1,0:T(8,128)(2,1)S(1)} %add_blocks.3.refs_0_), channel_id=1, source_target_pairs={{2,0},{3,1},{0,2},{1,3},{6,4},{7,5},{4,6},{5,7},{10,8},{11,9},{8,1... | collective-permute-start | bytes 589832 | tf_op jit(solution)/shard_map/ppermute | solution.py:278
  45.3 16.3 %collective-permute-start.27 = (bf16[192,512]{1,0:T(8,128)(2,1)S(1)}, bf16[192,512]{1,0:T(8,128)(2,1)S(1)}, u32[]{:S(2)}, u32[]{:S(2)}) collective-permute-start(bf16[192,512]{1,0:T(8,128)(2,1)S(1)} %add_blocks.3.refs_0_), channel_id=1, source_target_pairs={{3,0},{2,1},{1,2},{0,3},{7,4},{6,5},{5,6},{4,7},{11,8},{10,9},{9,1... | collective-permute-start | bytes 589832 | tf_op jit(solution)/shard_map/ppermute | solution.py:278
  54.5 3.2 %collective-permute-start.28 = (f32[8,512]{1,0:T(8,128)S(1)}, f32[8,512]{1,0:T(8,128)S(1)}, u32[]{:S(2)}, u32[]{:S(2)}) collective-permute-start(f32[8,512]{1,0:T(8,128)S(1)} %get-tuple-element.94.refs_4_), channel_id=1, source_target_pairs={{0,4},{4,8},{8,12},{12,0},{1,5},{5,9},{9,13},{13,1},{2,6},{6,10},{... | collective-permute-start | bytes 49160 | tf_op jit(solution)/shard_map/ppermute | solution.py:362
  54.5 3.8 %collective-permute-start.29 = (f32[8,512]{1,0:T(8,128)S(1)}, f32[8,512]{1,0:T(8,128)S(1)}, u32[]{:S(2)}, u32[]{:S(2)}) collective-permute-start(f32[8,512]{1,0:T(8,128)S(1)} %get-tuple-element.94.refs_4_), channel_id=1, source_target_pairs={{0,8},{4,12},{8,0},{12,4},{1,9},{5,13},{9,1},{13,5},{2,10},{6,14},... | collective-permute-start | bytes 49160 | tf_op jit(solution)/shard_map/ppermute | solution.py:362
  57.7 1.4 %collective-permute-start.30 = (f32[8,512]{1,0:T(8,128)S(1)}, f32[8,512]{1,0:T(8,128)S(1)}, u32[]{:S(2)}, u32[]{:S(2)}) collective-permute-start(f32[8,512]{1,0:T(8,128)S(1)} %get-tuple-element.94.refs_4_), channel_id=1, source_target_pairs={{0,12},{4,0},{8,4},{12,8},{1,13},{5,1},{9,5},{13,9},{2,14},{6,2},{... | collective-permute-start | bytes 49160 | tf_op jit(solution)/shard_map/ppermute | solution.py:362

commit v12 on v11

--- a/solution.py
+++ b/solution.py
@@ -250,16 +250,13 @@
         return lax.ppermute(value, ("dp", "tensor"), pairs)
 
     hops = [(db, dh) for db in range(n_dp) for dh in range(chips)]
-    first = (n_dp - 1) * chips
-    order = sorted(range(count), key=lambda index: (hops[index][0] == 0, -hops[index][1]))
 
     def dispatch(pieces):
-        arrived = {index: to_chip(pieces[hops[index][1]], *hops[index]) for index in order}
-        return [arrived[index] for index in range(count)]
+        return [to_chip(pieces[dh], db, dh) for db, dh in hops]
 
     def give_back(pieces):
-        arrived = {index: to_chip(pieces[index], *hops[index]) for index in order}
-        return [arrived[index] for index in range(count)]
+        arrived = [to_chip(piece, *hop) for piece, hop in zip(pieces, hops)]
+        return arrived[:chips] + list(lax.optimization_barrier(tuple(arrived[chips:])))
 
     def swap(pieces):
         return [to_core(piece, dc) for dc in range(cores) for piece in pieces]
@@ -319,14 +316,14 @@
         [pltpu.VMEM((tall, feats), BF16)] + [pltpu.VMEM((tall, hid_dev), BF16)] * 2,
         limit=24,
     )
-    out_pieces[first], backs = after(out_pieces[first], backs)
+    out_pieces[chips:], backs = after(out_pieces[chips:], backs)
     out_rows = add_blocks(swap(out_pieces))
     out_rows, backs = after(out_rows, backs)
     out_parts = {0: out_rows}
     for dz in direct:
         out_parts[dz] = across(out_parts, dz)
     back_pieces = give_back(backs)
-    back_pieces[0], out_parts = after(back_pieces[0], out_parts)
+    back_pieces[1], out_parts = after(back_pieces[1], out_parts)
     for dz in later:
         out_parts[dz] = across(out_parts, dz, dz & (dz - 1))
     back_rows = add_blocks(swap(back_pieces))

time: 63.3 us -> 63.8 us (level)
  starting transfers between devices: 28 us -> 28.7 us
    ppermute x10, starting transfers between devices: 1.27 us -> 2.08 us  [to_core(): return lax.ppermute(value, 'tensor', pairs)]
where the time goes in v12:
time: 63.8 us; the launch traced here: 63.6 us
  starting transfers between devices  28.7 us (45%)
  waiting for transfers between devices  24.1 us (38%)
  Pallas kernels  9.26 us (15%)
  local copies, waits for them, and re-layouts  0.83 us (1%)
  between operations  0.75 us (1%)
    ppermute x12, starting transfers between devices, to_chip(): return lax.ppermute(value, ('dp', 'tensor'), pairs)  16.3 us
    ppermute x6, waiting for transfers between devices, across(): return lax.ppermute(parts[first], 'expert', pairs)  10 us
    pallas_call x10, Pallas kernels, call(): pl.pallas_call(kernel, out_shape=out_shape, in_specs=[spec] * len(operand...  9.26 us
    ppermute x6, starting transfers between devices, across(): return lax.ppermute(parts[first], 'expert', pairs)  9.21 us
    ppermute x12, waiting for transfers between devices, to_chip(): return lax.ppermute(value, ('dp', 'tensor'), pairs)  7.94 us
    ppermute x3, waiting for transfers between devices, body(): gate_parts.append(lax.ppermute(gate_part, 'tensor', pairs))  3.52 us
    ppermute x10, waiting for transfers between devices, to_core(): return lax.ppermute(value, 'tensor', pairs)  2.58 us
    ppermute x10, starting transfers between devices, to_core(): return lax.ppermute(value, 'tensor', pairs)  2.08 us
  transfers between devices with their start and end apart: 31, of which 15 were waited for; matrix products, arithmetic and copies ran while one was open for 0% of the time, Pallas kernels for 12%

profile of v12, /device:TPU:0, one launch (start us, length us, event | category | flops | bytes accessed | tf_op | source)
XLA Modules:
  0.0 63.6 jit_solution(15142423528791167391)
XLA Ops:
  0.6 0.5 collective-permute-start
  1.2 0.7 %copy-done.4 = s32[512,8]{0,1:T(8,128)S(1)} copy-done((s32[512,8]{0,1:T(8,128)S(1)}, s32[512,8]{0,1:T(8,128)}, u32[]{:S(2)}) %copy-start.4) | copy-done | bytes 16408
  1.9 0.1 number.1.key_ref
  2.1 0.8 %collective-permute-done.refs_1_ = bf16[512,512]{1,0:T(8,128)(2,1)S(1)} collective-permute-done((bf16[512,512]{1,0:T(8,128)(2,1)}, bf16[512,512]{1,0:T(8,128)(2,1)S(1)}, u32[]{:S(2)}, u32[]{:S(2)}) %collective-permute-start) | collective-permute-done | bytes 524320 | tf_op jit(solution)/shard_map/ppermute | solution.py:240
  2.9 0.1 copy-done.7
  3.0 0.3 pick.2
  3.3 3.0 %collective-permute-start.2 = (bf16[48,1024]{1,0:T(8,128)(2,1)S(1)}, bf16[48,1024]{1,0:T(8,128)(2,1)S(1)}, u32[]{:S(2)}, u32[]{:S(2)}) collective-permute-start(bf16[48,1024]{1,0:T(8,128)(2,1)S(1)} %get-tuple-element.59), channel_id=1, source_target_pairs={{0,8},{4,12},{8,0},{12,4},{16,24},{20,28},{24,16},{28,20},{1,9},{5... | collective-permute-start | bytes 294920 | tf_op jit(solution)/shard_map/ppermute | solution.py:250
  6.3 1.5 %collective-permute-start.4 = (bf16[48,1024]{1,0:T(8,128)(2,1)S(1)}, bf16[48,1024]{1,0:T(8,128)(2,1)S(1)}, u32[]{:S(2)}, u32[]{:S(2)}) collective-permute-start(bf16[48,1024]{1,0:T(8,128)(2,1)S(1)} %get-tuple-element.59), channel_id=1, source_target_pairs={{0,24},{4,28},{8,16},{12,20},{16,8},{20,12},{24,0},{28,4},{1,25},{... | collective-permute-start | bytes 294920 | tf_op jit(solution)/shard_map/ppermute | solution.py:250
  7.8 0.1 collective-permute-start.3
  7.9 0.3 pick.3
  8.2 2.0 %collective-permute-start.5 = (bf16[48,1024]{1,0:T(8,128)(2,1)S(1)}, bf16[48,1024]{1,0:T(8,128)(2,1)S(1)}, u32[]{:S(2)}, u32[]{:S(2)}) collective-permute-start(bf16[48,1024]{1,0:T(8,128)(2,1)S(1)} %get-tuple-element.65), channel_id=1, source_target_pairs={{0,8},{4,12},{8,0},{12,4},{16,24},{20,28},{24,16},{28,20},{1,9},{5... | collective-permute-start | bytes 294920 | tf_op jit(solution)/shard_map/ppermute | solution.py:250
  10.1 1.5 %collective-permute-start.6 = (bf16[48,1024]{1,0:T(8,128)(2,1)S(1)}, bf16[48,1024]{1,0:T(8,128)(2,1)S(1)}, u32[]{:S(2)}, u32[]{:S(2)}) collective-permute-start(bf16[48,1024]{1,0:T(8,128)(2,1)S(1)} %get-tuple-element.72.refs_0_), channel_id=1, source_target_pairs={{0,16},{4,20},{8,24},{12,28},{16,0},{20,4},{24,8},{28,12},{1,17},{... | collective-permute-start | bytes 294920 | tf_op jit(solution)/shard_map/ppermute | solution.py:250
  11.7 1.2 %collective-permute-start.7 = (bf16[48,1024]{1,0:T(8,128)(2,1)S(1)}, bf16[48,1024]{1,0:T(8,128)(2,1)S(1)}, u32[]{:S(2)}, u32[]{:S(2)}) collective-permute-start(bf16[48,1024]{1,0:T(8,128)(2,1)S(1)} %get-tuple-element.65), channel_id=1, source_target_pairs={{0,24},{4,28},{8,16},{12,20},{16,8},{20,12},{24,0},{28,4},{1,25},{... | collective-permute-start | bytes 294920 | tf_op jit(solution)/shard_map/ppermute | solution.py:250
  12.9 2.9 %collective-permute-done.3.refs_2_ = bf16[48,1024]{1,0:T(8,128)(2,1)S(1)} collective-permute-done((bf16[48,1024]{1,0:T(8,128)(2,1)S(1)}, bf16[48,1024]{1,0:T(8,128)(2,1)S(1)}, u32[]{:S(2)}, u32[]{:S(2)}) %collective-permute-start.3) | collective-permute-done | bytes 98336 | tf_op jit(solution)/shard_map/ppermute | solution.py:250
  15.8 2.6 %forward.1 = (f32[96,768]{1,0:T(8,128)S(1)}, f32[96,768]{1,0:T(8,128)S(1)}, bf16[48,1024]{1,0:T(8,128)(2,1)S(1)}, bf16[48,1024]{1,0:T(8,128)(2,1)S(1)}, bf16[48,...) custom-call(bf16[48,1024]{1,0:T(8,128)(2,1)S(1)} %get-tuple-element.58.refs_0_, ...), custom_call_target="tpu_custom_call" | custom-call | flops 905969664 | bytes 10813440 | tf_op jit(solution)/shard_map/forward/pallas_call | solution.py:23
  18.4 0.2 collective-permute-start.9
  18.7 2.8 %collective-permute-start.10 = (bf16[48,1024]{1,0:T(8,128)(2,1)S(1)}, bf16[48,1024]{1,0:T(8,128)(2,1)S(1)}, u32[]{:S(2)}, u32[]{:S(2)}) collective-permute-start(bf16[48,1024]{1,0:T(8,128)(2,1)S(1)} %get-tuple-element.69), channel_id=1, source_target_pairs={{0,24},{4,28},{8,16},{12,20},{16,8},{20,12},{24,0},{28,4},{1,25},{... | collective-permute-start | bytes 294920 | tf_op jit(solution)/shard_map/ppermute | solution.py:250
  21.5 0.5 collective-permute-start.8
  22.0 2.4 %backward.1 = (bf16[48,1024]{1,0:T(8,128)(2,1)S(1)}, bf16[48,1024]{1,0:T(8,128)(2,1)S(1)}, bf16[48,1024]{1,0:T(8,128)(2,1)S(1)}, bf16[48,1024]{1,0:T(8,128)(2,1)S(1)}) custom-call(bf16[48,1024]{1,0:T(8,128)(2,1)S(1)} %get-tuple-element.72.refs_0_, bf16[48,1024]{1,0:T(8,128)(2,1)S(1)} %collective-permute-done.5.refs_1_, ...), custom_call_target="tpu_custom_call" | custom-call | flops 905969664 | bytes 10813440 | tf_op jit(solution)/shard_map/backward/pallas_call | solution.py:23
  24.5 0.1 collective-permute-done.10.refs_3_
  24.6 0.5 collective-permute-start.13
  25.1 1.1 %collective-permute-done.8.refs_1_ = bf16[48,1024]{1,0:T(8,128)(2,1)S(1)} collective-permute-done((bf16[48,1024]{1,0:T(8,128)(2,1)S(1)}, bf16[48,1024]{1,0:T(8,128)(2,1)S(1)}, u32[]{:S(2)}, u32[]{:S(2)}) %collective-permute-start.8) | collective-permute-done | bytes 98336 | tf_op jit(solution)/shard_map/ppermute | solution.py:250
  26.2 0.5 collective-permute-start.14
  26.7 0.8 %collective-permute-done.12.refs_5_ = bf16[48,1024]{1,0:T(8,128)(2,1)S(1)} collective-permute-done((bf16[48,1024]{1,0:T(8,128)(2,1)S(1)}, bf16[48,1024]{1,0:T(8,128)(2,1)S(1)}, u32[]{:S(2)}, u32[]{:S(2)}) %collective-permute-start.12) | collective-permute-done | bytes 98336 | tf_op jit(solution)/shard_map/ppermute | solution.py:240
  27.5 0.1 collective-permute-done.14.refs_7_
  27.7 1.8 %collective-permute-start.16 = (bf16[192,512]{1,0:T(8,128)(2,1)S(1)}, bf16[192,512]{1,0:T(8,128)(2,1)S(1)}, u32[]{:S(2)}, u32[]{:S(2)}) collective-permute-start(bf16[192,512]{1,0:T(8,128)(2,1)S(1)} %add_blocks.2.refs_0_), channel_id=1, source_target_pairs={{1,0},{0,1},{3,2},{2,3},{5,4},{4,5},{7,6},{6,7},{9,8},{8,9},{11,10... | collective-permute-start | bytes 589832 | tf_op jit(solution)/shard_map/ppermute | solution.py:275
  29.4 2.5 %collective-permute-start.17 = (bf16[192,512]{1,0:T(8,128)(2,1)S(1)}, bf16[192,512]{1,0:T(8,128)(2,1)S(1)}, u32[]{:S(2)}, u32[]{:S(2)}) collective-permute-start(bf16[192,512]{1,0:T(8,128)(2,1)S(1)} %add_blocks.2.refs_0_), channel_id=1, source_target_pairs={{2,0},{3,1},{0,2},{1,3},{6,4},{7,5},{4,6},{5,7},{10,8},{11,9},{8,1... | collective-permute-start | bytes 589832 | tf_op jit(solution)/shard_map/ppermute | solution.py:275
  32.0 0.4 collective-permute-start.18
  32.3 2.1 %collective-permute-start.19 = (bf16[48,1024]{1,0:T(8,128)(2,1)S(1)}, bf16[48,1024]{1,0:T(8,128)(2,1)S(1)}, u32[]{:S(2)}, u32[]{:S(2)}) collective-permute-start(bf16[48,1024]{1,0:T(8,128)(2,1)S(1)} %get-tuple-element.93), channel_id=1, source_target_pairs={{0,24},{4,28},{8,16},{12,20},{16,8},{20,12},{24,0},{28,4},{1,25},{... | collective-permute-start | bytes 294920 | tf_op jit(solution)/shard_map/ppermute | solution.py:250
  34.5 1.0 %collective-permute-start.15 = (bf16[48,1024]{1,0:T(8,128)(2,1)S(1)}, bf16[48,1024]{1,0:T(8,128)(2,1)S(1)}, u32[]{:S(2)}, u32[]{:S(2)}) collective-permute-start(bf16[48,1024]{1,0:T(8,128)(2,1)S(1)} %get-tuple-element.89), channel_id=1, source_target_pairs={{0,8},{4,12},{8,0},{12,4},{16,24},{20,28},{24,16},{28,20},{1,9},{5... | collective-permute-start | bytes 294920 | tf_op jit(solution)/shard_map/ppermute | solution.py:250
  35.5 3.1 %collective-permute-done.18.refs_2_ = bf16[48,1024]{1,0:T(8,128)(2,1)S(1)} collective-permute-done((bf16[48,1024]{1,0:T(8,128)(2,1)S(1)}, bf16[48,1024]{1,0:T(8,128)(2,1)S(1)}, u32[]{:S(2)}, u32[]{:S(2)}) %collective-permute-start.18) | collective-permute-done | bytes 98336 | tf_op jit(solution)/shard_map/ppermute | solution.py:250
  38.6 0.5 collective-permute-start.22
  39.0 0.7 %collective-permute-done.15.refs_1_ = bf16[48,1024]{1,0:T(8,128)(2,1)S(1)} collective-permute-done((bf16[48,1024]{1,0:T(8,128)(2,1)S(1)}, bf16[48,1024]{1,0:T(8,128)(2,1)S(1)}, u32[]{:S(2)}, u32[]{:S(2)}) %collective-permute-start.15) | collective-permute-done | bytes 98336 | tf_op jit(solution)/shard_map/ppermute | solution.py:250
  39.7 1.7 %collective-permute-done.17.refs_2_ = bf16[192,512]{1,0:T(8,128)(2,1)S(1)} collective-permute-done((bf16[192,512]{1,0:T(8,128)(2,1)S(1)}, bf16[192,512]{1,0:T(8,128)(2,1)S(1)}, u32[]{:S(2)}, u32[]{:S(2)}) %collective-permute-start.17) | collective-permute-done | bytes 196640 | tf_op jit(solution)/shard_map/ppermute | solution.py:275
  41.5 0.4 collective-permute-start.24
  41.9 0.8 %collective-permute-done.21.refs_5_ = bf16[48,1024]{1,0:T(8,128)(2,1)S(1)} collective-permute-done((bf16[48,1024]{1,0:T(8,128)(2,1)S(1)}, bf16[48,1024]{1,0:T(8,128)(2,1)S(1)}, u32[]{:S(2)}, u32[]{:S(2)}) %collective-permute-start.21) | collective-permute-done | bytes 98336 | tf_op jit(solution)/shard_map/ppermute | solution.py:240
  42.8 0.8 %collective-permute-start.25 = (bf16[192,512]{1,0:T(8,128)(2,1)S(1)}, bf16[192,512]{1,0:T(8,128)(2,1)S(1)}, u32[]{:S(2)}, u32[]{:S(2)}) collective-permute-start(bf16[192,512]{1,0:T(8,128)(2,1)S(1)} %add_blocks.3.refs_0_), channel_id=1, source_target_pairs={{1,0},{0,1},{3,2},{2,3},{5,4},{4,5},{7,6},{6,7},{9,8},{8,9},{11,10... | collective-permute-start | bytes 589832 | tf_op jit(solution)/shard_map/ppermute | solution.py:275
  43.6 2.3 %collective-permute-start.26 = (bf16[192,512]{1,0:T(8,128)(2,1)S(1)}, bf16[192,512]{1,0:T(8,128)(2,1)S(1)}, u32[]{:S(2)}, u32[]{:S(2)}) collective-permute-start(bf16[192,512]{1,0:T(8,128)(2,1)S(1)} %add_blocks.3.refs_0_), channel_id=1, source_target_pairs={{2,0},{3,1},{0,2},{1,3},{6,4},{7,5},{4,6},{5,7},{10,8},{11,9},{8,1... | collective-permute-start | bytes 589832 | tf_op jit(solution)/shard_map/ppermute | solution.py:275
  45.9 1.4 %collective-permute-start.27 = (bf16[192,512]{1,0:T(8,128)(2,1)S(1)}, bf16[192,512]{1,0:T(8,128)(2,1)S(1)}, u32[]{:S(2)}, u32[]{:S(2)}) collective-permute-start(bf16[192,512]{1,0:T(8,128)(2,1)S(1)} %add_blocks.3.refs_0_), channel_id=1, source_target_pairs={{3,0},{2,1},{1,2},{0,3},{7,4},{6,5},{5,6},{4,7},{11,8},{10,9},{9,1... | collective-permute-start | bytes 589832 | tf_op jit(solution)/shard_map/ppermute | solution.py:275
  47.3 0.3 weights.1.weight_ref
  47.6 5.8 %collective-permute-done.24.refs_3_ = bf16[192,512]{1,0:T(8,128)(2,1)S(1)} collective-permute-done((bf16[192,512]{1,0:T(8,128)(2,1)S(1)}, bf16[192,512]{1,0:T(8,128)(2,1)S(1)}, u32[]{:S(2)}, u32[]{:S(2)}) %collective-permute-start.24) | collective-permute-done | bytes 196640 | tf_op jit(solution)/shard_map/ppermute | solution.py:275
  53.4 1.7 %combine_gate.1 = (bf16[512,512]{1,0:T(8,128)(2,1)}, f32[8,512]{1,0:T(8,128)S(1)}) custom-call(bf16[512,768]{1,0:T(8,128)(2,1)S(1)} %weights.1.weight_ref, s32[8,512]{1,0:T(8,128)S(1)} %bitcast.5, f32[16,512]{1,0:T(8,128)S(1)} %number.1.key_ref, bf16[512,512]{1,0:T(8,128)(2,1)S(1)} %copy-done.3, bf16[192,512]{1,0:T(8,128)(2,1)S(1)} %add_blocks.2.refs_0_, ...), custom_call_target="tpu_custom_call" | custom-call | bytes 2686976 | tf_op jit(solution)/shard_map/combine_gate/pallas_call | solution.py:23
  55.1 1.1 %collective-permute-start.29 = (f32[8,512]{1,0:T(8,128)S(1)}, f32[8,512]{1,0:T(8,128)S(1)}, u32[]{:S(2)}, u32[]{:S(2)}) collective-permute-start(f32[8,512]{1,0:T(8,128)S(1)} %get-tuple-element.104.refs_4_), channel_id=1, source_target_pairs={{0,8},{4,12},{8,0},{12,4},{1,9},{5,13},{9,1},{13,5},{2,10},{6,14},... | collective-permute-start | bytes 49160 | tf_op jit(solution)/shard_map/ppermute | solution.py:359
  56.2 2.1 %collective-permute-done.28.refs_5_ = f32[8,512]{1,0:T(8,128)S(1)} collective-permute-done((f32[8,512]{1,0:T(8,128)S(1)}, f32[8,512]{1,0:T(8,128)S(1)}, u32[]{:S(2)}, u32[]{:S(2)}) %collective-permute-start.28) | collective-permute-done | bytes 16416 | tf_op jit(solution)/shard_map/ppermute | solution.py:359
  58.3 0.6 collective-permute-done.29.refs_6_
  58.9 0.8 %collective-permute-done.30.refs_7_ = f32[8,512]{1,0:T(8,128)S(1)} collective-permute-done((f32[8,512]{1,0:T(8,128)S(1)}, f32[8,512]{1,0:T(8,128)S(1)}, u32[]{:S(2)}, u32[]{:S(2)}) %collective-permute-start.30) | collective-permute-done | bytes 16416 | tf_op jit(solution)/shard_map/ppermute | solution.py:359
  59.7 2.5 %collective-permute-done.27.refs_3_ = bf16[192,512]{1,0:T(8,128)(2,1)S(1)} collective-permute-done((bf16[192,512]{1,0:T(8,128)(2,1)S(1)}, bf16[192,512]{1,0:T(8,128)(2,1)S(1)}, u32[]{:S(2)}, u32[]{:S(2)}) %collective-permute-start.27) | collective-permute-done | bytes 196640 | tf_op jit(solution)/shard_map/ppermute | solution.py:275
  62.2 1.4 %combine.1 = (bf16[512,512]{1,0:T(8,128)(2,1)}, f32[8,512]{1,0:T(8,128)}) custom-call(bf16[512,768]{1,0:T(8,128)(2,1)S(1)} %weights.1.weight_ref, bf16[192,512]{1,0:T(8,128)(2,1)S(1)} %add_blocks.3.refs_0_, bf16[192,512]{1,0:T(8,128)(2,1)S(1)} %collective-permute-done.25.refs_1_, bf16[192,512]{1,0:T(8,128)(2,1)S(1)} %collective-permute-done.26.refs_2_, ...), custom_call_target="tpu_custom_call" | custom-call | flops 402653184 | bytes 2179072 | tf_op jit(solution)/shard_map/combine/pallas_call | solution.py:23
  (40 shorter events, 0.3 us)
Async XLA Ops:
  0.6 2.3 %collective-permute-start = (bf16[512,512]{1,0:T(8,128)(2,1)}, bf16[512,512]{1,0:T(8,128)(2,1)S(1)}, u32[]{:S(2)}, u32[]{:S(2)}) collective-permute-start(bf16[512,512]{1,0:T(8,128)(2,1)} %refs_0_.2), channel_id=1, source_target_pairs={{0,4},{4,0},{8,12},{12,8},{1,5},{5,1},{9,13},{13,9},{2,6},{6,2},{1... | collective-permute-start | bytes 1572872 | tf_op jit(solution)/shard_map/ppermute | solution.py:240
  1.1 6.7 %collective-permute-start.1 = (bf16[512,512]{1,0:T(8,128)(2,1)}, bf16[512,512]{1,0:T(8,128)(2,1)S(1)}, u32[]{:S(2)}, u32[]{:S(2)}) collective-permute-start(bf16[512,512]{1,0:T(8,128)(2,1)} %grads_ref.1), channel_id=1, source_target_pairs={{0,4},{4,0},{8,12},{12,8},{1,5},{5,1},{9,13},{13,9},{2,6},{6,2},{1... | collective-permute-start | bytes 1572872 | tf_op jit(solution)/shard_map/ppermute | solution.py:240
  1.2 0.7 %copy-start.4 = (s32[512,8]{0,1:T(8,128)S(1)}, s32[512,8]{0,1:T(8,128)}, u32[]{:S(2)}) copy-start(s32[512,8]{0,1:T(8,128)} %param.9) | copy-start | bytes 49156
  1.9 1.0 %copy-start.7 = (bf16[512,512]{1,0:T(8,128)(2,1)S(1)}, bf16[512,512]{1,0:T(8,128)(2,1)}, u32[]{:S(2)}) copy-start(bf16[512,512]{1,0:T(8,128)(2,1)} %refs_0_.2) | copy-start | bytes 1572868
  2.1 5.8 %copy-start.3 = (bf16[512,512]{1,0:T(8,128)(2,1)S(1)}, bf16[512,512]{1,0:T(8,128)(2,1)}, u32[]{:S(2)}) copy-start(bf16[512,512]{1,0:T(8,128)(2,1)} %grads_ref.1) | copy-start | bytes 1572868
  3.3 8.4 %collective-permute-start.2 = (bf16[48,1024]{1,0:T(8,128)(2,1)S(1)}, bf16[48,1024]{1,0:T(8,128)(2,1)S(1)}, u32[]{:S(2)}, u32[]{:S(2)}) collective-permute-start(bf16[48,1024]{1,0:T(8,128)(2,1)S(1)} %get-tuple-element.59), channel_id=1, source_target_pairs={{0,8},{4,12},{8,0},{12,4},{16,24},{20,28},{24,16},{28,20},{1,9},{5... | collective-permute-start | bytes 294920 | tf_op jit(solution)/shard_map/ppermute | solution.py:250
  6.3 9.5 %collective-permute-start.4 = (bf16[48,1024]{1,0:T(8,128)(2,1)S(1)}, bf16[48,1024]{1,0:T(8,128)(2,1)S(1)}, u32[]{:S(2)}, u32[]{:S(2)}) collective-permute-start(bf16[48,1024]{1,0:T(8,128)(2,1)S(1)} %get-tuple-element.59), channel_id=1, source_target_pairs={{0,24},{4,28},{8,16},{12,20},{16,8},{20,12},{24,0},{28,4},{1,25},{... | collective-permute-start | bytes 294920 | tf_op jit(solution)/shard_map/ppermute | solution.py:250
  7.8 8.1 %copy-start = (bf16[1,768,2048]{2,1,0:T(8,128)(2,1)S(1)}, bf16[1,768,2048]{2,1,0:T(8,128)(2,1)}, u32[]{:S(2)}) copy-start(bf16[1,768,2048]{2,1,0:T(8,128)(2,1)} %refs_4_.3) | copy-start | bytes 9437188
  7.8 8.1 %copy-start.1 = (bf16[1,768,2048]{2,1,0:T(8,128)(2,1)S(1)}, bf16[1,768,2048]{2,1,0:T(8,128)(2,1)}, u32[]{:S(2)}) copy-start(bf16[1,768,2048]{2,1,0:T(8,128)(2,1)} %refs_5_.3) | copy-start | bytes 9437188
  7.8 8.1 %copy-start.2 = (bf16[1,768,2048]{2,1,0:T(8,128)(2,1)S(1)}, bf16[1,768,2048]{2,1,0:T(8,128)(2,1)}, u32[]{:S(2)}) copy-start(bf16[1,768,2048]{2,1,0:T(8,128)(2,1)} %refs_6_.3) | copy-start | bytes 9437188
  7.8 8.0 %collective-permute-start.3 = (bf16[48,1024]{1,0:T(8,128)(2,1)S(1)}, bf16[48,1024]{1,0:T(8,128)(2,1)S(1)}, u32[]{:S(2)}, u32[]{:S(2)}) collective-permute-start(bf16[48,1024]{1,0:T(8,128)(2,1)S(1)} %get-tuple-element.58.refs_0_), channel_id=1, source_target_pairs={{0,16},{4,20},{8,24},{12,28},{16,0},{20,4},{24,8},{28,12},{1,17},{... | collective-permute-start | bytes 294920 | tf_op jit(solution)/shard_map/ppermute | solution.py:250
  8.2 10.2 %collective-permute-start.5 = (bf16[48,1024]{1,0:T(8,128)(2,1)S(1)}, bf16[48,1024]{1,0:T(8,128)(2,1)S(1)}, u32[]{:S(2)}, u32[]{:S(2)}) collective-permute-start(bf16[48,1024]{1,0:T(8,128)(2,1)S(1)} %get-tuple-element.65), channel_id=1, source_target_pairs={{0,8},{4,12},{8,0},{12,4},{16,24},{20,28},{24,16},{28,20},{1,9},{5... | collective-permute-start | bytes 294920 | tf_op jit(solution)/shard_map/ppermute | solution.py:250
  10.1 8.3 %collective-permute-start.6 = (bf16[48,1024]{1,0:T(8,128)(2,1)S(1)}, bf16[48,1024]{1,0:T(8,128)(2,1)S(1)}, u32[]{:S(2)}, u32[]{:S(2)}) collective-permute-start(bf16[48,1024]{1,0:T(8,128)(2,1)S(1)} %get-tuple-element.72.refs_0_), channel_id=1, source_target_pairs={{0,16},{4,20},{8,24},{12,28},{16,0},{20,4},{24,8},{28,12},{1,17},{... | collective-permute-start | bytes 294920 | tf_op jit(solution)/shard_map/ppermute | solution.py:250
  11.7 6.8 %collective-permute-start.7 = (bf16[48,1024]{1,0:T(8,128)(2,1)S(1)}, bf16[48,1024]{1,0:T(8,128)(2,1)S(1)}, u32[]{:S(2)}, u32[]{:S(2)}) collective-permute-start(bf16[48,1024]{1,0:T(8,128)(2,1)S(1)} %get-tuple-element.65), channel_id=1, source_target_pairs={{0,24},{4,28},{8,16},{12,20},{16,8},{20,12},{24,0},{28,4},{1,25},{... | collective-permute-start | bytes 294920 | tf_op jit(solution)/shard_map/ppermute | solution.py:250
  18.4 6.0 %collective-permute-start.9 = (bf16[48,1024]{1,0:T(8,128)(2,1)S(1)}, bf16[48,1024]{1,0:T(8,128)(2,1)S(1)}, u32[]{:S(2)}, u32[]{:S(2)}) collective-permute-start(bf16[48,1024]{1,0:T(8,128)(2,1)S(1)} %get-tuple-element.68), channel_id=1, source_target_pairs={{0,16},{4,20},{8,24},{12,28},{16,0},{20,4},{24,8},{28,12},{1,17},{... | collective-permute-start | bytes 294920 | tf_op jit(solution)/shard_map/ppermute | solution.py:250
  18.7 5.9 %collective-permute-start.10 = (bf16[48,1024]{1,0:T(8,128)(2,1)S(1)}, bf16[48,1024]{1,0:T(8,128)(2,1)S(1)}, u32[]{:S(2)}, u32[]{:S(2)}) collective-permute-start(bf16[48,1024]{1,0:T(8,128)(2,1)S(1)} %get-tuple-element.69), channel_id=1, source_target_pairs={{0,24},{4,28},{8,16},{12,20},{16,8},{20,12},{24,0},{28,4},{1,25},{... | collective-permute-start | bytes 294920 | tf_op jit(solution)/shard_map/ppermute | solution.py:250
  21.5 4.6 %collective-permute-start.8 = (bf16[48,1024]{1,0:T(8,128)(2,1)S(1)}, bf16[48,1024]{1,0:T(8,128)(2,1)S(1)}, u32[]{:S(2)}, u32[]{:S(2)}) collective-permute-start(bf16[48,1024]{1,0:T(8,128)(2,1)S(1)} %get-tuple-element.67), channel_id=1, source_target_pairs={{0,8},{4,12},{8,0},{12,4},{16,24},{20,28},{24,16},{28,20},{1,9},{5... | collective-permute-start | bytes 294920 | tf_op jit(solution)/shard_map/ppermute | solution.py:250
  22.0 4.7 %collective-permute-start.11 = (bf16[48,1024]{1,0:T(8,128)(2,1)S(1)}, bf16[48,1024]{1,0:T(8,128)(2,1)S(1)}, u32[]{:S(2)}, u32[]{:S(2)}) collective-permute-start(bf16[48,1024]{1,0:T(8,128)(2,1)S(1)} %get-tuple-element.66.refs_0_), channel_id=1, source_target_pairs={{0,4},{4,0},{8,12},{12,8},{1,5},{5,1},{9,13},{13,9},{2,6},{6,2},{1... | collective-permute-start | bytes 294920 | tf_op jit(solution)/shard_map/ppermute | solution.py:240
  22.0 25.3 %copy-start.5 = (s32[512,8]{0,1:T(8,128)S(1)}, s32[512,8]{0,1:T(8,128)}, u32[]{:S(2)}) copy-start(s32[512,8]{0,1:T(8,128)} %param.9) | copy-start | bytes 49156
  22.0 25.3 %copy-start.6 = (f32[512,8]{0,1:T(8,128)S(1)}, f32[512,8]{0,1:T(8,128)}, u32[]{:S(2)}) copy-start(f32[512,8]{0,1:T(8,128)} %param.10) | copy-start | bytes 49156
  24.6 2.9 %collective-permute-start.13 = (bf16[48,1024]{1,0:T(8,128)(2,1)S(1)}, bf16[48,1024]{1,0:T(8,128)(2,1)S(1)}, u32[]{:S(2)}, u32[]{:S(2)}) collective-permute-start(bf16[48,1024]{1,0:T(8,128)(2,1)S(1)} %collective-permute-done.9.refs_2_), channel_id=1, source_target_pairs={{0,4},{4,0},{8,12},{12,8},{1,5},{5,1},{9,13},{13,9},{2,6},{6,2},{1... | collective-permute-start | bytes 294920 | tf_op jit(solution)/shard_map/ppermute | solution.py:240
  26.2 1.3 %collective-permute-start.12 = (bf16[48,1024]{1,0:T(8,128)(2,1)S(1)}, bf16[48,1024]{1,0:T(8,128)(2,1)S(1)}, u32[]{:S(2)}, u32[]{:S(2)}) collective-permute-start(bf16[48,1024]{1,0:T(8,128)(2,1)S(1)} %collective-permute-done.8.refs_1_), channel_id=1, source_target_pairs={{0,4},{4,0},{8,12},{12,8},{1,5},{5,1},{9,13},{13,9},{2,6},{6,2},{1... | collective-permute-start | bytes 294920 | tf_op jit(solution)/shard_map/ppermute | solution.py:240
  26.2 1.5 %collective-permute-start.14 = (bf16[48,1024]{1,0:T(8,128)(2,1)S(1)}, bf16[48,1024]{1,0:T(8,128)(2,1)S(1)}, u32[]{:S(2)}, u32[]{:S(2)}) collective-permute-start(bf16[48,1024]{1,0:T(8,128)(2,1)S(1)} %collective-permute-done.10.refs_3_), channel_id=1, source_target_pairs={{0,4},{4,0},{8,12},{12,8},{1,5},{5,1},{9,13},{13,9},{2,6},{6,2},{1... | collective-permute-start | bytes 294920 | tf_op jit(solution)/shard_map/ppermute | solution.py:240
  27.7 12.1 %collective-permute-start.16 = (bf16[192,512]{1,0:T(8,128)(2,1)S(1)}, bf16[192,512]{1,0:T(8,128)(2,1)S(1)}, u32[]{:S(2)}, u32[]{:S(2)}) collective-permute-start(bf16[192,512]{1,0:T(8,128)(2,1)S(1)} %add_blocks.2.refs_0_), channel_id=1, source_target_pairs={{1,0},{0,1},{3,2},{2,3},{5,4},{4,5},{7,6},{6,7},{9,8},{8,9},{11,10... | collective-permute-start | bytes 589832 | tf_op jit(solution)/shard_map/ppermute | solution.py:275
  29.4 12.0 %collective-permute-start.17 = (bf16[192,512]{1,0:T(8,128)(2,1)S(1)}, bf16[192,512]{1,0:T(8,128)(2,1)S(1)}, u32[]{:S(2)}, u32[]{:S(2)}) collective-permute-start(bf16[192,512]{1,0:T(8,128)(2,1)S(1)} %add_blocks.2.refs_0_), channel_id=1, source_target_pairs={{2,0},{3,1},{0,2},{1,3},{6,4},{7,5},{4,6},{5,7},{10,8},{11,9},{8,1... | collective-permute-start | bytes 589832 | tf_op jit(solution)/shard_map/ppermute | solution.py:275
  32.0 6.6 %collective-permute-start.18 = (bf16[48,1024]{1,0:T(8,128)(2,1)S(1)}, bf16[48,1024]{1,0:T(8,128)(2,1)S(1)}, u32[]{:S(2)}, u32[]{:S(2)}) collective-permute-start(bf16[48,1024]{1,0:T(8,128)(2,1)S(1)} %get-tuple-element.92), channel_id=1, source_target_pairs={{0,16},{4,20},{8,24},{12,28},{16,0},{20,4},{24,8},{28,12},{1,17},{... | collective-permute-start | bytes 294920 | tf_op jit(solution)/shard_map/ppermute | solution.py:250
  32.3 6.2 %collective-permute-start.19 = (bf16[48,1024]{1,0:T(8,128)(2,1)S(1)}, bf16[48,1024]{1,0:T(8,128)(2,1)S(1)}, u32[]{:S(2)}, u32[]{:S(2)}) collective-permute-start(bf16[48,1024]{1,0:T(8,128)(2,1)S(1)} %get-tuple-element.93), channel_id=1, source_target_pairs={{0,24},{4,28},{8,16},{12,20},{16,8},{20,12},{24,0},{28,4},{1,25},{... | collective-permute-start | bytes 294920 | tf_op jit(solution)/shard_map/ppermute | solution.py:250
  34.5 5.3 %collective-permute-start.15 = (bf16[48,1024]{1,0:T(8,128)(2,1)S(1)}, bf16[48,1024]{1,0:T(8,128)(2,1)S(1)}, u32[]{:S(2)}, u32[]{:S(2)}) collective-permute-start(bf16[48,1024]{1,0:T(8,128)(2,1)S(1)} %get-tuple-element.89), channel_id=1, source_target_pairs={{0,8},{4,12},{8,0},{12,4},{16,24},{20,28},{24,16},{28,20},{1,9},{5... | collective-permute-start | bytes 294920 | tf_op jit(solution)/shard_map/ppermute | solution.py:250
  38.5 3.4 %collective-permute-start.20 = (bf16[48,1024]{1,0:T(8,128)(2,1)S(1)}, bf16[48,1024]{1,0:T(8,128)(2,1)S(1)}, u32[]{:S(2)}, u32[]{:S(2)}) collective-permute-start(bf16[48,1024]{1,0:T(8,128)(2,1)S(1)} %get-tuple-element.88.refs_0_), channel_id=1, source_target_pairs={{0,4},{4,0},{8,12},{12,8},{1,5},{5,1},{9,13},{13,9},{2,6},{6,2},{1... | collective-permute-start | bytes 294920 | tf_op jit(solution)/shard_map/ppermute | solution.py:240
  38.6 3.4 %collective-permute-start.22 = (bf16[48,1024]{1,0:T(8,128)(2,1)S(1)}, bf16[48,1024]{1,0:T(8,128)(2,1)S(1)}, u32[]{:S(2)}, u32[]{:S(2)}) collective-permute-start(bf16[48,1024]{1,0:T(8,128)(2,1)S(1)} %collective-permute-done.18.refs_2_), channel_id=1, source_target_pairs={{0,4},{4,0},{8,12},{12,8},{1,5},{5,1},{9,13},{13,9},{2,6},{6,2},{1... | collective-permute-start | bytes 294920 | tf_op jit(solution)/shard_map/ppermute | solution.py:240
  39.7 2.2 %collective-permute-start.23 = (bf16[48,1024]{1,0:T(8,128)(2,1)S(1)}, bf16[48,1024]{1,0:T(8,128)(2,1)S(1)}, u32[]{:S(2)}, u32[]{:S(2)}) collective-permute-start(bf16[48,1024]{1,0:T(8,128)(2,1)S(1)} %collective-permute-done.19.refs_3_), channel_id=1, source_target_pairs={{0,4},{4,0},{8,12},{12,8},{1,5},{5,1},{9,13},{13,9},{2,6},{6,2},{1... | collective-permute-start | bytes 294920 | tf_op jit(solution)/shard_map/ppermute | solution.py:240
  41.5 1.3 %collective-permute-start.21 = (bf16[48,1024]{1,0:T(8,128)(2,1)S(1)}, bf16[48,1024]{1,0:T(8,128)(2,1)S(1)}, u32[]{:S(2)}, u32[]{:S(2)}) collective-permute-start(bf16[48,1024]{1,0:T(8,128)(2,1)S(1)} %collective-permute-done.15.refs_1_), channel_id=1, source_target_pairs={{0,4},{4,0},{8,12},{12,8},{1,5},{5,1},{9,13},{13,9},{2,6},{6,2},{1... | collective-permute-start | bytes 294920 | tf_op jit(solution)/shard_map/ppermute | solution.py:240
  41.5 11.9 %collective-permute-start.24 = (bf16[192,512]{1,0:T(8,128)(2,1)S(1)}, bf16[192,512]{1,0:T(8,128)(2,1)S(1)}, u32[]{:S(2)}, u32[]{:S(2)}) collective-permute-start(bf16[192,512]{1,0:T(8,128)(2,1)S(1)} %collective-permute-done.17.refs_2_), channel_id=1, source_target_pairs={{1,0},{0,1},{3,2},{2,3},{5,4},{4,5},{7,6},{6,7},{9,8},{8,9},{11,10... | collective-permute-start | bytes 589832 | tf_op jit(solution)/shard_map/ppermute | solution.py:275
  42.8 16.9 %collective-permute-start.25 = (bf16[192,512]{1,0:T(8,128)(2,1)S(1)}, bf16[192,512]{1,0:T(8,128)(2,1)S(1)}, u32[]{:S(2)}, u32[]{:S(2)}) collective-permute-start(bf16[192,512]{1,0:T(8,128)(2,1)S(1)} %add_blocks.3.refs_0_), channel_id=1, source_target_pairs={{1,0},{0,1},{3,2},{2,3},{5,4},{4,5},{7,6},{6,7},{9,8},{8,9},{11,10... | collective-permute-start | bytes 589832 | tf_op jit(solution)/shard_map/ppermute | solution.py:275
  43.6 16.1 %collective-permute-start.26 = (bf16[192,512]{1,0:T(8,128)(2,1)S(1)}, bf16[192,512]{1,0:T(8,128)(2,1)S(1)}, u32[]{:S(2)}, u32[]{:S(2)}) collective-permute-start(bf16[192,512]{1,0:T(8,128)(2,1)S(1)} %add_blocks.3.refs_0_), channel_id=1, source_target_pairs={{2,0},{3,1},{0,2},{1,3},{6,4},{7,5},{4,6},{5,7},{10,8},{11,9},{8,1... | collective-permute-start | bytes 589832 | tf_op jit(solution)/shard_map/ppermute | solution.py:275
  45.9 16.3 %collective-permute-start.27 = (bf16[192,512]{1,0:T(8,128)(2,1)S(1)}, bf16[192,512]{1,0:T(8,128)(2,1)S(1)}, u32[]{:S(2)}, u32[]{:S(2)}) collective-permute-start(bf16[192,512]{1,0:T(8,128)(2,1)S(1)} %add_blocks.3.refs_0_), channel_id=1, source_target_pairs={{3,0},{2,1},{1,2},{0,3},{7,4},{6,5},{5,6},{4,7},{11,8},{10,9},{9,1... | collective-permute-start | bytes 589832 | tf_op jit(solution)/shard_map/ppermute | solution.py:275
  55.1 3.2 %collective-permute-start.28 = (f32[8,512]{1,0:T(8,128)S(1)}, f32[8,512]{1,0:T(8,128)S(1)}, u32[]{:S(2)}, u32[]{:S(2)}) collective-permute-start(f32[8,512]{1,0:T(8,128)S(1)} %get-tuple-element.104.refs_4_), channel_id=1, source_target_pairs={{0,4},{4,8},{8,12},{12,0},{1,5},{5,9},{9,13},{13,1},{2,6},{6,10},{... | collective-permute-start | bytes 49160 | tf_op jit(solution)/shard_map/ppermute | solution.py:359
  55.1 3.8 %collective-permute-start.29 = (f32[8,512]{1,0:T(8,128)S(1)}, f32[8,512]{1,0:T(8,128)S(1)}, u32[]{:S(2)}, u32[]{:S(2)}) collective-permute-start(f32[8,512]{1,0:T(8,128)S(1)} %get-tuple-element.104.refs_4_), channel_id=1, source_target_pairs={{0,8},{4,12},{8,0},{12,4},{1,9},{5,13},{9,1},{13,5},{2,10},{6,14},... | collective-permute-start | bytes 49160 | tf_op jit(solution)/shard_map/ppermute | solution.py:359
  58.2 1.4 %collective-permute-start.30 = (f32[8,512]{1,0:T(8,128)S(1)}, f32[8,512]{1,0:T(8,128)S(1)}, u32[]{:S(2)}, u32[]{:S(2)}) collective-permute-start(f32[8,512]{1,0:T(8,128)S(1)} %get-tuple-element.104.refs_4_), channel_id=1, source_target_pairs={{0,12},{4,0},{8,4},{12,8},{1,13},{5,1},{9,5},{13,9},{2,14},{6,2},{... | collective-permute-start | bytes 49160 | tf_op jit(solution)/shard_map/ppermute | solution.py:359

commit v13 on v11

--- a/solution.py
+++ b/solution.py
@@ -290,8 +290,9 @@
         )
 
     token_sources = [to_core(tokens, dc) for dc in range(cores)]
-    grad_sources = [to_core(grad_out, dc) for dc in range(cores)]
     key = call(number_kernel, "number", shape(experts, rows, F32), [routes_t], EARLY)
+    grads, key = after(grad_out, key)
+    grad_sources = [to_core(grads, dc) for dc in range(cores)]
     tok_in = dispatch(pick(key, token_sources))
     tok_in[0], grad_pieces = lax.optimization_barrier((tok_in[0], pick(key, grad_sources)))
     grad_in = dispatch(grad_pieces)
@@ -326,7 +327,8 @@
     for dz in direct:
         out_parts[dz] = across(out_parts, dz)
     back_pieces = give_back(backs)
-    back_pieces[0], out_parts = after(back_pieces[0], out_parts)
+    out_parts[direct[0]] = lax.optimization_barrier(out_parts[direct[0]])
+    back_pieces[-1], out_parts = after(back_pieces[-1], out_parts)
     for dz in later:
         out_parts[dz] = across(out_parts, dz, dz & (dz - 1))
     back_rows = add_blocks(swap(back_pieces))

time: 63.3 us -> 62.8 us (level)
  waiting for transfers between devices: 24.1 us -> 21.8 us
  starting transfers between devices: 28 us -> 29.1 us
  local copies, waits for them, and re-layouts: 0.83 us -> 1.72 us
    ppermute x10, waiting for transfers between devices: 2.94 us -> 1.37 us  [to_core(): return lax.ppermute(value, 'tensor', pairs)]
    unnamed x16, local copies, waits for them, and re-layouts: 0.83 us -> 1.72 us
    ppermute x6, waiting for transfers between devices: 9.76 us -> 9.04 us  [across(): return lax.ppermute(parts[first], 'expert', pairs)]
    ppermute x6, starting transfers between devices: 9.13 us -> 9.8 us  [across(): return lax.ppermute(parts[first], 'expert', pairs)]
  transfers between devices with their start and end apart: 31 -> 31, of which waited for: 15 -> 14; matrix products, arithmetic and copies ran while one was open for 0% -> 0% of each run, Pallas kernels for 12% -> 13%
where the time goes in v13:
time: 62.8 us; the launch traced here: 62.6 us
  starting transfers between devices  29.1 us (46%)
  waiting for transfers between devices  21.8 us (35%)
  Pallas kernels  9.26 us (15%)
  local copies, waits for them, and re-layouts  1.72 us (3%)
  between operations  0.73 us (1%)
    ppermute x12, starting transfers between devices, to_chip(): return lax.ppermute(value, ('dp', 'tensor'), pairs)  16.2 us
    ppermute x6, starting transfers between devices, across(): return lax.ppermute(parts[first], 'expert', pairs)  9.8 us
    pallas_call x10, Pallas kernels, call(): pl.pallas_call(kernel, out_shape=out_shape, in_specs=[spec] * len(operand...  9.26 us
    ppermute x6, waiting for transfers between devices, across(): return lax.ppermute(parts[first], 'expert', pairs)  9.04 us
    ppermute x12, waiting for transfers between devices, to_chip(): return lax.ppermute(value, ('dp', 'tensor'), pairs)  8.13 us
    ppermute x3, waiting for transfers between devices, body(): gate_parts.append(lax.ppermute(gate_part, 'tensor', pairs))  3.22 us
    ppermute x10, starting transfers between devices, to_core(): return lax.ppermute(value, 'tensor', pairs)  1.76 us
    unnamed x16, local copies, waits for them, and re-layouts  1.72 us
  transfers between devices with their start and end apart: 31, of which 14 were waited for; matrix products, arithmetic and copies ran while one was open for 0% of the time, Pallas kernels for 13%

profile of v13, /device:TPU:0, one launch (start us, length us, event | category | flops | bytes accessed | tf_op | source)
XLA Modules:
  0.0 62.6 jit_solution(6304104858597549100)
XLA Ops:
  0.6 0.5 collective-permute-start
  1.1 0.7 %copy-done.4 = s32[512,8]{0,1:T(8,128)S(1)} copy-done((s32[512,8]{0,1:T(8,128)S(1)}, s32[512,8]{0,1:T(8,128)}, u32[]{:S(2)}) %copy-start.4) | copy-done | bytes 16408
  1.9 0.1 number.1.key_ref
  2.0 0.9 %copy-done.3 = bf16[512,512]{1,0:T(8,128)(2,1)S(1)} copy-done((bf16[512,512]{1,0:T(8,128)(2,1)S(1)}, bf16[512,512]{1,0:T(8,128)(2,1)}, u32[]{:S(2)}) %copy-start.3) | copy-done | bytes 524312
  3.0 0.1 copy-done.7
  3.1 0.3 pick.2
  3.4 2.9 %collective-permute-start.2 = (bf16[48,1024]{1,0:T(8,128)(2,1)S(1)}, bf16[48,1024]{1,0:T(8,128)(2,1)S(1)}, u32[]{:S(2)}, u32[]{:S(2)}) collective-permute-start(bf16[48,1024]{1,0:T(8,128)(2,1)S(1)} %get-tuple-element.58), channel_id=1, source_target_pairs={{0,8},{4,12},{8,0},{12,4},{16,24},{20,28},{24,16},{28,20},{1,9},{5... | collective-permute-start | bytes 294920 | tf_op jit(solution)/shard_map/ppermute | solution.py:250
  6.3 1.5 %collective-permute-start.4 = (bf16[48,1024]{1,0:T(8,128)(2,1)S(1)}, bf16[48,1024]{1,0:T(8,128)(2,1)S(1)}, u32[]{:S(2)}, u32[]{:S(2)}) collective-permute-start(bf16[48,1024]{1,0:T(8,128)(2,1)S(1)} %get-tuple-element.58), channel_id=1, source_target_pairs={{0,24},{4,28},{8,16},{12,20},{16,8},{20,12},{24,0},{28,4},{1,25},{... | collective-permute-start | bytes 294920 | tf_op jit(solution)/shard_map/ppermute | solution.py:250
  7.8 0.1 collective-permute-start.3
  7.9 0.3 pick.3
  8.2 2.0 %collective-permute-start.5 = (bf16[48,1024]{1,0:T(8,128)(2,1)S(1)}, bf16[48,1024]{1,0:T(8,128)(2,1)S(1)}, u32[]{:S(2)}, u32[]{:S(2)}) collective-permute-start(bf16[48,1024]{1,0:T(8,128)(2,1)S(1)} %get-tuple-element.64), channel_id=1, source_target_pairs={{0,8},{4,12},{8,0},{12,4},{16,24},{20,28},{24,16},{28,20},{1,9},{5... | collective-permute-start | bytes 294920 | tf_op jit(solution)/shard_map/ppermute | solution.py:250
  10.2 1.5 %collective-permute-start.6 = (bf16[48,1024]{1,0:T(8,128)(2,1)S(1)}, bf16[48,1024]{1,0:T(8,128)(2,1)S(1)}, u32[]{:S(2)}, u32[]{:S(2)}) collective-permute-start(bf16[48,1024]{1,0:T(8,128)(2,1)S(1)} %get-tuple-element.68.refs_0_), channel_id=1, source_target_pairs={{0,16},{4,20},{8,24},{12,28},{16,0},{20,4},{24,8},{28,12},{1,17},{... | collective-permute-start | bytes 294920 | tf_op jit(solution)/shard_map/ppermute | solution.py:250
  11.7 1.2 %collective-permute-start.7 = (bf16[48,1024]{1,0:T(8,128)(2,1)S(1)}, bf16[48,1024]{1,0:T(8,128)(2,1)S(1)}, u32[]{:S(2)}, u32[]{:S(2)}) collective-permute-start(bf16[48,1024]{1,0:T(8,128)(2,1)S(1)} %get-tuple-element.64), channel_id=1, source_target_pairs={{0,24},{4,28},{8,16},{12,20},{16,8},{20,12},{24,0},{28,4},{1,25},{... | collective-permute-start | bytes 294920 | tf_op jit(solution)/shard_map/ppermute | solution.py:250
  12.9 2.8 %collective-permute-done.3.refs_2_ = bf16[48,1024]{1,0:T(8,128)(2,1)S(1)} collective-permute-done((bf16[48,1024]{1,0:T(8,128)(2,1)S(1)}, bf16[48,1024]{1,0:T(8,128)(2,1)S(1)}, u32[]{:S(2)}, u32[]{:S(2)}) %collective-permute-start.3) | collective-permute-done | bytes 98336 | tf_op jit(solution)/shard_map/ppermute | solution.py:250
  15.7 2.6 %forward.1 = (f32[96,768]{1,0:T(8,128)S(1)}, f32[96,768]{1,0:T(8,128)S(1)}, bf16[48,1024]{1,0:T(8,128)(2,1)S(1)}, bf16[48,1024]{1,0:T(8,128)(2,1)S(1)}, bf16[48,...) custom-call(bf16[48,1024]{1,0:T(8,128)(2,1)S(1)} %get-tuple-element.57.refs_0_, ...), custom_call_target="tpu_custom_call" | custom-call | flops 905969664 | bytes 10813440 | tf_op jit(solution)/shard_map/forward/pallas_call | solution.py:23
  18.3 0.5 collective-permute-start.9
  18.8 1.6 %collective-permute-start.8 = (bf16[48,1024]{1,0:T(8,128)(2,1)S(1)}, bf16[48,1024]{1,0:T(8,128)(2,1)S(1)}, u32[]{:S(2)}, u32[]{:S(2)}) collective-permute-start(bf16[48,1024]{1,0:T(8,128)(2,1)S(1)} %get-tuple-element.66), channel_id=1, source_target_pairs={{0,8},{4,12},{8,0},{12,4},{16,24},{20,28},{24,16},{28,20},{1,9},{5... | collective-permute-start | bytes 294920 | tf_op jit(solution)/shard_map/ppermute | solution.py:250
  20.3 1.5 %collective-permute-start.10 = (bf16[48,1024]{1,0:T(8,128)(2,1)S(1)}, bf16[48,1024]{1,0:T(8,128)(2,1)S(1)}, u32[]{:S(2)}, u32[]{:S(2)}) collective-permute-start(bf16[48,1024]{1,0:T(8,128)(2,1)S(1)} %get-tuple-element.79), channel_id=1, source_target_pairs={{0,24},{4,28},{8,16},{12,20},{16,8},{20,12},{24,0},{28,4},{1,25},{... | collective-permute-start | bytes 294920 | tf_op jit(solution)/shard_map/ppermute | solution.py:250
  21.8 2.4 %backward.1 = (bf16[48,1024]{1,0:T(8,128)(2,1)S(1)}, bf16[48,1024]{1,0:T(8,128)(2,1)S(1)}, bf16[48,1024]{1,0:T(8,128)(2,1)S(1)}, bf16[48,1024]{1,0:T(8,128)(2,1)S(1)}) custom-call(bf16[48,1024]{1,0:T(8,128)(2,1)S(1)} %get-tuple-element.68.refs_0_, bf16[48,1024]{1,0:T(8,128)(2,1)S(1)} %collective-permute-done.5.refs_1_, ...), custom_call_target="tpu_custom_call" | custom-call | flops 905969664 | bytes 10813440 | tf_op jit(solution)/shard_map/backward/pallas_call | solution.py:23
  24.3 0.6 collective-permute-start.13
  24.9 0.1 collective-permute-start.12
  25.0 0.9 %collective-permute-done.10.refs_3_ = bf16[48,1024]{1,0:T(8,128)(2,1)S(1)} collective-permute-done((bf16[48,1024]{1,0:T(8,128)(2,1)S(1)}, bf16[48,1024]{1,0:T(8,128)(2,1)S(1)}, u32[]{:S(2)}, u32[]{:S(2)}) %collective-permute-start.10) | collective-permute-done | bytes 98336 | tf_op jit(solution)/shard_map/ppermute | solution.py:250
  25.9 0.3 collective-permute-done.12.refs_5_
  26.2 1.0 %collective-permute-done.14.refs_7_ = bf16[48,1024]{1,0:T(8,128)(2,1)S(1)} collective-permute-done((bf16[48,1024]{1,0:T(8,128)(2,1)S(1)}, bf16[48,1024]{1,0:T(8,128)(2,1)S(1)}, u32[]{:S(2)}, u32[]{:S(2)}) %collective-permute-start.14) | collective-permute-done | bytes 98336 | tf_op jit(solution)/shard_map/ppermute | solution.py:240
  27.2 2.7 %collective-permute-start.19 = (bf16[192,512]{1,0:T(8,128)(2,1)S(1)}, bf16[192,512]{1,0:T(8,128)(2,1)S(1)}, u32[]{:S(2)}, u32[]{:S(2)}) collective-permute-start(bf16[192,512]{1,0:T(8,128)(2,1)S(1)} %add_blocks.2.refs_0_), channel_id=1, source_target_pairs={{2,0},{3,1},{0,2},{1,3},{6,4},{7,5},{4,6},{5,7},{10,8},{11,9},{8,1... | collective-permute-start | bytes 589832 | tf_op jit(solution)/shard_map/ppermute | solution.py:278
  29.9 1.6 %collective-permute-start.18 = (bf16[192,512]{1,0:T(8,128)(2,1)S(1)}, bf16[192,512]{1,0:T(8,128)(2,1)S(1)}, u32[]{:S(2)}, u32[]{:S(2)}) collective-permute-start(bf16[192,512]{1,0:T(8,128)(2,1)S(1)} %add_blocks.2.refs_0_), channel_id=1, source_target_pairs={{1,0},{0,1},{3,2},{2,3},{5,4},{4,5},{7,6},{6,7},{9,8},{8,9},{11,10... | collective-permute-start | bytes 589832 | tf_op jit(solution)/shard_map/ppermute | solution.py:278
  31.4 1.3 %collective-permute-start.15 = (bf16[48,1024]{1,0:T(8,128)(2,1)S(1)}, bf16[48,1024]{1,0:T(8,128)(2,1)S(1)}, u32[]{:S(2)}, u32[]{:S(2)}) collective-permute-start(bf16[48,1024]{1,0:T(8,128)(2,1)S(1)} %get-tuple-element.85), channel_id=1, source_target_pairs={{0,8},{4,12},{8,0},{12,4},{16,24},{20,28},{24,16},{28,20},{1,9},{5... | collective-permute-start | bytes 294920 | tf_op jit(solution)/shard_map/ppermute | solution.py:250
  32.8 0.7 %collective-permute-start.16 = (bf16[48,1024]{1,0:T(8,128)(2,1)S(1)}, bf16[48,1024]{1,0:T(8,128)(2,1)S(1)}, u32[]{:S(2)}, u32[]{:S(2)}) collective-permute-start(bf16[48,1024]{1,0:T(8,128)(2,1)S(1)} %get-tuple-element.86), channel_id=1, source_target_pairs={{0,16},{4,20},{8,24},{12,28},{16,0},{20,4},{24,8},{28,12},{1,17},{... | collective-permute-start | bytes 294920 | tf_op jit(solution)/shard_map/ppermute | solution.py:250
  33.5 1.4 %collective-permute-start.17 = (bf16[48,1024]{1,0:T(8,128)(2,1)S(1)}, bf16[48,1024]{1,0:T(8,128)(2,1)S(1)}, u32[]{:S(2)}, u32[]{:S(2)}) collective-permute-start(bf16[48,1024]{1,0:T(8,128)(2,1)S(1)} %get-tuple-element.87), channel_id=1, source_target_pairs={{0,24},{4,28},{8,16},{12,20},{16,8},{20,12},{24,0},{28,4},{1,25},{... | collective-permute-start | bytes 294920 | tf_op jit(solution)/shard_map/ppermute | solution.py:250
  34.9 1.4 %collective-permute-done.15.refs_1_ = bf16[48,1024]{1,0:T(8,128)(2,1)S(1)} collective-permute-done((bf16[48,1024]{1,0:T(8,128)(2,1)S(1)}, bf16[48,1024]{1,0:T(8,128)(2,1)S(1)}, u32[]{:S(2)}, u32[]{:S(2)}) %collective-permute-start.15) | collective-permute-done | bytes 98336 | tf_op jit(solution)/shard_map/ppermute | solution.py:250
  36.3 3.0 %collective-permute-done.16.refs_2_ = bf16[48,1024]{1,0:T(8,128)(2,1)S(1)} collective-permute-done((bf16[48,1024]{1,0:T(8,128)(2,1)S(1)}, bf16[48,1024]{1,0:T(8,128)(2,1)S(1)}, u32[]{:S(2)}, u32[]{:S(2)}) %collective-permute-start.16) | collective-permute-done | bytes 98336 | tf_op jit(solution)/shard_map/ppermute | solution.py:250
  39.3 0.1 collective-permute-done.19.refs_2_
  39.4 0.4 collective-permute-start.22
  39.9 0.1 collective-permute-start.23
  40.0 1.1 %collective-permute-start.24 = (bf16[192,512]{1,0:T(8,128)(2,1)S(1)}, bf16[192,512]{1,0:T(8,128)(2,1)S(1)}, u32[]{:S(2)}, u32[]{:S(2)}) collective-permute-start(bf16[192,512]{1,0:T(8,128)(2,1)S(1)} %collective-permute-done.19.refs_2_), channel_id=1, source_target_pairs={{1,0},{0,1},{3,2},{2,3},{5,4},{4,5},{7,6},{6,7},{9,8},{8,9},{11,10... | collective-permute-start | bytes 589832 | tf_op jit(solution)/shard_map/ppermute | solution.py:278
  41.1 0.1 collective-permute-done.23.refs_7_
  41.2 1.3 %collective-permute-start.25 = (bf16[192,512]{1,0:T(8,128)(2,1)S(1)}, bf16[192,512]{1,0:T(8,128)(2,1)S(1)}, u32[]{:S(2)}, u32[]{:S(2)}) collective-permute-start(bf16[192,512]{1,0:T(8,128)(2,1)S(1)} %add_blocks.3.refs_0_), channel_id=1, source_target_pairs={{1,0},{0,1},{3,2},{2,3},{5,4},{4,5},{7,6},{6,7},{9,8},{8,9},{11,10... | collective-permute-start | bytes 589832 | tf_op jit(solution)/shard_map/ppermute | solution.py:278
  42.5 2.5 %collective-permute-start.26 = (bf16[192,512]{1,0:T(8,128)(2,1)S(1)}, bf16[192,512]{1,0:T(8,128)(2,1)S(1)}, u32[]{:S(2)}, u32[]{:S(2)}) collective-permute-start(bf16[192,512]{1,0:T(8,128)(2,1)S(1)} %add_blocks.3.refs_0_), channel_id=1, source_target_pairs={{2,0},{3,1},{0,2},{1,3},{6,4},{7,5},{4,6},{5,7},{10,8},{11,9},{8,1... | collective-permute-start | bytes 589832 | tf_op jit(solution)/shard_map/ppermute | solution.py:278
  45.0 0.7 %collective-permute-start.27 = (bf16[192,512]{1,0:T(8,128)(2,1)S(1)}, bf16[192,512]{1,0:T(8,128)(2,1)S(1)}, u32[]{:S(2)}, u32[]{:S(2)}) collective-permute-start(bf16[192,512]{1,0:T(8,128)(2,1)S(1)} %add_blocks.3.refs_0_), channel_id=1, source_target_pairs={{3,0},{2,1},{1,2},{0,3},{7,4},{6,5},{5,6},{4,7},{11,8},{10,9},{9,1... | collective-permute-start | bytes 589832 | tf_op jit(solution)/shard_map/ppermute | solution.py:278
  45.7 0.3 weights.1.weight_ref
  46.0 5.9 %collective-permute-done.24.refs_3_ = bf16[192,512]{1,0:T(8,128)(2,1)S(1)} collective-permute-done((bf16[192,512]{1,0:T(8,128)(2,1)S(1)}, bf16[192,512]{1,0:T(8,128)(2,1)S(1)}, u32[]{:S(2)}, u32[]{:S(2)}) %collective-permute-start.24) | collective-permute-done | bytes 196640 | tf_op jit(solution)/shard_map/ppermute | solution.py:278
  51.9 1.7 %combine_gate.1 = (bf16[512,512]{1,0:T(8,128)(2,1)}, f32[8,512]{1,0:T(8,128)S(1)}) custom-call(bf16[512,768]{1,0:T(8,128)(2,1)S(1)} %weights.1.weight_ref, s32[8,512]{1,0:T(8,128)S(1)} %bitcast.5, f32[16,512]{1,0:T(8,128)S(1)} %number.1.key_ref, bf16[512,512]{1,0:T(8,128)(2,1)S(1)} %copy-done.3, bf16[192,512]{1,0:T(8,128)(2,1)S(1)} %add_blocks.2.refs_0_, ...), custom_call_target="tpu_custom_call" | custom-call | bytes 2686976 | tf_op jit(solution)/shard_map/combine_gate/pallas_call | solution.py:23
  53.6 1.4 %collective-permute-start.29 = (f32[8,512]{1,0:T(8,128)S(1)}, f32[8,512]{1,0:T(8,128)S(1)}, u32[]{:S(2)}, u32[]{:S(2)}) collective-permute-start(f32[8,512]{1,0:T(8,128)S(1)} %get-tuple-element.98.refs_4_), channel_id=1, source_target_pairs={{0,8},{4,12},{8,0},{12,4},{1,9},{5,13},{9,1},{13,5},{2,10},{6,14},... | collective-permute-start | bytes 49160 | tf_op jit(solution)/shard_map/ppermute | solution.py:364
  55.0 1.8 %collective-permute-done.28.refs_5_ = f32[8,512]{1,0:T(8,128)S(1)} collective-permute-done((f32[8,512]{1,0:T(8,128)S(1)}, f32[8,512]{1,0:T(8,128)S(1)}, u32[]{:S(2)}, u32[]{:S(2)}) %collective-permute-start.28) | collective-permute-done | bytes 16416 | tf_op jit(solution)/shard_map/ppermute | solution.py:364
  56.8 0.6 collective-permute-done.29.refs_6_
  57.4 0.8 %collective-permute-done.30.refs_7_ = f32[8,512]{1,0:T(8,128)S(1)} collective-permute-done((f32[8,512]{1,0:T(8,128)S(1)}, f32[8,512]{1,0:T(8,128)S(1)}, u32[]{:S(2)}, u32[]{:S(2)}) %collective-permute-start.30) | collective-permute-done | bytes 16416 | tf_op jit(solution)/shard_map/ppermute | solution.py:364
  58.2 3.0 %collective-permute-done.27.refs_3_ = bf16[192,512]{1,0:T(8,128)(2,1)S(1)} collective-permute-done((bf16[192,512]{1,0:T(8,128)(2,1)S(1)}, bf16[192,512]{1,0:T(8,128)(2,1)S(1)}, u32[]{:S(2)}, u32[]{:S(2)}) %collective-permute-start.27) | collective-permute-done | bytes 196640 | tf_op jit(solution)/shard_map/ppermute | solution.py:278
  61.2 1.4 %combine.1 = (bf16[512,512]{1,0:T(8,128)(2,1)}, f32[8,512]{1,0:T(8,128)}) custom-call(bf16[512,768]{1,0:T(8,128)(2,1)S(1)} %weights.1.weight_ref, bf16[192,512]{1,0:T(8,128)(2,1)S(1)} %add_blocks.3.refs_0_, bf16[192,512]{1,0:T(8,128)(2,1)S(1)} %collective-permute-done.25.refs_1_, bf16[192,512]{1,0:T(8,128)(2,1)S(1)} %collective-permute-done.26.refs_2_, ...), custom_call_target="tpu_custom_call" | custom-call | flops 402653184 | bytes 2179072 | tf_op jit(solution)/shard_map/combine/pallas_call | solution.py:23
  (40 shorter events, 0.3 us)
Async XLA Ops:
  0.6 2.3 %collective-permute-start = (bf16[512,512]{1,0:T(8,128)(2,1)}, bf16[512,512]{1,0:T(8,128)(2,1)S(1)}, u32[]{:S(2)}, u32[]{:S(2)}) collective-permute-start(bf16[512,512]{1,0:T(8,128)(2,1)} %refs_0_.1), channel_id=1, source_target_pairs={{0,4},{4,0},{8,12},{12,8},{1,5},{5,1},{9,13},{13,9},{2,6},{6,2},{1... | collective-permute-start | bytes 1572872 | tf_op jit(solution)/shard_map/ppermute | solution.py:240
  1.1 0.7 %copy-start.4 = (s32[512,8]{0,1:T(8,128)S(1)}, s32[512,8]{0,1:T(8,128)}, u32[]{:S(2)}) copy-start(s32[512,8]{0,1:T(8,128)} %param.9) | copy-start | bytes 49156
  1.9 1.0 %copy-start.3 = (bf16[512,512]{1,0:T(8,128)(2,1)S(1)}, bf16[512,512]{1,0:T(8,128)(2,1)}, u32[]{:S(2)}) copy-start(bf16[512,512]{1,0:T(8,128)(2,1)} %grads_ref.1) | copy-start | bytes 1572868
  1.9 1.2 %copy-start.7 = (bf16[512,512]{1,0:T(8,128)(2,1)S(1)}, bf16[512,512]{1,0:T(8,128)(2,1)}, u32[]{:S(2)}) copy-start(bf16[512,512]{1,0:T(8,128)(2,1)} %refs_0_.1) | copy-start | bytes 1572868
  2.9 5.0 %collective-permute-start.1 = (bf16[512,512]{1,0:T(8,128)(2,1)S(1)}, bf16[512,512]{1,0:T(8,128)(2,1)S(1)}, u32[]{:S(2)}, u32[]{:S(2)}) collective-permute-start(bf16[512,512]{1,0:T(8,128)(2,1)S(1)} %copy-done.3), channel_id=1, source_target_pairs={{0,4},{4,0},{8,12},{12,8},{1,5},{5,1},{9,13},{13,9},{2,6},{6,2},{1... | collective-permute-start | bytes 1572872 | tf_op jit(solution)/shard_map/ppermute | solution.py:240
  3.4 8.3 %collective-permute-start.2 = (bf16[48,1024]{1,0:T(8,128)(2,1)S(1)}, bf16[48,1024]{1,0:T(8,128)(2,1)S(1)}, u32[]{:S(2)}, u32[]{:S(2)}) collective-permute-start(bf16[48,1024]{1,0:T(8,128)(2,1)S(1)} %get-tuple-element.58), channel_id=1, source_target_pairs={{0,8},{4,12},{8,0},{12,4},{16,24},{20,28},{24,16},{28,20},{1,9},{5... | collective-permute-start | bytes 294920 | tf_op jit(solution)/shard_map/ppermute | solution.py:250
  6.3 9.4 %collective-permute-start.4 = (bf16[48,1024]{1,0:T(8,128)(2,1)S(1)}, bf16[48,1024]{1,0:T(8,128)(2,1)S(1)}, u32[]{:S(2)}, u32[]{:S(2)}) collective-permute-start(bf16[48,1024]{1,0:T(8,128)(2,1)S(1)} %get-tuple-element.58), channel_id=1, source_target_pairs={{0,24},{4,28},{8,16},{12,20},{16,8},{20,12},{24,0},{28,4},{1,25},{... | collective-permute-start | bytes 294920 | tf_op jit(solution)/shard_map/ppermute | solution.py:250
  7.8 7.9 %copy-start = (bf16[1,768,2048]{2,1,0:T(8,128)(2,1)S(1)}, bf16[1,768,2048]{2,1,0:T(8,128)(2,1)}, u32[]{:S(2)}) copy-start(bf16[1,768,2048]{2,1,0:T(8,128)(2,1)} %refs_4_.3) | copy-start | bytes 9437188
  7.8 7.9 %copy-start.1 = (bf16[1,768,2048]{2,1,0:T(8,128)(2,1)S(1)}, bf16[1,768,2048]{2,1,0:T(8,128)(2,1)}, u32[]{:S(2)}) copy-start(bf16[1,768,2048]{2,1,0:T(8,128)(2,1)} %refs_5_.3) | copy-start | bytes 9437188
  7.8 7.9 %copy-start.2 = (bf16[1,768,2048]{2,1,0:T(8,128)(2,1)S(1)}, bf16[1,768,2048]{2,1,0:T(8,128)(2,1)}, u32[]{:S(2)}) copy-start(bf16[1,768,2048]{2,1,0:T(8,128)(2,1)} %refs_6_.3) | copy-start | bytes 9437188
  7.8 7.9 %collective-permute-start.3 = (bf16[48,1024]{1,0:T(8,128)(2,1)S(1)}, bf16[48,1024]{1,0:T(8,128)(2,1)S(1)}, u32[]{:S(2)}, u32[]{:S(2)}) collective-permute-start(bf16[48,1024]{1,0:T(8,128)(2,1)S(1)} %get-tuple-element.57.refs_0_), channel_id=1, source_target_pairs={{0,16},{4,20},{8,24},{12,28},{16,0},{20,4},{24,8},{28,12},{1,17},{... | collective-permute-start | bytes 294920 | tf_op jit(solution)/shard_map/ppermute | solution.py:250
  8.2 10.1 %collective-permute-start.5 = (bf16[48,1024]{1,0:T(8,128)(2,1)S(1)}, bf16[48,1024]{1,0:T(8,128)(2,1)S(1)}, u32[]{:S(2)}, u32[]{:S(2)}) collective-permute-start(bf16[48,1024]{1,0:T(8,128)(2,1)S(1)} %get-tuple-element.64), channel_id=1, source_target_pairs={{0,8},{4,12},{8,0},{12,4},{16,24},{20,28},{24,16},{28,20},{1,9},{5... | collective-permute-start | bytes 294920 | tf_op jit(solution)/shard_map/ppermute | solution.py:250
  10.2 8.2 %collective-permute-start.6 = (bf16[48,1024]{1,0:T(8,128)(2,1)S(1)}, bf16[48,1024]{1,0:T(8,128)(2,1)S(1)}, u32[]{:S(2)}, u32[]{:S(2)}) collective-permute-start(bf16[48,1024]{1,0:T(8,128)(2,1)S(1)} %get-tuple-element.68.refs_0_), channel_id=1, source_target_pairs={{0,16},{4,20},{8,24},{12,28},{16,0},{20,4},{24,8},{28,12},{1,17},{... | collective-permute-start | bytes 294920 | tf_op jit(solution)/shard_map/ppermute | solution.py:250
  11.7 6.6 %collective-permute-start.7 = (bf16[48,1024]{1,0:T(8,128)(2,1)S(1)}, bf16[48,1024]{1,0:T(8,128)(2,1)S(1)}, u32[]{:S(2)}, u32[]{:S(2)}) collective-permute-start(bf16[48,1024]{1,0:T(8,128)(2,1)S(1)} %get-tuple-element.64), channel_id=1, source_target_pairs={{0,24},{4,28},{8,16},{12,20},{16,8},{20,12},{24,0},{28,4},{1,25},{... | collective-permute-start | bytes 294920 | tf_op jit(solution)/shard_map/ppermute | solution.py:250
  18.3 6.0 %collective-permute-start.9 = (bf16[48,1024]{1,0:T(8,128)(2,1)S(1)}, bf16[48,1024]{1,0:T(8,128)(2,1)S(1)}, u32[]{:S(2)}, u32[]{:S(2)}) collective-permute-start(bf16[48,1024]{1,0:T(8,128)(2,1)S(1)} %get-tuple-element.67), channel_id=1, source_target_pairs={{0,16},{4,20},{8,24},{12,28},{16,0},{20,4},{24,8},{28,12},{1,17},{... | collective-permute-start | bytes 294920 | tf_op jit(solution)/shard_map/ppermute | solution.py:250
  18.8 6.1 %collective-permute-start.8 = (bf16[48,1024]{1,0:T(8,128)(2,1)S(1)}, bf16[48,1024]{1,0:T(8,128)(2,1)S(1)}, u32[]{:S(2)}, u32[]{:S(2)}) collective-permute-start(bf16[48,1024]{1,0:T(8,128)(2,1)S(1)} %get-tuple-element.66), channel_id=1, source_target_pairs={{0,8},{4,12},{8,0},{12,4},{16,24},{20,28},{24,16},{28,20},{1,9},{5... | collective-permute-start | bytes 294920 | tf_op jit(solution)/shard_map/ppermute | solution.py:250
  20.3 5.5 %collective-permute-start.10 = (bf16[48,1024]{1,0:T(8,128)(2,1)S(1)}, bf16[48,1024]{1,0:T(8,128)(2,1)S(1)}, u32[]{:S(2)}, u32[]{:S(2)}) collective-permute-start(bf16[48,1024]{1,0:T(8,128)(2,1)S(1)} %get-tuple-element.79), channel_id=1, source_target_pairs={{0,24},{4,28},{8,16},{12,20},{16,8},{20,12},{24,0},{28,4},{1,25},{... | collective-permute-start | bytes 294920 | tf_op jit(solution)/shard_map/ppermute | solution.py:250
  21.8 4.0 %collective-permute-start.11 = (bf16[48,1024]{1,0:T(8,128)(2,1)S(1)}, bf16[48,1024]{1,0:T(8,128)(2,1)S(1)}, u32[]{:S(2)}, u32[]{:S(2)}) collective-permute-start(bf16[48,1024]{1,0:T(8,128)(2,1)S(1)} %get-tuple-element.65.refs_0_), channel_id=1, source_target_pairs={{0,4},{4,0},{8,12},{12,8},{1,5},{5,1},{9,13},{13,9},{2,6},{6,2},{1... | collective-permute-start | bytes 294920 | tf_op jit(solution)/shard_map/ppermute | solution.py:240
  21.8 23.8 %copy-start.5 = (s32[512,8]{0,1:T(8,128)S(1)}, s32[512,8]{0,1:T(8,128)}, u32[]{:S(2)}) copy-start(s32[512,8]{0,1:T(8,128)} %param.9) | copy-start | bytes 49156
  21.8 23.8 %copy-start.6 = (f32[512,8]{0,1:T(8,128)S(1)}, f32[512,8]{0,1:T(8,128)}, u32[]{:S(2)}) copy-start(f32[512,8]{0,1:T(8,128)} %param.10) | copy-start | bytes 49156
  24.3 1.9 %collective-permute-start.13 = (bf16[48,1024]{1,0:T(8,128)(2,1)S(1)}, bf16[48,1024]{1,0:T(8,128)(2,1)S(1)}, u32[]{:S(2)}, u32[]{:S(2)}) collective-permute-start(bf16[48,1024]{1,0:T(8,128)(2,1)S(1)} %collective-permute-done.9.refs_2_), channel_id=1, source_target_pairs={{0,4},{4,0},{8,12},{12,8},{1,5},{5,1},{9,13},{13,9},{2,6},{6,2},{1... | collective-permute-start | bytes 294920 | tf_op jit(solution)/shard_map/ppermute | solution.py:240
  24.9 1.3 %collective-permute-start.12 = (bf16[48,1024]{1,0:T(8,128)(2,1)S(1)}, bf16[48,1024]{1,0:T(8,128)(2,1)S(1)}, u32[]{:S(2)}, u32[]{:S(2)}) collective-permute-start(bf16[48,1024]{1,0:T(8,128)(2,1)S(1)} %collective-permute-done.8.refs_1_), channel_id=1, source_target_pairs={{0,4},{4,0},{8,12},{12,8},{1,5},{5,1},{9,13},{13,9},{2,6},{6,2},{1... | collective-permute-start | bytes 294920 | tf_op jit(solution)/shard_map/ppermute | solution.py:240
  25.9 1.3 %collective-permute-start.14 = (bf16[48,1024]{1,0:T(8,128)(2,1)S(1)}, bf16[48,1024]{1,0:T(8,128)(2,1)S(1)}, u32[]{:S(2)}, u32[]{:S(2)}) collective-permute-start(bf16[48,1024]{1,0:T(8,128)(2,1)S(1)} %collective-permute-done.10.refs_3_), channel_id=1, source_target_pairs={{0,4},{4,0},{8,12},{12,8},{1,5},{5,1},{9,13},{13,9},{2,6},{6,2},{1... | collective-permute-start | bytes 294920 | tf_op jit(solution)/shard_map/ppermute | solution.py:240
  27.2 12.2 %collective-permute-start.19 = (bf16[192,512]{1,0:T(8,128)(2,1)S(1)}, bf16[192,512]{1,0:T(8,128)(2,1)S(1)}, u32[]{:S(2)}, u32[]{:S(2)}) collective-permute-start(bf16[192,512]{1,0:T(8,128)(2,1)S(1)} %add_blocks.2.refs_0_), channel_id=1, source_target_pairs={{2,0},{3,1},{0,2},{1,3},{6,4},{7,5},{4,6},{5,7},{10,8},{11,9},{8,1... | collective-permute-start | bytes 589832 | tf_op jit(solution)/shard_map/ppermute | solution.py:278
  29.9 10.0 %collective-permute-start.18 = (bf16[192,512]{1,0:T(8,128)(2,1)S(1)}, bf16[192,512]{1,0:T(8,128)(2,1)S(1)}, u32[]{:S(2)}, u32[]{:S(2)}) collective-permute-start(bf16[192,512]{1,0:T(8,128)(2,1)S(1)} %add_blocks.2.refs_0_), channel_id=1, source_target_pairs={{1,0},{0,1},{3,2},{2,3},{5,4},{4,5},{7,6},{6,7},{9,8},{8,9},{11,10... | collective-permute-start | bytes 589832 | tf_op jit(solution)/shard_map/ppermute | solution.py:278
  31.4 4.8 %collective-permute-start.15 = (bf16[48,1024]{1,0:T(8,128)(2,1)S(1)}, bf16[48,1024]{1,0:T(8,128)(2,1)S(1)}, u32[]{:S(2)}, u32[]{:S(2)}) collective-permute-start(bf16[48,1024]{1,0:T(8,128)(2,1)S(1)} %get-tuple-element.85), channel_id=1, source_target_pairs={{0,8},{4,12},{8,0},{12,4},{16,24},{20,28},{24,16},{28,20},{1,9},{5... | collective-permute-start | bytes 294920 | tf_op jit(solution)/shard_map/ppermute | solution.py:250
  32.8 6.6 %collective-permute-start.16 = (bf16[48,1024]{1,0:T(8,128)(2,1)S(1)}, bf16[48,1024]{1,0:T(8,128)(2,1)S(1)}, u32[]{:S(2)}, u32[]{:S(2)}) collective-permute-start(bf16[48,1024]{1,0:T(8,128)(2,1)S(1)} %get-tuple-element.86), channel_id=1, source_target_pairs={{0,16},{4,20},{8,24},{12,28},{16,0},{20,4},{24,8},{28,12},{1,17},{... | collective-permute-start | bytes 294920 | tf_op jit(solution)/shard_map/ppermute | solution.py:250
  33.5 6.4 %collective-permute-start.17 = (bf16[48,1024]{1,0:T(8,128)(2,1)S(1)}, bf16[48,1024]{1,0:T(8,128)(2,1)S(1)}, u32[]{:S(2)}, u32[]{:S(2)}) collective-permute-start(bf16[48,1024]{1,0:T(8,128)(2,1)S(1)} %get-tuple-element.87), channel_id=1, source_target_pairs={{0,24},{4,28},{8,16},{12,20},{16,8},{20,12},{24,0},{28,4},{1,25},{... | collective-permute-start | bytes 294920 | tf_op jit(solution)/shard_map/ppermute | solution.py:250
  36.3 4.8 %collective-permute-start.20 = (bf16[48,1024]{1,0:T(8,128)(2,1)S(1)}, bf16[48,1024]{1,0:T(8,128)(2,1)S(1)}, u32[]{:S(2)}, u32[]{:S(2)}) collective-permute-start(bf16[48,1024]{1,0:T(8,128)(2,1)S(1)} %get-tuple-element.84.refs_0_), channel_id=1, source_target_pairs={{0,4},{4,0},{8,12},{12,8},{1,5},{5,1},{9,13},{13,9},{2,6},{6,2},{1... | collective-permute-start | bytes 294920 | tf_op jit(solution)/shard_map/ppermute | solution.py:240
  39.3 1.8 %collective-permute-start.21 = (bf16[48,1024]{1,0:T(8,128)(2,1)S(1)}, bf16[48,1024]{1,0:T(8,128)(2,1)S(1)}, u32[]{:S(2)}, u32[]{:S(2)}) collective-permute-start(bf16[48,1024]{1,0:T(8,128)(2,1)S(1)} %collective-permute-done.15.refs_1_), channel_id=1, source_target_pairs={{0,4},{4,0},{8,12},{12,8},{1,5},{5,1},{9,13},{13,9},{2,6},{6,2},{1... | collective-permute-start | bytes 294920 | tf_op jit(solution)/shard_map/ppermute | solution.py:240
  39.4 1.6 %collective-permute-start.22 = (bf16[48,1024]{1,0:T(8,128)(2,1)S(1)}, bf16[48,1024]{1,0:T(8,128)(2,1)S(1)}, u32[]{:S(2)}, u32[]{:S(2)}) collective-permute-start(bf16[48,1024]{1,0:T(8,128)(2,1)S(1)} %collective-permute-done.16.refs_2_), channel_id=1, source_target_pairs={{0,4},{4,0},{8,12},{12,8},{1,5},{5,1},{9,13},{13,9},{2,6},{6,2},{1... | collective-permute-start | bytes 294920 | tf_op jit(solution)/shard_map/ppermute | solution.py:240
  39.9 1.3 %collective-permute-start.23 = (bf16[48,1024]{1,0:T(8,128)(2,1)S(1)}, bf16[48,1024]{1,0:T(8,128)(2,1)S(1)}, u32[]{:S(2)}, u32[]{:S(2)}) collective-permute-start(bf16[48,1024]{1,0:T(8,128)(2,1)S(1)} %collective-permute-done.17.refs_3_), channel_id=1, source_target_pairs={{0,4},{4,0},{8,12},{12,8},{1,5},{5,1},{9,13},{13,9},{2,6},{6,2},{1... | collective-permute-start | bytes 294920 | tf_op jit(solution)/shard_map/ppermute | solution.py:240
  40.0 11.9 %collective-permute-start.24 = (bf16[192,512]{1,0:T(8,128)(2,1)S(1)}, bf16[192,512]{1,0:T(8,128)(2,1)S(1)}, u32[]{:S(2)}, u32[]{:S(2)}) collective-permute-start(bf16[192,512]{1,0:T(8,128)(2,1)S(1)} %collective-permute-done.19.refs_2_), channel_id=1, source_target_pairs={{1,0},{0,1},{3,2},{2,3},{5,4},{4,5},{7,6},{6,7},{9,8},{8,9},{11,10... | collective-permute-start | bytes 589832 | tf_op jit(solution)/shard_map/ppermute | solution.py:278
  41.2 17.0 %collective-permute-start.25 = (bf16[192,512]{1,0:T(8,128)(2,1)S(1)}, bf16[192,512]{1,0:T(8,128)(2,1)S(1)}, u32[]{:S(2)}, u32[]{:S(2)}) collective-permute-start(bf16[192,512]{1,0:T(8,128)(2,1)S(1)} %add_blocks.3.refs_0_), channel_id=1, source_target_pairs={{1,0},{0,1},{3,2},{2,3},{5,4},{4,5},{7,6},{6,7},{9,8},{8,9},{11,10... | collective-permute-start | bytes 589832 | tf_op jit(solution)/shard_map/ppermute | solution.py:278
  42.5 15.7 %collective-permute-start.26 = (bf16[192,512]{1,0:T(8,128)(2,1)S(1)}, bf16[192,512]{1,0:T(8,128)(2,1)S(1)}, u32[]{:S(2)}, u32[]{:S(2)}) collective-permute-start(bf16[192,512]{1,0:T(8,128)(2,1)S(1)} %add_blocks.3.refs_0_), channel_id=1, source_target_pairs={{2,0},{3,1},{0,2},{1,3},{6,4},{7,5},{4,6},{5,7},{10,8},{11,9},{8,1... | collective-permute-start | bytes 589832 | tf_op jit(solution)/shard_map/ppermute | solution.py:278
  45.0 16.2 %collective-permute-start.27 = (bf16[192,512]{1,0:T(8,128)(2,1)S(1)}, bf16[192,512]{1,0:T(8,128)(2,1)S(1)}, u32[]{:S(2)}, u32[]{:S(2)}) collective-permute-start(bf16[192,512]{1,0:T(8,128)(2,1)S(1)} %add_blocks.3.refs_0_), channel_id=1, source_target_pairs={{3,0},{2,1},{1,2},{0,3},{7,4},{6,5},{5,6},{4,7},{11,8},{10,9},{9,1... | collective-permute-start | bytes 589832 | tf_op jit(solution)/shard_map/ppermute | solution.py:278
  53.6 3.2 %collective-permute-start.28 = (f32[8,512]{1,0:T(8,128)S(1)}, f32[8,512]{1,0:T(8,128)S(1)}, u32[]{:S(2)}, u32[]{:S(2)}) collective-permute-start(f32[8,512]{1,0:T(8,128)S(1)} %get-tuple-element.98.refs_4_), channel_id=1, source_target_pairs={{0,4},{4,8},{8,12},{12,0},{1,5},{5,9},{9,13},{13,1},{2,6},{6,10},{... | collective-permute-start | bytes 49160 | tf_op jit(solution)/shard_map/ppermute | solution.py:364
  53.6 3.8 %collective-permute-start.29 = (f32[8,512]{1,0:T(8,128)S(1)}, f32[8,512]{1,0:T(8,128)S(1)}, u32[]{:S(2)}, u32[]{:S(2)}) collective-permute-start(f32[8,512]{1,0:T(8,128)S(1)} %get-tuple-element.98.refs_4_), channel_id=1, source_target_pairs={{0,8},{4,12},{8,0},{12,4},{1,9},{5,13},{9,1},{13,5},{2,10},{6,14},... | collective-permute-start | bytes 49160 | tf_op jit(solution)/shard_map/ppermute | solution.py:364
  56.8 1.4 %collective-permute-start.30 = (f32[8,512]{1,0:T(8,128)S(1)}, f32[8,512]{1,0:T(8,128)S(1)}, u32[]{:S(2)}, u32[]{:S(2)}) collective-permute-start(f32[8,512]{1,0:T(8,128)S(1)} %get-tuple-element.98.refs_4_), channel_id=1, source_target_pairs={{0,12},{4,0},{8,4},{12,8},{1,13},{5,1},{9,5},{13,9},{2,14},{6,2},{... | collective-permute-start | bytes 49160 | tf_op jit(solution)/shard_map/ppermute | solution.py:364

commit v14 on v13

--- a/solution.py
+++ b/solution.py
@@ -192,7 +192,7 @@
 
 
 def combine_kernel(columns, weight_ref, *refs):
-    parts, gates = refs[:columns], refs[columns:-3]
+    parts, gates = refs[:columns][::-1], refs[columns:-3]
     out_ref, total_ref, all_ref = refs[-3:]
     place_parts(parts, all_ref)
     out_ref[...] = jnp.dot(weight_ref[...], all_ref[...], preferred_element_type=F32).astype(BF16)
@@ -333,7 +333,7 @@
         out_parts[dz] = across(out_parts, dz, dz & (dz - 1))
     back_rows = add_blocks(swap(back_pieces))
     back_parts = {0: back_rows}
-    for dz in direct + later:
+    for dz in later + direct:
         back_parts[dz] = across(back_parts, dz)
     _, out_parts = after(back_rows, out_parts)
 
@@ -366,7 +366,7 @@
         functools.partial(combine_kernel, columns),
         "combine",
         [shape(rows, width), shape(*gate_part.shape, F32)],
-        [weight_map, *[back_parts[dz] for dz in range(columns)], *gate_parts],
+        [weight_map, *[back_parts[dz] for dz in reversed(range(columns))], *gate_parts],
         combine_flops,
         [all_rows],
         limit=16,

time: 62.8 us -> 63.2 us (level)
  transfers between devices with their start and end apart: 31 -> 31, of which waited for: 14 -> 14; matrix products, arithmetic and copies ran while one was open for 0% -> 0% of each run, Pallas kernels for 13% -> 12%
where the time goes in v14:
time: 63.2 us; the launch traced here: 62.9 us
  starting transfers between devices  28.8 us (46%)
  waiting for transfers between devices  22.4 us (35%)
  Pallas kernels  9.26 us (15%)
  local copies, waits for them, and re-layouts  1.72 us (3%)
  between operations  0.73 us (1%)
    ppermute x12, starting transfers between devices, to_chip(): return lax.ppermute(value, ('dp', 'tensor'), pairs)  16.2 us
    ppermute x6, starting transfers between devices, across(): return lax.ppermute(parts[first], 'expert', pairs)  9.8 us
    ppermute x6, waiting for transfers between devices, across(): return lax.ppermute(parts[first], 'expert', pairs)  9.38 us
    pallas_call x10, Pallas kernels, call(): pl.pallas_call(kernel, out_shape=out_shape, in_specs=[spec] * len(operand...  9.26 us
    ppermute x12, waiting for transfers between devices, to_chip(): return lax.ppermute(value, ('dp', 'tensor'), pairs)  8.13 us
    ppermute x3, waiting for transfers between devices, body(): gate_parts.append(lax.ppermute(gate_part, 'tensor', pairs))  3.55 us
    ppermute x10, starting transfers between devices, to_core(): return lax.ppermute(value, 'tensor', pairs)  1.76 us
    unnamed x16, local copies, waits for them, and re-layouts  1.72 us
  transfers between devices with their start and end apart: 31, of which 14 were waited for; matrix products, arithmetic and copies ran while one was open for 0% of the time, Pallas kernels for 12%

profile of v14, /device:TPU:0, one launch (start us, length us, event | category | flops | bytes accessed | tf_op | source)
XLA Modules:
  0.0 62.9 jit_solution(11670305415549750231)
XLA Ops:
  0.6 0.5 collective-permute-start
  1.1 0.7 %copy-done.4 = s32[512,8]{0,1:T(8,128)S(1)} copy-done((s32[512,8]{0,1:T(8,128)S(1)}, s32[512,8]{0,1:T(8,128)}, u32[]{:S(2)}) %copy-start.4) | copy-done | bytes 16408
  1.9 0.1 number.1.key_ref
  2.0 0.9 %copy-done.3 = bf16[512,512]{1,0:T(8,128)(2,1)S(1)} copy-done((bf16[512,512]{1,0:T(8,128)(2,1)S(1)}, bf16[512,512]{1,0:T(8,128)(2,1)}, u32[]{:S(2)}) %copy-start.3) | copy-done | bytes 524312
  3.0 0.1 copy-done.7
  3.1 0.3 pick.2
  3.4 2.9 %collective-permute-start.2 = (bf16[48,1024]{1,0:T(8,128)(2,1)S(1)}, bf16[48,1024]{1,0:T(8,128)(2,1)S(1)}, u32[]{:S(2)}, u32[]{:S(2)}) collective-permute-start(bf16[48,1024]{1,0:T(8,128)(2,1)S(1)} %get-tuple-element.58), channel_id=1, source_target_pairs={{0,8},{4,12},{8,0},{12,4},{16,24},{20,28},{24,16},{28,20},{1,9},{5... | collective-permute-start | bytes 294920 | tf_op jit(solution)/shard_map/ppermute | solution.py:250
  6.3 1.5 %collective-permute-start.4 = (bf16[48,1024]{1,0:T(8,128)(2,1)S(1)}, bf16[48,1024]{1,0:T(8,128)(2,1)S(1)}, u32[]{:S(2)}, u32[]{:S(2)}) collective-permute-start(bf16[48,1024]{1,0:T(8,128)(2,1)S(1)} %get-tuple-element.58), channel_id=1, source_target_pairs={{0,24},{4,28},{8,16},{12,20},{16,8},{20,12},{24,0},{28,4},{1,25},{... | collective-permute-start | bytes 294920 | tf_op jit(solution)/shard_map/ppermute | solution.py:250
  7.8 0.1 collective-permute-start.3
  7.9 0.3 pick.3
  8.2 2.0 %collective-permute-start.5 = (bf16[48,1024]{1,0:T(8,128)(2,1)S(1)}, bf16[48,1024]{1,0:T(8,128)(2,1)S(1)}, u32[]{:S(2)}, u32[]{:S(2)}) collective-permute-start(bf16[48,1024]{1,0:T(8,128)(2,1)S(1)} %get-tuple-element.64), channel_id=1, source_target_pairs={{0,8},{4,12},{8,0},{12,4},{16,24},{20,28},{24,16},{28,20},{1,9},{5... | collective-permute-start | bytes 294920 | tf_op jit(solution)/shard_map/ppermute | solution.py:250
  10.2 1.5 %collective-permute-start.6 = (bf16[48,1024]{1,0:T(8,128)(2,1)S(1)}, bf16[48,1024]{1,0:T(8,128)(2,1)S(1)}, u32[]{:S(2)}, u32[]{:S(2)}) collective-permute-start(bf16[48,1024]{1,0:T(8,128)(2,1)S(1)} %get-tuple-element.68.refs_0_), channel_id=1, source_target_pairs={{0,16},{4,20},{8,24},{12,28},{16,0},{20,4},{24,8},{28,12},{1,17},{... | collective-permute-start | bytes 294920 | tf_op jit(solution)/shard_map/ppermute | solution.py:250
  11.7 1.2 %collective-permute-start.7 = (bf16[48,1024]{1,0:T(8,128)(2,1)S(1)}, bf16[48,1024]{1,0:T(8,128)(2,1)S(1)}, u32[]{:S(2)}, u32[]{:S(2)}) collective-permute-start(bf16[48,1024]{1,0:T(8,128)(2,1)S(1)} %get-tuple-element.64), channel_id=1, source_target_pairs={{0,24},{4,28},{8,16},{12,20},{16,8},{20,12},{24,0},{28,4},{1,25},{... | collective-permute-start | bytes 294920 | tf_op jit(solution)/shard_map/ppermute | solution.py:250
  12.9 2.8 %collective-permute-done.3.refs_2_ = bf16[48,1024]{1,0:T(8,128)(2,1)S(1)} collective-permute-done((bf16[48,1024]{1,0:T(8,128)(2,1)S(1)}, bf16[48,1024]{1,0:T(8,128)(2,1)S(1)}, u32[]{:S(2)}, u32[]{:S(2)}) %collective-permute-start.3) | collective-permute-done | bytes 98336 | tf_op jit(solution)/shard_map/ppermute | solution.py:250
  15.7 2.6 %forward.1 = (f32[96,768]{1,0:T(8,128)S(1)}, f32[96,768]{1,0:T(8,128)S(1)}, bf16[48,1024]{1,0:T(8,128)(2,1)S(1)}, bf16[48,1024]{1,0:T(8,128)(2,1)S(1)}, bf16[48,...) custom-call(bf16[48,1024]{1,0:T(8,128)(2,1)S(1)} %get-tuple-element.57.refs_0_, ...), custom_call_target="tpu_custom_call" | custom-call | flops 905969664 | bytes 10813440 | tf_op jit(solution)/shard_map/forward/pallas_call | solution.py:23
  18.2 0.1 collective-permute-done.6.refs_2_
  18.3 0.5 collective-permute-start.9
  18.8 1.6 %collective-permute-start.8 = (bf16[48,1024]{1,0:T(8,128)(2,1)S(1)}, bf16[48,1024]{1,0:T(8,128)(2,1)S(1)}, u32[]{:S(2)}, u32[]{:S(2)}) collective-permute-start(bf16[48,1024]{1,0:T(8,128)(2,1)S(1)} %get-tuple-element.66), channel_id=1, source_target_pairs={{0,8},{4,12},{8,0},{12,4},{16,24},{20,28},{24,16},{28,20},{1,9},{5... | collective-permute-start | bytes 294920 | tf_op jit(solution)/shard_map/ppermute | solution.py:250
  20.3 1.5 %collective-permute-start.10 = (bf16[48,1024]{1,0:T(8,128)(2,1)S(1)}, bf16[48,1024]{1,0:T(8,128)(2,1)S(1)}, u32[]{:S(2)}, u32[]{:S(2)}) collective-permute-start(bf16[48,1024]{1,0:T(8,128)(2,1)S(1)} %get-tuple-element.79), channel_id=1, source_target_pairs={{0,24},{4,28},{8,16},{12,20},{16,8},{20,12},{24,0},{28,4},{1,25},{... | collective-permute-start | bytes 294920 | tf_op jit(solution)/shard_map/ppermute | solution.py:250
  21.8 2.4 %backward.1 = (bf16[48,1024]{1,0:T(8,128)(2,1)S(1)}, bf16[48,1024]{1,0:T(8,128)(2,1)S(1)}, bf16[48,1024]{1,0:T(8,128)(2,1)S(1)}, bf16[48,1024]{1,0:T(8,128)(2,1)S(1)}) custom-call(bf16[48,1024]{1,0:T(8,128)(2,1)S(1)} %get-tuple-element.68.refs_0_, bf16[48,1024]{1,0:T(8,128)(2,1)S(1)} %collective-permute-done.5.refs_1_, ...), custom_call_target="tpu_custom_call" | custom-call | flops 905969664 | bytes 10813440 | tf_op jit(solution)/shard_map/backward/pallas_call | solution.py:23
  24.3 0.6 collective-permute-start.13
  24.9 0.1 collective-permute-start.12
  25.0 0.9 %collective-permute-done.10.refs_3_ = bf16[48,1024]{1,0:T(8,128)(2,1)S(1)} collective-permute-done((bf16[48,1024]{1,0:T(8,128)(2,1)S(1)}, bf16[48,1024]{1,0:T(8,128)(2,1)S(1)}, u32[]{:S(2)}, u32[]{:S(2)}) %collective-permute-start.10) | collective-permute-done | bytes 98336 | tf_op jit(solution)/shard_map/ppermute | solution.py:250
  25.9 0.3 collective-permute-done.12.refs_5_
  26.2 1.0 %collective-permute-done.14.refs_7_ = bf16[48,1024]{1,0:T(8,128)(2,1)S(1)} collective-permute-done((bf16[48,1024]{1,0:T(8,128)(2,1)S(1)}, bf16[48,1024]{1,0:T(8,128)(2,1)S(1)}, u32[]{:S(2)}, u32[]{:S(2)}) %collective-permute-start.14) | collective-permute-done | bytes 98336 | tf_op jit(solution)/shard_map/ppermute | solution.py:240
  27.2 2.7 %collective-permute-start.19 = (bf16[192,512]{1,0:T(8,128)(2,1)S(1)}, bf16[192,512]{1,0:T(8,128)(2,1)S(1)}, u32[]{:S(2)}, u32[]{:S(2)}) collective-permute-start(bf16[192,512]{1,0:T(8,128)(2,1)S(1)} %add_blocks.2.refs_0_), channel_id=1, source_target_pairs={{2,0},{3,1},{0,2},{1,3},{6,4},{7,5},{4,6},{5,7},{10,8},{11,9},{8,1... | collective-permute-start | bytes 589832 | tf_op jit(solution)/shard_map/ppermute | solution.py:278
  29.9 1.6 %collective-permute-start.18 = (bf16[192,512]{1,0:T(8,128)(2,1)S(1)}, bf16[192,512]{1,0:T(8,128)(2,1)S(1)}, u32[]{:S(2)}, u32[]{:S(2)}) collective-permute-start(bf16[192,512]{1,0:T(8,128)(2,1)S(1)} %add_blocks.2.refs_0_), channel_id=1, source_target_pairs={{1,0},{0,1},{3,2},{2,3},{5,4},{4,5},{7,6},{6,7},{9,8},{8,9},{11,10... | collective-permute-start | bytes 589832 | tf_op jit(solution)/shard_map/ppermute | solution.py:278
  31.4 1.3 %collective-permute-start.15 = (bf16[48,1024]{1,0:T(8,128)(2,1)S(1)}, bf16[48,1024]{1,0:T(8,128)(2,1)S(1)}, u32[]{:S(2)}, u32[]{:S(2)}) collective-permute-start(bf16[48,1024]{1,0:T(8,128)(2,1)S(1)} %get-tuple-element.85), channel_id=1, source_target_pairs={{0,8},{4,12},{8,0},{12,4},{16,24},{20,28},{24,16},{28,20},{1,9},{5... | collective-permute-start | bytes 294920 | tf_op jit(solution)/shard_map/ppermute | solution.py:250
  32.8 0.7 %collective-permute-start.16 = (bf16[48,1024]{1,0:T(8,128)(2,1)S(1)}, bf16[48,1024]{1,0:T(8,128)(2,1)S(1)}, u32[]{:S(2)}, u32[]{:S(2)}) collective-permute-start(bf16[48,1024]{1,0:T(8,128)(2,1)S(1)} %get-tuple-element.86), channel_id=1, source_target_pairs={{0,16},{4,20},{8,24},{12,28},{16,0},{20,4},{24,8},{28,12},{1,17},{... | collective-permute-start | bytes 294920 | tf_op jit(solution)/shard_map/ppermute | solution.py:250
  33.5 1.4 %collective-permute-start.17 = (bf16[48,1024]{1,0:T(8,128)(2,1)S(1)}, bf16[48,1024]{1,0:T(8,128)(2,1)S(1)}, u32[]{:S(2)}, u32[]{:S(2)}) collective-permute-start(bf16[48,1024]{1,0:T(8,128)(2,1)S(1)} %get-tuple-element.87), channel_id=1, source_target_pairs={{0,24},{4,28},{8,16},{12,20},{16,8},{20,12},{24,0},{28,4},{1,25},{... | collective-permute-start | bytes 294920 | tf_op jit(solution)/shard_map/ppermute | solution.py:250
  34.9 1.4 %collective-permute-done.15.refs_1_ = bf16[48,1024]{1,0:T(8,128)(2,1)S(1)} collective-permute-done((bf16[48,1024]{1,0:T(8,128)(2,1)S(1)}, bf16[48,1024]{1,0:T(8,128)(2,1)S(1)}, u32[]{:S(2)}, u32[]{:S(2)}) %collective-permute-start.15) | collective-permute-done | bytes 98336 | tf_op jit(solution)/shard_map/ppermute | solution.py:250
  36.3 3.0 %collective-permute-done.16.refs_2_ = bf16[48,1024]{1,0:T(8,128)(2,1)S(1)} collective-permute-done((bf16[48,1024]{1,0:T(8,128)(2,1)S(1)}, bf16[48,1024]{1,0:T(8,128)(2,1)S(1)}, u32[]{:S(2)}, u32[]{:S(2)}) %collective-permute-start.16) | collective-permute-done | bytes 98336 | tf_op jit(solution)/shard_map/ppermute | solution.py:250
  39.3 0.1 collective-permute-done.19.refs_2_
  39.4 0.4 collective-permute-start.22
  39.9 0.1 collective-permute-start.23
  40.0 1.1 %collective-permute-start.24 = (bf16[192,512]{1,0:T(8,128)(2,1)S(1)}, bf16[192,512]{1,0:T(8,128)(2,1)S(1)}, u32[]{:S(2)}, u32[]{:S(2)}) collective-permute-start(bf16[192,512]{1,0:T(8,128)(2,1)S(1)} %collective-permute-done.19.refs_2_), channel_id=1, source_target_pairs={{1,0},{0,1},{3,2},{2,3},{5,4},{4,5},{7,6},{6,7},{9,8},{8,9},{11,10... | collective-permute-start | bytes 589832 | tf_op jit(solution)/shard_map/ppermute | solution.py:278
  41.1 0.1 collective-permute-done.23.refs_7_
  41.2 3.2 %collective-permute-start.25 = (bf16[192,512]{1,0:T(8,128)(2,1)S(1)}, bf16[192,512]{1,0:T(8,128)(2,1)S(1)}, u32[]{:S(2)}, u32[]{:S(2)}) collective-permute-start(bf16[192,512]{1,0:T(8,128)(2,1)S(1)} %add_blocks.3.refs_3_), channel_id=1, source_target_pairs={{3,0},{2,1},{1,2},{0,3},{7,4},{6,5},{5,6},{4,7},{11,8},{10,9},{9,1... | collective-permute-start | bytes 589832 | tf_op jit(solution)/shard_map/ppermute | solution.py:278
  44.4 1.2 %collective-permute-start.27 = (bf16[192,512]{1,0:T(8,128)(2,1)S(1)}, bf16[192,512]{1,0:T(8,128)(2,1)S(1)}, u32[]{:S(2)}, u32[]{:S(2)}) collective-permute-start(bf16[192,512]{1,0:T(8,128)(2,1)S(1)} %add_blocks.3.refs_3_), channel_id=1, source_target_pairs={{1,0},{0,1},{3,2},{2,3},{5,4},{4,5},{7,6},{6,7},{9,8},{8,9},{11,10... | collective-permute-start | bytes 589832 | tf_op jit(solution)/shard_map/ppermute | solution.py:278
  45.7 0.3 weights.1.weight_ref
  46.0 1.3 %collective-permute-done.24.refs_3_ = bf16[192,512]{1,0:T(8,128)(2,1)S(1)} collective-permute-done((bf16[192,512]{1,0:T(8,128)(2,1)S(1)}, bf16[192,512]{1,0:T(8,128)(2,1)S(1)}, u32[]{:S(2)}, u32[]{:S(2)}) %collective-permute-start.24) | collective-permute-done | bytes 196640 | tf_op jit(solution)/shard_map/ppermute | solution.py:278
  47.3 1.7 %combine_gate.1 = (bf16[512,512]{1,0:T(8,128)(2,1)}, f32[8,512]{1,0:T(8,128)S(1)}) custom-call(bf16[512,768]{1,0:T(8,128)(2,1)S(1)} %weights.1.weight_ref, s32[8,512]{1,0:T(8,128)S(1)} %bitcast.5, f32[16,512]{1,0:T(8,128)S(1)} %number.1.key_ref, bf16[512,512]{1,0:T(8,128)(2,1)S(1)} %copy-done.3, bf16[192,512]{1,0:T(8,128)(2,1)S(1)} %add_blocks.2.refs_0_, ...), custom_call_target="tpu_custom_call" | custom-call | bytes 2686976 | tf_op jit(solution)/shard_map/combine_gate/pallas_call | solution.py:23
  49.0 1.1 %collective-permute-start.29 = (f32[8,512]{1,0:T(8,128)S(1)}, f32[8,512]{1,0:T(8,128)S(1)}, u32[]{:S(2)}, u32[]{:S(2)}) collective-permute-start(f32[8,512]{1,0:T(8,128)S(1)} %get-tuple-element.98.refs_4_), channel_id=1, source_target_pairs={{0,8},{4,12},{8,0},{12,4},{1,9},{5,13},{9,1},{13,5},{2,10},{6,14},... | collective-permute-start | bytes 49160 | tf_op jit(solution)/shard_map/ppermute | solution.py:364
  50.0 2.1 %collective-permute-done.28.refs_5_ = f32[8,512]{1,0:T(8,128)S(1)} collective-permute-done((f32[8,512]{1,0:T(8,128)S(1)}, f32[8,512]{1,0:T(8,128)S(1)}, u32[]{:S(2)}, u32[]{:S(2)}) %collective-permute-start.28) | collective-permute-done | bytes 16416 | tf_op jit(solution)/shard_map/ppermute | solution.py:364
  52.1 0.6 %collective-permute-done.29.refs_6_ = f32[8,512]{1,0:T(8,128)S(1)} collective-permute-done((f32[8,512]{1,0:T(8,128)S(1)}, f32[8,512]{1,0:T(8,128)S(1)}, u32[]{:S(2)}, u32[]{:S(2)}) %collective-permute-start.29) | collective-permute-done | bytes 16416 | tf_op jit(solution)/shard_map/ppermute | solution.py:364
  52.8 0.8 %collective-permute-done.30.refs_7_ = f32[8,512]{1,0:T(8,128)S(1)} collective-permute-done((f32[8,512]{1,0:T(8,128)S(1)}, f32[8,512]{1,0:T(8,128)S(1)}, u32[]{:S(2)}, u32[]{:S(2)}) %collective-permute-start.30) | collective-permute-done | bytes 16416 | tf_op jit(solution)/shard_map/ppermute | solution.py:364
  53.6 8.0 %collective-permute-done.26.refs_1_ = bf16[192,512]{1,0:T(8,128)(2,1)S(1)} collective-permute-done((bf16[192,512]{1,0:T(8,128)(2,1)S(1)}, bf16[192,512]{1,0:T(8,128)(2,1)S(1)}, u32[]{:S(2)}, u32[]{:S(2)}) %collective-permute-start.26) | collective-permute-done | bytes 196640 | tf_op jit(solution)/shard_map/ppermute | solution.py:278
  61.6 1.4 %combine.1 = (bf16[512,512]{1,0:T(8,128)(2,1)}, f32[8,512]{1,0:T(8,128)}) custom-call(bf16[512,768]{1,0:T(8,128)(2,1)S(1)} %weights.1.weight_ref, bf16[192,512]{1,0:T(8,128)(2,1)S(1)} %collective-permute-done.25.refs_0_, bf16[192,512]{1,0:T(8,128)(2,1)S(1)} %collective-permute-done.26.refs_1_, bf16[192,512]{1,0:T(8,128)(2,1)S(1)} %collective-permute-done.27.refs_2_, ...), custom_call_target="tpu_custom_call" | custom-call | flops 402653184 | bytes 2179072 | tf_op jit(solution)/shard_map/combine/pallas_call | solution.py:23
  (40 shorter events, 0.2 us)
Async XLA Ops:
  0.6 2.3 %collective-permute-start = (bf16[512,512]{1,0:T(8,128)(2,1)}, bf16[512,512]{1,0:T(8,128)(2,1)S(1)}, u32[]{:S(2)}, u32[]{:S(2)}) collective-permute-start(bf16[512,512]{1,0:T(8,128)(2,1)} %refs_0_.1), channel_id=1, source_target_pairs={{0,4},{4,0},{8,12},{12,8},{1,5},{5,1},{9,13},{13,9},{2,6},{6,2},{1... | collective-permute-start | bytes 1572872 | tf_op jit(solution)/shard_map/ppermute | solution.py:240
  1.1 0.7 %copy-start.4 = (s32[512,8]{0,1:T(8,128)S(1)}, s32[512,8]{0,1:T(8,128)}, u32[]{:S(2)}) copy-start(s32[512,8]{0,1:T(8,128)} %param.9) | copy-start | bytes 49156
  1.9 1.0 %copy-start.3 = (bf16[512,512]{1,0:T(8,128)(2,1)S(1)}, bf16[512,512]{1,0:T(8,128)(2,1)}, u32[]{:S(2)}) copy-start(bf16[512,512]{1,0:T(8,128)(2,1)} %grads_ref.1) | copy-start | bytes 1572868
  1.9 1.2 %copy-start.7 = (bf16[512,512]{1,0:T(8,128)(2,1)S(1)}, bf16[512,512]{1,0:T(8,128)(2,1)}, u32[]{:S(2)}) copy-start(bf16[512,512]{1,0:T(8,128)(2,1)} %refs_0_.1) | copy-start | bytes 1572868
  2.9 5.0 %collective-permute-start.1 = (bf16[512,512]{1,0:T(8,128)(2,1)S(1)}, bf16[512,512]{1,0:T(8,128)(2,1)S(1)}, u32[]{:S(2)}, u32[]{:S(2)}) collective-permute-start(bf16[512,512]{1,0:T(8,128)(2,1)S(1)} %copy-done.3), channel_id=1, source_target_pairs={{0,4},{4,0},{8,12},{12,8},{1,5},{5,1},{9,13},{13,9},{2,6},{6,2},{1... | collective-permute-start | bytes 1572872 | tf_op jit(solution)/shard_map/ppermute | solution.py:240
  3.4 8.3 %collective-permute-start.2 = (bf16[48,1024]{1,0:T(8,128)(2,1)S(1)}, bf16[48,1024]{1,0:T(8,128)(2,1)S(1)}, u32[]{:S(2)}, u32[]{:S(2)}) collective-permute-start(bf16[48,1024]{1,0:T(8,128)(2,1)S(1)} %get-tuple-element.58), channel_id=1, source_target_pairs={{0,8},{4,12},{8,0},{12,4},{16,24},{20,28},{24,16},{28,20},{1,9},{5... | collective-permute-start | bytes 294920 | tf_op jit(solution)/shard_map/ppermute | solution.py:250
  6.3 9.4 %collective-permute-start.4 = (bf16[48,1024]{1,0:T(8,128)(2,1)S(1)}, bf16[48,1024]{1,0:T(8,128)(2,1)S(1)}, u32[]{:S(2)}, u32[]{:S(2)}) collective-permute-start(bf16[48,1024]{1,0:T(8,128)(2,1)S(1)} %get-tuple-element.58), channel_id=1, source_target_pairs={{0,24},{4,28},{8,16},{12,20},{16,8},{20,12},{24,0},{28,4},{1,25},{... | collective-permute-start | bytes 294920 | tf_op jit(solution)/shard_map/ppermute | solution.py:250
  7.8 7.9 %copy-start = (bf16[1,768,2048]{2,1,0:T(8,128)(2,1)S(1)}, bf16[1,768,2048]{2,1,0:T(8,128)(2,1)}, u32[]{:S(2)}) copy-start(bf16[1,768,2048]{2,1,0:T(8,128)(2,1)} %refs_4_.3) | copy-start | bytes 9437188
  7.8 7.9 %copy-start.1 = (bf16[1,768,2048]{2,1,0:T(8,128)(2,1)S(1)}, bf16[1,768,2048]{2,1,0:T(8,128)(2,1)}, u32[]{:S(2)}) copy-start(bf16[1,768,2048]{2,1,0:T(8,128)(2,1)} %refs_5_.3) | copy-start | bytes 9437188
  7.8 7.9 %copy-start.2 = (bf16[1,768,2048]{2,1,0:T(8,128)(2,1)S(1)}, bf16[1,768,2048]{2,1,0:T(8,128)(2,1)}, u32[]{:S(2)}) copy-start(bf16[1,768,2048]{2,1,0:T(8,128)(2,1)} %refs_6_.3) | copy-start | bytes 9437188
  7.8 7.9 %collective-permute-start.3 = (bf16[48,1024]{1,0:T(8,128)(2,1)S(1)}, bf16[48,1024]{1,0:T(8,128)(2,1)S(1)}, u32[]{:S(2)}, u32[]{:S(2)}) collective-permute-start(bf16[48,1024]{1,0:T(8,128)(2,1)S(1)} %get-tuple-element.57.refs_0_), channel_id=1, source_target_pairs={{0,16},{4,20},{8,24},{12,28},{16,0},{20,4},{24,8},{28,12},{1,17},{... | collective-permute-start | bytes 294920 | tf_op jit(solution)/shard_map/ppermute | solution.py:250
  8.2 10.1 %collective-permute-start.5 = (bf16[48,1024]{1,0:T(8,128)(2,1)S(1)}, bf16[48,1024]{1,0:T(8,128)(2,1)S(1)}, u32[]{:S(2)}, u32[]{:S(2)}) collective-permute-start(bf16[48,1024]{1,0:T(8,128)(2,1)S(1)} %get-tuple-element.64), channel_id=1, source_target_pairs={{0,8},{4,12},{8,0},{12,4},{16,24},{20,28},{24,16},{28,20},{1,9},{5... | collective-permute-start | bytes 294920 | tf_op jit(solution)/shard_map/ppermute | solution.py:250
  10.2 8.2 %collective-permute-start.6 = (bf16[48,1024]{1,0:T(8,128)(2,1)S(1)}, bf16[48,1024]{1,0:T(8,128)(2,1)S(1)}, u32[]{:S(2)}, u32[]{:S(2)}) collective-permute-start(bf16[48,1024]{1,0:T(8,128)(2,1)S(1)} %get-tuple-element.68.refs_0_), channel_id=1, source_target_pairs={{0,16},{4,20},{8,24},{12,28},{16,0},{20,4},{24,8},{28,12},{1,17},{... | collective-permute-start | bytes 294920 | tf_op jit(solution)/shard_map/ppermute | solution.py:250
  11.7 6.6 %collective-permute-start.7 = (bf16[48,1024]{1,0:T(8,128)(2,1)S(1)}, bf16[48,1024]{1,0:T(8,128)(2,1)S(1)}, u32[]{:S(2)}, u32[]{:S(2)}) collective-permute-start(bf16[48,1024]{1,0:T(8,128)(2,1)S(1)} %get-tuple-element.64), channel_id=1, source_target_pairs={{0,24},{4,28},{8,16},{12,20},{16,8},{20,12},{24,0},{28,4},{1,25},{... | collective-permute-start | bytes 294920 | tf_op jit(solution)/shard_map/ppermute | solution.py:250
  18.3 6.0 %collective-permute-start.9 = (bf16[48,1024]{1,0:T(8,128)(2,1)S(1)}, bf16[48,1024]{1,0:T(8,128)(2,1)S(1)}, u32[]{:S(2)}, u32[]{:S(2)}) collective-permute-start(bf16[48,1024]{1,0:T(8,128)(2,1)S(1)} %get-tuple-element.67), channel_id=1, source_target_pairs={{0,16},{4,20},{8,24},{12,28},{16,0},{20,4},{24,8},{28,12},{1,17},{... | collective-permute-start | bytes 294920 | tf_op jit(solution)/shard_map/ppermute | solution.py:250
  18.8 6.1 %collective-permute-start.8 = (bf16[48,1024]{1,0:T(8,128)(2,1)S(1)}, bf16[48,1024]{1,0:T(8,128)(2,1)S(1)}, u32[]{:S(2)}, u32[]{:S(2)}) collective-permute-start(bf16[48,1024]{1,0:T(8,128)(2,1)S(1)} %get-tuple-element.66), channel_id=1, source_target_pairs={{0,8},{4,12},{8,0},{12,4},{16,24},{20,28},{24,16},{28,20},{1,9},{5... | collective-permute-start | bytes 294920 | tf_op jit(solution)/shard_map/ppermute | solution.py:250
  20.3 5.5 %collective-permute-start.10 = (bf16[48,1024]{1,0:T(8,128)(2,1)S(1)}, bf16[48,1024]{1,0:T(8,128)(2,1)S(1)}, u32[]{:S(2)}, u32[]{:S(2)}) collective-permute-start(bf16[48,1024]{1,0:T(8,128)(2,1)S(1)} %get-tuple-element.79), channel_id=1, source_target_pairs={{0,24},{4,28},{8,16},{12,20},{16,8},{20,12},{24,0},{28,4},{1,25},{... | collective-permute-start | bytes 294920 | tf_op jit(solution)/shard_map/ppermute | solution.py:250
  21.8 4.0 %collective-permute-start.11 = (bf16[48,1024]{1,0:T(8,128)(2,1)S(1)}, bf16[48,1024]{1,0:T(8,128)(2,1)S(1)}, u32[]{:S(2)}, u32[]{:S(2)}) collective-permute-start(bf16[48,1024]{1,0:T(8,128)(2,1)S(1)} %get-tuple-element.65.refs_0_), channel_id=1, source_target_pairs={{0,4},{4,0},{8,12},{12,8},{1,5},{5,1},{9,13},{13,9},{2,6},{6,2},{1... | collective-permute-start | bytes 294920 | tf_op jit(solution)/shard_map/ppermute | solution.py:240
  21.8 23.8 %copy-start.5 = (s32[512,8]{0,1:T(8,128)S(1)}, s32[512,8]{0,1:T(8,128)}, u32[]{:S(2)}) copy-start(s32[512,8]{0,1:T(8,128)} %param.9) | copy-start | bytes 49156
  21.8 23.8 %copy-start.6 = (f32[512,8]{0,1:T(8,128)S(1)}, f32[512,8]{0,1:T(8,128)}, u32[]{:S(2)}) copy-start(f32[512,8]{0,1:T(8,128)} %param.10) | copy-start | bytes 49156
  24.3 1.9 %collective-permute-start.13 = (bf16[48,1024]{1,0:T(8,128)(2,1)S(1)}, bf16[48,1024]{1,0:T(8,128)(2,1)S(1)}, u32[]{:S(2)}, u32[]{:S(2)}) collective-permute-start(bf16[48,1024]{1,0:T(8,128)(2,1)S(1)} %collective-permute-done.9.refs_2_), channel_id=1, source_target_pairs={{0,4},{4,0},{8,12},{12,8},{1,5},{5,1},{9,13},{13,9},{2,6},{6,2},{1... | collective-permute-start | bytes 294920 | tf_op jit(solution)/shard_map/ppermute | solution.py:240
  24.9 1.3 %collective-permute-start.12 = (bf16[48,1024]{1,0:T(8,128)(2,1)S(1)}, bf16[48,1024]{1,0:T(8,128)(2,1)S(1)}, u32[]{:S(2)}, u32[]{:S(2)}) collective-permute-start(bf16[48,1024]{1,0:T(8,128)(2,1)S(1)} %collective-permute-done.8.refs_1_), channel_id=1, source_target_pairs={{0,4},{4,0},{8,12},{12,8},{1,5},{5,1},{9,13},{13,9},{2,6},{6,2},{1... | collective-permute-start | bytes 294920 | tf_op jit(solution)/shard_map/ppermute | solution.py:240
  25.9 1.3 %collective-permute-start.14 = (bf16[48,1024]{1,0:T(8,128)(2,1)S(1)}, bf16[48,1024]{1,0:T(8,128)(2,1)S(1)}, u32[]{:S(2)}, u32[]{:S(2)}) collective-permute-start(bf16[48,1024]{1,0:T(8,128)(2,1)S(1)} %collective-permute-done.10.refs_3_), channel_id=1, source_target_pairs={{0,4},{4,0},{8,12},{12,8},{1,5},{5,1},{9,13},{13,9},{2,6},{6,2},{1... | collective-permute-start | bytes 294920 | tf_op jit(solution)/shard_map/ppermute | solution.py:240
  27.2 12.2 %collective-permute-start.19 = (bf16[192,512]{1,0:T(8,128)(2,1)S(1)}, bf16[192,512]{1,0:T(8,128)(2,1)S(1)}, u32[]{:S(2)}, u32[]{:S(2)}) collective-permute-start(bf16[192,512]{1,0:T(8,128)(2,1)S(1)} %add_blocks.2.refs_0_), channel_id=1, source_target_pairs={{2,0},{3,1},{0,2},{1,3},{6,4},{7,5},{4,6},{5,7},{10,8},{11,9},{8,1... | collective-permute-start | bytes 589832 | tf_op jit(solution)/shard_map/ppermute | solution.py:278
  29.9 10.0 %collective-permute-start.18 = (bf16[192,512]{1,0:T(8,128)(2,1)S(1)}, bf16[192,512]{1,0:T(8,128)(2,1)S(1)}, u32[]{:S(2)}, u32[]{:S(2)}) collective-permute-start(bf16[192,512]{1,0:T(8,128)(2,1)S(1)} %add_blocks.2.refs_0_), channel_id=1, source_target_pairs={{1,0},{0,1},{3,2},{2,3},{5,4},{4,5},{7,6},{6,7},{9,8},{8,9},{11,10... | collective-permute-start | bytes 589832 | tf_op jit(solution)/shard_map/ppermute | solution.py:278
  31.4 4.8 %collective-permute-start.15 = (bf16[48,1024]{1,0:T(8,128)(2,1)S(1)}, bf16[48,1024]{1,0:T(8,128)(2,1)S(1)}, u32[]{:S(2)}, u32[]{:S(2)}) collective-permute-start(bf16[48,1024]{1,0:T(8,128)(2,1)S(1)} %get-tuple-element.85), channel_id=1, source_target_pairs={{0,8},{4,12},{8,0},{12,4},{16,24},{20,28},{24,16},{28,20},{1,9},{5... | collective-permute-start | bytes 294920 | tf_op jit(solution)/shard_map/ppermute | solution.py:250
  32.8 6.6 %collective-permute-start.16 = (bf16[48,1024]{1,0:T(8,128)(2,1)S(1)}, bf16[48,1024]{1,0:T(8,128)(2,1)S(1)}, u32[]{:S(2)}, u32[]{:S(2)}) collective-permute-start(bf16[48,1024]{1,0:T(8,128)(2,1)S(1)} %get-tuple-element.86), channel_id=1, source_target_pairs={{0,16},{4,20},{8,24},{12,28},{16,0},{20,4},{24,8},{28,12},{1,17},{... | collective-permute-start | bytes 294920 | tf_op jit(solution)/shard_map/ppermute | solution.py:250
  33.5 6.4 %collective-permute-start.17 = (bf16[48,1024]{1,0:T(8,128)(2,1)S(1)}, bf16[48,1024]{1,0:T(8,128)(2,1)S(1)}, u32[]{:S(2)}, u32[]{:S(2)}) collective-permute-start(bf16[48,1024]{1,0:T(8,128)(2,1)S(1)} %get-tuple-element.87), channel_id=1, source_target_pairs={{0,24},{4,28},{8,16},{12,20},{16,8},{20,12},{24,0},{28,4},{1,25},{... | collective-permute-start | bytes 294920 | tf_op jit(solution)/shard_map/ppermute | solution.py:250
  36.3 4.8 %collective-permute-start.20 = (bf16[48,1024]{1,0:T(8,128)(2,1)S(1)}, bf16[48,1024]{1,0:T(8,128)(2,1)S(1)}, u32[]{:S(2)}, u32[]{:S(2)}) collective-permute-start(bf16[48,1024]{1,0:T(8,128)(2,1)S(1)} %get-tuple-element.84.refs_0_), channel_id=1, source_target_pairs={{0,4},{4,0},{8,12},{12,8},{1,5},{5,1},{9,13},{13,9},{2,6},{6,2},{1... | collective-permute-start | bytes 294920 | tf_op jit(solution)/shard_map/ppermute | solution.py:240
  39.3 1.8 %collective-permute-start.21 = (bf16[48,1024]{1,0:T(8,128)(2,1)S(1)}, bf16[48,1024]{1,0:T(8,128)(2,1)S(1)}, u32[]{:S(2)}, u32[]{:S(2)}) collective-permute-start(bf16[48,1024]{1,0:T(8,128)(2,1)S(1)} %collective-permute-done.15.refs_1_), channel_id=1, source_target_pairs={{0,4},{4,0},{8,12},{12,8},{1,5},{5,1},{9,13},{13,9},{2,6},{6,2},{1... | collective-permute-start | bytes 294920 | tf_op jit(solution)/shard_map/ppermute | solution.py:240
  39.4 1.6 %collective-permute-start.22 = (bf16[48,1024]{1,0:T(8,128)(2,1)S(1)}, bf16[48,1024]{1,0:T(8,128)(2,1)S(1)}, u32[]{:S(2)}, u32[]{:S(2)}) collective-permute-start(bf16[48,1024]{1,0:T(8,128)(2,1)S(1)} %collective-permute-done.16.refs_2_), channel_id=1, source_target_pairs={{0,4},{4,0},{8,12},{12,8},{1,5},{5,1},{9,13},{13,9},{2,6},{6,2},{1... | collective-permute-start | bytes 294920 | tf_op jit(solution)/shard_map/ppermute | solution.py:240
  39.9 1.3 %collective-permute-start.23 = (bf16[48,1024]{1,0:T(8,128)(2,1)S(1)}, bf16[48,1024]{1,0:T(8,128)(2,1)S(1)}, u32[]{:S(2)}, u32[]{:S(2)}) collective-permute-start(bf16[48,1024]{1,0:T(8,128)(2,1)S(1)} %collective-permute-done.17.refs_3_), channel_id=1, source_target_pairs={{0,4},{4,0},{8,12},{12,8},{1,5},{5,1},{9,13},{13,9},{2,6},{6,2},{1... | collective-permute-start | bytes 294920 | tf_op jit(solution)/shard_map/ppermute | solution.py:240
  40.0 7.3 %collective-permute-start.24 = (bf16[192,512]{1,0:T(8,128)(2,1)S(1)}, bf16[192,512]{1,0:T(8,128)(2,1)S(1)}, u32[]{:S(2)}, u32[]{:S(2)}) collective-permute-start(bf16[192,512]{1,0:T(8,128)(2,1)S(1)} %collective-permute-done.19.refs_2_), channel_id=1, source_target_pairs={{1,0},{0,1},{3,2},{2,3},{5,4},{4,5},{7,6},{6,7},{9,8},{8,9},{11,10... | collective-permute-start | bytes 589832 | tf_op jit(solution)/shard_map/ppermute | solution.py:278
  41.2 12.4 %collective-permute-start.25 = (bf16[192,512]{1,0:T(8,128)(2,1)S(1)}, bf16[192,512]{1,0:T(8,128)(2,1)S(1)}, u32[]{:S(2)}, u32[]{:S(2)}) collective-permute-start(bf16[192,512]{1,0:T(8,128)(2,1)S(1)} %add_blocks.3.refs_3_), channel_id=1, source_target_pairs={{3,0},{2,1},{1,2},{0,3},{7,4},{6,5},{5,6},{4,7},{11,8},{10,9},{9,1... | collective-permute-start | bytes 589832 | tf_op jit(solution)/shard_map/ppermute | solution.py:278
  44.4 17.2 %collective-permute-start.26 = (bf16[192,512]{1,0:T(8,128)(2,1)S(1)}, bf16[192,512]{1,0:T(8,128)(2,1)S(1)}, u32[]{:S(2)}, u32[]{:S(2)}) collective-permute-start(bf16[192,512]{1,0:T(8,128)(2,1)S(1)} %add_blocks.3.refs_3_), channel_id=1, source_target_pairs={{2,0},{3,1},{0,2},{1,3},{6,4},{7,5},{4,6},{5,7},{10,8},{11,9},{8,1... | collective-permute-start | bytes 589832 | tf_op jit(solution)/shard_map/ppermute | solution.py:278
  44.4 17.2 %collective-permute-start.27 = (bf16[192,512]{1,0:T(8,128)(2,1)S(1)}, bf16[192,512]{1,0:T(8,128)(2,1)S(1)}, u32[]{:S(2)}, u32[]{:S(2)}) collective-permute-start(bf16[192,512]{1,0:T(8,128)(2,1)S(1)} %add_blocks.3.refs_3_), channel_id=1, source_target_pairs={{1,0},{0,1},{3,2},{2,3},{5,4},{4,5},{7,6},{6,7},{9,8},{8,9},{11,10... | collective-permute-start | bytes 589832 | tf_op jit(solution)/shard_map/ppermute | solution.py:278
  49.0 3.2 %collective-permute-start.28 = (f32[8,512]{1,0:T(8,128)S(1)}, f32[8,512]{1,0:T(8,128)S(1)}, u32[]{:S(2)}, u32[]{:S(2)}) collective-permute-start(f32[8,512]{1,0:T(8,128)S(1)} %get-tuple-element.98.refs_4_), channel_id=1, source_target_pairs={{0,4},{4,8},{8,12},{12,0},{1,5},{5,9},{9,13},{13,1},{2,6},{6,10},{... | collective-permute-start | bytes 49160 | tf_op jit(solution)/shard_map/ppermute | solution.py:364
  49.0 3.8 %collective-permute-start.29 = (f32[8,512]{1,0:T(8,128)S(1)}, f32[8,512]{1,0:T(8,128)S(1)}, u32[]{:S(2)}, u32[]{:S(2)}) collective-permute-start(f32[8,512]{1,0:T(8,128)S(1)} %get-tuple-element.98.refs_4_), channel_id=1, source_target_pairs={{0,8},{4,12},{8,0},{12,4},{1,9},{5,13},{9,1},{13,5},{2,10},{6,14},... | collective-permute-start | bytes 49160 | tf_op jit(solution)/shard_map/ppermute | solution.py:364
  52.1 1.4 %collective-permute-start.30 = (f32[8,512]{1,0:T(8,128)S(1)}, f32[8,512]{1,0:T(8,128)S(1)}, u32[]{:S(2)}, u32[]{:S(2)}) collective-permute-start(f32[8,512]{1,0:T(8,128)S(1)} %get-tuple-element.98.refs_4_), channel_id=1, source_target_pairs={{0,12},{4,0},{8,4},{12,8},{1,13},{5,1},{9,5},{13,9},{2,14},{6,2},{... | collective-permute-start | bytes 49160 | tf_op jit(solution)/shard_map/ppermute | solution.py:364

commit v15 on v14

--- a/solution.py
+++ b/solution.py
@@ -135,8 +135,8 @@
 
 
 def add_blocks_kernel(chips, cores, *refs):
-    pieces, out_ref = refs[:-1], refs[-1]
-    width = out_ref.shape[1]
+    pieces, out_ref, halves = refs[:-3], refs[-3], refs[-2:]
+    height, width = halves[0].shape
     count = len(pieces) // cores
     _, core, _ = position(cores)
     column = pl.ds(pl.multiple_of(core * width, width), width)
@@ -148,6 +148,8 @@
                 total = term if total is None else total + term
             row = (dh * cores + dc) * CAP
             out_ref[row : row + CAP, :] = total.astype(BF16)
+    for index, half in enumerate(halves):
+        half[...] = out_ref[index * height : (index + 1) * height, :]
 
 
 def partner_column(e, dz, columns):
@@ -191,10 +193,11 @@
         all_ref[index * height : (index + 1) * height, :] = part[...]
 
 
-def combine_kernel(columns, weight_ref, *refs):
-    parts, gates = refs[:columns][::-1], refs[columns:-3]
+def combine_kernel(starts, weight_ref, *refs):
+    parts, gates = refs[: len(starts)], refs[len(starts) : -3]
     out_ref, total_ref, all_ref = refs[-3:]
-    place_parts(parts, all_ref)
+    for start, part in zip(starts, parts):
+        all_ref[start : start + part.shape[0], :] = part[...]
     out_ref[...] = jnp.dot(weight_ref[...], all_ref[...], preferred_element_type=F32).astype(BF16)
     total = gates[0][...]
     for gate in gates[1:]:
@@ -268,7 +271,7 @@
         return call(
             functools.partial(add_blocks_kernel, chips, cores),
             "add_blocks",
-            shape(slots, width),
+            [shape(slots, width)] + [shape(slots // 2, width)] * 2,
             pieces,
             2 * slots * width,
         )
@@ -321,7 +324,7 @@
         limit=24,
     )
     out_pieces[first], backs = after(out_pieces[first], backs)
-    out_rows = add_blocks(swap(out_pieces))
+    out_rows, _, _ = add_blocks(swap(out_pieces))
     out_rows, backs = after(out_rows, backs)
     out_parts = {0: out_rows}
     for dz in direct:
@@ -331,10 +334,15 @@
     back_pieces[-1], out_parts = after(back_pieces[-1], out_parts)
     for dz in later:
         out_parts[dz] = across(out_parts, dz, dz & (dz - 1))
-    back_rows = add_blocks(swap(back_pieces))
-    back_parts = {0: back_rows}
-    for dz in later + direct:
-        back_parts[dz] = across(back_parts, dz)
+    back_rows, low, high = add_blocks(swap(back_pieces))
+    lows, highs = {0: low}, {0: high}
+    for dz in range(2, columns):
+        lows[dz] = across(lows, dz, dz & (dz - 1))
+        highs[dz] = across(highs, dz)
+    back_parts = [(lows[dz], dz * slots) for dz in direct if dz > 1]
+    back_parts += [(highs[dz], dz * slots + slots // 2) for dz in reversed(range(2, columns))]
+    back_parts += [(across({0: back_rows}, 1), slots)] if columns > 1 else []
+    back_parts += [(back_rows, 0)] + [(lows[dz], dz * slots) for dz in later]
     _, out_parts = after(back_rows, out_parts)
 
     weight_map = call(
@@ -358,15 +366,15 @@
         [all_rows, pltpu.VMEM((experts * CAP, rows), F32)],
         limit=24,
     )
-    gate_parts = [gate_part]
-    for dt in range(1, groups):
-        pairs = [(t, (t + dt) % groups) for t in range(groups)]
-        gate_parts.append(lax.ppermute(gate_part, "tensor", pairs))
+    chip_part = gate_part
+    for dc in range(1, cores):
+        chip_part = chip_part + to_core(gate_part, dc)
+    gate_parts = [to_chip(chip_part, 0, dh) for dh in range(chips)]
     grad_tokens, grad_gates = call(
-        functools.partial(combine_kernel, columns),
+        functools.partial(combine_kernel, [start for _, start in back_parts]),
         "combine",
         [shape(rows, width), shape(*gate_part.shape, F32)],
-        [weight_map, *[back_parts[dz] for dz in reversed(range(columns))], *gate_parts],
+        [weight_map, *[part for part, _ in back_parts], *gate_parts],
         combine_flops,
         [all_rows],
         limit=16,

time: 63.2 us -> 65.1 us (1.030)
  starting transfers between devices: 28.8 us -> 34.2 us
  waiting for transfers between devices: 22.4 us -> 18.3 us
  Pallas kernels: 9.26 us -> 9.93 us
    ppermute x6 -> x8, starting transfers between devices: 9.8 us -> 14.9 us  [across(): return lax.ppermute(parts[first], 'expert', pairs)]
    ppermute x6 -> x8, waiting for transfers between devices: 9.38 us -> 5.22 us  [across(): return lax.ppermute(parts[first], 'expert', pairs)]
    ppermute x3 -> x0, waiting for transfers between devices: 3.55 us -> none  [body(): gate_parts.append(lax.ppermute(gate_part, 'tensor', pairs))]
    ppermute x12 -> x13, waiting for transfers between devices: 8.13 us -> 10.5 us  [to_chip(): return lax.ppermute(value, ('dp', 'tensor'), pairs)]
    ppermute x12 -> x13, starting transfers between devices: 16.2 us -> 17.5 us  [to_chip(): return lax.ppermute(value, ('dp', 'tensor'), pairs)]
    ppermute x10 -> x11, waiting for transfers between devices: 1.37 us -> 2.55 us  [to_core(): return lax.ppermute(value, 'tensor', pairs)]
    ppermute x3 -> x0, starting transfers between devices: 1.06 us -> none  [body(): gate_parts.append(lax.ppermute(gate_part, 'tensor', pairs))]
    pallas_call x10, Pallas kernels: 9.26 us -> 9.93 us  [call(): pl.pallas_call(kernel, out_shape=out_shape, in_specs=[spec] * len(operand...]
  transfers between devices with their start and end apart: 31 -> 32, of which waited for: 14 -> 12; matrix products, arithmetic and copies ran while one was open for 0% -> 0% of each run, Pallas kernels for 12% -> 12%
where the time goes in v15:
time: 65.1 us; the launch traced here: 64.9 us
  starting transfers between devices  34.2 us (53%)
  waiting for transfers between devices  18.3 us (28%)
  Pallas kernels  9.93 us (15%)
  local copies, waits for them, and re-layouts  1.72 us (3%)
  between operations  0.74 us (1%)
    ppermute x13, starting transfers between devices, to_chip(): return lax.ppermute(value, ('dp', 'tensor'), pairs)  17.5 us
    ppermute x8, starting transfers between devices, across(): return lax.ppermute(parts[first], 'expert', pairs)  14.9 us
    ppermute x13, waiting for transfers between devices, to_chip(): return lax.ppermute(value, ('dp', 'tensor'), pairs)  10.5 us
    pallas_call x10, Pallas kernels, call(): pl.pallas_call(kernel, out_shape=out_shape, in_specs=[spec] * len(operand...  9.93 us
    ppermute x8, waiting for transfers between devices, across(): return lax.ppermute(parts[first], 'expert', pairs)  5.22 us
    ppermute x11, waiting for transfers between devices, to_core(): return lax.ppermute(value, 'tensor', pairs)  2.55 us
    ppermute x11, starting transfers between devices, to_core(): return lax.ppermute(value, 'tensor', pairs)  1.76 us
    unnamed x16, local copies, waits for them, and re-layouts  1.72 us
  transfers between devices with their start and end apart: 32, of which 12 were waited for; matrix products, arithmetic and copies ran while one was open for 0% of the time, Pallas kernels for 12%

profile of v15, /device:TPU:0, one launch (start us, length us, event | category | flops | bytes accessed | tf_op | source)
XLA Modules:
  0.0 64.9 jit_solution(17781506535818464794)
XLA Ops:
  0.6 0.5 collective-permute-start
  1.1 0.7 %copy-done.4 = s32[512,8]{0,1:T(8,128)S(1)} copy-done((s32[512,8]{0,1:T(8,128)S(1)}, s32[512,8]{0,1:T(8,128)}, u32[]{:S(2)}) %copy-start.4) | copy-done | bytes 16408
  1.9 0.1 number.1.key_ref
  2.0 0.9 %copy-done.3 = bf16[512,512]{1,0:T(8,128)(2,1)S(1)} copy-done((bf16[512,512]{1,0:T(8,128)(2,1)S(1)}, bf16[512,512]{1,0:T(8,128)(2,1)}, u32[]{:S(2)}) %copy-start.3) | copy-done | bytes 524312
  3.0 0.1 copy-done.7
  3.1 0.3 pick.2
  3.4 2.9 %collective-permute-start.2 = (bf16[48,1024]{1,0:T(8,128)(2,1)S(1)}, bf16[48,1024]{1,0:T(8,128)(2,1)S(1)}, u32[]{:S(2)}, u32[]{:S(2)}) collective-permute-start(bf16[48,1024]{1,0:T(8,128)(2,1)S(1)} %get-tuple-element.62), channel_id=1, source_target_pairs={{0,8},{4,12},{8,0},{12,4},{16,24},{20,28},{24,16},{28,20},{1,9},{5... | collective-permute-start | bytes 294920 | tf_op jit(solution)/shard_map/ppermute | solution.py:253
  6.3 1.5 %collective-permute-start.4 = (bf16[48,1024]{1,0:T(8,128)(2,1)S(1)}, bf16[48,1024]{1,0:T(8,128)(2,1)S(1)}, u32[]{:S(2)}, u32[]{:S(2)}) collective-permute-start(bf16[48,1024]{1,0:T(8,128)(2,1)S(1)} %get-tuple-element.62), channel_id=1, source_target_pairs={{0,24},{4,28},{8,16},{12,20},{16,8},{20,12},{24,0},{28,4},{1,25},{... | collective-permute-start | bytes 294920 | tf_op jit(solution)/shard_map/ppermute | solution.py:253
  7.8 0.1 collective-permute-start.3
  7.9 0.3 pick.3
  8.2 2.0 %collective-permute-start.5 = (bf16[48,1024]{1,0:T(8,128)(2,1)S(1)}, bf16[48,1024]{1,0:T(8,128)(2,1)S(1)}, u32[]{:S(2)}, u32[]{:S(2)}) collective-permute-start(bf16[48,1024]{1,0:T(8,128)(2,1)S(1)} %get-tuple-element.68), channel_id=1, source_target_pairs={{0,8},{4,12},{8,0},{12,4},{16,24},{20,28},{24,16},{28,20},{1,9},{5... | collective-permute-start | bytes 294920 | tf_op jit(solution)/shard_map/ppermute | solution.py:253
  10.2 1.5 %collective-permute-start.6 = (bf16[48,1024]{1,0:T(8,128)(2,1)S(1)}, bf16[48,1024]{1,0:T(8,128)(2,1)S(1)}, u32[]{:S(2)}, u32[]{:S(2)}) collective-permute-start(bf16[48,1024]{1,0:T(8,128)(2,1)S(1)} %get-tuple-element.72.refs_0_), channel_id=1, source_target_pairs={{0,16},{4,20},{8,24},{12,28},{16,0},{20,4},{24,8},{28,12},{1,17},{... | collective-permute-start | bytes 294920 | tf_op jit(solution)/shard_map/ppermute | solution.py:253
  11.7 1.2 %collective-permute-start.7 = (bf16[48,1024]{1,0:T(8,128)(2,1)S(1)}, bf16[48,1024]{1,0:T(8,128)(2,1)S(1)}, u32[]{:S(2)}, u32[]{:S(2)}) collective-permute-start(bf16[48,1024]{1,0:T(8,128)(2,1)S(1)} %get-tuple-element.68), channel_id=1, source_target_pairs={{0,24},{4,28},{8,16},{12,20},{16,8},{20,12},{24,0},{28,4},{1,25},{... | collective-permute-start | bytes 294920 | tf_op jit(solution)/shard_map/ppermute | solution.py:253
  12.9 2.8 %collective-permute-done.3.refs_2_ = bf16[48,1024]{1,0:T(8,128)(2,1)S(1)} collective-permute-done((bf16[48,1024]{1,0:T(8,128)(2,1)S(1)}, bf16[48,1024]{1,0:T(8,128)(2,1)S(1)}, u32[]{:S(2)}, u32[]{:S(2)}) %collective-permute-start.3) | collective-permute-done | bytes 98336 | tf_op jit(solution)/shard_map/ppermute | solution.py:253
  15.7 2.6 %forward.1 = (f32[96,768]{1,0:T(8,128)S(1)}, f32[96,768]{1,0:T(8,128)S(1)}, bf16[48,1024]{1,0:T(8,128)(2,1)S(1)}, bf16[48,1024]{1,0:T(8,128)(2,1)S(1)}, bf16[48,...) custom-call(bf16[48,1024]{1,0:T(8,128)(2,1)S(1)} %get-tuple-element.61.refs_0_, ...), custom_call_target="tpu_custom_call" | custom-call | flops 905969664 | bytes 10813440 | tf_op jit(solution)/shard_map/forward/pallas_call | solution.py:23
  18.3 0.5 collective-permute-start.9
  18.8 1.6 %collective-permute-start.8 = (bf16[48,1024]{1,0:T(8,128)(2,1)S(1)}, bf16[48,1024]{1,0:T(8,128)(2,1)S(1)}, u32[]{:S(2)}, u32[]{:S(2)}) collective-permute-start(bf16[48,1024]{1,0:T(8,128)(2,1)S(1)} %get-tuple-element.70), channel_id=1, source_target_pairs={{0,8},{4,12},{8,0},{12,4},{16,24},{20,28},{24,16},{28,20},{1,9},{5... | collective-permute-start | bytes 294920 | tf_op jit(solution)/shard_map/ppermute | solution.py:253
  20.3 1.5 %collective-permute-start.10 = (bf16[48,1024]{1,0:T(8,128)(2,1)S(1)}, bf16[48,1024]{1,0:T(8,128)(2,1)S(1)}, u32[]{:S(2)}, u32[]{:S(2)}) collective-permute-start(bf16[48,1024]{1,0:T(8,128)(2,1)S(1)} %get-tuple-element.83), channel_id=1, source_target_pairs={{0,24},{4,28},{8,16},{12,20},{16,8},{20,12},{24,0},{28,4},{1,25},{... | collective-permute-start | bytes 294920 | tf_op jit(solution)/shard_map/ppermute | solution.py:253
  21.8 2.4 %backward.1 = (bf16[48,1024]{1,0:T(8,128)(2,1)S(1)}, bf16[48,1024]{1,0:T(8,128)(2,1)S(1)}, bf16[48,1024]{1,0:T(8,128)(2,1)S(1)}, bf16[48,1024]{1,0:T(8,128)(2,1)S(1)}) custom-call(bf16[48,1024]{1,0:T(8,128)(2,1)S(1)} %get-tuple-element.72.refs_0_, bf16[48,1024]{1,0:T(8,128)(2,1)S(1)} %collective-permute-done.5.refs_1_, ...), custom_call_target="tpu_custom_call" | custom-call | flops 905969664 | bytes 10813440 | tf_op jit(solution)/shard_map/backward/pallas_call | solution.py:23
  24.3 0.6 collective-permute-start.13
  24.9 0.1 collective-permute-start.12
  25.0 0.9 %collective-permute-done.10.refs_3_ = bf16[48,1024]{1,0:T(8,128)(2,1)S(1)} collective-permute-done((bf16[48,1024]{1,0:T(8,128)(2,1)S(1)}, bf16[48,1024]{1,0:T(8,128)(2,1)S(1)}, u32[]{:S(2)}, u32[]{:S(2)}) %collective-permute-start.10) | collective-permute-done | bytes 98336 | tf_op jit(solution)/shard_map/ppermute | solution.py:253
  25.9 0.3 collective-permute-done.12.refs_5_
  26.2 1.0 %collective-permute-done.14.refs_7_ = bf16[48,1024]{1,0:T(8,128)(2,1)S(1)} collective-permute-done((bf16[48,1024]{1,0:T(8,128)(2,1)S(1)}, bf16[48,1024]{1,0:T(8,128)(2,1)S(1)}, u32[]{:S(2)}, u32[]{:S(2)}) %collective-permute-start.14) | collective-permute-done | bytes 98336 | tf_op jit(solution)/shard_map/ppermute | solution.py:243
  27.2 0.7 %add_blocks.2 = (bf16[192,512]{1,0:T(8,128)(2,1)S(1)}, bf16[96,512]{1,0:T(8,128)(2,1)}, bf16[96,512]{1,0:T(8,128)(2,1)}) custom-call(bf16[48,1024]{1,0:T(8,128)(2,1)S(1)} %get-tuple-element.69.refs_0_, bf16[48,1024]{1,0:T(8,128)(2,1)S(1)} %collective-permute-done.8.refs_1_, bf16[48,1024]{1,0:T(8,128)(2,1)S(1)} %collective-permute-done.9.refs_2_, ...), custom_call_target="tpu_custom_call" | custom-call | flops 196608 | bytes 1179648 | tf_op jit(solution)/shard_map/add_blocks/pallas_call | solution.py:23
  27.9 2.6 %collective-permute-start.19 = (bf16[192,512]{1,0:T(8,128)(2,1)S(1)}, bf16[192,512]{1,0:T(8,128)(2,1)S(1)}, u32[]{:S(2)}, u32[]{:S(2)}) collective-permute-start(bf16[192,512]{1,0:T(8,128)(2,1)S(1)} %get-tuple-element.99.refs_0_), channel_id=1, source_target_pairs={{2,0},{3,1},{0,2},{1,3},{6,4},{7,5},{4,6},{5,7},{10,8},{11,9},{8,1... | collective-permute-start | bytes 589832 | tf_op jit(solution)/shard_map/ppermute | solution.py:281
  30.4 1.6 %collective-permute-start.18 = (bf16[192,512]{1,0:T(8,128)(2,1)S(1)}, bf16[192,512]{1,0:T(8,128)(2,1)S(1)}, u32[]{:S(2)}, u32[]{:S(2)}) collective-permute-start(bf16[192,512]{1,0:T(8,128)(2,1)S(1)} %get-tuple-element.99.refs_0_), channel_id=1, source_target_pairs={{1,0},{0,1},{3,2},{2,3},{5,4},{4,5},{7,6},{6,7},{9,8},{8,9},{11,10... | collective-permute-start | bytes 589832 | tf_op jit(solution)/shard_map/ppermute | solution.py:281
  32.0 1.3 %collective-permute-start.15 = (bf16[48,1024]{1,0:T(8,128)(2,1)S(1)}, bf16[48,1024]{1,0:T(8,128)(2,1)S(1)}, u32[]{:S(2)}, u32[]{:S(2)}) collective-permute-start(bf16[48,1024]{1,0:T(8,128)(2,1)S(1)} %get-tuple-element.90), channel_id=1, source_target_pairs={{0,8},{4,12},{8,0},{12,4},{16,24},{20,28},{24,16},{28,20},{1,9},{5... | collective-permute-start | bytes 294920 | tf_op jit(solution)/shard_map/ppermute | solution.py:253
  33.3 0.7 %collective-permute-start.16 = (bf16[48,1024]{1,0:T(8,128)(2,1)S(1)}, bf16[48,1024]{1,0:T(8,128)(2,1)S(1)}, u32[]{:S(2)}, u32[]{:S(2)}) collective-permute-start(bf16[48,1024]{1,0:T(8,128)(2,1)S(1)} %get-tuple-element.91), channel_id=1, source_target_pairs={{0,16},{4,20},{8,24},{12,28},{16,0},{20,4},{24,8},{28,12},{1,17},{... | collective-permute-start | bytes 294920 | tf_op jit(solution)/shard_map/ppermute | solution.py:253
  34.1 1.4 %collective-permute-start.17 = (bf16[48,1024]{1,0:T(8,128)(2,1)S(1)}, bf16[48,1024]{1,0:T(8,128)(2,1)S(1)}, u32[]{:S(2)}, u32[]{:S(2)}) collective-permute-start(bf16[48,1024]{1,0:T(8,128)(2,1)S(1)} %get-tuple-element.92), channel_id=1, source_target_pairs={{0,24},{4,28},{8,16},{12,20},{16,8},{20,12},{24,0},{28,4},{1,25},{... | collective-permute-start | bytes 294920 | tf_op jit(solution)/shard_map/ppermute | solution.py:253
  35.5 1.4 %collective-permute-done.15.refs_1_ = bf16[48,1024]{1,0:T(8,128)(2,1)S(1)} collective-permute-done((bf16[48,1024]{1,0:T(8,128)(2,1)S(1)}, bf16[48,1024]{1,0:T(8,128)(2,1)S(1)}, u32[]{:S(2)}, u32[]{:S(2)}) %collective-permute-start.15) | collective-permute-done | bytes 98336 | tf_op jit(solution)/shard_map/ppermute | solution.py:253
  36.9 3.0 %collective-permute-done.16.refs_2_ = bf16[48,1024]{1,0:T(8,128)(2,1)S(1)} collective-permute-done((bf16[48,1024]{1,0:T(8,128)(2,1)S(1)}, bf16[48,1024]{1,0:T(8,128)(2,1)S(1)}, u32[]{:S(2)}, u32[]{:S(2)}) %collective-permute-start.16) | collective-permute-done | bytes 98336 | tf_op jit(solution)/shard_map/ppermute | solution.py:253
  39.9 0.1 collective-permute-done.19.refs_2_
  40.0 0.4 collective-permute-start.22
  40.4 0.1 collective-permute-start.23
  40.6 1.1 %collective-permute-start.24 = (bf16[192,512]{1,0:T(8,128)(2,1)S(1)}, bf16[192,512]{1,0:T(8,128)(2,1)S(1)}, u32[]{:S(2)}, u32[]{:S(2)}) collective-permute-start(bf16[192,512]{1,0:T(8,128)(2,1)S(1)} %collective-permute-done.19.refs_2_), channel_id=1, source_target_pairs={{1,0},{0,1},{3,2},{2,3},{5,4},{4,5},{7,6},{6,7},{9,8},{8,9},{11,10... | collective-permute-start | bytes 589832 | tf_op jit(solution)/shard_map/ppermute | solution.py:281
  41.8 1.3 %collective-permute-start.28 = (bf16[192,512]{1,0:T(8,128)(2,1)S(1)}, bf16[192,512]{1,0:T(8,128)(2,1)S(1)}, u32[]{:S(2)}, u32[]{:S(2)}) collective-permute-start(bf16[192,512]{1,0:T(8,128)(2,1)S(1)} %get-tuple-element.95.refs_4_), channel_id=1, source_target_pairs={{1,0},{0,1},{3,2},{2,3},{5,4},{4,5},{7,6},{6,7},{9,8},{8,9},{11,10... | collective-permute-start | bytes 589832 | tf_op jit(solution)/shard_map/ppermute | solution.py:281
  43.1 2.5 %collective-permute-start.25 = (bf16[96,512]{1,0:T(8,128)(2,1)S(1)}, bf16[96,512]{1,0:T(8,128)(2,1)S(1)}, u32[]{:S(2)}, u32[]{:S(2)}) collective-permute-start(bf16[96,512]{1,0:T(8,128)(2,1)S(1)} %get-tuple-element.104), channel_id=1, source_target_pairs={{2,0},{3,1},{0,2},{1,3},{6,4},{7,5},{4,6},{5,7},{10,8},{11,9},{8,1... | collective-permute-start | bytes 294920 | tf_op jit(solution)/shard_map/ppermute | solution.py:281
  45.6 0.7 %collective-permute-start.26 = (bf16[96,512]{1,0:T(8,128)(2,1)S(1)}, bf16[96,512]{1,0:T(8,128)(2,1)S(1)}, u32[]{:S(2)}, u32[]{:S(2)}) collective-permute-start(bf16[96,512]{1,0:T(8,128)(2,1)S(1)} %get-tuple-element.105), channel_id=1, source_target_pairs={{3,0},{2,1},{1,2},{0,3},{7,4},{6,5},{5,6},{4,7},{11,8},{10,9},{9,1... | collective-permute-start | bytes 294920 | tf_op jit(solution)/shard_map/ppermute | solution.py:281
  46.3 1.9 %collective-permute-start.27 = (bf16[96,512]{1,0:T(8,128)(2,1)S(1)}, bf16[96,512]{1,0:T(8,128)(2,1)S(1)}, u32[]{:S(2)}, u32[]{:S(2)}) collective-permute-start(bf16[96,512]{1,0:T(8,128)(2,1)S(1)} %get-tuple-element.105), channel_id=1, source_target_pairs={{2,0},{3,1},{0,2},{1,3},{6,4},{7,5},{4,6},{5,7},{10,8},{11,9},{8,1... | collective-permute-start | bytes 294920 | tf_op jit(solution)/shard_map/ppermute | solution.py:281
  48.2 5.1 %collective-permute-done.25.refs_0_ = bf16[96,512]{1,0:T(8,128)(2,1)S(1)} collective-permute-done((bf16[96,512]{1,0:T(8,128)(2,1)S(1)}, bf16[96,512]{1,0:T(8,128)(2,1)S(1)}, u32[]{:S(2)}, u32[]{:S(2)}) %collective-permute-start.25) | collective-permute-done | bytes 98336 | tf_op jit(solution)/shard_map/ppermute | solution.py:281
  53.2 3.3 %collective-permute-start.29 = (bf16[96,512]{1,0:T(8,128)(2,1)S(1)}, bf16[96,512]{1,0:T(8,128)(2,1)S(1)}, u32[]{:S(2)}, u32[]{:S(2)}) collective-permute-start(bf16[96,512]{1,0:T(8,128)(2,1)S(1)} %collective-permute-done.25.refs_0_), channel_id=1, source_target_pairs={{1,0},{0,1},{3,2},{2,3},{5,4},{4,5},{7,6},{6,7},{9,8},{8,9},{11,10... | collective-permute-start | bytes 294920 | tf_op jit(solution)/shard_map/ppermute | solution.py:281
  56.5 0.3 weights.1.weight_ref
  56.8 1.7 %combine_gate.1 = (bf16[512,512]{1,0:T(8,128)(2,1)}, f32[8,512]{1,0:T(8,128)S(1)}) custom-call(bf16[512,768]{1,0:T(8,128)(2,1)S(1)} %weights.1.weight_ref, s32[8,512]{1,0:T(8,128)S(1)} %bitcast.5, f32[16,512]{1,0:T(8,128)S(1)} %number.1.key_ref, bf16[512,512]{1,0:T(8,128)(2,1)S(1)} %copy-done.3, bf16[192,512]{1,0:T(8,128)(2,1)S(1)} %get-tuple-element.99.refs_0_, ...), custom_call_target="tpu_custom_call" | custom-call | bytes 2686976 | tf_op jit(solution)/shard_map/combine_gate/pallas_call | solution.py:23
  58.6 1.2 %collective-permute-done.30 = f32[8,512]{1,0:T(8,128)S(1)} collective-permute-done((f32[8,512]{1,0:T(8,128)S(1)}, f32[8,512]{1,0:T(8,128)S(1)}, u32[]{:S(2)}, u32[]{:S(2)}) %collective-permute-start.30) | collective-permute-done | bytes 16416 | tf_op jit(solution)/shard_map/ppermute | solution.py:243
  59.8 1.3 %collective-permute-start.31 = (f32[8,512]{1,0:T(8,128)S(1)}, f32[8,512]{1,0:T(8,128)S(1)}, u32[]{:S(2)}, u32[]{:S(2)}) collective-permute-start(f32[8,512]{1,0:T(8,128)S(1)} %add.3.refs_6_), channel_id=1, source_target_pairs={{0,8},{4,12},{8,0},{12,4},{16,24},{20,28},{24,16},{28,20},{1,9},{5... | collective-permute-start | bytes 49160 | tf_op jit(solution)/shard_map/ppermute | solution.py:253
  61.1 2.4 %collective-permute-done.31.refs_7_ = f32[8,512]{1,0:T(8,128)S(1)} collective-permute-done((f32[8,512]{1,0:T(8,128)S(1)}, f32[8,512]{1,0:T(8,128)S(1)}, u32[]{:S(2)}, u32[]{:S(2)}) %collective-permute-start.31) | collective-permute-done | bytes 16416 | tf_op jit(solution)/shard_map/ppermute | solution.py:253
  63.5 1.4 %combine.1 = (bf16[512,512]{1,0:T(8,128)(2,1)}, f32[8,512]{1,0:T(8,128)}) custom-call(bf16[512,768]{1,0:T(8,128)(2,1)S(1)} %weights.1.weight_ref, bf16[96,512]{1,0:T(8,128)(2,1)S(1)} %collective-permute-done.25.refs_0_, bf16[96,512]{1,0:T(8,128)(2,1)S(1)} %collective-permute-done.26.refs_1_, bf16[96,512]{1,0:T(8,128)(2,1)S(1)} %collective-permute-done.27.refs_2_, ...), custom_call_target="tpu_custom_call" | custom-call | flops 402653184 | bytes 2146304 | tf_op jit(solution)/shard_map/combine/pallas_call | solution.py:23
  (43 shorter events, 0.3 us)
Async XLA Ops:
  0.6 2.3 %collective-permute-start = (bf16[512,512]{1,0:T(8,128)(2,1)}, bf16[512,512]{1,0:T(8,128)(2,1)S(1)}, u32[]{:S(2)}, u32[]{:S(2)}) collective-permute-start(bf16[512,512]{1,0:T(8,128)(2,1)} %refs_0_.1), channel_id=1, source_target_pairs={{0,4},{4,0},{8,12},{12,8},{1,5},{5,1},{9,13},{13,9},{2,6},{6,2},{1... | collective-permute-start | bytes 1572872 | tf_op jit(solution)/shard_map/ppermute | solution.py:243
  1.1 0.7 %copy-start.4 = (s32[512,8]{0,1:T(8,128)S(1)}, s32[512,8]{0,1:T(8,128)}, u32[]{:S(2)}) copy-start(s32[512,8]{0,1:T(8,128)} %param.9) | copy-start | bytes 49156
  1.9 1.0 %copy-start.3 = (bf16[512,512]{1,0:T(8,128)(2,1)S(1)}, bf16[512,512]{1,0:T(8,128)(2,1)}, u32[]{:S(2)}) copy-start(bf16[512,512]{1,0:T(8,128)(2,1)} %grads_ref.1) | copy-start | bytes 1572868
  1.9 1.2 %copy-start.7 = (bf16[512,512]{1,0:T(8,128)(2,1)S(1)}, bf16[512,512]{1,0:T(8,128)(2,1)}, u32[]{:S(2)}) copy-start(bf16[512,512]{1,0:T(8,128)(2,1)} %refs_0_.1) | copy-start | bytes 1572868
  2.9 5.0 %collective-permute-start.1 = (bf16[512,512]{1,0:T(8,128)(2,1)S(1)}, bf16[512,512]{1,0:T(8,128)(2,1)S(1)}, u32[]{:S(2)}, u32[]{:S(2)}) collective-permute-start(bf16[512,512]{1,0:T(8,128)(2,1)S(1)} %copy-done.3), channel_id=1, source_target_pairs={{0,4},{4,0},{8,12},{12,8},{1,5},{5,1},{9,13},{13,9},{2,6},{6,2},{1... | collective-permute-start | bytes 1572872 | tf_op jit(solution)/shard_map/ppermute | solution.py:243
  3.4 8.3 %collective-permute-start.2 = (bf16[48,1024]{1,0:T(8,128)(2,1)S(1)}, bf16[48,1024]{1,0:T(8,128)(2,1)S(1)}, u32[]{:S(2)}, u32[]{:S(2)}) collective-permute-start(bf16[48,1024]{1,0:T(8,128)(2,1)S(1)} %get-tuple-element.62), channel_id=1, source_target_pairs={{0,8},{4,12},{8,0},{12,4},{16,24},{20,28},{24,16},{28,20},{1,9},{5... | collective-permute-start | bytes 294920 | tf_op jit(solution)/shard_map/ppermute | solution.py:253
  6.3 9.4 %collective-permute-start.4 = (bf16[48,1024]{1,0:T(8,128)(2,1)S(1)}, bf16[48,1024]{1,0:T(8,128)(2,1)S(1)}, u32[]{:S(2)}, u32[]{:S(2)}) collective-permute-start(bf16[48,1024]{1,0:T(8,128)(2,1)S(1)} %get-tuple-element.62), channel_id=1, source_target_pairs={{0,24},{4,28},{8,16},{12,20},{16,8},{20,12},{24,0},{28,4},{1,25},{... | collective-permute-start | bytes 294920 | tf_op jit(solution)/shard_map/ppermute | solution.py:253
  7.8 7.9 %copy-start = (bf16[1,768,2048]{2,1,0:T(8,128)(2,1)S(1)}, bf16[1,768,2048]{2,1,0:T(8,128)(2,1)}, u32[]{:S(2)}) copy-start(bf16[1,768,2048]{2,1,0:T(8,128)(2,1)} %refs_4_.3) | copy-start | bytes 9437188
  7.8 7.9 %copy-start.1 = (bf16[1,768,2048]{2,1,0:T(8,128)(2,1)S(1)}, bf16[1,768,2048]{2,1,0:T(8,128)(2,1)}, u32[]{:S(2)}) copy-start(bf16[1,768,2048]{2,1,0:T(8,128)(2,1)} %refs_5_.3) | copy-start | bytes 9437188
  7.8 7.9 %copy-start.2 = (bf16[1,768,2048]{2,1,0:T(8,128)(2,1)S(1)}, bf16[1,768,2048]{2,1,0:T(8,128)(2,1)}, u32[]{:S(2)}) copy-start(bf16[1,768,2048]{2,1,0:T(8,128)(2,1)} %refs_6_.3) | copy-start | bytes 9437188
  7.8 7.9 %collective-permute-start.3 = (bf16[48,1024]{1,0:T(8,128)(2,1)S(1)}, bf16[48,1024]{1,0:T(8,128)(2,1)S(1)}, u32[]{:S(2)}, u32[]{:S(2)}) collective-permute-start(bf16[48,1024]{1,0:T(8,128)(2,1)S(1)} %get-tuple-element.61.refs_0_), channel_id=1, source_target_pairs={{0,16},{4,20},{8,24},{12,28},{16,0},{20,4},{24,8},{28,12},{1,17},{... | collective-permute-start | bytes 294920 | tf_op jit(solution)/shard_map/ppermute | solution.py:253
  8.2 10.1 %collective-permute-start.5 = (bf16[48,1024]{1,0:T(8,128)(2,1)S(1)}, bf16[48,1024]{1,0:T(8,128)(2,1)S(1)}, u32[]{:S(2)}, u32[]{:S(2)}) collective-permute-start(bf16[48,1024]{1,0:T(8,128)(2,1)S(1)} %get-tuple-element.68), channel_id=1, source_target_pairs={{0,8},{4,12},{8,0},{12,4},{16,24},{20,28},{24,16},{28,20},{1,9},{5... | collective-permute-start | bytes 294920 | tf_op jit(solution)/shard_map/ppermute | solution.py:253
  10.2 8.2 %collective-permute-start.6 = (bf16[48,1024]{1,0:T(8,128)(2,1)S(1)}, bf16[48,1024]{1,0:T(8,128)(2,1)S(1)}, u32[]{:S(2)}, u32[]{:S(2)}) collective-permute-start(bf16[48,1024]{1,0:T(8,128)(2,1)S(1)} %get-tuple-element.72.refs_0_), channel_id=1, source_target_pairs={{0,16},{4,20},{8,24},{12,28},{16,0},{20,4},{24,8},{28,12},{1,17},{... | collective-permute-start | bytes 294920 | tf_op jit(solution)/shard_map/ppermute | solution.py:253
  11.7 6.6 %collective-permute-start.7 = (bf16[48,1024]{1,0:T(8,128)(2,1)S(1)}, bf16[48,1024]{1,0:T(8,128)(2,1)S(1)}, u32[]{:S(2)}, u32[]{:S(2)}) collective-permute-start(bf16[48,1024]{1,0:T(8,128)(2,1)S(1)} %get-tuple-element.68), channel_id=1, source_target_pairs={{0,24},{4,28},{8,16},{12,20},{16,8},{20,12},{24,0},{28,4},{1,25},{... | collective-permute-start | bytes 294920 | tf_op jit(solution)/shard_map/ppermute | solution.py:253
  18.3 6.0 %collective-permute-start.9 = (bf16[48,1024]{1,0:T(8,128)(2,1)S(1)}, bf16[48,1024]{1,0:T(8,128)(2,1)S(1)}, u32[]{:S(2)}, u32[]{:S(2)}) collective-permute-start(bf16[48,1024]{1,0:T(8,128)(2,1)S(1)} %get-tuple-element.71), channel_id=1, source_target_pairs={{0,16},{4,20},{8,24},{12,28},{16,0},{20,4},{24,8},{28,12},{1,17},{... | collective-permute-start | bytes 294920 | tf_op jit(solution)/shard_map/ppermute | solution.py:253
  18.8 6.1 %collective-permute-start.8 = (bf16[48,1024]{1,0:T(8,128)(2,1)S(1)}, bf16[48,1024]{1,0:T(8,128)(2,1)S(1)}, u32[]{:S(2)}, u32[]{:S(2)}) collective-permute-start(bf16[48,1024]{1,0:T(8,128)(2,1)S(1)} %get-tuple-element.70), channel_id=1, source_target_pairs={{0,8},{4,12},{8,0},{12,4},{16,24},{20,28},{24,16},{28,20},{1,9},{5... | collective-permute-start | bytes 294920 | tf_op jit(solution)/shard_map/ppermute | solution.py:253
  20.3 5.5 %collective-permute-start.10 = (bf16[48,1024]{1,0:T(8,128)(2,1)S(1)}, bf16[48,1024]{1,0:T(8,128)(2,1)S(1)}, u32[]{:S(2)}, u32[]{:S(2)}) collective-permute-start(bf16[48,1024]{1,0:T(8,128)(2,1)S(1)} %get-tuple-element.83), channel_id=1, source_target_pairs={{0,24},{4,28},{8,16},{12,20},{16,8},{20,12},{24,0},{28,4},{1,25},{... | collective-permute-start | bytes 294920 | tf_op jit(solution)/shard_map/ppermute | solution.py:253
  21.8 4.0 %collective-permute-start.11 = (bf16[48,1024]{1,0:T(8,128)(2,1)S(1)}, bf16[48,1024]{1,0:T(8,128)(2,1)S(1)}, u32[]{:S(2)}, u32[]{:S(2)}) collective-permute-start(bf16[48,1024]{1,0:T(8,128)(2,1)S(1)} %get-tuple-element.69.refs_0_), channel_id=1, source_target_pairs={{0,4},{4,0},{8,12},{12,8},{1,5},{5,1},{9,13},{13,9},{2,6},{6,2},{1... | collective-permute-start | bytes 294920 | tf_op jit(solution)/shard_map/ppermute | solution.py:243
  21.8 34.7 %copy-start.5 = (s32[512,8]{0,1:T(8,128)S(1)}, s32[512,8]{0,1:T(8,128)}, u32[]{:S(2)}) copy-start(s32[512,8]{0,1:T(8,128)} %param.9) | copy-start | bytes 49156
  21.8 34.7 %copy-start.6 = (f32[512,8]{0,1:T(8,128)S(1)}, f32[512,8]{0,1:T(8,128)}, u32[]{:S(2)}) copy-start(f32[512,8]{0,1:T(8,128)} %param.10) | copy-start | bytes 49156
  24.3 1.9 %collective-permute-start.13 = (bf16[48,1024]{1,0:T(8,128)(2,1)S(1)}, bf16[48,1024]{1,0:T(8,128)(2,1)S(1)}, u32[]{:S(2)}, u32[]{:S(2)}) collective-permute-start(bf16[48,1024]{1,0:T(8,128)(2,1)S(1)} %collective-permute-done.9.refs_2_), channel_id=1, source_target_pairs={{0,4},{4,0},{8,12},{12,8},{1,5},{5,1},{9,13},{13,9},{2,6},{6,2},{1... | collective-permute-start | bytes 294920 | tf_op jit(solution)/shard_map/ppermute | solution.py:243
  24.9 1.3 %collective-permute-start.12 = (bf16[48,1024]{1,0:T(8,128)(2,1)S(1)}, bf16[48,1024]{1,0:T(8,128)(2,1)S(1)}, u32[]{:S(2)}, u32[]{:S(2)}) collective-permute-start(bf16[48,1024]{1,0:T(8,128)(2,1)S(1)} %collective-permute-done.8.refs_1_), channel_id=1, source_target_pairs={{0,4},{4,0},{8,12},{12,8},{1,5},{5,1},{9,13},{13,9},{2,6},{6,2},{1... | collective-permute-start | bytes 294920 | tf_op jit(solution)/shard_map/ppermute | solution.py:243
  25.9 1.3 %collective-permute-start.14 = (bf16[48,1024]{1,0:T(8,128)(2,1)S(1)}, bf16[48,1024]{1,0:T(8,128)(2,1)S(1)}, u32[]{:S(2)}, u32[]{:S(2)}) collective-permute-start(bf16[48,1024]{1,0:T(8,128)(2,1)S(1)} %collective-permute-done.10.refs_3_), channel_id=1, source_target_pairs={{0,4},{4,0},{8,12},{12,8},{1,5},{5,1},{9,13},{13,9},{2,6},{6,2},{1... | collective-permute-start | bytes 294920 | tf_op jit(solution)/shard_map/ppermute | solution.py:243
  27.9 12.2 %collective-permute-start.19 = (bf16[192,512]{1,0:T(8,128)(2,1)S(1)}, bf16[192,512]{1,0:T(8,128)(2,1)S(1)}, u32[]{:S(2)}, u32[]{:S(2)}) collective-permute-start(bf16[192,512]{1,0:T(8,128)(2,1)S(1)} %get-tuple-element.99.refs_0_), channel_id=1, source_target_pairs={{2,0},{3,1},{0,2},{1,3},{6,4},{7,5},{4,6},{5,7},{10,8},{11,9},{8,1... | collective-permute-start | bytes 589832 | tf_op jit(solution)/shard_map/ppermute | solution.py:281
  30.4 10.0 %collective-permute-start.18 = (bf16[192,512]{1,0:T(8,128)(2,1)S(1)}, bf16[192,512]{1,0:T(8,128)(2,1)S(1)}, u32[]{:S(2)}, u32[]{:S(2)}) collective-permute-start(bf16[192,512]{1,0:T(8,128)(2,1)S(1)} %get-tuple-element.99.refs_0_), channel_id=1, source_target_pairs={{1,0},{0,1},{3,2},{2,3},{5,4},{4,5},{7,6},{6,7},{9,8},{8,9},{11,10... | collective-permute-start | bytes 589832 | tf_op jit(solution)/shard_map/ppermute | solution.py:281
  32.0 4.8 %collective-permute-start.15 = (bf16[48,1024]{1,0:T(8,128)(2,1)S(1)}, bf16[48,1024]{1,0:T(8,128)(2,1)S(1)}, u32[]{:S(2)}, u32[]{:S(2)}) collective-permute-start(bf16[48,1024]{1,0:T(8,128)(2,1)S(1)} %get-tuple-element.90), channel_id=1, source_target_pairs={{0,8},{4,12},{8,0},{12,4},{16,24},{20,28},{24,16},{28,20},{1,9},{5... | collective-permute-start | bytes 294920 | tf_op jit(solution)/shard_map/ppermute | solution.py:253
  33.3 6.6 %collective-permute-start.16 = (bf16[48,1024]{1,0:T(8,128)(2,1)S(1)}, bf16[48,1024]{1,0:T(8,128)(2,1)S(1)}, u32[]{:S(2)}, u32[]{:S(2)}) collective-permute-start(bf16[48,1024]{1,0:T(8,128)(2,1)S(1)} %get-tuple-element.91), channel_id=1, source_target_pairs={{0,16},{4,20},{8,24},{12,28},{16,0},{20,4},{24,8},{28,12},{1,17},{... | collective-permute-start | bytes 294920 | tf_op jit(solution)/shard_map/ppermute | solution.py:253
  34.1 6.4 %collective-permute-start.17 = (bf16[48,1024]{1,0:T(8,128)(2,1)S(1)}, bf16[48,1024]{1,0:T(8,128)(2,1)S(1)}, u32[]{:S(2)}, u32[]{:S(2)}) collective-permute-start(bf16[48,1024]{1,0:T(8,128)(2,1)S(1)} %get-tuple-element.92), channel_id=1, source_target_pairs={{0,24},{4,28},{8,16},{12,20},{16,8},{20,12},{24,0},{28,4},{1,25},{... | collective-permute-start | bytes 294920 | tf_op jit(solution)/shard_map/ppermute | solution.py:253
  36.9 4.8 %collective-permute-start.20 = (bf16[48,1024]{1,0:T(8,128)(2,1)S(1)}, bf16[48,1024]{1,0:T(8,128)(2,1)S(1)}, u32[]{:S(2)}, u32[]{:S(2)}) collective-permute-start(bf16[48,1024]{1,0:T(8,128)(2,1)S(1)} %get-tuple-element.89.refs_0_), channel_id=1, source_target_pairs={{0,4},{4,0},{8,12},{12,8},{1,5},{5,1},{9,13},{13,9},{2,6},{6,2},{1... | collective-permute-start | bytes 294920 | tf_op jit(solution)/shard_map/ppermute | solution.py:243
  39.9 1.8 %collective-permute-start.21 = (bf16[48,1024]{1,0:T(8,128)(2,1)S(1)}, bf16[48,1024]{1,0:T(8,128)(2,1)S(1)}, u32[]{:S(2)}, u32[]{:S(2)}) collective-permute-start(bf16[48,1024]{1,0:T(8,128)(2,1)S(1)} %collective-permute-done.15.refs_1_), channel_id=1, source_target_pairs={{0,4},{4,0},{8,12},{12,8},{1,5},{5,1},{9,13},{13,9},{2,6},{6,2},{1... | collective-permute-start | bytes 294920 | tf_op jit(solution)/shard_map/ppermute | solution.py:243
  40.0 1.6 %collective-permute-start.22 = (bf16[48,1024]{1,0:T(8,128)(2,1)S(1)}, bf16[48,1024]{1,0:T(8,128)(2,1)S(1)}, u32[]{:S(2)}, u32[]{:S(2)}) collective-permute-start(bf16[48,1024]{1,0:T(8,128)(2,1)S(1)} %collective-permute-done.16.refs_2_), channel_id=1, source_target_pairs={{0,4},{4,0},{8,12},{12,8},{1,5},{5,1},{9,13},{13,9},{2,6},{6,2},{1... | collective-permute-start | bytes 294920 | tf_op jit(solution)/shard_map/ppermute | solution.py:243
  40.4 1.3 %collective-permute-start.23 = (bf16[48,1024]{1,0:T(8,128)(2,1)S(1)}, bf16[48,1024]{1,0:T(8,128)(2,1)S(1)}, u32[]{:S(2)}, u32[]{:S(2)}) collective-permute-start(bf16[48,1024]{1,0:T(8,128)(2,1)S(1)} %collective-permute-done.17.refs_3_), channel_id=1, source_target_pairs={{0,4},{4,0},{8,12},{12,8},{1,5},{5,1},{9,13},{13,9},{2,6},{6,2},{1... | collective-permute-start | bytes 294920 | tf_op jit(solution)/shard_map/ppermute | solution.py:243
  40.6 16.3 %collective-permute-start.24 = (bf16[192,512]{1,0:T(8,128)(2,1)S(1)}, bf16[192,512]{1,0:T(8,128)(2,1)S(1)}, u32[]{:S(2)}, u32[]{:S(2)}) collective-permute-start(bf16[192,512]{1,0:T(8,128)(2,1)S(1)} %collective-permute-done.19.refs_2_), channel_id=1, source_target_pairs={{1,0},{0,1},{3,2},{2,3},{5,4},{4,5},{7,6},{6,7},{9,8},{8,9},{11,10... | collective-permute-start | bytes 589832 | tf_op jit(solution)/shard_map/ppermute | solution.py:281
  41.8 21.7 %collective-permute-start.28 = (bf16[192,512]{1,0:T(8,128)(2,1)S(1)}, bf16[192,512]{1,0:T(8,128)(2,1)S(1)}, u32[]{:S(2)}, u32[]{:S(2)}) collective-permute-start(bf16[192,512]{1,0:T(8,128)(2,1)S(1)} %get-tuple-element.95.refs_4_), channel_id=1, source_target_pairs={{1,0},{0,1},{3,2},{2,3},{5,4},{4,5},{7,6},{6,7},{9,8},{8,9},{11,10... | collective-permute-start | bytes 589832 | tf_op jit(solution)/shard_map/ppermute | solution.py:281
  43.1 10.2 %collective-permute-start.25 = (bf16[96,512]{1,0:T(8,128)(2,1)S(1)}, bf16[96,512]{1,0:T(8,128)(2,1)S(1)}, u32[]{:S(2)}, u32[]{:S(2)}) collective-permute-start(bf16[96,512]{1,0:T(8,128)(2,1)S(1)} %get-tuple-element.104), channel_id=1, source_target_pairs={{2,0},{3,1},{0,2},{1,3},{6,4},{7,5},{4,6},{5,7},{10,8},{11,9},{8,1... | collective-permute-start | bytes 294920 | tf_op jit(solution)/shard_map/ppermute | solution.py:281
  45.6 15.5 %collective-permute-start.26 = (bf16[96,512]{1,0:T(8,128)(2,1)S(1)}, bf16[96,512]{1,0:T(8,128)(2,1)S(1)}, u32[]{:S(2)}, u32[]{:S(2)}) collective-permute-start(bf16[96,512]{1,0:T(8,128)(2,1)S(1)} %get-tuple-element.105), channel_id=1, source_target_pairs={{3,0},{2,1},{1,2},{0,3},{7,4},{6,5},{5,6},{4,7},{11,8},{10,9},{9,1... | collective-permute-start | bytes 294920 | tf_op jit(solution)/shard_map/ppermute | solution.py:281
  46.3 14.8 %collective-permute-start.27 = (bf16[96,512]{1,0:T(8,128)(2,1)S(1)}, bf16[96,512]{1,0:T(8,128)(2,1)S(1)}, u32[]{:S(2)}, u32[]{:S(2)}) collective-permute-start(bf16[96,512]{1,0:T(8,128)(2,1)S(1)} %get-tuple-element.105), channel_id=1, source_target_pairs={{2,0},{3,1},{0,2},{1,3},{6,4},{7,5},{4,6},{5,7},{10,8},{11,9},{8,1... | collective-permute-start | bytes 294920 | tf_op jit(solution)/shard_map/ppermute | solution.py:281
  53.2 10.3 %collective-permute-start.29 = (bf16[96,512]{1,0:T(8,128)(2,1)S(1)}, bf16[96,512]{1,0:T(8,128)(2,1)S(1)}, u32[]{:S(2)}, u32[]{:S(2)}) collective-permute-start(bf16[96,512]{1,0:T(8,128)(2,1)S(1)} %collective-permute-done.25.refs_0_), channel_id=1, source_target_pairs={{1,0},{0,1},{3,2},{2,3},{5,4},{4,5},{7,6},{6,7},{9,8},{8,9},{11,10... | collective-permute-start | bytes 294920 | tf_op jit(solution)/shard_map/ppermute | solution.py:281
  58.6 1.2 %collective-permute-start.30 = (f32[8,512]{1,0:T(8,128)S(1)}, f32[8,512]{1,0:T(8,128)S(1)}, u32[]{:S(2)}, u32[]{:S(2)}) collective-permute-start(f32[8,512]{1,0:T(8,128)S(1)} %get-tuple-element.106), channel_id=1, source_target_pairs={{0,4},{4,0},{8,12},{12,8},{1,5},{5,1},{9,13},{13,9},{2,6},{6,2},{1... | collective-permute-start | bytes 49160 | tf_op jit(solution)/shard_map/ppermute | solution.py:243
  59.8 3.7 %collective-permute-start.31 = (f32[8,512]{1,0:T(8,128)S(1)}, f32[8,512]{1,0:T(8,128)S(1)}, u32[]{:S(2)}, u32[]{:S(2)}) collective-permute-start(f32[8,512]{1,0:T(8,128)S(1)} %add.3.refs_6_), channel_id=1, source_target_pairs={{0,8},{4,12},{8,0},{12,4},{16,24},{20,28},{24,16},{28,20},{1,9},{5... | collective-permute-start | bytes 49160 | tf_op jit(solution)/shard_map/ppermute | solution.py:253

commit v16 on v13

--- a/solution.py
+++ b/solution.py
@@ -16,7 +16,7 @@
 CONTRACT_LAST = (((1,), (1,)), ((), ()))
 
 
-def call(kernel, name, out_shape, operands, flops, scratch=(), limit=8):
+def call(kernel, name, out_shape, operands, flops, scratch=(), limit=8, copied=0):
     outs = out_shape if isinstance(out_shape, list) else [out_shape]
     moved = sum(a.size * a.dtype.itemsize for a in [*operands, *outs])
     spec = pl.BlockSpec(memory_space=pltpu.VMEM)
@@ -24,7 +24,9 @@
         kernel,
         out_shape=out_shape,
         in_specs=[spec] * len(operands),
-        out_specs=[spec] * len(outs) if isinstance(out_shape, list) else spec,
+        out_specs=[pl.BlockSpec(memory_space=pl.ANY)] * copied + [spec] * (len(outs) - copied)
+        if isinstance(out_shape, list)
+        else spec,
         scratch_shapes=list(scratch),
         compiler_params=pltpu.CompilerParams(vmem_limit_bytes=limit * MIB),
         cost_estimate=pl.CostEstimate(flops=int(flops), bytes_accessed=int(moved), transcendentals=0),
@@ -192,14 +194,23 @@
 
 
 def combine_kernel(columns, weight_ref, *refs):
-    parts, gates = refs[:columns], refs[columns:-3]
-    out_ref, total_ref, all_ref = refs[-3:]
+    parts, gates = refs[:columns], refs[columns:-5]
+    out_ref, total_ref, all_ref, rows_ref, sem = refs[-5:]
     place_parts(parts, all_ref)
-    out_ref[...] = jnp.dot(weight_ref[...], all_ref[...], preferred_element_type=F32).astype(BF16)
+    height = rows_ref.shape[1]
+    copies = []
+    for index in range(rows_ref.shape[0]):
+        some = slice(index * height, (index + 1) * height)
+        rows_ref[index] = jnp.dot(weight_ref[some, :], all_ref[...], preferred_element_type=F32).astype(BF16)
+        copy = pltpu.make_async_copy(rows_ref.at[index], out_ref.at[pl.ds(index * height, height)], sem.at[index])
+        copy.start()
+        copies.append(copy)
     total = gates[0][...]
     for gate in gates[1:]:
         total = total + gate[...]
     total_ref[...] = total
+    for copy in copies:
+        copy.wait()
 
 
 def combine_gate_kernel(chips, cores, columns, weight_ref, routes_ref, key_ref, grads_ref, *refs):
@@ -291,8 +302,7 @@
 
     token_sources = [to_core(tokens, dc) for dc in range(cores)]
     key = call(number_kernel, "number", shape(experts, rows, F32), [routes_t], EARLY)
-    grads, key = after(grad_out, key)
-    grad_sources = [to_core(grads, dc) for dc in range(cores)]
+    grad_sources = [to_core(grad_out, dc) for dc in range(cores)]
     tok_in = dispatch(pick(key, token_sources))
     tok_in[0], grad_pieces = lax.optimization_barrier((tok_in[0], pick(key, grad_sources)))
     grad_in = dispatch(grad_pieces)
@@ -358,18 +368,19 @@
         [all_rows, pltpu.VMEM((experts * CAP, rows), F32)],
         limit=24,
     )
-    gate_parts = [gate_part]
-    for dt in range(1, groups):
-        pairs = [(t, (t + dt) % groups) for t in range(groups)]
-        gate_parts.append(lax.ppermute(gate_part, "tensor", pairs))
+    chip_part = gate_part
+    for dc in range(1, cores):
+        chip_part = chip_part + to_core(gate_part, dc)
+    gate_parts = [to_chip(chip_part, 0, dh) for dh in range(chips)]
     grad_tokens, grad_gates = call(
         functools.partial(combine_kernel, columns),
         "combine",
         [shape(rows, width), shape(*gate_part.shape, F32)],
         [weight_map, *[back_parts[dz] for dz in range(columns)], *gate_parts],
         combine_flops,
-        [all_rows],
+        [all_rows, pltpu.VMEM((2, rows // 2, width), BF16), pltpu.SemaphoreType.DMA((2,))],
         limit=16,
+        copied=1,
     )
     return (mixed, grad_tokens, grad_gates.T)
 

time: 62.8 us -> 63.5 us (1.011)
  waiting for transfers between devices: 21.8 us -> 23 us
  local copies, waits for them, and re-layouts: 1.72 us -> 0.83 us
    ppermute x3 -> x0, waiting for transfers between devices: 3.22 us -> none  [body(): gate_parts.append(lax.ppermute(gate_part, 'tensor', pairs))]
    ppermute x10 -> x11, waiting for transfers between devices: 1.37 us -> 3.28 us  [to_core(): return lax.ppermute(value, 'tensor', pairs)]
    ppermute x12 -> x13, waiting for transfers between devices: 8.13 us -> 9.63 us  [to_chip(): return lax.ppermute(value, ('dp', 'tensor'), pairs)]
    ppermute x3 -> x0, starting transfers between devices: 1.39 us -> none  [body(): gate_parts.append(lax.ppermute(gate_part, 'tensor', pairs))]
    ppermute x12 -> x13, starting transfers between devices: 16.2 us -> 17.5 us  [to_chip(): return lax.ppermute(value, ('dp', 'tensor'), pairs)]
    ppermute x6, waiting for transfers between devices: 9.04 us -> 10.1 us  [across(): return lax.ppermute(parts[first], 'expert', pairs)]
    unnamed x16, local copies, waits for them, and re-layouts: 1.72 us -> 0.83 us
    ppermute x10 -> x11, starting transfers between devices: 1.76 us -> 1.6 us  [to_core(): return lax.ppermute(value, 'tensor', pairs)]
  transfers between devices with their start and end apart: 31 -> 30, of which waited for: 14 -> 13; matrix products, arithmetic and copies ran while one was open for 0% -> 0% of each run, Pallas kernels for 13% -> 12%
where the time goes in v16:
time: 63.5 us; the launch traced here: 63.3 us
  starting transfers between devices  28.9 us (46%)
  waiting for transfers between devices  23 us (36%)
  Pallas kernels  9.8 us (15%)
  local copies, waits for them, and re-layouts  0.83 us (1%)
  between operations  0.76 us (1%)
    ppermute x13, starting transfers between devices, to_chip(): return lax.ppermute(value, ('dp', 'tensor'), pairs)  17.5 us
    ppermute x6, waiting for transfers between devices, across(): return lax.ppermute(parts[first], 'expert', pairs)  10.1 us
    pallas_call x10, Pallas kernels, call(): pl.pallas_call(kernel, out_shape=out_shape, in_specs=[spec] * len(operand...  9.8 us
    ppermute x6, starting transfers between devices, across(): return lax.ppermute(parts[first], 'expert', pairs)  9.8 us
    ppermute x13, waiting for transfers between devices, to_chip(): return lax.ppermute(value, ('dp', 'tensor'), pairs)  9.63 us
    ppermute x11, waiting for transfers between devices, to_core(): return lax.ppermute(value, 'tensor', pairs)  3.28 us
    ppermute x11, starting transfers between devices, to_core(): return lax.ppermute(value, 'tensor', pairs)  1.6 us
  transfers between devices with their start and end apart: 30, of which 13 were waited for; matrix products, arithmetic and copies ran while one was open for 0% of the time, Pallas kernels for 12%

profile of v16, /device:TPU:0, one launch (start us, length us, event | category | flops | bytes accessed | tf_op | source)
XLA Modules:
  0.0 63.3 jit_solution(7071734417363559420)
XLA Ops:
  0.6 0.5 collective-permute-start
  1.1 0.1 collective-permute-start.1
  1.2 0.7 %copy-done.4 = s32[512,8]{0,1:T(8,128)S(1)} copy-done((s32[512,8]{0,1:T(8,128)S(1)}, s32[512,8]{0,1:T(8,128)}, u32[]{:S(2)}) %copy-start.4) | copy-done | bytes 16408
  1.9 0.1 number.1.key_ref
  2.1 0.8 %collective-permute-done.refs_1_ = bf16[512,512]{1,0:T(8,128)(2,1)S(1)} collective-permute-done((bf16[512,512]{1,0:T(8,128)(2,1)}, bf16[512,512]{1,0:T(8,128)(2,1)S(1)}, u32[]{:S(2)}, u32[]{:S(2)}) %collective-permute-start) | collective-permute-done | bytes 524320 | tf_op jit(solution)/shard_map/ppermute | solution.py:251
  2.9 0.1 copy-done.7
  3.0 0.3 pick.2
  3.3 3.0 %collective-permute-start.2 = (bf16[48,1024]{1,0:T(8,128)(2,1)S(1)}, bf16[48,1024]{1,0:T(8,128)(2,1)S(1)}, u32[]{:S(2)}, u32[]{:S(2)}) collective-permute-start(bf16[48,1024]{1,0:T(8,128)(2,1)S(1)} %get-tuple-element.54), channel_id=1, source_target_pairs={{0,8},{4,12},{8,0},{12,4},{16,24},{20,28},{24,16},{28,20},{1,9},{5... | collective-permute-start | bytes 294920 | tf_op jit(solution)/shard_map/ppermute | solution.py:261
  6.3 1.5 %collective-permute-start.4 = (bf16[48,1024]{1,0:T(8,128)(2,1)S(1)}, bf16[48,1024]{1,0:T(8,128)(2,1)S(1)}, u32[]{:S(2)}, u32[]{:S(2)}) collective-permute-start(bf16[48,1024]{1,0:T(8,128)(2,1)S(1)} %get-tuple-element.54), channel_id=1, source_target_pairs={{0,24},{4,28},{8,16},{12,20},{16,8},{20,12},{24,0},{28,4},{1,25},{... | collective-permute-start | bytes 294920 | tf_op jit(solution)/shard_map/ppermute | solution.py:261
  7.8 0.1 collective-permute-start.3
  7.9 0.3 pick.3
  8.2 2.0 %collective-permute-start.5 = (bf16[48,1024]{1,0:T(8,128)(2,1)S(1)}, bf16[48,1024]{1,0:T(8,128)(2,1)S(1)}, u32[]{:S(2)}, u32[]{:S(2)}) collective-permute-start(bf16[48,1024]{1,0:T(8,128)(2,1)S(1)} %get-tuple-element.60), channel_id=1, source_target_pairs={{0,8},{4,12},{8,0},{12,4},{16,24},{20,28},{24,16},{28,20},{1,9},{5... | collective-permute-start | bytes 294920 | tf_op jit(solution)/shard_map/ppermute | solution.py:261
  10.1 1.5 %collective-permute-start.6 = (bf16[48,1024]{1,0:T(8,128)(2,1)S(1)}, bf16[48,1024]{1,0:T(8,128)(2,1)S(1)}, u32[]{:S(2)}, u32[]{:S(2)}) collective-permute-start(bf16[48,1024]{1,0:T(8,128)(2,1)S(1)} %get-tuple-element.64.refs_0_), channel_id=1, source_target_pairs={{0,16},{4,20},{8,24},{12,28},{16,0},{20,4},{24,8},{28,12},{1,17},{... | collective-permute-start | bytes 294920 | tf_op jit(solution)/shard_map/ppermute | solution.py:261
  11.7 1.2 %collective-permute-start.7 = (bf16[48,1024]{1,0:T(8,128)(2,1)S(1)}, bf16[48,1024]{1,0:T(8,128)(2,1)S(1)}, u32[]{:S(2)}, u32[]{:S(2)}) collective-permute-start(bf16[48,1024]{1,0:T(8,128)(2,1)S(1)} %get-tuple-element.60), channel_id=1, source_target_pairs={{0,24},{4,28},{8,16},{12,20},{16,8},{20,12},{24,0},{28,4},{1,25},{... | collective-permute-start | bytes 294920 | tf_op jit(solution)/shard_map/ppermute | solution.py:261
  12.9 2.9 %collective-permute-done.3.refs_2_ = bf16[48,1024]{1,0:T(8,128)(2,1)S(1)} collective-permute-done((bf16[48,1024]{1,0:T(8,128)(2,1)S(1)}, bf16[48,1024]{1,0:T(8,128)(2,1)S(1)}, u32[]{:S(2)}, u32[]{:S(2)}) %collective-permute-start.3) | collective-permute-done | bytes 98336 | tf_op jit(solution)/shard_map/ppermute | solution.py:261
  15.8 2.6 %forward.1 = (f32[96,768]{1,0:T(8,128)S(1)}, f32[96,768]{1,0:T(8,128)S(1)}, bf16[48,1024]{1,0:T(8,128)(2,1)S(1)}, bf16[48,1024]{1,0:T(8,128)(2,1)S(1)}, bf16[48,...) custom-call(bf16[48,1024]{1,0:T(8,128)(2,1)S(1)} %get-tuple-element.53.refs_0_, ...), custom_call_target="tpu_custom_call" | custom-call | flops 905969664 | bytes 10813440 | tf_op jit(solution)/shard_map/forward/pallas_call | solution.py:23
  18.4 0.2 collective-permute-start.9
  18.7 1.8 %collective-permute-start.8 = (bf16[48,1024]{1,0:T(8,128)(2,1)S(1)}, bf16[48,1024]{1,0:T(8,128)(2,1)S(1)}, u32[]{:S(2)}, u32[]{:S(2)}) collective-permute-start(bf16[48,1024]{1,0:T(8,128)(2,1)S(1)} %get-tuple-element.62), channel_id=1, source_target_pairs={{0,8},{4,12},{8,0},{12,4},{16,24},{20,28},{24,16},{28,20},{1,9},{5... | collective-permute-start | bytes 294920 | tf_op jit(solution)/shard_map/ppermute | solution.py:261
  20.5 1.5 %collective-permute-start.10 = (bf16[48,1024]{1,0:T(8,128)(2,1)S(1)}, bf16[48,1024]{1,0:T(8,128)(2,1)S(1)}, u32[]{:S(2)}, u32[]{:S(2)}) collective-permute-start(bf16[48,1024]{1,0:T(8,128)(2,1)S(1)} %get-tuple-element.75), channel_id=1, source_target_pairs={{0,24},{4,28},{8,16},{12,20},{16,8},{20,12},{24,0},{28,4},{1,25},{... | collective-permute-start | bytes 294920 | tf_op jit(solution)/shard_map/ppermute | solution.py:261
  22.0 2.4 %backward.1 = (bf16[48,1024]{1,0:T(8,128)(2,1)S(1)}, bf16[48,1024]{1,0:T(8,128)(2,1)S(1)}, bf16[48,1024]{1,0:T(8,128)(2,1)S(1)}, bf16[48,1024]{1,0:T(8,128)(2,1)S(1)}) custom-call(bf16[48,1024]{1,0:T(8,128)(2,1)S(1)} %get-tuple-element.64.refs_0_, bf16[48,1024]{1,0:T(8,128)(2,1)S(1)} %collective-permute-done.5.refs_1_, ...), custom_call_target="tpu_custom_call" | custom-call | flops 905969664 | bytes 10813440 | tf_op jit(solution)/shard_map/backward/pallas_call | solution.py:23
  24.5 0.6 collective-permute-start.13
  25.0 0.1 collective-permute-start.12
  25.1 0.9 %collective-permute-done.10.refs_3_ = bf16[48,1024]{1,0:T(8,128)(2,1)S(1)} collective-permute-done((bf16[48,1024]{1,0:T(8,128)(2,1)S(1)}, bf16[48,1024]{1,0:T(8,128)(2,1)S(1)}, u32[]{:S(2)}, u32[]{:S(2)}) %collective-permute-start.10) | collective-permute-done | bytes 98336 | tf_op jit(solution)/shard_map/ppermute | solution.py:261
  26.0 0.3 collective-permute-done.12.refs_5_
  26.4 1.0 %collective-permute-done.14.refs_7_ = bf16[48,1024]{1,0:T(8,128)(2,1)S(1)} collective-permute-done((bf16[48,1024]{1,0:T(8,128)(2,1)S(1)}, bf16[48,1024]{1,0:T(8,128)(2,1)S(1)}, u32[]{:S(2)}, u32[]{:S(2)}) %collective-permute-start.14) | collective-permute-done | bytes 98336 | tf_op jit(solution)/shard_map/ppermute | solution.py:251
  27.4 2.7 %collective-permute-start.19 = (bf16[192,512]{1,0:T(8,128)(2,1)S(1)}, bf16[192,512]{1,0:T(8,128)(2,1)S(1)}, u32[]{:S(2)}, u32[]{:S(2)}) collective-permute-start(bf16[192,512]{1,0:T(8,128)(2,1)S(1)} %add_blocks.2.refs_0_), channel_id=1, source_target_pairs={{2,0},{3,1},{0,2},{1,3},{6,4},{7,5},{4,6},{5,7},{10,8},{11,9},{8,1... | collective-permute-start | bytes 589832 | tf_op jit(solution)/shard_map/ppermute | solution.py:289
  30.0 1.6 %collective-permute-start.18 = (bf16[192,512]{1,0:T(8,128)(2,1)S(1)}, bf16[192,512]{1,0:T(8,128)(2,1)S(1)}, u32[]{:S(2)}, u32[]{:S(2)}) collective-permute-start(bf16[192,512]{1,0:T(8,128)(2,1)S(1)} %add_blocks.2.refs_0_), channel_id=1, source_target_pairs={{1,0},{0,1},{3,2},{2,3},{5,4},{4,5},{7,6},{6,7},{9,8},{8,9},{11,10... | collective-permute-start | bytes 589832 | tf_op jit(solution)/shard_map/ppermute | solution.py:289
  31.6 1.2 %collective-permute-start.15 = (bf16[48,1024]{1,0:T(8,128)(2,1)S(1)}, bf16[48,1024]{1,0:T(8,128)(2,1)S(1)}, u32[]{:S(2)}, u32[]{:S(2)}) collective-permute-start(bf16[48,1024]{1,0:T(8,128)(2,1)S(1)} %get-tuple-element.81), channel_id=1, source_target_pairs={{0,8},{4,12},{8,0},{12,4},{16,24},{20,28},{24,16},{28,20},{1,9},{5... | collective-permute-start | bytes 294920 | tf_op jit(solution)/shard_map/ppermute | solution.py:261
  32.9 0.8 %collective-permute-start.16 = (bf16[48,1024]{1,0:T(8,128)(2,1)S(1)}, bf16[48,1024]{1,0:T(8,128)(2,1)S(1)}, u32[]{:S(2)}, u32[]{:S(2)}) collective-permute-start(bf16[48,1024]{1,0:T(8,128)(2,1)S(1)} %get-tuple-element.82), channel_id=1, source_target_pairs={{0,16},{4,20},{8,24},{12,28},{16,0},{20,4},{24,8},{28,12},{1,17},{... | collective-permute-start | bytes 294920 | tf_op jit(solution)/shard_map/ppermute | solution.py:261
  33.7 1.4 %collective-permute-start.17 = (bf16[48,1024]{1,0:T(8,128)(2,1)S(1)}, bf16[48,1024]{1,0:T(8,128)(2,1)S(1)}, u32[]{:S(2)}, u32[]{:S(2)}) collective-permute-start(bf16[48,1024]{1,0:T(8,128)(2,1)S(1)} %get-tuple-element.83), channel_id=1, source_target_pairs={{0,24},{4,28},{8,16},{12,20},{16,8},{20,12},{24,0},{28,4},{1,25},{... | collective-permute-start | bytes 294920 | tf_op jit(solution)/shard_map/ppermute | solution.py:261
  35.1 1.5 %collective-permute-done.15.refs_1_ = bf16[48,1024]{1,0:T(8,128)(2,1)S(1)} collective-permute-done((bf16[48,1024]{1,0:T(8,128)(2,1)S(1)}, bf16[48,1024]{1,0:T(8,128)(2,1)S(1)}, u32[]{:S(2)}, u32[]{:S(2)}) %collective-permute-start.15) | collective-permute-done | bytes 98336 | tf_op jit(solution)/shard_map/ppermute | solution.py:261
  36.6 1.8 %collective-permute-done.16.refs_2_ = bf16[48,1024]{1,0:T(8,128)(2,1)S(1)} collective-permute-done((bf16[48,1024]{1,0:T(8,128)(2,1)S(1)}, bf16[48,1024]{1,0:T(8,128)(2,1)S(1)}, u32[]{:S(2)}, u32[]{:S(2)}) %collective-permute-start.16) | collective-permute-done | bytes 98336 | tf_op jit(solution)/shard_map/ppermute | solution.py:261
  38.4 1.2 %collective-permute-done.19.refs_2_ = bf16[192,512]{1,0:T(8,128)(2,1)S(1)} collective-permute-done((bf16[192,512]{1,0:T(8,128)(2,1)S(1)}, bf16[192,512]{1,0:T(8,128)(2,1)S(1)}, u32[]{:S(2)}, u32[]{:S(2)}) %collective-permute-start.19) | collective-permute-done | bytes 196640 | tf_op jit(solution)/shard_map/ppermute | solution.py:289
  39.6 0.2 collective-permute-done.18.refs_1_
  39.8 0.3 collective-permute-start.23
  40.1 1.1 %collective-permute-start.24 = (bf16[192,512]{1,0:T(8,128)(2,1)S(1)}, bf16[192,512]{1,0:T(8,128)(2,1)S(1)}, u32[]{:S(2)}, u32[]{:S(2)}) collective-permute-start(bf16[192,512]{1,0:T(8,128)(2,1)S(1)} %collective-permute-done.19.refs_2_), channel_id=1, source_target_pairs={{1,0},{0,1},{3,2},{2,3},{5,4},{4,5},{7,6},{6,7},{9,8},{8,9},{11,10... | collective-permute-start | bytes 589832 | tf_op jit(solution)/shard_map/ppermute | solution.py:289
  41.3 0.1 add_blocks.3.refs_0_
  41.4 1.3 %collective-permute-start.25 = (bf16[192,512]{1,0:T(8,128)(2,1)S(1)}, bf16[192,512]{1,0:T(8,128)(2,1)S(1)}, u32[]{:S(2)}, u32[]{:S(2)}) collective-permute-start(bf16[192,512]{1,0:T(8,128)(2,1)S(1)} %add_blocks.3.refs_0_), channel_id=1, source_target_pairs={{1,0},{0,1},{3,2},{2,3},{5,4},{4,5},{7,6},{6,7},{9,8},{8,9},{11,10... | collective-permute-start | bytes 589832 | tf_op jit(solution)/shard_map/ppermute | solution.py:289
  42.7 2.5 %collective-permute-start.26 = (bf16[192,512]{1,0:T(8,128)(2,1)S(1)}, bf16[192,512]{1,0:T(8,128)(2,1)S(1)}, u32[]{:S(2)}, u32[]{:S(2)}) collective-permute-start(bf16[192,512]{1,0:T(8,128)(2,1)S(1)} %add_blocks.3.refs_0_), channel_id=1, source_target_pairs={{2,0},{3,1},{0,2},{1,3},{6,4},{7,5},{4,6},{5,7},{10,8},{11,9},{8,1... | collective-permute-start | bytes 589832 | tf_op jit(solution)/shard_map/ppermute | solution.py:289
  45.2 0.6 %collective-permute-start.27 = (bf16[192,512]{1,0:T(8,128)(2,1)S(1)}, bf16[192,512]{1,0:T(8,128)(2,1)S(1)}, u32[]{:S(2)}, u32[]{:S(2)}) collective-permute-start(bf16[192,512]{1,0:T(8,128)(2,1)S(1)} %add_blocks.3.refs_0_), channel_id=1, source_target_pairs={{3,0},{2,1},{1,2},{0,3},{7,4},{6,5},{5,6},{4,7},{11,8},{10,9},{9,1... | collective-permute-start | bytes 589832 | tf_op jit(solution)/shard_map/ppermute | solution.py:289
  45.8 0.3 weights.1.weight_ref
  46.1 6.0 %collective-permute-done.24.refs_3_ = bf16[192,512]{1,0:T(8,128)(2,1)S(1)} collective-permute-done((bf16[192,512]{1,0:T(8,128)(2,1)S(1)}, bf16[192,512]{1,0:T(8,128)(2,1)S(1)}, u32[]{:S(2)}, u32[]{:S(2)}) %collective-permute-start.24) | collective-permute-done | bytes 196640 | tf_op jit(solution)/shard_map/ppermute | solution.py:289
  52.1 1.7 %combine_gate.1 = (bf16[512,512]{1,0:T(8,128)(2,1)}, f32[8,512]{1,0:T(8,128)S(1)}) custom-call(bf16[512,768]{1,0:T(8,128)(2,1)S(1)} %weights.1.weight_ref, s32[8,512]{1,0:T(8,128)S(1)} %bitcast.5, f32[16,512]{1,0:T(8,128)S(1)} %number.1.key_ref, bf16[512,512]{1,0:T(8,128)(2,1)S(1)} %copy-done.3, bf16[192,512]{1,0:T(8,128)(2,1)S(1)} %add_blocks.2.refs_0_, ...), custom_call_target="tpu_custom_call" | custom-call | bytes 2686976 | tf_op jit(solution)/shard_map/combine_gate/pallas_call | solution.py:23
  53.8 1.2 %collective-permute-done.28 = f32[8,512]{1,0:T(8,128)S(1)} collective-permute-done((f32[8,512]{1,0:T(8,128)S(1)}, f32[8,512]{1,0:T(8,128)S(1)}, u32[]{:S(2)}, u32[]{:S(2)}) %collective-permute-start.28) | collective-permute-done | bytes 16416 | tf_op jit(solution)/shard_map/ppermute | solution.py:251
  55.0 1.2 %collective-permute-start.29 = (f32[8,512]{1,0:T(8,128)S(1)}, f32[8,512]{1,0:T(8,128)S(1)}, u32[]{:S(2)}, u32[]{:S(2)}) collective-permute-start(f32[8,512]{1,0:T(8,128)S(1)} %add.3.refs_4_), channel_id=1, source_target_pairs={{0,8},{4,12},{8,0},{12,4},{16,24},{20,28},{24,16},{28,20},{1,9},{5... | collective-permute-start | bytes 49160 | tf_op jit(solution)/shard_map/ppermute | solution.py:261
  56.2 2.5 %collective-permute-done.29.refs_5_ = f32[8,512]{1,0:T(8,128)S(1)} collective-permute-done((f32[8,512]{1,0:T(8,128)S(1)}, f32[8,512]{1,0:T(8,128)S(1)}, u32[]{:S(2)}, u32[]{:S(2)}) %collective-permute-start.29) | collective-permute-done | bytes 16416 | tf_op jit(solution)/shard_map/ppermute | solution.py:261
  58.8 2.7 %collective-permute-done.27.refs_3_ = bf16[192,512]{1,0:T(8,128)(2,1)S(1)} collective-permute-done((bf16[192,512]{1,0:T(8,128)(2,1)S(1)}, bf16[192,512]{1,0:T(8,128)(2,1)S(1)}, u32[]{:S(2)}, u32[]{:S(2)}) %collective-permute-start.27) | collective-permute-done | bytes 196640 | tf_op jit(solution)/shard_map/ppermute | solution.py:289
  61.4 1.9 %combine.1 = (bf16[512,512]{1,0:T(8,128)(2,1)}, f32[8,512]{1,0:T(8,128)}) custom-call(bf16[512,768]{1,0:T(8,128)(2,1)S(1)} %weights.1.weight_ref, bf16[192,512]{1,0:T(8,128)(2,1)S(1)} %add_blocks.3.refs_0_, bf16[192,512]{1,0:T(8,128)(2,1)S(1)} %collective-permute-done.25.refs_1_, bf16[192,512]{1,0:T(8,128)(2,1)S(1)} %collective-permute-done.26.refs_2_, ...), custom_call_target="tpu_custom_call" | custom-call | flops 402653184 | bytes 2146304 | tf_op jit(solution)/shard_map/combine/pallas_call | solution.py:23
  (39 shorter events, 0.1 us)
Async XLA Ops:
  0.6 2.3 %collective-permute-start = (bf16[512,512]{1,0:T(8,128)(2,1)}, bf16[512,512]{1,0:T(8,128)(2,1)S(1)}, u32[]{:S(2)}, u32[]{:S(2)}) collective-permute-start(bf16[512,512]{1,0:T(8,128)(2,1)} %refs_0_.2), channel_id=1, source_target_pairs={{0,4},{4,0},{8,12},{12,8},{1,5},{5,1},{9,13},{13,9},{2,6},{6,2},{1... | collective-permute-start | bytes 1572872 | tf_op jit(solution)/shard_map/ppermute | solution.py:251
  1.1 6.7 %collective-permute-start.1 = (bf16[512,512]{1,0:T(8,128)(2,1)}, bf16[512,512]{1,0:T(8,128)(2,1)S(1)}, u32[]{:S(2)}, u32[]{:S(2)}) collective-permute-start(bf16[512,512]{1,0:T(8,128)(2,1)} %grads_ref.1), channel_id=1, source_target_pairs={{0,4},{4,0},{8,12},{12,8},{1,5},{5,1},{9,13},{13,9},{2,6},{6,2},{1... | collective-permute-start | bytes 1572872 | tf_op jit(solution)/shard_map/ppermute | solution.py:251
  1.2 0.7 %copy-start.4 = (s32[512,8]{0,1:T(8,128)S(1)}, s32[512,8]{0,1:T(8,128)}, u32[]{:S(2)}) copy-start(s32[512,8]{0,1:T(8,128)} %param.9) | copy-start | bytes 49156
  1.9 1.0 %copy-start.7 = (bf16[512,512]{1,0:T(8,128)(2,1)S(1)}, bf16[512,512]{1,0:T(8,128)(2,1)}, u32[]{:S(2)}) copy-start(bf16[512,512]{1,0:T(8,128)(2,1)} %refs_0_.2) | copy-start | bytes 1572868
  2.1 5.8 %copy-start.3 = (bf16[512,512]{1,0:T(8,128)(2,1)S(1)}, bf16[512,512]{1,0:T(8,128)(2,1)}, u32[]{:S(2)}) copy-start(bf16[512,512]{1,0:T(8,128)(2,1)} %grads_ref.1) | copy-start | bytes 1572868
  3.3 8.4 %collective-permute-start.2 = (bf16[48,1024]{1,0:T(8,128)(2,1)S(1)}, bf16[48,1024]{1,0:T(8,128)(2,1)S(1)}, u32[]{:S(2)}, u32[]{:S(2)}) collective-permute-start(bf16[48,1024]{1,0:T(8,128)(2,1)S(1)} %get-tuple-element.54), channel_id=1, source_target_pairs={{0,8},{4,12},{8,0},{12,4},{16,24},{20,28},{24,16},{28,20},{1,9},{5... | collective-permute-start | bytes 294920 | tf_op jit(solution)/shard_map/ppermute | solution.py:261
  6.3 9.5 %collective-permute-start.4 = (bf16[48,1024]{1,0:T(8,128)(2,1)S(1)}, bf16[48,1024]{1,0:T(8,128)(2,1)S(1)}, u32[]{:S(2)}, u32[]{:S(2)}) collective-permute-start(bf16[48,1024]{1,0:T(8,128)(2,1)S(1)} %get-tuple-element.54), channel_id=1, source_target_pairs={{0,24},{4,28},{8,16},{12,20},{16,8},{20,12},{24,0},{28,4},{1,25},{... | collective-permute-start | bytes 294920 | tf_op jit(solution)/shard_map/ppermute | solution.py:261
  7.8 8.1 %copy-start = (bf16[1,768,2048]{2,1,0:T(8,128)(2,1)S(1)}, bf16[1,768,2048]{2,1,0:T(8,128)(2,1)}, u32[]{:S(2)}) copy-start(bf16[1,768,2048]{2,1,0:T(8,128)(2,1)} %refs_4_.3) | copy-start | bytes 9437188
  7.8 8.1 %copy-start.1 = (bf16[1,768,2048]{2,1,0:T(8,128)(2,1)S(1)}, bf16[1,768,2048]{2,1,0:T(8,128)(2,1)}, u32[]{:S(2)}) copy-start(bf16[1,768,2048]{2,1,0:T(8,128)(2,1)} %refs_5_.3) | copy-start | bytes 9437188
  7.8 8.1 %copy-start.2 = (bf16[1,768,2048]{2,1,0:T(8,128)(2,1)S(1)}, bf16[1,768,2048]{2,1,0:T(8,128)(2,1)}, u32[]{:S(2)}) copy-start(bf16[1,768,2048]{2,1,0:T(8,128)(2,1)} %refs_6_.3) | copy-start | bytes 9437188
  7.8 8.0 %collective-permute-start.3 = (bf16[48,1024]{1,0:T(8,128)(2,1)S(1)}, bf16[48,1024]{1,0:T(8,128)(2,1)S(1)}, u32[]{:S(2)}, u32[]{:S(2)}) collective-permute-start(bf16[48,1024]{1,0:T(8,128)(2,1)S(1)} %get-tuple-element.53.refs_0_), channel_id=1, source_target_pairs={{0,16},{4,20},{8,24},{12,28},{16,0},{20,4},{24,8},{28,12},{1,17},{... | collective-permute-start | bytes 294920 | tf_op jit(solution)/shard_map/ppermute | solution.py:261
  8.2 10.2 %collective-permute-start.5 = (bf16[48,1024]{1,0:T(8,128)(2,1)S(1)}, bf16[48,1024]{1,0:T(8,128)(2,1)S(1)}, u32[]{:S(2)}, u32[]{:S(2)}) collective-permute-start(bf16[48,1024]{1,0:T(8,128)(2,1)S(1)} %get-tuple-element.60), channel_id=1, source_target_pairs={{0,8},{4,12},{8,0},{12,4},{16,24},{20,28},{24,16},{28,20},{1,9},{5... | collective-permute-start | bytes 294920 | tf_op jit(solution)/shard_map/ppermute | solution.py:261
  10.1 8.3 %collective-permute-start.6 = (bf16[48,1024]{1,0:T(8,128)(2,1)S(1)}, bf16[48,1024]{1,0:T(8,128)(2,1)S(1)}, u32[]{:S(2)}, u32[]{:S(2)}) collective-permute-start(bf16[48,1024]{1,0:T(8,128)(2,1)S(1)} %get-tuple-element.64.refs_0_), channel_id=1, source_target_pairs={{0,16},{4,20},{8,24},{12,28},{16,0},{20,4},{24,8},{28,12},{1,17},{... | collective-permute-start | bytes 294920 | tf_op jit(solution)/shard_map/ppermute | solution.py:261
  11.7 6.8 %collective-permute-start.7 = (bf16[48,1024]{1,0:T(8,128)(2,1)S(1)}, bf16[48,1024]{1,0:T(8,128)(2,1)S(1)}, u32[]{:S(2)}, u32[]{:S(2)}) collective-permute-start(bf16[48,1024]{1,0:T(8,128)(2,1)S(1)} %get-tuple-element.60), channel_id=1, source_target_pairs={{0,24},{4,28},{8,16},{12,20},{16,8},{20,12},{24,0},{28,4},{1,25},{... | collective-permute-start | bytes 294920 | tf_op jit(solution)/shard_map/ppermute | solution.py:261
  18.4 6.0 %collective-permute-start.9 = (bf16[48,1024]{1,0:T(8,128)(2,1)S(1)}, bf16[48,1024]{1,0:T(8,128)(2,1)S(1)}, u32[]{:S(2)}, u32[]{:S(2)}) collective-permute-start(bf16[48,1024]{1,0:T(8,128)(2,1)S(1)} %get-tuple-element.63), channel_id=1, source_target_pairs={{0,16},{4,20},{8,24},{12,28},{16,0},{20,4},{24,8},{28,12},{1,17},{... | collective-permute-start | bytes 294920 | tf_op jit(solution)/shard_map/ppermute | solution.py:261
  18.7 6.4 %collective-permute-start.8 = (bf16[48,1024]{1,0:T(8,128)(2,1)S(1)}, bf16[48,1024]{1,0:T(8,128)(2,1)S(1)}, u32[]{:S(2)}, u32[]{:S(2)}) collective-permute-start(bf16[48,1024]{1,0:T(8,128)(2,1)S(1)} %get-tuple-element.62), channel_id=1, source_target_pairs={{0,8},{4,12},{8,0},{12,4},{16,24},{20,28},{24,16},{28,20},{1,9},{5... | collective-permute-start | bytes 294920 | tf_op jit(solution)/shard_map/ppermute | solution.py:261
  20.5 5.5 %collective-permute-start.10 = (bf16[48,1024]{1,0:T(8,128)(2,1)S(1)}, bf16[48,1024]{1,0:T(8,128)(2,1)S(1)}, u32[]{:S(2)}, u32[]{:S(2)}) collective-permute-start(bf16[48,1024]{1,0:T(8,128)(2,1)S(1)} %get-tuple-element.75), channel_id=1, source_target_pairs={{0,24},{4,28},{8,16},{12,20},{16,8},{20,12},{24,0},{28,4},{1,25},{... | collective-permute-start | bytes 294920 | tf_op jit(solution)/shard_map/ppermute | solution.py:261
  22.0 4.0 %collective-permute-start.11 = (bf16[48,1024]{1,0:T(8,128)(2,1)S(1)}, bf16[48,1024]{1,0:T(8,128)(2,1)S(1)}, u32[]{:S(2)}, u32[]{:S(2)}) collective-permute-start(bf16[48,1024]{1,0:T(8,128)(2,1)S(1)} %get-tuple-element.61.refs_0_), channel_id=1, source_target_pairs={{0,4},{4,0},{8,12},{12,8},{1,5},{5,1},{9,13},{13,9},{2,6},{6,2},{1... | collective-permute-start | bytes 294920 | tf_op jit(solution)/shard_map/ppermute | solution.py:251
  22.0 23.8 %copy-start.5 = (s32[512,8]{0,1:T(8,128)S(1)}, s32[512,8]{0,1:T(8,128)}, u32[]{:S(2)}) copy-start(s32[512,8]{0,1:T(8,128)} %param.9) | copy-start | bytes 49156
  22.0 23.8 %copy-start.6 = (f32[512,8]{0,1:T(8,128)S(1)}, f32[512,8]{0,1:T(8,128)}, u32[]{:S(2)}) copy-start(f32[512,8]{0,1:T(8,128)} %param.10) | copy-start | bytes 49156
  24.5 1.9 %collective-permute-start.13 = (bf16[48,1024]{1,0:T(8,128)(2,1)S(1)}, bf16[48,1024]{1,0:T(8,128)(2,1)S(1)}, u32[]{:S(2)}, u32[]{:S(2)}) collective-permute-start(bf16[48,1024]{1,0:T(8,128)(2,1)S(1)} %collective-permute-done.9.refs_2_), channel_id=1, source_target_pairs={{0,4},{4,0},{8,12},{12,8},{1,5},{5,1},{9,13},{13,9},{2,6},{6,2},{1... | collective-permute-start | bytes 294920 | tf_op jit(solution)/shard_map/ppermute | solution.py:251
  25.0 1.3 %collective-permute-start.12 = (bf16[48,1024]{1,0:T(8,128)(2,1)S(1)}, bf16[48,1024]{1,0:T(8,128)(2,1)S(1)}, u32[]{:S(2)}, u32[]{:S(2)}) collective-permute-start(bf16[48,1024]{1,0:T(8,128)(2,1)S(1)} %collective-permute-done.8.refs_1_), channel_id=1, source_target_pairs={{0,4},{4,0},{8,12},{12,8},{1,5},{5,1},{9,13},{13,9},{2,6},{6,2},{1... | collective-permute-start | bytes 294920 | tf_op jit(solution)/shard_map/ppermute | solution.py:251
  26.0 1.3 %collective-permute-start.14 = (bf16[48,1024]{1,0:T(8,128)(2,1)S(1)}, bf16[48,1024]{1,0:T(8,128)(2,1)S(1)}, u32[]{:S(2)}, u32[]{:S(2)}) collective-permute-start(bf16[48,1024]{1,0:T(8,128)(2,1)S(1)} %collective-permute-done.10.refs_3_), channel_id=1, source_target_pairs={{0,4},{4,0},{8,12},{12,8},{1,5},{5,1},{9,13},{13,9},{2,6},{6,2},{1... | collective-permute-start | bytes 294920 | tf_op jit(solution)/shard_map/ppermute | solution.py:251
  27.4 12.2 %collective-permute-start.19 = (bf16[192,512]{1,0:T(8,128)(2,1)S(1)}, bf16[192,512]{1,0:T(8,128)(2,1)S(1)}, u32[]{:S(2)}, u32[]{:S(2)}) collective-permute-start(bf16[192,512]{1,0:T(8,128)(2,1)S(1)} %add_blocks.2.refs_0_), channel_id=1, source_target_pairs={{2,0},{3,1},{0,2},{1,3},{6,4},{7,5},{4,6},{5,7},{10,8},{11,9},{8,1... | collective-permute-start | bytes 589832 | tf_op jit(solution)/shard_map/ppermute | solution.py:289
  30.0 9.8 %collective-permute-start.18 = (bf16[192,512]{1,0:T(8,128)(2,1)S(1)}, bf16[192,512]{1,0:T(8,128)(2,1)S(1)}, u32[]{:S(2)}, u32[]{:S(2)}) collective-permute-start(bf16[192,512]{1,0:T(8,128)(2,1)S(1)} %add_blocks.2.refs_0_), channel_id=1, source_target_pairs={{1,0},{0,1},{3,2},{2,3},{5,4},{4,5},{7,6},{6,7},{9,8},{8,9},{11,10... | collective-permute-start | bytes 589832 | tf_op jit(solution)/shard_map/ppermute | solution.py:289
  31.6 4.9 %collective-permute-start.15 = (bf16[48,1024]{1,0:T(8,128)(2,1)S(1)}, bf16[48,1024]{1,0:T(8,128)(2,1)S(1)}, u32[]{:S(2)}, u32[]{:S(2)}) collective-permute-start(bf16[48,1024]{1,0:T(8,128)(2,1)S(1)} %get-tuple-element.81), channel_id=1, source_target_pairs={{0,8},{4,12},{8,0},{12,4},{16,24},{20,28},{24,16},{28,20},{1,9},{5... | collective-permute-start | bytes 294920 | tf_op jit(solution)/shard_map/ppermute | solution.py:261
  32.9 5.5 %collective-permute-start.16 = (bf16[48,1024]{1,0:T(8,128)(2,1)S(1)}, bf16[48,1024]{1,0:T(8,128)(2,1)S(1)}, u32[]{:S(2)}, u32[]{:S(2)}) collective-permute-start(bf16[48,1024]{1,0:T(8,128)(2,1)S(1)} %get-tuple-element.82), channel_id=1, source_target_pairs={{0,16},{4,20},{8,24},{12,28},{16,0},{20,4},{24,8},{28,12},{1,17},{... | collective-permute-start | bytes 294920 | tf_op jit(solution)/shard_map/ppermute | solution.py:261
  33.7 6.0 %collective-permute-start.17 = (bf16[48,1024]{1,0:T(8,128)(2,1)S(1)}, bf16[48,1024]{1,0:T(8,128)(2,1)S(1)}, u32[]{:S(2)}, u32[]{:S(2)}) collective-permute-start(bf16[48,1024]{1,0:T(8,128)(2,1)S(1)} %get-tuple-element.83), channel_id=1, source_target_pairs={{0,24},{4,28},{8,16},{12,20},{16,8},{20,12},{24,0},{28,4},{1,25},{... | collective-permute-start | bytes 294920 | tf_op jit(solution)/shard_map/ppermute | solution.py:261
  36.6 4.7 %collective-permute-start.20 = (bf16[48,1024]{1,0:T(8,128)(2,1)S(1)}, bf16[48,1024]{1,0:T(8,128)(2,1)S(1)}, u32[]{:S(2)}, u32[]{:S(2)}) collective-permute-start(bf16[48,1024]{1,0:T(8,128)(2,1)S(1)} %get-tuple-element.80.refs_0_), channel_id=1, source_target_pairs={{0,4},{4,0},{8,12},{12,8},{1,5},{5,1},{9,13},{13,9},{2,6},{6,2},{1... | collective-permute-start | bytes 294920 | tf_op jit(solution)/shard_map/ppermute | solution.py:251
  38.4 2.9 %collective-permute-start.21 = (bf16[48,1024]{1,0:T(8,128)(2,1)S(1)}, bf16[48,1024]{1,0:T(8,128)(2,1)S(1)}, u32[]{:S(2)}, u32[]{:S(2)}) collective-permute-start(bf16[48,1024]{1,0:T(8,128)(2,1)S(1)} %collective-permute-done.15.refs_1_), channel_id=1, source_target_pairs={{0,4},{4,0},{8,12},{12,8},{1,5},{5,1},{9,13},{13,9},{2,6},{6,2},{1... | collective-permute-start | bytes 294920 | tf_op jit(solution)/shard_map/ppermute | solution.py:251
  39.6 1.6 %collective-permute-start.22 = (bf16[48,1024]{1,0:T(8,128)(2,1)S(1)}, bf16[48,1024]{1,0:T(8,128)(2,1)S(1)}, u32[]{:S(2)}, u32[]{:S(2)}) collective-permute-start(bf16[48,1024]{1,0:T(8,128)(2,1)S(1)} %collective-permute-done.16.refs_2_), channel_id=1, source_target_pairs={{0,4},{4,0},{8,12},{12,8},{1,5},{5,1},{9,13},{13,9},{2,6},{6,2},{1... | collective-permute-start | bytes 294920 | tf_op jit(solution)/shard_map/ppermute | solution.py:251
  39.8 1.5 %collective-permute-start.23 = (bf16[48,1024]{1,0:T(8,128)(2,1)S(1)}, bf16[48,1024]{1,0:T(8,128)(2,1)S(1)}, u32[]{:S(2)}, u32[]{:S(2)}) collective-permute-start(bf16[48,1024]{1,0:T(8,128)(2,1)S(1)} %collective-permute-done.17.refs_3_), channel_id=1, source_target_pairs={{0,4},{4,0},{8,12},{12,8},{1,5},{5,1},{9,13},{13,9},{2,6},{6,2},{1... | collective-permute-start | bytes 294920 | tf_op jit(solution)/shard_map/ppermute | solution.py:251
  40.1 12.0 %collective-permute-start.24 = (bf16[192,512]{1,0:T(8,128)(2,1)S(1)}, bf16[192,512]{1,0:T(8,128)(2,1)S(1)}, u32[]{:S(2)}, u32[]{:S(2)}) collective-permute-start(bf16[192,512]{1,0:T(8,128)(2,1)S(1)} %collective-permute-done.19.refs_2_), channel_id=1, source_target_pairs={{1,0},{0,1},{3,2},{2,3},{5,4},{4,5},{7,6},{6,7},{9,8},{8,9},{11,10... | collective-permute-start | bytes 589832 | tf_op jit(solution)/shard_map/ppermute | solution.py:289
  41.4 17.4 %collective-permute-start.25 = (bf16[192,512]{1,0:T(8,128)(2,1)S(1)}, bf16[192,512]{1,0:T(8,128)(2,1)S(1)}, u32[]{:S(2)}, u32[]{:S(2)}) collective-permute-start(bf16[192,512]{1,0:T(8,128)(2,1)S(1)} %add_blocks.3.refs_0_), channel_id=1, source_target_pairs={{1,0},{0,1},{3,2},{2,3},{5,4},{4,5},{7,6},{6,7},{9,8},{8,9},{11,10... | collective-permute-start | bytes 589832 | tf_op jit(solution)/shard_map/ppermute | solution.py:289
  42.7 16.1 %collective-permute-start.26 = (bf16[192,512]{1,0:T(8,128)(2,1)S(1)}, bf16[192,512]{1,0:T(8,128)(2,1)S(1)}, u32[]{:S(2)}, u32[]{:S(2)}) collective-permute-start(bf16[192,512]{1,0:T(8,128)(2,1)S(1)} %add_blocks.3.refs_0_), channel_id=1, source_target_pairs={{2,0},{3,1},{0,2},{1,3},{6,4},{7,5},{4,6},{5,7},{10,8},{11,9},{8,1... | collective-permute-start | bytes 589832 | tf_op jit(solution)/shard_map/ppermute | solution.py:289
  45.2 16.2 %collective-permute-start.27 = (bf16[192,512]{1,0:T(8,128)(2,1)S(1)}, bf16[192,512]{1,0:T(8,128)(2,1)S(1)}, u32[]{:S(2)}, u32[]{:S(2)}) collective-permute-start(bf16[192,512]{1,0:T(8,128)(2,1)S(1)} %add_blocks.3.refs_0_), channel_id=1, source_target_pairs={{3,0},{2,1},{1,2},{0,3},{7,4},{6,5},{5,6},{4,7},{11,8},{10,9},{9,1... | collective-permute-start | bytes 589832 | tf_op jit(solution)/shard_map/ppermute | solution.py:289
  53.8 1.2 %collective-permute-start.28 = (f32[8,512]{1,0:T(8,128)S(1)}, f32[8,512]{1,0:T(8,128)S(1)}, u32[]{:S(2)}, u32[]{:S(2)}) collective-permute-start(f32[8,512]{1,0:T(8,128)S(1)} %get-tuple-element.94), channel_id=1, source_target_pairs={{0,4},{4,0},{8,12},{12,8},{1,5},{5,1},{9,13},{13,9},{2,6},{6,2},{1... | collective-permute-start | bytes 49160 | tf_op jit(solution)/shard_map/ppermute | solution.py:251
  55.0 3.7 %collective-permute-start.29 = (f32[8,512]{1,0:T(8,128)S(1)}, f32[8,512]{1,0:T(8,128)S(1)}, u32[]{:S(2)}, u32[]{:S(2)}) collective-permute-start(f32[8,512]{1,0:T(8,128)S(1)} %add.3.refs_4_), channel_id=1, source_target_pairs={{0,8},{4,12},{8,0},{12,4},{16,24},{20,28},{24,16},{28,20},{1,9},{5... | collective-permute-start | bytes 49160 | tf_op jit(solution)/shard_map/ppermute | solution.py:261

commit v17 on v14

--- a/solution.py
+++ b/solution.py
@@ -291,8 +291,7 @@
 
     token_sources = [to_core(tokens, dc) for dc in range(cores)]
     key = call(number_kernel, "number", shape(experts, rows, F32), [routes_t], EARLY)
-    grads, key = after(grad_out, key)
-    grad_sources = [to_core(grads, dc) for dc in range(cores)]
+    grad_sources = [to_core(grad_out, dc) for dc in range(cores)]
     tok_in = dispatch(pick(key, token_sources))
     tok_in[0], grad_pieces = lax.optimization_barrier((tok_in[0], pick(key, grad_sources)))
     grad_in = dispatch(grad_pieces)
@@ -358,10 +357,10 @@
         [all_rows, pltpu.VMEM((experts * CAP, rows), F32)],
         limit=24,
     )
-    gate_parts = [gate_part]
-    for dt in range(1, groups):
-        pairs = [(t, (t + dt) % groups) for t in range(groups)]
-        gate_parts.append(lax.ppermute(gate_part, "tensor", pairs))
+    chip_part = gate_part
+    for dc in range(1, cores):
+        chip_part = chip_part + to_core(gate_part, dc)
+    gate_parts = [to_chip(chip_part, 0, dh) for dh in range(chips)]
     grad_tokens, grad_gates = call(
         functools.partial(combine_kernel, columns),
         "combine",

time: 63.2 us -> 63.4 us (level)
  waiting for transfers between devices: 22.4 us -> 23.3 us
  local copies, waits for them, and re-layouts: 1.72 us -> 0.83 us
    ppermute x3 -> x0, waiting for transfers between devices: 3.55 us -> none  [body(): gate_parts.append(lax.ppermute(gate_part, 'tensor', pairs))]
    ppermute x10 -> x11, waiting for transfers between devices: 1.37 us -> 3.28 us  [to_core(): return lax.ppermute(value, 'tensor', pairs)]
    ppermute x12 -> x13, waiting for transfers between devices: 8.13 us -> 9.63 us  [to_chip(): return lax.ppermute(value, ('dp', 'tensor'), pairs)]
    ppermute x12 -> x13, starting transfers between devices: 16.2 us -> 17.5 us  [to_chip(): return lax.ppermute(value, ('dp', 'tensor'), pairs)]
    ppermute x3 -> x0, starting transfers between devices: 1.06 us -> none  [body(): gate_parts.append(lax.ppermute(gate_part, 'tensor', pairs))]
    ppermute x6, waiting for transfers between devices: 9.38 us -> 10.4 us  [across(): return lax.ppermute(parts[first], 'expert', pairs)]
    unnamed x16, local copies, waits for them, and re-layouts: 1.72 us -> 0.83 us
    ppermute x10 -> x11, starting transfers between devices: 1.76 us -> 1.6 us  [to_core(): return lax.ppermute(value, 'tensor', pairs)]
  transfers between devices with their start and end apart: 31 -> 30, of which waited for: 14 -> 13; matrix products, arithmetic and copies ran while one was open for 0% -> 0% of each run, Pallas kernels for 12% -> 12%
where the time goes in v17:
time: 63.4 us; the launch traced here: 63.1 us
  starting transfers between devices  28.9 us (46%)
  waiting for transfers between devices  23.3 us (37%)
  Pallas kernels  9.28 us (15%)
  local copies, waits for them, and re-layouts  0.83 us (1%)
  between operations  0.76 us (1%)
    ppermute x13, starting transfers between devices, to_chip(): return lax.ppermute(value, ('dp', 'tensor'), pairs)  17.5 us
    ppermute x6, waiting for transfers between devices, across(): return lax.ppermute(parts[first], 'expert', pairs)  10.4 us
    ppermute x6, starting transfers between devices, across(): return lax.ppermute(parts[first], 'expert', pairs)  9.8 us
    ppermute x13, waiting for transfers between devices, to_chip(): return lax.ppermute(value, ('dp', 'tensor'), pairs)  9.63 us
    pallas_call x10, Pallas kernels, call(): pl.pallas_call(kernel, out_shape=out_shape, in_specs=[spec] * len(operand...  9.28 us
    ppermute x11, waiting for transfers between devices, to_core(): return lax.ppermute(value, 'tensor', pairs)  3.28 us
    ppermute x11, starting transfers between devices, to_core(): return lax.ppermute(value, 'tensor', pairs)  1.6 us
  transfers between devices with their start and end apart: 30, of which 13 were waited for; matrix products, arithmetic and copies ran while one was open for 0% of the time, Pallas kernels for 12%

profile of v17, /device:TPU:0, one launch (start us, length us, event | category | flops | bytes accessed | tf_op | source)
XLA Modules:
  0.0 63.1 jit_solution(17868408459557970529)
XLA Ops:
  0.6 0.5 collective-permute-start
  1.1 0.1 collective-permute-start.1
  1.2 0.7 %copy-done.4 = s32[512,8]{0,1:T(8,128)S(1)} copy-done((s32[512,8]{0,1:T(8,128)S(1)}, s32[512,8]{0,1:T(8,128)}, u32[]{:S(2)}) %copy-start.4) | copy-done | bytes 16408
  1.9 0.1 number.1.key_ref
  2.1 0.8 %collective-permute-done.refs_1_ = bf16[512,512]{1,0:T(8,128)(2,1)S(1)} collective-permute-done((bf16[512,512]{1,0:T(8,128)(2,1)}, bf16[512,512]{1,0:T(8,128)(2,1)S(1)}, u32[]{:S(2)}, u32[]{:S(2)}) %collective-permute-start) | collective-permute-done | bytes 524320 | tf_op jit(solution)/shard_map/ppermute | solution.py:240
  2.9 0.1 copy-done.7
  3.0 0.3 pick.2
  3.3 3.0 %collective-permute-start.2 = (bf16[48,1024]{1,0:T(8,128)(2,1)S(1)}, bf16[48,1024]{1,0:T(8,128)(2,1)S(1)}, u32[]{:S(2)}, u32[]{:S(2)}) collective-permute-start(bf16[48,1024]{1,0:T(8,128)(2,1)S(1)} %get-tuple-element.54), channel_id=1, source_target_pairs={{0,8},{4,12},{8,0},{12,4},{16,24},{20,28},{24,16},{28,20},{1,9},{5... | collective-permute-start | bytes 294920 | tf_op jit(solution)/shard_map/ppermute | solution.py:250
  6.3 1.5 %collective-permute-start.4 = (bf16[48,1024]{1,0:T(8,128)(2,1)S(1)}, bf16[48,1024]{1,0:T(8,128)(2,1)S(1)}, u32[]{:S(2)}, u32[]{:S(2)}) collective-permute-start(bf16[48,1024]{1,0:T(8,128)(2,1)S(1)} %get-tuple-element.54), channel_id=1, source_target_pairs={{0,24},{4,28},{8,16},{12,20},{16,8},{20,12},{24,0},{28,4},{1,25},{... | collective-permute-start | bytes 294920 | tf_op jit(solution)/shard_map/ppermute | solution.py:250
  7.8 0.1 collective-permute-start.3
  7.9 0.3 pick.3
  8.2 2.0 %collective-permute-start.5 = (bf16[48,1024]{1,0:T(8,128)(2,1)S(1)}, bf16[48,1024]{1,0:T(8,128)(2,1)S(1)}, u32[]{:S(2)}, u32[]{:S(2)}) collective-permute-start(bf16[48,1024]{1,0:T(8,128)(2,1)S(1)} %get-tuple-element.60), channel_id=1, source_target_pairs={{0,8},{4,12},{8,0},{12,4},{16,24},{20,28},{24,16},{28,20},{1,9},{5... | collective-permute-start | bytes 294920 | tf_op jit(solution)/shard_map/ppermute | solution.py:250
  10.1 1.5 %collective-permute-start.6 = (bf16[48,1024]{1,0:T(8,128)(2,1)S(1)}, bf16[48,1024]{1,0:T(8,128)(2,1)S(1)}, u32[]{:S(2)}, u32[]{:S(2)}) collective-permute-start(bf16[48,1024]{1,0:T(8,128)(2,1)S(1)} %get-tuple-element.64.refs_0_), channel_id=1, source_target_pairs={{0,16},{4,20},{8,24},{12,28},{16,0},{20,4},{24,8},{28,12},{1,17},{... | collective-permute-start | bytes 294920 | tf_op jit(solution)/shard_map/ppermute | solution.py:250
  11.7 0.0 collective-permute-done.2.refs_1_
  11.7 1.2 %collective-permute-start.7 = (bf16[48,1024]{1,0:T(8,128)(2,1)S(1)}, bf16[48,1024]{1,0:T(8,128)(2,1)S(1)}, u32[]{:S(2)}, u32[]{:S(2)}) collective-permute-start(bf16[48,1024]{1,0:T(8,128)(2,1)S(1)} %get-tuple-element.60), channel_id=1, source_target_pairs={{0,24},{4,28},{8,16},{12,20},{16,8},{20,12},{24,0},{28,4},{1,25},{... | collective-permute-start | bytes 294920 | tf_op jit(solution)/shard_map/ppermute | solution.py:250
  12.9 2.9 %collective-permute-done.3.refs_2_ = bf16[48,1024]{1,0:T(8,128)(2,1)S(1)} collective-permute-done((bf16[48,1024]{1,0:T(8,128)(2,1)S(1)}, bf16[48,1024]{1,0:T(8,128)(2,1)S(1)}, u32[]{:S(2)}, u32[]{:S(2)}) %collective-permute-start.3) | collective-permute-done | bytes 98336 | tf_op jit(solution)/shard_map/ppermute | solution.py:250
  15.8 2.6 %forward.1 = (f32[96,768]{1,0:T(8,128)S(1)}, f32[96,768]{1,0:T(8,128)S(1)}, bf16[48,1024]{1,0:T(8,128)(2,1)S(1)}, bf16[48,1024]{1,0:T(8,128)(2,1)S(1)}, bf16[48,...) custom-call(bf16[48,1024]{1,0:T(8,128)(2,1)S(1)} %get-tuple-element.53.refs_0_, ...), custom_call_target="tpu_custom_call" | custom-call | flops 905969664 | bytes 10813440 | tf_op jit(solution)/shard_map/forward/pallas_call | solution.py:23
  18.4 0.2 collective-permute-start.9
  18.7 1.8 %collective-permute-start.8 = (bf16[48,1024]{1,0:T(8,128)(2,1)S(1)}, bf16[48,1024]{1,0:T(8,128)(2,1)S(1)}, u32[]{:S(2)}, u32[]{:S(2)}) collective-permute-start(bf16[48,1024]{1,0:T(8,128)(2,1)S(1)} %get-tuple-element.62), channel_id=1, source_target_pairs={{0,8},{4,12},{8,0},{12,4},{16,24},{20,28},{24,16},{28,20},{1,9},{5... | collective-permute-start | bytes 294920 | tf_op jit(solution)/shard_map/ppermute | solution.py:250
  20.5 1.5 %collective-permute-start.10 = (bf16[48,1024]{1,0:T(8,128)(2,1)S(1)}, bf16[48,1024]{1,0:T(8,128)(2,1)S(1)}, u32[]{:S(2)}, u32[]{:S(2)}) collective-permute-start(bf16[48,1024]{1,0:T(8,128)(2,1)S(1)} %get-tuple-element.75), channel_id=1, source_target_pairs={{0,24},{4,28},{8,16},{12,20},{16,8},{20,12},{24,0},{28,4},{1,25},{... | collective-permute-start | bytes 294920 | tf_op jit(solution)/shard_map/ppermute | solution.py:250
  22.0 2.4 %backward.1 = (bf16[48,1024]{1,0:T(8,128)(2,1)S(1)}, bf16[48,1024]{1,0:T(8,128)(2,1)S(1)}, bf16[48,1024]{1,0:T(8,128)(2,1)S(1)}, bf16[48,1024]{1,0:T(8,128)(2,1)S(1)}) custom-call(bf16[48,1024]{1,0:T(8,128)(2,1)S(1)} %get-tuple-element.64.refs_0_, bf16[48,1024]{1,0:T(8,128)(2,1)S(1)} %collective-permute-done.5.refs_1_, ...), custom_call_target="tpu_custom_call" | custom-call | flops 905969664 | bytes 10813440 | tf_op jit(solution)/shard_map/backward/pallas_call | solution.py:23
  24.5 0.6 collective-permute-start.13
  25.0 0.1 collective-permute-start.12
  25.1 0.9 %collective-permute-done.10.refs_3_ = bf16[48,1024]{1,0:T(8,128)(2,1)S(1)} collective-permute-done((bf16[48,1024]{1,0:T(8,128)(2,1)S(1)}, bf16[48,1024]{1,0:T(8,128)(2,1)S(1)}, u32[]{:S(2)}, u32[]{:S(2)}) %collective-permute-start.10) | collective-permute-done | bytes 98336 | tf_op jit(solution)/shard_map/ppermute | solution.py:250
  26.0 0.3 collective-permute-done.12.refs_5_
  26.4 1.0 %collective-permute-done.14.refs_7_ = bf16[48,1024]{1,0:T(8,128)(2,1)S(1)} collective-permute-done((bf16[48,1024]{1,0:T(8,128)(2,1)S(1)}, bf16[48,1024]{1,0:T(8,128)(2,1)S(1)}, u32[]{:S(2)}, u32[]{:S(2)}) %collective-permute-start.14) | collective-permute-done | bytes 98336 | tf_op jit(solution)/shard_map/ppermute | solution.py:240
  27.4 2.7 %collective-permute-start.19 = (bf16[192,512]{1,0:T(8,128)(2,1)S(1)}, bf16[192,512]{1,0:T(8,128)(2,1)S(1)}, u32[]{:S(2)}, u32[]{:S(2)}) collective-permute-start(bf16[192,512]{1,0:T(8,128)(2,1)S(1)} %add_blocks.2.refs_0_), channel_id=1, source_target_pairs={{2,0},{3,1},{0,2},{1,3},{6,4},{7,5},{4,6},{5,7},{10,8},{11,9},{8,1... | collective-permute-start | bytes 589832 | tf_op jit(solution)/shard_map/ppermute | solution.py:278
  30.0 1.6 %collective-permute-start.18 = (bf16[192,512]{1,0:T(8,128)(2,1)S(1)}, bf16[192,512]{1,0:T(8,128)(2,1)S(1)}, u32[]{:S(2)}, u32[]{:S(2)}) collective-permute-start(bf16[192,512]{1,0:T(8,128)(2,1)S(1)} %add_blocks.2.refs_0_), channel_id=1, source_target_pairs={{1,0},{0,1},{3,2},{2,3},{5,4},{4,5},{7,6},{6,7},{9,8},{8,9},{11,10... | collective-permute-start | bytes 589832 | tf_op jit(solution)/shard_map/ppermute | solution.py:278
  31.6 1.2 %collective-permute-start.15 = (bf16[48,1024]{1,0:T(8,128)(2,1)S(1)}, bf16[48,1024]{1,0:T(8,128)(2,1)S(1)}, u32[]{:S(2)}, u32[]{:S(2)}) collective-permute-start(bf16[48,1024]{1,0:T(8,128)(2,1)S(1)} %get-tuple-element.81), channel_id=1, source_target_pairs={{0,8},{4,12},{8,0},{12,4},{16,24},{20,28},{24,16},{28,20},{1,9},{5... | collective-permute-start | bytes 294920 | tf_op jit(solution)/shard_map/ppermute | solution.py:250
  32.9 0.8 %collective-permute-start.16 = (bf16[48,1024]{1,0:T(8,128)(2,1)S(1)}, bf16[48,1024]{1,0:T(8,128)(2,1)S(1)}, u32[]{:S(2)}, u32[]{:S(2)}) collective-permute-start(bf16[48,1024]{1,0:T(8,128)(2,1)S(1)} %get-tuple-element.82), channel_id=1, source_target_pairs={{0,16},{4,20},{8,24},{12,28},{16,0},{20,4},{24,8},{28,12},{1,17},{... | collective-permute-start | bytes 294920 | tf_op jit(solution)/shard_map/ppermute | solution.py:250
  33.7 1.4 %collective-permute-start.17 = (bf16[48,1024]{1,0:T(8,128)(2,1)S(1)}, bf16[48,1024]{1,0:T(8,128)(2,1)S(1)}, u32[]{:S(2)}, u32[]{:S(2)}) collective-permute-start(bf16[48,1024]{1,0:T(8,128)(2,1)S(1)} %get-tuple-element.83), channel_id=1, source_target_pairs={{0,24},{4,28},{8,16},{12,20},{16,8},{20,12},{24,0},{28,4},{1,25},{... | collective-permute-start | bytes 294920 | tf_op jit(solution)/shard_map/ppermute | solution.py:250
  35.1 1.5 %collective-permute-done.15.refs_1_ = bf16[48,1024]{1,0:T(8,128)(2,1)S(1)} collective-permute-done((bf16[48,1024]{1,0:T(8,128)(2,1)S(1)}, bf16[48,1024]{1,0:T(8,128)(2,1)S(1)}, u32[]{:S(2)}, u32[]{:S(2)}) %collective-permute-start.15) | collective-permute-done | bytes 98336 | tf_op jit(solution)/shard_map/ppermute | solution.py:250
  36.6 1.8 %collective-permute-done.16.refs_2_ = bf16[48,1024]{1,0:T(8,128)(2,1)S(1)} collective-permute-done((bf16[48,1024]{1,0:T(8,128)(2,1)S(1)}, bf16[48,1024]{1,0:T(8,128)(2,1)S(1)}, u32[]{:S(2)}, u32[]{:S(2)}) %collective-permute-start.16) | collective-permute-done | bytes 98336 | tf_op jit(solution)/shard_map/ppermute | solution.py:250
  38.4 1.2 %collective-permute-done.19.refs_2_ = bf16[192,512]{1,0:T(8,128)(2,1)S(1)} collective-permute-done((bf16[192,512]{1,0:T(8,128)(2,1)S(1)}, bf16[192,512]{1,0:T(8,128)(2,1)S(1)}, u32[]{:S(2)}, u32[]{:S(2)}) %collective-permute-start.19) | collective-permute-done | bytes 196640 | tf_op jit(solution)/shard_map/ppermute | solution.py:278
  39.6 0.2 collective-permute-done.18.refs_1_
  39.8 0.3 collective-permute-start.23
  40.1 1.1 %collective-permute-start.24 = (bf16[192,512]{1,0:T(8,128)(2,1)S(1)}, bf16[192,512]{1,0:T(8,128)(2,1)S(1)}, u32[]{:S(2)}, u32[]{:S(2)}) collective-permute-start(bf16[192,512]{1,0:T(8,128)(2,1)S(1)} %collective-permute-done.19.refs_2_), channel_id=1, source_target_pairs={{1,0},{0,1},{3,2},{2,3},{5,4},{4,5},{7,6},{6,7},{9,8},{8,9},{11,10... | collective-permute-start | bytes 589832 | tf_op jit(solution)/shard_map/ppermute | solution.py:278
  41.3 0.1 add_blocks.3.refs_3_
  41.4 3.2 %collective-permute-start.25 = (bf16[192,512]{1,0:T(8,128)(2,1)S(1)}, bf16[192,512]{1,0:T(8,128)(2,1)S(1)}, u32[]{:S(2)}, u32[]{:S(2)}) collective-permute-start(bf16[192,512]{1,0:T(8,128)(2,1)S(1)} %add_blocks.3.refs_3_), channel_id=1, source_target_pairs={{3,0},{2,1},{1,2},{0,3},{7,4},{6,5},{5,6},{4,7},{11,8},{10,9},{9,1... | collective-permute-start | bytes 589832 | tf_op jit(solution)/shard_map/ppermute | solution.py:278
  44.6 1.2 %collective-permute-start.27 = (bf16[192,512]{1,0:T(8,128)(2,1)S(1)}, bf16[192,512]{1,0:T(8,128)(2,1)S(1)}, u32[]{:S(2)}, u32[]{:S(2)}) collective-permute-start(bf16[192,512]{1,0:T(8,128)(2,1)S(1)} %add_blocks.3.refs_3_), channel_id=1, source_target_pairs={{1,0},{0,1},{3,2},{2,3},{5,4},{4,5},{7,6},{6,7},{9,8},{8,9},{11,10... | collective-permute-start | bytes 589832 | tf_op jit(solution)/shard_map/ppermute | solution.py:278
  45.8 0.3 weights.1.weight_ref
  46.1 1.0 %collective-permute-done.24.refs_3_ = bf16[192,512]{1,0:T(8,128)(2,1)S(1)} collective-permute-done((bf16[192,512]{1,0:T(8,128)(2,1)S(1)}, bf16[192,512]{1,0:T(8,128)(2,1)S(1)}, u32[]{:S(2)}, u32[]{:S(2)}) %collective-permute-start.24) | collective-permute-done | bytes 196640 | tf_op jit(solution)/shard_map/ppermute | solution.py:278
  47.1 1.7 %combine_gate.1 = (bf16[512,512]{1,0:T(8,128)(2,1)}, f32[8,512]{1,0:T(8,128)S(1)}) custom-call(bf16[512,768]{1,0:T(8,128)(2,1)S(1)} %weights.1.weight_ref, s32[8,512]{1,0:T(8,128)S(1)} %bitcast.5, f32[16,512]{1,0:T(8,128)S(1)} %number.1.key_ref, bf16[512,512]{1,0:T(8,128)(2,1)S(1)} %copy-done.3, bf16[192,512]{1,0:T(8,128)(2,1)S(1)} %add_blocks.2.refs_0_, ...), custom_call_target="tpu_custom_call" | custom-call | bytes 2686976 | tf_op jit(solution)/shard_map/combine_gate/pallas_call | solution.py:23
  48.9 1.2 %collective-permute-done.28 = f32[8,512]{1,0:T(8,128)S(1)} collective-permute-done((f32[8,512]{1,0:T(8,128)S(1)}, f32[8,512]{1,0:T(8,128)S(1)}, u32[]{:S(2)}, u32[]{:S(2)}) %collective-permute-start.28) | collective-permute-done | bytes 16416 | tf_op jit(solution)/shard_map/ppermute | solution.py:240
  50.0 1.2 %collective-permute-start.29 = (f32[8,512]{1,0:T(8,128)S(1)}, f32[8,512]{1,0:T(8,128)S(1)}, u32[]{:S(2)}, u32[]{:S(2)}) collective-permute-start(f32[8,512]{1,0:T(8,128)S(1)} %add.3.refs_4_), channel_id=1, source_target_pairs={{0,8},{4,12},{8,0},{12,4},{16,24},{20,28},{24,16},{28,20},{1,9},{5... | collective-permute-start | bytes 49160 | tf_op jit(solution)/shard_map/ppermute | solution.py:250
  51.3 2.5 %collective-permute-done.29.refs_5_ = f32[8,512]{1,0:T(8,128)S(1)} collective-permute-done((f32[8,512]{1,0:T(8,128)S(1)}, f32[8,512]{1,0:T(8,128)S(1)}, u32[]{:S(2)}, u32[]{:S(2)}) %collective-permute-start.29) | collective-permute-done | bytes 16416 | tf_op jit(solution)/shard_map/ppermute | solution.py:250
  53.8 8.0 %collective-permute-done.26.refs_1_ = bf16[192,512]{1,0:T(8,128)(2,1)S(1)} collective-permute-done((bf16[192,512]{1,0:T(8,128)(2,1)S(1)}, bf16[192,512]{1,0:T(8,128)(2,1)S(1)}, u32[]{:S(2)}, u32[]{:S(2)}) %collective-permute-start.26) | collective-permute-done | bytes 196640 | tf_op jit(solution)/shard_map/ppermute | solution.py:278
  61.8 1.4 %combine.1 = (bf16[512,512]{1,0:T(8,128)(2,1)}, f32[8,512]{1,0:T(8,128)}) custom-call(bf16[512,768]{1,0:T(8,128)(2,1)S(1)} %weights.1.weight_ref, bf16[192,512]{1,0:T(8,128)(2,1)S(1)} %collective-permute-done.25.refs_0_, bf16[192,512]{1,0:T(8,128)(2,1)S(1)} %collective-permute-done.26.refs_1_, bf16[192,512]{1,0:T(8,128)(2,1)S(1)} %collective-permute-done.27.refs_2_, ...), custom_call_target="tpu_custom_call" | custom-call | flops 402653184 | bytes 2146304 | tf_op jit(solution)/shard_map/combine/pallas_call | solution.py:23
  (39 shorter events, 0.1 us)
Async XLA Ops:
  0.6 2.3 %collective-permute-start = (bf16[512,512]{1,0:T(8,128)(2,1)}, bf16[512,512]{1,0:T(8,128)(2,1)S(1)}, u32[]{:S(2)}, u32[]{:S(2)}) collective-permute-start(bf16[512,512]{1,0:T(8,128)(2,1)} %refs_0_.2), channel_id=1, source_target_pairs={{0,4},{4,0},{8,12},{12,8},{1,5},{5,1},{9,13},{13,9},{2,6},{6,2},{1... | collective-permute-start | bytes 1572872 | tf_op jit(solution)/shard_map/ppermute | solution.py:240
  1.1 6.7 %collective-permute-start.1 = (bf16[512,512]{1,0:T(8,128)(2,1)}, bf16[512,512]{1,0:T(8,128)(2,1)S(1)}, u32[]{:S(2)}, u32[]{:S(2)}) collective-permute-start(bf16[512,512]{1,0:T(8,128)(2,1)} %grads_ref.1), channel_id=1, source_target_pairs={{0,4},{4,0},{8,12},{12,8},{1,5},{5,1},{9,13},{13,9},{2,6},{6,2},{1... | collective-permute-start | bytes 1572872 | tf_op jit(solution)/shard_map/ppermute | solution.py:240
  1.2 0.7 %copy-start.4 = (s32[512,8]{0,1:T(8,128)S(1)}, s32[512,8]{0,1:T(8,128)}, u32[]{:S(2)}) copy-start(s32[512,8]{0,1:T(8,128)} %param.9) | copy-start | bytes 49156
  1.9 1.0 %copy-start.7 = (bf16[512,512]{1,0:T(8,128)(2,1)S(1)}, bf16[512,512]{1,0:T(8,128)(2,1)}, u32[]{:S(2)}) copy-start(bf16[512,512]{1,0:T(8,128)(2,1)} %refs_0_.2) | copy-start | bytes 1572868
  2.1 5.8 %copy-start.3 = (bf16[512,512]{1,0:T(8,128)(2,1)S(1)}, bf16[512,512]{1,0:T(8,128)(2,1)}, u32[]{:S(2)}) copy-start(bf16[512,512]{1,0:T(8,128)(2,1)} %grads_ref.1) | copy-start | bytes 1572868
  3.3 8.4 %collective-permute-start.2 = (bf16[48,1024]{1,0:T(8,128)(2,1)S(1)}, bf16[48,1024]{1,0:T(8,128)(2,1)S(1)}, u32[]{:S(2)}, u32[]{:S(2)}) collective-permute-start(bf16[48,1024]{1,0:T(8,128)(2,1)S(1)} %get-tuple-element.54), channel_id=1, source_target_pairs={{0,8},{4,12},{8,0},{12,4},{16,24},{20,28},{24,16},{28,20},{1,9},{5... | collective-permute-start | bytes 294920 | tf_op jit(solution)/shard_map/ppermute | solution.py:250
  6.3 9.5 %collective-permute-start.4 = (bf16[48,1024]{1,0:T(8,128)(2,1)S(1)}, bf16[48,1024]{1,0:T(8,128)(2,1)S(1)}, u32[]{:S(2)}, u32[]{:S(2)}) collective-permute-start(bf16[48,1024]{1,0:T(8,128)(2,1)S(1)} %get-tuple-element.54), channel_id=1, source_target_pairs={{0,24},{4,28},{8,16},{12,20},{16,8},{20,12},{24,0},{28,4},{1,25},{... | collective-permute-start | bytes 294920 | tf_op jit(solution)/shard_map/ppermute | solution.py:250
  7.8 8.1 %copy-start = (bf16[1,768,2048]{2,1,0:T(8,128)(2,1)S(1)}, bf16[1,768,2048]{2,1,0:T(8,128)(2,1)}, u32[]{:S(2)}) copy-start(bf16[1,768,2048]{2,1,0:T(8,128)(2,1)} %refs_4_.3) | copy-start | bytes 9437188
  7.8 8.1 %copy-start.1 = (bf16[1,768,2048]{2,1,0:T(8,128)(2,1)S(1)}, bf16[1,768,2048]{2,1,0:T(8,128)(2,1)}, u32[]{:S(2)}) copy-start(bf16[1,768,2048]{2,1,0:T(8,128)(2,1)} %refs_5_.3) | copy-start | bytes 9437188
  7.8 8.1 %copy-start.2 = (bf16[1,768,2048]{2,1,0:T(8,128)(2,1)S(1)}, bf16[1,768,2048]{2,1,0:T(8,128)(2,1)}, u32[]{:S(2)}) copy-start(bf16[1,768,2048]{2,1,0:T(8,128)(2,1)} %refs_6_.3) | copy-start | bytes 9437188
  7.8 8.0 %collective-permute-start.3 = (bf16[48,1024]{1,0:T(8,128)(2,1)S(1)}, bf16[48,1024]{1,0:T(8,128)(2,1)S(1)}, u32[]{:S(2)}, u32[]{:S(2)}) collective-permute-start(bf16[48,1024]{1,0:T(8,128)(2,1)S(1)} %get-tuple-element.53.refs_0_), channel_id=1, source_target_pairs={{0,16},{4,20},{8,24},{12,28},{16,0},{20,4},{24,8},{28,12},{1,17},{... | collective-permute-start | bytes 294920 | tf_op jit(solution)/shard_map/ppermute | solution.py:250
  8.2 10.2 %collective-permute-start.5 = (bf16[48,1024]{1,0:T(8,128)(2,1)S(1)}, bf16[48,1024]{1,0:T(8,128)(2,1)S(1)}, u32[]{:S(2)}, u32[]{:S(2)}) collective-permute-start(bf16[48,1024]{1,0:T(8,128)(2,1)S(1)} %get-tuple-element.60), channel_id=1, source_target_pairs={{0,8},{4,12},{8,0},{12,4},{16,24},{20,28},{24,16},{28,20},{1,9},{5... | collective-permute-start | bytes 294920 | tf_op jit(solution)/shard_map/ppermute | solution.py:250
  10.1 8.3 %collective-permute-start.6 = (bf16[48,1024]{1,0:T(8,128)(2,1)S(1)}, bf16[48,1024]{1,0:T(8,128)(2,1)S(1)}, u32[]{:S(2)}, u32[]{:S(2)}) collective-permute-start(bf16[48,1024]{1,0:T(8,128)(2,1)S(1)} %get-tuple-element.64.refs_0_), channel_id=1, source_target_pairs={{0,16},{4,20},{8,24},{12,28},{16,0},{20,4},{24,8},{28,12},{1,17},{... | collective-permute-start | bytes 294920 | tf_op jit(solution)/shard_map/ppermute | solution.py:250
  11.7 6.8 %collective-permute-start.7 = (bf16[48,1024]{1,0:T(8,128)(2,1)S(1)}, bf16[48,1024]{1,0:T(8,128)(2,1)S(1)}, u32[]{:S(2)}, u32[]{:S(2)}) collective-permute-start(bf16[48,1024]{1,0:T(8,128)(2,1)S(1)} %get-tuple-element.60), channel_id=1, source_target_pairs={{0,24},{4,28},{8,16},{12,20},{16,8},{20,12},{24,0},{28,4},{1,25},{... | collective-permute-start | bytes 294920 | tf_op jit(solution)/shard_map/ppermute | solution.py:250
  18.4 6.0 %collective-permute-start.9 = (bf16[48,1024]{1,0:T(8,128)(2,1)S(1)}, bf16[48,1024]{1,0:T(8,128)(2,1)S(1)}, u32[]{:S(2)}, u32[]{:S(2)}) collective-permute-start(bf16[48,1024]{1,0:T(8,128)(2,1)S(1)} %get-tuple-element.63), channel_id=1, source_target_pairs={{0,16},{4,20},{8,24},{12,28},{16,0},{20,4},{24,8},{28,12},{1,17},{... | collective-permute-start | bytes 294920 | tf_op jit(solution)/shard_map/ppermute | solution.py:250
  18.7 6.4 %collective-permute-start.8 = (bf16[48,1024]{1,0:T(8,128)(2,1)S(1)}, bf16[48,1024]{1,0:T(8,128)(2,1)S(1)}, u32[]{:S(2)}, u32[]{:S(2)}) collective-permute-start(bf16[48,1024]{1,0:T(8,128)(2,1)S(1)} %get-tuple-element.62), channel_id=1, source_target_pairs={{0,8},{4,12},{8,0},{12,4},{16,24},{20,28},{24,16},{28,20},{1,9},{5... | collective-permute-start | bytes 294920 | tf_op jit(solution)/shard_map/ppermute | solution.py:250
  20.5 5.5 %collective-permute-start.10 = (bf16[48,1024]{1,0:T(8,128)(2,1)S(1)}, bf16[48,1024]{1,0:T(8,128)(2,1)S(1)}, u32[]{:S(2)}, u32[]{:S(2)}) collective-permute-start(bf16[48,1024]{1,0:T(8,128)(2,1)S(1)} %get-tuple-element.75), channel_id=1, source_target_pairs={{0,24},{4,28},{8,16},{12,20},{16,8},{20,12},{24,0},{28,4},{1,25},{... | collective-permute-start | bytes 294920 | tf_op jit(solution)/shard_map/ppermute | solution.py:250
  22.0 4.0 %collective-permute-start.11 = (bf16[48,1024]{1,0:T(8,128)(2,1)S(1)}, bf16[48,1024]{1,0:T(8,128)(2,1)S(1)}, u32[]{:S(2)}, u32[]{:S(2)}) collective-permute-start(bf16[48,1024]{1,0:T(8,128)(2,1)S(1)} %get-tuple-element.61.refs_0_), channel_id=1, source_target_pairs={{0,4},{4,0},{8,12},{12,8},{1,5},{5,1},{9,13},{13,9},{2,6},{6,2},{1... | collective-permute-start | bytes 294920 | tf_op jit(solution)/shard_map/ppermute | solution.py:240
  22.0 23.8 %copy-start.5 = (s32[512,8]{0,1:T(8,128)S(1)}, s32[512,8]{0,1:T(8,128)}, u32[]{:S(2)}) copy-start(s32[512,8]{0,1:T(8,128)} %param.9) | copy-start | bytes 49156
  22.0 23.8 %copy-start.6 = (f32[512,8]{0,1:T(8,128)S(1)}, f32[512,8]{0,1:T(8,128)}, u32[]{:S(2)}) copy-start(f32[512,8]{0,1:T(8,128)} %param.10) | copy-start | bytes 49156
  24.5 1.9 %collective-permute-start.13 = (bf16[48,1024]{1,0:T(8,128)(2,1)S(1)}, bf16[48,1024]{1,0:T(8,128)(2,1)S(1)}, u32[]{:S(2)}, u32[]{:S(2)}) collective-permute-start(bf16[48,1024]{1,0:T(8,128)(2,1)S(1)} %collective-permute-done.9.refs_2_), channel_id=1, source_target_pairs={{0,4},{4,0},{8,12},{12,8},{1,5},{5,1},{9,13},{13,9},{2,6},{6,2},{1... | collective-permute-start | bytes 294920 | tf_op jit(solution)/shard_map/ppermute | solution.py:240
  25.0 1.3 %collective-permute-start.12 = (bf16[48,1024]{1,0:T(8,128)(2,1)S(1)}, bf16[48,1024]{1,0:T(8,128)(2,1)S(1)}, u32[]{:S(2)}, u32[]{:S(2)}) collective-permute-start(bf16[48,1024]{1,0:T(8,128)(2,1)S(1)} %collective-permute-done.8.refs_1_), channel_id=1, source_target_pairs={{0,4},{4,0},{8,12},{12,8},{1,5},{5,1},{9,13},{13,9},{2,6},{6,2},{1... | collective-permute-start | bytes 294920 | tf_op jit(solution)/shard_map/ppermute | solution.py:240
  26.0 1.3 %collective-permute-start.14 = (bf16[48,1024]{1,0:T(8,128)(2,1)S(1)}, bf16[48,1024]{1,0:T(8,128)(2,1)S(1)}, u32[]{:S(2)}, u32[]{:S(2)}) collective-permute-start(bf16[48,1024]{1,0:T(8,128)(2,1)S(1)} %collective-permute-done.10.refs_3_), channel_id=1, source_target_pairs={{0,4},{4,0},{8,12},{12,8},{1,5},{5,1},{9,13},{13,9},{2,6},{6,2},{1... | collective-permute-start | bytes 294920 | tf_op jit(solution)/shard_map/ppermute | solution.py:240
  27.4 12.2 %collective-permute-start.19 = (bf16[192,512]{1,0:T(8,128)(2,1)S(1)}, bf16[192,512]{1,0:T(8,128)(2,1)S(1)}, u32[]{:S(2)}, u32[]{:S(2)}) collective-permute-start(bf16[192,512]{1,0:T(8,128)(2,1)S(1)} %add_blocks.2.refs_0_), channel_id=1, source_target_pairs={{2,0},{3,1},{0,2},{1,3},{6,4},{7,5},{4,6},{5,7},{10,8},{11,9},{8,1... | collective-permute-start | bytes 589832 | tf_op jit(solution)/shard_map/ppermute | solution.py:278
  30.0 9.8 %collective-permute-start.18 = (bf16[192,512]{1,0:T(8,128)(2,1)S(1)}, bf16[192,512]{1,0:T(8,128)(2,1)S(1)}, u32[]{:S(2)}, u32[]{:S(2)}) collective-permute-start(bf16[192,512]{1,0:T(8,128)(2,1)S(1)} %add_blocks.2.refs_0_), channel_id=1, source_target_pairs={{1,0},{0,1},{3,2},{2,3},{5,4},{4,5},{7,6},{6,7},{9,8},{8,9},{11,10... | collective-permute-start | bytes 589832 | tf_op jit(solution)/shard_map/ppermute | solution.py:278
  31.6 4.9 %collective-permute-start.15 = (bf16[48,1024]{1,0:T(8,128)(2,1)S(1)}, bf16[48,1024]{1,0:T(8,128)(2,1)S(1)}, u32[]{:S(2)}, u32[]{:S(2)}) collective-permute-start(bf16[48,1024]{1,0:T(8,128)(2,1)S(1)} %get-tuple-element.81), channel_id=1, source_target_pairs={{0,8},{4,12},{8,0},{12,4},{16,24},{20,28},{24,16},{28,20},{1,9},{5... | collective-permute-start | bytes 294920 | tf_op jit(solution)/shard_map/ppermute | solution.py:250
  32.9 5.5 %collective-permute-start.16 = (bf16[48,1024]{1,0:T(8,128)(2,1)S(1)}, bf16[48,1024]{1,0:T(8,128)(2,1)S(1)}, u32[]{:S(2)}, u32[]{:S(2)}) collective-permute-start(bf16[48,1024]{1,0:T(8,128)(2,1)S(1)} %get-tuple-element.82), channel_id=1, source_target_pairs={{0,16},{4,20},{8,24},{12,28},{16,0},{20,4},{24,8},{28,12},{1,17},{... | collective-permute-start | bytes 294920 | tf_op jit(solution)/shard_map/ppermute | solution.py:250
  33.7 6.0 %collective-permute-start.17 = (bf16[48,1024]{1,0:T(8,128)(2,1)S(1)}, bf16[48,1024]{1,0:T(8,128)(2,1)S(1)}, u32[]{:S(2)}, u32[]{:S(2)}) collective-permute-start(bf16[48,1024]{1,0:T(8,128)(2,1)S(1)} %get-tuple-element.83), channel_id=1, source_target_pairs={{0,24},{4,28},{8,16},{12,20},{16,8},{20,12},{24,0},{28,4},{1,25},{... | collective-permute-start | bytes 294920 | tf_op jit(solution)/shard_map/ppermute | solution.py:250
  36.6 4.7 %collective-permute-start.20 = (bf16[48,1024]{1,0:T(8,128)(2,1)S(1)}, bf16[48,1024]{1,0:T(8,128)(2,1)S(1)}, u32[]{:S(2)}, u32[]{:S(2)}) collective-permute-start(bf16[48,1024]{1,0:T(8,128)(2,1)S(1)} %get-tuple-element.80.refs_0_), channel_id=1, source_target_pairs={{0,4},{4,0},{8,12},{12,8},{1,5},{5,1},{9,13},{13,9},{2,6},{6,2},{1... | collective-permute-start | bytes 294920 | tf_op jit(solution)/shard_map/ppermute | solution.py:240
  38.4 2.9 %collective-permute-start.21 = (bf16[48,1024]{1,0:T(8,128)(2,1)S(1)}, bf16[48,1024]{1,0:T(8,128)(2,1)S(1)}, u32[]{:S(2)}, u32[]{:S(2)}) collective-permute-start(bf16[48,1024]{1,0:T(8,128)(2,1)S(1)} %collective-permute-done.15.refs_1_), channel_id=1, source_target_pairs={{0,4},{4,0},{8,12},{12,8},{1,5},{5,1},{9,13},{13,9},{2,6},{6,2},{1... | collective-permute-start | bytes 294920 | tf_op jit(solution)/shard_map/ppermute | solution.py:240
  39.6 1.6 %collective-permute-start.22 = (bf16[48,1024]{1,0:T(8,128)(2,1)S(1)}, bf16[48,1024]{1,0:T(8,128)(2,1)S(1)}, u32[]{:S(2)}, u32[]{:S(2)}) collective-permute-start(bf16[48,1024]{1,0:T(8,128)(2,1)S(1)} %collective-permute-done.16.refs_2_), channel_id=1, source_target_pairs={{0,4},{4,0},{8,12},{12,8},{1,5},{5,1},{9,13},{13,9},{2,6},{6,2},{1... | collective-permute-start | bytes 294920 | tf_op jit(solution)/shard_map/ppermute | solution.py:240
  39.8 1.5 %collective-permute-start.23 = (bf16[48,1024]{1,0:T(8,128)(2,1)S(1)}, bf16[48,1024]{1,0:T(8,128)(2,1)S(1)}, u32[]{:S(2)}, u32[]{:S(2)}) collective-permute-start(bf16[48,1024]{1,0:T(8,128)(2,1)S(1)} %collective-permute-done.17.refs_3_), channel_id=1, source_target_pairs={{0,4},{4,0},{8,12},{12,8},{1,5},{5,1},{9,13},{13,9},{2,6},{6,2},{1... | collective-permute-start | bytes 294920 | tf_op jit(solution)/shard_map/ppermute | solution.py:240
  40.1 7.0 %collective-permute-start.24 = (bf16[192,512]{1,0:T(8,128)(2,1)S(1)}, bf16[192,512]{1,0:T(8,128)(2,1)S(1)}, u32[]{:S(2)}, u32[]{:S(2)}) collective-permute-start(bf16[192,512]{1,0:T(8,128)(2,1)S(1)} %collective-permute-done.19.refs_2_), channel_id=1, source_target_pairs={{1,0},{0,1},{3,2},{2,3},{5,4},{4,5},{7,6},{6,7},{9,8},{8,9},{11,10... | collective-permute-start | bytes 589832 | tf_op jit(solution)/shard_map/ppermute | solution.py:278
  41.4 12.4 %collective-permute-start.25 = (bf16[192,512]{1,0:T(8,128)(2,1)S(1)}, bf16[192,512]{1,0:T(8,128)(2,1)S(1)}, u32[]{:S(2)}, u32[]{:S(2)}) collective-permute-start(bf16[192,512]{1,0:T(8,128)(2,1)S(1)} %add_blocks.3.refs_3_), channel_id=1, source_target_pairs={{3,0},{2,1},{1,2},{0,3},{7,4},{6,5},{5,6},{4,7},{11,8},{10,9},{9,1... | collective-permute-start | bytes 589832 | tf_op jit(solution)/shard_map/ppermute | solution.py:278
  44.6 17.2 %collective-permute-start.26 = (bf16[192,512]{1,0:T(8,128)(2,1)S(1)}, bf16[192,512]{1,0:T(8,128)(2,1)S(1)}, u32[]{:S(2)}, u32[]{:S(2)}) collective-permute-start(bf16[192,512]{1,0:T(8,128)(2,1)S(1)} %add_blocks.3.refs_3_), channel_id=1, source_target_pairs={{2,0},{3,1},{0,2},{1,3},{6,4},{7,5},{4,6},{5,7},{10,8},{11,9},{8,1... | collective-permute-start | bytes 589832 | tf_op jit(solution)/shard_map/ppermute | solution.py:278
  44.6 17.2 %collective-permute-start.27 = (bf16[192,512]{1,0:T(8,128)(2,1)S(1)}, bf16[192,512]{1,0:T(8,128)(2,1)S(1)}, u32[]{:S(2)}, u32[]{:S(2)}) collective-permute-start(bf16[192,512]{1,0:T(8,128)(2,1)S(1)} %add_blocks.3.refs_3_), channel_id=1, source_target_pairs={{1,0},{0,1},{3,2},{2,3},{5,4},{4,5},{7,6},{6,7},{9,8},{8,9},{11,10... | collective-permute-start | bytes 589832 | tf_op jit(solution)/shard_map/ppermute | solution.py:278
  48.9 1.2 %collective-permute-start.28 = (f32[8,512]{1,0:T(8,128)S(1)}, f32[8,512]{1,0:T(8,128)S(1)}, u32[]{:S(2)}, u32[]{:S(2)}) collective-permute-start(f32[8,512]{1,0:T(8,128)S(1)} %get-tuple-element.94), channel_id=1, source_target_pairs={{0,4},{4,0},{8,12},{12,8},{1,5},{5,1},{9,13},{13,9},{2,6},{6,2},{1... | collective-permute-start | bytes 49160 | tf_op jit(solution)/shard_map/ppermute | solution.py:240
  50.0 3.7 %collective-permute-start.29 = (f32[8,512]{1,0:T(8,128)S(1)}, f32[8,512]{1,0:T(8,128)S(1)}, u32[]{:S(2)}, u32[]{:S(2)}) collective-permute-start(f32[8,512]{1,0:T(8,128)S(1)} %add.3.refs_4_), channel_id=1, source_target_pairs={{0,8},{4,12},{8,0},{12,4},{16,24},{20,28},{24,16},{28,20},{1,9},{5... | collective-permute-start | bytes 49160 | tf_op jit(solution)/shard_map/ppermute | solution.py:250
